TPU v7x, 32 devices: a whole 2x2x4 slice. The times are simulated.
32 devices in a mesh: tm: 4 (over y, x), space: 8 (over z, core).
Axes of the slice: x: 2, y: 2, z: 4, core: 2. Of those that a mesh axis runs over, the one named last changes fastest.
Arguments:
- snapshots: float32 [128, 3, 8, 16, 128], P('tm', None, 'space'), may hold values from -6 to 6
- coeffs: float32 [128, 128], replicated, may hold values from -0.5 to 0.5
- pair_table: int32 [2048, 2], replicated, may hold values from 0 to 127
Outputs:
- tensor: float32 [2048, 128], P(('tm', 'space'))
Inputs may be any that keep to these rules, and one draw needn't show every extreme that they name: `pair_table`: column 0 names the carrying mode, column 1 the carried mode.
All inputs are finite; a program needn't handle non-finite values.
Results may differ from a plain program's by a relative error of at most 0.00016.
Values sent between devices are 32-bit elements; how exact they have to be, the bound alone decides.
No kernel may reach another device: no remote copies, remote signals or barrier semaphores. Data moves between devices by JAX's collectives and lax.ppermute only.
A program may use at most 192 MiB of HBM per device.

v0:
```python
import math

import jax
import jax.numpy as jnp
from jax import lax
from jax.sharding import PartitionSpec as P


def padded(block, sides, width, periodic):
    for axis, dim in sides:
        count = lax.axis_size(axis)
        forward = [(i, i + 1) for i in range(count - 1)]
        if periodic:
            forward.append((count - 1, 0))
        backward = [(target, source) for source, target in forward]
        low = lax.ppermute(
            lax.slice_in_dim(block, block.shape[dim] - width, None, axis=dim), axis, forward
        )
        high = lax.ppermute(lax.slice_in_dim(block, 0, width, axis=dim), axis, backward)
        block = jnp.concatenate([low, block, high], axis=dim)
    return block


def slope_field(center, padded_x, padded_y):
    stream_slope = (padded_x[:, :, 2:] - padded_x[:, :, :-2]) * 0.5
    normal_slope = (padded_y[:, :, :, 2:] - padded_y[:, :, :, :-2]) * 0.5
    span_slope = (jnp.roll(center, -1, 4) - jnp.roll(center, 1, 4)) * 0.5
    return jnp.stack([stream_slope, normal_slope, span_slope], axis=1)


def pair_block(pair_rows, table_modes, table_slopes, flat_modes):
    modes_count = table_modes.shape[0]
    cells = flat_modes.shape[2]
    group_size = pair_rows.shape[0]
    levels = lax.broadcasted_iota(jnp.int32, (group_size, modes_count), 1)
    first_pick = (pair_rows[:, 0:1] == levels).astype(jnp.float32)
    second_pick = (pair_rows[:, 1:2] == levels).astype(jnp.float32)
    first_modes = jnp.dot(
        first_pick, table_modes, precision=lax.Precision.HIGHEST, preferred_element_type=jnp.float32
    ).reshape(group_size, 3, cells)
    second_slopes = jnp.dot(
        second_pick,
        table_slopes,
        precision=lax.Precision.HIGHEST,
        preferred_element_type=jnp.float32,
    ).reshape(group_size, 3, 3, cells)
    convection = jnp.einsum(
        "bdl,bdcl->bcl", first_modes, second_slopes, precision=lax.Precision.HIGHEST
    )
    return jnp.einsum("bcl,kcl->bk", convection, flat_modes, precision=lax.Precision.HIGHEST)


def pair_terms(pair_source, flat_modes, flat_slopes, factor, row_count):
    modes_count = flat_modes.shape[0]
    table_modes = flat_modes.reshape(modes_count, -1)
    table_slopes = flat_slopes.reshape(modes_count, -1)
    group_size = math.gcd(row_count, 64)
    grouped = pair_source.reshape(row_count // group_size, group_size, 2)

    def one_group(group_rows):
        return pair_block(group_rows, table_modes, table_slopes, flat_modes)

    result = lax.map(one_group, grouped)
    return result.reshape(row_count, -1) * factor


def shards(snapshots, coeffs, pair_table):
    mode_field = jnp.einsum(
        "sk,scxyz->kcxyz",
        coeffs,
        lax.all_to_all(snapshots, "tm", split_axis=3, concat_axis=0, tiled=True),
        precision=lax.Precision.HIGHEST,
    )
    tm_count = lax.axis_size("tm")
    space_count = lax.axis_size("space")
    total_cells = (
        mode_field.shape[2] * mode_field.shape[3] * mode_field.shape[4] * tm_count * space_count
    )
    factor = float(total_cells) ** (-0.5)
    modes_count = mode_field.shape[0]
    padded_x = padded(mode_field, (("space", 2),), 1, True)
    padded_y = padded(mode_field, (("tm", 3),), 1, False)
    slopes = slope_field(mode_field, padded_x, padded_y)
    flat_modes = mode_field.reshape(modes_count, 3, -1)
    flat_slopes = slopes.reshape(modes_count, 3, 3, -1)
    share_rows = pair_table.shape[0] // (tm_count * space_count)
    tensor = lax.psum_scatter(
        pair_terms(
            pair_table, flat_modes, flat_slopes, factor, lax.axis_size(("tm", "space")) * share_rows
        ),
        ("tm", "space"),
        scatter_dimension=0,
        tiled=True,
    )
    return tensor


def solution(mesh):
    placed = (P("tm", None, "space", None, None), P(), P())
    return jax.shard_map(
        shards, mesh=mesh, in_specs=placed, out_specs=P(("tm", "space"), None), check_vma=False
    )
```

profile of v0, /device:TPU:0, one launch (start us, length us, event | category | flops | bytes accessed | tf_op | source)
XLA Modules:
  0.0 443.6 jit_solution(14245102003313045698)
XLA Ops:
  8.9 5.2 %all-to-all-start = ((f32[32,3,1,16,128]{4,0,1,2,3:T(8,128)}), f32[32,3,1,16,128]{4,0,1,2,3:T(8,128)S(1)}, u32[]{:S(2)}, u32[]{:S(2)}) async-start(f32[32,3,1,16,128]{4,0,1,2,3:T(8,128)} %copy.26), calls=%async_computation | async-start | bytes 1572864 | tf_op jit(solution)/shard_map/all_to_all | solution.py:71
  14.1 10.7 %all-to-all-done = f32[32,3,1,16,128]{4,0,1,2,3:T(8,128)S(1)} async-done(((f32[32,3,1,16,128]{4,0,1,2,3:T(8,128)}), f32[32,3,1,16,128]{4,0,1,2,3:T(8,128)S(1)}, u32[]{:S(2)}, u32[]{:S(2)}) %all-to-all-start) | async-done | bytes 786464 | tf_op jit(solution)/shard_map/all_to_all | solution.py:71
  30.3 5.2 %collective-permute-start.3 = (f32[128,3,1,1,128]{0,4,3,1,2:T(8,128)S(1)}, f32[128,3,1,1,128]{0,4,3,1,2:T(8,128)}, u32[]{:S(2)}, u32[]{:S(2)}) collective-permute-start(f32[128,3,1,1,128]{0,4,3,1,2:T(8,128)S(1)} %get-tuple-element.77), channel_id=1, source_target_pairs={{0,8},{8,16},{16,24},{1,9},{9,17},{17,25},{2,10},{10,18},{18,26},{... | collective-permute-start | bytes 589832 | tf_op jit(solution)/shard_map/ppermute | solution.py:16
  39.6 5.6 %collective-permute-done = f32[128,3,1,4,128]{0,4,3,1,2:T(8,128)S(1)} collective-permute-done((f32[128,3,1,4,128]{0,4,3,1,2:T(8,128)S(1)}, f32[128,3,1,4,128]{0,4,3,1,2:T(8,128)S(1)}, u32[]{:S(2)}, u32[]{:S(2)}) %collective-permute-start) | collective-permute-done | bytes 786464 | tf_op jit(solution)/shard_map/ppermute | solution.py:19
  45.2 3.0 collective-permute-done.1
  51.7 249.5 %while.10 = (s32[]{:T(128)}, f32[32,64,128]{2,1,0:T(8,128)}, s32[32,64,2]{1,0,2:T(8,128)S(1)}, f32[128,4608]{1,0:T(8,128)}, f32[128,1536]{1,0:T(8,128)}, /*index=5*/f32[128,3,512]{2,0,1:T(8,128)}, s32[]{:T(128)}) while((s32[]{:T(128)}, f32[32,64,128]{2,1,0:T(8,128)}, s32[32,64,2]{1,0,2:T(8,128)S(1)}, f32[128,4608]{1,0:T(8,128)}, ...), condition=%wide.region_1.2_spmd, body=%wide.region_0.1_spmd.sunk | while | flops 755482624 | bytes 14191725 | solution.py:63
  51.7 2.7 fusion.29
  59.5 2.7 fusion.29
  67.3 2.7 fusion.29
  75.1 2.7 fusion.29
  82.9 2.7 fusion.29
  90.7 2.7 fusion.29
  98.5 2.7 fusion.29
  106.3 2.7 fusion.29
  114.1 2.7 fusion.29
  121.9 2.7 fusion.29
  129.7 2.7 fusion.29
  137.5 2.7 fusion.29
  145.3 2.7 fusion.29
  153.1 2.7 fusion.29
  160.9 2.7 fusion.29
  168.7 2.7 fusion.29
  176.5 2.7 fusion.29
  184.3 2.7 fusion.29
  192.1 2.7 fusion.29
  207.7 2.7 fusion.29
  215.5 2.7 fusion.29
  254.5 2.7 fusion.29
  262.3 2.7 fusion.29
  277.9 2.7 fusion.29
  285.7 2.7 fusion.29
  303.6 133.1 %reduce-scatter.2.cloned.1.call-done = f32[64,128]{1,0:T(8,128)} async-done(((f32[2048,128]{1,0:T(8,128)}), f32[64,128]{1,0:T(8,128)}) %reduce-scatter.2.cloned.1.call-update) | async-done | bytes 32784 | tf_op jit(solution)/shard_map/reduce_scatter | solution.py:87
  (324 shorter events, 198.9 us)
Async XLA Ops:
  6.5 18.7 %copy-start = (f32[128,128]{1,0:T(8,128)S(1)}, f32[128,128]{1,0:T(8,128)}, u32[]{:S(2)}) copy-start(f32[128,128]{1,0:T(8,128)} %param.6) | copy-start | bytes 196612
  6.5 7.5 %copy-start.2 = (s32[2048,2]{0,1:T(2,128)S(1)}, s32[2048,2]{0,1:T(2,128)}, u32[]{:S(2)}) copy-start(s32[2048,2]{0,1:T(2,128)} %param.7) | copy-start | bytes 49156
  8.9 16.0 %all-to-all-start = ((f32[32,3,1,16,128]{4,0,1,2,3:T(8,128)}), f32[32,3,1,16,128]{4,0,1,2,3:T(8,128)S(1)}, u32[]{:S(2)}, u32[]{:S(2)}) async-start(f32[32,3,1,16,128]{4,0,1,2,3:T(8,128)} %copy.26), calls=%async_computation | async-start | bytes 1572864 | tf_op jit(solution)/shard_map/all_to_all | solution.py:71
  14.0 422.7 %reduce-scatter.2.cloned.1.call-start = ((), (), s32[]{:S(2)}) async-start(), calls=%async_computation.2 | async-start | bytes 1081344 | tf_op jit(solution)/shard_map/reduce_scatter | solution.py:87
  26.0 19.1 %collective-permute-start = (f32[128,3,1,4,128]{0,4,3,1,2:T(8,128)S(1)}, f32[128,3,1,4,128]{0,4,3,1,2:T(8,128)S(1)}, u32[]{:S(2)}, u32[]{:S(2)}) collective-permute-start(f32[128,3,1,4,128]{0,4,3,1,2:T(8,128)S(1)} %bitcast.74), channel_id=1, source_target_pairs={{1,0},{2,1},{3,2},{4,3},{5,4},{6,5},{7,6},{0,7},{9,8},{10,9},{11,1... | collective-permute-start | bytes 2359304 | tf_op jit(solution)/shard_map/ppermute | solution.py:19
  28.3 19.9 %collective-permute-start.1 = (f32[128,3,1,4,128]{0,4,3,1,2:T(8,128)S(1)}, f32[128,3,1,4,128]{0,4,3,1,2:T(8,128)}, u32[]{:S(2)}, u32[]{:S(2)}) collective-permute-start(f32[128,3,1,4,128]{0,4,3,1,2:T(8,128)S(1)} %bitcast.75), channel_id=1, source_target_pairs={{0,1},{1,2},{2,3},{3,4},{4,5},{5,6},{6,7},{7,0},{8,9},{9,10},{10,1... | collective-permute-start | bytes 2359304 | tf_op jit(solution)/shard_map/ppermute | solution.py:16
  29.1 9.1 %collective-permute-start.2 = (f32[128,3,1,1,128]{0,4,3,1,2:T(8,128)}, f32[128,3,1,1,128]{0,4,3,1,2:T(8,128)}, u32[]{:S(2)}, u32[]{:S(2)}) collective-permute-start(f32[128,3,1,1,128]{0,4,3,1,2:T(8,128)} %get-tuple-element.76), channel_id=1, source_target_pairs={{8,0},{16,8},{24,16},{9,1},{17,9},{25,17},{10,2},{18,10},{26,18},{... | collective-permute-start | bytes 589832 | tf_op jit(solution)/shard_map/ppermute | solution.py:19
  30.3 8.1 %collective-permute-start.3 = (f32[128,3,1,1,128]{0,4,3,1,2:T(8,128)S(1)}, f32[128,3,1,1,128]{0,4,3,1,2:T(8,128)}, u32[]{:S(2)}, u32[]{:S(2)}) collective-permute-start(f32[128,3,1,1,128]{0,4,3,1,2:T(8,128)S(1)} %get-tuple-element.77), channel_id=1, source_target_pairs={{0,8},{8,16},{16,24},{1,9},{9,17},{17,25},{2,10},{10,18},{18,26},{... | collective-permute-start | bytes 589832 | tf_op jit(solution)/shard_map/ppermute | solution.py:16
  55.3 2.6 copy-start.1
  63.1 2.6 copy-start.1
  86.5 2.6 copy-start.1
  94.3 2.6 copy-start.1
  117.7 2.6 copy-start.1
  125.5 2.6 copy-start.1
  133.3 2.6 copy-start.1
  141.1 2.6 copy-start.1
  148.9 2.6 copy-start.1
  156.7 2.6 copy-start.1
  164.5 2.6 copy-start.1
  172.3 2.6 copy-start.1
  187.9 2.6 copy-start.1
  195.7 2.6 copy-start.1
  211.3 2.6 copy-start.1
  219.1 2.6 copy-start.1
  226.9 2.6 copy-start.1
  234.7 2.6 copy-start.1
  242.5 2.6 copy-start.1
  250.3 2.6 copy-start.1
  265.8 2.6 copy-start.1
  273.7 2.6 copy-start.1
  281.5 2.6 copy-start.1
  289.3 2.6 copy-start.1
  (8 other events, 21.0 us)
Sparse Core Ops, SparseCore 0:
  303.7 132.9 reduce-scatter.1
where the time goes:
time: 446 us; the launch traced here: 444 us
  matrix products  188 us (42%)
  waiting for transfers between devices  153 us (34%)
  local copies, waits for them, and re-layouts  46.5 us (10%)
  other arithmetic  26.7 us (6%)
  starting transfers between devices  14 us (3%)
  between operations  13.5 us (3%)
    reduce_scatter x1, waiting for transfers between devices, shards(): lax.psum_scatter(pair_terms(pair_table, flat_modes, flat_slopes, factor,...  133 us
    dot_general x32, matrix products, pair_block(): jnp.dot(second_pick, table_slopes, precision=lax.Precision.HIGHEST, prefe...  85.1 us
    dot_general x32, matrix products, pair_block(): jnp.dot(first_pick, table_modes, precision=lax.Precision.HIGHEST, preferr...  52.5 us
    dot_general x32, matrix products, pair_block(): jnp.einsum('bcl,kcl->bk', convection, flat_modes, precision=lax.Precision...  50 us
    reshape x32, local copies, waits for them, and re-layouts, pair_block(): second_slopes = jnp.dot(second_pick, table_slopes, precision=lax.Precisio...  28.9 us
    while x32, other arithmetic  21.7 us
    all_to_all x1, waiting for transfers between devices, shards(): lax.all_to_all(snapshots, 'tm', split_axis=3, concat_axis=0, tiled=True)  10.7 us
    reshape x32, local copies, waits for them, and re-layouts, pair_block(): first_modes = jnp.dot(first_pick, table_modes, precision=lax.Precision.HI...  9.06 us
  transfers between devices with their start and end apart: 6, of which 5 were waited for; matrix products, arithmetic and copies ran while one was open for 1% of the time, Pallas kernels for 0%

commit v1 on v0

v1 whole, which is shorter than its diff:
```python
import functools

import jax
import jax.numpy as jnp
from jax import lax
from jax.experimental import pallas as pl
from jax.experimental.pallas import tpu as pltpu
from jax.sharding import PartitionSpec as P

F32 = jnp.float32
BF16 = jnp.bfloat16
VMEM_BYTES = 56 * 2**20


def split_high_low(values):
    high = values.astype(BF16)
    low = (values - high.astype(F32)).astype(BF16)
    return high, low


def pack_kernel(where_ref, field_ref, *out_refs, sizes):
    local_s, rows_y, block_rows, tm_count = sizes
    t = where_ref[0]
    for peer in range(tm_count):
        first_row = jnp.bitwise_xor(t, peer) * block_rows
        for row in range(block_rows + 2):
            y = first_row + row if row < block_rows else (first_row - 1 if row == block_rows else first_row + block_rows)
            inside = jnp.logical_and(y >= 0, y < rows_y)
            y = jnp.clip(y, 0, rows_y - 1)
            for c in range(3):
                slab = field_ref[pl.ds(c * rows_y + y, local_s, stride=3 * rows_y), :]
                if row >= block_rows:
                    slab = jnp.where(inside, slab, 0.0)
                out_refs[peer][row * 3 + c] = slab


def mode_weights(where_ref, coeffs_ref, local_s, tm_count):
    t = where_ref[0]
    ordered = jnp.concatenate(
        [
            coeffs_ref[pl.ds(pl.multiple_of(jnp.bitwise_xor(t, peer) * local_s, 8), local_s), :]
            for peer in range(tm_count)
        ],
        axis=0,
    )
    high, low = split_high_low(ordered.T)
    return jnp.concatenate([high, low, high, low], axis=1)


def modes_of(weights, slab):
    high, low = split_high_low(slab)
    return jnp.dot(weights, jnp.concatenate([high, high, low, low], axis=0), preferred_element_type=F32)


def store_projection(rhs_ref, place, mode_slab):
    high, low = split_high_low(mode_slab.T)
    modes = mode_slab.shape[0]
    lanes = mode_slab.shape[1]
    rhs_ref[place * lanes : (place + 1) * lanes, 0:modes] = high
    rhs_ref[place * lanes : (place + 1) * lanes, modes : 2 * modes] = low


def pair_position(where_ref, group, sizes):
    tm_count, chips, share = sizes
    t, chip, core = where_ref[0], where_ref[1], where_ref[2]
    peer, ahead = lax.div(group, chips), lax.rem(group, chips)
    to_t = jnp.bitwise_xor(t, peer)
    to_chip = lax.rem(chip + ahead, chips)
    return ((to_t * chips + to_chip) * 2 + core) * share


def project(conv_ref, lhs_ref, rhs_ref, block, places, lanes):
    for place in range(places):
        values = conv_ref[pl.ds(place, block, stride=places), :]
        high, low = split_high_low(values)
        lhs_ref[0:block, place * lanes : (place + 1) * lanes] = high
        lhs_ref[block : 2 * block, place * lanes : (place + 1) * lanes] = low
    both = jnp.dot(lhs_ref[...], rhs_ref[...], preferred_element_type=F32)
    modes = both.shape[1] // 2
    return (both[:block, :modes] + both[:block, modes:]) + (both[block:, :modes] + both[block:, modes:])


def main_kernel(
    where_ref, pairs_ref, coeffs_ref, *refs, sizes
):
    local_s, block_rows, tm_count, chips, share = sizes
    own, other = refs[:tm_count], refs[tm_count : 2 * tm_count]
    out_ref, next_ref = refs[2 * tm_count : 2 * tm_count + 2]
    field_ref, slab_ref, carry_ref, slope_ref, rhs_ref, conv_ref, lhs_ref = refs[2 * tm_count + 2 :]
    core = where_ref[2]
    modes, lanes = coeffs_ref.shape[1], own[0].shape[2]
    height = 2 * block_rows
    for peer in range(tm_count):
        rows = pl.ds(peer * local_s, local_s)
        field_ref[core, :, rows, :] = own[peer][...]
        field_ref[1 - core, :, rows, :] = other[peer][...]
    weights = mode_weights(where_ref, coeffs_ref, local_s, tm_count)

    def one_slab(index, _):
        both = jnp.concatenate([field_ref[0, index], field_ref[1, index]], axis=1)
        result = modes_of(weights, both)
        slab_ref[0, index] = result[:, :lanes]
        slab_ref[1, index] = result[:, lanes:]
        return 0

    lax.fori_loop(0, (block_rows + 2) * 3, one_slab, 0, unroll=2)
    for c in range(3):
        for row in range(block_rows):
            above = (row + 1 if row + 1 < block_rows else block_rows + 1) * 3 + c
            below = (row - 1 if row > 0 else block_rows) * 3 + c
            center = row * 3 + c
            for plane in range(2):
                place = plane * block_rows + row
                value = slab_ref[plane, center]
                other_plane = slab_ref[1 - plane, center]
                stream = other_plane * (0.5 if plane == 0 else -0.5)
                normal = (slab_ref[plane, above] - slab_ref[plane, below]) * 0.5
                span = (pltpu.roll(value, lanes - 1, 1) - pltpu.roll(value, 1, 1)) * 0.5
                carry_ref[pl.ds(c * height + place, modes, stride=3 * height), :] = value
                for d, slope in enumerate((stream, normal, span)):
                    slope_ref[pl.ds((d * 3 + c) * height + place, modes, stride=9 * height), :] = slope
                store_projection(rhs_ref, c * height + place, value)
                if plane == 1:
                    next_ref[row * 3 + c] = value
    block = conv_ref.shape[0] // (3 * height)

    def one_block(number, _):
        first = number * block

        def one_pair(q, _):
            position = pair_position(where_ref, lax.div(first + q, share), (tm_count, chips, share)) + lax.rem(
                first + q, share
            )
            i, j = pairs_ref[2 * position], pairs_ref[2 * position + 1]
            carry = carry_ref[pl.ds(pl.multiple_of(i * (3 * height), 8), 3 * height), :]
            slope = slope_ref[pl.ds(pl.multiple_of(j * (9 * height), 8), 9 * height), :]
            rows = [
                sum(
                    carry[d * height : (d + 1) * height] * slope[(d * 3 + c) * height : (d * 3 + c + 1) * height]
                    for d in range(3)
                )
                for c in range(3)
            ]
            conv_ref[pl.ds(pl.multiple_of(q * (3 * height), 8), 3 * height), :] = jnp.concatenate(rows, axis=0)
            return 0

        lax.fori_loop(0, block, one_pair, 0, unroll=8)
        out_ref[pl.ds(pl.multiple_of(first, 8), block), :] = project(
            conv_ref, lhs_ref, rhs_ref, block, 3 * height, lanes
        )
        return 0

    lax.fori_loop(0, out_ref.shape[0] // block, one_block, 0)


def edge_kernel(where_ref, pairs_ref, coeffs_ref, *refs, sizes):
    local_s, block_rows, tm_count, chips, share = sizes
    own_ref, other_ref, near_ref, partial_ref = refs[:4]
    out_ref = refs[4]
    field_ref, carry_ref, slope_ref, rhs_ref, conv_ref, lhs_ref = refs[5:]
    core = where_ref[2]
    modes, lanes = coeffs_ref.shape[1], own_ref.shape[3]
    height = 2 * block_rows
    half = tm_count // 2
    for place in range(half):
        field_ref[:, pl.ds(pl.multiple_of((core * half + place) * local_s, 8), local_s), :] = own_ref[place]
        field_ref[:, pl.ds(pl.multiple_of(((1 - core) * half + place) * local_s, 8), local_s), :] = other_ref[place]
    weights = mode_weights(where_ref, coeffs_ref, local_s, tm_count)
    for c in range(3):
        for row in range(block_rows):
            near = near_ref[row * 3 + c]
            far = modes_of(weights, field_ref[row * 3 + c])
            for place, value, across in ((row, near, far * 0.5), (block_rows + row, far, near * -0.5)):
                if c == 0:
                    carry_ref[pl.ds(place, modes, stride=height), :] = value
                slope_ref[pl.ds(c * height + place, modes, stride=3 * height), :] = across
                store_projection(rhs_ref, c * height + place, value)
    block = conv_ref.shape[0] // (3 * height)

    def one_block(number, _):
        first = number * block

        def one_pair(q, _):
            position = pair_position(where_ref, lax.div(first + q, share), (tm_count, chips, share)) + lax.rem(
                first + q, share
            )
            i, j = pairs_ref[2 * position], pairs_ref[2 * position + 1]
            carry = carry_ref[pl.ds(pl.multiple_of(i * height, 8), height), :]
            slope = slope_ref[pl.ds(pl.multiple_of(j * (3 * height), 8), 3 * height), :]
            rows = [carry * slope[c * height : (c + 1) * height] for c in range(3)]
            conv_ref[pl.ds(pl.multiple_of(q * (3 * height), 8), 3 * height), :] = jnp.concatenate(rows, axis=0)
            return 0

        lax.fori_loop(0, block, one_pair, 0, unroll=8)
        rows = pl.ds(pl.multiple_of(first, 8), block)
        out_ref[rows, :] = partial_ref[rows, :] + project(conv_ref, lhs_ref, rhs_ref, block, 3 * height, lanes)
        return 0

    lax.fori_loop(0, out_ref.shape[0] // block, one_block, 0)


def shards(snapshots, coeffs, pair_table):
    tm_count, space_count = lax.axis_size("tm"), lax.axis_size("space")
    chips = space_count // 2
    t, place = lax.axis_index("tm"), lax.axis_index("space")
    core = lax.rem(place, 2)
    where = jnp.stack([t, lax.div(place, 2), core]).astype(jnp.int32)
    local_s, _, _, rows_y, lanes = snapshots.shape
    block_rows = rows_y // tm_count
    modes = coeffs.shape[1]
    share = pair_table.shape[0] // (tm_count * space_count)
    count = tm_count * chips * share
    factor = float(space_count * rows_y * lanes) ** (-0.5)
    pairs = pair_table.reshape(-1)
    smem = pl.BlockSpec(memory_space=pltpu.SMEM)
    vmem = pl.BlockSpec(memory_space=pltpu.VMEM)
    params = pltpu.CompilerParams(vmem_limit_bytes=VMEM_BYTES)
    height = 2 * block_rows
    block = 128

    swap = [(2 * chip + c, 2 * chip + 1 - c) for chip in range(chips) for c in range(2)]

    def across(peer):
        return [(i, i ^ peer) for i in range(tm_count)]

    with jax.named_scope("pack"):
        packed = pl.pallas_call(
            functools.partial(pack_kernel, sizes=(local_s, rows_y, block_rows, tm_count)),
            out_shape=[jax.ShapeDtypeStruct(((block_rows + 2) * 3, local_s, lanes), F32)] * tm_count,
            in_specs=[smem, vmem],
            out_specs=[vmem] * tm_count,
            compiler_params=params,
        )(where, snapshots.reshape(-1, lanes))
    with jax.named_scope("to_rows"):
        own = [packed[0]] + [lax.ppermute(packed[peer], "tm", across(peer)) for peer in range(1, tm_count)]
    with jax.named_scope("to_next_chip"):
        half = tm_count // 2
        halves = [
            jnp.stack([piece[: block_rows * 3] for piece in own[c * half : (c + 1) * half]]) for c in range(2)
        ]
        ahead = [
            lax.ppermute(
                halves[c], "space", [(2 * ((chip + 1) % chips), 2 * chip + c) for chip in range(chips)]
            )
            for c in range(2)
        ]
        next_own = jnp.where(core == 0, ahead[0], ahead[1])
    with jax.named_scope("to_other_core"):
        other = [lax.ppermute(piece, "space", swap) for piece in own]
        next_other = lax.ppermute(next_own, "space", swap)
    with jax.named_scope("inner_terms"):
        sizes = (local_s, block_rows, tm_count, chips, share)
        snaps = local_s * tm_count
        partial, near = pl.pallas_call(
            functools.partial(main_kernel, sizes=sizes),
            out_shape=[
                jax.ShapeDtypeStruct((count, modes), F32),
                jax.ShapeDtypeStruct((block_rows * 3, modes, lanes), F32),
            ],
            in_specs=[smem, smem] + [vmem] * (1 + 2 * tm_count),
            out_specs=[vmem, vmem],
            scratch_shapes=[
                pltpu.VMEM((2, (block_rows + 2) * 3, snaps, lanes), F32),
                pltpu.VMEM((2, (block_rows + 2) * 3, modes, lanes), F32),
                pltpu.VMEM((modes * 3 * height, lanes), F32),
                pltpu.VMEM((modes * 9 * height, lanes), F32),
                pltpu.VMEM((3 * height * lanes, 2 * modes), BF16),
                pltpu.VMEM((block * 3 * height, lanes), F32),
                pltpu.VMEM((2 * block, 3 * height * lanes), BF16),
            ],
            compiler_params=params,
        )(where, pairs, coeffs, *own, *other)
    with jax.named_scope("edge_terms"):
        total = pl.pallas_call(
            functools.partial(edge_kernel, sizes=sizes),
            out_shape=jax.ShapeDtypeStruct((count, modes), F32),
            in_specs=[smem, smem] + [vmem] * 5,
            out_specs=vmem,
            scratch_shapes=[
                pltpu.VMEM((block_rows * 3, snaps, lanes), F32),
                pltpu.VMEM((modes * height, lanes), F32),
                pltpu.VMEM((modes * 3 * height, lanes), F32),
                pltpu.VMEM((3 * height * lanes, 2 * modes), BF16),
                pltpu.VMEM((block * 3 * height, lanes), F32),
                pltpu.VMEM((2 * block, 3 * height * lanes), BF16),
            ],
            compiler_params=params,
        )(where, pairs, coeffs, next_own, next_other, near, partial)
    with jax.named_scope("sum_over_rows"):
        blocks = total.reshape(tm_count, chips * share, modes)
        summed = blocks[0]
        for peer in range(1, tm_count):
            summed = summed + lax.ppermute(blocks[peer], "tm", across(peer))
    with jax.named_scope("sum_over_chips"):
        shares = summed.reshape(chips, share, modes)
        result = shares[0]
        for step in range(1, chips):
            shift = [
                (2 * chip + c, 2 * ((chip + step) % chips) + c) for chip in range(chips) for c in range(2)
            ]
            result = result + lax.ppermute(shares[step], "space", shift)
        return result * factor


def solution(mesh):
    placed = (P("tm", None, "space", None, None), P(), P())
    return jax.shard_map(
        shards, mesh=mesh, in_specs=placed, out_specs=P(("tm", "space"), None), check_vma=False
    )
```

time: 446 us -> 109 us (0.24)
  matrix products: 188 us -> 0 us
  waiting for transfers between devices: 153 us -> 30.2 us
  Pallas kernels: 0 us -> 49.8 us
  local copies, waits for them, and re-layouts: 46.5 us -> 4.27 us
  other arithmetic: 26.7 us -> 2.33 us
  between operations: 13.5 us -> 0.18 us
  starting transfers between devices: 14 us -> 21.5 us
    dot_general x96 -> x0, matrix products: 188 us -> none  [the longest x32 85.1 us: pair_block(): jnp.dot(second_pick, table_slopes, precision=lax.Precision.HIGHEST, prefe...]
    reduce_scatter x1 -> x0, waiting for transfers between devices: 133 us -> none  [shards(): lax.psum_scatter(pair_terms(pair_table, flat_modes, flat_slopes, factor,...]
    pallas_call x0 -> x3, Pallas kernels: none -> 49.8 us  [the longest x1 25.6 us: shards(): pl.pallas_call(functools.partial(main_kernel, sizes=sizes), out_shape=[ja...]
    reshape x66 -> x1, local copies, waits for them, and re-layouts: 38.3 us -> 1.07 us  [shards(): pairs = pair_table.reshape(-1)]
    while x32 -> x0, other arithmetic: 21.7 us -> none
    ppermute x4 -> x16, waiting for transfers between devices: 8.94 us -> 30.2 us  [the longest x3 12 us: shards(): lax.ppermute(packed[peer], 'tm', across(peer))]
    ppermute x4 -> x16, starting transfers between devices: 8.82 us -> 21.5 us  [the longest x2 7.7 us: shards(): lax.ppermute(halves[c], 'space', [(2 * ((chip + 1) % chips), 2 * chip + c...]
    all_to_all x1 -> x0, waiting for transfers between devices: 10.7 us -> none  [shards(): lax.all_to_all(snapshots, 'tm', split_axis=3, concat_axis=0, tiled=True)]
  transfers between devices with their start and end apart: 6 -> 16, of which waited for: 5 -> 12; matrix products, arithmetic and copies ran while one was open for 1% -> 2% of each run, Pallas kernels for 0% -> 24%
where the time goes in v1:
time: 109 us; the launch traced here: 108 us
  Pallas kernels  49.8 us (46%)
  waiting for transfers between devices  30.2 us (28%)
  starting transfers between devices  21.5 us (20%)
  local copies, waits for them, and re-layouts  4.27 us (4%)
  other arithmetic  2.33 us (2%)
    pallas_call x1, Pallas kernels, shards(): pl.pallas_call(functools.partial(main_kernel, sizes=sizes), out_shape=[ja...  25.6 us
    pallas_call x1, Pallas kernels, shards(): pl.pallas_call(functools.partial(edge_kernel, sizes=sizes), out_shape=jax...  21.4 us
    ppermute x3, waiting for transfers between devices, shards(): lax.ppermute(packed[peer], 'tm', across(peer))  12 us
    ppermute x2, starting transfers between devices, shards(): lax.ppermute(halves[c], 'space', [(2 * ((chip + 1) % chips), 2 * chip + c...  7.7 us
    ppermute x2, waiting for transfers between devices, shards(): lax.ppermute(halves[c], 'space', [(2 * ((chip + 1) % chips), 2 * chip + c...  7.28 us
    ppermute x3, waiting for transfers between devices, shards(): summed = summed + lax.ppermute(blocks[peer], 'tm', across(peer))  6.09 us
    ppermute x3, starting transfers between devices, shards(): result = result + lax.ppermute(shares[step], 'space', shift)  4.6 us
    ppermute x3, starting transfers between devices, shards(): lax.ppermute(packed[peer], 'tm', across(peer))  4.46 us
  transfers between devices with their start and end apart: 16, of which 12 were waited for; matrix products, arithmetic and copies ran while one was open for 2% of the time, Pallas kernels for 24%

profile of v1, /device:TPU:0, one launch (start us, length us, event | category | flops | bytes accessed | tf_op | source)
XLA Modules:
  0.0 108.3 jit_solution(13022013861704751185)
XLA Ops:
  0.0 0.6 pad_add_fusion.where_ref
  0.7 2.8 %pack.1 = (f32[18,32,128]{2,1,0:T(8,128)}, f32[18,32,128]{2,1,0:T(8,128)}, f32[18,32,128]{2,1,0:T(8,128)}, f32[18,32,128]{2,1,0:T(8,128)}) custom-call(s32[3]{0:T(128)} %pad_add_fusion.where_ref, f32[1536,128]{1,0:T(8,128)} %bitcast.12), custom_call_target="tpu_custom_call" | custom-call | tf_op jit(solution)/shard_map/pack/pallas_call | solution.py:227
  3.4 3.9 %collective-permute-start.3 = (f32[18,32,128]{2,1,0:T(8,128)}, f32[18,32,128]{2,1,0:T(8,128)S(1)}, u32[]{:S(2)}, u32[]{:S(2)}) collective-permute-start(f32[18,32,128]{2,1,0:T(8,128)} %get-tuple-element.14), channel_id=1, source_target_pairs={{0,24},{8,16},{16,8},{24,0},{1,25},{9,17},{17,9},{25,1},{2,26},{10... | collective-permute-start | bytes 884744 | tf_op jit(solution)/shard_map/to_rows/ppermute | solution.py:235
  7.3 0.5 collective-permute-start
  7.9 0.9 slice_bitcast_fusion.3
  8.9 6.6 %collective-permute-done.3.refs_3_ = f32[18,32,128]{2,1,0:T(8,128)S(1)} collective-permute-done((f32[18,32,128]{2,1,0:T(8,128)}, f32[18,32,128]{2,1,0:T(8,128)S(1)}, u32[]{:S(2)}, u32[]{:S(2)}) %collective-permute-start.3) | collective-permute-done | bytes 294944 | tf_op jit(solution)/shard_map/to_rows/ppermute | solution.py:235
  15.4 5.4 %collective-permute-done.2.refs_2_ = f32[18,32,128]{2,1,0:T(8,128)S(1)} collective-permute-done((f32[18,32,128]{2,1,0:T(8,128)}, f32[18,32,128]{2,1,0:T(8,128)S(1)}, u32[]{:S(2)}, u32[]{:S(2)}) %collective-permute-start.2) | collective-permute-done | bytes 294944 | tf_op jit(solution)/shard_map/to_rows/ppermute | solution.py:235
  20.9 5.3 %collective-permute-start.4 = (f32[2,12,32,128]{3,2,1,0:T(8,128)S(1)}, f32[2,12,32,128]{3,2,1,0:T(8,128)S(1)}, u32[]{:S(2)}, u32[]{:S(2)}) collective-permute-start(f32[2,12,32,128]{3,2,1,0:T(8,128)S(1)} %pad_maximum_fusion.1), channel_id=1, source_target_pairs={{2,1},{4,3},{6,5},{0,7},{10,9},{12,11},{14,13},{8,15},{18,17},{20,... | collective-permute-start | bytes 1179656 | tf_op jit(solution)/shard_map/to_next_chip/ppermute | solution.py:242
  26.4 2.4 %collective-permute-start.1 = (f32[2,12,32,128]{3,2,1,0:T(8,128)S(1)}, f32[2,12,32,128]{3,2,1,0:T(8,128)S(1)}, u32[]{:S(2)}, u32[]{:S(2)}) collective-permute-start(f32[2,12,32,128]{3,2,1,0:T(8,128)S(1)} %pad_maximum_fusion), channel_id=1, source_target_pairs={{2,0},{4,2},{6,4},{0,6},{10,8},{12,10},{14,12},{8,14},{18,16},{20,... | collective-permute-start | bytes 1179656 | tf_op jit(solution)/shard_map/to_next_chip/ppermute | solution.py:242
  28.8 2.8 %collective-permute-done.4 = f32[2,12,32,128]{3,2,1,0:T(8,128)S(1)} collective-permute-done((f32[2,12,32,128]{3,2,1,0:T(8,128)S(1)}, f32[2,12,32,128]{3,2,1,0:T(8,128)S(1)}, u32[]{:S(2)}, u32[]{:S(2)}) %collective-permute-start.4) | collective-permute-done | bytes 393248 | tf_op jit(solution)/shard_map/to_next_chip/ppermute | solution.py:242
  31.5 4.5 %collective-permute-done.1 = f32[2,12,32,128]{3,2,1,0:T(8,128)S(1)} collective-permute-done((f32[2,12,32,128]{3,2,1,0:T(8,128)S(1)}, f32[2,12,32,128]{3,2,1,0:T(8,128)S(1)}, u32[]{:S(2)}, u32[]{:S(2)}) %collective-permute-start.1) | collective-permute-done | bytes 393248 | tf_op jit(solution)/shard_map/to_next_chip/ppermute | solution.py:242
  36.2 0.5 collective-permute-start.6
  36.8 0.4 collective-permute-start.8
  37.3 0.4 copy.4
  37.7 1.1 reshape.24.pairs_ref
  38.9 0.4 collective-permute-done.8.refs_6_
  39.3 0.4 collective-permute-done.9.refs_7_
  39.7 25.6 %inner_terms.1 = (f32[1024,128]{1,0:T(8,128)}, f32[12,128,128]{2,1,0:T(8,128)}) custom-call(s32[3]{0:T(128)} %pad_add_fusion.where_ref, s32[4096]{0:T(1024)} %reshape.24.pairs_ref, f32[128,128]{1,0:T(8,128)} %coeffs_ref.3, f32[18,32,128]{2,1,0:T(8,128)} %get-tuple-element.11.refs_0_, f32[18,32,128]{2,1,0:T(8,128)} %copy-done.3, f32[18,32,128]{2,1,0:T(8,128)} %copy-done.4, ...), custom_call_target="tpu_custom_call" | custom-call | tf_op jit(solution)/shard_map/inner_terms/pallas_call | solution.py:254
  65.3 0.8 copy-done.5
  66.1 21.4 %edge_terms.1 = f32[1024,128]{1,0:T(8,128)} custom-call(s32[3]{0:T(128)} %pad_add_fusion.where_ref, s32[4096]{0:T(1024)} %reshape.24.pairs_ref, f32[128,128]{1,0:T(8,128)} %coeffs_ref.3, f32[2,12,32,128]{3,2,1,0:T(8,128)} %copy-done, f32[2,12,32,128]{3,2,1,0:T(8,128)} %copy-done.5, f32[12,128,128]{2,1,0:T(8,128)} %get-tuple-element.15.refs_2_, ...), custom_call_target="tpu_custom_call" | custom-call | tf_op jit(solution)/shard_map/edge_terms/pallas_call | solution.py:274
  87.5 1.1 fusion.5
  88.5 1.6 %collective-permute-start.10 = (f32[256,128]{1,0:T(8,128)S(1)}, f32[256,128]{1,0:T(8,128)S(1)}, u32[]{:S(2)}, u32[]{:S(2)}) collective-permute-start(f32[256,128]{1,0:T(8,128)S(1)} %get-tuple-element.17), channel_id=1, source_target_pairs={{0,8},{8,0},{16,24},{24,16},{1,9},{9,1},{17,25},{25,17},{2,10},{10... | collective-permute-start | bytes 393224 | tf_op jit(solution)/shard_map/sum_over_rows/ppermute | solution.py:293
  90.1 1.5 %collective-permute-start.11 = (f32[256,128]{1,0:T(8,128)S(1)}, f32[256,128]{1,0:T(8,128)S(1)}, u32[]{:S(2)}, u32[]{:S(2)}) collective-permute-start(f32[256,128]{1,0:T(8,128)S(1)} %get-tuple-element.19), channel_id=1, source_target_pairs={{0,16},{8,24},{16,0},{24,8},{1,17},{9,25},{17,1},{25,9},{2,18},{10... | collective-permute-start | bytes 393224 | tf_op jit(solution)/shard_map/sum_over_rows/ppermute | solution.py:293
  91.6 0.5 collective-permute-start.12
  92.1 2.4 %collective-permute-done.10 = f32[256,128]{1,0:T(8,128)S(1)} collective-permute-done((f32[256,128]{1,0:T(8,128)S(1)}, f32[256,128]{1,0:T(8,128)S(1)}, u32[]{:S(2)}, u32[]{:S(2)}) %collective-permute-start.10) | collective-permute-done | bytes 131104 | tf_op jit(solution)/shard_map/sum_over_rows/ppermute | solution.py:293
  94.5 3.6 %collective-permute-done.11 = f32[256,128]{1,0:T(8,128)S(1)} collective-permute-done((f32[256,128]{1,0:T(8,128)S(1)}, f32[256,128]{1,0:T(8,128)S(1)}, u32[]{:S(2)}, u32[]{:S(2)}) %collective-permute-start.11) | collective-permute-done | bytes 131104 | tf_op jit(solution)/shard_map/sum_over_rows/ppermute | solution.py:293
  98.2 0.9 fusion.1
  99.4 4.4 %collective-permute-start.14 = (f32[64,128]{1,0:T(8,128)S(1)}, f32[64,128]{1,0:T(8,128)S(1)}, u32[]{:S(2)}, u32[]{:S(2)}) collective-permute-start(f32[64,128]{1,0:T(8,128)S(1)} %get-tuple-element.22), channel_id=1, source_target_pairs={{0,4},{1,5},{2,6},{3,7},{4,0},{5,1},{6,2},{7,3},{8,12},{9,13},{10,... | collective-permute-start | bytes 98312 | tf_op jit(solution)/shard_map/sum_over_chips/ppermute | solution.py:301
  103.7 1.5 %collective-permute-done.13 = f32[64,128]{1,0:T(8,128)S(1)} collective-permute-done((f32[64,128]{1,0:T(8,128)S(1)}, f32[64,128]{1,0:T(8,128)S(1)}, u32[]{:S(2)}, u32[]{:S(2)}) %collective-permute-start.13) | collective-permute-done | bytes 32800 | tf_op jit(solution)/shard_map/sum_over_chips/ppermute | solution.py:301
  105.2 0.6 collective-permute-done.14
  105.9 1.8 %collective-permute-done.15 = f32[64,128]{1,0:T(8,128)S(1)} collective-permute-done((f32[64,128]{1,0:T(8,128)S(1)}, f32[64,128]{1,0:T(8,128)S(1)}, u32[]{:S(2)}, u32[]{:S(2)}) %collective-permute-start.15) | collective-permute-done | bytes 32800 | tf_op jit(solution)/shard_map/sum_over_chips/ppermute | solution.py:301
  107.7 0.6 fusion.4
  (33 shorter events, 0.8 us)
Async XLA Ops:
  3.4 12.0 %collective-permute-start.3 = (f32[18,32,128]{2,1,0:T(8,128)}, f32[18,32,128]{2,1,0:T(8,128)S(1)}, u32[]{:S(2)}, u32[]{:S(2)}) collective-permute-start(f32[18,32,128]{2,1,0:T(8,128)} %get-tuple-element.14), channel_id=1, source_target_pairs={{0,24},{8,16},{16,8},{24,0},{1,25},{9,17},{17,9},{25,1},{2,26},{10... | collective-permute-start | bytes 884744 | tf_op jit(solution)/shard_map/to_rows/ppermute | solution.py:235
  7.3 18.9 %collective-permute-start = (f32[18,32,128]{2,1,0:T(8,128)}, f32[18,32,128]{2,1,0:T(8,128)S(1)}, u32[]{:S(2)}, u32[]{:S(2)}) collective-permute-start(f32[18,32,128]{2,1,0:T(8,128)} %get-tuple-element.12), channel_id=1, source_target_pairs={{0,8},{8,0},{16,24},{24,16},{1,9},{9,1},{17,25},{25,17},{2,10},{10... | collective-permute-start | bytes 884744 | tf_op jit(solution)/shard_map/to_rows/ppermute | solution.py:235
  7.9 13.0 %collective-permute-start.2 = (f32[18,32,128]{2,1,0:T(8,128)}, f32[18,32,128]{2,1,0:T(8,128)S(1)}, u32[]{:S(2)}, u32[]{:S(2)}) collective-permute-start(f32[18,32,128]{2,1,0:T(8,128)} %get-tuple-element.13), channel_id=1, source_target_pairs={{0,16},{8,24},{16,0},{24,8},{1,17},{9,25},{17,1},{25,9},{2,18},{10... | collective-permute-start | bytes 884744 | tf_op jit(solution)/shard_map/to_rows/ppermute | solution.py:235
  15.4 21.8 %copy-start.2 = (f32[18,32,128]{2,1,0:T(8,128)}, f32[18,32,128]{2,1,0:T(8,128)S(1)}, u32[]{:S(2)}) copy-start(f32[18,32,128]{2,1,0:T(8,128)S(1)} %collective-permute-done.3.refs_3_) | copy-start | bytes 884740
  20.9 15.9 %copy-start.4 = (f32[18,32,128]{2,1,0:T(8,128)}, f32[18,32,128]{2,1,0:T(8,128)S(1)}, u32[]{:S(2)}) copy-start(f32[18,32,128]{2,1,0:T(8,128)S(1)} %collective-permute-done.2.refs_2_) | copy-start | bytes 884740
  20.9 10.6 %collective-permute-start.4 = (f32[2,12,32,128]{3,2,1,0:T(8,128)S(1)}, f32[2,12,32,128]{3,2,1,0:T(8,128)S(1)}, u32[]{:S(2)}, u32[]{:S(2)}) collective-permute-start(f32[2,12,32,128]{3,2,1,0:T(8,128)S(1)} %pad_maximum_fusion.1), channel_id=1, source_target_pairs={{2,1},{4,3},{6,5},{0,7},{10,9},{12,11},{14,13},{8,15},{18,17},{20,... | collective-permute-start | bytes 1179656 | tf_op jit(solution)/shard_map/to_next_chip/ppermute | solution.py:242
  26.3 10.4 %copy-start.3 = (f32[18,32,128]{2,1,0:T(8,128)}, f32[18,32,128]{2,1,0:T(8,128)S(1)}, u32[]{:S(2)}) copy-start(f32[18,32,128]{2,1,0:T(8,128)S(1)} %collective-permute-done.refs_1_) | copy-start | bytes 884740
  26.4 9.7 %collective-permute-start.1 = (f32[2,12,32,128]{3,2,1,0:T(8,128)S(1)}, f32[2,12,32,128]{3,2,1,0:T(8,128)S(1)}, u32[]{:S(2)}, u32[]{:S(2)}) collective-permute-start(f32[2,12,32,128]{3,2,1,0:T(8,128)S(1)} %pad_maximum_fusion), channel_id=1, source_target_pairs={{2,0},{4,2},{6,4},{0,6},{10,8},{12,10},{14,12},{8,14},{18,16},{20,... | collective-permute-start | bytes 1179656 | tf_op jit(solution)/shard_map/to_next_chip/ppermute | solution.py:242
  28.7 7.4 %copy-start.1 = (f32[18,32,128]{2,1,0:T(8,128)S(1)}, f32[18,32,128]{2,1,0:T(8,128)}, u32[]{:S(2)}) copy-start(f32[18,32,128]{2,1,0:T(8,128)} %get-tuple-element.11.refs_0_) | copy-start | bytes 884740
  28.7 8.5 %copy-start.7 = (s32[2048,2]{0,1:T(2,128)S(1)}, s32[2048,2]{0,1:T(2,128)}, u32[]{:S(2)}) copy-start(s32[2048,2]{0,1:T(2,128)} %param.5) | copy-start | bytes 49156
  36.1 1.6 %copy-start = (f32[2,12,32,128]{3,2,1,0:T(8,128)}, f32[2,12,32,128]{3,2,1,0:T(8,128)S(1)}, u32[]{:S(2)}) copy-start(f32[2,12,32,128]{3,2,1,0:T(8,128)S(1)} %broadcast_select_fusion.refs_0_) | copy-start | bytes 1179652
  36.1 29.2 %collective-permute-start.5 = (f32[2,12,32,128]{3,2,1,0:T(8,128)S(1)}, f32[2,12,32,128]{3,2,1,0:T(8,128)S(1)}, u32[]{:S(2)}, u32[]{:S(2)}) collective-permute-start(f32[2,12,32,128]{3,2,1,0:T(8,128)S(1)} %broadcast_select_fusion.refs_0_), channel_id=1, source_target_pairs={{0,1},{1,0},{2,3},{3,2},{4,5},{5,4},{6,7},{7,6},{8,9},{9,8},{10,11... | collective-permute-start | bytes 1179656 | tf_op jit(solution)/shard_map/to_other_core/ppermute | solution.py:250
  36.2 2.6 %collective-permute-start.6 = (f32[18,32,128]{2,1,0:T(8,128)S(1)}, f32[18,32,128]{2,1,0:T(8,128)S(1)}, u32[]{:S(2)}, u32[]{:S(2)}) collective-permute-start(f32[18,32,128]{2,1,0:T(8,128)S(1)} %copy-done.1), channel_id=1, source_target_pairs={{0,1},{1,0},{2,3},{3,2},{4,5},{5,4},{6,7},{7,6},{8,9},{9,8},{10,11... | collective-permute-start | bytes 884744 | tf_op jit(solution)/shard_map/to_other_core/ppermute | solution.py:249
  36.7 2.2 %collective-permute-start.7 = (f32[18,32,128]{2,1,0:T(8,128)S(1)}, f32[18,32,128]{2,1,0:T(8,128)}, u32[]{:S(2)}, u32[]{:S(2)}) collective-permute-start(f32[18,32,128]{2,1,0:T(8,128)S(1)} %collective-permute-done.refs_1_), channel_id=1, source_target_pairs={{0,1},{1,0},{2,3},{3,2},{4,5},{5,4},{6,7},{7,6},{8,9},{9,8},{10,11... | collective-permute-start | bytes 884744 | tf_op jit(solution)/shard_map/to_other_core/ppermute | solution.py:249
  36.8 2.5 %collective-permute-start.8 = (f32[18,32,128]{2,1,0:T(8,128)S(1)}, f32[18,32,128]{2,1,0:T(8,128)}, u32[]{:S(2)}, u32[]{:S(2)}) collective-permute-start(f32[18,32,128]{2,1,0:T(8,128)S(1)} %collective-permute-done.2.refs_2_), channel_id=1, source_target_pairs={{0,1},{1,0},{2,3},{3,2},{4,5},{5,4},{6,7},{7,6},{8,9},{9,8},{10,11... | collective-permute-start | bytes 884744 | tf_op jit(solution)/shard_map/to_other_core/ppermute | solution.py:249
  37.2 2.5 %collective-permute-start.9 = (f32[18,32,128]{2,1,0:T(8,128)S(1)}, f32[18,32,128]{2,1,0:T(8,128)}, u32[]{:S(2)}, u32[]{:S(2)}) collective-permute-start(f32[18,32,128]{2,1,0:T(8,128)S(1)} %collective-permute-done.3.refs_3_), channel_id=1, source_target_pairs={{0,1},{1,0},{2,3},{3,2},{4,5},{5,4},{6,7},{7,6},{8,9},{9,8},{10,11... | collective-permute-start | bytes 884744 | tf_op jit(solution)/shard_map/to_other_core/ppermute | solution.py:249
  38.7 1.0 copy-start.6
  65.3 0.8 copy-start.5
  88.5 6.0 %collective-permute-start.10 = (f32[256,128]{1,0:T(8,128)S(1)}, f32[256,128]{1,0:T(8,128)S(1)}, u32[]{:S(2)}, u32[]{:S(2)}) collective-permute-start(f32[256,128]{1,0:T(8,128)S(1)} %get-tuple-element.17), channel_id=1, source_target_pairs={{0,8},{8,0},{16,24},{24,16},{1,9},{9,1},{17,25},{25,17},{2,10},{10... | collective-permute-start | bytes 393224 | tf_op jit(solution)/shard_map/sum_over_rows/ppermute | solution.py:293
  90.1 8.1 %collective-permute-start.11 = (f32[256,128]{1,0:T(8,128)S(1)}, f32[256,128]{1,0:T(8,128)S(1)}, u32[]{:S(2)}, u32[]{:S(2)}) collective-permute-start(f32[256,128]{1,0:T(8,128)S(1)} %get-tuple-element.19), channel_id=1, source_target_pairs={{0,16},{8,24},{16,0},{24,8},{1,17},{9,25},{17,1},{25,9},{2,18},{10... | collective-permute-start | bytes 393224 | tf_op jit(solution)/shard_map/sum_over_rows/ppermute | solution.py:293
  91.6 6.6 %collective-permute-start.12 = (f32[256,128]{1,0:T(8,128)S(1)}, f32[256,128]{1,0:T(8,128)S(1)}, u32[]{:S(2)}, u32[]{:S(2)}) collective-permute-start(f32[256,128]{1,0:T(8,128)S(1)} %get-tuple-element.18), channel_id=1, source_target_pairs={{0,24},{8,16},{16,8},{24,0},{1,25},{9,17},{17,9},{25,1},{2,26},{10... | collective-permute-start | bytes 393224 | tf_op jit(solution)/shard_map/sum_over_rows/ppermute | solution.py:293
  99.1 6.1 %collective-permute-start.13 = (f32[64,128]{1,0:T(8,128)S(1)}, f32[64,128]{1,0:T(8,128)S(1)}, u32[]{:S(2)}, u32[]{:S(2)}) collective-permute-start(f32[64,128]{1,0:T(8,128)S(1)} %get-tuple-element.20), channel_id=1, source_target_pairs={{0,2},{1,3},{2,4},{3,5},{4,6},{5,7},{6,0},{7,1},{8,10},{9,11},{10,... | collective-permute-start | bytes 98312 | tf_op jit(solution)/shard_map/sum_over_chips/ppermute | solution.py:301
  99.4 6.5 %collective-permute-start.14 = (f32[64,128]{1,0:T(8,128)S(1)}, f32[64,128]{1,0:T(8,128)S(1)}, u32[]{:S(2)}, u32[]{:S(2)}) collective-permute-start(f32[64,128]{1,0:T(8,128)S(1)} %get-tuple-element.22), channel_id=1, source_target_pairs={{0,4},{1,5},{2,6},{3,7},{4,0},{5,1},{6,2},{7,3},{8,12},{9,13},{10,... | collective-permute-start | bytes 98312 | tf_op jit(solution)/shard_map/sum_over_chips/ppermute | solution.py:301
  103.7 3.9 %collective-permute-start.15 = (f32[64,128]{1,0:T(8,128)S(1)}, f32[64,128]{1,0:T(8,128)S(1)}, u32[]{:S(2)}, u32[]{:S(2)}) collective-permute-start(f32[64,128]{1,0:T(8,128)S(1)} %get-tuple-element.21), channel_id=1, source_target_pairs={{0,6},{1,7},{2,0},{3,1},{4,2},{5,3},{6,4},{7,5},{8,14},{9,15},{10,... | collective-permute-start | bytes 98312 | tf_op jit(solution)/shard_map/sum_over_chips/ppermute | solution.py:301

commit v2 on v1

--- a/solution.py
+++ b/solution.py
@@ -127,24 +127,26 @@
     def one_block(number, _):
         first = number * block
 
-        def one_pair(q, _):
-            position = pair_position(where_ref, lax.div(first + q, share), (tm_count, chips, share)) + lax.rem(
-                first + q, share
-            )
-            i, j = pairs_ref[2 * position], pairs_ref[2 * position + 1]
-            carry = carry_ref[pl.ds(pl.multiple_of(i * (3 * height), 8), 3 * height), :]
-            slope = slope_ref[pl.ds(pl.multiple_of(j * (9 * height), 8), 9 * height), :]
-            rows = [
-                sum(
-                    carry[d * height : (d + 1) * height] * slope[(d * 3 + c) * height : (d * 3 + c + 1) * height]
-                    for d in range(3)
-                )
-                for c in range(3)
-            ]
-            conv_ref[pl.ds(pl.multiple_of(q * (3 * height), 8), 3 * height), :] = jnp.concatenate(rows, axis=0)
-            return 0
-
-        lax.fori_loop(0, block, one_pair, 0, unroll=8)
+        for group in range(block // share):
+            base = pair_position(where_ref, number * (block // share) + group, (tm_count, chips, share))
+
+            def one_pair(q, _):
+                position = 2 * (base + q)
+                i, j = pairs_ref[position], pairs_ref[position + 1]
+                carry = carry_ref[pl.ds(pl.multiple_of(i * (3 * height), 8), 3 * height), :]
+                slope = slope_ref[pl.ds(pl.multiple_of(j * (9 * height), 8), 9 * height), :]
+                rows = [
+                    sum(
+                        carry[d * height : (d + 1) * height] * slope[(d * 3 + c) * height : (d * 3 + c + 1) * height]
+                        for d in range(3)
+                    )
+                    for c in range(3)
+                ]
+                target = pl.ds(pl.multiple_of((group * share + q) * (3 * height), 8), 3 * height)
+                conv_ref[target, :] = jnp.concatenate(rows, axis=0)
+                return 0
+
+            lax.fori_loop(0, share, one_pair, 0, unroll=16)
         out_ref[pl.ds(pl.multiple_of(first, 8), block), :] = project(
             conv_ref, lhs_ref, rhs_ref, block, 3 * height, lanes
         )
@@ -180,18 +182,20 @@
     def one_block(number, _):
         first = number * block
 
-        def one_pair(q, _):
-            position = pair_position(where_ref, lax.div(first + q, share), (tm_count, chips, share)) + lax.rem(
-                first + q, share
-            )
-            i, j = pairs_ref[2 * position], pairs_ref[2 * position + 1]
-            carry = carry_ref[pl.ds(pl.multiple_of(i * height, 8), height), :]
-            slope = slope_ref[pl.ds(pl.multiple_of(j * (3 * height), 8), 3 * height), :]
-            rows = [carry * slope[c * height : (c + 1) * height] for c in range(3)]
-            conv_ref[pl.ds(pl.multiple_of(q * (3 * height), 8), 3 * height), :] = jnp.concatenate(rows, axis=0)
-            return 0
-
-        lax.fori_loop(0, block, one_pair, 0, unroll=8)
+        for group in range(block // share):
+            base = pair_position(where_ref, number * (block // share) + group, (tm_count, chips, share))
+
+            def one_pair(q, _):
+                position = 2 * (base + q)
+                i, j = pairs_ref[position], pairs_ref[position + 1]
+                carry = carry_ref[pl.ds(pl.multiple_of(i * height, 8), height), :]
+                slope = slope_ref[pl.ds(pl.multiple_of(j * (3 * height), 8), 3 * height), :]
+                rows = [carry * slope[c * height : (c + 1) * height] for c in range(3)]
+                target = pl.ds(pl.multiple_of((group * share + q) * (3 * height), 8), 3 * height)
+                conv_ref[target, :] = jnp.concatenate(rows, axis=0)
+                return 0
+
+            lax.fori_loop(0, share, one_pair, 0, unroll=16)
         rows = pl.ds(pl.multiple_of(first, 8), block)
         out_ref[rows, :] = partial_ref[rows, :] + project(conv_ref, lhs_ref, rhs_ref, block, 3 * height, lanes)
         return 0
@@ -244,10 +248,8 @@
             )
             for c in range(2)
         ]
-        next_own = jnp.where(core == 0, ahead[0], ahead[1])
     with jax.named_scope("to_other_core"):
         other = [lax.ppermute(piece, "space", swap) for piece in own]
-        next_other = lax.ppermute(next_own, "space", swap)
     with jax.named_scope("inner_terms"):
         sizes = (local_s, block_rows, tm_count, chips, share)
         snaps = local_s * tm_count
@@ -269,7 +271,12 @@
                 pltpu.VMEM((2 * block, 3 * height * lanes), BF16),
             ],
             compiler_params=params,
+            cost_estimate=pl.CostEstimate(flops=30 * 10**9, bytes_accessed=10**7, transcendentals=0),
         )(where, pairs, coeffs, *own, *other)
+    with jax.named_scope("next_to_other_core"):
+        ahead, partial = lax.optimization_barrier((ahead, partial))
+        next_own = jnp.where(core == 0, ahead[0], ahead[1])
+        next_other = lax.ppermute(next_own, "space", swap)
     with jax.named_scope("edge_terms"):
         total = pl.pallas_call(
             functools.partial(edge_kernel, sizes=sizes),

time: 109 us -> 81.7 us (0.75)
  Pallas kernels: 49.8 us -> 31.1 us
  waiting for transfers between devices: 30.2 us -> 21 us
  local copies, waits for them, and re-layouts: 4.27 us -> 6.37 us
    pallas_call x1, Pallas kernels: 25.6 us -> 16.2 us  [shards(): pl.pallas_call(functools.partial(main_kernel, sizes=sizes), out_shape=[ja...]
    pallas_call x1, Pallas kernels: 21.4 us -> 12.2 us  [shards(): pl.pallas_call(functools.partial(edge_kernel, sizes=sizes), out_shape=jax...]
    ppermute x2, waiting for transfers between devices: 7.28 us -> 0.01 us  [shards(): lax.ppermute(halves[c], 'space', [(2 * ((chip + 1) % chips), 2 * chip + c...]
    unnamed x17 -> x21, local copies, waits for them, and re-layouts: 1.16 us -> 3.24 us
    ppermute x1, waiting for transfers between devices: 0.01 us -> 1.71 us  [shards(): next_other = lax.ppermute(next_own, 'space', swap)]
    ppermute x3, waiting for transfers between devices: 12 us -> 10.5 us  [shards(): lax.ppermute(packed[peer], 'tm', across(peer))]
    ppermute x3, waiting for transfers between devices: 3.91 us -> 2.64 us  [shards(): result = result + lax.ppermute(shares[step], 'space', shift)]
  transfers between devices with their start and end apart: 16 -> 16, of which waited for: 12 -> 8; matrix products, arithmetic and copies ran while one was open for 2% -> 3% of each run, Pallas kernels for 24% -> 20%
where the time goes in v2:
time: 81.7 us; the launch traced here: 81.4 us
  Pallas kernels  31.1 us (38%)
  waiting for transfers between devices  21 us (26%)
  starting transfers between devices  20.5 us (25%)
  local copies, waits for them, and re-layouts  6.37 us (8%)
  other arithmetic  2.3 us (3%)
    pallas_call x1, Pallas kernels, shards(): pl.pallas_call(functools.partial(main_kernel, sizes=sizes), out_shape=[ja...  16.2 us
    pallas_call x1, Pallas kernels, shards(): pl.pallas_call(functools.partial(edge_kernel, sizes=sizes), out_shape=jax...  12.2 us
    ppermute x3, waiting for transfers between devices, shards(): lax.ppermute(packed[peer], 'tm', across(peer))  10.5 us
    ppermute x2, starting transfers between devices, shards(): lax.ppermute(halves[c], 'space', [(2 * ((chip + 1) % chips), 2 * chip + c...  7.69 us
    ppermute x3, waiting for transfers between devices, shards(): summed = summed + lax.ppermute(blocks[peer], 'tm', across(peer))  6.08 us
    ppermute x3, starting transfers between devices, shards(): lax.ppermute(packed[peer], 'tm', across(peer))  4.46 us
    ppermute x3, starting transfers between devices, shards(): result = result + lax.ppermute(shares[step], 'space', shift)  4.04 us
    ppermute x3, starting transfers between devices, shards(): summed = summed + lax.ppermute(blocks[peer], 'tm', across(peer))  3.55 us
  transfers between devices with their start and end apart: 16, of which 8 were waited for; matrix products, arithmetic and copies ran while one was open for 3% of the time, Pallas kernels for 20%

profile of v2, /device:TPU:0, one launch (start us, length us, event | category | flops | bytes accessed | tf_op | source)
XLA Modules:
  0.0 81.4 jit_solution(13309850350678709085)
XLA Ops:
  0.0 0.6 pad_add_fusion.where_ref
  0.6 2.8 %pack.1 = (f32[18,32,128]{2,1,0:T(8,128)}, f32[18,32,128]{2,1,0:T(8,128)}, f32[18,32,128]{2,1,0:T(8,128)}, f32[18,32,128]{2,1,0:T(8,128)}) custom-call(s32[3]{0:T(128)} %pad_add_fusion.where_ref, f32[1536,128]{1,0:T(8,128)} %bitcast.12), custom_call_target="tpu_custom_call" | custom-call | tf_op jit(solution)/shard_map/pack/pallas_call | solution.py:231
  3.4 3.9 %collective-permute-start.3 = (f32[18,32,128]{2,1,0:T(8,128)}, f32[18,32,128]{2,1,0:T(8,128)S(1)}, u32[]{:S(2)}, u32[]{:S(2)}) collective-permute-start(f32[18,32,128]{2,1,0:T(8,128)} %get-tuple-element.17), channel_id=1, source_target_pairs={{0,24},{8,16},{16,8},{24,0},{1,25},{9,17},{17,9},{25,1},{2,26},{10... | collective-permute-start | bytes 884744 | tf_op jit(solution)/shard_map/to_rows/ppermute | solution.py:239
  7.3 0.5 collective-permute-start
  7.9 0.9 %slice_bitcast_fusion.3 = f32[1,12,32,128]{3,2,1,0:T(8,128)S(1)} fusion(f32[18,32,128]{2,1,0:T(8,128)} %get-tuple-element.14.refs_0_), kind=kLoop, calls=%fused_computation.5 | loop fusion | bytes 393216 | tf_op jit(solution)/shard_map/to_next_chip/stack | solution.py:243
  8.8 0.4 copy.4
  9.2 1.1 %reshape.24.pairs_ref = s32[4096]{0:T(1024)} reshape(s32[2048,2]{1,0:T(8,128)S(1)} %copy.4) | data formatting | bytes 32768 | tf_op jit(solution)/shard_map/reshape | solution.py:218
  10.3 5.1 %collective-permute-done.3.refs_3_ = f32[18,32,128]{2,1,0:T(8,128)S(1)} collective-permute-done((f32[18,32,128]{2,1,0:T(8,128)}, f32[18,32,128]{2,1,0:T(8,128)S(1)}, u32[]{:S(2)}, u32[]{:S(2)}) %collective-permute-start.3) | collective-permute-done | bytes 294944 | tf_op jit(solution)/shard_map/to_rows/ppermute | solution.py:239
  15.4 5.4 %collective-permute-done.2.refs_2_ = f32[18,32,128]{2,1,0:T(8,128)S(1)} collective-permute-done((f32[18,32,128]{2,1,0:T(8,128)}, f32[18,32,128]{2,1,0:T(8,128)S(1)}, u32[]{:S(2)}, u32[]{:S(2)}) %collective-permute-start.2) | collective-permute-done | bytes 294944 | tf_op jit(solution)/shard_map/to_rows/ppermute | solution.py:239
  20.9 5.3 %collective-permute-start.4 = (f32[2,12,32,128]{3,2,1,0:T(8,128)S(1)}, f32[2,12,32,128]{3,2,1,0:T(8,128)S(1)}, u32[]{:S(2)}, u32[]{:S(2)}) collective-permute-start(f32[2,12,32,128]{3,2,1,0:T(8,128)S(1)} %pad_maximum_fusion.1), channel_id=1, source_target_pairs={{2,1},{4,3},{6,5},{0,7},{10,9},{12,11},{14,13},{8,15},{18,17},{20,... | collective-permute-start | bytes 1179656 | tf_op jit(solution)/shard_map/to_next_chip/ppermute | solution.py:246
  26.3 0.5 collective-permute-start.8
  27.0 0.6 copy-done.3
  27.6 2.3 %collective-permute-start.1 = (f32[2,12,32,128]{3,2,1,0:T(8,128)S(1)}, f32[2,12,32,128]{3,2,1,0:T(8,128)S(1)}, u32[]{:S(2)}, u32[]{:S(2)}) collective-permute-start(f32[2,12,32,128]{3,2,1,0:T(8,128)S(1)} %pad_maximum_fusion), channel_id=1, source_target_pairs={{2,0},{4,2},{6,4},{0,6},{10,8},{12,10},{14,12},{8,14},{18,16},{20,... | collective-permute-start | bytes 1179656 | tf_op jit(solution)/shard_map/to_next_chip/ppermute | solution.py:246
  30.0 0.7 copy-done.9
  30.6 0.1 copy-done.7
  30.8 0.7 copy-done.8
  31.5 16.2 %inner_terms.1 = (f32[1024,128]{1,0:T(8,128)}, f32[12,128,128]{2,1,0:T(8,128)}) custom-call(s32[3]{0:T(128)} %pad_add_fusion.where_ref, s32[4096]{0:T(1024)} %reshape.24.pairs_ref, f32[128,128]{1,0:T(8,128)} %coeffs_ref.3, f32[18,32,128]{2,1,0:T(8,128)} %get-tuple-element.14.refs_0_, f32[18,32,128]{2,1,0:T(8,128)} %copy-done.3, f32[18,32,128]{2,1,0:T(8,128)} %copy-done.4, ...), custom_call_target="tpu_custom_call" | custom-call | flops 30000001024 | bytes 10000000 | tf_op jit(solution)/shard_map/inner_terms/pallas_call | solution.py:256
  47.9 1.7 %collective-permute-done.9.refs_1_ = f32[2,12,32,128]{3,2,1,0:T(8,128)S(1)} collective-permute-done((f32[2,12,32,128]{3,2,1,0:T(8,128)S(1)}, f32[2,12,32,128]{3,2,1,0:T(8,128)S(1)}, u32[]{:S(2)}, u32[]{:S(2)}) %collective-permute-start.9) | collective-permute-done | bytes 393248 | tf_op jit(solution)/shard_map/next_to_other_core/ppermute | solution.py:279
  49.6 0.8 copy-done.1
  50.3 12.2 %edge_terms.1 = f32[1024,128]{1,0:T(8,128)} custom-call(s32[3]{0:T(128)} %pad_add_fusion.where_ref, s32[4096]{0:T(1024)} %reshape.24.pairs_ref, f32[128,128]{1,0:T(8,128)} %coeffs_ref.3, f32[2,12,32,128]{3,2,1,0:T(8,128)} %copy-done, f32[2,12,32,128]{3,2,1,0:T(8,128)} %copy-done.1, f32[12,128,128]{2,1,0:T(8,128)} %get-tuple-element.21.refs_2_, ...), custom_call_target="tpu_custom_call" | custom-call | tf_op jit(solution)/shard_map/edge_terms/pallas_call | solution.py:281
  62.5 1.1 %fusion.5 = (f32[256,128]{1,0:T(8,128)S(1)}, f32[256,128]{1,0:T(8,128)S(1)}, f32[256,128]{1,0:T(8,128)S(1)}) fusion(f32[1024,128]{1,0:T(8,128)} %edge_terms.1), kind=kLoop, calls=%fused_computation.15 | loop fusion | bytes 786432 | tf_op jit(solution)/shard_map/sum_over_rows/slice | solution.py:300
  63.5 1.6 %collective-permute-start.10 = (f32[256,128]{1,0:T(8,128)S(1)}, f32[256,128]{1,0:T(8,128)S(1)}, u32[]{:S(2)}, u32[]{:S(2)}) collective-permute-start(f32[256,128]{1,0:T(8,128)S(1)} %get-tuple-element.23), channel_id=1, source_target_pairs={{0,8},{8,0},{16,24},{24,16},{1,9},{9,1},{17,25},{25,17},{2,10},{10... | collective-permute-start | bytes 393224 | tf_op jit(solution)/shard_map/sum_over_rows/ppermute | solution.py:300
  65.1 1.5 %collective-permute-start.11 = (f32[256,128]{1,0:T(8,128)S(1)}, f32[256,128]{1,0:T(8,128)S(1)}, u32[]{:S(2)}, u32[]{:S(2)}) collective-permute-start(f32[256,128]{1,0:T(8,128)S(1)} %get-tuple-element.25), channel_id=1, source_target_pairs={{0,16},{8,24},{16,0},{24,8},{1,17},{9,25},{17,1},{25,9},{2,18},{10... | collective-permute-start | bytes 393224 | tf_op jit(solution)/shard_map/sum_over_rows/ppermute | solution.py:300
  66.6 0.5 collective-permute-start.12
  67.1 2.4 %collective-permute-done.10 = f32[256,128]{1,0:T(8,128)S(1)} collective-permute-done((f32[256,128]{1,0:T(8,128)S(1)}, f32[256,128]{1,0:T(8,128)S(1)}, u32[]{:S(2)}, u32[]{:S(2)}) %collective-permute-start.10) | collective-permute-done | bytes 131104 | tf_op jit(solution)/shard_map/sum_over_rows/ppermute | solution.py:300
  69.5 3.7 %collective-permute-done.11 = f32[256,128]{1,0:T(8,128)S(1)} collective-permute-done((f32[256,128]{1,0:T(8,128)S(1)}, f32[256,128]{1,0:T(8,128)S(1)}, u32[]{:S(2)}, u32[]{:S(2)}) %collective-permute-start.11) | collective-permute-done | bytes 131104 | tf_op jit(solution)/shard_map/sum_over_rows/ppermute | solution.py:300
  73.2 0.9 %fusion.1 = f32[256,128]{1,0:T(8,128)S(1)} fusion(f32[256,128]{1,0:T(8,128)S(1)} %collective-permute-done.12, f32[256,128]{1,0:T(8,128)S(1)} %collective-permute-done.11, f32[256,128]{1,0:T(8,128)S(1)} %collective-permute-done.10, f32[1024,128]{1,0:T(8,128)} %edge_terms.1), kind=kLoop, calls=%fused_computation.9 | loop fusion | flops 98304 | bytes 655360 | tf_op jit(solution)/shard_map/sum_over_rows/add | solution.py:300
  74.1 1.6 %collective-permute-start.13 = (f32[64,128]{1,0:T(8,128)S(1)}, f32[64,128]{1,0:T(8,128)S(1)}, u32[]{:S(2)}, u32[]{:S(2)}) collective-permute-start(f32[64,128]{1,0:T(8,128)S(1)} %get-tuple-element.26), channel_id=1, source_target_pairs={{0,2},{1,3},{2,4},{3,5},{4,6},{5,7},{6,0},{7,1},{8,10},{9,11},{10,... | collective-permute-start | bytes 98312 | tf_op jit(solution)/shard_map/sum_over_chips/ppermute | solution.py:308
  75.7 2.4 %collective-permute-start.15 = (f32[64,128]{1,0:T(8,128)S(1)}, f32[64,128]{1,0:T(8,128)S(1)}, u32[]{:S(2)}, u32[]{:S(2)}) collective-permute-start(f32[64,128]{1,0:T(8,128)S(1)} %get-tuple-element.27), channel_id=1, source_target_pairs={{0,6},{1,7},{2,0},{3,1},{4,2},{5,3},{6,4},{7,5},{8,14},{9,15},{10,... | collective-permute-start | bytes 98312 | tf_op jit(solution)/shard_map/sum_over_chips/ppermute | solution.py:308
  78.2 1.7 %collective-permute-done.13 = f32[64,128]{1,0:T(8,128)S(1)} collective-permute-done((f32[64,128]{1,0:T(8,128)S(1)}, f32[64,128]{1,0:T(8,128)S(1)}, u32[]{:S(2)}, u32[]{:S(2)}) %collective-permute-start.13) | collective-permute-done | bytes 32800 | tf_op jit(solution)/shard_map/sum_over_chips/ppermute | solution.py:308
  79.9 0.8 collective-permute-done.14
  80.8 0.6 fusion.4
  (37 shorter events, 0.6 us)
Async XLA Ops:
  3.4 12.0 %collective-permute-start.3 = (f32[18,32,128]{2,1,0:T(8,128)}, f32[18,32,128]{2,1,0:T(8,128)S(1)}, u32[]{:S(2)}, u32[]{:S(2)}) collective-permute-start(f32[18,32,128]{2,1,0:T(8,128)} %get-tuple-element.17), channel_id=1, source_target_pairs={{0,24},{8,16},{16,8},{24,0},{1,25},{9,17},{17,9},{25,1},{2,26},{10... | collective-permute-start | bytes 884744 | tf_op jit(solution)/shard_map/to_rows/ppermute | solution.py:239
  7.3 19.5 %collective-permute-start = (f32[18,32,128]{2,1,0:T(8,128)}, f32[18,32,128]{2,1,0:T(8,128)S(1)}, u32[]{:S(2)}, u32[]{:S(2)}) collective-permute-start(f32[18,32,128]{2,1,0:T(8,128)} %get-tuple-element.15), channel_id=1, source_target_pairs={{0,8},{8,0},{16,24},{24,16},{1,9},{9,1},{17,25},{25,17},{2,10},{10... | collective-permute-start | bytes 884744 | tf_op jit(solution)/shard_map/to_rows/ppermute | solution.py:239
  7.8 13.0 %collective-permute-start.2 = (f32[18,32,128]{2,1,0:T(8,128)}, f32[18,32,128]{2,1,0:T(8,128)S(1)}, u32[]{:S(2)}, u32[]{:S(2)}) collective-permute-start(f32[18,32,128]{2,1,0:T(8,128)} %get-tuple-element.16), channel_id=1, source_target_pairs={{0,16},{8,24},{16,0},{24,8},{1,17},{9,25},{17,1},{25,9},{2,18},{10... | collective-permute-start | bytes 884744 | tf_op jit(solution)/shard_map/to_rows/ppermute | solution.py:239
  7.9 1.0 %copy-start.5 = (s32[2048,2]{0,1:T(2,128)S(1)}, s32[2048,2]{0,1:T(2,128)}, u32[]{:S(2)}) copy-start(s32[2048,2]{0,1:T(2,128)} %param.5) | copy-start | bytes 49156
  7.9 19.7 %collective-permute-start.5 = (f32[18,32,128]{2,1,0:T(8,128)}, f32[18,32,128]{2,1,0:T(8,128)S(1)}, u32[]{:S(2)}, u32[]{:S(2)}) collective-permute-start(f32[18,32,128]{2,1,0:T(8,128)} %get-tuple-element.14.refs_0_), channel_id=1, source_target_pairs={{0,1},{1,0},{2,3},{3,2},{4,5},{5,4},{6,7},{7,6},{8,9},{9,8},{10,11... | collective-permute-start | bytes 884744 | tf_op jit(solution)/shard_map/to_other_core/ppermute | solution.py:252
  15.4 10.9 %copy-start.2 = (f32[18,32,128]{2,1,0:T(8,128)}, f32[18,32,128]{2,1,0:T(8,128)S(1)}, u32[]{:S(2)}) copy-start(f32[18,32,128]{2,1,0:T(8,128)S(1)} %collective-permute-done.3.refs_3_) | copy-start | bytes 884740
  20.8 5.4 %copy-start.4 = (f32[18,32,128]{2,1,0:T(8,128)}, f32[18,32,128]{2,1,0:T(8,128)S(1)}, u32[]{:S(2)}) copy-start(f32[18,32,128]{2,1,0:T(8,128)S(1)} %collective-permute-done.2.refs_2_) | copy-start | bytes 884740
  20.9 26.8 %collective-permute-start.4 = (f32[2,12,32,128]{3,2,1,0:T(8,128)S(1)}, f32[2,12,32,128]{3,2,1,0:T(8,128)S(1)}, u32[]{:S(2)}, u32[]{:S(2)}) collective-permute-start(f32[2,12,32,128]{3,2,1,0:T(8,128)S(1)} %pad_maximum_fusion.1), channel_id=1, source_target_pairs={{2,1},{4,3},{6,5},{0,7},{10,9},{12,11},{14,13},{8,15},{18,17},{20,... | collective-permute-start | bytes 1179656 | tf_op jit(solution)/shard_map/to_next_chip/ppermute | solution.py:246
  26.2 3.7 %collective-permute-start.7 = (f32[18,32,128]{2,1,0:T(8,128)S(1)}, f32[18,32,128]{2,1,0:T(8,128)S(1)}, u32[]{:S(2)}, u32[]{:S(2)}) collective-permute-start(f32[18,32,128]{2,1,0:T(8,128)S(1)} %collective-permute-done.2.refs_2_), channel_id=1, source_target_pairs={{0,1},{1,0},{2,3},{3,2},{4,5},{5,4},{6,7},{7,6},{8,9},{9,8},{10,11... | collective-permute-start | bytes 884744 | tf_op jit(solution)/shard_map/to_other_core/ppermute | solution.py:252
  26.3 3.6 %collective-permute-start.8 = (f32[18,32,128]{2,1,0:T(8,128)S(1)}, f32[18,32,128]{2,1,0:T(8,128)S(1)}, u32[]{:S(2)}, u32[]{:S(2)}) collective-permute-start(f32[18,32,128]{2,1,0:T(8,128)S(1)} %collective-permute-done.3.refs_3_), channel_id=1, source_target_pairs={{0,1},{1,0},{2,3},{3,2},{4,5},{5,4},{6,7},{7,6},{8,9},{9,8},{10,11... | collective-permute-start | bytes 884744 | tf_op jit(solution)/shard_map/to_other_core/ppermute | solution.py:252
  26.8 0.7 copy-start.3
  26.8 3.1 %collective-permute-start.6 = (f32[18,32,128]{2,1,0:T(8,128)S(1)}, f32[18,32,128]{2,1,0:T(8,128)S(1)}, u32[]{:S(2)}, u32[]{:S(2)}) collective-permute-start(f32[18,32,128]{2,1,0:T(8,128)S(1)} %collective-permute-done.refs_1_), channel_id=1, source_target_pairs={{0,1},{1,0},{2,3},{3,2},{4,5},{5,4},{6,7},{7,6},{8,9},{9,8},{10,11... | collective-permute-start | bytes 884744 | tf_op jit(solution)/shard_map/to_other_core/ppermute | solution.py:252
  27.6 2.4 %copy-start.6 = (f32[18,32,128]{2,1,0:T(8,128)}, f32[18,32,128]{2,1,0:T(8,128)S(1)}, u32[]{:S(2)}) copy-start(f32[18,32,128]{2,1,0:T(8,128)S(1)} %collective-permute-done.5.refs_4_) | copy-start | bytes 884740
  27.6 20.1 %collective-permute-start.1 = (f32[2,12,32,128]{3,2,1,0:T(8,128)S(1)}, f32[2,12,32,128]{3,2,1,0:T(8,128)S(1)}, u32[]{:S(2)}, u32[]{:S(2)}) collective-permute-start(f32[2,12,32,128]{3,2,1,0:T(8,128)S(1)} %pad_maximum_fusion), channel_id=1, source_target_pairs={{2,0},{4,2},{6,4},{0,6},{10,8},{12,10},{14,12},{8,14},{18,16},{20,... | collective-permute-start | bytes 1179656 | tf_op jit(solution)/shard_map/to_next_chip/ppermute | solution.py:246
  29.9 0.7 copy-start.9
  29.9 0.8 %copy-start.7 = (f32[18,32,128]{2,1,0:T(8,128)}, f32[18,32,128]{2,1,0:T(8,128)S(1)}, u32[]{:S(2)}) copy-start(f32[18,32,128]{2,1,0:T(8,128)S(1)} %collective-permute-done.7.refs_6_) | copy-start | bytes 884740
  30.8 0.7 copy-start.8
  47.8 1.8 %copy-start = (f32[2,12,32,128]{3,2,1,0:T(8,128)}, f32[2,12,32,128]{3,2,1,0:T(8,128)S(1)}, u32[]{:S(2)}) copy-start(f32[2,12,32,128]{3,2,1,0:T(8,128)S(1)} %broadcast_select_fusion.refs_0_) | copy-start | bytes 1179652
  47.8 1.8 %collective-permute-start.9 = (f32[2,12,32,128]{3,2,1,0:T(8,128)S(1)}, f32[2,12,32,128]{3,2,1,0:T(8,128)S(1)}, u32[]{:S(2)}, u32[]{:S(2)}) collective-permute-start(f32[2,12,32,128]{3,2,1,0:T(8,128)S(1)} %broadcast_select_fusion.refs_0_), channel_id=1, source_target_pairs={{0,1},{1,0},{2,3},{3,2},{4,5},{5,4},{6,7},{7,6},{8,9},{9,8},{10,11... | collective-permute-start | bytes 1179656 | tf_op jit(solution)/shard_map/next_to_other_core/ppermute | solution.py:279
  49.6 0.8 copy-start.1
  63.5 6.0 %collective-permute-start.10 = (f32[256,128]{1,0:T(8,128)S(1)}, f32[256,128]{1,0:T(8,128)S(1)}, u32[]{:S(2)}, u32[]{:S(2)}) collective-permute-start(f32[256,128]{1,0:T(8,128)S(1)} %get-tuple-element.23), channel_id=1, source_target_pairs={{0,8},{8,0},{16,24},{24,16},{1,9},{9,1},{17,25},{25,17},{2,10},{10... | collective-permute-start | bytes 393224 | tf_op jit(solution)/shard_map/sum_over_rows/ppermute | solution.py:300
  65.1 8.1 %collective-permute-start.11 = (f32[256,128]{1,0:T(8,128)S(1)}, f32[256,128]{1,0:T(8,128)S(1)}, u32[]{:S(2)}, u32[]{:S(2)}) collective-permute-start(f32[256,128]{1,0:T(8,128)S(1)} %get-tuple-element.25), channel_id=1, source_target_pairs={{0,16},{8,24},{16,0},{24,8},{1,17},{9,25},{17,1},{25,9},{2,18},{10... | collective-permute-start | bytes 393224 | tf_op jit(solution)/shard_map/sum_over_rows/ppermute | solution.py:300
  66.6 6.6 %collective-permute-start.12 = (f32[256,128]{1,0:T(8,128)S(1)}, f32[256,128]{1,0:T(8,128)S(1)}, u32[]{:S(2)}, u32[]{:S(2)}) collective-permute-start(f32[256,128]{1,0:T(8,128)S(1)} %get-tuple-element.24), channel_id=1, source_target_pairs={{0,24},{8,16},{16,8},{24,0},{1,25},{9,17},{17,9},{25,1},{2,26},{10... | collective-permute-start | bytes 393224 | tf_op jit(solution)/shard_map/sum_over_rows/ppermute | solution.py:300
  74.1 5.8 %collective-permute-start.13 = (f32[64,128]{1,0:T(8,128)S(1)}, f32[64,128]{1,0:T(8,128)S(1)}, u32[]{:S(2)}, u32[]{:S(2)}) collective-permute-start(f32[64,128]{1,0:T(8,128)S(1)} %get-tuple-element.26), channel_id=1, source_target_pairs={{0,2},{1,3},{2,4},{3,5},{4,6},{5,7},{6,0},{7,1},{8,10},{9,11},{10,... | collective-permute-start | bytes 98312 | tf_op jit(solution)/shard_map/sum_over_chips/ppermute | solution.py:308
  75.7 5.0 %collective-permute-start.14 = (f32[64,128]{1,0:T(8,128)S(1)}, f32[64,128]{1,0:T(8,128)S(1)}, u32[]{:S(2)}, u32[]{:S(2)}) collective-permute-start(f32[64,128]{1,0:T(8,128)S(1)} %get-tuple-element.28), channel_id=1, source_target_pairs={{0,4},{1,5},{2,6},{3,7},{4,0},{5,1},{6,2},{7,3},{8,12},{9,13},{10,... | collective-permute-start | bytes 98312 | tf_op jit(solution)/shard_map/sum_over_chips/ppermute | solution.py:308
  75.7 5.1 %collective-permute-start.15 = (f32[64,128]{1,0:T(8,128)S(1)}, f32[64,128]{1,0:T(8,128)S(1)}, u32[]{:S(2)}, u32[]{:S(2)}) collective-permute-start(f32[64,128]{1,0:T(8,128)S(1)} %get-tuple-element.27), channel_id=1, source_target_pairs={{0,6},{1,7},{2,0},{3,1},{4,2},{5,3},{6,4},{7,5},{8,14},{9,15},{10,... | collective-permute-start | bytes 98312 | tf_op jit(solution)/shard_map/sum_over_chips/ppermute | solution.py:308

commit v3 on v2

v3 whole, which is shorter than its diff:
```python
import functools

import jax
import jax.numpy as jnp
from jax import lax
from jax.experimental import pallas as pl
from jax.experimental.pallas import tpu as pltpu
from jax.sharding import PartitionSpec as P

F32 = jnp.float32
BF16 = jnp.bfloat16
VMEM_BYTES = 56 * 2**20


def split_high_low(values):
    high = values.astype(BF16)
    low = (values - high.astype(F32)).astype(BF16)
    return high, low


def pack_kernel(where_ref, field_ref, *out_refs, sizes):
    local_s, rows_y, block_rows, tm_count = sizes
    t = where_ref[0]
    half_s = local_s // 2
    for peer in range(tm_count):
        first_row = jnp.bitwise_xor(t, peer) * block_rows
        for row in range(block_rows + 2):
            if row < block_rows:
                y = first_row + row
            else:
                y = first_row - 1 if row == block_rows else first_row + block_rows
                inside = jnp.logical_and(y >= 0, y < rows_y)
                y = jnp.clip(y, 0, rows_y - 1)
            for c in range(3):
                slab = field_ref[pl.ds(c * rows_y + y, local_s, stride=3 * rows_y), :]
                if row < block_rows:
                    for part in range(2):
                        out_refs[tm_count + part][peer, row * 3 + c] = slab[part * half_s : (part + 1) * half_s]
                else:
                    slab = jnp.where(inside, slab, 0.0)
                out_refs[peer][row * 3 + c] = slab


def mode_weights(where_ref, coeffs_ref, local_s, tm_count):
    t = where_ref[0]
    ordered = jnp.concatenate(
        [
            coeffs_ref[pl.ds(pl.multiple_of(jnp.bitwise_xor(t, peer) * local_s, 8), local_s), :]
            for peer in range(tm_count)
        ],
        axis=0,
    )
    high, low = split_high_low(ordered.T)
    return jnp.concatenate([high, low, high, low], axis=1)


def modes_of(weights, slab):
    high, low = split_high_low(slab)
    return jnp.dot(weights, jnp.concatenate([high, high, low, low], axis=0), preferred_element_type=F32)


def store_projection(rhs_ref, place, mode_slab):
    high, low = split_high_low(mode_slab.T)
    modes, lanes = mode_slab.shape
    rhs_ref[place * lanes : (place + 1) * lanes, 0:modes] = high
    rhs_ref[place * lanes : (place + 1) * lanes, modes : 2 * modes] = low


def project(conv_ref, lhs_ref, rhs_ref, block, places, pitch, lanes):
    for place in range(places):
        values = conv_ref[pl.ds(place, block, stride=pitch), :]
        high, low = split_high_low(values)
        lhs_ref[0:block, place * lanes : (place + 1) * lanes] = high
        lhs_ref[block : 2 * block, place * lanes : (place + 1) * lanes] = low
    both = jnp.dot(lhs_ref[...], rhs_ref[...], preferred_element_type=F32)
    modes = both.shape[1] // 2
    return (both[:block, :modes] + both[:block, modes:]) + (both[block:, :modes] + both[block:, modes:])


def round_up(count):
    return -(-count // 8) * 8


def terms_kernel(where_ref, pairs_ref, coeffs_ref, *refs, sizes):
    local_s, block_rows, tm_count, chips, share = sizes
    own, other = refs[:tm_count], refs[tm_count : 2 * tm_count]
    next_own, next_other = refs[2 * tm_count : 3 * tm_count], refs[3 * tm_count]
    out_refs = refs[3 * tm_count + 1 : 4 * tm_count + 1]
    slab_ref, far_ref, carry_ref, slope_ref, rhs_ref, conv_ref, lhs_ref = refs[4 * tm_count + 1 :]
    t, chip, core = where_ref[0], where_ref[1], where_ref[2]
    modes, lanes = coeffs_ref.shape[1], own[0].shape[2]
    height = 2 * block_rows
    inner = 3 * height
    pitch = inner + round_up(3 * block_rows)
    slope_pitch = 3 * inner + round_up(3 * block_rows)
    weights = mode_weights(where_ref, coeffs_ref, local_s, tm_count)

    def one_slab(index, _):
        own_slab = jnp.concatenate([piece[index] for piece in own], axis=0)
        other_slab = jnp.concatenate([piece[index] for piece in other], axis=0)
        is_first = core == 0
        both = jnp.concatenate(
            [jnp.where(is_first, own_slab, other_slab), jnp.where(is_first, other_slab, own_slab)], axis=1
        )
        result = modes_of(weights, both)
        slab_ref[0, index] = result[:, :lanes]
        slab_ref[1, index] = result[:, lanes:]
        return 0

    lax.fori_loop(0, (block_rows + 2) * 3, one_slab, 0, unroll=3)

    def one_far(index, _):
        slabs = []
        for slab in (2 * index, 2 * index + 1):
            halves = []
            for peer in range(tm_count):
                mine, theirs = next_own[peer][slab], next_other[peer, slab]
                halves += [jnp.where(core == 0, mine, theirs), jnp.where(core == 0, theirs, mine)]
            slabs.append(jnp.concatenate(halves, axis=0))
        result = modes_of(weights, jnp.concatenate(slabs, axis=1))
        far_ref[2 * index] = result[:, :lanes]
        far_ref[2 * index + 1] = result[:, lanes:]
        return 0

    lax.fori_loop(0, block_rows * 3 // 2, one_far, 0, unroll=3)
    for c in range(3):
        for row in range(block_rows):
            above = (row + 1 if row + 1 < block_rows else block_rows + 1) * 3 + c
            below = (row - 1 if row > 0 else block_rows) * 3 + c
            center = row * 3 + c
            first, second, far = slab_ref[0, center], slab_ref[1, center], far_ref[center]
            streams = (second * 0.5, (far - first) * 0.5)
            for plane, value in enumerate((first, second)):
                place = plane * block_rows + row
                normal = (slab_ref[plane, above] - slab_ref[plane, below]) * 0.5
                span = (pltpu.roll(value, lanes - 1, 1) - pltpu.roll(value, 1, 1)) * 0.5
                carry_ref[pl.ds(c * height + place, modes, stride=pitch), :] = value
                for d, slope in enumerate((streams[plane], normal, span)):
                    slope_ref[pl.ds((d * 3 + c) * height + place, modes, stride=slope_pitch), :] = slope
                store_projection(rhs_ref, c * height + place, value)
            if c == 0:
                for copy in range(3):
                    carry_ref[pl.ds(inner + copy * block_rows + row, modes, stride=pitch), :] = far
            slope_ref[pl.ds(3 * inner + c * block_rows + row, modes, stride=slope_pitch), :] = second * -0.5
            store_projection(rhs_ref, inner + c * block_rows + row, far)
    block = chips * share
    for peer in range(tm_count):
        to_t = jnp.bitwise_xor(t, peer)
        for ahead in range(chips):
            base = ((to_t * chips + lax.rem(chip + ahead, chips)) * 2 + core) * share

            def one_pair(q, _):
                position = 2 * (base + q)
                i, j = pairs_ref[position], pairs_ref[position + 1]
                carry = carry_ref[pl.ds(pl.multiple_of(i * pitch, 8), pitch), :]
                slope = slope_ref[pl.ds(pl.multiple_of(j * slope_pitch, 8), slope_pitch), :]
                rows = [
                    sum(
                        carry[d * height : (d + 1) * height] * slope[(d * 3 + c) * height : (d * 3 + c + 1) * height]
                        for d in range(3)
                    )
                    for c in range(3)
                ]
                rows.append(carry[inner:] * slope[3 * inner :])
                target = pl.ds(pl.multiple_of((ahead * share + q) * pitch, 8), pitch)
                conv_ref[target, :] = jnp.concatenate(rows, axis=0)
                return 0

            lax.fori_loop(0, share, one_pair, 0, unroll=16)
        out_refs[peer][...] = project(conv_ref, lhs_ref, rhs_ref, block, inner + 3 * block_rows, pitch, lanes)


def in_vmem(array):
    return pltpu.with_memory_space_constraint(array, pltpu.VMEM)


def shards(snapshots, coeffs, pair_table):
    tm_count, space_count = lax.axis_size("tm"), lax.axis_size("space")
    chips = space_count // 2
    t, place = lax.axis_index("tm"), lax.axis_index("space")
    core = lax.rem(place, 2)
    where = jnp.stack([t, lax.div(place, 2), core]).astype(jnp.int32)
    local_s, _, _, rows_y, lanes = snapshots.shape
    modes = coeffs.shape[1]
    block_rows = rows_y // tm_count
    share = pair_table.shape[0] // (tm_count * space_count)
    factor = float(space_count * rows_y * lanes) ** (-0.5)
    pairs = pair_table.reshape(-1)
    smem = pl.BlockSpec(memory_space=pltpu.SMEM)
    vmem = pl.BlockSpec(memory_space=pltpu.VMEM)
    params = pltpu.CompilerParams(vmem_limit_bytes=VMEM_BYTES)
    half_s = local_s // 2
    block = chips * share
    height = 2 * block_rows
    depth = 3 * height + 3 * block_rows
    pitch = 3 * height + round_up(3 * block_rows)
    slope_pitch = 9 * height + round_up(3 * block_rows)

    swap = [(2 * chip + c, 2 * chip + 1 - c) for chip in range(chips) for c in range(2)]

    def across(peer):
        return [(i, i ^ peer) for i in range(tm_count)]

    with jax.named_scope("pack"):
        packed = pl.pallas_call(
            functools.partial(pack_kernel, sizes=(local_s, rows_y, block_rows, tm_count)),
            out_shape=[jax.ShapeDtypeStruct(((block_rows + 2) * 3, local_s, lanes), F32)] * tm_count
            + [jax.ShapeDtypeStruct((tm_count, block_rows * 3, half_s, lanes), F32)] * 2,
            in_specs=[smem, vmem],
            out_specs=[vmem] * (tm_count + 2),
            compiler_params=params,
        )(where, snapshots.reshape(-1, lanes))
    with jax.named_scope("to_chip_before"):
        ahead = [
            lax.ppermute(
                packed[tm_count + c], "space", [(2 * ((chip + 1) % chips), 2 * chip + c) for chip in range(chips)]
            )
            for c in range(2)
        ]
    with jax.named_scope("to_rows"):
        own = [packed[0]] + [lax.ppermute(packed[peer], "tm", across(peer)) for peer in range(1, tm_count)]
    with jax.named_scope("to_other_core"):
        other = [lax.ppermute(piece, "space", swap) for piece in own]
    with jax.named_scope("next_to_rows"):
        ahead, own = lax.optimization_barrier((ahead, own))
        parts = [jnp.where(core == 0, ahead[0][peer], ahead[1][peer]) for peer in range(tm_count)]
        next_own = [parts[0]] + [lax.ppermute(parts[peer], "tm", across(peer)) for peer in range(1, tm_count)]
    with jax.named_scope("next_to_other_core"):
        next_other = lax.ppermute(jnp.stack(next_own), "space", swap)
    with jax.named_scope("terms"):
        blocks = pl.pallas_call(
            functools.partial(terms_kernel, sizes=(local_s, block_rows, tm_count, chips, share)),
            out_shape=[jax.ShapeDtypeStruct((block, modes), F32)] * tm_count,
            in_specs=[smem, smem] + [vmem] * (3 * tm_count + 2),
            out_specs=[vmem] * tm_count,
            scratch_shapes=[
                pltpu.VMEM((2, (block_rows + 2) * 3, modes, lanes), F32),
                pltpu.VMEM((block_rows * 3, modes, lanes), F32),
                pltpu.VMEM((modes * pitch, lanes), F32),
                pltpu.VMEM((modes * slope_pitch, lanes), F32),
                pltpu.VMEM((depth * lanes, 2 * modes), BF16),
                pltpu.VMEM((block * pitch, lanes), F32),
                pltpu.VMEM((2 * block, depth * lanes), BF16),
            ],
            compiler_params=params,
        )(where, pairs, coeffs, *[in_vmem(piece) for piece in (*own, *other, *next_own, next_other)])
    with jax.named_scope("sum_over_rows"):
        summed = blocks[0]
        for peer in range(1, tm_count):
            summed = summed + lax.ppermute(blocks[peer], "tm", across(peer))
    with jax.named_scope("sum_over_chips"):
        shares = summed.reshape(chips, share, modes)
        result = shares[0]
        for step in range(1, chips):
            shift = [
                (2 * chip + c, 2 * ((chip + step) % chips) + c) for chip in range(chips) for c in range(2)
            ]
            result = result + lax.ppermute(shares[step], "space", shift)
        return result * factor


def solution(mesh):
    placed = (P("tm", None, "space", None, None), P(), P())
    return jax.shard_map(
        shards, mesh=mesh, in_specs=placed, out_specs=P(("tm", "space"), None), check_vma=False
    )
```

time: 81.7 us -> 78.4 us (0.960)
  Pallas kernels: 31.1 us -> 23.8 us
  starting transfers between devices: 20.5 us -> 24.2 us
  waiting for transfers between devices: 21 us -> 23.3 us
  local copies, waits for them, and re-layouts: 6.37 us -> 4.52 us
    pallas_call x2 -> x1, Pallas kernels: 28.3 us -> 20.8 us  [shards(): pl.pallas_call(functools.partial(terms_kernel, sizes=(local_s, block_rows...]
    ppermute x3 -> x6, starting transfers between devices: 7.76 us -> 11.9 us  [the longest x2 8.26 us: shards(): lax.ppermute(packed[tm_count + c], 'space', [(2 * ((chip + 1) % chips), 2...]
    ppermute x3 -> x6, waiting for transfers between devices: 1.71 us -> 3.65 us  [the longest x3 3.64 us: shards(): lax.ppermute(parts[peer], 'tm', across(peer))]
    ppermute x3, waiting for transfers between devices: 2.64 us -> 4.44 us  [shards(): result = result + lax.ppermute(shares[step], 'space', shift)]
    ppermute x3, waiting for transfers between devices: 10.5 us -> 9.31 us  [shards(): lax.ppermute(packed[peer], 'tm', across(peer))]
    reshape x1, local copies, waits for them, and re-layouts: 1.08 us -> 2.29 us  [shards(): pairs = pair_table.reshape(-1)]
    slice x1 -> x0, local copies, waits for them, and re-layouts: 1.06 us -> none  [shards(): summed = summed + lax.ppermute(blocks[peer], 'tm', across(peer))]
    unnamed x21 -> x5, local copies, waits for them, and re-layouts: 3.24 us -> 2.22 us
  transfers between devices with their start and end apart: 16 -> 19, of which waited for: 8 -> 9; matrix products, arithmetic and copies ran while one was open for 3% -> 5% of each run, Pallas kernels for 20% -> 0%
where the time goes in v3:
time: 78.4 us; the launch traced here: 78.1 us
  starting transfers between devices  24.2 us (31%)
  Pallas kernels  23.8 us (30%)
  waiting for transfers between devices  23.3 us (30%)
  local copies, waits for them, and re-layouts  4.52 us (6%)
  other arithmetic  2.25 us (3%)
    pallas_call x1, Pallas kernels, shards(): pl.pallas_call(functools.partial(terms_kernel, sizes=(local_s, block_rows...  20.8 us
    ppermute x3, waiting for transfers between devices, shards(): lax.ppermute(packed[peer], 'tm', across(peer))  9.31 us
    ppermute x2, starting transfers between devices, shards(): lax.ppermute(packed[tm_count + c], 'space', [(2 * ((chip + 1) % chips), 2...  8.26 us
    ppermute x3, waiting for transfers between devices, shards(): summed = summed + lax.ppermute(blocks[peer], 'tm', across(peer))  5.87 us
    ppermute x3, waiting for transfers between devices, shards(): result = result + lax.ppermute(shares[step], 'space', shift)  4.44 us
    ppermute x3, starting transfers between devices, shards(): result = result + lax.ppermute(shares[step], 'space', shift)  4.25 us
    ppermute x3, waiting for transfers between devices, shards(): lax.ppermute(parts[peer], 'tm', across(peer))  3.64 us
    ppermute x3, starting transfers between devices, shards(): lax.ppermute(parts[peer], 'tm', across(peer))  3.55 us
  transfers between devices with their start and end apart: 19, of which 9 were waited for; matrix products, arithmetic and copies ran while one was open for 5% of the time, Pallas kernels for 0%

profile of v3, /device:TPU:0, one launch (start us, length us, event | category | flops | bytes accessed | tf_op | source)
XLA Modules:
  0.0 78.1 jit_solution(13138280226615309871)
XLA Ops:
  0.0 0.6 pad_add_fusion.where_ref
  0.6 2.9 %pack.1 = (f32[18,32,128]{2,1,0:T(8,128)}, f32[18,32,128]{2,1,0:T(8,128)}, f32[18,32,128]{2,1,0:T(8,128)}, f32[18,32,128]{2,1,0:T(8,128)}, f32[4,12,16,128]{3,2,1,0:T(8,128)}, /*index=5*/f32[4,12,16,128]{3,2,1,0:T(8,128)}) custom-call(s32[3]{0:T(128)} %pad_add_fusion.where_ref, f32[1536,128]{1,0:T(8,128)} %bitcast.18), custom_call_target="tpu_custom_call" | custom-call | tf_op jit(solution)/shard_map/pack/pallas_call | solution.py:205
  3.5 6.9 %collective-permute-start = (f32[4,12,16,128]{3,2,1,0:T(8,128)}, f32[4,12,16,128]{3,2,1,0:T(8,128)S(1)}, u32[]{:S(2)}, u32[]{:S(2)}) collective-permute-start(f32[4,12,16,128]{3,2,1,0:T(8,128)} %get-tuple-element.21), channel_id=1, source_target_pairs={{2,0},{4,2},{6,4},{0,6},{10,8},{12,10},{14,12},{8,14},{18,16},{20,... | collective-permute-start | bytes 1179656 | tf_op jit(solution)/shard_map/to_chip_before/ppermute | solution.py:215
  10.5 1.3 %collective-permute-start.1 = (f32[4,12,16,128]{3,2,1,0:T(8,128)}, f32[4,12,16,128]{3,2,1,0:T(8,128)S(1)}, u32[]{:S(2)}, u32[]{:S(2)}) collective-permute-start(f32[4,12,16,128]{3,2,1,0:T(8,128)} %get-tuple-element.22), channel_id=1, source_target_pairs={{2,1},{4,3},{6,5},{0,7},{10,9},{12,11},{14,13},{8,15},{18,17},{20,... | collective-permute-start | bytes 1179656 | tf_op jit(solution)/shard_map/to_chip_before/ppermute | solution.py:215
  11.8 1.6 %collective-permute-start.2 = (f32[18,32,128]{2,1,0:T(8,128)}, f32[18,32,128]{2,1,0:T(8,128)S(1)}, u32[]{:S(2)}, u32[]{:S(2)}) collective-permute-start(f32[18,32,128]{2,1,0:T(8,128)} %get-tuple-element.24), channel_id=1, source_target_pairs={{0,8},{8,0},{16,24},{24,16},{1,9},{9,1},{17,25},{25,17},{2,10},{10... | collective-permute-start | bytes 884744 | tf_op jit(solution)/shard_map/to_rows/ppermute | solution.py:221
  13.4 1.5 %collective-permute-start.3 = (f32[18,32,128]{2,1,0:T(8,128)}, f32[18,32,128]{2,1,0:T(8,128)S(1)}, u32[]{:S(2)}, u32[]{:S(2)}) collective-permute-start(f32[18,32,128]{2,1,0:T(8,128)} %get-tuple-element.25), channel_id=1, source_target_pairs={{0,16},{8,24},{16,0},{24,8},{1,17},{9,25},{17,1},{25,9},{2,18},{10... | collective-permute-start | bytes 884744 | tf_op jit(solution)/shard_map/to_rows/ppermute | solution.py:221
  14.9 0.5 collective-permute-start.4
  15.3 3.6 %collective-permute-done.2.refs_1_ = f32[18,32,128]{2,1,0:T(8,128)S(1)} collective-permute-done((f32[18,32,128]{2,1,0:T(8,128)}, f32[18,32,128]{2,1,0:T(8,128)S(1)}, u32[]{:S(2)}, u32[]{:S(2)}) %collective-permute-start.2) | collective-permute-done | bytes 294944 | tf_op jit(solution)/shard_map/to_rows/ppermute | solution.py:221
  18.9 5.7 %collective-permute-done.3.refs_2_ = f32[18,32,128]{2,1,0:T(8,128)S(1)} collective-permute-done((f32[18,32,128]{2,1,0:T(8,128)}, f32[18,32,128]{2,1,0:T(8,128)S(1)}, u32[]{:S(2)}, u32[]{:S(2)}) %collective-permute-start.3) | collective-permute-done | bytes 294944 | tf_op jit(solution)/shard_map/to_rows/ppermute | solution.py:221
  24.7 0.5 collective-permute-start.11
  25.2 1.6 %collective-permute-start.10 = (f32[12,16,128]{2,1,0:T(8,128)S(1)}, f32[12,16,128]{2,1,0:T(8,128)S(1)}, u32[]{:S(2)}, u32[]{:S(2)}) collective-permute-start(f32[12,16,128]{2,1,0:T(8,128)S(1)} %get-tuple-element.38), channel_id=1, source_target_pairs={{0,16},{8,24},{16,0},{24,8},{1,17},{9,25},{17,1},{25,9},{2,18},{10... | collective-permute-start | bytes 294920 | tf_op jit(solution)/shard_map/next_to_rows/ppermute | solution.py:227
  26.9 1.4 %collective-permute-start.9 = (f32[12,16,128]{2,1,0:T(8,128)S(1)}, f32[12,16,128]{2,1,0:T(8,128)S(1)}, u32[]{:S(2)}, u32[]{:S(2)}) collective-permute-start(f32[12,16,128]{2,1,0:T(8,128)S(1)} %get-tuple-element.39), channel_id=1, source_target_pairs={{0,8},{8,0},{16,24},{24,16},{1,9},{9,1},{17,25},{25,17},{2,10},{10... | collective-permute-start | bytes 294920 | tf_op jit(solution)/shard_map/next_to_rows/ppermute | solution.py:227
  28.3 2.1 %collective-permute-done.11.refs_11_ = f32[12,16,128]{2,1,0:T(8,128)S(1)} collective-permute-done((f32[12,16,128]{2,1,0:T(8,128)S(1)}, f32[12,16,128]{2,1,0:T(8,128)S(1)}, u32[]{:S(2)}, u32[]{:S(2)}) %collective-permute-start.11) | collective-permute-done | bytes 98336 | tf_op jit(solution)/shard_map/next_to_rows/ppermute | solution.py:227
  30.4 0.5 collective-permute-done.10.refs_10_
  30.9 1.0 %collective-permute-done.9.refs_9_ = f32[12,16,128]{2,1,0:T(8,128)S(1)} collective-permute-done((f32[12,16,128]{2,1,0:T(8,128)S(1)}, f32[12,16,128]{2,1,0:T(8,128)S(1)}, u32[]{:S(2)}, u32[]{:S(2)}) %collective-permute-start.9) | collective-permute-done | bytes 98336 | tf_op jit(solution)/shard_map/next_to_rows/ppermute | solution.py:227
  32.0 0.8 %copy-done = f32[18,32,128]{2,1,0:T(8,128)S(1)} copy-done((f32[18,32,128]{2,1,0:T(8,128)S(1)}, f32[18,32,128]{2,1,0:T(8,128)}, u32[]{:S(2)}) %copy-start) | copy-done | bytes 294936
  32.9 0.5 collective-permute-start.6
  33.4 0.5 collective-permute-start.8
  33.9 1.4 %copy.4 = s32[2048,2]{1,0:T(8,128)} copy(s32[2048,2]{0,1:T(2,128)S(1)} %copy-done.1) | data formatting | bytes 32768 | tf_op args[2]
  35.3 2.3 %reshape.23.pairs_ref = s32[4096]{0:T(1024)} reshape(s32[2048,2]{1,0:T(8,128)} %copy.4) | data formatting | bytes 32768 | tf_op jit(solution)/shard_map/reshape | solution.py:188
  37.6 20.8 %terms.1 = (f32[256,128]{1,0:T(8,128)}, f32[256,128]{1,0:T(8,128)}, f32[256,128]{1,0:T(8,128)}, f32[256,128]{1,0:T(8,128)}) custom-call(s32[3]{0:T(128)} %pad_add_fusion.where_ref, s32[4096]{0:T(1024)} %reshape.23.pairs_ref, f32[128,128]{1,0:T(8,128)} %coeffs_ref.1, f32[18,32,128]{2,1,0:T(8,128)S(1)} %copy-done, ...), custom_call_target="tpu_custom_call" | custom-call | tf_op jit(solution)/shard_map/terms/pallas_call | solution.py:231
  58.4 1.0 %collective-permute-start.13 = (f32[256,128]{1,0:T(8,128)}, f32[256,128]{1,0:T(8,128)S(1)}, u32[]{:S(2)}, u32[]{:S(2)}) collective-permute-start(f32[256,128]{1,0:T(8,128)} %get-tuple-element.34), channel_id=1, source_target_pairs={{0,8},{8,0},{16,24},{24,16},{1,9},{9,1},{17,25},{25,17},{2,10},{10... | collective-permute-start | bytes 393224 | tf_op jit(solution)/shard_map/sum_over_rows/ppermute | solution.py:250
  59.4 2.0 %collective-permute-start.14 = (f32[256,128]{1,0:T(8,128)}, f32[256,128]{1,0:T(8,128)S(1)}, u32[]{:S(2)}, u32[]{:S(2)}) collective-permute-start(f32[256,128]{1,0:T(8,128)} %get-tuple-element.35), channel_id=1, source_target_pairs={{0,16},{8,24},{16,0},{24,8},{1,17},{9,25},{17,1},{25,9},{2,18},{10... | collective-permute-start | bytes 393224 | tf_op jit(solution)/shard_map/sum_over_rows/ppermute | solution.py:250
  61.4 0.5 collective-permute-start.15
  61.9 2.8 %collective-permute-done.13 = f32[256,128]{1,0:T(8,128)S(1)} collective-permute-done((f32[256,128]{1,0:T(8,128)}, f32[256,128]{1,0:T(8,128)S(1)}, u32[]{:S(2)}, u32[]{:S(2)}) %collective-permute-start.13) | collective-permute-done | bytes 131104 | tf_op jit(solution)/shard_map/sum_over_rows/ppermute | solution.py:250
  64.7 3.1 %collective-permute-done.14 = f32[256,128]{1,0:T(8,128)S(1)} collective-permute-done((f32[256,128]{1,0:T(8,128)}, f32[256,128]{1,0:T(8,128)S(1)}, u32[]{:S(2)}, u32[]{:S(2)}) %collective-permute-start.14) | collective-permute-done | bytes 131104 | tf_op jit(solution)/shard_map/sum_over_rows/ppermute | solution.py:250
  67.8 0.9 %add_add_fusion = f32[256,128]{1,0:T(8,128)S(1)} fusion(f32[256,128]{1,0:T(8,128)S(1)} %collective-permute-done.15, f32[256,128]{1,0:T(8,128)S(1)} %collective-permute-done.14, f32[256,128]{1,0:T(8,128)} %get-tuple-element.33, f32[256,128]{1,0:T(8,128)S(1)} %collective-permute-done.13), kind=kLoop, calls=%fused_computation.1 | loop fusion | flops 98304 | bytes 655360 | tf_op jit(solution)/shard_map/sum_over_rows/add | solution.py:250
  69.0 3.6 %collective-permute-start.18 = (f32[64,128]{1,0:T(8,128)S(1)}, f32[64,128]{1,0:T(8,128)S(1)}, u32[]{:S(2)}, u32[]{:S(2)}) collective-permute-start(f32[64,128]{1,0:T(8,128)S(1)} %get-tuple-element.42), channel_id=1, source_target_pairs={{0,6},{1,7},{2,0},{3,1},{4,2},{5,3},{6,4},{7,5},{8,14},{9,15},{10,... | collective-permute-start | bytes 98312 | tf_op jit(solution)/shard_map/sum_over_chips/ppermute | solution.py:258
  72.6 0.4 collective-permute-start.17
  73.0 1.6 %collective-permute-done.16 = f32[64,128]{1,0:T(8,128)S(1)} collective-permute-done((f32[64,128]{1,0:T(8,128)S(1)}, f32[64,128]{1,0:T(8,128)S(1)}, u32[]{:S(2)}, u32[]{:S(2)}) %collective-permute-start.16) | collective-permute-done | bytes 32800 | tf_op jit(solution)/shard_map/sum_over_chips/ppermute | solution.py:258
  74.6 2.8 %collective-permute-done.17 = f32[64,128]{1,0:T(8,128)S(1)} collective-permute-done((f32[64,128]{1,0:T(8,128)S(1)}, f32[64,128]{1,0:T(8,128)S(1)}, u32[]{:S(2)}, u32[]{:S(2)}) %collective-permute-start.17) | collective-permute-done | bytes 32800 | tf_op jit(solution)/shard_map/sum_over_chips/ppermute | solution.py:258
  77.5 0.6 fusion.2
  (20 shorter events, 0.4 us)
Async XLA Ops:
  3.5 21.1 %collective-permute-start = (f32[4,12,16,128]{3,2,1,0:T(8,128)}, f32[4,12,16,128]{3,2,1,0:T(8,128)S(1)}, u32[]{:S(2)}, u32[]{:S(2)}) collective-permute-start(f32[4,12,16,128]{3,2,1,0:T(8,128)} %get-tuple-element.21), channel_id=1, source_target_pairs={{2,0},{4,2},{6,4},{0,6},{10,8},{12,10},{14,12},{8,14},{18,16},{20,... | collective-permute-start | bytes 1179656 | tf_op jit(solution)/shard_map/to_chip_before/ppermute | solution.py:215
  10.5 14.2 %collective-permute-start.1 = (f32[4,12,16,128]{3,2,1,0:T(8,128)}, f32[4,12,16,128]{3,2,1,0:T(8,128)S(1)}, u32[]{:S(2)}, u32[]{:S(2)}) collective-permute-start(f32[4,12,16,128]{3,2,1,0:T(8,128)} %get-tuple-element.22), channel_id=1, source_target_pairs={{2,1},{4,3},{6,5},{0,7},{10,9},{12,11},{14,13},{8,15},{18,17},{20,... | collective-permute-start | bytes 1179656 | tf_op jit(solution)/shard_map/to_chip_before/ppermute | solution.py:215
  11.8 7.1 %collective-permute-start.2 = (f32[18,32,128]{2,1,0:T(8,128)}, f32[18,32,128]{2,1,0:T(8,128)S(1)}, u32[]{:S(2)}, u32[]{:S(2)}) collective-permute-start(f32[18,32,128]{2,1,0:T(8,128)} %get-tuple-element.24), channel_id=1, source_target_pairs={{0,8},{8,0},{16,24},{24,16},{1,9},{9,1},{17,25},{25,17},{2,10},{10... | collective-permute-start | bytes 884744 | tf_op jit(solution)/shard_map/to_rows/ppermute | solution.py:221
  13.4 11.3 %collective-permute-start.3 = (f32[18,32,128]{2,1,0:T(8,128)}, f32[18,32,128]{2,1,0:T(8,128)S(1)}, u32[]{:S(2)}, u32[]{:S(2)}) collective-permute-start(f32[18,32,128]{2,1,0:T(8,128)} %get-tuple-element.25), channel_id=1, source_target_pairs={{0,16},{8,24},{16,0},{24,8},{1,17},{9,25},{17,1},{25,9},{2,18},{10... | collective-permute-start | bytes 884744 | tf_op jit(solution)/shard_map/to_rows/ppermute | solution.py:221
  14.9 9.8 %collective-permute-start.4 = (f32[18,32,128]{2,1,0:T(8,128)}, f32[18,32,128]{2,1,0:T(8,128)S(1)}, u32[]{:S(2)}, u32[]{:S(2)}) collective-permute-start(f32[18,32,128]{2,1,0:T(8,128)} %get-tuple-element.26), channel_id=1, source_target_pairs={{0,24},{8,16},{16,8},{24,0},{1,25},{9,17},{17,9},{25,1},{2,26},{10... | collective-permute-start | bytes 884744 | tf_op jit(solution)/shard_map/to_rows/ppermute | solution.py:221
  24.7 5.7 %collective-permute-start.11 = (f32[12,16,128]{2,1,0:T(8,128)S(1)}, f32[12,16,128]{2,1,0:T(8,128)S(1)}, u32[]{:S(2)}, u32[]{:S(2)}) collective-permute-start(f32[12,16,128]{2,1,0:T(8,128)S(1)} %get-tuple-element.37), channel_id=1, source_target_pairs={{0,24},{8,16},{16,8},{24,0},{1,25},{9,17},{17,9},{25,1},{2,26},{10... | collective-permute-start | bytes 294920 | tf_op jit(solution)/shard_map/next_to_rows/ppermute | solution.py:227
  25.2 5.7 %collective-permute-start.10 = (f32[12,16,128]{2,1,0:T(8,128)S(1)}, f32[12,16,128]{2,1,0:T(8,128)S(1)}, u32[]{:S(2)}, u32[]{:S(2)}) collective-permute-start(f32[12,16,128]{2,1,0:T(8,128)S(1)} %get-tuple-element.38), channel_id=1, source_target_pairs={{0,16},{8,24},{16,0},{24,8},{1,17},{9,25},{17,1},{25,9},{2,18},{10... | collective-permute-start | bytes 294920 | tf_op jit(solution)/shard_map/next_to_rows/ppermute | solution.py:227
  26.9 5.1 %collective-permute-start.9 = (f32[12,16,128]{2,1,0:T(8,128)S(1)}, f32[12,16,128]{2,1,0:T(8,128)S(1)}, u32[]{:S(2)}, u32[]{:S(2)}) collective-permute-start(f32[12,16,128]{2,1,0:T(8,128)S(1)} %get-tuple-element.39), channel_id=1, source_target_pairs={{0,8},{8,0},{16,24},{24,16},{1,9},{9,1},{17,25},{25,17},{2,10},{10... | collective-permute-start | bytes 294920 | tf_op jit(solution)/shard_map/next_to_rows/ppermute | solution.py:227
  31.9 1.0 %copy-start = (f32[18,32,128]{2,1,0:T(8,128)S(1)}, f32[18,32,128]{2,1,0:T(8,128)}, u32[]{:S(2)}) copy-start(f32[18,32,128]{2,1,0:T(8,128)} %get-tuple-element.27.refs_0_) | copy-start | bytes 884740
  31.9 2.0 %copy-start.1 = (s32[2048,2]{0,1:T(2,128)S(1)}, s32[2048,2]{0,1:T(2,128)}, u32[]{:S(2)}) copy-start(s32[2048,2]{0,1:T(2,128)} %param.5) | copy-start | bytes 49156
  32.0 5.6 %collective-permute-start.12 = (f32[4,12,16,128]{3,2,1,0:T(8,128)S(1)}, f32[4,12,16,128]{3,2,1,0:T(8,128)S(1)}, u32[]{:S(2)}, u32[]{:S(2)}) collective-permute-start(f32[4,12,16,128]{3,2,1,0:T(8,128)S(1)} %pad_maximum_fusion), channel_id=1, source_target_pairs={{0,1},{1,0},{2,3},{3,2},{4,5},{5,4},{6,7},{7,6},{8,9},{9,8},{10,11... | collective-permute-start | bytes 1179656 | tf_op jit(solution)/shard_map/next_to_other_core/ppermute | solution.py:229
  32.9 4.7 %collective-permute-start.5 = (f32[18,32,128]{2,1,0:T(8,128)S(1)}, f32[18,32,128]{2,1,0:T(8,128)S(1)}, u32[]{:S(2)}, u32[]{:S(2)}) collective-permute-start(f32[18,32,128]{2,1,0:T(8,128)S(1)} %copy-done), channel_id=1, source_target_pairs={{0,1},{1,0},{2,3},{3,2},{4,5},{5,4},{6,7},{7,6},{8,9},{9,8},{10,11... | collective-permute-start | bytes 884744 | tf_op jit(solution)/shard_map/to_other_core/ppermute | solution.py:223
  32.9 4.7 %collective-permute-start.6 = (f32[18,32,128]{2,1,0:T(8,128)S(1)}, f32[18,32,128]{2,1,0:T(8,128)S(1)}, u32[]{:S(2)}, u32[]{:S(2)}) collective-permute-start(f32[18,32,128]{2,1,0:T(8,128)S(1)} %collective-permute-done.2.refs_1_), channel_id=1, source_target_pairs={{0,1},{1,0},{2,3},{3,2},{4,5},{5,4},{6,7},{7,6},{8,9},{9,8},{10,11... | collective-permute-start | bytes 884744 | tf_op jit(solution)/shard_map/to_other_core/ppermute | solution.py:223
  33.4 4.2 %collective-permute-start.7 = (f32[18,32,128]{2,1,0:T(8,128)S(1)}, f32[18,32,128]{2,1,0:T(8,128)S(1)}, u32[]{:S(2)}, u32[]{:S(2)}) collective-permute-start(f32[18,32,128]{2,1,0:T(8,128)S(1)} %collective-permute-done.3.refs_2_), channel_id=1, source_target_pairs={{0,1},{1,0},{2,3},{3,2},{4,5},{5,4},{6,7},{7,6},{8,9},{9,8},{10,11... | collective-permute-start | bytes 884744 | tf_op jit(solution)/shard_map/to_other_core/ppermute | solution.py:223
  33.4 4.2 %collective-permute-start.8 = (f32[18,32,128]{2,1,0:T(8,128)S(1)}, f32[18,32,128]{2,1,0:T(8,128)S(1)}, u32[]{:S(2)}, u32[]{:S(2)}) collective-permute-start(f32[18,32,128]{2,1,0:T(8,128)S(1)} %collective-permute-done.4.refs_3_), channel_id=1, source_target_pairs={{0,1},{1,0},{2,3},{3,2},{4,5},{5,4},{6,7},{7,6},{8,9},{9,8},{10,11... | collective-permute-start | bytes 884744 | tf_op jit(solution)/shard_map/to_other_core/ppermute | solution.py:223
  58.4 6.3 %collective-permute-start.13 = (f32[256,128]{1,0:T(8,128)}, f32[256,128]{1,0:T(8,128)S(1)}, u32[]{:S(2)}, u32[]{:S(2)}) collective-permute-start(f32[256,128]{1,0:T(8,128)} %get-tuple-element.34), channel_id=1, source_target_pairs={{0,8},{8,0},{16,24},{24,16},{1,9},{9,1},{17,25},{25,17},{2,10},{10... | collective-permute-start | bytes 393224 | tf_op jit(solution)/shard_map/sum_over_rows/ppermute | solution.py:250
  59.4 8.4 %collective-permute-start.14 = (f32[256,128]{1,0:T(8,128)}, f32[256,128]{1,0:T(8,128)S(1)}, u32[]{:S(2)}, u32[]{:S(2)}) collective-permute-start(f32[256,128]{1,0:T(8,128)} %get-tuple-element.35), channel_id=1, source_target_pairs={{0,16},{8,24},{16,0},{24,8},{1,17},{9,25},{17,1},{25,9},{2,18},{10... | collective-permute-start | bytes 393224 | tf_op jit(solution)/shard_map/sum_over_rows/ppermute | solution.py:250
  61.4 6.4 %collective-permute-start.15 = (f32[256,128]{1,0:T(8,128)}, f32[256,128]{1,0:T(8,128)S(1)}, u32[]{:S(2)}, u32[]{:S(2)}) collective-permute-start(f32[256,128]{1,0:T(8,128)} %get-tuple-element.36), channel_id=1, source_target_pairs={{0,24},{8,16},{16,8},{24,0},{1,25},{9,17},{17,9},{25,1},{2,26},{10... | collective-permute-start | bytes 393224 | tf_op jit(solution)/shard_map/sum_over_rows/ppermute | solution.py:250
  68.8 5.9 %collective-permute-start.16 = (f32[64,128]{1,0:T(8,128)S(1)}, f32[64,128]{1,0:T(8,128)S(1)}, u32[]{:S(2)}, u32[]{:S(2)}) collective-permute-start(f32[64,128]{1,0:T(8,128)S(1)} %get-tuple-element.41), channel_id=1, source_target_pairs={{0,2},{1,3},{2,4},{3,5},{4,6},{5,7},{6,0},{7,1},{8,10},{9,11},{10,... | collective-permute-start | bytes 98312 | tf_op jit(solution)/shard_map/sum_over_chips/ppermute | solution.py:258
  69.0 5.6 %collective-permute-start.18 = (f32[64,128]{1,0:T(8,128)S(1)}, f32[64,128]{1,0:T(8,128)S(1)}, u32[]{:S(2)}, u32[]{:S(2)}) collective-permute-start(f32[64,128]{1,0:T(8,128)S(1)} %get-tuple-element.42), channel_id=1, source_target_pairs={{0,6},{1,7},{2,0},{3,1},{4,2},{5,3},{6,4},{7,5},{8,14},{9,15},{10,... | collective-permute-start | bytes 98312 | tf_op jit(solution)/shard_map/sum_over_chips/ppermute | solution.py:258
  72.6 4.8 %collective-permute-start.17 = (f32[64,128]{1,0:T(8,128)S(1)}, f32[64,128]{1,0:T(8,128)S(1)}, u32[]{:S(2)}, u32[]{:S(2)}) collective-permute-start(f32[64,128]{1,0:T(8,128)S(1)} %get-tuple-element.43), channel_id=1, source_target_pairs={{0,4},{1,5},{2,6},{3,7},{4,0},{5,1},{6,2},{7,3},{8,12},{9,13},{10,... | collective-permute-start | bytes 98312 | tf_op jit(solution)/shard_map/sum_over_chips/ppermute | solution.py:258

commit v4 on v3

v4 whole, which is shorter than its diff:
```python
import functools

import jax
import jax.numpy as jnp
from jax import lax
from jax.experimental import pallas as pl
from jax.experimental.pallas import tpu as pltpu
from jax.sharding import PartitionSpec as P

F32 = jnp.float32
BF16 = jnp.bfloat16


def split_high_low(values):
    high = values.astype(BF16)
    low = (values - high.astype(F32)).astype(BF16)
    return high, low


def pack_kernel(where_ref, field_ref, *out_refs, sizes):
    local_s, rows_y, block_rows, tm_count = sizes
    t = where_ref[0]
    half_s = local_s // 2
    for peer in range(tm_count):
        first_row = jnp.bitwise_xor(t, peer) * block_rows
        for row in range(block_rows + 2):
            if row < block_rows:
                y = first_row + row
            else:
                y = first_row - 1 if row == block_rows else first_row + block_rows
                inside = jnp.logical_and(y >= 0, y < rows_y)
                y = jnp.clip(y, 0, rows_y - 1)
            for c in range(3):
                slab = field_ref[pl.ds(c * rows_y + y, local_s, stride=3 * rows_y), :]
                if row < block_rows:
                    for part in range(2):
                        out_refs[tm_count + part][peer, row * 3 + c] = slab[part * half_s : (part + 1) * half_s]
                else:
                    slab = jnp.where(inside, slab, 0.0)
                out_refs[peer][row * 3 + c] = slab


def mode_weights(where_ref, coeffs_ref, local_s, tm_count):
    t = where_ref[0]
    ordered = jnp.concatenate(
        [
            coeffs_ref[pl.ds(pl.multiple_of(jnp.bitwise_xor(t, peer) * local_s, 8), local_s), :]
            for peer in range(tm_count)
        ],
        axis=0,
    )
    high, low = split_high_low(ordered.T)
    return jnp.concatenate([high, low, high, low], axis=1)


def modes_of(weights, slab):
    high, low = split_high_low(slab)
    return jnp.dot(weights, jnp.concatenate([high, high, low, low], axis=0), preferred_element_type=F32)


def store_projection(rhs_ref, place, mode_slab):
    high, low = split_high_low(mode_slab.T)
    modes, lanes = mode_slab.shape
    rhs_ref[place * lanes : (place + 1) * lanes, 0:modes] = high
    rhs_ref[place * lanes : (place + 1) * lanes, modes : 2 * modes] = low


def project(conv_ref, lhs_ref, rhs_ref, block, places, lanes):
    for place in range(places):
        values = conv_ref[pl.ds(place, block, stride=places), :]
        high, low = split_high_low(values)
        lhs_ref[0:block, place * lanes : (place + 1) * lanes] = high
        lhs_ref[block : 2 * block, place * lanes : (place + 1) * lanes] = low
    both = jnp.dot(lhs_ref[...], rhs_ref[...], preferred_element_type=F32)
    modes = both.shape[1] // 2
    return (both[:block, :modes] + both[:block, modes:]) + (both[block:, :modes] + both[block:, modes:])


def for_pairs_of(where_ref, pairs_ref, peer, sizes, one_pair):
    chips, share = sizes
    t, chip, core = where_ref[0], where_ref[1], where_ref[2]
    to_t = jnp.bitwise_xor(t, peer)
    for ahead in range(chips):
        base = ((to_t * chips + lax.rem(chip + ahead, chips)) * 2 + core) * share

        def one(q, _):
            one_pair(ahead * share + q, pairs_ref[0, base + q], pairs_ref[1, base + q])
            return 0

        lax.fori_loop(0, share, one, 0, unroll=16)


def inner_kernel(where_ref, pairs_ref, coeffs_ref, *refs, peers, sizes):
    local_s, block_rows, tm_count, chips, share = sizes
    own, other = refs[:tm_count], refs[tm_count : 2 * tm_count]
    near_ref, carry_ref, slope_ref, rhs_ref = refs[2 * tm_count : 2 * tm_count + 4]
    *out_refs, slab_ref, conv_ref, lhs_ref = refs[2 * tm_count + 4 :]
    core = where_ref[2]
    modes, lanes = coeffs_ref.shape[1], own[0].shape[2]
    height = 2 * block_rows
    weights = mode_weights(where_ref, coeffs_ref, local_s, tm_count)

    def one_slab(index, _):
        own_slab = jnp.concatenate([piece[index] for piece in own], axis=0)
        other_slab = jnp.concatenate([piece[index] for piece in other], axis=0)
        is_first = core == 0
        both = jnp.concatenate(
            [jnp.where(is_first, own_slab, other_slab), jnp.where(is_first, other_slab, own_slab)], axis=1
        )
        result = modes_of(weights, both)
        slab_ref[0, index] = result[:, :lanes]
        slab_ref[1, index] = result[:, lanes:]
        return 0

    lax.fori_loop(0, (block_rows + 2) * 3, one_slab, 0, unroll=3)
    for c in range(3):
        for row in range(block_rows):
            above = (row + 1 if row + 1 < block_rows else block_rows + 1) * 3 + c
            below = (row - 1 if row > 0 else block_rows) * 3 + c
            center = row * 3 + c
            for plane in range(2):
                place = plane * block_rows + row
                value = slab_ref[plane, center]
                stream = slab_ref[1 - plane, center] * (0.5 if plane == 0 else -0.5)
                normal = (slab_ref[plane, above] - slab_ref[plane, below]) * 0.5
                span = (pltpu.roll(value, lanes - 1, 1) - pltpu.roll(value, 1, 1)) * 0.5
                carry_ref[pl.ds(c * height + place, modes, stride=3 * height), :] = value
                for d, slope in enumerate((stream, normal, span)):
                    slope_ref[pl.ds((d * 3 + c) * height + place, modes, stride=9 * height), :] = slope
                store_projection(rhs_ref, c * height + place, value)
                if plane == 1:
                    near_ref[center] = value

    pairs_kernel(
        where_ref, pairs_ref, carry_ref, slope_ref, rhs_ref, *out_refs, conv_ref, lhs_ref,
        peers=peers, sizes=(height, chips, share),
    )


def pairs_kernel(where_ref, pairs_ref, carry_ref, slope_ref, rhs_ref, *refs, peers, sizes):
    *out_refs, conv_ref, lhs_ref = refs
    height, chips, share = sizes

    def one_pair(slot, i, j):
        carry = carry_ref[pl.ds(pl.multiple_of(i * (3 * height), 8), 3 * height), :]
        slope = slope_ref[pl.ds(pl.multiple_of(j * (9 * height), 8), 9 * height), :]
        rows = [
            sum(
                carry[d * height : (d + 1) * height] * slope[(d * 3 + c) * height : (d * 3 + c + 1) * height]
                for d in range(3)
            )
            for c in range(3)
        ]
        conv_ref[pl.ds(pl.multiple_of(slot * (3 * height), 8), 3 * height), :] = jnp.concatenate(rows, axis=0)

    for peer, out_ref in zip(peers, out_refs):
        for_pairs_of(where_ref, pairs_ref, peer, (chips, share), one_pair)
        out_ref[...] = project(conv_ref, lhs_ref, rhs_ref, chips * share, 3 * height, conv_ref.shape[1])


def far_kernel(where_ref, coeffs_ref, *refs, sizes):
    local_s, block_rows, tm_count = sizes
    next_own, next_other, near_ref = refs[:tm_count], refs[tm_count], refs[tm_count + 1]
    carry_ref, slope_ref, rhs_ref = refs[tm_count + 2 :]
    is_first = where_ref[2] == 0
    modes, lanes = near_ref.shape[1:]
    height = 2 * block_rows
    weights = mode_weights(where_ref, coeffs_ref, local_s, tm_count)
    for pair in range(3 * block_rows // 2):
        slabs = []
        for slab in (2 * pair, 2 * pair + 1):
            halves = []
            for peer in range(tm_count):
                mine, theirs = next_own[peer][slab], next_other[peer, slab]
                halves += [jnp.where(is_first, mine, theirs), jnp.where(is_first, theirs, mine)]
            slabs.append(jnp.concatenate(halves, axis=0))
        result = modes_of(weights, jnp.concatenate(slabs, axis=1))
        for part in range(2):
            row, c = divmod(2 * pair + part, 3)
            near, far = near_ref[2 * pair + part], result[:, part * lanes : (part + 1) * lanes]
            for place, value, across in ((row, near, far * 0.5), (block_rows + row, far, near * -0.5)):
                if c == 0:
                    carry_ref[pl.ds(place, modes, stride=height), :] = value
                slope_ref[pl.ds(c * height + place, modes, stride=3 * height), :] = across
                store_projection(rhs_ref, c * height + place, value)


def edge_kernel(
    where_ref, pairs_ref, carry_ref, slope_ref, rhs_ref, inner_ref, out_ref, conv_ref, lhs_ref, *, peer, sizes
):
    chips, share = sizes
    modes, lanes = out_ref.shape[1], carry_ref.shape[1]
    height = carry_ref.shape[0] // modes

    def one_pair(slot, i, j):
        carry = carry_ref[pl.ds(pl.multiple_of(i * height, 8), height), :]
        slope = slope_ref[pl.ds(pl.multiple_of(j * (3 * height), 8), 3 * height), :]
        rows = [carry * slope[c * height : (c + 1) * height] for c in range(3)]
        conv_ref[pl.ds(pl.multiple_of(slot * (3 * height), 8), 3 * height), :] = jnp.concatenate(rows, axis=0)

    for_pairs_of(where_ref, pairs_ref, peer, sizes, one_pair)
    out_ref[...] = inner_ref[...] + project(conv_ref, lhs_ref, rhs_ref, chips * share, 3 * height, lanes)


def vmem_limit(mebibytes):
    return pltpu.CompilerParams(vmem_limit_bytes=mebibytes * 2**20)


def in_vmem(array):
    return pltpu.with_memory_space_constraint(array, pltpu.VMEM)


def shards(snapshots, coeffs, pair_table):
    tm_count, space_count = lax.axis_size("tm"), lax.axis_size("space")
    chips = space_count // 2
    t, place = lax.axis_index("tm"), lax.axis_index("space")
    core = lax.rem(place, 2)
    where = jnp.stack([t, lax.div(place, 2), core]).astype(jnp.int32)
    local_s, _, _, rows_y, lanes = snapshots.shape
    modes = coeffs.shape[1]
    block_rows = rows_y // tm_count
    share = pair_table.shape[0] // (tm_count * space_count)
    factor = float(space_count * rows_y * lanes) ** (-0.5)
    pairs = pair_table.T
    smem = pl.BlockSpec(memory_space=pltpu.SMEM)
    vmem = pl.BlockSpec(memory_space=pltpu.VMEM)
    half_s = local_s // 2
    block = chips * share
    height = 2 * block_rows
    depth = 3 * height * lanes

    swap = [(2 * chip + c, 2 * chip + 1 - c) for chip in range(chips) for c in range(2)]

    def across(peer):
        return [(i, i ^ peer) for i in range(tm_count)]

    with jax.named_scope("pack"):
        packed = pl.pallas_call(
            functools.partial(pack_kernel, sizes=(local_s, rows_y, block_rows, tm_count)),
            out_shape=[pltpu.VMEM(((block_rows + 2) * 3, local_s, lanes), F32)] * tm_count
            + [pltpu.VMEM((tm_count, block_rows * 3, half_s, lanes), F32)] * 2,
            in_specs=[smem, vmem],
            out_specs=[vmem] * (tm_count + 2),
            compiler_params=vmem_limit(16),
        )(where, snapshots.reshape(-1, lanes))
    with jax.named_scope("to_chip_before"):
        ahead = [
            lax.ppermute(
                packed[tm_count + c], "space", [(2 * ((chip + 1) % chips), 2 * chip + c) for chip in range(chips)]
            )
            for c in range(2)
        ]
    with jax.named_scope("to_rows"):
        own = [packed[0]] + [lax.ppermute(packed[peer], "tm", across(peer)) for peer in range(1, tm_count)]
    with jax.named_scope("to_other_core"):
        other = [lax.ppermute(piece, "space", swap) for piece in own]
    with jax.named_scope("next_to_rows"):
        ahead, own, other = lax.optimization_barrier((ahead, own, other))
        parts = [jnp.where(core == 0, ahead[0][peer], ahead[1][peer]) for peer in range(tm_count)]
        next_own = [parts[0]] + [lax.ppermute(parts[peer], "tm", across(peer)) for peer in range(1, tm_count)]
    early, late = range(tm_count - 1, tm_count // 2 - 1, -1), range(tm_count // 2 - 1, -1, -1)
    work = [pltpu.VMEM((block * 3 * height, lanes), F32), pltpu.VMEM((2 * block, depth), BF16)]
    group = pltpu.VMEM((block, modes), F32)
    with jax.named_scope("inner_terms"):
        near, *inner_tables_and_early = pl.pallas_call(
            functools.partial(inner_kernel, peers=early, sizes=(local_s, block_rows, tm_count, chips, share)),
            out_shape=[
                pltpu.VMEM((block_rows * 3, modes, lanes), F32),
                pltpu.VMEM((modes * 3 * height, lanes), F32),
                pltpu.VMEM((modes * 9 * height, lanes), F32),
                pltpu.VMEM((depth, 2 * modes), BF16),
            ]
            + [group] * len(early),
            in_specs=[smem, smem] + [vmem] * (2 * tm_count + 1),
            out_specs=[vmem] * (4 + len(early)),
            scratch_shapes=[pltpu.VMEM((2, (block_rows + 2) * 3, modes, lanes), F32)] + work,
            compiler_params=vmem_limit(24),
            cost_estimate=pl.CostEstimate(flops=12 * 10**9, bytes_accessed=10**7, transcendentals=0),
        )(where, pairs, coeffs, *[in_vmem(piece) for piece in (*own, *other)])
        inner_tables, early_sums = inner_tables_and_early[:3], inner_tables_and_early[3:]
    with jax.named_scope("next_to_other_core"):
        next_own, inner_tables = lax.optimization_barrier((next_own, inner_tables))
        next_other = lax.ppermute(jnp.stack(next_own), "space", swap)
    with jax.named_scope("inner_terms"):
        late_sums = pl.pallas_call(
            functools.partial(pairs_kernel, peers=late, sizes=(height, chips, share)),
            out_shape=[group] * len(late),
            in_specs=[smem, smem] + [vmem] * 3,
            out_specs=[vmem] * len(late),
            scratch_shapes=work,
            compiler_params=vmem_limit(16),
            cost_estimate=pl.CostEstimate(flops=8 * 10**9, bytes_accessed=10**7, transcendentals=0),
        )(where, pairs, *[in_vmem(table) for table in inner_tables])
        inner = [*reversed(late_sums), *reversed(early_sums)]
    with jax.named_scope("edge_tables"):
        tables = pl.pallas_call(
            functools.partial(far_kernel, sizes=(local_s, block_rows, tm_count)),
            out_shape=[
                pltpu.VMEM((modes * height, lanes), F32),
                pltpu.VMEM((modes * 3 * height, lanes), F32),
                pltpu.VMEM((depth, 2 * modes), BF16),
            ],
            in_specs=[smem] + [vmem] * (tm_count + 3),
            out_specs=[vmem] * 3,
            compiler_params=vmem_limit(16),
        )(where, coeffs, *[in_vmem(piece) for piece in (*next_own, next_other, near)])
    sums = [None] * tm_count
    arrived = []
    for peer in reversed(range(tm_count)):
        with jax.named_scope("edge_terms"):
            sums[peer] = pl.pallas_call(
                functools.partial(edge_kernel, peer=peer, sizes=(chips, share)),
                out_shape=group,
                in_specs=[smem, smem] + [vmem] * 4,
                out_specs=vmem,
                scratch_shapes=work,
                compiler_params=vmem_limit(16),
                cost_estimate=pl.CostEstimate(flops=4 * 10**9, bytes_accessed=10**7, transcendentals=0),
            )(where, pairs, *[in_vmem(table) for table in (*tables, inner[peer])])
        with jax.named_scope("sum_over_rows"):
            if peer:
                arrived.append(lax.ppermute(sums[peer], "tm", across(peer)))
                inner[peer - 1], _ = lax.optimization_barrier((inner[peer - 1], sums[peer]))
    with jax.named_scope("sum_over_rows"):
        summed = sums[0]
        for part in arrived:
            summed = summed + part
    with jax.named_scope("sum_over_chips"):
        shares = summed.reshape(chips, share, modes)
        result = shares[0]
        for step in range(1, chips):
            shift = [
                (2 * chip + c, 2 * ((chip + step) % chips) + c) for chip in range(chips) for c in range(2)
            ]
            result = result + lax.ppermute(shares[step], "space", shift)
        return result * factor


def solution(mesh):
    placed = (P("tm", None, "space", None, None), P(), P())
    return jax.shard_map(
        shards, mesh=mesh, in_specs=placed, out_specs=P(("tm", "space"), None), check_vma=False
    )
```

time: 78.4 us -> 73.7 us (0.940)
  waiting for transfers between devices: 23.3 us -> 10.8 us
  Pallas kernels: 23.8 us -> 32.6 us
  local copies, waits for them, and re-layouts: 4.52 us -> 1.15 us
  starting transfers between devices: 24.2 us -> 26.8 us
    pallas_call x1 -> x7, Pallas kernels: 20.8 us -> 31.6 us  [the longest x4 12.9 us: shards(): pl.pallas_call(functools.partial(edge_kernel, peer=peer, sizes=(chips, sh...]
    ppermute x3, waiting for transfers between devices: 9.31 us -> 3.04 us  [shards(): lax.ppermute(packed[peer], 'tm', across(peer))]
    ppermute x3, waiting for transfers between devices: 5.87 us -> 1.42 us  [shards(): arrived.append(lax.ppermute(sums[peer], 'tm', across(peer)))]
    ppermute x3, waiting for transfers between devices: 3.64 us -> 0.01 us  [shards(): lax.ppermute(parts[peer], 'tm', across(peer))]
    reshape x1 -> x0, local copies, waits for them, and re-layouts: 2.29 us -> none  [shards(): pairs = pair_table.reshape(-1)]
    ppermute x2, starting transfers between devices: 8.26 us -> 10.2 us  [shards(): lax.ppermute(packed[tm_count + c], 'space', [(2 * ((chip + 1) % chips), 2...]
    pallas_call x1, Pallas kernels: 2.92 us -> 1 us  [shards(): pl.pallas_call(functools.partial(pack_kernel, sizes=(local_s, rows_y, blo...]
    ppermute x2, waiting for transfers between devices: 0.01 us -> 1.62 us  [shards(): lax.ppermute(packed[tm_count + c], 'space', [(2 * ((chip + 1) % chips), 2...]
  transfers between devices with their start and end apart: 19 -> 19, of which waited for: 9 -> 7; matrix products, arithmetic and copies ran while one was open for 5% -> 0% of each run, Pallas kernels for 0% -> 36%
where the time goes in v4:
time: 73.7 us; the launch traced here: 73.5 us
  Pallas kernels  32.6 us (44%)
  starting transfers between devices  26.8 us (36%)
  waiting for transfers between devices  10.8 us (15%)
  other arithmetic  2.02 us (3%)
  local copies, waits for them, and re-layouts  1.15 us (2%)
    pallas_call x4, Pallas kernels, shards(): pl.pallas_call(functools.partial(edge_kernel, peer=peer, sizes=(chips, sh...  12.9 us
    pallas_call x1, Pallas kernels, shards(): pl.pallas_call(functools.partial(inner_kernel, peers=early, sizes=(local_...  10.6 us
    ppermute x2, starting transfers between devices, shards(): lax.ppermute(packed[tm_count + c], 'space', [(2 * ((chip + 1) % chips), 2...  10.2 us
    pallas_call x1, Pallas kernels, shards(): pl.pallas_call(functools.partial(pairs_kernel, peers=late, sizes=(height,...  6.58 us
    ppermute x3, starting transfers between devices, shards(): lax.ppermute(packed[peer], 'tm', across(peer))  4.54 us
    ppermute x3, waiting for transfers between devices, shards(): result = result + lax.ppermute(shares[step], 'space', shift)  4.49 us
    ppermute x3, starting transfers between devices, shards(): result = result + lax.ppermute(shares[step], 'space', shift)  4.19 us
    ppermute x3, starting transfers between devices, shards(): arrived.append(lax.ppermute(sums[peer], 'tm', across(peer)))  3.69 us
  transfers between devices with their start and end apart: 19, of which 7 were waited for; matrix products, arithmetic and copies ran while one was open for 0% of the time, Pallas kernels for 36%

profile of v4, /device:TPU:0, one launch (start us, length us, event | category | flops | bytes accessed | tf_op | source)
XLA Modules:
  0.0 73.5 jit_solution(9158813720849462835)
XLA Ops:
  0.1 1.1 %copy-done = f32[32,3,1,16,128]{4,3,2,1,0:T(8,128)S(1)} copy-done((f32[32,3,1,16,128]{4,3,2,1,0:T(8,128)S(1)}, f32[32,3,1,16,128]{4,3,2,1,0:T(8,128)}, u32[]{:S(2)}) %copy-start) | copy-done | bytes 786456
  1.2 1.0 %pack.1 = (f32[18,32,128]{2,1,0:T(8,128)S(1)}, f32[18,32,128]{2,1,0:T(8,128)S(1)}, f32[18,32,128]{2,1,0:T(8,128)S(1)}, f32[18,32,128]{2,1,0:T(8,128)S(1)}, f32[4...) custom-call(s32[3]{0:T(128)S(1)} %pad_add_fusion.where_ref, f32[1536,128]{1,0:T(8,128)S(1)} %bitcast.18), custom_call_target="tpu_custom_call" | custom-call | tf_op jit(solution)/shard_map/pack/pallas_call | solution.py:238
  2.2 3.0 %collective-permute-start.2 = (f32[18,32,128]{2,1,0:T(8,128)S(1)}, f32[18,32,128]{2,1,0:T(8,128)S(1)}, u32[]{:S(2)}, u32[]{:S(2)}) collective-permute-start(f32[18,32,128]{2,1,0:T(8,128)S(1)} %get-tuple-element.45), channel_id=1, source_target_pairs={{0,8},{8,0},{16,24},{24,16},{1,9},{9,1},{17,25},{25,17},{2,10},{10... | collective-permute-start | bytes 884744 | tf_op jit(solution)/shard_map/to_rows/ppermute | solution.py:254
  5.2 1.5 %collective-permute-start.3 = (f32[18,32,128]{2,1,0:T(8,128)S(1)}, f32[18,32,128]{2,1,0:T(8,128)S(1)}, u32[]{:S(2)}, u32[]{:S(2)}) collective-permute-start(f32[18,32,128]{2,1,0:T(8,128)S(1)} %get-tuple-element.46), channel_id=1, source_target_pairs={{0,16},{8,24},{16,0},{24,8},{1,17},{9,25},{17,1},{25,9},{2,18},{10... | collective-permute-start | bytes 884744 | tf_op jit(solution)/shard_map/to_rows/ppermute | solution.py:254
  6.8 6.0 %collective-permute-start = (f32[4,12,16,128]{3,2,1,0:T(8,128)S(1)}, f32[4,12,16,128]{3,2,1,0:T(8,128)}, u32[]{:S(2)}, u32[]{:S(2)}) collective-permute-start(f32[4,12,16,128]{3,2,1,0:T(8,128)S(1)} %get-tuple-element.42), channel_id=1, source_target_pairs={{2,0},{4,2},{6,4},{0,6},{10,8},{12,10},{14,12},{8,14},{18,16},{20,... | collective-permute-start | bytes 1179656 | tf_op jit(solution)/shard_map/to_chip_before/ppermute | solution.py:248
  12.7 0.3 collective-permute-done.2.refs_1_
  13.1 4.2 %collective-permute-start.1 = (f32[4,12,16,128]{3,2,1,0:T(8,128)S(1)}, f32[4,12,16,128]{3,2,1,0:T(8,128)}, u32[]{:S(2)}, u32[]{:S(2)}) collective-permute-start(f32[4,12,16,128]{3,2,1,0:T(8,128)S(1)} %get-tuple-element.43), channel_id=1, source_target_pairs={{2,1},{4,3},{6,5},{0,7},{10,9},{12,11},{14,13},{8,15},{18,17},{20,... | collective-permute-start | bytes 1179656 | tf_op jit(solution)/shard_map/to_chip_before/ppermute | solution.py:248
  17.3 2.7 %collective-permute-done.3.refs_2_ = f32[18,32,128]{2,1,0:T(8,128)S(1)} collective-permute-done((f32[18,32,128]{2,1,0:T(8,128)S(1)}, f32[18,32,128]{2,1,0:T(8,128)S(1)}, u32[]{:S(2)}, u32[]{:S(2)}) %collective-permute-start.3) | collective-permute-done | bytes 294944 | tf_op jit(solution)/shard_map/to_rows/ppermute | solution.py:254
  20.0 0.5 collective-permute-start.7
  20.6 1.6 %collective-permute-done.1 = f32[4,12,16,128]{3,2,1,0:T(8,128)} collective-permute-done((f32[4,12,16,128]{3,2,1,0:T(8,128)S(1)}, f32[4,12,16,128]{3,2,1,0:T(8,128)}, u32[]{:S(2)}, u32[]{:S(2)}) %collective-permute-start.1) | collective-permute-done | bytes 393248 | tf_op jit(solution)/shard_map/to_chip_before/ppermute | solution.py:248
  22.2 0.2 collective-permute-done.8.refs_7_
  22.4 1.3 %select_bitcast_fusion = (f32[12,16,128]{2,1,0:T(8,128)S(1)}, f32[12,16,128]{2,1,0:T(8,128)S(1)}, f32[12,16,128]{2,1,0:T(8,128)S(1)}, f32[12,16,128]{2,1,0:T(8,128)S(1)}) fusion(f32[4,12,16,128]{3,2,1,0:T(8,128)} %collective-permute-done.1, f32[4,12,16,128]{3,2,1,0:T(8,128)} %collective-permute-done, pred[]{:T(512)S(6)} %eq.2), kind=kLoop, calls=%fused_computation.2 | loop fusion | flops 98304 | bytes 1179649 | tf_op jit(solution)/shard_map/next_to_rows/jit(_where)/select_n | solution.py:259
  23.7 2.3 %collective-permute-start.11 = (f32[12,16,128]{2,1,0:T(8,128)S(1)}, f32[12,16,128]{2,1,0:T(8,128)S(1)}, u32[]{:S(2)}, u32[]{:S(2)}) collective-permute-start(f32[12,16,128]{2,1,0:T(8,128)S(1)} %get-tuple-element.79), channel_id=1, source_target_pairs={{0,24},{8,16},{16,8},{24,0},{1,25},{9,17},{17,9},{25,1},{2,26},{10... | collective-permute-start | bytes 294920 | tf_op jit(solution)/shard_map/next_to_rows/ppermute | solution.py:260
  26.0 0.5 collective-permute-start.10
  26.5 0.7 %collective-permute-start.9 = (f32[12,16,128]{2,1,0:T(8,128)S(1)}, f32[12,16,128]{2,1,0:T(8,128)S(1)}, u32[]{:S(2)}, u32[]{:S(2)}) collective-permute-start(f32[12,16,128]{2,1,0:T(8,128)S(1)} %get-tuple-element.81), channel_id=1, source_target_pairs={{0,8},{8,0},{16,24},{24,16},{1,9},{9,1},{17,25},{25,17},{2,10},{10... | collective-permute-start | bytes 294920 | tf_op jit(solution)/shard_map/next_to_rows/ppermute | solution.py:260
  27.3 10.6 %inner_terms.2 = (f32[12,128,128]{2,1,0:T(8,128)S(1)}, f32[3072,128]{1,0:T(8,128)S(1)}, f32[9216,128]{1,0:T(8,128)S(1)}, bf16[3072,256]{1,0:T(8,128)(2,1)S(1)}, ...) custom-call(s32[3]{0:T(128)S(1)} %pad_add_fusion.where_ref, s32[2,2048]{1,0:T(2,128)S(1)} %bitcast.22, ...), custom_call_target="tpu_custom_call" | custom-call | flops 12000000000 | bytes 10000000 | tf_op jit(solution)/shard_map/inner_terms/pallas_call | solution.py:265
  38.0 6.6 %inner_terms.3 = (f32[256,128]{1,0:T(8,128)S(1)}, f32[256,128]{1,0:T(8,128)S(1)}) custom-call(s32[3]{0:T(128)S(1)} %pad_add_fusion.where_ref, s32[2,2048]{1,0:T(2,128)S(1)} %bitcast.23, f32[3072,128]{1,0:T(8,128)S(1)} %get-tuple-element.69.carry_ref, f32[9216,128]{1,0:T(8,128)S(1)} %get-tuple-element.70.slope_ref, ...), custom_call_target="tpu_custom_call" | custom-call | flops 8000000000 | bytes 10000000 | tf_op jit(solution)/shard_map/inner_terms/pallas_call | solution.py:285
  44.6 1.4 %edge_tables.1 = (f32[1024,128]{1,0:T(8,128)S(1)}, f32[3072,128]{1,0:T(8,128)S(1)}, bf16[3072,256]{1,0:T(8,128)(2,1)S(1)}) custom-call(s32[3]{0:T(128)S(1)} %pad_add_fusion.where_ref, f32[128,128]{1,0:T(8,128)S(1)} %copy-done.1, f32[12,16,128]{2,1,0:T(8,128)S(1)} %get-tuple-element.61.refs_0_, f32[12,16,128]{2,1,0:T(8,128)S(1)} %collective-permute-done.9.refs_1_, ...), custom_call_target="tpu_custom_call" | custom-call | tf_op jit(solution)/shard_map/edge_tables/pallas_call | solution.py:296
  46.1 3.4 %edge_terms.4 = f32[256,128]{1,0:T(8,128)S(1)} custom-call(s32[3]{0:T(128)S(1)} %pad_add_fusion.where_ref, s32[2,2048]{1,0:T(2,128)S(1)} %bitcast.24, f32[1024,128]{1,0:T(8,128)S(1)} %get-tuple-element.66.carry_ref, f32[3072,128]{1,0:T(8,128)S(1)} %get-tuple-element.67.slope_ref, bf16[3072,256]{1,0:T(8,128)(2,1)S(1)} %get-tuple-element.68.rhs_ref, ...), custom_call_target="tpu_custom_call" | custom-call | flops 4000000000 | bytes 10000000 | tf_op jit(solution)/shard_map/edge_terms/pallas_call | solution.py:311
  49.5 2.3 %collective-permute-start.13 = (f32[256,128]{1,0:T(8,128)S(1)}, f32[256,128]{1,0:T(8,128)S(1)}, u32[]{:S(2)}, u32[]{:S(2)}) collective-permute-start(f32[256,128]{1,0:T(8,128)S(1)} %edge_terms.4), channel_id=1, source_target_pairs={{0,24},{8,16},{16,8},{24,0},{1,25},{9,17},{17,9},{25,1},{2,26},{10... | collective-permute-start | bytes 393224 | tf_op jit(solution)/shard_map/sum_over_rows/ppermute | solution.py:322
  51.8 3.2 %edge_terms.5 = f32[256,128]{1,0:T(8,128)S(1)} custom-call(s32[3]{0:T(128)S(1)} %pad_add_fusion.where_ref, s32[2,2048]{1,0:T(2,128)S(1)} %bitcast.25, f32[1024,128]{1,0:T(8,128)S(1)} %get-tuple-element.66.carry_ref, f32[3072,128]{1,0:T(8,128)S(1)} %get-tuple-element.67.slope_ref, bf16[3072,256]{1,0:T(8,128)(2,1)S(1)} %get-tuple-element.68.rhs_ref, ...), custom_call_target="tpu_custom_call" | custom-call | flops 4000000000 | bytes 10000000 | tf_op jit(solution)/shard_map/edge_terms/pallas_call | solution.py:311
  55.0 0.6 collective-permute-start.14
  55.5 3.2 %edge_terms.6 = f32[256,128]{1,0:T(8,128)S(1)} custom-call(s32[3]{0:T(128)S(1)} %pad_add_fusion.where_ref, s32[2,2048]{1,0:T(2,128)S(1)} %bitcast.26, f32[1024,128]{1,0:T(8,128)S(1)} %get-tuple-element.66.carry_ref, f32[3072,128]{1,0:T(8,128)S(1)} %get-tuple-element.67.slope_ref, bf16[3072,256]{1,0:T(8,128)(2,1)S(1)} %get-tuple-element.68.rhs_ref, ...), custom_call_target="tpu_custom_call" | custom-call | flops 4000000000 | bytes 10000000 | tf_op jit(solution)/shard_map/edge_terms/pallas_call | solution.py:311
  58.7 0.8 %collective-permute-start.15 = (f32[256,128]{1,0:T(8,128)S(1)}, f32[256,128]{1,0:T(8,128)S(1)}, u32[]{:S(2)}, u32[]{:S(2)}) collective-permute-start(f32[256,128]{1,0:T(8,128)S(1)} %edge_terms.6), channel_id=1, source_target_pairs={{0,8},{8,0},{16,24},{24,16},{1,9},{9,1},{17,25},{25,17},{2,10},{10... | collective-permute-start | bytes 393224 | tf_op jit(solution)/shard_map/sum_over_rows/ppermute | solution.py:322
  59.5 3.2 %edge_terms.7 = f32[256,128]{1,0:T(8,128)S(1)} custom-call(s32[3]{0:T(128)S(1)} %pad_add_fusion.where_ref, s32[2,2048]{1,0:T(2,128)S(1)} %bitcast.27, f32[1024,128]{1,0:T(8,128)S(1)} %get-tuple-element.66.carry_ref, f32[3072,128]{1,0:T(8,128)S(1)} %get-tuple-element.67.slope_ref, bf16[3072,256]{1,0:T(8,128)(2,1)S(1)} %get-tuple-element.68.rhs_ref, ...), custom_call_target="tpu_custom_call" | custom-call | flops 4000000000 | bytes 10000000 | tf_op jit(solution)/shard_map/edge_terms/pallas_call | solution.py:311
  62.7 1.4 %collective-permute-done.15 = f32[256,128]{1,0:T(8,128)S(1)} collective-permute-done((f32[256,128]{1,0:T(8,128)S(1)}, f32[256,128]{1,0:T(8,128)S(1)}, u32[]{:S(2)}, u32[]{:S(2)}) %collective-permute-start.15) | collective-permute-done | bytes 131104 | tf_op jit(solution)/shard_map/sum_over_rows/ppermute | solution.py:322
  64.2 1.2 %collective-permute-start.16 = (f32[64,128]{1,0:T(8,128)S(1)}, f32[64,128]{1,0:T(8,128)S(1)}, u32[]{:S(2)}, u32[]{:S(2)}) collective-permute-start(f32[64,128]{1,0:T(8,128)S(1)} %get-tuple-element.83), channel_id=1, source_target_pairs={{0,2},{1,3},{2,4},{3,5},{4,6},{5,7},{6,0},{7,1},{8,10},{9,11},{10,... | collective-permute-start | bytes 98312 | tf_op jit(solution)/shard_map/sum_over_chips/ppermute | solution.py:335
  65.3 2.7 %collective-permute-start.18 = (f32[64,128]{1,0:T(8,128)S(1)}, f32[64,128]{1,0:T(8,128)S(1)}, u32[]{:S(2)}, u32[]{:S(2)}) collective-permute-start(f32[64,128]{1,0:T(8,128)S(1)} %get-tuple-element.84), channel_id=1, source_target_pairs={{0,6},{1,7},{2,0},{3,1},{4,2},{5,3},{6,4},{7,5},{8,14},{9,15},{10,... | collective-permute-start | bytes 98312 | tf_op jit(solution)/shard_map/sum_over_chips/ppermute | solution.py:335
  68.1 0.3 collective-permute-start.17
  68.4 1.6 %collective-permute-done.16 = f32[64,128]{1,0:T(8,128)S(1)} collective-permute-done((f32[64,128]{1,0:T(8,128)S(1)}, f32[64,128]{1,0:T(8,128)S(1)}, u32[]{:S(2)}, u32[]{:S(2)}) %collective-permute-start.16) | collective-permute-done | bytes 32800 | tf_op jit(solution)/shard_map/sum_over_chips/ppermute | solution.py:335
  69.9 2.9 %collective-permute-done.17 = f32[64,128]{1,0:T(8,128)S(1)} collective-permute-done((f32[64,128]{1,0:T(8,128)S(1)}, f32[64,128]{1,0:T(8,128)S(1)}, u32[]{:S(2)}, u32[]{:S(2)}) %collective-permute-start.17) | collective-permute-done | bytes 32800 | tf_op jit(solution)/shard_map/sum_over_chips/ppermute | solution.py:335
  72.9 0.6 fusion.2
  (26 shorter events, 0.3 us)
Async XLA Ops:
  0.0 27.3 %copy-start.2 = (s32[2048,2]{0,1:T(2,128)S(1)}, s32[2048,2]{0,1:T(2,128)}, u32[]{:S(2)}) copy-start(s32[2048,2]{0,1:T(2,128)} %param.5) | copy-start | bytes 49156
  0.1 1.1 %copy-start = (f32[32,3,1,16,128]{4,3,2,1,0:T(8,128)S(1)}, f32[32,3,1,16,128]{4,3,2,1,0:T(8,128)}, u32[]{:S(2)}) copy-start(f32[32,3,1,16,128]{4,3,2,1,0:T(8,128)} %param.3) | copy-start | bytes 2359300
  1.2 26.1 %copy-start.1 = (f32[128,128]{1,0:T(8,128)S(1)}, f32[128,128]{1,0:T(8,128)}, u32[]{:S(2)}) copy-start(f32[128,128]{1,0:T(8,128)} %coeffs_ref.3) | copy-start | bytes 196612
  2.2 10.8 %collective-permute-start.2 = (f32[18,32,128]{2,1,0:T(8,128)S(1)}, f32[18,32,128]{2,1,0:T(8,128)S(1)}, u32[]{:S(2)}, u32[]{:S(2)}) collective-permute-start(f32[18,32,128]{2,1,0:T(8,128)S(1)} %get-tuple-element.45), channel_id=1, source_target_pairs={{0,8},{8,0},{16,24},{24,16},{1,9},{9,1},{17,25},{25,17},{2,10},{10... | collective-permute-start | bytes 884744 | tf_op jit(solution)/shard_map/to_rows/ppermute | solution.py:254
  5.2 14.8 %collective-permute-start.3 = (f32[18,32,128]{2,1,0:T(8,128)S(1)}, f32[18,32,128]{2,1,0:T(8,128)S(1)}, u32[]{:S(2)}, u32[]{:S(2)}) collective-permute-start(f32[18,32,128]{2,1,0:T(8,128)S(1)} %get-tuple-element.46), channel_id=1, source_target_pairs={{0,16},{8,24},{16,0},{24,8},{1,17},{9,25},{17,1},{25,9},{2,18},{10... | collective-permute-start | bytes 884744 | tf_op jit(solution)/shard_map/to_rows/ppermute | solution.py:254
  6.7 13.3 %collective-permute-start.4 = (f32[18,32,128]{2,1,0:T(8,128)S(1)}, f32[18,32,128]{2,1,0:T(8,128)S(1)}, u32[]{:S(2)}, u32[]{:S(2)}) collective-permute-start(f32[18,32,128]{2,1,0:T(8,128)S(1)} %get-tuple-element.47), channel_id=1, source_target_pairs={{0,24},{8,16},{16,8},{24,0},{1,25},{9,17},{17,9},{25,1},{2,26},{10... | collective-permute-start | bytes 884744 | tf_op jit(solution)/shard_map/to_rows/ppermute | solution.py:254
  6.8 13.8 %collective-permute-start.5 = (f32[18,32,128]{2,1,0:T(8,128)S(1)}, f32[18,32,128]{2,1,0:T(8,128)S(1)}, u32[]{:S(2)}, u32[]{:S(2)}) collective-permute-start(f32[18,32,128]{2,1,0:T(8,128)S(1)} %get-tuple-element.50.refs_0_), channel_id=1, source_target_pairs={{0,1},{1,0},{2,3},{3,2},{4,5},{5,4},{6,7},{7,6},{8,9},{9,8},{10,11... | collective-permute-start | bytes 884744 | tf_op jit(solution)/shard_map/to_other_core/ppermute | solution.py:256
  6.8 13.8 %collective-permute-start = (f32[4,12,16,128]{3,2,1,0:T(8,128)S(1)}, f32[4,12,16,128]{3,2,1,0:T(8,128)}, u32[]{:S(2)}, u32[]{:S(2)}) collective-permute-start(f32[4,12,16,128]{3,2,1,0:T(8,128)S(1)} %get-tuple-element.42), channel_id=1, source_target_pairs={{2,0},{4,2},{6,4},{0,6},{10,8},{12,10},{14,12},{8,14},{18,16},{20,... | collective-permute-start | bytes 1179656 | tf_op jit(solution)/shard_map/to_chip_before/ppermute | solution.py:248
  13.1 9.2 %collective-permute-start.1 = (f32[4,12,16,128]{3,2,1,0:T(8,128)S(1)}, f32[4,12,16,128]{3,2,1,0:T(8,128)}, u32[]{:S(2)}, u32[]{:S(2)}) collective-permute-start(f32[4,12,16,128]{3,2,1,0:T(8,128)S(1)} %get-tuple-element.43), channel_id=1, source_target_pairs={{2,1},{4,3},{6,5},{0,7},{10,9},{12,11},{14,13},{8,15},{18,17},{20,... | collective-permute-start | bytes 1179656 | tf_op jit(solution)/shard_map/to_chip_before/ppermute | solution.py:248
  20.0 2.2 %collective-permute-start.6 = (f32[18,32,128]{2,1,0:T(8,128)S(1)}, f32[18,32,128]{2,1,0:T(8,128)S(1)}, u32[]{:S(2)}, u32[]{:S(2)}) collective-permute-start(f32[18,32,128]{2,1,0:T(8,128)S(1)} %collective-permute-done.2.refs_1_), channel_id=1, source_target_pairs={{0,1},{1,0},{2,3},{3,2},{4,5},{5,4},{6,7},{7,6},{8,9},{9,8},{10,11... | collective-permute-start | bytes 884744 | tf_op jit(solution)/shard_map/to_other_core/ppermute | solution.py:256
  20.0 2.2 %collective-permute-start.7 = (f32[18,32,128]{2,1,0:T(8,128)S(1)}, f32[18,32,128]{2,1,0:T(8,128)S(1)}, u32[]{:S(2)}, u32[]{:S(2)}) collective-permute-start(f32[18,32,128]{2,1,0:T(8,128)S(1)} %collective-permute-done.3.refs_2_), channel_id=1, source_target_pairs={{0,1},{1,0},{2,3},{3,2},{4,5},{5,4},{6,7},{7,6},{8,9},{9,8},{10,11... | collective-permute-start | bytes 884744 | tf_op jit(solution)/shard_map/to_other_core/ppermute | solution.py:256
  20.5 1.9 %collective-permute-start.8 = (f32[18,32,128]{2,1,0:T(8,128)S(1)}, f32[18,32,128]{2,1,0:T(8,128)S(1)}, u32[]{:S(2)}, u32[]{:S(2)}) collective-permute-start(f32[18,32,128]{2,1,0:T(8,128)S(1)} %collective-permute-done.4.refs_3_), channel_id=1, source_target_pairs={{0,1},{1,0},{2,3},{3,2},{4,5},{5,4},{6,7},{7,6},{8,9},{9,8},{10,11... | collective-permute-start | bytes 884744 | tf_op jit(solution)/shard_map/to_other_core/ppermute | solution.py:256
  23.7 14.2 %collective-permute-start.11 = (f32[12,16,128]{2,1,0:T(8,128)S(1)}, f32[12,16,128]{2,1,0:T(8,128)S(1)}, u32[]{:S(2)}, u32[]{:S(2)}) collective-permute-start(f32[12,16,128]{2,1,0:T(8,128)S(1)} %get-tuple-element.79), channel_id=1, source_target_pairs={{0,24},{8,16},{16,8},{24,0},{1,25},{9,17},{17,9},{25,1},{2,26},{10... | collective-permute-start | bytes 294920 | tf_op jit(solution)/shard_map/next_to_rows/ppermute | solution.py:260
  26.0 11.9 %collective-permute-start.10 = (f32[12,16,128]{2,1,0:T(8,128)S(1)}, f32[12,16,128]{2,1,0:T(8,128)S(1)}, u32[]{:S(2)}, u32[]{:S(2)}) collective-permute-start(f32[12,16,128]{2,1,0:T(8,128)S(1)} %get-tuple-element.80), channel_id=1, source_target_pairs={{0,16},{8,24},{16,0},{24,8},{1,17},{9,25},{17,1},{25,9},{2,18},{10... | collective-permute-start | bytes 294920 | tf_op jit(solution)/shard_map/next_to_rows/ppermute | solution.py:260
  26.5 11.4 %collective-permute-start.9 = (f32[12,16,128]{2,1,0:T(8,128)S(1)}, f32[12,16,128]{2,1,0:T(8,128)S(1)}, u32[]{:S(2)}, u32[]{:S(2)}) collective-permute-start(f32[12,16,128]{2,1,0:T(8,128)S(1)} %get-tuple-element.81), channel_id=1, source_target_pairs={{0,8},{8,0},{16,24},{24,16},{1,9},{9,1},{17,25},{25,17},{2,10},{10... | collective-permute-start | bytes 294920 | tf_op jit(solution)/shard_map/next_to_rows/ppermute | solution.py:260
  38.0 6.7 %collective-permute-start.12 = (f32[4,12,16,128]{3,2,1,0:T(8,128)S(1)}, f32[4,12,16,128]{3,2,1,0:T(8,128)S(1)}, u32[]{:S(2)}, u32[]{:S(2)}) collective-permute-start(f32[4,12,16,128]{3,2,1,0:T(8,128)S(1)} %pad_maximum_fusion), channel_id=1, source_target_pairs={{0,1},{1,0},{2,3},{3,2},{4,5},{5,4},{6,7},{7,6},{8,9},{9,8},{10,11... | collective-permute-start | bytes 1179656 | tf_op jit(solution)/shard_map/next_to_other_core/ppermute | solution.py:283
  49.5 14.7 %collective-permute-start.13 = (f32[256,128]{1,0:T(8,128)S(1)}, f32[256,128]{1,0:T(8,128)S(1)}, u32[]{:S(2)}, u32[]{:S(2)}) collective-permute-start(f32[256,128]{1,0:T(8,128)S(1)} %edge_terms.4), channel_id=1, source_target_pairs={{0,24},{8,16},{16,8},{24,0},{1,25},{9,17},{17,9},{25,1},{2,26},{10... | collective-permute-start | bytes 393224 | tf_op jit(solution)/shard_map/sum_over_rows/ppermute | solution.py:322
  55.0 9.2 %collective-permute-start.14 = (f32[256,128]{1,0:T(8,128)S(1)}, f32[256,128]{1,0:T(8,128)S(1)}, u32[]{:S(2)}, u32[]{:S(2)}) collective-permute-start(f32[256,128]{1,0:T(8,128)S(1)} %edge_terms.5), channel_id=1, source_target_pairs={{0,16},{8,24},{16,0},{24,8},{1,17},{9,25},{17,1},{25,9},{2,18},{10... | collective-permute-start | bytes 393224 | tf_op jit(solution)/shard_map/sum_over_rows/ppermute | solution.py:322
  58.7 5.4 %collective-permute-start.15 = (f32[256,128]{1,0:T(8,128)S(1)}, f32[256,128]{1,0:T(8,128)S(1)}, u32[]{:S(2)}, u32[]{:S(2)}) collective-permute-start(f32[256,128]{1,0:T(8,128)S(1)} %edge_terms.6), channel_id=1, source_target_pairs={{0,8},{8,0},{16,24},{24,16},{1,9},{9,1},{17,25},{25,17},{2,10},{10... | collective-permute-start | bytes 393224 | tf_op jit(solution)/shard_map/sum_over_rows/ppermute | solution.py:322
  64.2 5.8 %collective-permute-start.16 = (f32[64,128]{1,0:T(8,128)S(1)}, f32[64,128]{1,0:T(8,128)S(1)}, u32[]{:S(2)}, u32[]{:S(2)}) collective-permute-start(f32[64,128]{1,0:T(8,128)S(1)} %get-tuple-element.83), channel_id=1, source_target_pairs={{0,2},{1,3},{2,4},{3,5},{4,6},{5,7},{6,0},{7,1},{8,10},{9,11},{10,... | collective-permute-start | bytes 98312 | tf_op jit(solution)/shard_map/sum_over_chips/ppermute | solution.py:335
  65.3 4.6 %collective-permute-start.18 = (f32[64,128]{1,0:T(8,128)S(1)}, f32[64,128]{1,0:T(8,128)S(1)}, u32[]{:S(2)}, u32[]{:S(2)}) collective-permute-start(f32[64,128]{1,0:T(8,128)S(1)} %get-tuple-element.84), channel_id=1, source_target_pairs={{0,6},{1,7},{2,0},{3,1},{4,2},{5,3},{6,4},{7,5},{8,14},{9,15},{10,... | collective-permute-start | bytes 98312 | tf_op jit(solution)/shard_map/sum_over_chips/ppermute | solution.py:335
  68.1 4.8 %collective-permute-start.17 = (f32[64,128]{1,0:T(8,128)S(1)}, f32[64,128]{1,0:T(8,128)S(1)}, u32[]{:S(2)}, u32[]{:S(2)}) collective-permute-start(f32[64,128]{1,0:T(8,128)S(1)} %get-tuple-element.85), channel_id=1, source_target_pairs={{0,4},{1,5},{2,6},{3,7},{4,0},{5,1},{6,2},{7,3},{8,12},{9,13},{10,... | collective-permute-start | bytes 98312 | tf_op jit(solution)/shard_map/sum_over_chips/ppermute | solution.py:335

commit v5 on v4

--- a/solution.py
+++ b/solution.py
@@ -19,8 +19,8 @@
 
 def pack_kernel(where_ref, field_ref, *out_refs, sizes):
     local_s, rows_y, block_rows, tm_count = sizes
-    t = where_ref[0]
-    half_s = local_s // 2
+    t, core = where_ref[0], where_ref[2]
+    half = block_rows // 2
     for peer in range(tm_count):
         first_row = jnp.bitwise_xor(t, peer) * block_rows
         for row in range(block_rows + 2):
@@ -32,12 +32,10 @@
                 y = jnp.clip(y, 0, rows_y - 1)
             for c in range(3):
                 slab = field_ref[pl.ds(c * rows_y + y, local_s, stride=3 * rows_y), :]
-                if row < block_rows:
-                    for part in range(2):
-                        out_refs[tm_count + part][peer, row * 3 + c] = slab[part * half_s : (part + 1) * half_s]
-                else:
+                if row >= block_rows:
                     slab = jnp.where(inside, slab, 0.0)
                 out_refs[peer][row * 3 + c] = slab
+        out_refs[tm_count][peer] = out_refs[peer][pl.ds(core * (half * 3), half * 3)]
 
 
 def mode_weights(where_ref, coeffs_ref, local_s, tm_count):
@@ -65,36 +63,44 @@
     rhs_ref[place * lanes : (place + 1) * lanes, modes : 2 * modes] = low
 
 
-def project(conv_ref, lhs_ref, rhs_ref, block, places, lanes):
-    for place in range(places):
-        values = conv_ref[pl.ds(place, block, stride=places), :]
-        high, low = split_high_low(values)
-        lhs_ref[0:block, place * lanes : (place + 1) * lanes] = high
-        lhs_ref[block : 2 * block, place * lanes : (place + 1) * lanes] = low
-    both = jnp.dot(lhs_ref[...], rhs_ref[...], preferred_element_type=F32)
+def project(conv_ref, rhs_ref, block, places, lanes):
+    both = None
+    for place in range(0, places, 2):
+        highs, lows = zip(
+            *(split_high_low(conv_ref[pl.ds(place + k, block, stride=places), :]) for k in range(2))
+        )
+        lhs = jnp.concatenate([jnp.concatenate(highs, axis=1), jnp.concatenate(lows, axis=1)], axis=0)
+        part = jnp.dot(lhs, rhs_ref[place * lanes : (place + 2) * lanes, :], preferred_element_type=F32)
+        both = part if both is None else both + part
     modes = both.shape[1] // 2
     return (both[:block, :modes] + both[:block, modes:]) + (both[block:, :modes] + both[block:, modes:])
 
 
-def for_pairs_of(where_ref, pairs_ref, peer, sizes, one_pair):
-    chips, share = sizes
+def for_pairs_of(where_ref, codes_ref, peer, sizes, one_pair):
+    chips, share, bits = sizes
     t, chip, core = where_ref[0], where_ref[1], where_ref[2]
-    to_t = jnp.bitwise_xor(t, peer)
-    for ahead in range(chips):
-        base = ((to_t * chips + lax.rem(chip + ahead, chips)) * 2 + core) * share
+    first_chip = jnp.bitwise_xor(t, peer) * chips
+
+    def one_share(ahead, _):
+        to_chip = chip + ahead
+        to_chip = jnp.where(to_chip >= chips, to_chip - chips, to_chip)
+        base = ((first_chip + to_chip) * 2 + core) * share
 
         def one(q, _):
-            one_pair(ahead * share + q, pairs_ref[0, base + q], pairs_ref[1, base + q])
+            code = codes_ref[base + q]
+            one_pair(ahead * share + q, lax.shift_right_logical(code, bits), jnp.bitwise_and(code, 2**bits - 1))
             return 0
 
-        lax.fori_loop(0, share, one, 0, unroll=16)
-
-
-def inner_kernel(where_ref, pairs_ref, coeffs_ref, *refs, peers, sizes):
-    local_s, block_rows, tm_count, chips, share = sizes
+        return lax.fori_loop(0, share, one, 0, unroll=32)
+
+    lax.fori_loop(0, chips, one_share, 0)
+
+
+def inner_kernel(where_ref, codes_ref, coeffs_ref, *refs, peers, sizes):
+    local_s, block_rows, tm_count, chips, share, bits = sizes
     own, other = refs[:tm_count], refs[tm_count : 2 * tm_count]
     near_ref, carry_ref, slope_ref, rhs_ref = refs[2 * tm_count : 2 * tm_count + 4]
-    *out_refs, slab_ref, conv_ref, lhs_ref = refs[2 * tm_count + 4 :]
+    *out_refs, slab_ref, conv_ref = refs[2 * tm_count + 4 :]
     core = where_ref[2]
     modes, lanes = coeffs_ref.shape[1], own[0].shape[2]
     height = 2 * block_rows
@@ -128,18 +134,18 @@
                 for d, slope in enumerate((stream, normal, span)):
                     slope_ref[pl.ds((d * 3 + c) * height + place, modes, stride=9 * height), :] = slope
                 store_projection(rhs_ref, c * height + place, value)
-                if plane == 1:
+                if (plane == 1) == (row < block_rows // 2):
                     near_ref[center] = value
 
     pairs_kernel(
-        where_ref, pairs_ref, carry_ref, slope_ref, rhs_ref, *out_refs, conv_ref, lhs_ref,
-        peers=peers, sizes=(height, chips, share),
+        where_ref, codes_ref, carry_ref, slope_ref, rhs_ref, *out_refs, conv_ref,
+        peers=peers, sizes=(height, chips, share, bits),
     )
 
 
-def pairs_kernel(where_ref, pairs_ref, carry_ref, slope_ref, rhs_ref, *refs, peers, sizes):
-    *out_refs, conv_ref, lhs_ref = refs
-    height, chips, share = sizes
+def pairs_kernel(where_ref, codes_ref, carry_ref, slope_ref, rhs_ref, *refs, peers, sizes):
+    *out_refs, conv_ref = refs
+    height, chips, share, bits = sizes
 
     def one_pair(slot, i, j):
         carry = carry_ref[pl.ds(pl.multiple_of(i * (3 * height), 8), 3 * height), :]
@@ -154,8 +160,8 @@
         conv_ref[pl.ds(pl.multiple_of(slot * (3 * height), 8), 3 * height), :] = jnp.concatenate(rows, axis=0)
 
     for peer, out_ref in zip(peers, out_refs):
-        for_pairs_of(where_ref, pairs_ref, peer, (chips, share), one_pair)
-        out_ref[...] = project(conv_ref, lhs_ref, rhs_ref, chips * share, 3 * height, conv_ref.shape[1])
+        for_pairs_of(where_ref, codes_ref, peer, (chips, share, bits), one_pair)
+        out_ref[...] = project(conv_ref, rhs_ref, chips * share, 3 * height, conv_ref.shape[1])
 
 
 def far_kernel(where_ref, coeffs_ref, *refs, sizes):
@@ -165,30 +171,28 @@
     is_first = where_ref[2] == 0
     modes, lanes = near_ref.shape[1:]
     height = 2 * block_rows
+    half = block_rows // 2 * 3
     weights = mode_weights(where_ref, coeffs_ref, local_s, tm_count)
-    for pair in range(3 * block_rows // 2):
-        slabs = []
-        for slab in (2 * pair, 2 * pair + 1):
-            halves = []
-            for peer in range(tm_count):
-                mine, theirs = next_own[peer][slab], next_other[peer, slab]
-                halves += [jnp.where(is_first, mine, theirs), jnp.where(is_first, theirs, mine)]
-            slabs.append(jnp.concatenate(halves, axis=0))
-        result = modes_of(weights, jnp.concatenate(slabs, axis=1))
-        for part in range(2):
-            row, c = divmod(2 * pair + part, 3)
-            near, far = near_ref[2 * pair + part], result[:, part * lanes : (part + 1) * lanes]
-            for place, value, across in ((row, near, far * 0.5), (block_rows + row, far, near * -0.5)):
+    for slab in range(half):
+        mine = jnp.concatenate([next_own[peer][slab] for peer in range(tm_count)], axis=0)
+        theirs = jnp.concatenate([next_other[peer, slab] for peer in range(tm_count)], axis=0)
+        after, before = jnp.where(is_first, theirs, mine), jnp.where(is_first, mine, theirs)
+        result = modes_of(weights, jnp.concatenate([after, before], axis=1))
+        row, c = divmod(slab, 3)
+        edges = ((near_ref[slab], result[:, :lanes]), (result[:, lanes:], near_ref[half + slab]))
+        for number, (low, high) in enumerate(edges):
+            place = number * block_rows + 2 * row
+            for at, value, across in ((place, low, high * 0.5), (place + 1, high, low * -0.5)):
                 if c == 0:
-                    carry_ref[pl.ds(place, modes, stride=height), :] = value
-                slope_ref[pl.ds(c * height + place, modes, stride=3 * height), :] = across
-                store_projection(rhs_ref, c * height + place, value)
+                    carry_ref[pl.ds(at, modes, stride=height), :] = value
+                slope_ref[pl.ds(c * height + at, modes, stride=3 * height), :] = across
+                store_projection(rhs_ref, c * height + at, value)
 
 
 def edge_kernel(
-    where_ref, pairs_ref, carry_ref, slope_ref, rhs_ref, inner_ref, out_ref, conv_ref, lhs_ref, *, peer, sizes
+    where_ref, codes_ref, carry_ref, slope_ref, rhs_ref, inner_ref, out_ref, conv_ref, *, peer, sizes
 ):
-    chips, share = sizes
+    chips, share, _ = sizes
     modes, lanes = out_ref.shape[1], carry_ref.shape[1]
     height = carry_ref.shape[0] // modes
 
@@ -198,8 +202,8 @@
         rows = [carry * slope[c * height : (c + 1) * height] for c in range(3)]
         conv_ref[pl.ds(pl.multiple_of(slot * (3 * height), 8), 3 * height), :] = jnp.concatenate(rows, axis=0)
 
-    for_pairs_of(where_ref, pairs_ref, peer, sizes, one_pair)
-    out_ref[...] = inner_ref[...] + project(conv_ref, lhs_ref, rhs_ref, chips * share, 3 * height, lanes)
+    for_pairs_of(where_ref, codes_ref, peer, sizes, one_pair)
+    out_ref[...] = inner_ref[...] + project(conv_ref, rhs_ref, chips * share, 3 * height, lanes)
 
 
 def vmem_limit(mebibytes):
@@ -221,10 +225,11 @@
     block_rows = rows_y // tm_count
     share = pair_table.shape[0] // (tm_count * space_count)
     factor = float(space_count * rows_y * lanes) ** (-0.5)
-    pairs = pair_table.T
+    bits = modes.bit_length() - 1
+    assert modes == 2**bits
+    codes = pair_table[:, 0] * modes + pair_table[:, 1]
     smem = pl.BlockSpec(memory_space=pltpu.SMEM)
     vmem = pl.BlockSpec(memory_space=pltpu.VMEM)
-    half_s = local_s // 2
     block = chips * share
     height = 2 * block_rows
     depth = 3 * height * lanes
@@ -238,32 +243,28 @@
         packed = pl.pallas_call(
             functools.partial(pack_kernel, sizes=(local_s, rows_y, block_rows, tm_count)),
             out_shape=[pltpu.VMEM(((block_rows + 2) * 3, local_s, lanes), F32)] * tm_count
-            + [pltpu.VMEM((tm_count, block_rows * 3, half_s, lanes), F32)] * 2,
+            + [pltpu.VMEM((tm_count, block_rows // 2 * 3, local_s, lanes), F32)],
             in_specs=[smem, vmem],
-            out_specs=[vmem] * (tm_count + 2),
+            out_specs=[vmem] * (tm_count + 1),
             compiler_params=vmem_limit(16),
         )(where, snapshots.reshape(-1, lanes))
-    with jax.named_scope("to_chip_before"):
-        ahead = [
-            lax.ppermute(
-                packed[tm_count + c], "space", [(2 * ((chip + 1) % chips), 2 * chip + c) for chip in range(chips)]
-            )
-            for c in range(2)
-        ]
+    with jax.named_scope("to_next_plane"):
+        ring = [(place, (place + (1 if place % 2 else -1)) % space_count) for place in range(space_count)]
+        across_edge = lax.ppermute(packed[tm_count], "space", ring)
     with jax.named_scope("to_rows"):
         own = [packed[0]] + [lax.ppermute(packed[peer], "tm", across(peer)) for peer in range(1, tm_count)]
     with jax.named_scope("to_other_core"):
         other = [lax.ppermute(piece, "space", swap) for piece in own]
     with jax.named_scope("next_to_rows"):
-        ahead, own, other = lax.optimization_barrier((ahead, own, other))
-        parts = [jnp.where(core == 0, ahead[0][peer], ahead[1][peer]) for peer in range(tm_count)]
+        across_edge, own, other = lax.optimization_barrier((across_edge, own, other))
+        parts = [across_edge[peer] for peer in range(tm_count)]
         next_own = [parts[0]] + [lax.ppermute(parts[peer], "tm", across(peer)) for peer in range(1, tm_count)]
     early, late = range(tm_count - 1, tm_count // 2 - 1, -1), range(tm_count // 2 - 1, -1, -1)
-    work = [pltpu.VMEM((block * 3 * height, lanes), F32), pltpu.VMEM((2 * block, depth), BF16)]
+    work = [pltpu.VMEM((block * 3 * height, lanes), F32)]
     group = pltpu.VMEM((block, modes), F32)
     with jax.named_scope("inner_terms"):
         near, *inner_tables_and_early = pl.pallas_call(
-            functools.partial(inner_kernel, peers=early, sizes=(local_s, block_rows, tm_count, chips, share)),
+            functools.partial(inner_kernel, peers=early, sizes=(local_s, block_rows, tm_count, chips, share, bits)),
             out_shape=[
                 pltpu.VMEM((block_rows * 3, modes, lanes), F32),
                 pltpu.VMEM((modes * 3 * height, lanes), F32),
@@ -276,21 +277,21 @@
             scratch_shapes=[pltpu.VMEM((2, (block_rows + 2) * 3, modes, lanes), F32)] + work,
             compiler_params=vmem_limit(24),
             cost_estimate=pl.CostEstimate(flops=12 * 10**9, bytes_accessed=10**7, transcendentals=0),
-        )(where, pairs, coeffs, *[in_vmem(piece) for piece in (*own, *other)])
+        )(where, codes, coeffs, *[in_vmem(piece) for piece in (*own, *other)])
         inner_tables, early_sums = inner_tables_and_early[:3], inner_tables_and_early[3:]
     with jax.named_scope("next_to_other_core"):
         next_own, inner_tables = lax.optimization_barrier((next_own, inner_tables))
         next_other = lax.ppermute(jnp.stack(next_own), "space", swap)
     with jax.named_scope("inner_terms"):
         late_sums = pl.pallas_call(
-            functools.partial(pairs_kernel, peers=late, sizes=(height, chips, share)),
+            functools.partial(pairs_kernel, peers=late, sizes=(height, chips, share, bits)),
             out_shape=[group] * len(late),
             in_specs=[smem, smem] + [vmem] * 3,
             out_specs=[vmem] * len(late),
             scratch_shapes=work,
             compiler_params=vmem_limit(16),
             cost_estimate=pl.CostEstimate(flops=8 * 10**9, bytes_accessed=10**7, transcendentals=0),
-        )(where, pairs, *[in_vmem(table) for table in inner_tables])
+        )(where, codes, *[in_vmem(table) for table in inner_tables])
         inner = [*reversed(late_sums), *reversed(early_sums)]
     with jax.named_scope("edge_tables"):
         tables = pl.pallas_call(
@@ -309,14 +310,14 @@
     for peer in reversed(range(tm_count)):
         with jax.named_scope("edge_terms"):
             sums[peer] = pl.pallas_call(
-                functools.partial(edge_kernel, peer=peer, sizes=(chips, share)),
+                functools.partial(edge_kernel, peer=peer, sizes=(chips, share, bits)),
                 out_shape=group,
                 in_specs=[smem, smem] + [vmem] * 4,
                 out_specs=vmem,
                 scratch_shapes=work,
                 compiler_params=vmem_limit(16),
                 cost_estimate=pl.CostEstimate(flops=4 * 10**9, bytes_accessed=10**7, transcendentals=0),
-            )(where, pairs, *[in_vmem(table) for table in (*tables, inner[peer])])
+            )(where, codes, *[in_vmem(table) for table in (*tables, inner[peer])])
         with jax.named_scope("sum_over_rows"):
             if peer:
                 arrived.append(lax.ppermute(sums[peer], "tm", across(peer)))

time: 73.7 us -> 67.3 us (0.913)
  starting transfers between devices: 26.8 us -> 21.2 us
  Pallas kernels: 32.6 us -> 27.5 us
  waiting for transfers between devices: 10.8 us -> 15.5 us
    ppermute x3, waiting for transfers between devices: 3.04 us -> 9.07 us  [shards(): lax.ppermute(packed[peer], 'tm', across(peer))]
    ppermute x2 -> x1, starting transfers between devices: 10.2 us -> 4.17 us  [shards(): across_edge = lax.ppermute(packed[tm_count], 'space', ring)]
    pallas_call x4, Pallas kernels: 12.9 us -> 9.81 us  [shards(): pl.pallas_call(functools.partial(edge_kernel, peer=peer, sizes=(chips, sh...]
    ppermute x2 -> x1, waiting for transfers between devices: 1.62 us -> 0.01 us  [shards(): across_edge = lax.ppermute(packed[tm_count], 'space', ring)]
    select_n x1 -> x0, other arithmetic: 1.26 us -> none  [shards(): jnp.where(core == 0, ahead[0][peer], ahead[1][peer])]
    pallas_call x1, Pallas kernels: 6.58 us -> 5.62 us  [shards(): pl.pallas_call(functools.partial(pairs_kernel, peers=late, sizes=(height,...]
    pallas_call x1, Pallas kernels: 10.6 us -> 9.71 us  [shards(): pl.pallas_call(functools.partial(inner_kernel, peers=early, sizes=(local_...]
    add x0 -> x1, other arithmetic: none -> 0.81 us  [shards(): codes = pair_table[:, 0] * modes + pair_table[:, 1]]
  transfers between devices with their start and end apart: 19 -> 18, of which waited for: 7 -> 7; matrix products, arithmetic and copies ran while one was open for 0% -> 1% of each run, Pallas kernels for 36% -> 34%
where the time goes in v5:
time: 67.3 us; the launch traced here: 67.1 us
  Pallas kernels  27.5 us (41%)
  starting transfers between devices  21.2 us (32%)
  waiting for transfers between devices  15.5 us (23%)
  other arithmetic  1.56 us (2%)
  local copies, waits for them, and re-layouts  1.17 us (2%)
    pallas_call x4, Pallas kernels, shards(): pl.pallas_call(functools.partial(edge_kernel, peer=peer, sizes=(chips, sh...  9.81 us
    pallas_call x1, Pallas kernels, shards(): pl.pallas_call(functools.partial(inner_kernel, peers=early, sizes=(local_...  9.71 us
    ppermute x3, waiting for transfers between devices, shards(): lax.ppermute(packed[peer], 'tm', across(peer))  9.07 us
    pallas_call x1, Pallas kernels, shards(): pl.pallas_call(functools.partial(pairs_kernel, peers=late, sizes=(height,...  5.62 us
    ppermute x3, starting transfers between devices, shards(): result = result + lax.ppermute(shares[step], 'space', shift)  4.67 us
    ppermute x3, starting transfers between devices, shards(): lax.ppermute(packed[peer], 'tm', across(peer))  4.54 us
    ppermute x1, starting transfers between devices, shards(): across_edge = lax.ppermute(packed[tm_count], 'space', ring)  4.17 us
    ppermute x3, waiting for transfers between devices, shards(): result = result + lax.ppermute(shares[step], 'space', shift)  4.02 us
  transfers between devices with their start and end apart: 18, of which 7 were waited for; matrix products, arithmetic and copies ran while one was open for 1% of the time, Pallas kernels for 34%

profile of v5, /device:TPU:0, one launch (start us, length us, event | category | flops | bytes accessed | tf_op | source)
XLA Modules:
  0.0 67.1 jit_solution(12442028992696194400)
XLA Ops:
  0.0 0.1 pad_add_fusion.where_ref
  0.1 1.1 %copy-done = f32[32,3,1,16,128]{4,3,2,1,0:T(8,128)S(1)} copy-done((f32[32,3,1,16,128]{4,3,2,1,0:T(8,128)S(1)}, f32[32,3,1,16,128]{4,3,2,1,0:T(8,128)}, u32[]{:S(2)}) %copy-start) | copy-done | bytes 786456
  1.2 1.0 %pack.1 = (f32[18,32,128]{2,1,0:T(8,128)S(1)}, f32[18,32,128]{2,1,0:T(8,128)S(1)}, f32[18,32,128]{2,1,0:T(8,128)S(1)}, f32[18,32,128]{2,1,0:T(8,128)S(1)}, f32[4,6,32,128]{3,2,1,0:T(8,128)S(1)}) custom-call(s32[3]{0:T(128)S(1)} %pad_add_fusion.where_ref, f32[1536,128]{1,0:T(8,128)S(1)} %bitcast.18), custom_call_target="tpu_custom_call" | custom-call | tf_op jit(solution)/shard_map/pack/pallas_call | solution.py:243
  2.2 3.0 %collective-permute-start.1 = (f32[18,32,128]{2,1,0:T(8,128)S(1)}, f32[18,32,128]{2,1,0:T(8,128)S(1)}, u32[]{:S(2)}, u32[]{:S(2)}) collective-permute-start(f32[18,32,128]{2,1,0:T(8,128)S(1)} %get-tuple-element.42), channel_id=1, source_target_pairs={{0,8},{8,0},{16,24},{24,16},{1,9},{9,1},{17,25},{25,17},{2,10},{10... | collective-permute-start | bytes 884744 | tf_op jit(solution)/shard_map/to_rows/ppermute | solution.py:255
  5.2 1.5 %collective-permute-start.2 = (f32[18,32,128]{2,1,0:T(8,128)S(1)}, f32[18,32,128]{2,1,0:T(8,128)S(1)}, u32[]{:S(2)}, u32[]{:S(2)}) collective-permute-start(f32[18,32,128]{2,1,0:T(8,128)S(1)} %get-tuple-element.43), channel_id=1, source_target_pairs={{0,16},{8,24},{16,0},{24,8},{1,17},{9,25},{17,1},{25,9},{2,18},{10... | collective-permute-start | bytes 884744 | tf_op jit(solution)/shard_map/to_rows/ppermute | solution.py:255
  6.8 4.2 %collective-permute-start = (f32[4,6,32,128]{3,2,1,0:T(8,128)S(1)}, f32[4,6,32,128]{3,2,1,0:T(8,128)S(1)}, u32[]{:S(2)}, u32[]{:S(2)}) collective-permute-start(f32[4,6,32,128]{3,2,1,0:T(8,128)S(1)} %get-tuple-element.40), channel_id=1, source_target_pairs={{0,7},{1,2},{2,1},{3,4},{4,3},{5,6},{6,5},{7,0},{8,15},{9,10},{10,... | collective-permute-start | bytes 1179656 | tf_op jit(solution)/shard_map/to_next_plane/ppermute | solution.py:253
  10.9 2.1 %collective-permute-done.1.refs_1_ = f32[18,32,128]{2,1,0:T(8,128)S(1)} collective-permute-done((f32[18,32,128]{2,1,0:T(8,128)S(1)}, f32[18,32,128]{2,1,0:T(8,128)S(1)}, u32[]{:S(2)}, u32[]{:S(2)}) %collective-permute-start.1) | collective-permute-done | bytes 294944 | tf_op jit(solution)/shard_map/to_rows/ppermute | solution.py:255
  13.1 6.9 %collective-permute-done.2.refs_2_ = f32[18,32,128]{2,1,0:T(8,128)S(1)} collective-permute-done((f32[18,32,128]{2,1,0:T(8,128)S(1)}, f32[18,32,128]{2,1,0:T(8,128)S(1)}, u32[]{:S(2)}, u32[]{:S(2)}) %collective-permute-start.2) | collective-permute-done | bytes 294944 | tf_op jit(solution)/shard_map/to_rows/ppermute | solution.py:255
  20.0 0.5 collective-permute-start.7
  20.5 0.8 %slice_add_fusion.1 = s32[2048,1]{0,1:T(1,128)S(1)} fusion(s32[2048,2]{0,1:T(2,128)} %param.5), kind=kLoop, calls=%fused_computation.10 | loop fusion | flops 4096 | bytes 24576 | tf_op jit(solution)/shard_map/add | solution.py:230
  21.4 0.2 collective-permute-done.6.refs_6_
  21.6 0.4 collective-permute-done.7.refs_7_
  22.1 1.5 %collective-permute-start.10 = (f32[6,32,128]{2,1,0:T(8,128)S(1)}, f32[6,32,128]{2,1,0:T(8,128)S(1)}, u32[]{:S(2)}, u32[]{:S(2)}) collective-permute-start(f32[6,32,128]{2,1,0:T(8,128)S(1)} %get-tuple-element.75), channel_id=1, source_target_pairs={{0,24},{8,16},{16,8},{24,0},{1,25},{9,17},{17,9},{25,1},{2,26},{10... | collective-permute-start | bytes 294920 | tf_op jit(solution)/shard_map/next_to_rows/ppermute | solution.py:261
  23.6 0.8 %collective-permute-start.9 = (f32[6,32,128]{2,1,0:T(8,128)S(1)}, f32[6,32,128]{2,1,0:T(8,128)S(1)}, u32[]{:S(2)}, u32[]{:S(2)}) collective-permute-start(f32[6,32,128]{2,1,0:T(8,128)S(1)} %get-tuple-element.76), channel_id=1, source_target_pairs={{0,16},{8,24},{16,0},{24,8},{1,17},{9,25},{17,1},{25,9},{2,18},{10... | collective-permute-start | bytes 294920 | tf_op jit(solution)/shard_map/next_to_rows/ppermute | solution.py:261
  24.4 1.2 %collective-permute-start.8 = (f32[6,32,128]{2,1,0:T(8,128)S(1)}, f32[6,32,128]{2,1,0:T(8,128)S(1)}, u32[]{:S(2)}, u32[]{:S(2)}) collective-permute-start(f32[6,32,128]{2,1,0:T(8,128)S(1)} %get-tuple-element.77), channel_id=1, source_target_pairs={{0,8},{8,0},{16,24},{24,16},{1,9},{9,1},{17,25},{25,17},{2,10},{10... | collective-permute-start | bytes 294920 | tf_op jit(solution)/shard_map/next_to_rows/ppermute | solution.py:261
  25.6 9.7 %inner_terms.2 = (f32[12,128,128]{2,1,0:T(8,128)S(1)}, f32[3072,128]{1,0:T(8,128)S(1)}, f32[9216,128]{1,0:T(8,128)S(1)}, bf16[3072,256]{1,0:T(8,128)(2,1)S(1)}, ...) custom-call(s32[3]{0:T(128)S(1)} %pad_add_fusion.where_ref, s32[2048]{0:T(1024)S(1)} %bitcast.22, ...), custom_call_target="tpu_custom_call" | custom-call | flops 12000000000 | bytes 10000000 | tf_op jit(solution)/shard_map/inner_terms/pallas_call | solution.py:266
  35.5 5.6 %inner_terms.3 = (f32[256,128]{1,0:T(8,128)S(1)}, f32[256,128]{1,0:T(8,128)S(1)}) custom-call(s32[3]{0:T(128)S(1)} %pad_add_fusion.where_ref, s32[2048]{0:T(1024)S(1)} %bitcast.23, f32[3072,128]{1,0:T(8,128)S(1)} %get-tuple-element.65.carry_ref, f32[9216,128]{1,0:T(8,128)S(1)} %get-tuple-element.66.slope_ref, bf16[3072,256]{1,0:T(8,128)(2,1)S(1)} %get-tuple-element.67.rhs_ref), custom_call_target="tpu_custom_call" | custom-call | flops 8000000000 | bytes 10000000 | tf_op jit(solution)/shard_map/inner_terms/pallas_call | solution.py:286
  41.1 1.4 %edge_tables.1 = (f32[1024,128]{1,0:T(8,128)S(1)}, f32[3072,128]{1,0:T(8,128)S(1)}, bf16[3072,256]{1,0:T(8,128)(2,1)S(1)}) custom-call(s32[3]{0:T(128)S(1)} %pad_add_fusion.where_ref, f32[128,128]{1,0:T(8,128)S(1)} %copy-done.1, f32[6,32,128]{2,1,0:T(8,128)S(1)} %get-tuple-element.57.refs_0_, f32[6,32,128]{2,1,0:T(8,128)S(1)} %collective-permute-done.8.refs_1_, ...), custom_call_target="tpu_custom_call" | custom-call | tf_op jit(solution)/shard_map/edge_tables/pallas_call | solution.py:297
  42.5 2.4 %edge_terms.4 = f32[256,128]{1,0:T(8,128)S(1)} custom-call(s32[3]{0:T(128)S(1)} %pad_add_fusion.where_ref, s32[2048]{0:T(1024)S(1)} %bitcast.24, f32[1024,128]{1,0:T(8,128)S(1)} %get-tuple-element.62.carry_ref, f32[3072,128]{1,0:T(8,128)S(1)} %get-tuple-element.63.slope_ref, bf16[3072,256]{1,0:T(8,128)(2,1)S(1)} %get-tuple-element.64.rhs_ref, ...), custom_call_target="tpu_custom_call" | custom-call | flops 4000000000 | bytes 10000000 | tf_op jit(solution)/shard_map/edge_terms/pallas_call | solution.py:312
  44.9 1.5 %collective-permute-start.12 = (f32[256,128]{1,0:T(8,128)S(1)}, f32[256,128]{1,0:T(8,128)S(1)}, u32[]{:S(2)}, u32[]{:S(2)}) collective-permute-start(f32[256,128]{1,0:T(8,128)S(1)} %edge_terms.4), channel_id=1, source_target_pairs={{0,24},{8,16},{16,8},{24,0},{1,25},{9,17},{17,9},{25,1},{2,26},{10... | collective-permute-start | bytes 393224 | tf_op jit(solution)/shard_map/sum_over_rows/ppermute | solution.py:323
  46.4 2.4 %edge_terms.5 = f32[256,128]{1,0:T(8,128)S(1)} custom-call(s32[3]{0:T(128)S(1)} %pad_add_fusion.where_ref, s32[2048]{0:T(1024)S(1)} %bitcast.25, f32[1024,128]{1,0:T(8,128)S(1)} %get-tuple-element.62.carry_ref, f32[3072,128]{1,0:T(8,128)S(1)} %get-tuple-element.63.slope_ref, bf16[3072,256]{1,0:T(8,128)(2,1)S(1)} %get-tuple-element.64.rhs_ref, ...), custom_call_target="tpu_custom_call" | custom-call | flops 4000000000 | bytes 10000000 | tf_op jit(solution)/shard_map/edge_terms/pallas_call | solution.py:312
  48.9 0.9 %collective-permute-start.13 = (f32[256,128]{1,0:T(8,128)S(1)}, f32[256,128]{1,0:T(8,128)S(1)}, u32[]{:S(2)}, u32[]{:S(2)}) collective-permute-start(f32[256,128]{1,0:T(8,128)S(1)} %edge_terms.5), channel_id=1, source_target_pairs={{0,16},{8,24},{16,0},{24,8},{1,17},{9,25},{17,1},{25,9},{2,18},{10... | collective-permute-start | bytes 393224 | tf_op jit(solution)/shard_map/sum_over_rows/ppermute | solution.py:323
  49.7 2.6 %edge_terms.6 = f32[256,128]{1,0:T(8,128)S(1)} custom-call(s32[3]{0:T(128)S(1)} %pad_add_fusion.where_ref, s32[2048]{0:T(1024)S(1)} %bitcast.26, f32[1024,128]{1,0:T(8,128)S(1)} %get-tuple-element.62.carry_ref, f32[3072,128]{1,0:T(8,128)S(1)} %get-tuple-element.63.slope_ref, bf16[3072,256]{1,0:T(8,128)(2,1)S(1)} %get-tuple-element.64.rhs_ref, ...), custom_call_target="tpu_custom_call" | custom-call | flops 4000000000 | bytes 10000000 | tf_op jit(solution)/shard_map/edge_terms/pallas_call | solution.py:312
  52.3 1.3 %collective-permute-start.14 = (f32[256,128]{1,0:T(8,128)S(1)}, f32[256,128]{1,0:T(8,128)S(1)}, u32[]{:S(2)}, u32[]{:S(2)}) collective-permute-start(f32[256,128]{1,0:T(8,128)S(1)} %edge_terms.6), channel_id=1, source_target_pairs={{0,8},{8,0},{16,24},{24,16},{1,9},{9,1},{17,25},{25,17},{2,10},{10... | collective-permute-start | bytes 393224 | tf_op jit(solution)/shard_map/sum_over_rows/ppermute | solution.py:323
  53.6 2.4 %edge_terms.7 = f32[256,128]{1,0:T(8,128)S(1)} custom-call(s32[3]{0:T(128)S(1)} %pad_add_fusion.where_ref, s32[2048]{0:T(1024)S(1)} %bitcast.27, f32[1024,128]{1,0:T(8,128)S(1)} %get-tuple-element.62.carry_ref, f32[3072,128]{1,0:T(8,128)S(1)} %get-tuple-element.63.slope_ref, bf16[3072,256]{1,0:T(8,128)(2,1)S(1)} %get-tuple-element.64.rhs_ref, ...), custom_call_target="tpu_custom_call" | custom-call | flops 4000000000 | bytes 10000000 | tf_op jit(solution)/shard_map/edge_terms/pallas_call | solution.py:312
  56.0 1.7 %collective-permute-done.14 = f32[256,128]{1,0:T(8,128)S(1)} collective-permute-done((f32[256,128]{1,0:T(8,128)S(1)}, f32[256,128]{1,0:T(8,128)S(1)}, u32[]{:S(2)}, u32[]{:S(2)}) %collective-permute-start.14) | collective-permute-done | bytes 131104 | tf_op jit(solution)/shard_map/sum_over_rows/ppermute | solution.py:323
  57.7 1.6 %collective-permute-start.15 = (f32[64,128]{1,0:T(8,128)S(1)}, f32[64,128]{1,0:T(8,128)S(1)}, u32[]{:S(2)}, u32[]{:S(2)}) collective-permute-start(f32[64,128]{1,0:T(8,128)S(1)} %get-tuple-element.79), channel_id=1, source_target_pairs={{0,2},{1,3},{2,4},{3,5},{4,6},{5,7},{6,0},{7,1},{8,10},{9,11},{10,... | collective-permute-start | bytes 98312 | tf_op jit(solution)/shard_map/sum_over_chips/ppermute | solution.py:336
  59.4 2.2 %collective-permute-start.17 = (f32[64,128]{1,0:T(8,128)S(1)}, f32[64,128]{1,0:T(8,128)S(1)}, u32[]{:S(2)}, u32[]{:S(2)}) collective-permute-start(f32[64,128]{1,0:T(8,128)S(1)} %get-tuple-element.80), channel_id=1, source_target_pairs={{0,6},{1,7},{2,0},{3,1},{4,2},{5,3},{6,4},{7,5},{8,14},{9,15},{10,... | collective-permute-start | bytes 98312 | tf_op jit(solution)/shard_map/sum_over_chips/ppermute | solution.py:336
  61.6 0.8 %collective-permute-start.16 = (f32[64,128]{1,0:T(8,128)S(1)}, f32[64,128]{1,0:T(8,128)S(1)}, u32[]{:S(2)}, u32[]{:S(2)}) collective-permute-start(f32[64,128]{1,0:T(8,128)S(1)} %get-tuple-element.81), channel_id=1, source_target_pairs={{0,4},{1,5},{2,6},{3,7},{4,0},{5,1},{6,2},{7,3},{8,12},{9,13},{10,... | collective-permute-start | bytes 98312 | tf_op jit(solution)/shard_map/sum_over_chips/ppermute | solution.py:336
  62.4 1.4 %collective-permute-done.15 = f32[64,128]{1,0:T(8,128)S(1)} collective-permute-done((f32[64,128]{1,0:T(8,128)S(1)}, f32[64,128]{1,0:T(8,128)S(1)}, u32[]{:S(2)}, u32[]{:S(2)}) %collective-permute-start.15) | collective-permute-done | bytes 32800 | tf_op jit(solution)/shard_map/sum_over_chips/ppermute | solution.py:336
  63.8 2.7 %collective-permute-done.16 = f32[64,128]{1,0:T(8,128)S(1)} collective-permute-done((f32[64,128]{1,0:T(8,128)S(1)}, f32[64,128]{1,0:T(8,128)S(1)}, u32[]{:S(2)}, u32[]{:S(2)}) %collective-permute-start.16) | collective-permute-done | bytes 32800 | tf_op jit(solution)/shard_map/sum_over_chips/ppermute | solution.py:336
  66.4 0.6 fusion.2
  (23 shorter events, 0.2 us)
Async XLA Ops:
  0.1 1.1 %copy-start = (f32[32,3,1,16,128]{4,3,2,1,0:T(8,128)S(1)}, f32[32,3,1,16,128]{4,3,2,1,0:T(8,128)}, u32[]{:S(2)}) copy-start(f32[32,3,1,16,128]{4,3,2,1,0:T(8,128)} %param.3) | copy-start | bytes 2359300
  1.2 24.4 %copy-start.1 = (f32[128,128]{1,0:T(8,128)S(1)}, f32[128,128]{1,0:T(8,128)}, u32[]{:S(2)}) copy-start(f32[128,128]{1,0:T(8,128)} %coeffs_ref.3) | copy-start | bytes 196612
  2.2 10.8 %collective-permute-start.1 = (f32[18,32,128]{2,1,0:T(8,128)S(1)}, f32[18,32,128]{2,1,0:T(8,128)S(1)}, u32[]{:S(2)}, u32[]{:S(2)}) collective-permute-start(f32[18,32,128]{2,1,0:T(8,128)S(1)} %get-tuple-element.42), channel_id=1, source_target_pairs={{0,8},{8,0},{16,24},{24,16},{1,9},{9,1},{17,25},{25,17},{2,10},{10... | collective-permute-start | bytes 884744 | tf_op jit(solution)/shard_map/to_rows/ppermute | solution.py:255
  5.2 14.8 %collective-permute-start.2 = (f32[18,32,128]{2,1,0:T(8,128)S(1)}, f32[18,32,128]{2,1,0:T(8,128)S(1)}, u32[]{:S(2)}, u32[]{:S(2)}) collective-permute-start(f32[18,32,128]{2,1,0:T(8,128)S(1)} %get-tuple-element.43), channel_id=1, source_target_pairs={{0,16},{8,24},{16,0},{24,8},{1,17},{9,25},{17,1},{25,9},{2,18},{10... | collective-permute-start | bytes 884744 | tf_op jit(solution)/shard_map/to_rows/ppermute | solution.py:255
  6.7 13.3 %collective-permute-start.3 = (f32[18,32,128]{2,1,0:T(8,128)S(1)}, f32[18,32,128]{2,1,0:T(8,128)S(1)}, u32[]{:S(2)}, u32[]{:S(2)}) collective-permute-start(f32[18,32,128]{2,1,0:T(8,128)S(1)} %get-tuple-element.44), channel_id=1, source_target_pairs={{0,24},{8,16},{16,8},{24,0},{1,25},{9,17},{17,9},{25,1},{2,26},{10... | collective-permute-start | bytes 884744 | tf_op jit(solution)/shard_map/to_rows/ppermute | solution.py:255
  6.8 14.6 %collective-permute-start.4 = (f32[18,32,128]{2,1,0:T(8,128)S(1)}, f32[18,32,128]{2,1,0:T(8,128)S(1)}, u32[]{:S(2)}, u32[]{:S(2)}) collective-permute-start(f32[18,32,128]{2,1,0:T(8,128)S(1)} %get-tuple-element.46.refs_0_), channel_id=1, source_target_pairs={{0,1},{1,0},{2,3},{3,2},{4,5},{5,4},{6,7},{7,6},{8,9},{9,8},{10,11... | collective-permute-start | bytes 884744 | tf_op jit(solution)/shard_map/to_other_core/ppermute | solution.py:257
  6.8 14.6 %collective-permute-start = (f32[4,6,32,128]{3,2,1,0:T(8,128)S(1)}, f32[4,6,32,128]{3,2,1,0:T(8,128)S(1)}, u32[]{:S(2)}, u32[]{:S(2)}) collective-permute-start(f32[4,6,32,128]{3,2,1,0:T(8,128)S(1)} %get-tuple-element.40), channel_id=1, source_target_pairs={{0,7},{1,2},{2,1},{3,4},{4,3},{5,6},{6,5},{7,0},{8,15},{9,10},{10,... | collective-permute-start | bytes 1179656 | tf_op jit(solution)/shard_map/to_next_plane/ppermute | solution.py:253
  13.1 8.3 %collective-permute-start.5 = (f32[18,32,128]{2,1,0:T(8,128)S(1)}, f32[18,32,128]{2,1,0:T(8,128)S(1)}, u32[]{:S(2)}, u32[]{:S(2)}) collective-permute-start(f32[18,32,128]{2,1,0:T(8,128)S(1)} %collective-permute-done.1.refs_1_), channel_id=1, source_target_pairs={{0,1},{1,0},{2,3},{3,2},{4,5},{5,4},{6,7},{7,6},{8,9},{9,8},{10,11... | collective-permute-start | bytes 884744 | tf_op jit(solution)/shard_map/to_other_core/ppermute | solution.py:257
  20.0 1.6 %collective-permute-start.6 = (f32[18,32,128]{2,1,0:T(8,128)S(1)}, f32[18,32,128]{2,1,0:T(8,128)S(1)}, u32[]{:S(2)}, u32[]{:S(2)}) collective-permute-start(f32[18,32,128]{2,1,0:T(8,128)S(1)} %collective-permute-done.2.refs_2_), channel_id=1, source_target_pairs={{0,1},{1,0},{2,3},{3,2},{4,5},{5,4},{6,7},{7,6},{8,9},{9,8},{10,11... | collective-permute-start | bytes 884744 | tf_op jit(solution)/shard_map/to_other_core/ppermute | solution.py:257
  20.0 2.0 %collective-permute-start.7 = (f32[18,32,128]{2,1,0:T(8,128)S(1)}, f32[18,32,128]{2,1,0:T(8,128)S(1)}, u32[]{:S(2)}, u32[]{:S(2)}) collective-permute-start(f32[18,32,128]{2,1,0:T(8,128)S(1)} %collective-permute-done.3.refs_3_), channel_id=1, source_target_pairs={{0,1},{1,0},{2,3},{3,2},{4,5},{5,4},{6,7},{7,6},{8,9},{9,8},{10,11... | collective-permute-start | bytes 884744 | tf_op jit(solution)/shard_map/to_other_core/ppermute | solution.py:257
  22.1 13.3 %collective-permute-start.10 = (f32[6,32,128]{2,1,0:T(8,128)S(1)}, f32[6,32,128]{2,1,0:T(8,128)S(1)}, u32[]{:S(2)}, u32[]{:S(2)}) collective-permute-start(f32[6,32,128]{2,1,0:T(8,128)S(1)} %get-tuple-element.75), channel_id=1, source_target_pairs={{0,24},{8,16},{16,8},{24,0},{1,25},{9,17},{17,9},{25,1},{2,26},{10... | collective-permute-start | bytes 294920 | tf_op jit(solution)/shard_map/next_to_rows/ppermute | solution.py:261
  23.6 11.7 %collective-permute-start.9 = (f32[6,32,128]{2,1,0:T(8,128)S(1)}, f32[6,32,128]{2,1,0:T(8,128)S(1)}, u32[]{:S(2)}, u32[]{:S(2)}) collective-permute-start(f32[6,32,128]{2,1,0:T(8,128)S(1)} %get-tuple-element.76), channel_id=1, source_target_pairs={{0,16},{8,24},{16,0},{24,8},{1,17},{9,25},{17,1},{25,9},{2,18},{10... | collective-permute-start | bytes 294920 | tf_op jit(solution)/shard_map/next_to_rows/ppermute | solution.py:261
  24.4 11.0 %collective-permute-start.8 = (f32[6,32,128]{2,1,0:T(8,128)S(1)}, f32[6,32,128]{2,1,0:T(8,128)S(1)}, u32[]{:S(2)}, u32[]{:S(2)}) collective-permute-start(f32[6,32,128]{2,1,0:T(8,128)S(1)} %get-tuple-element.77), channel_id=1, source_target_pairs={{0,8},{8,0},{16,24},{24,16},{1,9},{9,1},{17,25},{25,17},{2,10},{10... | collective-permute-start | bytes 294920 | tf_op jit(solution)/shard_map/next_to_rows/ppermute | solution.py:261
  35.4 5.7 %collective-permute-start.11 = (f32[4,6,32,128]{3,2,1,0:T(8,128)S(1)}, f32[4,6,32,128]{3,2,1,0:T(8,128)S(1)}, u32[]{:S(2)}, u32[]{:S(2)}) collective-permute-start(f32[4,6,32,128]{3,2,1,0:T(8,128)S(1)} %pad_maximum_fusion), channel_id=1, source_target_pairs={{0,1},{1,0},{2,3},{3,2},{4,5},{5,4},{6,7},{7,6},{8,9},{9,8},{10,11... | collective-permute-start | bytes 1179656 | tf_op jit(solution)/shard_map/next_to_other_core/ppermute | solution.py:284
  44.9 12.8 %collective-permute-start.12 = (f32[256,128]{1,0:T(8,128)S(1)}, f32[256,128]{1,0:T(8,128)S(1)}, u32[]{:S(2)}, u32[]{:S(2)}) collective-permute-start(f32[256,128]{1,0:T(8,128)S(1)} %edge_terms.4), channel_id=1, source_target_pairs={{0,24},{8,16},{16,8},{24,0},{1,25},{9,17},{17,9},{25,1},{2,26},{10... | collective-permute-start | bytes 393224 | tf_op jit(solution)/shard_map/sum_over_rows/ppermute | solution.py:323
  48.9 8.8 %collective-permute-start.13 = (f32[256,128]{1,0:T(8,128)S(1)}, f32[256,128]{1,0:T(8,128)S(1)}, u32[]{:S(2)}, u32[]{:S(2)}) collective-permute-start(f32[256,128]{1,0:T(8,128)S(1)} %edge_terms.5), channel_id=1, source_target_pairs={{0,16},{8,24},{16,0},{24,8},{1,17},{9,25},{17,1},{25,9},{2,18},{10... | collective-permute-start | bytes 393224 | tf_op jit(solution)/shard_map/sum_over_rows/ppermute | solution.py:323
  52.3 5.4 %collective-permute-start.14 = (f32[256,128]{1,0:T(8,128)S(1)}, f32[256,128]{1,0:T(8,128)S(1)}, u32[]{:S(2)}, u32[]{:S(2)}) collective-permute-start(f32[256,128]{1,0:T(8,128)S(1)} %edge_terms.6), channel_id=1, source_target_pairs={{0,8},{8,0},{16,24},{24,16},{1,9},{9,1},{17,25},{25,17},{2,10},{10... | collective-permute-start | bytes 393224 | tf_op jit(solution)/shard_map/sum_over_rows/ppermute | solution.py:323
  57.7 6.0 %collective-permute-start.15 = (f32[64,128]{1,0:T(8,128)S(1)}, f32[64,128]{1,0:T(8,128)S(1)}, u32[]{:S(2)}, u32[]{:S(2)}) collective-permute-start(f32[64,128]{1,0:T(8,128)S(1)} %get-tuple-element.79), channel_id=1, source_target_pairs={{0,2},{1,3},{2,4},{3,5},{4,6},{5,7},{6,0},{7,1},{8,10},{9,11},{10,... | collective-permute-start | bytes 98312 | tf_op jit(solution)/shard_map/sum_over_chips/ppermute | solution.py:336
  59.4 4.4 %collective-permute-start.17 = (f32[64,128]{1,0:T(8,128)S(1)}, f32[64,128]{1,0:T(8,128)S(1)}, u32[]{:S(2)}, u32[]{:S(2)}) collective-permute-start(f32[64,128]{1,0:T(8,128)S(1)} %get-tuple-element.80), channel_id=1, source_target_pairs={{0,6},{1,7},{2,0},{3,1},{4,2},{5,3},{6,4},{7,5},{8,14},{9,15},{10,... | collective-permute-start | bytes 98312 | tf_op jit(solution)/shard_map/sum_over_chips/ppermute | solution.py:336
  61.6 4.8 %collective-permute-start.16 = (f32[64,128]{1,0:T(8,128)S(1)}, f32[64,128]{1,0:T(8,128)S(1)}, u32[]{:S(2)}, u32[]{:S(2)}) collective-permute-start(f32[64,128]{1,0:T(8,128)S(1)} %get-tuple-element.81), channel_id=1, source_target_pairs={{0,4},{1,5},{2,6},{3,7},{4,0},{5,1},{6,2},{7,3},{8,12},{9,13},{10,... | collective-permute-start | bytes 98312 | tf_op jit(solution)/shard_map/sum_over_chips/ppermute | solution.py:336

commit v6 on v5

--- a/solution.py
+++ b/solution.py
@@ -96,11 +96,11 @@
     lax.fori_loop(0, chips, one_share, 0)
 
 
-def inner_kernel(where_ref, codes_ref, coeffs_ref, *refs, peers, sizes):
+def inner_kernel(where_ref, codes_ref, coeffs_ref, *refs, first_peer, sizes):
     local_s, block_rows, tm_count, chips, share, bits = sizes
     own, other = refs[:tm_count], refs[tm_count : 2 * tm_count]
     near_ref, carry_ref, slope_ref, rhs_ref = refs[2 * tm_count : 2 * tm_count + 4]
-    *out_refs, slab_ref, conv_ref = refs[2 * tm_count + 4 :]
+    out_ref, slab_ref, conv_ref = refs[2 * tm_count + 4 :]
     core = where_ref[2]
     modes, lanes = coeffs_ref.shape[1], own[0].shape[2]
     height = 2 * block_rows
@@ -138,13 +138,14 @@
                     near_ref[center] = value
 
     pairs_kernel(
-        where_ref, codes_ref, carry_ref, slope_ref, rhs_ref, *out_refs, conv_ref,
-        peers=peers, sizes=(height, chips, share, bits),
+        where_ref, codes_ref, carry_ref, slope_ref, rhs_ref, out_ref, conv_ref,
+        first_peer=first_peer, sizes=(height, chips, share, bits),
     )
 
 
-def pairs_kernel(where_ref, codes_ref, carry_ref, slope_ref, rhs_ref, *refs, peers, sizes):
-    *out_refs, conv_ref = refs
+def pairs_kernel(
+    where_ref, codes_ref, carry_ref, slope_ref, rhs_ref, out_ref, conv_ref, *, first_peer, sizes
+):
     height, chips, share, bits = sizes
 
     def one_pair(slot, i, j):
@@ -159,9 +160,12 @@
         ]
         conv_ref[pl.ds(pl.multiple_of(slot * (3 * height), 8), 3 * height), :] = jnp.concatenate(rows, axis=0)
 
-    for peer, out_ref in zip(peers, out_refs):
-        for_pairs_of(where_ref, codes_ref, peer, (chips, share, bits), one_pair)
-        out_ref[...] = project(conv_ref, rhs_ref, chips * share, 3 * height, conv_ref.shape[1])
+    def one_peer(number, _):
+        for_pairs_of(where_ref, codes_ref, first_peer + number, (chips, share, bits), one_pair)
+        out_ref[number] = project(conv_ref, rhs_ref, chips * share, 3 * height, conv_ref.shape[1])
+        return 0
+
+    lax.fori_loop(0, out_ref.shape[0], one_peer, 0)
 
 
 def far_kernel(where_ref, coeffs_ref, *refs, sizes):
@@ -190,8 +194,9 @@
 
 
 def edge_kernel(
-    where_ref, codes_ref, carry_ref, slope_ref, rhs_ref, inner_ref, out_ref, conv_ref, *, peer, sizes
+    where_ref, codes_ref, carry_ref, slope_ref, rhs_ref, inner_ref, *refs, peer, sizes
 ):
+    *arrived_refs, out_ref, conv_ref = refs
     chips, share, _ = sizes
     modes, lanes = out_ref.shape[1], carry_ref.shape[1]
     height = carry_ref.shape[0] // modes
@@ -203,7 +208,10 @@
         conv_ref[pl.ds(pl.multiple_of(slot * (3 * height), 8), 3 * height), :] = jnp.concatenate(rows, axis=0)
 
     for_pairs_of(where_ref, codes_ref, peer, sizes, one_pair)
-    out_ref[...] = inner_ref[...] + project(conv_ref, rhs_ref, chips * share, 3 * height, lanes)
+    total = inner_ref[peer % inner_ref.shape[0]]
+    for arrived_ref in arrived_refs:
+        total = total + arrived_ref[...]
+    out_ref[...] = total + project(conv_ref, rhs_ref, chips * share, 3 * height, lanes)
 
 
 def vmem_limit(mebibytes):
@@ -253,48 +261,47 @@
         across_edge = lax.ppermute(packed[tm_count], "space", ring)
     with jax.named_scope("to_rows"):
         own = [packed[0]] + [lax.ppermute(packed[peer], "tm", across(peer)) for peer in range(1, tm_count)]
+    with jax.named_scope("next_to_rows"):
+        across_edge, own[:3] = lax.optimization_barrier((across_edge, own[:3]))
+        parts = [across_edge[peer] for peer in range(tm_count)]
+        parts, own[3:] = lax.optimization_barrier((parts, own[3:]))
+        next_own = [parts[0]] + [lax.ppermute(parts[peer], "tm", across(peer)) for peer in range(1, tm_count)]
     with jax.named_scope("to_other_core"):
         other = [lax.ppermute(piece, "space", swap) for piece in own]
-    with jax.named_scope("next_to_rows"):
-        across_edge, own, other = lax.optimization_barrier((across_edge, own, other))
-        parts = [across_edge[peer] for peer in range(tm_count)]
-        next_own = [parts[0]] + [lax.ppermute(parts[peer], "tm", across(peer)) for peer in range(1, tm_count)]
-    early, late = range(tm_count - 1, tm_count // 2 - 1, -1), range(tm_count // 2 - 1, -1, -1)
+    early = tm_count // 2
     work = [pltpu.VMEM((block * 3 * height, lanes), F32)]
-    group = pltpu.VMEM((block, modes), F32)
+    groups = pltpu.VMEM((early, block, modes), F32)
     with jax.named_scope("inner_terms"):
-        near, *inner_tables_and_early = pl.pallas_call(
-            functools.partial(inner_kernel, peers=early, sizes=(local_s, block_rows, tm_count, chips, share, bits)),
+        near, *inner_tables, early_sums = pl.pallas_call(
+            functools.partial(inner_kernel, first_peer=early, sizes=(local_s, block_rows, tm_count, chips, share, bits)),
             out_shape=[
                 pltpu.VMEM((block_rows * 3, modes, lanes), F32),
                 pltpu.VMEM((modes * 3 * height, lanes), F32),
                 pltpu.VMEM((modes * 9 * height, lanes), F32),
                 pltpu.VMEM((depth, 2 * modes), BF16),
-            ]
-            + [group] * len(early),
+                groups,
+            ],
             in_specs=[smem, smem] + [vmem] * (2 * tm_count + 1),
-            out_specs=[vmem] * (4 + len(early)),
+            out_specs=[vmem] * 5,
             scratch_shapes=[pltpu.VMEM((2, (block_rows + 2) * 3, modes, lanes), F32)] + work,
             compiler_params=vmem_limit(24),
             cost_estimate=pl.CostEstimate(flops=12 * 10**9, bytes_accessed=10**7, transcendentals=0),
         )(where, codes, coeffs, *[in_vmem(piece) for piece in (*own, *other)])
-        inner_tables, early_sums = inner_tables_and_early[:3], inner_tables_and_early[3:]
     with jax.named_scope("next_to_other_core"):
         next_own, inner_tables = lax.optimization_barrier((next_own, inner_tables))
         next_other = lax.ppermute(jnp.stack(next_own), "space", swap)
     with jax.named_scope("inner_terms"):
         late_sums = pl.pallas_call(
-            functools.partial(pairs_kernel, peers=late, sizes=(height, chips, share, bits)),
-            out_shape=[group] * len(late),
+            functools.partial(pairs_kernel, first_peer=0, sizes=(height, chips, share, bits)),
+            out_shape=groups,
             in_specs=[smem, smem] + [vmem] * 3,
-            out_specs=[vmem] * len(late),
+            out_specs=vmem,
             scratch_shapes=work,
             compiler_params=vmem_limit(16),
             cost_estimate=pl.CostEstimate(flops=8 * 10**9, bytes_accessed=10**7, transcendentals=0),
         )(where, codes, *[in_vmem(table) for table in inner_tables])
-        inner = [*reversed(late_sums), *reversed(early_sums)]
     with jax.named_scope("edge_tables"):
-        tables = pl.pallas_call(
+        tables = list(pl.pallas_call(
             functools.partial(far_kernel, sizes=(local_s, block_rows, tm_count)),
             out_shape=[
                 pltpu.VMEM((modes * height, lanes), F32),
@@ -304,28 +311,30 @@
             in_specs=[smem] + [vmem] * (tm_count + 3),
             out_specs=[vmem] * 3,
             compiler_params=vmem_limit(16),
-        )(where, coeffs, *[in_vmem(piece) for piece in (*next_own, next_other, near)])
-    sums = [None] * tm_count
+        )(where, coeffs, *[in_vmem(piece) for piece in (*next_own, next_other, near)]))
     arrived = []
     for peer in reversed(range(tm_count)):
         with jax.named_scope("edge_terms"):
-            sums[peer] = pl.pallas_call(
+            parts = arrived[:-1] if peer == 0 else []
+            summed = pl.pallas_call(
                 functools.partial(edge_kernel, peer=peer, sizes=(chips, share, bits)),
-                out_shape=group,
-                in_specs=[smem, smem] + [vmem] * 4,
+                out_shape=pltpu.VMEM((block, modes), F32),
+                in_specs=[smem, smem] + [vmem] * (4 + len(parts)),
                 out_specs=vmem,
                 scratch_shapes=work,
                 compiler_params=vmem_limit(16),
-                cost_estimate=pl.CostEstimate(flops=4 * 10**9, bytes_accessed=10**7, transcendentals=0),
-            )(where, codes, *[in_vmem(table) for table in (*tables, inner[peer])])
+                cost_estimate=pl.CostEstimate(flops=10**8, bytes_accessed=10**5, transcendentals=0),
+            )(
+                where,
+                codes,
+                *[in_vmem(table) for table in (*tables, early_sums if peer >= early else late_sums, *parts)],
+            )
         with jax.named_scope("sum_over_rows"):
             if peer:
-                arrived.append(lax.ppermute(sums[peer], "tm", across(peer)))
-                inner[peer - 1], _ = lax.optimization_barrier((inner[peer - 1], sums[peer]))
+                arrived.append(lax.ppermute(summed, "tm", across(peer)))
+                tables[0], _ = lax.optimization_barrier((tables[0], summed))
     with jax.named_scope("sum_over_rows"):
-        summed = sums[0]
-        for part in arrived:
-            summed = summed + part
+        summed = summed + arrived[-1]
     with jax.named_scope("sum_over_chips"):
         shares = summed.reshape(chips, share, modes)
         result = shares[0]

time: 67.3 us -> 66.2 us (0.984)
  waiting for transfers between devices: 15.5 us -> 19 us
  Pallas kernels: 27.5 us -> 24.5 us
  starting transfers between devices: 21.2 us -> 20.4 us
  other arithmetic: 1.56 us -> 0.76 us
    pallas_call x2, Pallas kernels: 15.3 us -> 12.5 us  [the longest x1 8.3 us: shards(): pl.pallas_call(functools.partial(inner_kernel, first_peer=early, sizes=(l...]
    ppermute x3, waiting for transfers between devices: 9.07 us -> 11.6 us  [shards(): lax.ppermute(packed[peer], 'tm', across(peer))]
    ppermute x3, starting transfers between devices: 4.54 us -> 3.49 us  [shards(): lax.ppermute(packed[peer], 'tm', across(peer))]
    ppermute x3, waiting for transfers between devices: 1.7 us -> 2.75 us  [shards(): arrived.append(lax.ppermute(summed, 'tm', across(peer)))]
    add x1, other arithmetic: 0.81 us -> 0.01 us  [shards(): codes = pair_table[:, 0] * modes + pair_table[:, 1]]
  transfers between devices with their start and end apart: 18 -> 18, of which waited for: 7 -> 5; matrix products, arithmetic and copies ran while one was open for 1% -> 0% of each run, Pallas kernels for 34% -> 26%
where the time goes in v6:
time: 66.2 us; the launch traced here: 66.1 us
  Pallas kernels  24.5 us (37%)
  starting transfers between devices  20.4 us (31%)
  waiting for transfers between devices  19 us (29%)
  local copies, waits for them, and re-layouts  1.18 us (2%)
  other arithmetic  0.76 us (1%)
    ppermute x3, waiting for transfers between devices, shards(): lax.ppermute(packed[peer], 'tm', across(peer))  11.6 us
    pallas_call x4, Pallas kernels, shards(): pl.pallas_call(functools.partial(edge_kernel, peer=peer, sizes=(chips, sh...  9.64 us
    pallas_call x1, Pallas kernels, shards(): pl.pallas_call(functools.partial(inner_kernel, first_peer=early, sizes=(l...  8.3 us
    ppermute x3, waiting for transfers between devices, shards(): result = result + lax.ppermute(shares[step], 'space', shift)  4.66 us
    ppermute x1, starting transfers between devices, shards(): across_edge = lax.ppermute(packed[tm_count], 'space', ring)  4.55 us
    pallas_call x1, Pallas kernels, shards(): pl.pallas_call(functools.partial(pairs_kernel, first_peer=0, sizes=(heigh...  4.21 us
    ppermute x3, starting transfers between devices, shards(): result = result + lax.ppermute(shares[step], 'space', shift)  4.03 us
    ppermute x3, starting transfers between devices, shards(): arrived.append(lax.ppermute(summed, 'tm', across(peer)))  3.62 us
  transfers between devices with their start and end apart: 18, of which 5 were waited for; matrix products, arithmetic and copies ran while one was open for 0% of the time, Pallas kernels for 26%

profile of v6, /device:TPU:0, one launch (start us, length us, event | category | flops | bytes accessed | tf_op | source)
XLA Modules:
  0.0 66.1 jit_solution(12136056943460720645)
XLA Ops:
  0.0 0.1 pad_add_fusion.where_ref
  0.1 1.1 %copy-done = f32[32,3,1,16,128]{4,3,2,1,0:T(8,128)S(1)} copy-done((f32[32,3,1,16,128]{4,3,2,1,0:T(8,128)S(1)}, f32[32,3,1,16,128]{4,3,2,1,0:T(8,128)}, u32[]{:S(2)}) %copy-start) | copy-done | bytes 786456
  1.2 1.0 %pack.1 = (f32[18,32,128]{2,1,0:T(8,128)S(1)}, f32[18,32,128]{2,1,0:T(8,128)S(1)}, f32[18,32,128]{2,1,0:T(8,128)S(1)}, f32[18,32,128]{2,1,0:T(8,128)S(1)}, f32[4,6,32,128]{3,2,1,0:T(8,128)S(1)}) custom-call(s32[3]{0:T(128)S(1)} %pad_add_fusion.where_ref, f32[1536,128]{1,0:T(8,128)S(1)} %bitcast.18), custom_call_target="tpu_custom_call" | custom-call | tf_op jit(solution)/shard_map/pack/pallas_call | solution.py:251
  2.2 4.6 %collective-permute-start = (f32[4,6,32,128]{3,2,1,0:T(8,128)S(1)}, f32[4,6,32,128]{3,2,1,0:T(8,128)S(1)}, u32[]{:S(2)}, u32[]{:S(2)}) collective-permute-start(f32[4,6,32,128]{3,2,1,0:T(8,128)S(1)} %get-tuple-element.37), channel_id=1, source_target_pairs={{0,7},{1,2},{2,1},{3,4},{4,3},{5,6},{6,5},{7,0},{8,15},{9,10},{10,... | collective-permute-start | bytes 1179656 | tf_op jit(solution)/shard_map/to_next_plane/ppermute | solution.py:261
  6.8 1.5 %collective-permute-start.1 = (f32[18,32,128]{2,1,0:T(8,128)S(1)}, f32[18,32,128]{2,1,0:T(8,128)S(1)}, u32[]{:S(2)}, u32[]{:S(2)}) collective-permute-start(f32[18,32,128]{2,1,0:T(8,128)S(1)} %get-tuple-element.39), channel_id=1, source_target_pairs={{0,8},{8,0},{16,24},{24,16},{1,9},{9,1},{17,25},{25,17},{2,10},{10... | collective-permute-start | bytes 884744 | tf_op jit(solution)/shard_map/to_rows/ppermute | solution.py:263
  8.3 1.5 %collective-permute-start.2 = (f32[18,32,128]{2,1,0:T(8,128)S(1)}, f32[18,32,128]{2,1,0:T(8,128)S(1)}, u32[]{:S(2)}, u32[]{:S(2)}) collective-permute-start(f32[18,32,128]{2,1,0:T(8,128)S(1)} %get-tuple-element.40), channel_id=1, source_target_pairs={{0,16},{8,24},{16,0},{24,8},{1,17},{9,25},{17,1},{25,9},{2,18},{10... | collective-permute-start | bytes 884744 | tf_op jit(solution)/shard_map/to_rows/ppermute | solution.py:263
  9.8 0.5 collective-permute-start.3
  10.3 6.5 %collective-permute-done.1.refs_1_ = f32[18,32,128]{2,1,0:T(8,128)S(1)} collective-permute-done((f32[18,32,128]{2,1,0:T(8,128)S(1)}, f32[18,32,128]{2,1,0:T(8,128)S(1)}, u32[]{:S(2)}, u32[]{:S(2)}) %collective-permute-start.1) | collective-permute-done | bytes 294944 | tf_op jit(solution)/shard_map/to_rows/ppermute | solution.py:263
  16.7 5.2 %collective-permute-done.2.refs_2_ = f32[18,32,128]{2,1,0:T(8,128)S(1)} collective-permute-done((f32[18,32,128]{2,1,0:T(8,128)S(1)}, f32[18,32,128]{2,1,0:T(8,128)S(1)}, u32[]{:S(2)}, u32[]{:S(2)}) %collective-permute-start.2) | collective-permute-done | bytes 294944 | tf_op jit(solution)/shard_map/to_rows/ppermute | solution.py:263
  22.0 0.5 collective-permute-start.7
  22.5 0.1 collective-permute-start.8
  22.6 0.4 collective-permute-start.9
  23.0 1.2 %collective-permute-start.4 = (f32[6,32,128]{2,1,0:T(8,128)S(1)}, f32[6,32,128]{2,1,0:T(8,128)S(1)}, u32[]{:S(2)}, u32[]{:S(2)}) collective-permute-start(f32[6,32,128]{2,1,0:T(8,128)S(1)} %get-tuple-element.44), channel_id=1, source_target_pairs={{0,8},{8,0},{16,24},{24,16},{1,9},{9,1},{17,25},{25,17},{2,10},{10... | collective-permute-start | bytes 294920 | tf_op jit(solution)/shard_map/next_to_rows/ppermute | solution.py:268
  24.2 0.9 %collective-permute-start.5 = (f32[6,32,128]{2,1,0:T(8,128)S(1)}, f32[6,32,128]{2,1,0:T(8,128)S(1)}, u32[]{:S(2)}, u32[]{:S(2)}) collective-permute-start(f32[6,32,128]{2,1,0:T(8,128)S(1)} %get-tuple-element.45), channel_id=1, source_target_pairs={{0,16},{8,24},{16,0},{24,8},{1,17},{9,25},{17,1},{25,9},{2,18},{10... | collective-permute-start | bytes 294920 | tf_op jit(solution)/shard_map/next_to_rows/ppermute | solution.py:268
  25.2 1.4 %collective-permute-start.6 = (f32[6,32,128]{2,1,0:T(8,128)S(1)}, f32[6,32,128]{2,1,0:T(8,128)S(1)}, u32[]{:S(2)}, u32[]{:S(2)}) collective-permute-start(f32[6,32,128]{2,1,0:T(8,128)S(1)} %get-tuple-element.46), channel_id=1, source_target_pairs={{0,24},{8,16},{16,8},{24,0},{1,25},{9,17},{17,9},{25,1},{2,26},{10... | collective-permute-start | bytes 294920 | tf_op jit(solution)/shard_map/next_to_rows/ppermute | solution.py:268
  26.6 8.3 %inner_terms.2 = (f32[12,128,128]{2,1,0:T(8,128)S(1)}, f32[3072,128]{1,0:T(8,128)S(1)}, f32[9216,128]{1,0:T(8,128)S(1)}, bf16[3072,256]{1,0:T(8,128)(2,1)S(1)}, f32[2,256,128]{2,1,0:T(8,128)S(1)}) custom-call(s32[3]{0:T(128)S(1)} %pad_add_fusion.where_ref, s32[2048]{0:T(1024)S(1)} %bitcast.22, f32[128,128]{1,0:T(8,128)S(1)} %copy-done.1, ...), custom_call_target="tpu_custom_call" | custom-call | flops 12000000000 | bytes 10000000 | tf_op jit(solution)/shard_map/inner_terms/pallas_call | solution.py:275
  35.1 4.2 %inner_terms.3.inner_ref = f32[2,256,128]{2,1,0:T(8,128)S(1)} custom-call(s32[3]{0:T(128)S(1)} %pad_add_fusion.where_ref, s32[2048]{0:T(1024)S(1)} %bitcast.23, f32[3072,128]{1,0:T(8,128)S(1)} %get-tuple-element.65.carry_ref, f32[9216,128]{1,0:T(8,128)S(1)} %get-tuple-element.66.slope_ref, bf16[3072,256]{1,0:T(8,128)(2,1)S(1)} %get-tuple-element.67.rhs_ref), custom_call_target="tpu_custom_call" | custom-call | flops 8000000000 | bytes 10000000 | tf_op jit(solution)/shard_map/inner_terms/pallas_call | solution.py:294
  39.3 1.4 %edge_tables.1 = (f32[1024,128]{1,0:T(8,128)S(1)}, f32[3072,128]{1,0:T(8,128)S(1)}, bf16[3072,256]{1,0:T(8,128)(2,1)S(1)}) custom-call(s32[3]{0:T(128)S(1)} %pad_add_fusion.where_ref, f32[128,128]{1,0:T(8,128)S(1)} %copy-done.1, f32[6,32,128]{2,1,0:T(8,128)S(1)} %get-tuple-element.54.refs_0_, f32[6,32,128]{2,1,0:T(8,128)S(1)} %collective-permute-done.4.refs_1_, ...), custom_call_target="tpu_custom_call" | custom-call | tf_op jit(solution)/shard_map/edge_tables/pallas_call | solution.py:304
  40.7 2.4 %edge_terms.4 = f32[256,128]{1,0:T(8,128)S(1)} custom-call(s32[3]{0:T(128)S(1)} %pad_add_fusion.where_ref, s32[2048]{0:T(1024)S(1)} %bitcast.24, f32[1024,128]{1,0:T(8,128)S(1)} %get-tuple-element.68.carry_ref, f32[3072,128]{1,0:T(8,128)S(1)} %get-tuple-element.60.slope_ref, bf16[3072,256]{1,0:T(8,128)(2,1)S(1)} %get-tuple-element.61.rhs_ref, ...), custom_call_target="tpu_custom_call" | custom-call | flops 100000000 | bytes 100000 | tf_op jit(solution)/shard_map/edge_terms/pallas_call | solution.py:319
  43.1 2.4 %edge_terms.5 = f32[256,128]{1,0:T(8,128)S(1)} custom-call(s32[3]{0:T(128)S(1)} %pad_add_fusion.where_ref, s32[2048]{0:T(1024)S(1)} %bitcast.25, f32[1024,128]{1,0:T(8,128)S(1)} %get-tuple-element.68.carry_ref, f32[3072,128]{1,0:T(8,128)S(1)} %get-tuple-element.60.slope_ref, bf16[3072,256]{1,0:T(8,128)(2,1)S(1)} %get-tuple-element.61.rhs_ref, ...), custom_call_target="tpu_custom_call" | custom-call | flops 100000000 | bytes 100000 | tf_op jit(solution)/shard_map/edge_terms/pallas_call | solution.py:319
  45.5 1.6 %collective-permute-start.13 = (f32[256,128]{1,0:T(8,128)S(1)}, f32[256,128]{1,0:T(8,128)S(1)}, u32[]{:S(2)}, u32[]{:S(2)}) collective-permute-start(f32[256,128]{1,0:T(8,128)S(1)} %edge_terms.5), channel_id=1, source_target_pairs={{0,16},{8,24},{16,0},{24,8},{1,17},{9,25},{17,1},{25,9},{2,18},{10... | collective-permute-start | bytes 393224 | tf_op jit(solution)/shard_map/sum_over_rows/ppermute | solution.py:334
  47.1 1.1 %collective-permute-start.12 = (f32[256,128]{1,0:T(8,128)S(1)}, f32[256,128]{1,0:T(8,128)S(1)}, u32[]{:S(2)}, u32[]{:S(2)}) collective-permute-start(f32[256,128]{1,0:T(8,128)S(1)} %edge_terms.4), channel_id=1, source_target_pairs={{0,24},{8,16},{16,8},{24,0},{1,25},{9,17},{17,9},{25,1},{2,26},{10... | collective-permute-start | bytes 393224 | tf_op jit(solution)/shard_map/sum_over_rows/ppermute | solution.py:334
  48.1 2.4 %edge_terms.6 = f32[256,128]{1,0:T(8,128)S(1)} custom-call(s32[3]{0:T(128)S(1)} %pad_add_fusion.where_ref, s32[2048]{0:T(1024)S(1)} %bitcast.26, f32[1024,128]{1,0:T(8,128)S(1)} %get-tuple-element.68.carry_ref, f32[3072,128]{1,0:T(8,128)S(1)} %get-tuple-element.60.slope_ref, bf16[3072,256]{1,0:T(8,128)(2,1)S(1)} %get-tuple-element.61.rhs_ref, ...), custom_call_target="tpu_custom_call" | custom-call | flops 100000000 | bytes 100000 | tf_op jit(solution)/shard_map/edge_terms/pallas_call | solution.py:319
  50.5 1.0 %collective-permute-start.14 = (f32[256,128]{1,0:T(8,128)S(1)}, f32[256,128]{1,0:T(8,128)S(1)}, u32[]{:S(2)}, u32[]{:S(2)}) collective-permute-start(f32[256,128]{1,0:T(8,128)S(1)} %edge_terms.6), channel_id=1, source_target_pairs={{0,8},{8,0},{16,24},{24,16},{1,9},{9,1},{17,25},{25,17},{2,10},{10... | collective-permute-start | bytes 393224 | tf_op jit(solution)/shard_map/sum_over_rows/ppermute | solution.py:334
  51.5 2.7 %collective-permute-done.13.refs_1_ = f32[256,128]{1,0:T(8,128)S(1)} collective-permute-done((f32[256,128]{1,0:T(8,128)S(1)}, f32[256,128]{1,0:T(8,128)S(1)}, u32[]{:S(2)}, u32[]{:S(2)}) %collective-permute-start.13) | collective-permute-done | bytes 131104 | tf_op jit(solution)/shard_map/sum_over_rows/ppermute | solution.py:334
  54.3 2.4 %edge_terms.7 = f32[256,128]{1,0:T(8,128)S(1)} custom-call(s32[3]{0:T(128)S(1)} %pad_add_fusion.where_ref, s32[2048]{0:T(1024)S(1)} %bitcast.27, f32[1024,128]{1,0:T(8,128)S(1)} %get-tuple-element.68.carry_ref, f32[3072,128]{1,0:T(8,128)S(1)} %get-tuple-element.60.slope_ref, bf16[3072,256]{1,0:T(8,128)(2,1)S(1)} %get-tuple-element.61.rhs_ref, ...), custom_call_target="tpu_custom_call" | custom-call | flops 100000000 | bytes 100000 | tf_op jit(solution)/shard_map/edge_terms/pallas_call | solution.py:319
  56.7 1.0 %collective-permute-start.15 = (f32[64,128]{1,0:T(8,128)S(1)}, f32[64,128]{1,0:T(8,128)S(1)}, u32[]{:S(2)}, u32[]{:S(2)}) collective-permute-start(f32[64,128]{1,0:T(8,128)S(1)} %get-tuple-element.73), channel_id=1, source_target_pairs={{0,2},{1,3},{2,4},{3,5},{4,6},{5,7},{6,0},{7,1},{8,10},{9,11},{10,... | collective-permute-start | bytes 98312 | tf_op jit(solution)/shard_map/sum_over_chips/ppermute | solution.py:345
  57.7 2.9 %collective-permute-start.17 = (f32[64,128]{1,0:T(8,128)S(1)}, f32[64,128]{1,0:T(8,128)S(1)}, u32[]{:S(2)}, u32[]{:S(2)}) collective-permute-start(f32[64,128]{1,0:T(8,128)S(1)} %get-tuple-element.74), channel_id=1, source_target_pairs={{0,6},{1,7},{2,0},{3,1},{4,2},{5,3},{6,4},{7,5},{8,14},{9,15},{10,... | collective-permute-start | bytes 98312 | tf_op jit(solution)/shard_map/sum_over_chips/ppermute | solution.py:345
  60.6 0.2 collective-permute-start.16
  60.8 1.8 %collective-permute-done.15 = f32[64,128]{1,0:T(8,128)S(1)} collective-permute-done((f32[64,128]{1,0:T(8,128)S(1)}, f32[64,128]{1,0:T(8,128)S(1)}, u32[]{:S(2)}, u32[]{:S(2)}) %collective-permute-start.15) | collective-permute-done | bytes 32800 | tf_op jit(solution)/shard_map/sum_over_chips/ppermute | solution.py:345
  62.6 2.9 %collective-permute-done.16 = f32[64,128]{1,0:T(8,128)S(1)} collective-permute-done((f32[64,128]{1,0:T(8,128)S(1)}, f32[64,128]{1,0:T(8,128)S(1)}, u32[]{:S(2)}, u32[]{:S(2)}) %collective-permute-start.16) | collective-permute-done | bytes 32800 | tf_op jit(solution)/shard_map/sum_over_chips/ppermute | solution.py:345
  65.4 0.6 fusion.2
  (25 shorter events, 0.3 us)
Async XLA Ops:
  0.0 23.0 %copy-start.2 = (s32[2048,2]{0,1:T(2,128)S(1)}, s32[2048,2]{0,1:T(2,128)}, u32[]{:S(2)}) copy-start(s32[2048,2]{0,1:T(2,128)} %param.5) | copy-start | bytes 49156
  0.1 1.1 %copy-start = (f32[32,3,1,16,128]{4,3,2,1,0:T(8,128)S(1)}, f32[32,3,1,16,128]{4,3,2,1,0:T(8,128)}, u32[]{:S(2)}) copy-start(f32[32,3,1,16,128]{4,3,2,1,0:T(8,128)} %param.3) | copy-start | bytes 2359300
  1.2 25.4 %copy-start.1 = (f32[128,128]{1,0:T(8,128)S(1)}, f32[128,128]{1,0:T(8,128)}, u32[]{:S(2)}) copy-start(f32[128,128]{1,0:T(8,128)} %coeffs_ref.3) | copy-start | bytes 196612
  2.2 19.7 %collective-permute-start = (f32[4,6,32,128]{3,2,1,0:T(8,128)S(1)}, f32[4,6,32,128]{3,2,1,0:T(8,128)S(1)}, u32[]{:S(2)}, u32[]{:S(2)}) collective-permute-start(f32[4,6,32,128]{3,2,1,0:T(8,128)S(1)} %get-tuple-element.37), channel_id=1, source_target_pairs={{0,7},{1,2},{2,1},{3,4},{4,3},{5,6},{6,5},{7,0},{8,15},{9,10},{10,... | collective-permute-start | bytes 1179656 | tf_op jit(solution)/shard_map/to_next_plane/ppermute | solution.py:261
  6.8 9.9 %collective-permute-start.1 = (f32[18,32,128]{2,1,0:T(8,128)S(1)}, f32[18,32,128]{2,1,0:T(8,128)S(1)}, u32[]{:S(2)}, u32[]{:S(2)}) collective-permute-start(f32[18,32,128]{2,1,0:T(8,128)S(1)} %get-tuple-element.39), channel_id=1, source_target_pairs={{0,8},{8,0},{16,24},{24,16},{1,9},{9,1},{17,25},{25,17},{2,10},{10... | collective-permute-start | bytes 884744 | tf_op jit(solution)/shard_map/to_rows/ppermute | solution.py:263
  8.3 13.6 %collective-permute-start.2 = (f32[18,32,128]{2,1,0:T(8,128)S(1)}, f32[18,32,128]{2,1,0:T(8,128)S(1)}, u32[]{:S(2)}, u32[]{:S(2)}) collective-permute-start(f32[18,32,128]{2,1,0:T(8,128)S(1)} %get-tuple-element.40), channel_id=1, source_target_pairs={{0,16},{8,24},{16,0},{24,8},{1,17},{9,25},{17,1},{25,9},{2,18},{10... | collective-permute-start | bytes 884744 | tf_op jit(solution)/shard_map/to_rows/ppermute | solution.py:263
  9.8 12.1 %collective-permute-start.3 = (f32[18,32,128]{2,1,0:T(8,128)S(1)}, f32[18,32,128]{2,1,0:T(8,128)S(1)}, u32[]{:S(2)}, u32[]{:S(2)}) collective-permute-start(f32[18,32,128]{2,1,0:T(8,128)S(1)} %get-tuple-element.42), channel_id=1, source_target_pairs={{0,24},{8,16},{16,8},{24,0},{1,25},{9,17},{17,9},{25,1},{2,26},{10... | collective-permute-start | bytes 884744 | tf_op jit(solution)/shard_map/to_rows/ppermute | solution.py:263
  21.9 2.3 %collective-permute-start.10 = (f32[18,32,128]{2,1,0:T(8,128)S(1)}, f32[18,32,128]{2,1,0:T(8,128)S(1)}, u32[]{:S(2)}, u32[]{:S(2)}) collective-permute-start(f32[18,32,128]{2,1,0:T(8,128)S(1)} %collective-permute-done.3.refs_3_), channel_id=1, source_target_pairs={{0,1},{1,0},{2,3},{3,2},{4,5},{5,4},{6,7},{7,6},{8,9},{9,8},{10,11... | collective-permute-start | bytes 884744 | tf_op jit(solution)/shard_map/to_other_core/ppermute | solution.py:270
  22.0 3.1 %collective-permute-start.7 = (f32[18,32,128]{2,1,0:T(8,128)S(1)}, f32[18,32,128]{2,1,0:T(8,128)S(1)}, u32[]{:S(2)}, u32[]{:S(2)}) collective-permute-start(f32[18,32,128]{2,1,0:T(8,128)S(1)} %get-tuple-element.47.refs_0_), channel_id=1, source_target_pairs={{0,1},{1,0},{2,3},{3,2},{4,5},{5,4},{6,7},{7,6},{8,9},{9,8},{10,11... | collective-permute-start | bytes 884744 | tf_op jit(solution)/shard_map/to_other_core/ppermute | solution.py:270
  22.5 4.1 %collective-permute-start.8 = (f32[18,32,128]{2,1,0:T(8,128)S(1)}, f32[18,32,128]{2,1,0:T(8,128)S(1)}, u32[]{:S(2)}, u32[]{:S(2)}) collective-permute-start(f32[18,32,128]{2,1,0:T(8,128)S(1)} %collective-permute-done.1.refs_1_), channel_id=1, source_target_pairs={{0,1},{1,0},{2,3},{3,2},{4,5},{5,4},{6,7},{7,6},{8,9},{9,8},{10,11... | collective-permute-start | bytes 884744 | tf_op jit(solution)/shard_map/to_other_core/ppermute | solution.py:270
  22.6 4.0 %collective-permute-start.9 = (f32[18,32,128]{2,1,0:T(8,128)S(1)}, f32[18,32,128]{2,1,0:T(8,128)S(1)}, u32[]{:S(2)}, u32[]{:S(2)}) collective-permute-start(f32[18,32,128]{2,1,0:T(8,128)S(1)} %collective-permute-done.2.refs_2_), channel_id=1, source_target_pairs={{0,1},{1,0},{2,3},{3,2},{4,5},{5,4},{6,7},{7,6},{8,9},{9,8},{10,11... | collective-permute-start | bytes 884744 | tf_op jit(solution)/shard_map/to_other_core/ppermute | solution.py:270
  23.0 11.9 %collective-permute-start.4 = (f32[6,32,128]{2,1,0:T(8,128)S(1)}, f32[6,32,128]{2,1,0:T(8,128)S(1)}, u32[]{:S(2)}, u32[]{:S(2)}) collective-permute-start(f32[6,32,128]{2,1,0:T(8,128)S(1)} %get-tuple-element.44), channel_id=1, source_target_pairs={{0,8},{8,0},{16,24},{24,16},{1,9},{9,1},{17,25},{25,17},{2,10},{10... | collective-permute-start | bytes 294920 | tf_op jit(solution)/shard_map/next_to_rows/ppermute | solution.py:268
  24.2 10.7 %collective-permute-start.5 = (f32[6,32,128]{2,1,0:T(8,128)S(1)}, f32[6,32,128]{2,1,0:T(8,128)S(1)}, u32[]{:S(2)}, u32[]{:S(2)}) collective-permute-start(f32[6,32,128]{2,1,0:T(8,128)S(1)} %get-tuple-element.45), channel_id=1, source_target_pairs={{0,16},{8,24},{16,0},{24,8},{1,17},{9,25},{17,1},{25,9},{2,18},{10... | collective-permute-start | bytes 294920 | tf_op jit(solution)/shard_map/next_to_rows/ppermute | solution.py:268
  25.2 9.8 %collective-permute-start.6 = (f32[6,32,128]{2,1,0:T(8,128)S(1)}, f32[6,32,128]{2,1,0:T(8,128)S(1)}, u32[]{:S(2)}, u32[]{:S(2)}) collective-permute-start(f32[6,32,128]{2,1,0:T(8,128)S(1)} %get-tuple-element.46), channel_id=1, source_target_pairs={{0,24},{8,16},{16,8},{24,0},{1,25},{9,17},{17,9},{25,1},{2,26},{10... | collective-permute-start | bytes 294920 | tf_op jit(solution)/shard_map/next_to_rows/ppermute | solution.py:268
  35.0 4.3 %collective-permute-start.11 = (f32[4,6,32,128]{3,2,1,0:T(8,128)S(1)}, f32[4,6,32,128]{3,2,1,0:T(8,128)S(1)}, u32[]{:S(2)}, u32[]{:S(2)}) collective-permute-start(f32[4,6,32,128]{3,2,1,0:T(8,128)S(1)} %pad_maximum_fusion), channel_id=1, source_target_pairs={{0,1},{1,0},{2,3},{3,2},{4,5},{5,4},{6,7},{7,6},{8,9},{9,8},{10,11... | collective-permute-start | bytes 1179656 | tf_op jit(solution)/shard_map/next_to_other_core/ppermute | solution.py:292
  45.5 8.8 %collective-permute-start.13 = (f32[256,128]{1,0:T(8,128)S(1)}, f32[256,128]{1,0:T(8,128)S(1)}, u32[]{:S(2)}, u32[]{:S(2)}) collective-permute-start(f32[256,128]{1,0:T(8,128)S(1)} %edge_terms.5), channel_id=1, source_target_pairs={{0,16},{8,24},{16,0},{24,8},{1,17},{9,25},{17,1},{25,9},{2,18},{10... | collective-permute-start | bytes 393224 | tf_op jit(solution)/shard_map/sum_over_rows/ppermute | solution.py:334
  47.1 7.2 %collective-permute-start.12 = (f32[256,128]{1,0:T(8,128)S(1)}, f32[256,128]{1,0:T(8,128)S(1)}, u32[]{:S(2)}, u32[]{:S(2)}) collective-permute-start(f32[256,128]{1,0:T(8,128)S(1)} %edge_terms.4), channel_id=1, source_target_pairs={{0,24},{8,16},{16,8},{24,0},{1,25},{9,17},{17,9},{25,1},{2,26},{10... | collective-permute-start | bytes 393224 | tf_op jit(solution)/shard_map/sum_over_rows/ppermute | solution.py:334
  50.5 6.1 %collective-permute-start.14 = (f32[256,128]{1,0:T(8,128)S(1)}, f32[256,128]{1,0:T(8,128)S(1)}, u32[]{:S(2)}, u32[]{:S(2)}) collective-permute-start(f32[256,128]{1,0:T(8,128)S(1)} %edge_terms.6), channel_id=1, source_target_pairs={{0,8},{8,0},{16,24},{24,16},{1,9},{9,1},{17,25},{25,17},{2,10},{10... | collective-permute-start | bytes 393224 | tf_op jit(solution)/shard_map/sum_over_rows/ppermute | solution.py:334
  56.7 5.8 %collective-permute-start.15 = (f32[64,128]{1,0:T(8,128)S(1)}, f32[64,128]{1,0:T(8,128)S(1)}, u32[]{:S(2)}, u32[]{:S(2)}) collective-permute-start(f32[64,128]{1,0:T(8,128)S(1)} %get-tuple-element.73), channel_id=1, source_target_pairs={{0,2},{1,3},{2,4},{3,5},{4,6},{5,7},{6,0},{7,1},{8,10},{9,11},{10,... | collective-permute-start | bytes 98312 | tf_op jit(solution)/shard_map/sum_over_chips/ppermute | solution.py:345
  57.7 4.8 %collective-permute-start.17 = (f32[64,128]{1,0:T(8,128)S(1)}, f32[64,128]{1,0:T(8,128)S(1)}, u32[]{:S(2)}, u32[]{:S(2)}) collective-permute-start(f32[64,128]{1,0:T(8,128)S(1)} %get-tuple-element.74), channel_id=1, source_target_pairs={{0,6},{1,7},{2,0},{3,1},{4,2},{5,3},{6,4},{7,5},{8,14},{9,15},{10,... | collective-permute-start | bytes 98312 | tf_op jit(solution)/shard_map/sum_over_chips/ppermute | solution.py:345
  60.6 4.8 %collective-permute-start.16 = (f32[64,128]{1,0:T(8,128)S(1)}, f32[64,128]{1,0:T(8,128)S(1)}, u32[]{:S(2)}, u32[]{:S(2)}) collective-permute-start(f32[64,128]{1,0:T(8,128)S(1)} %get-tuple-element.75), channel_id=1, source_target_pairs={{0,4},{1,5},{2,6},{3,7},{4,0},{5,1},{6,2},{7,3},{8,12},{9,13},{10,... | collective-permute-start | bytes 98312 | tf_op jit(solution)/shard_map/sum_over_chips/ppermute | solution.py:345

commit v7 on v6

--- a/solution.py
+++ b/solution.py
@@ -17,25 +17,49 @@
     return high, low
 
 
+def border_lane(rows_y, lanes, c):
+    per_slab = lanes // (2 * rows_y)
+    return c // per_slab, c % per_slab * 2 * rows_y
+
+
+def border_slabs(rows_y, lanes):
+    return border_lane(rows_y, lanes, 2)[0] + 1
+
+
 def pack_kernel(where_ref, field_ref, *out_refs, sizes):
-    local_s, rows_y, block_rows, tm_count = sizes
+    local_s, rows_y, tm_count = sizes
+    lanes = field_ref.shape[1]
     t, core = where_ref[0], where_ref[2]
-    half = block_rows // 2
+    width, groups = lanes // tm_count, rows_y // tm_count
+    lane = lax.broadcasted_iota(jnp.int32, (local_s, lanes), 1)
+    starts = [jnp.bitwise_xor(t, peer) * width for peer in range(tm_count)]
+    borders = [[jnp.zeros((local_s, lanes), F32) for _ in range(tm_count)] for _ in range(border_slabs(rows_y, lanes))]
+    for c in range(3):
+        slab, first_lane = border_lane(rows_y, lanes, c)
+
+        def one_group(g, border, c=c, first_lane=first_lane):
+            border = list(border)
+            main = [None] * tm_count
+            for q in range(tm_count):
+                y = q * groups + g
+                row = field_ref[pl.ds(c * rows_y + y, local_s, stride=3 * rows_y), :]
+                for peer, start in enumerate(starts):
+                    moved = pltpu.roll(row, jnp.bitwise_and(q * width - start, lanes - 1), 1)
+                    main[peer] = moved if q == 0 else jnp.where(lane < q * width, main[peer], moved)
+                    for side, column in ((0, start - 1), (1, start + width)):
+                        target = first_lane + side * rows_y + y
+                        moved = pltpu.roll(row, jnp.bitwise_and(target - column, lanes - 1), 1)
+                        border[peer] = jnp.where(lane == target, moved, border[peer])
+            for peer in range(tm_count):
+                out_refs[peer][g * 3 + c] = main[peer]
+            return tuple(border)
+
+        borders[slab] = lax.fori_loop(0, groups, one_group, tuple(borders[slab]))
+    half = groups // 2 * 3
     for peer in range(tm_count):
-        first_row = jnp.bitwise_xor(t, peer) * block_rows
-        for row in range(block_rows + 2):
-            if row < block_rows:
-                y = first_row + row
-            else:
-                y = first_row - 1 if row == block_rows else first_row + block_rows
-                inside = jnp.logical_and(y >= 0, y < rows_y)
-                y = jnp.clip(y, 0, rows_y - 1)
-            for c in range(3):
-                slab = field_ref[pl.ds(c * rows_y + y, local_s, stride=3 * rows_y), :]
-                if row >= block_rows:
-                    slab = jnp.where(inside, slab, 0.0)
-                out_refs[peer][row * 3 + c] = slab
-        out_refs[tm_count][peer] = out_refs[peer][pl.ds(core * (half * 3), half * 3)]
+        for slab, border in enumerate(borders):
+            out_refs[peer][groups * 3 + slab] = border[peer]
+        out_refs[tm_count][peer] = out_refs[peer][pl.ds(core * half, half)]
 
 
 def mode_weights(where_ref, coeffs_ref, local_s, tm_count):
@@ -118,18 +142,43 @@
         slab_ref[1, index] = result[:, lanes:]
         return 0
 
-    lax.fori_loop(0, (block_rows + 2) * 3, one_slab, 0, unroll=3)
+    slabs = own[0].shape[0]
+    lax.fori_loop(0, slabs, one_slab, 0, unroll=2 if slabs % 2 == 0 else 1)
+    width, rows_y = lanes // tm_count, block_rows * tm_count
+    lane = lax.broadcasted_iota(jnp.int32, (1, lanes), 1)
+    part, column = lax.div(lane, width), lax.rem(lane, width)
+    has_border = jnp.where(column == 0, -0.5, jnp.where(column == width - 1, 0.5, 0.0))
+    border_of = jnp.where(column == 0, 0, rows_y) + part * block_rows
+    border_lanes = lax.broadcasted_iota(jnp.int32, (2 * lanes, lanes), 0)
+    border_lanes = jnp.where(border_lanes >= lanes, border_lanes - lanes, border_lanes)
+    borders = []
+    for slab in range(3 * block_rows, slabs):
+        both = jnp.concatenate([slab_ref[0, slab], slab_ref[1, slab]], axis=0)
+        borders.append(jnp.concatenate(split_high_low(both), axis=1))
     for c in range(3):
+        slab, first_lane = border_lane(rows_y, lanes, c)
         for row in range(block_rows):
-            above = (row + 1 if row + 1 < block_rows else block_rows + 1) * 3 + c
-            below = (row - 1 if row > 0 else block_rows) * 3 + c
             center = row * 3 + c
+            pick = jnp.where(border_lanes == border_of + (first_lane + row), has_border, 0.0).astype(BF16)
+            border = jnp.dot(borders[slab], pick, preferred_element_type=F32)
             for plane in range(2):
                 place = plane * block_rows + row
                 value = slab_ref[plane, center]
                 stream = slab_ref[1 - plane, center] * (0.5 if plane == 0 else -0.5)
-                normal = (slab_ref[plane, above] - slab_ref[plane, below]) * 0.5
-                span = (pltpu.roll(value, lanes - 1, 1) - pltpu.roll(value, 1, 1)) * 0.5
+                if row + 1 < block_rows:
+                    above = slab_ref[plane, center + 3]
+                else:
+                    above = pltpu.roll(slab_ref[plane, c], lanes - width, 1)
+                    above = jnp.where(lane < lanes - width, above, 0.0)
+                if row > 0:
+                    below = slab_ref[plane, center - 3]
+                else:
+                    below = pltpu.roll(slab_ref[plane, 3 * (block_rows - 1) + c], width, 1)
+                    below = jnp.where(lane >= width, below, 0.0)
+                normal = (above - below) * 0.5
+                after = jnp.where(column < width - 1, pltpu.roll(value, lanes - 1, 1), 0.0)
+                before = jnp.where(column > 0, pltpu.roll(value, 1, 1), 0.0)
+                span = (after - before) * 0.5 + border[plane * modes : (plane + 1) * modes]
                 carry_ref[pl.ds(c * height + place, modes, stride=3 * height), :] = value
                 for d, slope in enumerate((stream, normal, span)):
                     slope_ref[pl.ds((d * 3 + c) * height + place, modes, stride=9 * height), :] = slope
@@ -231,6 +280,7 @@
     local_s, _, _, rows_y, lanes = snapshots.shape
     modes = coeffs.shape[1]
     block_rows = rows_y // tm_count
+    slabs = 3 * block_rows + border_slabs(rows_y, lanes)
     share = pair_table.shape[0] // (tm_count * space_count)
     factor = float(space_count * rows_y * lanes) ** (-0.5)
     bits = modes.bit_length() - 1
@@ -249,8 +299,8 @@
 
     with jax.named_scope("pack"):
         packed = pl.pallas_call(
-            functools.partial(pack_kernel, sizes=(local_s, rows_y, block_rows, tm_count)),
-            out_shape=[pltpu.VMEM(((block_rows + 2) * 3, local_s, lanes), F32)] * tm_count
+            functools.partial(pack_kernel, sizes=(local_s, rows_y, tm_count)),
+            out_shape=[pltpu.VMEM((slabs, local_s, lanes), F32)] * tm_count
             + [pltpu.VMEM((tm_count, block_rows // 2 * 3, local_s, lanes), F32)],
             in_specs=[smem, vmem],
             out_specs=[vmem] * (tm_count + 1),
@@ -259,15 +309,14 @@
     with jax.named_scope("to_next_plane"):
         ring = [(place, (place + (1 if place % 2 else -1)) % space_count) for place in range(space_count)]
         across_edge = lax.ppermute(packed[tm_count], "space", ring)
-    with jax.named_scope("to_rows"):
+    with jax.named_scope("to_columns"):
         own = [packed[0]] + [lax.ppermute(packed[peer], "tm", across(peer)) for peer in range(1, tm_count)]
-    with jax.named_scope("next_to_rows"):
-        across_edge, own[:3] = lax.optimization_barrier((across_edge, own[:3]))
-        parts = [across_edge[peer] for peer in range(tm_count)]
-        parts, own[3:] = lax.optimization_barrier((parts, own[3:]))
-        next_own = [parts[0]] + [lax.ppermute(parts[peer], "tm", across(peer)) for peer in range(1, tm_count)]
     with jax.named_scope("to_other_core"):
         other = [lax.ppermute(piece, "space", swap) for piece in own]
+    with jax.named_scope("next_to_columns"):
+        across_edge, own, other = lax.optimization_barrier((across_edge, own, other))
+        parts = [across_edge[peer] for peer in range(tm_count)]
+        next_own = [parts[0]] + [lax.ppermute(parts[peer], "tm", across(peer)) for peer in range(1, tm_count)]
     early = tm_count // 2
     work = [pltpu.VMEM((block * 3 * height, lanes), F32)]
     groups = pltpu.VMEM((early, block, modes), F32)
@@ -283,7 +332,7 @@
             ],
             in_specs=[smem, smem] + [vmem] * (2 * tm_count + 1),
             out_specs=[vmem] * 5,
-            scratch_shapes=[pltpu.VMEM((2, (block_rows + 2) * 3, modes, lanes), F32)] + work,
+            scratch_shapes=[pltpu.VMEM((2, slabs, modes, lanes), F32)] + work,
             compiler_params=vmem_limit(24),
             cost_estimate=pl.CostEstimate(flops=12 * 10**9, bytes_accessed=10**7, transcendentals=0),
         )(where, codes, coeffs, *[in_vmem(piece) for piece in (*own, *other)])
@@ -329,11 +378,14 @@
                 codes,
                 *[in_vmem(table) for table in (*tables, early_sums if peer >= early else late_sums, *parts)],
             )
-        with jax.named_scope("sum_over_rows"):
+        with jax.named_scope("sum_over_columns"):
             if peer:
                 arrived.append(lax.ppermute(summed, "tm", across(peer)))
-                tables[0], _ = lax.optimization_barrier((tables[0], summed))
-    with jax.named_scope("sum_over_rows"):
+                if peer > early:
+                    early_sums, _ = lax.optimization_barrier((early_sums, summed))
+                else:
+                    late_sums, _ = lax.optimization_barrier((late_sums, summed))
+    with jax.named_scope("sum_over_columns"):
         summed = summed + arrived[-1]
     with jax.named_scope("sum_over_chips"):
         shares = summed.reshape(chips, share, modes)

time: 66.2 us -> 66.7 us (level)
  waiting for transfers between devices: 19 us -> 14.8 us
  Pallas kernels: 24.5 us -> 28.4 us
  other arithmetic: 0.76 us -> 1.55 us
    ppermute x3, waiting for transfers between devices: 11.6 us -> 5.56 us  [shards(): lax.ppermute(packed[peer], 'tm', across(peer))]
    pallas_call x1, Pallas kernels: 1.01 us -> 3.89 us  [shards(): pl.pallas_call(functools.partial(pack_kernel, sizes=(local_s, rows_y, tm_...]
    ppermute x1, waiting for transfers between devices: 0.01 us -> 2.07 us  [shards(): across_edge = lax.ppermute(packed[tm_count], 'space', ring)]
    ppermute x3, starting transfers between devices: 3.49 us -> 4.54 us  [shards(): lax.ppermute(packed[peer], 'tm', across(peer))]
    pallas_call x1, Pallas kernels: 8.3 us -> 9.25 us  [shards(): pl.pallas_call(functools.partial(inner_kernel, first_peer=early, sizes=(l...]
    add x1, other arithmetic: 0.01 us -> 0.81 us  [shards(): codes = pair_table[:, 0] * modes + pair_table[:, 1]]
  transfers between devices with their start and end apart: 18 -> 18, of which waited for: 5 -> 7; matrix products, arithmetic and copies ran while one was open for 0% -> 1% of each run, Pallas kernels for 26% -> 31%
where the time goes in v7:
time: 66.7 us; the launch traced here: 66.5 us
  Pallas kernels  28.4 us (43%)
  starting transfers between devices  20.4 us (31%)
  waiting for transfers between devices  14.8 us (22%)
  other arithmetic  1.55 us (2%)
  local copies, waits for them, and re-layouts  1.18 us (2%)
    pallas_call x4, Pallas kernels, shards(): pl.pallas_call(functools.partial(edge_kernel, peer=peer, sizes=(chips, sh...  9.63 us
    pallas_call x1, Pallas kernels, shards(): pl.pallas_call(functools.partial(inner_kernel, first_peer=early, sizes=(l...  9.25 us
    ppermute x3, waiting for transfers between devices, shards(): lax.ppermute(packed[peer], 'tm', across(peer))  5.56 us
    ppermute x3, waiting for transfers between devices, shards(): result = result + lax.ppermute(shares[step], 'space', shift)  4.81 us
    ppermute x3, starting transfers between devices, shards(): lax.ppermute(packed[peer], 'tm', across(peer))  4.54 us
    pallas_call x1, Pallas kernels, shards(): pl.pallas_call(functools.partial(pairs_kernel, first_peer=0, sizes=(heigh...  4.21 us
    ppermute x1, starting transfers between devices, shards(): across_edge = lax.ppermute(packed[tm_count], 'space', ring)  4.17 us
    pallas_call x1, Pallas kernels, shards(): pl.pallas_call(functools.partial(pack_kernel, sizes=(local_s, rows_y, tm_...  3.89 us
  transfers between devices with their start and end apart: 18, of which 7 were waited for; matrix products, arithmetic and copies ran while one was open for 1% of the time, Pallas kernels for 31%

profile of v7, /device:TPU:0, one launch (start us, length us, event | category | flops | bytes accessed | tf_op | source)
XLA Modules:
  0.0 66.5 jit_solution(7857639239145129532)
XLA Ops:
  0.0 0.1 pad_add_fusion.where_ref
  0.1 1.1 %copy-done = f32[32,3,1,16,128]{4,3,2,1,0:T(8,128)S(1)} copy-done((f32[32,3,1,16,128]{4,3,2,1,0:T(8,128)S(1)}, f32[32,3,1,16,128]{4,3,2,1,0:T(8,128)}, u32[]{:S(2)}) %copy-start) | copy-done | bytes 786456
  1.2 3.9 %pack.1 = (f32[13,32,128]{2,1,0:T(8,128)S(1)}, f32[13,32,128]{2,1,0:T(8,128)S(1)}, f32[13,32,128]{2,1,0:T(8,128)S(1)}, f32[13,32,128]{2,1,0:T(8,128)S(1)}, f32[4,6,32,128]{3,2,1,0:T(8,128)S(1)}) custom-call(s32[3]{0:T(128)S(1)} %pad_add_fusion.where_ref, f32[1536,128]{1,0:T(8,128)S(1)} %bitcast.18), custom_call_target="tpu_custom_call" | custom-call | tf_op jit(solution)/shard_map/pack/pallas_call | solution.py:301
  5.1 3.0 %collective-permute-start.1 = (f32[13,32,128]{2,1,0:T(8,128)S(1)}, f32[13,32,128]{2,1,0:T(8,128)S(1)}, u32[]{:S(2)}, u32[]{:S(2)}) collective-permute-start(f32[13,32,128]{2,1,0:T(8,128)S(1)} %get-tuple-element.39), channel_id=1, source_target_pairs={{0,8},{8,0},{16,24},{24,16},{1,9},{9,1},{17,25},{25,17},{2,10},{10... | collective-permute-start | bytes 638984 | tf_op jit(solution)/shard_map/to_columns/ppermute | solution.py:313
  8.1 1.5 %collective-permute-start.2 = (f32[13,32,128]{2,1,0:T(8,128)S(1)}, f32[13,32,128]{2,1,0:T(8,128)S(1)}, u32[]{:S(2)}, u32[]{:S(2)}) collective-permute-start(f32[13,32,128]{2,1,0:T(8,128)S(1)} %get-tuple-element.40), channel_id=1, source_target_pairs={{0,16},{8,24},{16,0},{24,8},{1,17},{9,25},{17,1},{25,9},{2,18},{10... | collective-permute-start | bytes 638984 | tf_op jit(solution)/shard_map/to_columns/ppermute | solution.py:313
  9.7 4.2 %collective-permute-start = (f32[4,6,32,128]{3,2,1,0:T(8,128)S(1)}, f32[4,6,32,128]{3,2,1,0:T(8,128)S(1)}, u32[]{:S(2)}, u32[]{:S(2)}) collective-permute-start(f32[4,6,32,128]{3,2,1,0:T(8,128)S(1)} %get-tuple-element.37), channel_id=1, source_target_pairs={{0,7},{1,2},{2,1},{3,4},{4,3},{5,6},{6,5},{7,0},{8,15},{9,10},{10,... | collective-permute-start | bytes 1179656 | tf_op jit(solution)/shard_map/to_next_plane/ppermute | solution.py:311
  13.8 0.4 collective-permute-done.1.refs_1_
  14.2 5.2 %collective-permute-done.2.refs_2_ = f32[13,32,128]{2,1,0:T(8,128)S(1)} collective-permute-done((f32[13,32,128]{2,1,0:T(8,128)S(1)}, f32[13,32,128]{2,1,0:T(8,128)S(1)}, u32[]{:S(2)}, u32[]{:S(2)}) %collective-permute-start.2) | collective-permute-done | bytes 213024 | tf_op jit(solution)/shard_map/to_columns/ppermute | solution.py:313
  19.4 0.5 collective-permute-start.7
  19.9 0.8 %slice_add_fusion.1 = s32[2048,1]{0,1:T(1,128)S(1)} fusion(s32[2048,2]{0,1:T(2,128)} %param.5), kind=kLoop, calls=%fused_computation.9 | loop fusion | flops 4096 | bytes 24576 | tf_op jit(solution)/shard_map/add | solution.py:288
  20.7 2.1 %collective-permute-done = f32[4,6,32,128]{3,2,1,0:T(8,128)S(1)} collective-permute-done((f32[4,6,32,128]{3,2,1,0:T(8,128)S(1)}, f32[4,6,32,128]{3,2,1,0:T(8,128)S(1)}, u32[]{:S(2)}, u32[]{:S(2)}) %collective-permute-start) | collective-permute-done | bytes 393248 | tf_op jit(solution)/shard_map/to_next_plane/ppermute | solution.py:311
  22.8 2.5 %collective-permute-start.10 = (f32[6,32,128]{2,1,0:T(8,128)S(1)}, f32[6,32,128]{2,1,0:T(8,128)S(1)}, u32[]{:S(2)}, u32[]{:S(2)}) collective-permute-start(f32[6,32,128]{2,1,0:T(8,128)S(1)} %get-tuple-element.69), channel_id=1, source_target_pairs={{0,24},{8,16},{16,8},{24,0},{1,25},{9,17},{17,9},{25,1},{2,26},{10... | collective-permute-start | bytes 294920 | tf_op jit(solution)/shard_map/next_to_columns/ppermute | solution.py:319
  25.4 0.5 collective-permute-start.9
  25.9 0.5 collective-permute-start.8
  26.4 9.3 %inner_terms.2 = (f32[12,128,128]{2,1,0:T(8,128)S(1)}, f32[3072,128]{1,0:T(8,128)S(1)}, f32[9216,128]{1,0:T(8,128)S(1)}, bf16[3072,256]{1,0:T(8,128)(2,1)S(1)}, f32[2,256,128]{2,1,0:T(8,128)S(1)}) custom-call(s32[3]{0:T(128)S(1)} %pad_add_fusion.where_ref, s32[2048]{0:T(1024)S(1)} %bitcast.22, f32[128,128]{1,0:T(8,128)S(1)} %copy-done.1, ...), custom_call_target="tpu_custom_call" | custom-call | flops 12000000000 | bytes 10000000 | tf_op jit(solution)/shard_map/inner_terms/pallas_call | solution.py:324
  35.7 0.1 collective-permute-start.11
  35.8 4.2 %inner_terms.3.inner_ref = f32[2,256,128]{2,1,0:T(8,128)S(1)} custom-call(s32[3]{0:T(128)S(1)} %pad_add_fusion.where_ref, s32[2048]{0:T(1024)S(1)} %bitcast.23, f32[3072,128]{1,0:T(8,128)S(1)} %get-tuple-element.62.carry_ref, f32[9216,128]{1,0:T(8,128)S(1)} %get-tuple-element.63.slope_ref, bf16[3072,256]{1,0:T(8,128)(2,1)S(1)} %get-tuple-element.64.rhs_ref), custom_call_target="tpu_custom_call" | custom-call | flops 8000000000 | bytes 10000000 | tf_op jit(solution)/shard_map/inner_terms/pallas_call | solution.py:343
  40.0 1.4 %edge_tables.1 = (f32[1024,128]{1,0:T(8,128)S(1)}, f32[3072,128]{1,0:T(8,128)S(1)}, bf16[3072,256]{1,0:T(8,128)(2,1)S(1)}) custom-call(s32[3]{0:T(128)S(1)} %pad_add_fusion.where_ref, f32[128,128]{1,0:T(8,128)S(1)} %copy-done.1, f32[6,32,128]{2,1,0:T(8,128)S(1)} %get-tuple-element.54.refs_0_, f32[6,32,128]{2,1,0:T(8,128)S(1)} %collective-permute-done.8.refs_1_, ...), custom_call_target="tpu_custom_call" | custom-call | tf_op jit(solution)/shard_map/edge_tables/pallas_call | solution.py:353
  41.4 2.4 %edge_terms.4 = f32[256,128]{1,0:T(8,128)S(1)} custom-call(s32[3]{0:T(128)S(1)} %pad_add_fusion.where_ref, s32[2048]{0:T(1024)S(1)} %bitcast.24, f32[1024,128]{1,0:T(8,128)S(1)} %get-tuple-element.59.carry_ref, f32[3072,128]{1,0:T(8,128)S(1)} %get-tuple-element.60.slope_ref, bf16[3072,256]{1,0:T(8,128)(2,1)S(1)} %get-tuple-element.61.rhs_ref, ...), custom_call_target="tpu_custom_call" | custom-call | flops 100000000 | bytes 100000 | tf_op jit(solution)/shard_map/edge_terms/pallas_call | solution.py:368
  43.8 2.5 %collective-permute-start.12 = (f32[256,128]{1,0:T(8,128)S(1)}, f32[256,128]{1,0:T(8,128)S(1)}, u32[]{:S(2)}, u32[]{:S(2)}) collective-permute-start(f32[256,128]{1,0:T(8,128)S(1)} %edge_terms.4), channel_id=1, source_target_pairs={{0,24},{8,16},{16,8},{24,0},{1,25},{9,17},{17,9},{25,1},{2,26},{10... | collective-permute-start | bytes 393224 | tf_op jit(solution)/shard_map/sum_over_columns/ppermute | solution.py:383
  46.3 2.4 %edge_terms.5 = f32[256,128]{1,0:T(8,128)S(1)} custom-call(s32[3]{0:T(128)S(1)} %pad_add_fusion.where_ref, s32[2048]{0:T(1024)S(1)} %bitcast.25, f32[1024,128]{1,0:T(8,128)S(1)} %get-tuple-element.59.carry_ref, f32[3072,128]{1,0:T(8,128)S(1)} %get-tuple-element.60.slope_ref, bf16[3072,256]{1,0:T(8,128)(2,1)S(1)} %get-tuple-element.61.rhs_ref, ...), custom_call_target="tpu_custom_call" | custom-call | flops 100000000 | bytes 100000 | tf_op jit(solution)/shard_map/edge_terms/pallas_call | solution.py:368
  48.7 0.6 collective-permute-start.13
  49.3 2.4 %edge_terms.6 = f32[256,128]{1,0:T(8,128)S(1)} custom-call(s32[3]{0:T(128)S(1)} %pad_add_fusion.where_ref, s32[2048]{0:T(1024)S(1)} %bitcast.26, f32[1024,128]{1,0:T(8,128)S(1)} %get-tuple-element.59.carry_ref, f32[3072,128]{1,0:T(8,128)S(1)} %get-tuple-element.60.slope_ref, bf16[3072,256]{1,0:T(8,128)(2,1)S(1)} %get-tuple-element.61.rhs_ref, ...), custom_call_target="tpu_custom_call" | custom-call | flops 100000000 | bytes 100000 | tf_op jit(solution)/shard_map/edge_terms/pallas_call | solution.py:368
  51.7 0.6 collective-permute-start.14
  52.3 2.1 %collective-permute-done.13.refs_1_ = f32[256,128]{1,0:T(8,128)S(1)} collective-permute-done((f32[256,128]{1,0:T(8,128)S(1)}, f32[256,128]{1,0:T(8,128)S(1)}, u32[]{:S(2)}, u32[]{:S(2)}) %collective-permute-start.13) | collective-permute-done | bytes 131104 | tf_op jit(solution)/shard_map/sum_over_columns/ppermute | solution.py:383
  54.4 2.4 %edge_terms.7 = f32[256,128]{1,0:T(8,128)S(1)} custom-call(s32[3]{0:T(128)S(1)} %pad_add_fusion.where_ref, s32[2048]{0:T(1024)S(1)} %bitcast.27, f32[1024,128]{1,0:T(8,128)S(1)} %get-tuple-element.59.carry_ref, f32[3072,128]{1,0:T(8,128)S(1)} %get-tuple-element.60.slope_ref, bf16[3072,256]{1,0:T(8,128)(2,1)S(1)} %get-tuple-element.61.rhs_ref, ...), custom_call_target="tpu_custom_call" | custom-call | flops 100000000 | bytes 100000 | tf_op jit(solution)/shard_map/edge_terms/pallas_call | solution.py:368
  56.9 0.3 collective-permute-done.14
  57.2 0.1 collective-permute-start.15
  57.2 3.8 %collective-permute-start.17 = (f32[64,128]{1,0:T(8,128)S(1)}, f32[64,128]{1,0:T(8,128)S(1)}, u32[]{:S(2)}, u32[]{:S(2)}) collective-permute-start(f32[64,128]{1,0:T(8,128)S(1)} %get-tuple-element.74), channel_id=1, source_target_pairs={{0,6},{1,7},{2,0},{3,1},{4,2},{5,3},{6,4},{7,5},{8,14},{9,15},{10,... | collective-permute-start | bytes 98312 | tf_op jit(solution)/shard_map/sum_over_chips/ppermute | solution.py:397
  61.0 1.9 %collective-permute-done.15 = f32[64,128]{1,0:T(8,128)S(1)} collective-permute-done((f32[64,128]{1,0:T(8,128)S(1)}, f32[64,128]{1,0:T(8,128)S(1)}, u32[]{:S(2)}, u32[]{:S(2)}) %collective-permute-start.15) | collective-permute-done | bytes 32800 | tf_op jit(solution)/shard_map/sum_over_chips/ppermute | solution.py:397
  62.9 2.9 %collective-permute-done.16 = f32[64,128]{1,0:T(8,128)S(1)} collective-permute-done((f32[64,128]{1,0:T(8,128)S(1)}, f32[64,128]{1,0:T(8,128)S(1)}, u32[]{:S(2)}, u32[]{:S(2)}) %collective-permute-start.16) | collective-permute-done | bytes 32800 | tf_op jit(solution)/shard_map/sum_over_chips/ppermute | solution.py:397
  65.9 0.6 fusion.2
  (23 shorter events, 0.1 us)
Async XLA Ops:
  0.1 1.1 %copy-start = (f32[32,3,1,16,128]{4,3,2,1,0:T(8,128)S(1)}, f32[32,3,1,16,128]{4,3,2,1,0:T(8,128)}, u32[]{:S(2)}) copy-start(f32[32,3,1,16,128]{4,3,2,1,0:T(8,128)} %param.3) | copy-start | bytes 2359300
  1.2 25.2 %copy-start.1 = (f32[128,128]{1,0:T(8,128)S(1)}, f32[128,128]{1,0:T(8,128)}, u32[]{:S(2)}) copy-start(f32[128,128]{1,0:T(8,128)} %coeffs_ref.3) | copy-start | bytes 196612
  5.1 9.1 %collective-permute-start.1 = (f32[13,32,128]{2,1,0:T(8,128)S(1)}, f32[13,32,128]{2,1,0:T(8,128)S(1)}, u32[]{:S(2)}, u32[]{:S(2)}) collective-permute-start(f32[13,32,128]{2,1,0:T(8,128)S(1)} %get-tuple-element.39), channel_id=1, source_target_pairs={{0,8},{8,0},{16,24},{24,16},{1,9},{9,1},{17,25},{25,17},{2,10},{10... | collective-permute-start | bytes 638984 | tf_op jit(solution)/shard_map/to_columns/ppermute | solution.py:313
  8.1 11.3 %collective-permute-start.2 = (f32[13,32,128]{2,1,0:T(8,128)S(1)}, f32[13,32,128]{2,1,0:T(8,128)S(1)}, u32[]{:S(2)}, u32[]{:S(2)}) collective-permute-start(f32[13,32,128]{2,1,0:T(8,128)S(1)} %get-tuple-element.40), channel_id=1, source_target_pairs={{0,16},{8,24},{16,0},{24,8},{1,17},{9,25},{17,1},{25,9},{2,18},{10... | collective-permute-start | bytes 638984 | tf_op jit(solution)/shard_map/to_columns/ppermute | solution.py:313
  9.6 9.8 %collective-permute-start.3 = (f32[13,32,128]{2,1,0:T(8,128)S(1)}, f32[13,32,128]{2,1,0:T(8,128)S(1)}, u32[]{:S(2)}, u32[]{:S(2)}) collective-permute-start(f32[13,32,128]{2,1,0:T(8,128)S(1)} %get-tuple-element.41), channel_id=1, source_target_pairs={{0,24},{8,16},{16,8},{24,0},{1,25},{9,17},{17,9},{25,1},{2,26},{10... | collective-permute-start | bytes 638984 | tf_op jit(solution)/shard_map/to_columns/ppermute | solution.py:313
  9.7 11.1 %collective-permute-start.4 = (f32[13,32,128]{2,1,0:T(8,128)S(1)}, f32[13,32,128]{2,1,0:T(8,128)S(1)}, u32[]{:S(2)}, u32[]{:S(2)}) collective-permute-start(f32[13,32,128]{2,1,0:T(8,128)S(1)} %get-tuple-element.43.refs_0_), channel_id=1, source_target_pairs={{0,1},{1,0},{2,3},{3,2},{4,5},{5,4},{6,7},{7,6},{8,9},{9,8},{10,11... | collective-permute-start | bytes 638984 | tf_op jit(solution)/shard_map/to_other_core/ppermute | solution.py:315
  9.7 13.1 %collective-permute-start = (f32[4,6,32,128]{3,2,1,0:T(8,128)S(1)}, f32[4,6,32,128]{3,2,1,0:T(8,128)S(1)}, u32[]{:S(2)}, u32[]{:S(2)}) collective-permute-start(f32[4,6,32,128]{3,2,1,0:T(8,128)S(1)} %get-tuple-element.37), channel_id=1, source_target_pairs={{0,7},{1,2},{2,1},{3,4},{4,3},{5,6},{6,5},{7,0},{8,15},{9,10},{10,... | collective-permute-start | bytes 1179656 | tf_op jit(solution)/shard_map/to_next_plane/ppermute | solution.py:311
  14.2 8.6 %collective-permute-start.5 = (f32[13,32,128]{2,1,0:T(8,128)S(1)}, f32[13,32,128]{2,1,0:T(8,128)S(1)}, u32[]{:S(2)}, u32[]{:S(2)}) collective-permute-start(f32[13,32,128]{2,1,0:T(8,128)S(1)} %collective-permute-done.1.refs_1_), channel_id=1, source_target_pairs={{0,1},{1,0},{2,3},{3,2},{4,5},{5,4},{6,7},{7,6},{8,9},{9,8},{10,11... | collective-permute-start | bytes 638984 | tf_op jit(solution)/shard_map/to_other_core/ppermute | solution.py:315
  19.4 3.4 %collective-permute-start.6 = (f32[13,32,128]{2,1,0:T(8,128)S(1)}, f32[13,32,128]{2,1,0:T(8,128)S(1)}, u32[]{:S(2)}, u32[]{:S(2)}) collective-permute-start(f32[13,32,128]{2,1,0:T(8,128)S(1)} %collective-permute-done.2.refs_2_), channel_id=1, source_target_pairs={{0,1},{1,0},{2,3},{3,2},{4,5},{5,4},{6,7},{7,6},{8,9},{9,8},{10,11... | collective-permute-start | bytes 638984 | tf_op jit(solution)/shard_map/to_other_core/ppermute | solution.py:315
  19.4 3.4 %collective-permute-start.7 = (f32[13,32,128]{2,1,0:T(8,128)S(1)}, f32[13,32,128]{2,1,0:T(8,128)S(1)}, u32[]{:S(2)}, u32[]{:S(2)}) collective-permute-start(f32[13,32,128]{2,1,0:T(8,128)S(1)} %collective-permute-done.3.refs_3_), channel_id=1, source_target_pairs={{0,1},{1,0},{2,3},{3,2},{4,5},{5,4},{6,7},{7,6},{8,9},{9,8},{10,11... | collective-permute-start | bytes 638984 | tf_op jit(solution)/shard_map/to_other_core/ppermute | solution.py:315
  22.8 12.8 %collective-permute-start.10 = (f32[6,32,128]{2,1,0:T(8,128)S(1)}, f32[6,32,128]{2,1,0:T(8,128)S(1)}, u32[]{:S(2)}, u32[]{:S(2)}) collective-permute-start(f32[6,32,128]{2,1,0:T(8,128)S(1)} %get-tuple-element.69), channel_id=1, source_target_pairs={{0,24},{8,16},{16,8},{24,0},{1,25},{9,17},{17,9},{25,1},{2,26},{10... | collective-permute-start | bytes 294920 | tf_op jit(solution)/shard_map/next_to_columns/ppermute | solution.py:319
  25.4 10.3 %collective-permute-start.9 = (f32[6,32,128]{2,1,0:T(8,128)S(1)}, f32[6,32,128]{2,1,0:T(8,128)S(1)}, u32[]{:S(2)}, u32[]{:S(2)}) collective-permute-start(f32[6,32,128]{2,1,0:T(8,128)S(1)} %get-tuple-element.70), channel_id=1, source_target_pairs={{0,16},{8,24},{16,0},{24,8},{1,17},{9,25},{17,1},{25,9},{2,18},{10... | collective-permute-start | bytes 294920 | tf_op jit(solution)/shard_map/next_to_columns/ppermute | solution.py:319
  25.9 9.8 %collective-permute-start.8 = (f32[6,32,128]{2,1,0:T(8,128)S(1)}, f32[6,32,128]{2,1,0:T(8,128)S(1)}, u32[]{:S(2)}, u32[]{:S(2)}) collective-permute-start(f32[6,32,128]{2,1,0:T(8,128)S(1)} %get-tuple-element.71), channel_id=1, source_target_pairs={{0,8},{8,0},{16,24},{24,16},{1,9},{9,1},{17,25},{25,17},{2,10},{10... | collective-permute-start | bytes 294920 | tf_op jit(solution)/shard_map/next_to_columns/ppermute | solution.py:319
  35.7 4.3 %collective-permute-start.11 = (f32[4,6,32,128]{3,2,1,0:T(8,128)S(1)}, f32[4,6,32,128]{3,2,1,0:T(8,128)S(1)}, u32[]{:S(2)}, u32[]{:S(2)}) collective-permute-start(f32[4,6,32,128]{3,2,1,0:T(8,128)S(1)} %pad_maximum_fusion), channel_id=1, source_target_pairs={{0,1},{1,0},{2,3},{3,2},{4,5},{5,4},{6,7},{7,6},{8,9},{9,8},{10,11... | collective-permute-start | bytes 1179656 | tf_op jit(solution)/shard_map/next_to_other_core/ppermute | solution.py:341
  43.8 10.6 %collective-permute-start.12 = (f32[256,128]{1,0:T(8,128)S(1)}, f32[256,128]{1,0:T(8,128)S(1)}, u32[]{:S(2)}, u32[]{:S(2)}) collective-permute-start(f32[256,128]{1,0:T(8,128)S(1)} %edge_terms.4), channel_id=1, source_target_pairs={{0,24},{8,16},{16,8},{24,0},{1,25},{9,17},{17,9},{25,1},{2,26},{10... | collective-permute-start | bytes 393224 | tf_op jit(solution)/shard_map/sum_over_columns/ppermute | solution.py:383
  48.7 5.7 %collective-permute-start.13 = (f32[256,128]{1,0:T(8,128)S(1)}, f32[256,128]{1,0:T(8,128)S(1)}, u32[]{:S(2)}, u32[]{:S(2)}) collective-permute-start(f32[256,128]{1,0:T(8,128)S(1)} %edge_terms.5), channel_id=1, source_target_pairs={{0,16},{8,24},{16,0},{24,8},{1,17},{9,25},{17,1},{25,9},{2,18},{10... | collective-permute-start | bytes 393224 | tf_op jit(solution)/shard_map/sum_over_columns/ppermute | solution.py:383
  51.7 5.4 %collective-permute-start.14 = (f32[256,128]{1,0:T(8,128)S(1)}, f32[256,128]{1,0:T(8,128)S(1)}, u32[]{:S(2)}, u32[]{:S(2)}) collective-permute-start(f32[256,128]{1,0:T(8,128)S(1)} %edge_terms.6), channel_id=1, source_target_pairs={{0,8},{8,0},{16,24},{24,16},{1,9},{9,1},{17,25},{25,17},{2,10},{10... | collective-permute-start | bytes 393224 | tf_op jit(solution)/shard_map/sum_over_columns/ppermute | solution.py:383
  57.2 5.8 %collective-permute-start.15 = (f32[64,128]{1,0:T(8,128)S(1)}, f32[64,128]{1,0:T(8,128)S(1)}, u32[]{:S(2)}, u32[]{:S(2)}) collective-permute-start(f32[64,128]{1,0:T(8,128)S(1)} %get-tuple-element.73), channel_id=1, source_target_pairs={{0,2},{1,3},{2,4},{3,5},{4,6},{5,7},{6,0},{7,1},{8,10},{9,11},{10,... | collective-permute-start | bytes 98312 | tf_op jit(solution)/shard_map/sum_over_chips/ppermute | solution.py:397
  57.2 5.7 %collective-permute-start.17 = (f32[64,128]{1,0:T(8,128)S(1)}, f32[64,128]{1,0:T(8,128)S(1)}, u32[]{:S(2)}, u32[]{:S(2)}) collective-permute-start(f32[64,128]{1,0:T(8,128)S(1)} %get-tuple-element.74), channel_id=1, source_target_pairs={{0,6},{1,7},{2,0},{3,1},{4,2},{5,3},{6,4},{7,5},{8,14},{9,15},{10,... | collective-permute-start | bytes 98312 | tf_op jit(solution)/shard_map/sum_over_chips/ppermute | solution.py:397
  61.0 4.8 %collective-permute-start.16 = (f32[64,128]{1,0:T(8,128)S(1)}, f32[64,128]{1,0:T(8,128)S(1)}, u32[]{:S(2)}, u32[]{:S(2)}) collective-permute-start(f32[64,128]{1,0:T(8,128)S(1)} %get-tuple-element.75), channel_id=1, source_target_pairs={{0,4},{1,5},{2,6},{3,7},{4,0},{5,1},{6,2},{7,3},{8,12},{9,13},{10,... | collective-permute-start | bytes 98312 | tf_op jit(solution)/shard_map/sum_over_chips/ppermute | solution.py:397

commit v8 on v7

--- a/solution.py
+++ b/solution.py
@@ -26,40 +26,58 @@
     return border_lane(rows_y, lanes, 2)[0] + 1
 
 
-def pack_kernel(where_ref, field_ref, *out_refs, sizes):
+def exchange_blocks(rows, lane, width, lanes):
+    rows = list(rows)
+    step = len(rows) // 2
+    while step:
+        keeps = jnp.bitwise_and(lane, step * width) == 0
+        for low in range(len(rows)):
+            if low & step == 0:
+                first, second = rows[low], rows[low + step]
+                rows[low] = jnp.where(keeps, first, pltpu.roll(second, step * width, 1))
+                rows[low + step] = jnp.where(keeps, pltpu.roll(first, lanes - step * width, 1), second)
+        step //= 2
+    return rows
+
+
+def pack_kernel(where_ref, field_ref, *refs, sizes):
+    *out_refs, sorted_ref = refs
     local_s, rows_y, tm_count = sizes
     lanes = field_ref.shape[1]
     t, core = where_ref[0], where_ref[2]
     width, groups = lanes // tm_count, rows_y // tm_count
     lane = lax.broadcasted_iota(jnp.int32, (local_s, lanes), 1)
-    starts = [jnp.bitwise_xor(t, peer) * width for peer in range(tm_count)]
     borders = [[jnp.zeros((local_s, lanes), F32) for _ in range(tm_count)] for _ in range(border_slabs(rows_y, lanes))]
     for c in range(3):
         slab, first_lane = border_lane(rows_y, lanes, c)
 
         def one_group(g, border, c=c, first_lane=first_lane):
             border = list(border)
-            main = [None] * tm_count
+            rows = []
             for q in range(tm_count):
                 y = q * groups + g
                 row = field_ref[pl.ds(c * rows_y + y, local_s, stride=3 * rows_y), :]
-                for peer, start in enumerate(starts):
-                    moved = pltpu.roll(row, jnp.bitwise_and(q * width - start, lanes - 1), 1)
-                    main[peer] = moved if q == 0 else jnp.where(lane < q * width, main[peer], moved)
-                    for side, column in ((0, start - 1), (1, start + width)):
-                        target = first_lane + side * rows_y + y
-                        moved = pltpu.roll(row, jnp.bitwise_and(target - column, lanes - 1), 1)
-                        border[peer] = jnp.where(lane == target, moved, border[peer])
-            for peer in range(tm_count):
-                out_refs[peer][g * 3 + c] = main[peer]
+                rows.append(row)
+                for side in range(2):
+                    shift = first_lane + side * (rows_y - width - 1) + y
+                    moved = pltpu.roll(row, jnp.bitwise_and(shift, lanes - 1), 1)
+                    for block in range(tm_count):
+                        column = (block + 1) * width if side else block * width - 1
+                        is_here = lane == jnp.bitwise_and(shift + column, lanes - 1)
+                        border[block] = jnp.where(is_here, moved, border[block])
+            for block, main in enumerate(exchange_blocks(rows, lane, width, lanes)):
+                sorted_ref[block, g * 3 + c] = main
             return tuple(border)
 
         borders[slab] = lax.fori_loop(0, groups, one_group, tuple(borders[slab]))
     half = groups // 2 * 3
+    for slab, border in enumerate(borders):
+        for block in range(tm_count):
+            sorted_ref[block, groups * 3 + slab] = border[block]
     for peer in range(tm_count):
-        for slab, border in enumerate(borders):
-            out_refs[peer][groups * 3 + slab] = border[peer]
-        out_refs[tm_count][peer] = out_refs[peer][pl.ds(core * half, half)]
+        block = jnp.bitwise_xor(t, peer)
+        out_refs[peer][...] = sorted_ref[block]
+        out_refs[tm_count][peer] = sorted_ref[block, pl.ds(core * half, half)]
 
 
 def mode_weights(where_ref, coeffs_ref, local_s, tm_count):
@@ -148,7 +166,8 @@
     lane = lax.broadcasted_iota(jnp.int32, (1, lanes), 1)
     part, column = lax.div(lane, width), lax.rem(lane, width)
     has_border = jnp.where(column == 0, -0.5, jnp.where(column == width - 1, 0.5, 0.0))
-    border_of = jnp.where(column == 0, 0, rows_y) + part * block_rows
+    t = where_ref[0]
+    border_of = jnp.where(column == 0, 0, rows_y) + t * width - 1 + part * block_rows
     border_lanes = lax.broadcasted_iota(jnp.int32, (2 * lanes, lanes), 0)
     border_lanes = jnp.where(border_lanes >= lanes, border_lanes - lanes, border_lanes)
     borders = []
@@ -159,8 +178,14 @@
         slab, first_lane = border_lane(rows_y, lanes, c)
         for row in range(block_rows):
             center = row * 3 + c
-            pick = jnp.where(border_lanes == border_of + (first_lane + row), has_border, 0.0).astype(BF16)
-            border = jnp.dot(borders[slab], pick, preferred_element_type=F32)
+            if row % 2 == 0:
+                picks = [
+                    jnp.where(
+                        border_lanes == jnp.bitwise_and(border_of + (first_lane + row + k), lanes - 1), has_border, 0.0
+                    ).astype(BF16)
+                    for k in range(2)
+                ]
+                border = jnp.dot(borders[slab], jnp.concatenate(picks, axis=1), preferred_element_type=F32)
             for plane in range(2):
                 place = plane * block_rows + row
                 value = slab_ref[plane, center]
@@ -178,7 +203,7 @@
                 normal = (above - below) * 0.5
                 after = jnp.where(column < width - 1, pltpu.roll(value, lanes - 1, 1), 0.0)
                 before = jnp.where(column > 0, pltpu.roll(value, 1, 1), 0.0)
-                span = (after - before) * 0.5 + border[plane * modes : (plane + 1) * modes]
+                span = (after - before) * 0.5 + border[plane * modes : (plane + 1) * modes, row % 2 * lanes : (row % 2 + 1) * lanes]
                 carry_ref[pl.ds(c * height + place, modes, stride=3 * height), :] = value
                 for d, slope in enumerate((stream, normal, span)):
                     slope_ref[pl.ds((d * 3 + c) * height + place, modes, stride=9 * height), :] = slope
@@ -304,6 +329,7 @@
             + [pltpu.VMEM((tm_count, block_rows // 2 * 3, local_s, lanes), F32)],
             in_specs=[smem, vmem],
             out_specs=[vmem] * (tm_count + 1),
+            scratch_shapes=[pltpu.VMEM((tm_count, slabs, local_s, lanes), F32)],
             compiler_params=vmem_limit(16),
         )(where, snapshots.reshape(-1, lanes))
     with jax.named_scope("to_next_plane"):
@@ -311,12 +337,13 @@
         across_edge = lax.ppermute(packed[tm_count], "space", ring)
     with jax.named_scope("to_columns"):
         own = [packed[0]] + [lax.ppermute(packed[peer], "tm", across(peer)) for peer in range(1, tm_count)]
+    with jax.named_scope("next_to_columns"):
+        across_edge, own[:3] = lax.optimization_barrier((across_edge, own[:3]))
+        parts = [across_edge[peer] for peer in range(tm_count)]
+        parts, own[3:] = lax.optimization_barrier((parts, own[3:]))
+        next_own = [parts[0]] + [lax.ppermute(parts[peer], "tm", across(peer)) for peer in range(1, tm_count)]
     with jax.named_scope("to_other_core"):
         other = [lax.ppermute(piece, "space", swap) for piece in own]
-    with jax.named_scope("next_to_columns"):
-        across_edge, own, other = lax.optimization_barrier((across_edge, own, other))
-        parts = [across_edge[peer] for peer in range(tm_count)]
-        next_own = [parts[0]] + [lax.ppermute(parts[peer], "tm", across(peer)) for peer in range(1, tm_count)]
     early = tm_count // 2
     work = [pltpu.VMEM((block * 3 * height, lanes), F32)]
     groups = pltpu.VMEM((early, block, modes), F32)

time: 66.7 us -> 64.5 us (0.967)
  Pallas kernels: 28.4 us -> 27.1 us
  other arithmetic: 1.55 us -> 0.76 us
    ppermute x3, waiting for transfers between devices: 5.56 us -> 8.18 us  [shards(): lax.ppermute(packed[peer], 'tm', across(peer))]
    ppermute x1, waiting for transfers between devices: 2.07 us -> 0.01 us  [shards(): across_edge = lax.ppermute(packed[tm_count], 'space', ring)]
    pallas_call x1, Pallas kernels: 3.89 us -> 2.66 us  [shards(): pl.pallas_call(functools.partial(pack_kernel, sizes=(local_s, rows_y, tm_...]
    ppermute x3, starting transfers between devices: 4.54 us -> 3.49 us  [shards(): lax.ppermute(packed[peer], 'tm', across(peer))]
    add x1, other arithmetic: 0.81 us -> 0.01 us  [shards(): codes = pair_table[:, 0] * modes + pair_table[:, 1]]
  transfers between devices with their start and end apart: 18 -> 18, of which waited for: 7 -> 6; matrix products, arithmetic and copies ran while one was open for 1% -> 0% of each run, Pallas kernels for 31% -> 32%
where the time goes in v8:
time: 64.5 us; the launch traced here: 64.4 us
  Pallas kernels  27.1 us (42%)
  starting transfers between devices  20.3 us (31%)
  waiting for transfers between devices  14.9 us (23%)
  local copies, waits for them, and re-layouts  1.18 us (2%)
  other arithmetic  0.76 us (1%)
    pallas_call x4, Pallas kernels, shards(): pl.pallas_call(functools.partial(edge_kernel, peer=peer, sizes=(chips, sh...  9.63 us
    pallas_call x1, Pallas kernels, shards(): pl.pallas_call(functools.partial(inner_kernel, first_peer=early, sizes=(l...  9.19 us
    ppermute x3, waiting for transfers between devices, shards(): lax.ppermute(packed[peer], 'tm', across(peer))  8.18 us
    ppermute x3, waiting for transfers between devices, shards(): result = result + lax.ppermute(shares[step], 'space', shift)  4.81 us
    ppermute x1, starting transfers between devices, shards(): across_edge = lax.ppermute(packed[tm_count], 'space', ring)  4.55 us
    pallas_call x1, Pallas kernels, shards(): pl.pallas_call(functools.partial(pairs_kernel, first_peer=0, sizes=(heigh...  4.21 us
    ppermute x3, starting transfers between devices, shards(): result = result + lax.ppermute(shares[step], 'space', shift)  3.88 us
    ppermute x3, starting transfers between devices, shards(): arrived.append(lax.ppermute(summed, 'tm', across(peer)))  3.68 us
  transfers between devices with their start and end apart: 18, of which 6 were waited for; matrix products, arithmetic and copies ran while one was open for 0% of the time, Pallas kernels for 32%

profile of v8, /device:TPU:0, one launch (start us, length us, event | category | flops | bytes accessed | tf_op | source)
XLA Modules:
  0.0 64.4 jit_solution(9313188342962772280)
XLA Ops:
  0.0 0.1 pad_add_fusion.where_ref
  0.1 1.1 %copy-done = f32[32,3,1,16,128]{4,3,2,1,0:T(8,128)S(1)} copy-done((f32[32,3,1,16,128]{4,3,2,1,0:T(8,128)S(1)}, f32[32,3,1,16,128]{4,3,2,1,0:T(8,128)}, u32[]{:S(2)}) %copy-start) | copy-done | bytes 786456
  1.2 2.7 %pack.1 = (f32[13,32,128]{2,1,0:T(8,128)S(1)}, f32[13,32,128]{2,1,0:T(8,128)S(1)}, f32[13,32,128]{2,1,0:T(8,128)S(1)}, f32[13,32,128]{2,1,0:T(8,128)S(1)}, f32[4,6,32,128]{3,2,1,0:T(8,128)S(1)}) custom-call(s32[3]{0:T(128)S(1)} %pad_add_fusion.where_ref, f32[1536,128]{1,0:T(8,128)S(1)} %bitcast.18), custom_call_target="tpu_custom_call" | custom-call | tf_op jit(solution)/shard_map/pack/pallas_call | solution.py:326
  3.9 4.6 %collective-permute-start = (f32[4,6,32,128]{3,2,1,0:T(8,128)S(1)}, f32[4,6,32,128]{3,2,1,0:T(8,128)S(1)}, u32[]{:S(2)}, u32[]{:S(2)}) collective-permute-start(f32[4,6,32,128]{3,2,1,0:T(8,128)S(1)} %get-tuple-element.37), channel_id=1, source_target_pairs={{0,7},{1,2},{2,1},{3,4},{4,3},{5,6},{6,5},{7,0},{8,15},{9,10},{10,... | collective-permute-start | bytes 1179656 | tf_op jit(solution)/shard_map/to_next_plane/ppermute | solution.py:337
  8.4 1.5 %collective-permute-start.1 = (f32[13,32,128]{2,1,0:T(8,128)S(1)}, f32[13,32,128]{2,1,0:T(8,128)S(1)}, u32[]{:S(2)}, u32[]{:S(2)}) collective-permute-start(f32[13,32,128]{2,1,0:T(8,128)S(1)} %get-tuple-element.39), channel_id=1, source_target_pairs={{0,8},{8,0},{16,24},{24,16},{1,9},{9,1},{17,25},{25,17},{2,10},{10... | collective-permute-start | bytes 638984 | tf_op jit(solution)/shard_map/to_columns/ppermute | solution.py:339
  9.9 1.5 %collective-permute-start.2 = (f32[13,32,128]{2,1,0:T(8,128)S(1)}, f32[13,32,128]{2,1,0:T(8,128)S(1)}, u32[]{:S(2)}, u32[]{:S(2)}) collective-permute-start(f32[13,32,128]{2,1,0:T(8,128)S(1)} %get-tuple-element.40), channel_id=1, source_target_pairs={{0,16},{8,24},{16,0},{24,8},{1,17},{9,25},{17,1},{25,9},{2,18},{10... | collective-permute-start | bytes 638984 | tf_op jit(solution)/shard_map/to_columns/ppermute | solution.py:339
  11.5 0.5 collective-permute-start.3
  11.9 4.6 %collective-permute-done.1.refs_1_ = f32[13,32,128]{2,1,0:T(8,128)S(1)} collective-permute-done((f32[13,32,128]{2,1,0:T(8,128)S(1)}, f32[13,32,128]{2,1,0:T(8,128)S(1)}, u32[]{:S(2)}, u32[]{:S(2)}) %collective-permute-start.1) | collective-permute-done | bytes 213024 | tf_op jit(solution)/shard_map/to_columns/ppermute | solution.py:339
  16.5 3.6 %collective-permute-done.2.refs_2_ = f32[13,32,128]{2,1,0:T(8,128)S(1)} collective-permute-done((f32[13,32,128]{2,1,0:T(8,128)S(1)}, f32[13,32,128]{2,1,0:T(8,128)S(1)}, u32[]{:S(2)}, u32[]{:S(2)}) %collective-permute-start.2) | collective-permute-done | bytes 213024 | tf_op jit(solution)/shard_map/to_columns/ppermute | solution.py:339
  20.2 0.5 collective-permute-start.7
  20.7 0.1 collective-permute-start.8
  20.8 0.4 collective-permute-start.9
  21.3 1.1 %collective-permute-start.4 = (f32[6,32,128]{2,1,0:T(8,128)S(1)}, f32[6,32,128]{2,1,0:T(8,128)S(1)}, u32[]{:S(2)}, u32[]{:S(2)}) collective-permute-start(f32[6,32,128]{2,1,0:T(8,128)S(1)} %get-tuple-element.44), channel_id=1, source_target_pairs={{0,8},{8,0},{16,24},{24,16},{1,9},{9,1},{17,25},{25,17},{2,10},{10... | collective-permute-start | bytes 294920 | tf_op jit(solution)/shard_map/next_to_columns/ppermute | solution.py:344
  22.4 0.9 %collective-permute-start.5 = (f32[6,32,128]{2,1,0:T(8,128)S(1)}, f32[6,32,128]{2,1,0:T(8,128)S(1)}, u32[]{:S(2)}, u32[]{:S(2)}) collective-permute-start(f32[6,32,128]{2,1,0:T(8,128)S(1)} %get-tuple-element.45), channel_id=1, source_target_pairs={{0,16},{8,24},{16,0},{24,8},{1,17},{9,25},{17,1},{25,9},{2,18},{10... | collective-permute-start | bytes 294920 | tf_op jit(solution)/shard_map/next_to_columns/ppermute | solution.py:344
  23.3 1.5 %collective-permute-start.6 = (f32[6,32,128]{2,1,0:T(8,128)S(1)}, f32[6,32,128]{2,1,0:T(8,128)S(1)}, u32[]{:S(2)}, u32[]{:S(2)}) collective-permute-start(f32[6,32,128]{2,1,0:T(8,128)S(1)} %get-tuple-element.46), channel_id=1, source_target_pairs={{0,24},{8,16},{16,8},{24,0},{1,25},{9,17},{17,9},{25,1},{2,26},{10... | collective-permute-start | bytes 294920 | tf_op jit(solution)/shard_map/next_to_columns/ppermute | solution.py:344
  24.8 9.2 %inner_terms.2 = (f32[12,128,128]{2,1,0:T(8,128)S(1)}, f32[3072,128]{1,0:T(8,128)S(1)}, f32[9216,128]{1,0:T(8,128)S(1)}, bf16[3072,256]{1,0:T(8,128)(2,1)S(1)}, f32[2,256,128]{2,1,0:T(8,128)S(1)}) custom-call(s32[3]{0:T(128)S(1)} %pad_add_fusion.where_ref, s32[2048]{0:T(1024)S(1)} %bitcast.22, f32[128,128]{1,0:T(8,128)S(1)} %copy-done.1, ...), custom_call_target="tpu_custom_call" | custom-call | flops 12000000000 | bytes 10000000 | tf_op jit(solution)/shard_map/inner_terms/pallas_call | solution.py:351
  34.2 4.2 %inner_terms.3.inner_ref = f32[2,256,128]{2,1,0:T(8,128)S(1)} custom-call(s32[3]{0:T(128)S(1)} %pad_add_fusion.where_ref, s32[2048]{0:T(1024)S(1)} %bitcast.23, f32[3072,128]{1,0:T(8,128)S(1)} %get-tuple-element.62.carry_ref, f32[9216,128]{1,0:T(8,128)S(1)} %get-tuple-element.63.slope_ref, bf16[3072,256]{1,0:T(8,128)(2,1)S(1)} %get-tuple-element.64.rhs_ref), custom_call_target="tpu_custom_call" | custom-call | flops 8000000000 | bytes 10000000 | tf_op jit(solution)/shard_map/inner_terms/pallas_call | solution.py:370
  38.4 1.4 %edge_tables.1 = (f32[1024,128]{1,0:T(8,128)S(1)}, f32[3072,128]{1,0:T(8,128)S(1)}, bf16[3072,256]{1,0:T(8,128)(2,1)S(1)}) custom-call(s32[3]{0:T(128)S(1)} %pad_add_fusion.where_ref, f32[128,128]{1,0:T(8,128)S(1)} %copy-done.1, f32[6,32,128]{2,1,0:T(8,128)S(1)} %get-tuple-element.54.refs_0_, f32[6,32,128]{2,1,0:T(8,128)S(1)} %collective-permute-done.4.refs_1_, ...), custom_call_target="tpu_custom_call" | custom-call | tf_op jit(solution)/shard_map/edge_tables/pallas_call | solution.py:380
  39.8 2.4 %edge_terms.4 = f32[256,128]{1,0:T(8,128)S(1)} custom-call(s32[3]{0:T(128)S(1)} %pad_add_fusion.where_ref, s32[2048]{0:T(1024)S(1)} %bitcast.24, f32[1024,128]{1,0:T(8,128)S(1)} %get-tuple-element.59.carry_ref, f32[3072,128]{1,0:T(8,128)S(1)} %get-tuple-element.60.slope_ref, bf16[3072,256]{1,0:T(8,128)(2,1)S(1)} %get-tuple-element.61.rhs_ref, ...), custom_call_target="tpu_custom_call" | custom-call | flops 100000000 | bytes 100000 | tf_op jit(solution)/shard_map/edge_terms/pallas_call | solution.py:395
  42.2 1.5 %collective-permute-start.12 = (f32[256,128]{1,0:T(8,128)S(1)}, f32[256,128]{1,0:T(8,128)S(1)}, u32[]{:S(2)}, u32[]{:S(2)}) collective-permute-start(f32[256,128]{1,0:T(8,128)S(1)} %edge_terms.4), channel_id=1, source_target_pairs={{0,24},{8,16},{16,8},{24,0},{1,25},{9,17},{17,9},{25,1},{2,26},{10... | collective-permute-start | bytes 393224 | tf_op jit(solution)/shard_map/sum_over_columns/ppermute | solution.py:410
  43.7 2.4 %edge_terms.5 = f32[256,128]{1,0:T(8,128)S(1)} custom-call(s32[3]{0:T(128)S(1)} %pad_add_fusion.where_ref, s32[2048]{0:T(1024)S(1)} %bitcast.25, f32[1024,128]{1,0:T(8,128)S(1)} %get-tuple-element.59.carry_ref, f32[3072,128]{1,0:T(8,128)S(1)} %get-tuple-element.60.slope_ref, bf16[3072,256]{1,0:T(8,128)(2,1)S(1)} %get-tuple-element.61.rhs_ref, ...), custom_call_target="tpu_custom_call" | custom-call | flops 100000000 | bytes 100000 | tf_op jit(solution)/shard_map/edge_terms/pallas_call | solution.py:395
  46.1 1.2 %collective-permute-start.13 = (f32[256,128]{1,0:T(8,128)S(1)}, f32[256,128]{1,0:T(8,128)S(1)}, u32[]{:S(2)}, u32[]{:S(2)}) collective-permute-start(f32[256,128]{1,0:T(8,128)S(1)} %edge_terms.5), channel_id=1, source_target_pairs={{0,16},{8,24},{16,0},{24,8},{1,17},{9,25},{17,1},{25,9},{2,18},{10... | collective-permute-start | bytes 393224 | tf_op jit(solution)/shard_map/sum_over_columns/ppermute | solution.py:410
  47.2 2.4 %edge_terms.6 = f32[256,128]{1,0:T(8,128)S(1)} custom-call(s32[3]{0:T(128)S(1)} %pad_add_fusion.where_ref, s32[2048]{0:T(1024)S(1)} %bitcast.26, f32[1024,128]{1,0:T(8,128)S(1)} %get-tuple-element.59.carry_ref, f32[3072,128]{1,0:T(8,128)S(1)} %get-tuple-element.60.slope_ref, bf16[3072,256]{1,0:T(8,128)(2,1)S(1)} %get-tuple-element.61.rhs_ref, ...), custom_call_target="tpu_custom_call" | custom-call | flops 100000000 | bytes 100000 | tf_op jit(solution)/shard_map/edge_terms/pallas_call | solution.py:395
  49.6 1.1 %collective-permute-start.14 = (f32[256,128]{1,0:T(8,128)S(1)}, f32[256,128]{1,0:T(8,128)S(1)}, u32[]{:S(2)}, u32[]{:S(2)}) collective-permute-start(f32[256,128]{1,0:T(8,128)S(1)} %edge_terms.6), channel_id=1, source_target_pairs={{0,8},{8,0},{16,24},{24,16},{1,9},{9,1},{17,25},{25,17},{2,10},{10... | collective-permute-start | bytes 393224 | tf_op jit(solution)/shard_map/sum_over_columns/ppermute | solution.py:410
  50.7 1.2 %collective-permute-done.13.refs_1_ = f32[256,128]{1,0:T(8,128)S(1)} collective-permute-done((f32[256,128]{1,0:T(8,128)S(1)}, f32[256,128]{1,0:T(8,128)S(1)}, u32[]{:S(2)}, u32[]{:S(2)}) %collective-permute-start.13) | collective-permute-done | bytes 131104 | tf_op jit(solution)/shard_map/sum_over_columns/ppermute | solution.py:410
  51.9 2.4 %edge_terms.7 = f32[256,128]{1,0:T(8,128)S(1)} custom-call(s32[3]{0:T(128)S(1)} %pad_add_fusion.where_ref, s32[2048]{0:T(1024)S(1)} %bitcast.27, f32[1024,128]{1,0:T(8,128)S(1)} %get-tuple-element.59.carry_ref, f32[3072,128]{1,0:T(8,128)S(1)} %get-tuple-element.60.slope_ref, bf16[3072,256]{1,0:T(8,128)(2,1)S(1)} %get-tuple-element.61.rhs_ref, ...), custom_call_target="tpu_custom_call" | custom-call | flops 100000000 | bytes 100000 | tf_op jit(solution)/shard_map/edge_terms/pallas_call | solution.py:395
  54.3 0.8 %collective-permute-done.14 = f32[256,128]{1,0:T(8,128)S(1)} collective-permute-done((f32[256,128]{1,0:T(8,128)S(1)}, f32[256,128]{1,0:T(8,128)S(1)}, u32[]{:S(2)}, u32[]{:S(2)}) %collective-permute-start.14) | collective-permute-done | bytes 131104 | tf_op jit(solution)/shard_map/sum_over_columns/ppermute | solution.py:410
  55.1 0.4 collective-permute-start.15
  55.5 3.5 %collective-permute-start.17 = (f32[64,128]{1,0:T(8,128)S(1)}, f32[64,128]{1,0:T(8,128)S(1)}, u32[]{:S(2)}, u32[]{:S(2)}) collective-permute-start(f32[64,128]{1,0:T(8,128)S(1)} %get-tuple-element.74), channel_id=1, source_target_pairs={{0,6},{1,7},{2,0},{3,1},{4,2},{5,3},{6,4},{7,5},{8,14},{9,15},{10,... | collective-permute-start | bytes 98312 | tf_op jit(solution)/shard_map/sum_over_chips/ppermute | solution.py:424
  59.0 1.9 %collective-permute-done.15 = f32[64,128]{1,0:T(8,128)S(1)} collective-permute-done((f32[64,128]{1,0:T(8,128)S(1)}, f32[64,128]{1,0:T(8,128)S(1)}, u32[]{:S(2)}, u32[]{:S(2)}) %collective-permute-start.15) | collective-permute-done | bytes 32800 | tf_op jit(solution)/shard_map/sum_over_chips/ppermute | solution.py:424
  60.9 2.9 %collective-permute-done.16 = f32[64,128]{1,0:T(8,128)S(1)} collective-permute-done((f32[64,128]{1,0:T(8,128)S(1)}, f32[64,128]{1,0:T(8,128)S(1)}, u32[]{:S(2)}, u32[]{:S(2)}) %collective-permute-start.16) | collective-permute-done | bytes 32800 | tf_op jit(solution)/shard_map/sum_over_chips/ppermute | solution.py:424
  63.8 0.6 fusion.2
  (25 shorter events, 0.3 us)
Async XLA Ops:
  0.0 21.2 %copy-start.2 = (s32[2048,2]{0,1:T(2,128)S(1)}, s32[2048,2]{0,1:T(2,128)}, u32[]{:S(2)}) copy-start(s32[2048,2]{0,1:T(2,128)} %param.5) | copy-start | bytes 49156
  0.1 1.1 %copy-start = (f32[32,3,1,16,128]{4,3,2,1,0:T(8,128)S(1)}, f32[32,3,1,16,128]{4,3,2,1,0:T(8,128)}, u32[]{:S(2)}) copy-start(f32[32,3,1,16,128]{4,3,2,1,0:T(8,128)} %param.3) | copy-start | bytes 2359300
  1.2 23.6 %copy-start.1 = (f32[128,128]{1,0:T(8,128)S(1)}, f32[128,128]{1,0:T(8,128)}, u32[]{:S(2)}) copy-start(f32[128,128]{1,0:T(8,128)} %coeffs_ref.3) | copy-start | bytes 196612
  3.9 16.2 %collective-permute-start = (f32[4,6,32,128]{3,2,1,0:T(8,128)S(1)}, f32[4,6,32,128]{3,2,1,0:T(8,128)S(1)}, u32[]{:S(2)}, u32[]{:S(2)}) collective-permute-start(f32[4,6,32,128]{3,2,1,0:T(8,128)S(1)} %get-tuple-element.37), channel_id=1, source_target_pairs={{0,7},{1,2},{2,1},{3,4},{4,3},{5,6},{6,5},{7,0},{8,15},{9,10},{10,... | collective-permute-start | bytes 1179656 | tf_op jit(solution)/shard_map/to_next_plane/ppermute | solution.py:337
  8.4 8.1 %collective-permute-start.1 = (f32[13,32,128]{2,1,0:T(8,128)S(1)}, f32[13,32,128]{2,1,0:T(8,128)S(1)}, u32[]{:S(2)}, u32[]{:S(2)}) collective-permute-start(f32[13,32,128]{2,1,0:T(8,128)S(1)} %get-tuple-element.39), channel_id=1, source_target_pairs={{0,8},{8,0},{16,24},{24,16},{1,9},{9,1},{17,25},{25,17},{2,10},{10... | collective-permute-start | bytes 638984 | tf_op jit(solution)/shard_map/to_columns/ppermute | solution.py:339
  9.9 10.2 %collective-permute-start.2 = (f32[13,32,128]{2,1,0:T(8,128)S(1)}, f32[13,32,128]{2,1,0:T(8,128)S(1)}, u32[]{:S(2)}, u32[]{:S(2)}) collective-permute-start(f32[13,32,128]{2,1,0:T(8,128)S(1)} %get-tuple-element.40), channel_id=1, source_target_pairs={{0,16},{8,24},{16,0},{24,8},{1,17},{9,25},{17,1},{25,9},{2,18},{10... | collective-permute-start | bytes 638984 | tf_op jit(solution)/shard_map/to_columns/ppermute | solution.py:339
  11.5 8.7 %collective-permute-start.3 = (f32[13,32,128]{2,1,0:T(8,128)S(1)}, f32[13,32,128]{2,1,0:T(8,128)S(1)}, u32[]{:S(2)}, u32[]{:S(2)}) collective-permute-start(f32[13,32,128]{2,1,0:T(8,128)S(1)} %get-tuple-element.42), channel_id=1, source_target_pairs={{0,24},{8,16},{16,8},{24,0},{1,25},{9,17},{17,9},{25,1},{2,26},{10... | collective-permute-start | bytes 638984 | tf_op jit(solution)/shard_map/to_columns/ppermute | solution.py:339
  20.2 2.2 %collective-permute-start.10 = (f32[13,32,128]{2,1,0:T(8,128)S(1)}, f32[13,32,128]{2,1,0:T(8,128)S(1)}, u32[]{:S(2)}, u32[]{:S(2)}) collective-permute-start(f32[13,32,128]{2,1,0:T(8,128)S(1)} %collective-permute-done.3.refs_3_), channel_id=1, source_target_pairs={{0,1},{1,0},{2,3},{3,2},{4,5},{5,4},{6,7},{7,6},{8,9},{9,8},{10,11... | collective-permute-start | bytes 638984 | tf_op jit(solution)/shard_map/to_other_core/ppermute | solution.py:346
  20.2 3.1 %collective-permute-start.7 = (f32[13,32,128]{2,1,0:T(8,128)S(1)}, f32[13,32,128]{2,1,0:T(8,128)S(1)}, u32[]{:S(2)}, u32[]{:S(2)}) collective-permute-start(f32[13,32,128]{2,1,0:T(8,128)S(1)} %get-tuple-element.47.refs_0_), channel_id=1, source_target_pairs={{0,1},{1,0},{2,3},{3,2},{4,5},{5,4},{6,7},{7,6},{8,9},{9,8},{10,11... | collective-permute-start | bytes 638984 | tf_op jit(solution)/shard_map/to_other_core/ppermute | solution.py:346
  20.7 4.1 %collective-permute-start.8 = (f32[13,32,128]{2,1,0:T(8,128)S(1)}, f32[13,32,128]{2,1,0:T(8,128)S(1)}, u32[]{:S(2)}, u32[]{:S(2)}) collective-permute-start(f32[13,32,128]{2,1,0:T(8,128)S(1)} %collective-permute-done.1.refs_1_), channel_id=1, source_target_pairs={{0,1},{1,0},{2,3},{3,2},{4,5},{5,4},{6,7},{7,6},{8,9},{9,8},{10,11... | collective-permute-start | bytes 638984 | tf_op jit(solution)/shard_map/to_other_core/ppermute | solution.py:346
  20.8 4.0 %collective-permute-start.9 = (f32[13,32,128]{2,1,0:T(8,128)S(1)}, f32[13,32,128]{2,1,0:T(8,128)S(1)}, u32[]{:S(2)}, u32[]{:S(2)}) collective-permute-start(f32[13,32,128]{2,1,0:T(8,128)S(1)} %collective-permute-done.2.refs_2_), channel_id=1, source_target_pairs={{0,1},{1,0},{2,3},{3,2},{4,5},{5,4},{6,7},{7,6},{8,9},{9,8},{10,11... | collective-permute-start | bytes 638984 | tf_op jit(solution)/shard_map/to_other_core/ppermute | solution.py:346
  21.3 12.8 %collective-permute-start.4 = (f32[6,32,128]{2,1,0:T(8,128)S(1)}, f32[6,32,128]{2,1,0:T(8,128)S(1)}, u32[]{:S(2)}, u32[]{:S(2)}) collective-permute-start(f32[6,32,128]{2,1,0:T(8,128)S(1)} %get-tuple-element.44), channel_id=1, source_target_pairs={{0,8},{8,0},{16,24},{24,16},{1,9},{9,1},{17,25},{25,17},{2,10},{10... | collective-permute-start | bytes 294920 | tf_op jit(solution)/shard_map/next_to_columns/ppermute | solution.py:344
  22.4 11.7 %collective-permute-start.5 = (f32[6,32,128]{2,1,0:T(8,128)S(1)}, f32[6,32,128]{2,1,0:T(8,128)S(1)}, u32[]{:S(2)}, u32[]{:S(2)}) collective-permute-start(f32[6,32,128]{2,1,0:T(8,128)S(1)} %get-tuple-element.45), channel_id=1, source_target_pairs={{0,16},{8,24},{16,0},{24,8},{1,17},{9,25},{17,1},{25,9},{2,18},{10... | collective-permute-start | bytes 294920 | tf_op jit(solution)/shard_map/next_to_columns/ppermute | solution.py:344
  23.3 10.8 %collective-permute-start.6 = (f32[6,32,128]{2,1,0:T(8,128)S(1)}, f32[6,32,128]{2,1,0:T(8,128)S(1)}, u32[]{:S(2)}, u32[]{:S(2)}) collective-permute-start(f32[6,32,128]{2,1,0:T(8,128)S(1)} %get-tuple-element.46), channel_id=1, source_target_pairs={{0,24},{8,16},{16,8},{24,0},{1,25},{9,17},{17,9},{25,1},{2,26},{10... | collective-permute-start | bytes 294920 | tf_op jit(solution)/shard_map/next_to_columns/ppermute | solution.py:344
  34.1 4.3 %collective-permute-start.11 = (f32[4,6,32,128]{3,2,1,0:T(8,128)S(1)}, f32[4,6,32,128]{3,2,1,0:T(8,128)S(1)}, u32[]{:S(2)}, u32[]{:S(2)}) collective-permute-start(f32[4,6,32,128]{3,2,1,0:T(8,128)S(1)} %pad_maximum_fusion), channel_id=1, source_target_pairs={{0,1},{1,0},{2,3},{3,2},{4,5},{5,4},{6,7},{7,6},{8,9},{9,8},{10,11... | collective-permute-start | bytes 1179656 | tf_op jit(solution)/shard_map/next_to_other_core/ppermute | solution.py:368
  42.2 9.7 %collective-permute-start.12 = (f32[256,128]{1,0:T(8,128)S(1)}, f32[256,128]{1,0:T(8,128)S(1)}, u32[]{:S(2)}, u32[]{:S(2)}) collective-permute-start(f32[256,128]{1,0:T(8,128)S(1)} %edge_terms.4), channel_id=1, source_target_pairs={{0,24},{8,16},{16,8},{24,0},{1,25},{9,17},{17,9},{25,1},{2,26},{10... | collective-permute-start | bytes 393224 | tf_op jit(solution)/shard_map/sum_over_columns/ppermute | solution.py:410
  46.1 5.8 %collective-permute-start.13 = (f32[256,128]{1,0:T(8,128)S(1)}, f32[256,128]{1,0:T(8,128)S(1)}, u32[]{:S(2)}, u32[]{:S(2)}) collective-permute-start(f32[256,128]{1,0:T(8,128)S(1)} %edge_terms.5), channel_id=1, source_target_pairs={{0,16},{8,24},{16,0},{24,8},{1,17},{9,25},{17,1},{25,9},{2,18},{10... | collective-permute-start | bytes 393224 | tf_op jit(solution)/shard_map/sum_over_columns/ppermute | solution.py:410
  49.6 5.4 %collective-permute-start.14 = (f32[256,128]{1,0:T(8,128)S(1)}, f32[256,128]{1,0:T(8,128)S(1)}, u32[]{:S(2)}, u32[]{:S(2)}) collective-permute-start(f32[256,128]{1,0:T(8,128)S(1)} %edge_terms.6), channel_id=1, source_target_pairs={{0,8},{8,0},{16,24},{24,16},{1,9},{9,1},{17,25},{25,17},{2,10},{10... | collective-permute-start | bytes 393224 | tf_op jit(solution)/shard_map/sum_over_columns/ppermute | solution.py:410
  55.1 5.8 %collective-permute-start.15 = (f32[64,128]{1,0:T(8,128)S(1)}, f32[64,128]{1,0:T(8,128)S(1)}, u32[]{:S(2)}, u32[]{:S(2)}) collective-permute-start(f32[64,128]{1,0:T(8,128)S(1)} %get-tuple-element.73), channel_id=1, source_target_pairs={{0,2},{1,3},{2,4},{3,5},{4,6},{5,7},{6,0},{7,1},{8,10},{9,11},{10,... | collective-permute-start | bytes 98312 | tf_op jit(solution)/shard_map/sum_over_chips/ppermute | solution.py:424
  55.5 5.4 %collective-permute-start.17 = (f32[64,128]{1,0:T(8,128)S(1)}, f32[64,128]{1,0:T(8,128)S(1)}, u32[]{:S(2)}, u32[]{:S(2)}) collective-permute-start(f32[64,128]{1,0:T(8,128)S(1)} %get-tuple-element.74), channel_id=1, source_target_pairs={{0,6},{1,7},{2,0},{3,1},{4,2},{5,3},{6,4},{7,5},{8,14},{9,15},{10,... | collective-permute-start | bytes 98312 | tf_op jit(solution)/shard_map/sum_over_chips/ppermute | solution.py:424
  59.0 4.8 %collective-permute-start.16 = (f32[64,128]{1,0:T(8,128)S(1)}, f32[64,128]{1,0:T(8,128)S(1)}, u32[]{:S(2)}, u32[]{:S(2)}) collective-permute-start(f32[64,128]{1,0:T(8,128)S(1)} %get-tuple-element.75), channel_id=1, source_target_pairs={{0,4},{1,5},{2,6},{3,7},{4,0},{5,1},{6,2},{7,3},{8,12},{9,13},{10,... | collective-permute-start | bytes 98312 | tf_op jit(solution)/shard_map/sum_over_chips/ppermute | solution.py:424

commit v9 on v8

--- a/solution.py
+++ b/solution.py
@@ -41,22 +41,27 @@
 
 
 def pack_kernel(where_ref, field_ref, *refs, sizes):
-    *out_refs, sorted_ref = refs
+    *out_refs, sorted_ref, held_ref, sems = refs
     local_s, rows_y, tm_count = sizes
-    lanes = field_ref.shape[1]
+    lanes = field_ref.shape[3]
+    copies = [pltpu.make_async_copy(field_ref.at[:, c], held_ref.at[c], sems.at[c]) for c in range(3)]
+    for copy in copies:
+        copy.start()
+    rows_ref = held_ref.reshape(3 * local_s * rows_y, lanes)
     t, core = where_ref[0], where_ref[2]
     width, groups = lanes // tm_count, rows_y // tm_count
     lane = lax.broadcasted_iota(jnp.int32, (local_s, lanes), 1)
     borders = [[jnp.zeros((local_s, lanes), F32) for _ in range(tm_count)] for _ in range(border_slabs(rows_y, lanes))]
     for c in range(3):
         slab, first_lane = border_lane(rows_y, lanes, c)
+        copies[c].wait()
 
         def one_group(g, border, c=c, first_lane=first_lane):
             border = list(border)
             rows = []
             for q in range(tm_count):
                 y = q * groups + g
-                row = field_ref[pl.ds(c * rows_y + y, local_s, stride=3 * rows_y), :]
+                row = rows_ref[pl.ds(c * local_s * rows_y + y, local_s, stride=rows_y), :]
                 rows.append(row)
                 for side in range(2):
                     shift = first_lane + side * (rows_y - width - 1) + y
@@ -124,9 +129,7 @@
     first_chip = jnp.bitwise_xor(t, peer) * chips
 
     def one_share(ahead, _):
-        to_chip = chip + ahead
-        to_chip = jnp.where(to_chip >= chips, to_chip - chips, to_chip)
-        base = ((first_chip + to_chip) * 2 + core) * share
+        base = ((first_chip + jnp.bitwise_xor(chip, ahead)) * 2 + core) * share
 
         def one(q, _):
             code = codes_ref[base + q]
@@ -161,7 +164,7 @@
         return 0
 
     slabs = own[0].shape[0]
-    lax.fori_loop(0, slabs, one_slab, 0, unroll=2 if slabs % 2 == 0 else 1)
+    lax.fori_loop(0, slabs, one_slab, 0, unroll=True)
     width, rows_y = lanes // tm_count, block_rows * tm_count
     lane = lax.broadcasted_iota(jnp.int32, (1, lanes), 1)
     part, column = lax.div(lane, width), lax.rem(lane, width)
@@ -242,10 +245,10 @@
     lax.fori_loop(0, out_ref.shape[0], one_peer, 0)
 
 
-def far_kernel(where_ref, coeffs_ref, *refs, sizes):
-    local_s, block_rows, tm_count = sizes
-    next_own, next_other, near_ref = refs[:tm_count], refs[tm_count], refs[tm_count + 1]
-    carry_ref, slope_ref, rhs_ref = refs[tm_count + 2 :]
+def far_kernel(where_ref, codes_ref, coeffs_ref, *refs, peer, sizes):
+    local_s, block_rows, tm_count, chips, share, bits = sizes
+    next_own, next_other, near_ref, inner_ref = refs[:tm_count], *refs[tm_count : tm_count + 3]
+    carry_ref, slope_ref, rhs_ref, out_ref, conv_ref = refs[tm_count + 3 :]
     is_first = where_ref[2] == 0
     modes, lanes = near_ref.shape[1:]
     height = 2 * block_rows
@@ -267,12 +270,14 @@
                 store_projection(rhs_ref, c * height + at, value)
 
 
-def edge_kernel(
-    where_ref, codes_ref, carry_ref, slope_ref, rhs_ref, inner_ref, *refs, peer, sizes
-):
-    *arrived_refs, out_ref, conv_ref = refs
+    out_ref[...] = edge_sum(
+        where_ref, codes_ref, carry_ref, slope_ref, rhs_ref, inner_ref, conv_ref, peer, (chips, share, bits)
+    )
+
+
+def edge_sum(where_ref, codes_ref, carry_ref, slope_ref, rhs_ref, inner_ref, conv_ref, peer, sizes):
     chips, share, _ = sizes
-    modes, lanes = out_ref.shape[1], carry_ref.shape[1]
+    modes, lanes = inner_ref.shape[2], carry_ref.shape[1]
     height = carry_ref.shape[0] // modes
 
     def one_pair(slot, i, j):
@@ -282,10 +287,15 @@
         conv_ref[pl.ds(pl.multiple_of(slot * (3 * height), 8), 3 * height), :] = jnp.concatenate(rows, axis=0)
 
     for_pairs_of(where_ref, codes_ref, peer, sizes, one_pair)
-    total = inner_ref[peer % inner_ref.shape[0]]
+    return inner_ref[peer % inner_ref.shape[0]] + project(conv_ref, rhs_ref, chips * share, 3 * height, lanes)
+
+
+def edge_kernel(where_ref, codes_ref, carry_ref, slope_ref, rhs_ref, inner_ref, *refs, peer, sizes):
+    *arrived_refs, out_ref, conv_ref = refs
+    total = edge_sum(where_ref, codes_ref, carry_ref, slope_ref, rhs_ref, inner_ref, conv_ref, peer, sizes)
     for arrived_ref in arrived_refs:
         total = total + arrived_ref[...]
-    out_ref[...] = total + project(conv_ref, rhs_ref, chips * share, 3 * height, lanes)
+    out_ref[...] = total
 
 
 def vmem_limit(mebibytes):
@@ -327,11 +337,15 @@
             functools.partial(pack_kernel, sizes=(local_s, rows_y, tm_count)),
             out_shape=[pltpu.VMEM((slabs, local_s, lanes), F32)] * tm_count
             + [pltpu.VMEM((tm_count, block_rows // 2 * 3, local_s, lanes), F32)],
-            in_specs=[smem, vmem],
+            in_specs=[smem, pl.BlockSpec(memory_space=pltpu.HBM)],
             out_specs=[vmem] * (tm_count + 1),
-            scratch_shapes=[pltpu.VMEM((tm_count, slabs, local_s, lanes), F32)],
+            scratch_shapes=[
+                pltpu.VMEM((tm_count, slabs, local_s, lanes), F32),
+                pltpu.VMEM((3, local_s, rows_y, lanes), F32),
+                pltpu.SemaphoreType.DMA((3,)),
+            ],
             compiler_params=vmem_limit(16),
-        )(where, snapshots.reshape(-1, lanes))
+        )(where, pltpu.with_memory_space_constraint(snapshots.reshape(local_s, 3, rows_y, lanes), pltpu.HBM))
     with jax.named_scope("to_next_plane"):
         ring = [(place, (place + (1 if place % 2 else -1)) % space_count) for place in range(space_count)]
         across_edge = lax.ppermute(packed[tm_count], "space", ring)
@@ -376,20 +390,30 @@
             compiler_params=vmem_limit(16),
             cost_estimate=pl.CostEstimate(flops=8 * 10**9, bytes_accessed=10**7, transcendentals=0),
         )(where, codes, *[in_vmem(table) for table in inner_tables])
-    with jax.named_scope("edge_tables"):
-        tables = list(pl.pallas_call(
-            functools.partial(far_kernel, sizes=(local_s, block_rows, tm_count)),
+    with jax.named_scope("edge_terms"):
+        *tables, summed = pl.pallas_call(
+            functools.partial(
+                far_kernel, peer=tm_count - 1, sizes=(local_s, block_rows, tm_count, chips, share, bits)
+            ),
             out_shape=[
                 pltpu.VMEM((modes * height, lanes), F32),
                 pltpu.VMEM((modes * 3 * height, lanes), F32),
                 pltpu.VMEM((depth, 2 * modes), BF16),
+                pltpu.VMEM((block, modes), F32),
             ],
-            in_specs=[smem] + [vmem] * (tm_count + 3),
-            out_specs=[vmem] * 3,
+            in_specs=[smem, smem] + [vmem] * (tm_count + 4),
+            out_specs=[vmem] * 4,
+            scratch_shapes=work,
             compiler_params=vmem_limit(16),
-        )(where, coeffs, *[in_vmem(piece) for piece in (*next_own, next_other, near)]))
+        )(where, codes, coeffs, *[in_vmem(piece) for piece in (*next_own, next_other, near, early_sums)])
     arrived = []
-    for peer in reversed(range(tm_count)):
+    for peer in reversed(range(tm_count - 1)):
+        with jax.named_scope("sum_over_columns"):
+            arrived.append(lax.ppermute(summed, "tm", across(peer + 1)))
+            if peer >= early:
+                early_sums, _ = lax.optimization_barrier((early_sums, summed))
+            else:
+                late_sums, _ = lax.optimization_barrier((late_sums, summed))
         with jax.named_scope("edge_terms"):
             parts = arrived[:-1] if peer == 0 else []
             summed = pl.pallas_call(
@@ -405,23 +429,14 @@
                 codes,
                 *[in_vmem(table) for table in (*tables, early_sums if peer >= early else late_sums, *parts)],
             )
-        with jax.named_scope("sum_over_columns"):
-            if peer:
-                arrived.append(lax.ppermute(summed, "tm", across(peer)))
-                if peer > early:
-                    early_sums, _ = lax.optimization_barrier((early_sums, summed))
-                else:
-                    late_sums, _ = lax.optimization_barrier((late_sums, summed))
     with jax.named_scope("sum_over_columns"):
         summed = summed + arrived[-1]
     with jax.named_scope("sum_over_chips"):
         shares = summed.reshape(chips, share, modes)
         result = shares[0]
         for step in range(1, chips):
-            shift = [
-                (2 * chip + c, 2 * ((chip + step) % chips) + c) for chip in range(chips) for c in range(2)
-            ]
-            result = result + lax.ppermute(shares[step], "space", shift)
+            pairing = [(2 * chip + c, 2 * (chip ^ step) + c) for chip in range(chips) for c in range(2)]
+            result = result + lax.ppermute(shares[step], "space", pairing)
         return result * factor
 
 

time: 64.5 us -> 60.7 us (0.941)
  Pallas kernels: 27.1 us -> 25.1 us
  local copies, waits for them, and re-layouts: 1.18 us -> 0.04 us
    pallas_call x4 -> x3, Pallas kernels: 9.63 us -> 7.21 us  [shards(): pl.pallas_call(functools.partial(edge_kernel, peer=peer, sizes=(chips, sh...]
    pallas_call x1, Pallas kernels: 9.19 us -> 6.79 us  [shards(): pl.pallas_call(functools.partial(inner_kernel, first_peer=early, sizes=(l...]
    pallas_call x1, Pallas kernels: 1.37 us -> 3.22 us  [shards(): pl.pallas_call(functools.partial(far_kernel, peer=tm_count - 1, sizes=(lo...]
    unnamed x6 -> x4, local copies, waits for them, and re-layouts: 1.14 us -> 0.01 us
    pallas_call x1, Pallas kernels: 2.66 us -> 3.65 us  [shards(): pl.pallas_call(functools.partial(pack_kernel, sizes=(local_s, rows_y, tm_...]
  transfers between devices with their start and end apart: 18 -> 18, of which waited for: 6 -> 7; matrix products, arithmetic and copies ran while one was open for 0% -> 0% of each run, Pallas kernels for 32% -> 30%
where the time goes in v9:
time: 60.7 us; the launch traced here: 60.6 us
  Pallas kernels  25.1 us (41%)
  starting transfers between devices  20 us (33%)
  waiting for transfers between devices  14.6 us (24%)
  other arithmetic  0.76 us (1%)
    ppermute x3, waiting for transfers between devices, shards(): lax.ppermute(packed[peer], 'tm', across(peer))  8.18 us
    pallas_call x3, Pallas kernels, shards(): pl.pallas_call(functools.partial(edge_kernel, peer=peer, sizes=(chips, sh...  7.21 us
    pallas_call x1, Pallas kernels, shards(): pl.pallas_call(functools.partial(inner_kernel, first_peer=early, sizes=(l...  6.79 us
    ppermute x1, starting transfers between devices, shards(): across_edge = lax.ppermute(packed[tm_count], 'space', ring)  4.55 us
    ppermute x3, waiting for transfers between devices, shards(): result = result + lax.ppermute(shares[step], 'space', pairing)  4.48 us
    pallas_call x1, Pallas kernels, shards(): pl.pallas_call(functools.partial(pairs_kernel, first_peer=0, sizes=(heigh...  4.19 us
    ppermute x3, starting transfers between devices, shards(): arrived.append(lax.ppermute(summed, 'tm', across(peer + 1)))  3.68 us
    pallas_call x1, Pallas kernels, shards(): pl.pallas_call(functools.partial(pack_kernel, sizes=(local_s, rows_y, tm_...  3.65 us
  transfers between devices with their start and end apart: 18, of which 7 were waited for; matrix products, arithmetic and copies ran while one was open for 0% of the time, Pallas kernels for 30%

profile of v9, /device:TPU:0, one launch (start us, length us, event | category | flops | bytes accessed | tf_op | source)
XLA Modules:
  0.0 60.6 jit_solution(15418934762927711355)
XLA Ops:
  0.0 0.1 pad_add_fusion.where_ref
  0.1 3.6 %pack.1 = (f32[13,32,128]{2,1,0:T(8,128)S(1)}, f32[13,32,128]{2,1,0:T(8,128)S(1)}, f32[13,32,128]{2,1,0:T(8,128)S(1)}, f32[13,32,128]{2,1,0:T(8,128)S(1)}, f32[4,6,32,128]{3,2,1,0:T(8,128)S(1)}) custom-call(s32[3]{0:T(128)S(1)} %pad_add_fusion.where_ref, f32[32,3,16,128]{3,2,1,0:T(8,128)} %bitcast.27), custom_call_target="tpu_custom_call" | custom-call | tf_op jit(solution)/shard_map/pack/pallas_call | solution.py:336
  3.7 4.6 %collective-permute-start = (f32[4,6,32,128]{3,2,1,0:T(8,128)S(1)}, f32[4,6,32,128]{3,2,1,0:T(8,128)S(1)}, u32[]{:S(2)}, u32[]{:S(2)}) collective-permute-start(f32[4,6,32,128]{3,2,1,0:T(8,128)S(1)} %get-tuple-element.38), channel_id=1, source_target_pairs={{0,7},{1,2},{2,1},{3,4},{4,3},{5,6},{6,5},{7,0},{8,15},{9,10},{10,... | collective-permute-start | bytes 1179656 | tf_op jit(solution)/shard_map/to_next_plane/ppermute | solution.py:351
  8.3 1.5 %collective-permute-start.1 = (f32[13,32,128]{2,1,0:T(8,128)S(1)}, f32[13,32,128]{2,1,0:T(8,128)S(1)}, u32[]{:S(2)}, u32[]{:S(2)}) collective-permute-start(f32[13,32,128]{2,1,0:T(8,128)S(1)} %get-tuple-element.40), channel_id=1, source_target_pairs={{0,8},{8,0},{16,24},{24,16},{1,9},{9,1},{17,25},{25,17},{2,10},{10... | collective-permute-start | bytes 638984 | tf_op jit(solution)/shard_map/to_columns/ppermute | solution.py:353
  9.8 1.5 %collective-permute-start.2 = (f32[13,32,128]{2,1,0:T(8,128)S(1)}, f32[13,32,128]{2,1,0:T(8,128)S(1)}, u32[]{:S(2)}, u32[]{:S(2)}) collective-permute-start(f32[13,32,128]{2,1,0:T(8,128)S(1)} %get-tuple-element.41), channel_id=1, source_target_pairs={{0,16},{8,24},{16,0},{24,8},{1,17},{9,25},{17,1},{25,9},{2,18},{10... | collective-permute-start | bytes 638984 | tf_op jit(solution)/shard_map/to_columns/ppermute | solution.py:353
  11.3 0.5 collective-permute-start.3
  11.8 4.6 %collective-permute-done.1.refs_1_ = f32[13,32,128]{2,1,0:T(8,128)S(1)} collective-permute-done((f32[13,32,128]{2,1,0:T(8,128)S(1)}, f32[13,32,128]{2,1,0:T(8,128)S(1)}, u32[]{:S(2)}, u32[]{:S(2)}) %collective-permute-start.1) | collective-permute-done | bytes 213024 | tf_op jit(solution)/shard_map/to_columns/ppermute | solution.py:353
  16.3 3.6 %collective-permute-done.2.refs_2_ = f32[13,32,128]{2,1,0:T(8,128)S(1)} collective-permute-done((f32[13,32,128]{2,1,0:T(8,128)S(1)}, f32[13,32,128]{2,1,0:T(8,128)S(1)}, u32[]{:S(2)}, u32[]{:S(2)}) %collective-permute-start.2) | collective-permute-done | bytes 213024 | tf_op jit(solution)/shard_map/to_columns/ppermute | solution.py:353
  20.1 0.5 collective-permute-start.7
  20.6 0.1 collective-permute-start.8
  20.7 0.4 collective-permute-start.9
  21.1 1.1 %collective-permute-start.4 = (f32[6,32,128]{2,1,0:T(8,128)S(1)}, f32[6,32,128]{2,1,0:T(8,128)S(1)}, u32[]{:S(2)}, u32[]{:S(2)}) collective-permute-start(f32[6,32,128]{2,1,0:T(8,128)S(1)} %get-tuple-element.45), channel_id=1, source_target_pairs={{0,8},{8,0},{16,24},{24,16},{1,9},{9,1},{17,25},{25,17},{2,10},{10... | collective-permute-start | bytes 294920 | tf_op jit(solution)/shard_map/next_to_columns/ppermute | solution.py:358
  22.2 0.9 %collective-permute-start.5 = (f32[6,32,128]{2,1,0:T(8,128)S(1)}, f32[6,32,128]{2,1,0:T(8,128)S(1)}, u32[]{:S(2)}, u32[]{:S(2)}) collective-permute-start(f32[6,32,128]{2,1,0:T(8,128)S(1)} %get-tuple-element.46), channel_id=1, source_target_pairs={{0,16},{8,24},{16,0},{24,8},{1,17},{9,25},{17,1},{25,9},{2,18},{10... | collective-permute-start | bytes 294920 | tf_op jit(solution)/shard_map/next_to_columns/ppermute | solution.py:358
  23.2 1.5 %collective-permute-start.6 = (f32[6,32,128]{2,1,0:T(8,128)S(1)}, f32[6,32,128]{2,1,0:T(8,128)S(1)}, u32[]{:S(2)}, u32[]{:S(2)}) collective-permute-start(f32[6,32,128]{2,1,0:T(8,128)S(1)} %get-tuple-element.47), channel_id=1, source_target_pairs={{0,24},{8,16},{16,8},{24,0},{1,25},{9,17},{17,9},{25,1},{2,26},{10... | collective-permute-start | bytes 294920 | tf_op jit(solution)/shard_map/next_to_columns/ppermute | solution.py:358
  24.7 6.8 %inner_terms.2 = (f32[12,128,128]{2,1,0:T(8,128)S(1)}, f32[3072,128]{1,0:T(8,128)S(1)}, f32[9216,128]{1,0:T(8,128)S(1)}, bf16[3072,256]{1,0:T(8,128)(2,1)S(1)}, f32[2,256,128]{2,1,0:T(8,128)S(1)}) custom-call(s32[3]{0:T(128)S(1)} %pad_add_fusion.where_ref, s32[2048]{0:T(1024)S(1)} %bitcast.21, f32[128,128]{1,0:T(8,128)S(1)} %copy-done, ...), custom_call_target="tpu_custom_call" | custom-call | flops 12000000000 | bytes 10000000 | tf_op jit(solution)/shard_map/inner_terms/pallas_call | solution.py:365
  31.6 4.2 %inner_terms.3.inner_ref = f32[2,256,128]{2,1,0:T(8,128)S(1)} custom-call(s32[3]{0:T(128)S(1)} %pad_add_fusion.where_ref, s32[2048]{0:T(1024)S(1)} %bitcast.22, f32[3072,128]{1,0:T(8,128)S(1)} %get-tuple-element.64.carry_ref, f32[9216,128]{1,0:T(8,128)S(1)} %get-tuple-element.65.slope_ref, bf16[3072,256]{1,0:T(8,128)(2,1)S(1)} %get-tuple-element.66.rhs_ref), custom_call_target="tpu_custom_call" | custom-call | flops 8000000000 | bytes 10000000 | tf_op jit(solution)/shard_map/inner_terms/pallas_call | solution.py:384
  35.8 3.2 %edge_terms.4 = (f32[1024,128]{1,0:T(8,128)S(1)}, f32[3072,128]{1,0:T(8,128)S(1)}, bf16[3072,256]{1,0:T(8,128)(2,1)S(1)}, f32[256,128]{1,0:T(8,128)S(1)}) custom-call(s32[3]{0:T(128)S(1)} %pad_add_fusion.where_ref, s32[2048]{0:T(1024)S(1)} %bitcast.23, f32[128,128]{1,0:T(8,128)S(1)} %copy-done, f32[6,32,128]{2,1,0:T(8,128)S(1)} %get-tuple-element.55.refs_0_, ...), custom_call_target="tpu_custom_call" | custom-call | tf_op jit(solution)/shard_map/edge_terms/pallas_call | solution.py:394
  39.1 1.5 %collective-permute-start.12 = (f32[256,128]{1,0:T(8,128)S(1)}, f32[256,128]{1,0:T(8,128)S(1)}, u32[]{:S(2)}, u32[]{:S(2)}) collective-permute-start(f32[256,128]{1,0:T(8,128)S(1)} %get-tuple-element.67), channel_id=1, source_target_pairs={{0,24},{8,16},{16,8},{24,0},{1,25},{9,17},{17,9},{25,1},{2,26},{10... | collective-permute-start | bytes 393224 | tf_op jit(solution)/shard_map/sum_over_columns/ppermute | solution.py:412
  40.5 2.4 %edge_terms.5 = f32[256,128]{1,0:T(8,128)S(1)} custom-call(s32[3]{0:T(128)S(1)} %pad_add_fusion.where_ref, s32[2048]{0:T(1024)S(1)} %bitcast.24, f32[1024,128]{1,0:T(8,128)S(1)} %get-tuple-element.61.carry_ref, f32[3072,128]{1,0:T(8,128)S(1)} %get-tuple-element.62.slope_ref, bf16[3072,256]{1,0:T(8,128)(2,1)S(1)} %get-tuple-element.63.rhs_ref, ...), custom_call_target="tpu_custom_call" | custom-call | flops 100000000 | bytes 100000 | tf_op jit(solution)/shard_map/edge_terms/pallas_call | solution.py:419
  42.9 1.2 %collective-permute-start.13 = (f32[256,128]{1,0:T(8,128)S(1)}, f32[256,128]{1,0:T(8,128)S(1)}, u32[]{:S(2)}, u32[]{:S(2)}) collective-permute-start(f32[256,128]{1,0:T(8,128)S(1)} %edge_terms.5), channel_id=1, source_target_pairs={{0,16},{8,24},{16,0},{24,8},{1,17},{9,25},{17,1},{25,9},{2,18},{10... | collective-permute-start | bytes 393224 | tf_op jit(solution)/shard_map/sum_over_columns/ppermute | solution.py:412
  44.1 2.4 %edge_terms.6 = f32[256,128]{1,0:T(8,128)S(1)} custom-call(s32[3]{0:T(128)S(1)} %pad_add_fusion.where_ref, s32[2048]{0:T(1024)S(1)} %bitcast.25, f32[1024,128]{1,0:T(8,128)S(1)} %get-tuple-element.61.carry_ref, f32[3072,128]{1,0:T(8,128)S(1)} %get-tuple-element.62.slope_ref, bf16[3072,256]{1,0:T(8,128)(2,1)S(1)} %get-tuple-element.63.rhs_ref, ...), custom_call_target="tpu_custom_call" | custom-call | flops 100000000 | bytes 100000 | tf_op jit(solution)/shard_map/edge_terms/pallas_call | solution.py:419
  46.5 1.1 %collective-permute-start.14 = (f32[256,128]{1,0:T(8,128)S(1)}, f32[256,128]{1,0:T(8,128)S(1)}, u32[]{:S(2)}, u32[]{:S(2)}) collective-permute-start(f32[256,128]{1,0:T(8,128)S(1)} %edge_terms.6), channel_id=1, source_target_pairs={{0,8},{8,0},{16,24},{24,16},{1,9},{9,1},{17,25},{25,17},{2,10},{10... | collective-permute-start | bytes 393224 | tf_op jit(solution)/shard_map/sum_over_columns/ppermute | solution.py:412
  47.6 1.2 %collective-permute-done.13.refs_1_ = f32[256,128]{1,0:T(8,128)S(1)} collective-permute-done((f32[256,128]{1,0:T(8,128)S(1)}, f32[256,128]{1,0:T(8,128)S(1)}, u32[]{:S(2)}, u32[]{:S(2)}) %collective-permute-start.13) | collective-permute-done | bytes 131104 | tf_op jit(solution)/shard_map/sum_over_columns/ppermute | solution.py:412
  48.7 2.4 %edge_terms.7 = f32[256,128]{1,0:T(8,128)S(1)} custom-call(s32[3]{0:T(128)S(1)} %pad_add_fusion.where_ref, s32[2048]{0:T(1024)S(1)} %bitcast.26, f32[1024,128]{1,0:T(8,128)S(1)} %get-tuple-element.61.carry_ref, f32[3072,128]{1,0:T(8,128)S(1)} %get-tuple-element.62.slope_ref, bf16[3072,256]{1,0:T(8,128)(2,1)S(1)} %get-tuple-element.63.rhs_ref, ...), custom_call_target="tpu_custom_call" | custom-call | flops 100000000 | bytes 100000 | tf_op jit(solution)/shard_map/edge_terms/pallas_call | solution.py:419
  51.2 0.7 %collective-permute-done.14 = f32[256,128]{1,0:T(8,128)S(1)} collective-permute-done((f32[256,128]{1,0:T(8,128)S(1)}, f32[256,128]{1,0:T(8,128)S(1)}, u32[]{:S(2)}, u32[]{:S(2)}) %collective-permute-start.14) | collective-permute-done | bytes 131104 | tf_op jit(solution)/shard_map/sum_over_columns/ppermute | solution.py:412
  51.9 0.4 collective-permute-start.15
  52.4 2.5 %collective-permute-start.17 = (f32[64,128]{1,0:T(8,128)S(1)}, f32[64,128]{1,0:T(8,128)S(1)}, u32[]{:S(2)}, u32[]{:S(2)}) collective-permute-start(f32[64,128]{1,0:T(8,128)S(1)} %get-tuple-element.76), channel_id=1, source_target_pairs={{0,6},{1,7},{2,4},{3,5},{4,2},{5,3},{6,0},{7,1},{8,14},{9,15},{10,... | collective-permute-start | bytes 98312 | tf_op jit(solution)/shard_map/sum_over_chips/ppermute | solution.py:439
  54.8 0.7 %collective-permute-start.16 = (f32[64,128]{1,0:T(8,128)S(1)}, f32[64,128]{1,0:T(8,128)S(1)}, u32[]{:S(2)}, u32[]{:S(2)}) collective-permute-start(f32[64,128]{1,0:T(8,128)S(1)} %get-tuple-element.77), channel_id=1, source_target_pairs={{0,4},{1,5},{2,6},{3,7},{4,0},{5,1},{6,2},{7,3},{8,12},{9,13},{10,... | collective-permute-start | bytes 98312 | tf_op jit(solution)/shard_map/sum_over_chips/ppermute | solution.py:439
  55.5 0.8 %collective-permute-done.15 = f32[64,128]{1,0:T(8,128)S(1)} collective-permute-done((f32[64,128]{1,0:T(8,128)S(1)}, f32[64,128]{1,0:T(8,128)S(1)}, u32[]{:S(2)}, u32[]{:S(2)}) %collective-permute-start.15) | collective-permute-done | bytes 32800 | tf_op jit(solution)/shard_map/sum_over_chips/ppermute | solution.py:439
  56.3 1.9 %collective-permute-done.17 = f32[64,128]{1,0:T(8,128)S(1)} collective-permute-done((f32[64,128]{1,0:T(8,128)S(1)}, f32[64,128]{1,0:T(8,128)S(1)}, u32[]{:S(2)}, u32[]{:S(2)}) %collective-permute-start.17) | collective-permute-done | bytes 32800 | tf_op jit(solution)/shard_map/sum_over_chips/ppermute | solution.py:439
  58.2 1.8 %collective-permute-done.16 = f32[64,128]{1,0:T(8,128)S(1)} collective-permute-done((f32[64,128]{1,0:T(8,128)S(1)}, f32[64,128]{1,0:T(8,128)S(1)}, u32[]{:S(2)}, u32[]{:S(2)}) %collective-permute-start.16) | collective-permute-done | bytes 32800 | tf_op jit(solution)/shard_map/sum_over_chips/ppermute | solution.py:439
  60.0 0.6 %fusion.2 = f32[64,128]{1,0:T(8,128)} fusion(f32[64,128]{1,0:T(8,128)S(1)} %collective-permute-done.17, f32[64,128]{1,0:T(8,128)S(1)} %collective-permute-done.16, f32[64,128]{1,0:T(8,128)S(1)} %collective-permute-done.15, f32[256,128]{1,0:T(8,128)S(1)} %add.19), kind=kLoop, calls=%fused_computation.8 | loop fusion | flops 32768 | bytes 163840 | tf_op jit(solution)/shard_map/sum_over_chips/mul | solution.py:440
  (22 shorter events, 0.3 us)
Async XLA Ops:
  0.0 21.1 %copy-start.1 = (s32[2048,2]{0,1:T(2,128)S(1)}, s32[2048,2]{0,1:T(2,128)}, u32[]{:S(2)}) copy-start(s32[2048,2]{0,1:T(2,128)} %param.5) | copy-start | bytes 49156
  0.0 24.7 %copy-start = (f32[128,128]{1,0:T(8,128)S(1)}, f32[128,128]{1,0:T(8,128)}, u32[]{:S(2)}) copy-start(f32[128,128]{1,0:T(8,128)} %coeffs_ref.3) | copy-start | bytes 196612
  3.7 16.2 %collective-permute-start = (f32[4,6,32,128]{3,2,1,0:T(8,128)S(1)}, f32[4,6,32,128]{3,2,1,0:T(8,128)S(1)}, u32[]{:S(2)}, u32[]{:S(2)}) collective-permute-start(f32[4,6,32,128]{3,2,1,0:T(8,128)S(1)} %get-tuple-element.38), channel_id=1, source_target_pairs={{0,7},{1,2},{2,1},{3,4},{4,3},{5,6},{6,5},{7,0},{8,15},{9,10},{10,... | collective-permute-start | bytes 1179656 | tf_op jit(solution)/shard_map/to_next_plane/ppermute | solution.py:351
  8.3 8.1 %collective-permute-start.1 = (f32[13,32,128]{2,1,0:T(8,128)S(1)}, f32[13,32,128]{2,1,0:T(8,128)S(1)}, u32[]{:S(2)}, u32[]{:S(2)}) collective-permute-start(f32[13,32,128]{2,1,0:T(8,128)S(1)} %get-tuple-element.40), channel_id=1, source_target_pairs={{0,8},{8,0},{16,24},{24,16},{1,9},{9,1},{17,25},{25,17},{2,10},{10... | collective-permute-start | bytes 638984 | tf_op jit(solution)/shard_map/to_columns/ppermute | solution.py:353
  9.8 10.2 %collective-permute-start.2 = (f32[13,32,128]{2,1,0:T(8,128)S(1)}, f32[13,32,128]{2,1,0:T(8,128)S(1)}, u32[]{:S(2)}, u32[]{:S(2)}) collective-permute-start(f32[13,32,128]{2,1,0:T(8,128)S(1)} %get-tuple-element.41), channel_id=1, source_target_pairs={{0,16},{8,24},{16,0},{24,8},{1,17},{9,25},{17,1},{25,9},{2,18},{10... | collective-permute-start | bytes 638984 | tf_op jit(solution)/shard_map/to_columns/ppermute | solution.py:353
  11.3 8.7 %collective-permute-start.3 = (f32[13,32,128]{2,1,0:T(8,128)S(1)}, f32[13,32,128]{2,1,0:T(8,128)S(1)}, u32[]{:S(2)}, u32[]{:S(2)}) collective-permute-start(f32[13,32,128]{2,1,0:T(8,128)S(1)} %get-tuple-element.43), channel_id=1, source_target_pairs={{0,24},{8,16},{16,8},{24,0},{1,25},{9,17},{17,9},{25,1},{2,26},{10... | collective-permute-start | bytes 638984 | tf_op jit(solution)/shard_map/to_columns/ppermute | solution.py:353
  20.0 2.2 %collective-permute-start.10 = (f32[13,32,128]{2,1,0:T(8,128)S(1)}, f32[13,32,128]{2,1,0:T(8,128)S(1)}, u32[]{:S(2)}, u32[]{:S(2)}) collective-permute-start(f32[13,32,128]{2,1,0:T(8,128)S(1)} %collective-permute-done.3.refs_3_), channel_id=1, source_target_pairs={{0,1},{1,0},{2,3},{3,2},{4,5},{5,4},{6,7},{7,6},{8,9},{9,8},{10,11... | collective-permute-start | bytes 638984 | tf_op jit(solution)/shard_map/to_other_core/ppermute | solution.py:360
  20.1 3.1 %collective-permute-start.7 = (f32[13,32,128]{2,1,0:T(8,128)S(1)}, f32[13,32,128]{2,1,0:T(8,128)S(1)}, u32[]{:S(2)}, u32[]{:S(2)}) collective-permute-start(f32[13,32,128]{2,1,0:T(8,128)S(1)} %get-tuple-element.48.refs_0_), channel_id=1, source_target_pairs={{0,1},{1,0},{2,3},{3,2},{4,5},{5,4},{6,7},{7,6},{8,9},{9,8},{10,11... | collective-permute-start | bytes 638984 | tf_op jit(solution)/shard_map/to_other_core/ppermute | solution.py:360
  20.6 4.1 %collective-permute-start.8 = (f32[13,32,128]{2,1,0:T(8,128)S(1)}, f32[13,32,128]{2,1,0:T(8,128)S(1)}, u32[]{:S(2)}, u32[]{:S(2)}) collective-permute-start(f32[13,32,128]{2,1,0:T(8,128)S(1)} %collective-permute-done.1.refs_1_), channel_id=1, source_target_pairs={{0,1},{1,0},{2,3},{3,2},{4,5},{5,4},{6,7},{7,6},{8,9},{9,8},{10,11... | collective-permute-start | bytes 638984 | tf_op jit(solution)/shard_map/to_other_core/ppermute | solution.py:360
  20.7 4.0 %collective-permute-start.9 = (f32[13,32,128]{2,1,0:T(8,128)S(1)}, f32[13,32,128]{2,1,0:T(8,128)S(1)}, u32[]{:S(2)}, u32[]{:S(2)}) collective-permute-start(f32[13,32,128]{2,1,0:T(8,128)S(1)} %collective-permute-done.2.refs_2_), channel_id=1, source_target_pairs={{0,1},{1,0},{2,3},{3,2},{4,5},{5,4},{6,7},{7,6},{8,9},{9,8},{10,11... | collective-permute-start | bytes 638984 | tf_op jit(solution)/shard_map/to_other_core/ppermute | solution.py:360
  21.1 10.4 %collective-permute-start.4 = (f32[6,32,128]{2,1,0:T(8,128)S(1)}, f32[6,32,128]{2,1,0:T(8,128)S(1)}, u32[]{:S(2)}, u32[]{:S(2)}) collective-permute-start(f32[6,32,128]{2,1,0:T(8,128)S(1)} %get-tuple-element.45), channel_id=1, source_target_pairs={{0,8},{8,0},{16,24},{24,16},{1,9},{9,1},{17,25},{25,17},{2,10},{10... | collective-permute-start | bytes 294920 | tf_op jit(solution)/shard_map/next_to_columns/ppermute | solution.py:358
  22.2 9.3 %collective-permute-start.5 = (f32[6,32,128]{2,1,0:T(8,128)S(1)}, f32[6,32,128]{2,1,0:T(8,128)S(1)}, u32[]{:S(2)}, u32[]{:S(2)}) collective-permute-start(f32[6,32,128]{2,1,0:T(8,128)S(1)} %get-tuple-element.46), channel_id=1, source_target_pairs={{0,16},{8,24},{16,0},{24,8},{1,17},{9,25},{17,1},{25,9},{2,18},{10... | collective-permute-start | bytes 294920 | tf_op jit(solution)/shard_map/next_to_columns/ppermute | solution.py:358
  23.2 8.4 %collective-permute-start.6 = (f32[6,32,128]{2,1,0:T(8,128)S(1)}, f32[6,32,128]{2,1,0:T(8,128)S(1)}, u32[]{:S(2)}, u32[]{:S(2)}) collective-permute-start(f32[6,32,128]{2,1,0:T(8,128)S(1)} %get-tuple-element.47), channel_id=1, source_target_pairs={{0,24},{8,16},{16,8},{24,0},{1,25},{9,17},{17,9},{25,1},{2,26},{10... | collective-permute-start | bytes 294920 | tf_op jit(solution)/shard_map/next_to_columns/ppermute | solution.py:358
  31.6 4.3 %collective-permute-start.11 = (f32[4,6,32,128]{3,2,1,0:T(8,128)S(1)}, f32[4,6,32,128]{3,2,1,0:T(8,128)S(1)}, u32[]{:S(2)}, u32[]{:S(2)}) collective-permute-start(f32[4,6,32,128]{3,2,1,0:T(8,128)S(1)} %pad_maximum_fusion), channel_id=1, source_target_pairs={{0,1},{1,0},{2,3},{3,2},{4,5},{5,4},{6,7},{7,6},{8,9},{9,8},{10,11... | collective-permute-start | bytes 1179656 | tf_op jit(solution)/shard_map/next_to_other_core/ppermute | solution.py:382
  39.1 9.7 %collective-permute-start.12 = (f32[256,128]{1,0:T(8,128)S(1)}, f32[256,128]{1,0:T(8,128)S(1)}, u32[]{:S(2)}, u32[]{:S(2)}) collective-permute-start(f32[256,128]{1,0:T(8,128)S(1)} %get-tuple-element.67), channel_id=1, source_target_pairs={{0,24},{8,16},{16,8},{24,0},{1,25},{9,17},{17,9},{25,1},{2,26},{10... | collective-permute-start | bytes 393224 | tf_op jit(solution)/shard_map/sum_over_columns/ppermute | solution.py:412
  42.9 5.8 %collective-permute-start.13 = (f32[256,128]{1,0:T(8,128)S(1)}, f32[256,128]{1,0:T(8,128)S(1)}, u32[]{:S(2)}, u32[]{:S(2)}) collective-permute-start(f32[256,128]{1,0:T(8,128)S(1)} %edge_terms.5), channel_id=1, source_target_pairs={{0,16},{8,24},{16,0},{24,8},{1,17},{9,25},{17,1},{25,9},{2,18},{10... | collective-permute-start | bytes 393224 | tf_op jit(solution)/shard_map/sum_over_columns/ppermute | solution.py:412
  46.5 5.4 %collective-permute-start.14 = (f32[256,128]{1,0:T(8,128)S(1)}, f32[256,128]{1,0:T(8,128)S(1)}, u32[]{:S(2)}, u32[]{:S(2)}) collective-permute-start(f32[256,128]{1,0:T(8,128)S(1)} %edge_terms.6), channel_id=1, source_target_pairs={{0,8},{8,0},{16,24},{24,16},{1,9},{9,1},{17,25},{25,17},{2,10},{10... | collective-permute-start | bytes 393224 | tf_op jit(solution)/shard_map/sum_over_columns/ppermute | solution.py:412
  51.9 4.3 %collective-permute-start.15 = (f32[64,128]{1,0:T(8,128)S(1)}, f32[64,128]{1,0:T(8,128)S(1)}, u32[]{:S(2)}, u32[]{:S(2)}) collective-permute-start(f32[64,128]{1,0:T(8,128)S(1)} %get-tuple-element.75), channel_id=1, source_target_pairs={{0,2},{1,3},{2,0},{3,1},{4,6},{5,7},{6,4},{7,5},{8,10},{9,11},{10,... | collective-permute-start | bytes 98312 | tf_op jit(solution)/shard_map/sum_over_chips/ppermute | solution.py:439
  52.4 5.8 %collective-permute-start.17 = (f32[64,128]{1,0:T(8,128)S(1)}, f32[64,128]{1,0:T(8,128)S(1)}, u32[]{:S(2)}, u32[]{:S(2)}) collective-permute-start(f32[64,128]{1,0:T(8,128)S(1)} %get-tuple-element.76), channel_id=1, source_target_pairs={{0,6},{1,7},{2,4},{3,5},{4,2},{5,3},{6,0},{7,1},{8,14},{9,15},{10,... | collective-permute-start | bytes 98312 | tf_op jit(solution)/shard_map/sum_over_chips/ppermute | solution.py:439
  54.8 5.2 %collective-permute-start.16 = (f32[64,128]{1,0:T(8,128)S(1)}, f32[64,128]{1,0:T(8,128)S(1)}, u32[]{:S(2)}, u32[]{:S(2)}) collective-permute-start(f32[64,128]{1,0:T(8,128)S(1)} %get-tuple-element.77), channel_id=1, source_target_pairs={{0,4},{1,5},{2,6},{3,7},{4,0},{5,1},{6,2},{7,3},{8,12},{9,13},{10,... | collective-permute-start | bytes 98312 | tf_op jit(solution)/shard_map/sum_over_chips/ppermute | solution.py:439

commit v10 on v9

--- a/solution.py
+++ b/solution.py
@@ -123,25 +123,25 @@
     return (both[:block, :modes] + both[:block, modes:]) + (both[block:, :modes] + both[block:, modes:])
 
 
-def for_pairs_of(where_ref, codes_ref, peer, sizes, one_pair):
-    chips, share, bits = sizes
+def for_pairs_of(where_ref, codes_ref, group, sizes, one_pair):
+    tm_count, chips, share, bits = sizes
     t, chip, core = where_ref[0], where_ref[1], where_ref[2]
-    first_chip = jnp.bitwise_xor(t, peer) * chips
-
-    def one_share(ahead, _):
-        base = ((first_chip + jnp.bitwise_xor(chip, ahead)) * 2 + core) * share
+    to_chip = jnp.bitwise_xor(chip, group)
+
+    def one_share(peer, _):
+        base = ((jnp.bitwise_xor(t, peer) * chips + to_chip) * 2 + core) * share
 
         def one(q, _):
             code = codes_ref[base + q]
-            one_pair(ahead * share + q, lax.shift_right_logical(code, bits), jnp.bitwise_and(code, 2**bits - 1))
+            one_pair(peer * share + q, lax.shift_right_logical(code, bits), jnp.bitwise_and(code, 2**bits - 1))
             return 0
 
         return lax.fori_loop(0, share, one, 0, unroll=32)
 
-    lax.fori_loop(0, chips, one_share, 0)
-
-
-def inner_kernel(where_ref, codes_ref, coeffs_ref, *refs, first_peer, sizes):
+    lax.fori_loop(0, tm_count, one_share, 0)
+
+
+def inner_kernel(where_ref, codes_ref, coeffs_ref, *refs, first_group, sizes):
     local_s, block_rows, tm_count, chips, share, bits = sizes
     own, other = refs[:tm_count], refs[tm_count : 2 * tm_count]
     near_ref, carry_ref, slope_ref, rhs_ref = refs[2 * tm_count : 2 * tm_count + 4]
@@ -216,14 +216,15 @@
 
     pairs_kernel(
         where_ref, codes_ref, carry_ref, slope_ref, rhs_ref, out_ref, conv_ref,
-        first_peer=first_peer, sizes=(height, chips, share, bits),
+        first_group=first_group, sizes=(tm_count, chips, share, bits),
     )
 
 
 def pairs_kernel(
-    where_ref, codes_ref, carry_ref, slope_ref, rhs_ref, out_ref, conv_ref, *, first_peer, sizes
+    where_ref, codes_ref, carry_ref, slope_ref, rhs_ref, out_ref, conv_ref, *, first_group, sizes
 ):
-    height, chips, share, bits = sizes
+    modes, lanes = out_ref.shape[2], conv_ref.shape[1]
+    height = carry_ref.shape[0] // (3 * modes)
 
     def one_pair(slot, i, j):
         carry = carry_ref[pl.ds(pl.multiple_of(i * (3 * height), 8), 3 * height), :]
@@ -237,15 +238,15 @@
         ]
         conv_ref[pl.ds(pl.multiple_of(slot * (3 * height), 8), 3 * height), :] = jnp.concatenate(rows, axis=0)
 
-    def one_peer(number, _):
-        for_pairs_of(where_ref, codes_ref, first_peer + number, (chips, share, bits), one_pair)
-        out_ref[number] = project(conv_ref, rhs_ref, chips * share, 3 * height, conv_ref.shape[1])
+    def one_group(number, _):
+        for_pairs_of(where_ref, codes_ref, first_group + number, sizes, one_pair)
+        out_ref[number] = project(conv_ref, rhs_ref, out_ref.shape[1], 3 * height, lanes)
         return 0
 
-    lax.fori_loop(0, out_ref.shape[0], one_peer, 0)
-
-
-def far_kernel(where_ref, codes_ref, coeffs_ref, *refs, peer, sizes):
+    lax.fori_loop(0, out_ref.shape[0], one_group, 0)
+
+
+def far_kernel(where_ref, codes_ref, coeffs_ref, *refs, group, sizes):
     local_s, block_rows, tm_count, chips, share, bits = sizes
     next_own, next_other, near_ref, inner_ref = refs[:tm_count], *refs[tm_count : tm_count + 3]
     carry_ref, slope_ref, rhs_ref, out_ref, conv_ref = refs[tm_count + 3 :]
@@ -271,13 +272,13 @@
 
 
     out_ref[...] = edge_sum(
-        where_ref, codes_ref, carry_ref, slope_ref, rhs_ref, inner_ref, conv_ref, peer, (chips, share, bits)
+        where_ref, codes_ref, carry_ref, slope_ref, rhs_ref, inner_ref, conv_ref, group, (tm_count, chips, share, bits)
     )
 
 
-def edge_sum(where_ref, codes_ref, carry_ref, slope_ref, rhs_ref, inner_ref, conv_ref, peer, sizes):
-    chips, share, _ = sizes
-    modes, lanes = inner_ref.shape[2], carry_ref.shape[1]
+def edge_sum(where_ref, codes_ref, carry_ref, slope_ref, rhs_ref, inner_ref, conv_ref, group, sizes):
+    block, modes = inner_ref.shape[1:]
+    lanes = carry_ref.shape[1]
     height = carry_ref.shape[0] // modes
 
     def one_pair(slot, i, j):
@@ -286,13 +287,13 @@
         rows = [carry * slope[c * height : (c + 1) * height] for c in range(3)]
         conv_ref[pl.ds(pl.multiple_of(slot * (3 * height), 8), 3 * height), :] = jnp.concatenate(rows, axis=0)
 
-    for_pairs_of(where_ref, codes_ref, peer, sizes, one_pair)
-    return inner_ref[peer % inner_ref.shape[0]] + project(conv_ref, rhs_ref, chips * share, 3 * height, lanes)
-
-
-def edge_kernel(where_ref, codes_ref, carry_ref, slope_ref, rhs_ref, inner_ref, *refs, peer, sizes):
+    for_pairs_of(where_ref, codes_ref, group, sizes, one_pair)
+    return inner_ref[group % inner_ref.shape[0]] + project(conv_ref, rhs_ref, block, 3 * height, lanes)
+
+
+def edge_kernel(where_ref, codes_ref, carry_ref, slope_ref, rhs_ref, inner_ref, *refs, group, sizes):
     *arrived_refs, out_ref, conv_ref = refs
-    total = edge_sum(where_ref, codes_ref, carry_ref, slope_ref, rhs_ref, inner_ref, conv_ref, peer, sizes)
+    total = edge_sum(where_ref, codes_ref, carry_ref, slope_ref, rhs_ref, inner_ref, conv_ref, group, sizes)
     for arrived_ref in arrived_refs:
         total = total + arrived_ref[...]
     out_ref[...] = total
@@ -323,7 +324,7 @@
     codes = pair_table[:, 0] * modes + pair_table[:, 1]
     smem = pl.BlockSpec(memory_space=pltpu.SMEM)
     vmem = pl.BlockSpec(memory_space=pltpu.VMEM)
-    block = chips * share
+    block = tm_count * share
     height = 2 * block_rows
     depth = 3 * height * lanes
 
@@ -358,12 +359,12 @@
         next_own = [parts[0]] + [lax.ppermute(parts[peer], "tm", across(peer)) for peer in range(1, tm_count)]
     with jax.named_scope("to_other_core"):
         other = [lax.ppermute(piece, "space", swap) for piece in own]
-    early = tm_count // 2
+    early = chips // 2
     work = [pltpu.VMEM((block * 3 * height, lanes), F32)]
     groups = pltpu.VMEM((early, block, modes), F32)
     with jax.named_scope("inner_terms"):
         near, *inner_tables, early_sums = pl.pallas_call(
-            functools.partial(inner_kernel, first_peer=early, sizes=(local_s, block_rows, tm_count, chips, share, bits)),
+            functools.partial(inner_kernel, first_group=early, sizes=(local_s, block_rows, tm_count, chips, share, bits)),
             out_shape=[
                 pltpu.VMEM((block_rows * 3, modes, lanes), F32),
                 pltpu.VMEM((modes * 3 * height, lanes), F32),
@@ -382,7 +383,7 @@
         next_other = lax.ppermute(jnp.stack(next_own), "space", swap)
     with jax.named_scope("inner_terms"):
         late_sums = pl.pallas_call(
-            functools.partial(pairs_kernel, first_peer=0, sizes=(height, chips, share, bits)),
+            functools.partial(pairs_kernel, first_group=0, sizes=(tm_count, chips, share, bits)),
             out_shape=groups,
             in_specs=[smem, smem] + [vmem] * 3,
             out_specs=vmem,
@@ -393,7 +394,7 @@
     with jax.named_scope("edge_terms"):
         *tables, summed = pl.pallas_call(
             functools.partial(
-                far_kernel, peer=tm_count - 1, sizes=(local_s, block_rows, tm_count, chips, share, bits)
+                far_kernel, group=chips - 1, sizes=(local_s, block_rows, tm_count, chips, share, bits)
             ),
             out_shape=[
                 pltpu.VMEM((modes * height, lanes), F32),
@@ -407,17 +408,18 @@
             compiler_params=vmem_limit(16),
         )(where, codes, coeffs, *[in_vmem(piece) for piece in (*next_own, next_other, near, early_sums)])
     arrived = []
-    for peer in reversed(range(tm_count - 1)):
-        with jax.named_scope("sum_over_columns"):
-            arrived.append(lax.ppermute(summed, "tm", across(peer + 1)))
-            if peer >= early:
+    for group in reversed(range(chips - 1)):
+        with jax.named_scope("sum_over_chips"):
+            pairing = [(2 * chip + c, 2 * (chip ^ (group + 1)) + c) for chip in range(chips) for c in range(2)]
+            arrived.append(lax.ppermute(summed, "space", pairing))
+            if group >= early:
                 early_sums, _ = lax.optimization_barrier((early_sums, summed))
             else:
                 late_sums, _ = lax.optimization_barrier((late_sums, summed))
         with jax.named_scope("edge_terms"):
-            parts = arrived[:-1] if peer == 0 else []
+            parts = arrived[:-1] if group == 0 else []
             summed = pl.pallas_call(
-                functools.partial(edge_kernel, peer=peer, sizes=(chips, share, bits)),
+                functools.partial(edge_kernel, group=group, sizes=(tm_count, chips, share, bits)),
                 out_shape=pltpu.VMEM((block, modes), F32),
                 in_specs=[smem, smem] + [vmem] * (4 + len(parts)),
                 out_specs=vmem,
@@ -427,16 +429,14 @@
             )(
                 where,
                 codes,
-                *[in_vmem(table) for table in (*tables, early_sums if peer >= early else late_sums, *parts)],
+                *[in_vmem(table) for table in (*tables, early_sums if group >= early else late_sums, *parts)],
             )
+    with jax.named_scope("sum_over_chips"):
+        shares = (summed + arrived[-1]).reshape(tm_count, share, modes)
     with jax.named_scope("sum_over_columns"):
-        summed = summed + arrived[-1]
-    with jax.named_scope("sum_over_chips"):
-        shares = summed.reshape(chips, share, modes)
         result = shares[0]
-        for step in range(1, chips):
-            pairing = [(2 * chip + c, 2 * (chip ^ step) + c) for chip in range(chips) for c in range(2)]
-            result = result + lax.ppermute(shares[step], "space", pairing)
+        for peer in range(1, tm_count):
+            result = result + lax.ppermute(shares[peer], "tm", across(peer))
         return result * factor
 
 

time: 60.7 us -> 64.1 us (1.056)
  waiting for transfers between devices: 14.6 us -> 17 us
  starting transfers between devices: 20 us -> 20.9 us
    ppermute x6, waiting for transfers between devices: 6.4 us -> 8.79 us  [the longest x3 5.39 us: shards(): arrived.append(lax.ppermute(summed, 'space', pairing))]
    ppermute x6, starting transfers between devices: 7.24 us -> 8.14 us  [the longest x3 4.58 us: shards(): arrived.append(lax.ppermute(summed, 'space', pairing))]
  transfers between devices with their start and end apart: 18 -> 18, of which waited for: 7 -> 6; matrix products, arithmetic and copies ran while one was open for 0% -> 0% of each run, Pallas kernels for 30% -> 29%
where the time goes in v10:
time: 64.1 us; the launch traced here: 63.9 us
  Pallas kernels  25.1 us (39%)
  starting transfers between devices  20.9 us (33%)
  waiting for transfers between devices  17 us (27%)
  other arithmetic  0.76 us (1%)
    ppermute x3, waiting for transfers between devices, shards(): lax.ppermute(packed[peer], 'tm', across(peer))  8.18 us
    pallas_call x3, Pallas kernels, shards(): pl.pallas_call(functools.partial(edge_kernel, group=group, sizes=(tm_coun...  7.22 us
    pallas_call x1, Pallas kernels, shards(): pl.pallas_call(functools.partial(inner_kernel, first_group=early, sizes=(...  6.8 us
    ppermute x3, waiting for transfers between devices, shards(): arrived.append(lax.ppermute(summed, 'space', pairing))  5.39 us
    ppermute x3, starting transfers between devices, shards(): arrived.append(lax.ppermute(summed, 'space', pairing))  4.58 us
    ppermute x1, starting transfers between devices, shards(): across_edge = lax.ppermute(packed[tm_count], 'space', ring)  4.55 us
    pallas_call x1, Pallas kernels, shards(): pl.pallas_call(functools.partial(pairs_kernel, first_group=0, sizes=(tm_c...  4.2 us
    pallas_call x1, Pallas kernels, shards(): pl.pallas_call(functools.partial(pack_kernel, sizes=(local_s, rows_y, tm_...  3.65 us
  transfers between devices with their start and end apart: 18, of which 6 were waited for; matrix products, arithmetic and copies ran while one was open for 0% of the time, Pallas kernels for 29%

profile of v10, /device:TPU:0, one launch (start us, length us, event | category | flops | bytes accessed | tf_op | source)
XLA Modules:
  0.0 63.9 jit_solution(12215221477346573301)
XLA Ops:
  0.0 0.1 pad_add_fusion.where_ref
  0.1 3.6 %pack.1 = (f32[13,32,128]{2,1,0:T(8,128)S(1)}, f32[13,32,128]{2,1,0:T(8,128)S(1)}, f32[13,32,128]{2,1,0:T(8,128)S(1)}, f32[13,32,128]{2,1,0:T(8,128)S(1)}, f32[4,6,32,128]{3,2,1,0:T(8,128)S(1)}) custom-call(s32[3]{0:T(128)S(1)} %pad_add_fusion.where_ref, f32[32,3,16,128]{3,2,1,0:T(8,128)} %bitcast.27), custom_call_target="tpu_custom_call" | custom-call | tf_op jit(solution)/shard_map/pack/pallas_call | solution.py:337
  3.7 4.6 %collective-permute-start = (f32[4,6,32,128]{3,2,1,0:T(8,128)S(1)}, f32[4,6,32,128]{3,2,1,0:T(8,128)S(1)}, u32[]{:S(2)}, u32[]{:S(2)}) collective-permute-start(f32[4,6,32,128]{3,2,1,0:T(8,128)S(1)} %get-tuple-element.38), channel_id=1, source_target_pairs={{0,7},{1,2},{2,1},{3,4},{4,3},{5,6},{6,5},{7,0},{8,15},{9,10},{10,... | collective-permute-start | bytes 1179656 | tf_op jit(solution)/shard_map/to_next_plane/ppermute | solution.py:352
  8.3 1.5 %collective-permute-start.1 = (f32[13,32,128]{2,1,0:T(8,128)S(1)}, f32[13,32,128]{2,1,0:T(8,128)S(1)}, u32[]{:S(2)}, u32[]{:S(2)}) collective-permute-start(f32[13,32,128]{2,1,0:T(8,128)S(1)} %get-tuple-element.40), channel_id=1, source_target_pairs={{0,8},{8,0},{16,24},{24,16},{1,9},{9,1},{17,25},{25,17},{2,10},{10... | collective-permute-start | bytes 638984 | tf_op jit(solution)/shard_map/to_columns/ppermute | solution.py:354
  9.8 1.5 %collective-permute-start.2 = (f32[13,32,128]{2,1,0:T(8,128)S(1)}, f32[13,32,128]{2,1,0:T(8,128)S(1)}, u32[]{:S(2)}, u32[]{:S(2)}) collective-permute-start(f32[13,32,128]{2,1,0:T(8,128)S(1)} %get-tuple-element.41), channel_id=1, source_target_pairs={{0,16},{8,24},{16,0},{24,8},{1,17},{9,25},{17,1},{25,9},{2,18},{10... | collective-permute-start | bytes 638984 | tf_op jit(solution)/shard_map/to_columns/ppermute | solution.py:354
  11.3 0.5 collective-permute-start.3
  11.8 4.6 %collective-permute-done.1.refs_1_ = f32[13,32,128]{2,1,0:T(8,128)S(1)} collective-permute-done((f32[13,32,128]{2,1,0:T(8,128)S(1)}, f32[13,32,128]{2,1,0:T(8,128)S(1)}, u32[]{:S(2)}, u32[]{:S(2)}) %collective-permute-start.1) | collective-permute-done | bytes 213024 | tf_op jit(solution)/shard_map/to_columns/ppermute | solution.py:354
  16.3 3.6 %collective-permute-done.2.refs_2_ = f32[13,32,128]{2,1,0:T(8,128)S(1)} collective-permute-done((f32[13,32,128]{2,1,0:T(8,128)S(1)}, f32[13,32,128]{2,1,0:T(8,128)S(1)}, u32[]{:S(2)}, u32[]{:S(2)}) %collective-permute-start.2) | collective-permute-done | bytes 213024 | tf_op jit(solution)/shard_map/to_columns/ppermute | solution.py:354
  20.0 0.1 collective-permute-start.10
  20.1 0.5 collective-permute-start.7
  20.6 0.1 collective-permute-start.8
  20.7 0.4 collective-permute-start.9
  21.1 1.1 %collective-permute-start.4 = (f32[6,32,128]{2,1,0:T(8,128)S(1)}, f32[6,32,128]{2,1,0:T(8,128)S(1)}, u32[]{:S(2)}, u32[]{:S(2)}) collective-permute-start(f32[6,32,128]{2,1,0:T(8,128)S(1)} %get-tuple-element.45), channel_id=1, source_target_pairs={{0,8},{8,0},{16,24},{24,16},{1,9},{9,1},{17,25},{25,17},{2,10},{10... | collective-permute-start | bytes 294920 | tf_op jit(solution)/shard_map/next_to_columns/ppermute | solution.py:359
  22.2 0.9 %collective-permute-start.5 = (f32[6,32,128]{2,1,0:T(8,128)S(1)}, f32[6,32,128]{2,1,0:T(8,128)S(1)}, u32[]{:S(2)}, u32[]{:S(2)}) collective-permute-start(f32[6,32,128]{2,1,0:T(8,128)S(1)} %get-tuple-element.46), channel_id=1, source_target_pairs={{0,16},{8,24},{16,0},{24,8},{1,17},{9,25},{17,1},{25,9},{2,18},{10... | collective-permute-start | bytes 294920 | tf_op jit(solution)/shard_map/next_to_columns/ppermute | solution.py:359
  23.2 1.5 %collective-permute-start.6 = (f32[6,32,128]{2,1,0:T(8,128)S(1)}, f32[6,32,128]{2,1,0:T(8,128)S(1)}, u32[]{:S(2)}, u32[]{:S(2)}) collective-permute-start(f32[6,32,128]{2,1,0:T(8,128)S(1)} %get-tuple-element.47), channel_id=1, source_target_pairs={{0,24},{8,16},{16,8},{24,0},{1,25},{9,17},{17,9},{25,1},{2,26},{10... | collective-permute-start | bytes 294920 | tf_op jit(solution)/shard_map/next_to_columns/ppermute | solution.py:359
  24.7 6.8 %inner_terms.2 = (f32[12,128,128]{2,1,0:T(8,128)S(1)}, f32[3072,128]{1,0:T(8,128)S(1)}, f32[9216,128]{1,0:T(8,128)S(1)}, bf16[3072,256]{1,0:T(8,128)(2,1)S(1)}, f32[2,256,128]{2,1,0:T(8,128)S(1)}) custom-call(s32[3]{0:T(128)S(1)} %pad_add_fusion.where_ref, s32[2048]{0:T(1024)S(1)} %bitcast.21, f32[128,128]{1,0:T(8,128)S(1)} %copy-done, ...), custom_call_target="tpu_custom_call" | custom-call | flops 12000000000 | bytes 10000000 | tf_op jit(solution)/shard_map/inner_terms/pallas_call | solution.py:366
  31.6 4.2 %inner_terms.3.inner_ref = f32[2,256,128]{2,1,0:T(8,128)S(1)} custom-call(s32[3]{0:T(128)S(1)} %pad_add_fusion.where_ref, s32[2048]{0:T(1024)S(1)} %bitcast.22, f32[3072,128]{1,0:T(8,128)S(1)} %get-tuple-element.64.carry_ref, f32[9216,128]{1,0:T(8,128)S(1)} %get-tuple-element.65.slope_ref, bf16[3072,256]{1,0:T(8,128)(2,1)S(1)} %get-tuple-element.66.rhs_ref), custom_call_target="tpu_custom_call" | custom-call | flops 8000000000 | bytes 10000000 | tf_op jit(solution)/shard_map/inner_terms/pallas_call | solution.py:385
  35.9 3.2 %edge_terms.4 = (f32[1024,128]{1,0:T(8,128)S(1)}, f32[3072,128]{1,0:T(8,128)S(1)}, bf16[3072,256]{1,0:T(8,128)(2,1)S(1)}, f32[256,128]{1,0:T(8,128)S(1)}) custom-call(s32[3]{0:T(128)S(1)} %pad_add_fusion.where_ref, s32[2048]{0:T(1024)S(1)} %bitcast.23, f32[128,128]{1,0:T(8,128)S(1)} %copy-done, f32[6,32,128]{2,1,0:T(8,128)S(1)} %get-tuple-element.55.refs_0_, ...), custom_call_target="tpu_custom_call" | custom-call | tf_op jit(solution)/shard_map/edge_terms/pallas_call | solution.py:395
  39.1 2.2 %collective-permute-start.12 = (f32[256,128]{1,0:T(8,128)S(1)}, f32[256,128]{1,0:T(8,128)S(1)}, u32[]{:S(2)}, u32[]{:S(2)}) collective-permute-start(f32[256,128]{1,0:T(8,128)S(1)} %get-tuple-element.67), channel_id=1, source_target_pairs={{0,6},{1,7},{2,4},{3,5},{4,2},{5,3},{6,0},{7,1},{8,14},{9,15},{10,... | collective-permute-start | bytes 393224 | tf_op jit(solution)/shard_map/sum_over_chips/ppermute | solution.py:414
  41.3 2.4 %edge_terms.5 = f32[256,128]{1,0:T(8,128)S(1)} custom-call(s32[3]{0:T(128)S(1)} %pad_add_fusion.where_ref, s32[2048]{0:T(1024)S(1)} %bitcast.24, f32[1024,128]{1,0:T(8,128)S(1)} %get-tuple-element.61.carry_ref, f32[3072,128]{1,0:T(8,128)S(1)} %get-tuple-element.62.slope_ref, bf16[3072,256]{1,0:T(8,128)(2,1)S(1)} %get-tuple-element.63.rhs_ref, ...), custom_call_target="tpu_custom_call" | custom-call | flops 100000000 | bytes 100000 | tf_op jit(solution)/shard_map/edge_terms/pallas_call | solution.py:421
  43.7 0.2 collective-permute-start.13
  43.9 2.4 %edge_terms.6 = f32[256,128]{1,0:T(8,128)S(1)} custom-call(s32[3]{0:T(128)S(1)} %pad_add_fusion.where_ref, s32[2048]{0:T(1024)S(1)} %bitcast.25, f32[1024,128]{1,0:T(8,128)S(1)} %get-tuple-element.61.carry_ref, f32[3072,128]{1,0:T(8,128)S(1)} %get-tuple-element.62.slope_ref, bf16[3072,256]{1,0:T(8,128)(2,1)S(1)} %get-tuple-element.63.rhs_ref, ...), custom_call_target="tpu_custom_call" | custom-call | flops 100000000 | bytes 100000 | tf_op jit(solution)/shard_map/edge_terms/pallas_call | solution.py:421
  46.3 2.1 %collective-permute-start.14 = (f32[256,128]{1,0:T(8,128)S(1)}, f32[256,128]{1,0:T(8,128)S(1)}, u32[]{:S(2)}, u32[]{:S(2)}) collective-permute-start(f32[256,128]{1,0:T(8,128)S(1)} %edge_terms.6), channel_id=1, source_target_pairs={{0,2},{1,3},{2,0},{3,1},{4,6},{5,7},{6,4},{7,5},{8,10},{9,11},{10,... | collective-permute-start | bytes 393224 | tf_op jit(solution)/shard_map/sum_over_chips/ppermute | solution.py:414
  48.5 5.4 %collective-permute-done.13.refs_1_ = f32[256,128]{1,0:T(8,128)S(1)} collective-permute-done((f32[256,128]{1,0:T(8,128)S(1)}, f32[256,128]{1,0:T(8,128)S(1)}, u32[]{:S(2)}, u32[]{:S(2)}) %collective-permute-start.13) | collective-permute-done | bytes 131104 | tf_op jit(solution)/shard_map/sum_over_chips/ppermute | solution.py:414
  53.9 2.4 %edge_terms.7 = f32[256,128]{1,0:T(8,128)S(1)} custom-call(s32[3]{0:T(128)S(1)} %pad_add_fusion.where_ref, s32[2048]{0:T(1024)S(1)} %bitcast.26, f32[1024,128]{1,0:T(8,128)S(1)} %get-tuple-element.61.carry_ref, f32[3072,128]{1,0:T(8,128)S(1)} %get-tuple-element.62.slope_ref, bf16[3072,256]{1,0:T(8,128)(2,1)S(1)} %get-tuple-element.63.rhs_ref, ...), custom_call_target="tpu_custom_call" | custom-call | flops 100000000 | bytes 100000 | tf_op jit(solution)/shard_map/edge_terms/pallas_call | solution.py:421
  56.3 0.6 collective-permute-start.15
  56.9 2.5 %collective-permute-start.17 = (f32[64,128]{1,0:T(8,128)S(1)}, f32[64,128]{1,0:T(8,128)S(1)}, u32[]{:S(2)}, u32[]{:S(2)}) collective-permute-start(f32[64,128]{1,0:T(8,128)S(1)} %get-tuple-element.76), channel_id=1, source_target_pairs={{0,24},{8,16},{16,8},{24,0},{1,25},{9,17},{17,9},{25,1},{2,26},{10... | collective-permute-start | bytes 98312 | tf_op jit(solution)/shard_map/sum_over_columns/ppermute | solution.py:439
  59.4 0.5 collective-permute-start.16
  59.9 0.7 %collective-permute-done.15 = f32[64,128]{1,0:T(8,128)S(1)} collective-permute-done((f32[64,128]{1,0:T(8,128)S(1)}, f32[64,128]{1,0:T(8,128)S(1)}, u32[]{:S(2)}, u32[]{:S(2)}) %collective-permute-start.15) | collective-permute-done | bytes 32800 | tf_op jit(solution)/shard_map/sum_over_columns/ppermute | solution.py:439
  60.6 1.2 %collective-permute-done.17 = f32[64,128]{1,0:T(8,128)S(1)} collective-permute-done((f32[64,128]{1,0:T(8,128)S(1)}, f32[64,128]{1,0:T(8,128)S(1)}, u32[]{:S(2)}, u32[]{:S(2)}) %collective-permute-start.17) | collective-permute-done | bytes 32800 | tf_op jit(solution)/shard_map/sum_over_columns/ppermute | solution.py:439
  61.8 1.5 %collective-permute-done.16 = f32[64,128]{1,0:T(8,128)S(1)} collective-permute-done((f32[64,128]{1,0:T(8,128)S(1)}, f32[64,128]{1,0:T(8,128)S(1)}, u32[]{:S(2)}, u32[]{:S(2)}) %collective-permute-start.16) | collective-permute-done | bytes 32800 | tf_op jit(solution)/shard_map/sum_over_columns/ppermute | solution.py:439
  63.3 0.6 fusion.2
  (22 shorter events, 0.2 us)
Async XLA Ops:
  0.0 21.1 %copy-start.1 = (s32[2048,2]{0,1:T(2,128)S(1)}, s32[2048,2]{0,1:T(2,128)}, u32[]{:S(2)}) copy-start(s32[2048,2]{0,1:T(2,128)} %param.5) | copy-start | bytes 49156
  0.0 24.7 %copy-start = (f32[128,128]{1,0:T(8,128)S(1)}, f32[128,128]{1,0:T(8,128)}, u32[]{:S(2)}) copy-start(f32[128,128]{1,0:T(8,128)} %coeffs_ref.3) | copy-start | bytes 196612
  3.7 16.2 %collective-permute-start = (f32[4,6,32,128]{3,2,1,0:T(8,128)S(1)}, f32[4,6,32,128]{3,2,1,0:T(8,128)S(1)}, u32[]{:S(2)}, u32[]{:S(2)}) collective-permute-start(f32[4,6,32,128]{3,2,1,0:T(8,128)S(1)} %get-tuple-element.38), channel_id=1, source_target_pairs={{0,7},{1,2},{2,1},{3,4},{4,3},{5,6},{6,5},{7,0},{8,15},{9,10},{10,... | collective-permute-start | bytes 1179656 | tf_op jit(solution)/shard_map/to_next_plane/ppermute | solution.py:352
  8.3 8.1 %collective-permute-start.1 = (f32[13,32,128]{2,1,0:T(8,128)S(1)}, f32[13,32,128]{2,1,0:T(8,128)S(1)}, u32[]{:S(2)}, u32[]{:S(2)}) collective-permute-start(f32[13,32,128]{2,1,0:T(8,128)S(1)} %get-tuple-element.40), channel_id=1, source_target_pairs={{0,8},{8,0},{16,24},{24,16},{1,9},{9,1},{17,25},{25,17},{2,10},{10... | collective-permute-start | bytes 638984 | tf_op jit(solution)/shard_map/to_columns/ppermute | solution.py:354
  9.8 10.2 %collective-permute-start.2 = (f32[13,32,128]{2,1,0:T(8,128)S(1)}, f32[13,32,128]{2,1,0:T(8,128)S(1)}, u32[]{:S(2)}, u32[]{:S(2)}) collective-permute-start(f32[13,32,128]{2,1,0:T(8,128)S(1)} %get-tuple-element.41), channel_id=1, source_target_pairs={{0,16},{8,24},{16,0},{24,8},{1,17},{9,25},{17,1},{25,9},{2,18},{10... | collective-permute-start | bytes 638984 | tf_op jit(solution)/shard_map/to_columns/ppermute | solution.py:354
  11.3 8.7 %collective-permute-start.3 = (f32[13,32,128]{2,1,0:T(8,128)S(1)}, f32[13,32,128]{2,1,0:T(8,128)S(1)}, u32[]{:S(2)}, u32[]{:S(2)}) collective-permute-start(f32[13,32,128]{2,1,0:T(8,128)S(1)} %get-tuple-element.43), channel_id=1, source_target_pairs={{0,24},{8,16},{16,8},{24,0},{1,25},{9,17},{17,9},{25,1},{2,26},{10... | collective-permute-start | bytes 638984 | tf_op jit(solution)/shard_map/to_columns/ppermute | solution.py:354
  20.0 2.2 %collective-permute-start.10 = (f32[13,32,128]{2,1,0:T(8,128)S(1)}, f32[13,32,128]{2,1,0:T(8,128)S(1)}, u32[]{:S(2)}, u32[]{:S(2)}) collective-permute-start(f32[13,32,128]{2,1,0:T(8,128)S(1)} %collective-permute-done.3.refs_3_), channel_id=1, source_target_pairs={{0,1},{1,0},{2,3},{3,2},{4,5},{5,4},{6,7},{7,6},{8,9},{9,8},{10,11... | collective-permute-start | bytes 638984 | tf_op jit(solution)/shard_map/to_other_core/ppermute | solution.py:361
  20.1 3.1 %collective-permute-start.7 = (f32[13,32,128]{2,1,0:T(8,128)S(1)}, f32[13,32,128]{2,1,0:T(8,128)S(1)}, u32[]{:S(2)}, u32[]{:S(2)}) collective-permute-start(f32[13,32,128]{2,1,0:T(8,128)S(1)} %get-tuple-element.48.refs_0_), channel_id=1, source_target_pairs={{0,1},{1,0},{2,3},{3,2},{4,5},{5,4},{6,7},{7,6},{8,9},{9,8},{10,11... | collective-permute-start | bytes 638984 | tf_op jit(solution)/shard_map/to_other_core/ppermute | solution.py:361
  20.6 4.1 %collective-permute-start.8 = (f32[13,32,128]{2,1,0:T(8,128)S(1)}, f32[13,32,128]{2,1,0:T(8,128)S(1)}, u32[]{:S(2)}, u32[]{:S(2)}) collective-permute-start(f32[13,32,128]{2,1,0:T(8,128)S(1)} %collective-permute-done.1.refs_1_), channel_id=1, source_target_pairs={{0,1},{1,0},{2,3},{3,2},{4,5},{5,4},{6,7},{7,6},{8,9},{9,8},{10,11... | collective-permute-start | bytes 638984 | tf_op jit(solution)/shard_map/to_other_core/ppermute | solution.py:361
  20.7 4.0 %collective-permute-start.9 = (f32[13,32,128]{2,1,0:T(8,128)S(1)}, f32[13,32,128]{2,1,0:T(8,128)S(1)}, u32[]{:S(2)}, u32[]{:S(2)}) collective-permute-start(f32[13,32,128]{2,1,0:T(8,128)S(1)} %collective-permute-done.2.refs_2_), channel_id=1, source_target_pairs={{0,1},{1,0},{2,3},{3,2},{4,5},{5,4},{6,7},{7,6},{8,9},{9,8},{10,11... | collective-permute-start | bytes 638984 | tf_op jit(solution)/shard_map/to_other_core/ppermute | solution.py:361
  21.1 10.4 %collective-permute-start.4 = (f32[6,32,128]{2,1,0:T(8,128)S(1)}, f32[6,32,128]{2,1,0:T(8,128)S(1)}, u32[]{:S(2)}, u32[]{:S(2)}) collective-permute-start(f32[6,32,128]{2,1,0:T(8,128)S(1)} %get-tuple-element.45), channel_id=1, source_target_pairs={{0,8},{8,0},{16,24},{24,16},{1,9},{9,1},{17,25},{25,17},{2,10},{10... | collective-permute-start | bytes 294920 | tf_op jit(solution)/shard_map/next_to_columns/ppermute | solution.py:359
  22.2 9.3 %collective-permute-start.5 = (f32[6,32,128]{2,1,0:T(8,128)S(1)}, f32[6,32,128]{2,1,0:T(8,128)S(1)}, u32[]{:S(2)}, u32[]{:S(2)}) collective-permute-start(f32[6,32,128]{2,1,0:T(8,128)S(1)} %get-tuple-element.46), channel_id=1, source_target_pairs={{0,16},{8,24},{16,0},{24,8},{1,17},{9,25},{17,1},{25,9},{2,18},{10... | collective-permute-start | bytes 294920 | tf_op jit(solution)/shard_map/next_to_columns/ppermute | solution.py:359
  23.2 8.4 %collective-permute-start.6 = (f32[6,32,128]{2,1,0:T(8,128)S(1)}, f32[6,32,128]{2,1,0:T(8,128)S(1)}, u32[]{:S(2)}, u32[]{:S(2)}) collective-permute-start(f32[6,32,128]{2,1,0:T(8,128)S(1)} %get-tuple-element.47), channel_id=1, source_target_pairs={{0,24},{8,16},{16,8},{24,0},{1,25},{9,17},{17,9},{25,1},{2,26},{10... | collective-permute-start | bytes 294920 | tf_op jit(solution)/shard_map/next_to_columns/ppermute | solution.py:359
  31.6 4.3 %collective-permute-start.11 = (f32[4,6,32,128]{3,2,1,0:T(8,128)S(1)}, f32[4,6,32,128]{3,2,1,0:T(8,128)S(1)}, u32[]{:S(2)}, u32[]{:S(2)}) collective-permute-start(f32[4,6,32,128]{3,2,1,0:T(8,128)S(1)} %pad_maximum_fusion), channel_id=1, source_target_pairs={{0,1},{1,0},{2,3},{3,2},{4,5},{5,4},{6,7},{7,6},{8,9},{9,8},{10,11... | collective-permute-start | bytes 1179656 | tf_op jit(solution)/shard_map/next_to_other_core/ppermute | solution.py:383
  39.1 14.8 %collective-permute-start.12 = (f32[256,128]{1,0:T(8,128)S(1)}, f32[256,128]{1,0:T(8,128)S(1)}, u32[]{:S(2)}, u32[]{:S(2)}) collective-permute-start(f32[256,128]{1,0:T(8,128)S(1)} %get-tuple-element.67), channel_id=1, source_target_pairs={{0,6},{1,7},{2,4},{3,5},{4,2},{5,3},{6,0},{7,1},{8,14},{9,15},{10,... | collective-permute-start | bytes 393224 | tf_op jit(solution)/shard_map/sum_over_chips/ppermute | solution.py:414
  43.7 10.2 %collective-permute-start.13 = (f32[256,128]{1,0:T(8,128)S(1)}, f32[256,128]{1,0:T(8,128)S(1)}, u32[]{:S(2)}, u32[]{:S(2)}) collective-permute-start(f32[256,128]{1,0:T(8,128)S(1)} %edge_terms.5), channel_id=1, source_target_pairs={{0,4},{1,5},{2,6},{3,7},{4,0},{5,1},{6,2},{7,3},{8,12},{9,13},{10,... | collective-permute-start | bytes 393224 | tf_op jit(solution)/shard_map/sum_over_chips/ppermute | solution.py:414
  46.3 9.9 %collective-permute-start.14 = (f32[256,128]{1,0:T(8,128)S(1)}, f32[256,128]{1,0:T(8,128)S(1)}, u32[]{:S(2)}, u32[]{:S(2)}) collective-permute-start(f32[256,128]{1,0:T(8,128)S(1)} %edge_terms.6), channel_id=1, source_target_pairs={{0,2},{1,3},{2,0},{3,1},{4,6},{5,7},{6,4},{7,5},{8,10},{9,11},{10,... | collective-permute-start | bytes 393224 | tf_op jit(solution)/shard_map/sum_over_chips/ppermute | solution.py:414
  56.3 4.2 %collective-permute-start.15 = (f32[64,128]{1,0:T(8,128)S(1)}, f32[64,128]{1,0:T(8,128)S(1)}, u32[]{:S(2)}, u32[]{:S(2)}) collective-permute-start(f32[64,128]{1,0:T(8,128)S(1)} %get-tuple-element.75), channel_id=1, source_target_pairs={{0,8},{8,0},{16,24},{24,16},{1,9},{9,1},{17,25},{25,17},{2,10},{10... | collective-permute-start | bytes 98312 | tf_op jit(solution)/shard_map/sum_over_columns/ppermute | solution.py:439
  56.9 4.8 %collective-permute-start.17 = (f32[64,128]{1,0:T(8,128)S(1)}, f32[64,128]{1,0:T(8,128)S(1)}, u32[]{:S(2)}, u32[]{:S(2)}) collective-permute-start(f32[64,128]{1,0:T(8,128)S(1)} %get-tuple-element.76), channel_id=1, source_target_pairs={{0,24},{8,16},{16,8},{24,0},{1,25},{9,17},{17,9},{25,1},{2,26},{10... | collective-permute-start | bytes 98312 | tf_op jit(solution)/shard_map/sum_over_columns/ppermute | solution.py:439
  59.4 3.9 %collective-permute-start.16 = (f32[64,128]{1,0:T(8,128)S(1)}, f32[64,128]{1,0:T(8,128)S(1)}, u32[]{:S(2)}, u32[]{:S(2)}) collective-permute-start(f32[64,128]{1,0:T(8,128)S(1)} %get-tuple-element.77), channel_id=1, source_target_pairs={{0,16},{8,24},{16,0},{24,8},{1,17},{9,25},{17,1},{25,9},{2,18},{10... | collective-permute-start | bytes 98312 | tf_op jit(solution)/shard_map/sum_over_columns/ppermute | solution.py:439

commit v11 on v9

--- a/solution.py
+++ b/solution.py
@@ -9,6 +9,11 @@
 
 F32 = jnp.float32
 BF16 = jnp.bfloat16
+
+
+def place_of_device():
+    place = lax.axis_index("space")
+    return lax.axis_index("tm"), lax.shift_right_logical(place, 1), jnp.bitwise_and(place, 1)
 
 
 def split_high_low(values):
@@ -40,7 +45,7 @@
     return rows
 
 
-def pack_kernel(where_ref, field_ref, *refs, sizes):
+def pack_kernel(field_ref, *refs, sizes):
     *out_refs, sorted_ref, held_ref, sems = refs
     local_s, rows_y, tm_count = sizes
     lanes = field_ref.shape[3]
@@ -48,7 +53,7 @@
     for copy in copies:
         copy.start()
     rows_ref = held_ref.reshape(3 * local_s * rows_y, lanes)
-    t, core = where_ref[0], where_ref[2]
+    t, _, core = place_of_device()
     width, groups = lanes // tm_count, rows_y // tm_count
     lane = lax.broadcasted_iota(jnp.int32, (local_s, lanes), 1)
     borders = [[jnp.zeros((local_s, lanes), F32) for _ in range(tm_count)] for _ in range(border_slabs(rows_y, lanes))]
@@ -85,8 +90,8 @@
         out_refs[tm_count][peer] = sorted_ref[block, pl.ds(core * half, half)]
 
 
-def mode_weights(where_ref, coeffs_ref, local_s, tm_count):
-    t = where_ref[0]
+def mode_weights(coeffs_ref, local_s, tm_count):
+    t, _, _ = place_of_device()
     ordered = jnp.concatenate(
         [
             coeffs_ref[pl.ds(pl.multiple_of(jnp.bitwise_xor(t, peer) * local_s, 8), local_s), :]
@@ -123,9 +128,9 @@
     return (both[:block, :modes] + both[:block, modes:]) + (both[block:, :modes] + both[block:, modes:])
 
 
-def for_pairs_of(where_ref, codes_ref, peer, sizes, one_pair):
+def for_pairs_of(codes_ref, peer, sizes, one_pair):
     chips, share, bits = sizes
-    t, chip, core = where_ref[0], where_ref[1], where_ref[2]
+    t, chip, core = place_of_device()
     first_chip = jnp.bitwise_xor(t, peer) * chips
 
     def one_share(ahead, _):
@@ -141,15 +146,21 @@
     lax.fori_loop(0, chips, one_share, 0)
 
 
-def inner_kernel(where_ref, codes_ref, coeffs_ref, *refs, first_peer, sizes):
+def copy_of_codes(codes_ref, held_codes_ref, sem):
+    copy = pltpu.make_async_copy(codes_ref, held_codes_ref, sem)
+    copy.start()
+    return copy
+
+
+def inner_kernel(codes_ref, coeffs_ref, *refs, first_peer, sizes):
     local_s, block_rows, tm_count, chips, share, bits = sizes
     own, other = refs[:tm_count], refs[tm_count : 2 * tm_count]
-    near_ref, carry_ref, slope_ref, rhs_ref = refs[2 * tm_count : 2 * tm_count + 4]
-    out_ref, slab_ref, conv_ref = refs[2 * tm_count + 4 :]
-    core = where_ref[2]
+    near_ref, carry_ref, slope_ref, rhs_ref, out_ref, conv_ref, slab_ref, held_codes_ref, sem = refs[2 * tm_count :]
+    codes = copy_of_codes(codes_ref, held_codes_ref, sem)
+    t, _, core = place_of_device()
     modes, lanes = coeffs_ref.shape[1], own[0].shape[2]
     height = 2 * block_rows
-    weights = mode_weights(where_ref, coeffs_ref, local_s, tm_count)
+    weights = mode_weights(coeffs_ref, local_s, tm_count)
 
     def one_slab(index, _):
         own_slab = jnp.concatenate([piece[index] for piece in own], axis=0)
@@ -169,7 +180,6 @@
     lane = lax.broadcasted_iota(jnp.int32, (1, lanes), 1)
     part, column = lax.div(lane, width), lax.rem(lane, width)
     has_border = jnp.where(column == 0, -0.5, jnp.where(column == width - 1, 0.5, 0.0))
-    t = where_ref[0]
     border_of = jnp.where(column == 0, 0, rows_y) + t * width - 1 + part * block_rows
     border_lanes = lax.broadcasted_iota(jnp.int32, (2 * lanes, lanes), 0)
     border_lanes = jnp.where(border_lanes >= lanes, border_lanes - lanes, border_lanes)
@@ -214,20 +224,24 @@
                 if (plane == 1) == (row < block_rows // 2):
                     near_ref[center] = value
 
-    pairs_kernel(
-        where_ref, codes_ref, carry_ref, slope_ref, rhs_ref, out_ref, conv_ref,
-        first_peer=first_peer, sizes=(height, chips, share, bits),
-    )
-
-
-def pairs_kernel(
-    where_ref, codes_ref, carry_ref, slope_ref, rhs_ref, out_ref, conv_ref, *, first_peer, sizes
-):
-    height, chips, share, bits = sizes
+    codes.wait()
+
+    def one_peer(number, _):
+        pick_inner(held_codes_ref, carry_ref, slope_ref, conv_ref, first_peer + number, (chips, share, bits))
+        out_ref[number] = project(conv_ref, rhs_ref, chips * share, 3 * height, lanes)
+        return 0
+
+    lax.fori_loop(0, out_ref.shape[0], one_peer, 0)
+    pick_inner(held_codes_ref, carry_ref, slope_ref, conv_ref, 0, (chips, share, bits))
+
+
+def pick_inner(codes_ref, carry_ref, slope_ref, conv_ref, peer, sizes):
+    places = conv_ref.shape[0] // (sizes[0] * sizes[1])
+    height = places // 3
 
     def one_pair(slot, i, j):
-        carry = carry_ref[pl.ds(pl.multiple_of(i * (3 * height), 8), 3 * height), :]
-        slope = slope_ref[pl.ds(pl.multiple_of(j * (9 * height), 8), 9 * height), :]
+        carry = carry_ref[pl.ds(pl.multiple_of(i * places, 8), places), :]
+        slope = slope_ref[pl.ds(pl.multiple_of(j * (3 * places), 8), 3 * places), :]
         rows = [
             sum(
                 carry[d * height : (d + 1) * height] * slope[(d * 3 + c) * height : (d * 3 + c + 1) * height]
@@ -235,25 +249,40 @@
             )
             for c in range(3)
         ]
-        conv_ref[pl.ds(pl.multiple_of(slot * (3 * height), 8), 3 * height), :] = jnp.concatenate(rows, axis=0)
-
-    def one_peer(number, _):
-        for_pairs_of(where_ref, codes_ref, first_peer + number, (chips, share, bits), one_pair)
-        out_ref[number] = project(conv_ref, rhs_ref, chips * share, 3 * height, conv_ref.shape[1])
+        conv_ref[pl.ds(pl.multiple_of(slot * places, 8), places), :] = jnp.concatenate(rows, axis=0)
+
+    for_pairs_of(codes_ref, peer, sizes, one_pair)
+
+
+def rest_kernel(
+    codes_ref, carry_ref, slope_ref, rhs_ref, picked_ref, out_ref, conv_ref, held_codes_ref, sem, *, sizes
+):
+    chips, share, _ = sizes
+    codes = copy_of_codes(codes_ref, held_codes_ref, sem)
+    block, lanes = chips * share, conv_ref.shape[1]
+    places = conv_ref.shape[0] // block
+    out_ref[0] = project(picked_ref, rhs_ref, block, places, lanes)
+    codes.wait()
+
+    def one_peer(peer, _):
+        pick_inner(held_codes_ref, carry_ref, slope_ref, conv_ref, peer, sizes)
+        out_ref[peer] = project(conv_ref, rhs_ref, block, places, lanes)
         return 0
 
-    lax.fori_loop(0, out_ref.shape[0], one_peer, 0)
-
-
-def far_kernel(where_ref, codes_ref, coeffs_ref, *refs, peer, sizes):
+    lax.fori_loop(1, out_ref.shape[0], one_peer, 0)
+
+
+def far_kernel(codes_ref, coeffs_ref, *refs, peer, sizes):
     local_s, block_rows, tm_count, chips, share, bits = sizes
     next_own, next_other, near_ref, inner_ref = refs[:tm_count], *refs[tm_count : tm_count + 3]
-    carry_ref, slope_ref, rhs_ref, out_ref, conv_ref = refs[tm_count + 3 :]
-    is_first = where_ref[2] == 0
+    carry_ref, slope_ref, rhs_ref, out_ref, conv_ref, held_codes_ref, sem = refs[tm_count + 3 :]
+    codes = copy_of_codes(codes_ref, held_codes_ref, sem)
+    _, _, core = place_of_device()
+    is_first = core == 0
     modes, lanes = near_ref.shape[1:]
     height = 2 * block_rows
     half = block_rows // 2 * 3
-    weights = mode_weights(where_ref, coeffs_ref, local_s, tm_count)
+    weights = mode_weights(coeffs_ref, local_s, tm_count)
     for slab in range(half):
         mine = jnp.concatenate([next_own[peer][slab] for peer in range(tm_count)], axis=0)
         theirs = jnp.concatenate([next_other[peer, slab] for peer in range(tm_count)], axis=0)
@@ -270,29 +299,44 @@
                 store_projection(rhs_ref, c * height + at, value)
 
 
-    out_ref[...] = edge_sum(
-        where_ref, codes_ref, carry_ref, slope_ref, rhs_ref, inner_ref, conv_ref, peer, (chips, share, bits)
-    )
-
-
-def edge_sum(where_ref, codes_ref, carry_ref, slope_ref, rhs_ref, inner_ref, conv_ref, peer, sizes):
-    chips, share, _ = sizes
-    modes, lanes = inner_ref.shape[2], carry_ref.shape[1]
-    height = carry_ref.shape[0] // modes
+    codes.wait()
+    pick_edge(held_codes_ref, carry_ref, slope_ref, conv_ref, peer, (chips, share, bits))
+    out_ref[...] = edge_sum(conv_ref, rhs_ref, inner_ref, peer)
+    pick_edge(held_codes_ref, carry_ref, slope_ref, conv_ref, peer - 1, (chips, share, bits))
+
+
+def pick_edge(codes_ref, carry_ref, slope_ref, conv_ref, peer, sizes):
+    places = conv_ref.shape[0] // (sizes[0] * sizes[1])
+    height = places // 3
 
     def one_pair(slot, i, j):
         carry = carry_ref[pl.ds(pl.multiple_of(i * height, 8), height), :]
-        slope = slope_ref[pl.ds(pl.multiple_of(j * (3 * height), 8), 3 * height), :]
+        slope = slope_ref[pl.ds(pl.multiple_of(j * places, 8), places), :]
         rows = [carry * slope[c * height : (c + 1) * height] for c in range(3)]
-        conv_ref[pl.ds(pl.multiple_of(slot * (3 * height), 8), 3 * height), :] = jnp.concatenate(rows, axis=0)
-
-    for_pairs_of(where_ref, codes_ref, peer, sizes, one_pair)
-    return inner_ref[peer % inner_ref.shape[0]] + project(conv_ref, rhs_ref, chips * share, 3 * height, lanes)
-
-
-def edge_kernel(where_ref, codes_ref, carry_ref, slope_ref, rhs_ref, inner_ref, *refs, peer, sizes):
-    *arrived_refs, out_ref, conv_ref = refs
-    total = edge_sum(where_ref, codes_ref, carry_ref, slope_ref, rhs_ref, inner_ref, conv_ref, peer, sizes)
+        conv_ref[pl.ds(pl.multiple_of(slot * places, 8), places), :] = jnp.concatenate(rows, axis=0)
+
+    for_pairs_of(codes_ref, peer, sizes, one_pair)
+
+
+def edge_sum(picked_ref, rhs_ref, inner_ref, peer):
+    block = inner_ref.shape[1]
+    places = picked_ref.shape[0] // block
+    return inner_ref[peer % inner_ref.shape[0]] + project(picked_ref, rhs_ref, block, places, picked_ref.shape[1])
+
+
+def edge_kernel(
+    codes_ref, carry_ref, slope_ref, rhs_ref, inner_ref, picked_ref, out_ref, conv_ref, held_codes_ref, sem, *,
+    peer, sizes
+):
+    codes = copy_of_codes(codes_ref, held_codes_ref, sem)
+    out_ref[...] = edge_sum(picked_ref, rhs_ref, inner_ref, peer)
+    codes.wait()
+    pick_edge(held_codes_ref, carry_ref, slope_ref, conv_ref, peer - 1, sizes)
+
+
+def last_edge_kernel(rhs_ref, inner_ref, picked_ref, *refs):
+    *arrived_refs, out_ref = refs
+    total = edge_sum(picked_ref, rhs_ref, inner_ref, 0)
     for arrived_ref in arrived_refs:
         total = total + arrived_ref[...]
     out_ref[...] = total
@@ -309,9 +353,6 @@
 def shards(snapshots, coeffs, pair_table):
     tm_count, space_count = lax.axis_size("tm"), lax.axis_size("space")
     chips = space_count // 2
-    t, place = lax.axis_index("tm"), lax.axis_index("space")
-    core = lax.rem(place, 2)
-    where = jnp.stack([t, lax.div(place, 2), core]).astype(jnp.int32)
     local_s, _, _, rows_y, lanes = snapshots.shape
     modes = coeffs.shape[1]
     block_rows = rows_y // tm_count
@@ -320,8 +361,7 @@
     factor = float(space_count * rows_y * lanes) ** (-0.5)
     bits = modes.bit_length() - 1
     assert modes == 2**bits
-    codes = pair_table[:, 0] * modes + pair_table[:, 1]
-    smem = pl.BlockSpec(memory_space=pltpu.SMEM)
+    codes = in_vmem(pair_table[:, 0] * modes + pair_table[:, 1])
     vmem = pl.BlockSpec(memory_space=pltpu.VMEM)
     block = chips * share
     height = 2 * block_rows
@@ -337,7 +377,7 @@
             functools.partial(pack_kernel, sizes=(local_s, rows_y, tm_count)),
             out_shape=[pltpu.VMEM((slabs, local_s, lanes), F32)] * tm_count
             + [pltpu.VMEM((tm_count, block_rows // 2 * 3, local_s, lanes), F32)],
-            in_specs=[smem, pl.BlockSpec(memory_space=pltpu.HBM)],
+            in_specs=[pl.BlockSpec(memory_space=pltpu.HBM)],
             out_specs=[vmem] * (tm_count + 1),
             scratch_shapes=[
                 pltpu.VMEM((tm_count, slabs, local_s, lanes), F32),
@@ -345,7 +385,7 @@
                 pltpu.SemaphoreType.DMA((3,)),
             ],
             compiler_params=vmem_limit(16),
-        )(where, pltpu.with_memory_space_constraint(snapshots.reshape(local_s, 3, rows_y, lanes), pltpu.HBM))
+        )(pltpu.with_memory_space_constraint(snapshots.reshape(local_s, 3, rows_y, lanes), pltpu.HBM))
     with jax.named_scope("to_next_plane"):
         ring = [(place, (place + (1 if place % 2 else -1)) % space_count) for place in range(space_count)]
         across_edge = lax.ppermute(packed[tm_count], "space", ring)
@@ -359,10 +399,11 @@
     with jax.named_scope("to_other_core"):
         other = [lax.ppermute(piece, "space", swap) for piece in own]
     early = tm_count // 2
-    work = [pltpu.VMEM((block * 3 * height, lanes), F32)]
+    picked = pltpu.VMEM((block * 3 * height, lanes), F32)
+    held_codes = [pltpu.SMEM(codes.shape, jnp.int32), pltpu.SemaphoreType.DMA]
     groups = pltpu.VMEM((early, block, modes), F32)
     with jax.named_scope("inner_terms"):
-        near, *inner_tables, early_sums = pl.pallas_call(
+        near, *inner_tables, early_sums, first_picked = pl.pallas_call(
             functools.partial(inner_kernel, first_peer=early, sizes=(local_s, block_rows, tm_count, chips, share, bits)),
             out_shape=[
                 pltpu.VMEM((block_rows * 3, modes, lanes), F32),
@@ -370,28 +411,29 @@
                 pltpu.VMEM((modes * 9 * height, lanes), F32),
                 pltpu.VMEM((depth, 2 * modes), BF16),
                 groups,
+                picked,
             ],
-            in_specs=[smem, smem] + [vmem] * (2 * tm_count + 1),
-            out_specs=[vmem] * 5,
-            scratch_shapes=[pltpu.VMEM((2, slabs, modes, lanes), F32)] + work,
+            in_specs=[vmem] * (2 * tm_count + 2),
+            out_specs=[vmem] * 6,
+            scratch_shapes=[pltpu.VMEM((2, slabs, modes, lanes), F32)] + held_codes,
             compiler_params=vmem_limit(24),
             cost_estimate=pl.CostEstimate(flops=12 * 10**9, bytes_accessed=10**7, transcendentals=0),
-        )(where, codes, coeffs, *[in_vmem(piece) for piece in (*own, *other)])
+        )(codes, coeffs, *[in_vmem(piece) for piece in (*own, *other)])
     with jax.named_scope("next_to_other_core"):
         next_own, inner_tables = lax.optimization_barrier((next_own, inner_tables))
         next_other = lax.ppermute(jnp.stack(next_own), "space", swap)
     with jax.named_scope("inner_terms"):
         late_sums = pl.pallas_call(
-            functools.partial(pairs_kernel, first_peer=0, sizes=(height, chips, share, bits)),
+            functools.partial(rest_kernel, sizes=(chips, share, bits)),
             out_shape=groups,
-            in_specs=[smem, smem] + [vmem] * 3,
+            in_specs=[vmem] * 5,
             out_specs=vmem,
-            scratch_shapes=work,
+            scratch_shapes=[picked] + held_codes,
             compiler_params=vmem_limit(16),
             cost_estimate=pl.CostEstimate(flops=8 * 10**9, bytes_accessed=10**7, transcendentals=0),
-        )(where, codes, *[in_vmem(table) for table in inner_tables])
+        )(codes, *[in_vmem(table) for table in (*inner_tables, first_picked)])
     with jax.named_scope("edge_terms"):
-        *tables, summed = pl.pallas_call(
+        *tables, summed, next_picked = pl.pallas_call(
             functools.partial(
                 far_kernel, peer=tm_count - 1, sizes=(local_s, block_rows, tm_count, chips, share, bits)
             ),
@@ -400,12 +442,13 @@
                 pltpu.VMEM((modes * 3 * height, lanes), F32),
                 pltpu.VMEM((depth, 2 * modes), BF16),
                 pltpu.VMEM((block, modes), F32),
+                picked,
             ],
-            in_specs=[smem, smem] + [vmem] * (tm_count + 4),
-            out_specs=[vmem] * 4,
-            scratch_shapes=work,
+            in_specs=[vmem] * (tm_count + 5),
+            out_specs=[vmem] * 5,
+            scratch_shapes=held_codes,
             compiler_params=vmem_limit(16),
-        )(where, codes, coeffs, *[in_vmem(piece) for piece in (*next_own, next_other, near, early_sums)])
+        )(codes, coeffs, *[in_vmem(piece) for piece in (*next_own, next_other, near, early_sums)])
     arrived = []
     for peer in reversed(range(tm_count - 1)):
         with jax.named_scope("sum_over_columns"):
@@ -415,20 +458,26 @@
             else:
                 late_sums, _ = lax.optimization_barrier((late_sums, summed))
         with jax.named_scope("edge_terms"):
-            parts = arrived[:-1] if peer == 0 else []
-            summed = pl.pallas_call(
-                functools.partial(edge_kernel, peer=peer, sizes=(chips, share, bits)),
-                out_shape=pltpu.VMEM((block, modes), F32),
-                in_specs=[smem, smem] + [vmem] * (4 + len(parts)),
-                out_specs=vmem,
-                scratch_shapes=work,
-                compiler_params=vmem_limit(16),
-                cost_estimate=pl.CostEstimate(flops=10**8, bytes_accessed=10**5, transcendentals=0),
-            )(
-                where,
-                codes,
-                *[in_vmem(table) for table in (*tables, early_sums if peer >= early else late_sums, *parts)],
-            )
+            inner_sums = early_sums if peer >= early else late_sums
+            if peer:
+                summed, next_picked = pl.pallas_call(
+                    functools.partial(edge_kernel, peer=peer, sizes=(chips, share, bits)),
+                    out_shape=[pltpu.VMEM((block, modes), F32), picked],
+                    in_specs=[vmem] * 6,
+                    out_specs=[vmem] * 2,
+                    scratch_shapes=held_codes,
+                    compiler_params=vmem_limit(16),
+                    cost_estimate=pl.CostEstimate(flops=10**8, bytes_accessed=10**5, transcendentals=0),
+                )(codes, *[in_vmem(table) for table in (*tables, inner_sums, next_picked)])
+            else:
+                summed = pl.pallas_call(
+                    last_edge_kernel,
+                    out_shape=pltpu.VMEM((block, modes), F32),
+                    in_specs=[vmem] * (2 + len(arrived)),
+                    out_specs=vmem,
+                    compiler_params=vmem_limit(16),
+                    cost_estimate=pl.CostEstimate(flops=10**8, bytes_accessed=10**5, transcendentals=0),
+                )(*[in_vmem(table) for table in (tables[2], inner_sums, next_picked, *arrived[:-1])])
     with jax.named_scope("sum_over_columns"):
         summed = summed + arrived[-1]
     with jax.named_scope("sum_over_chips"):

time: 60.7 us -> 61.7 us (1.016)
  Pallas kernels: 25.1 us -> 22.9 us
  waiting for transfers between devices: 14.6 us -> 16 us
  local copies, waits for them, and re-layouts: 0.04 us -> 0.88 us
  other arithmetic: 0.76 us -> 1.48 us
    pallas_call x3 -> x2, Pallas kernels: 7.21 us -> 3.72 us  [shards(): pl.pallas_call(functools.partial(edge_kernel, peer=peer, sizes=(chips, sh...]
    ppermute x3, waiting for transfers between devices: 1.92 us -> 3.26 us  [shards(): arrived.append(lax.ppermute(summed, 'tm', across(peer + 1)))]
    pallas_call x1 -> x2, Pallas kernels: 4.19 us -> 5.35 us  [the longest x1 4.28 us: shards(): pl.pallas_call(functools.partial(rest_kernel, sizes=(chips, share, bits))...]
    unnamed x4, local copies, waits for them, and re-layouts: 0.01 us -> 0.84 us
    add x1, other arithmetic: 0.01 us -> 0.81 us  [shards(): codes = in_vmem(pair_table[:, 0] * modes + pair_table[:, 1])]
    pallas_call x1, Pallas kernels: 6.79 us -> 7.49 us  [shards(): pl.pallas_call(functools.partial(inner_kernel, first_peer=early, sizes=(l...]
  transfers between devices with their start and end apart: 18 -> 18, of which waited for: 7 -> 7; matrix products, arithmetic and copies ran while one was open for 0% -> 1% of each run, Pallas kernels for 30% -> 27%
where the time goes in v11:
time: 61.7 us; the launch traced here: 61.4 us
  Pallas kernels  22.9 us (37%)
  starting transfers between devices  20 us (32%)
  waiting for transfers between devices  16 us (26%)
  other arithmetic  1.48 us (2%)
  local copies, waits for them, and re-layouts  0.88 us (1%)
    ppermute x3, waiting for transfers between devices, shards(): lax.ppermute(packed[peer], 'tm', across(peer))  8.18 us
    pallas_call x1, Pallas kernels, shards(): pl.pallas_call(functools.partial(inner_kernel, first_peer=early, sizes=(l...  7.49 us
    ppermute x1, starting transfers between devices, shards(): across_edge = lax.ppermute(packed[tm_count], 'space', ring)  4.55 us
    ppermute x3, waiting for transfers between devices, shards(): result = result + lax.ppermute(shares[step], 'space', pairing)  4.49 us
    pallas_call x1, Pallas kernels, shards(): pl.pallas_call(functools.partial(rest_kernel, sizes=(chips, share, bits))...  4.28 us
    pallas_call x2, Pallas kernels, shards(): pl.pallas_call(functools.partial(edge_kernel, peer=peer, sizes=(chips, sh...  3.72 us
    ppermute x3, starting transfers between devices, shards(): arrived.append(lax.ppermute(summed, 'tm', across(peer + 1)))  3.68 us
    ppermute x3, starting transfers between devices, shards(): lax.ppermute(parts[peer], 'tm', across(peer))  3.55 us
  transfers between devices with their start and end apart: 18, of which 7 were waited for; matrix products, arithmetic and copies ran while one was open for 1% of the time, Pallas kernels for 27%

profile of v11, /device:TPU:0, one launch (start us, length us, event | category | flops | bytes accessed | tf_op | source)
XLA Modules:
  0.0 61.4 jit_solution(4839389223663555346)
XLA Ops:
  0.0 3.1 %pack.1 = (f32[13,32,128]{2,1,0:T(8,128)S(1)}, f32[13,32,128]{2,1,0:T(8,128)S(1)}, f32[13,32,128]{2,1,0:T(8,128)S(1)}, f32[13,32,128]{2,1,0:T(8,128)S(1)}, f32[4,6,32,128]{3,2,1,0:T(8,128)S(1)}) custom-call(f32[32,3,16,128]{3,2,1,0:T(8,128)} %bitcast.23), custom_call_target="tpu_custom_call" | custom-call | tf_op jit(solution)/shard_map/pack/pallas_call | solution.py:376
  3.1 4.6 %collective-permute-start = (f32[4,6,32,128]{3,2,1,0:T(8,128)S(1)}, f32[4,6,32,128]{3,2,1,0:T(8,128)S(1)}, u32[]{:S(2)}, u32[]{:S(2)}) collective-permute-start(f32[4,6,32,128]{3,2,1,0:T(8,128)S(1)} %get-tuple-element.44), channel_id=1, source_target_pairs={{0,7},{1,2},{2,1},{3,4},{4,3},{5,6},{6,5},{7,0},{8,15},{9,10},{10,... | collective-permute-start | bytes 1179656 | tf_op jit(solution)/shard_map/to_next_plane/ppermute | solution.py:391
  7.7 1.5 %collective-permute-start.1 = (f32[13,32,128]{2,1,0:T(8,128)S(1)}, f32[13,32,128]{2,1,0:T(8,128)S(1)}, u32[]{:S(2)}, u32[]{:S(2)}) collective-permute-start(f32[13,32,128]{2,1,0:T(8,128)S(1)} %get-tuple-element.46), channel_id=1, source_target_pairs={{0,8},{8,0},{16,24},{24,16},{1,9},{9,1},{17,25},{25,17},{2,10},{10... | collective-permute-start | bytes 638984 | tf_op jit(solution)/shard_map/to_columns/ppermute | solution.py:393
  9.2 1.5 %collective-permute-start.2 = (f32[13,32,128]{2,1,0:T(8,128)S(1)}, f32[13,32,128]{2,1,0:T(8,128)S(1)}, u32[]{:S(2)}, u32[]{:S(2)}) collective-permute-start(f32[13,32,128]{2,1,0:T(8,128)S(1)} %get-tuple-element.47), channel_id=1, source_target_pairs={{0,16},{8,24},{16,0},{24,8},{1,17},{9,25},{17,1},{25,9},{2,18},{10... | collective-permute-start | bytes 638984 | tf_op jit(solution)/shard_map/to_columns/ppermute | solution.py:393
  10.7 0.5 collective-permute-start.3
  11.2 4.6 %collective-permute-done.1.refs_1_ = f32[13,32,128]{2,1,0:T(8,128)S(1)} collective-permute-done((f32[13,32,128]{2,1,0:T(8,128)S(1)}, f32[13,32,128]{2,1,0:T(8,128)S(1)}, u32[]{:S(2)}, u32[]{:S(2)}) %collective-permute-start.1) | collective-permute-done | bytes 213024 | tf_op jit(solution)/shard_map/to_columns/ppermute | solution.py:393
  15.7 3.6 %collective-permute-done.2.refs_2_ = f32[13,32,128]{2,1,0:T(8,128)S(1)} collective-permute-done((f32[13,32,128]{2,1,0:T(8,128)S(1)}, f32[13,32,128]{2,1,0:T(8,128)S(1)}, u32[]{:S(2)}, u32[]{:S(2)}) %collective-permute-start.2) | collective-permute-done | bytes 213024 | tf_op jit(solution)/shard_map/to_columns/ppermute | solution.py:393
  19.5 0.5 collective-permute-start.7
  20.0 0.4 collective-permute-start.9
  20.5 0.8 %slice_add_fusion.1 = s32[2048,1]{0,1:T(1,128)S(1)} fusion(s32[2048,2]{0,1:T(2,128)} %param.5), kind=kLoop, calls=%fused_computation.9 | loop fusion | flops 4096 | bytes 24576 | tf_op jit(solution)/shard_map/add | solution.py:364
  21.3 1.1 %collective-permute-start.4 = (f32[6,32,128]{2,1,0:T(8,128)S(1)}, f32[6,32,128]{2,1,0:T(8,128)S(1)}, u32[]{:S(2)}, u32[]{:S(2)}) collective-permute-start(f32[6,32,128]{2,1,0:T(8,128)S(1)} %get-tuple-element.51), channel_id=1, source_target_pairs={{0,8},{8,0},{16,24},{24,16},{1,9},{9,1},{17,25},{25,17},{2,10},{10... | collective-permute-start | bytes 294920 | tf_op jit(solution)/shard_map/next_to_columns/ppermute | solution.py:398
  22.4 0.9 %collective-permute-start.5 = (f32[6,32,128]{2,1,0:T(8,128)S(1)}, f32[6,32,128]{2,1,0:T(8,128)S(1)}, u32[]{:S(2)}, u32[]{:S(2)}) collective-permute-start(f32[6,32,128]{2,1,0:T(8,128)S(1)} %get-tuple-element.52), channel_id=1, source_target_pairs={{0,16},{8,24},{16,0},{24,8},{1,17},{9,25},{17,1},{25,9},{2,18},{10... | collective-permute-start | bytes 294920 | tf_op jit(solution)/shard_map/next_to_columns/ppermute | solution.py:398
  23.3 1.5 %collective-permute-start.6 = (f32[6,32,128]{2,1,0:T(8,128)S(1)}, f32[6,32,128]{2,1,0:T(8,128)S(1)}, u32[]{:S(2)}, u32[]{:S(2)}) collective-permute-start(f32[6,32,128]{2,1,0:T(8,128)S(1)} %get-tuple-element.53), channel_id=1, source_target_pairs={{0,24},{8,16},{16,8},{24,0},{1,25},{9,17},{17,9},{25,1},{2,26},{10... | collective-permute-start | bytes 294920 | tf_op jit(solution)/shard_map/next_to_columns/ppermute | solution.py:398
  24.9 0.8 %copy-done = f32[128,128]{1,0:T(8,128)S(1)} copy-done((f32[128,128]{1,0:T(8,128)S(1)}, f32[128,128]{1,0:T(8,128)}, u32[]{:S(2)}) %copy-start) | copy-done | bytes 65560
  25.7 7.5 %inner_terms.2 = (f32[12,128,128]{2,1,0:T(8,128)S(1)}, f32[3072,128]{1,0:T(8,128)S(1)}, f32[9216,128]{1,0:T(8,128)S(1)}, bf16[3072,256]{1,0:T(8,128)(2,1)S(1)}, ...) custom-call(s32[2048]{0:T(1024)S(1)} %bitcast.18, f32[128,128]{1,0:T(8,128)S(1)} %copy-done, ...), custom_call_target="tpu_custom_call" | custom-call | flops 12000000000 | bytes 10000000 | tf_op jit(solution)/shard_map/inner_terms/pallas_call | solution.py:406
  33.4 4.3 %inner_terms.3.inner_ref = f32[2,256,128]{2,1,0:T(8,128)S(1)} custom-call(s32[2048]{0:T(1024)S(1)} %bitcast.19, f32[3072,128]{1,0:T(8,128)S(1)} %get-tuple-element.68.carry_ref, f32[9216,128]{1,0:T(8,128)S(1)} %get-tuple-element.69.slope_ref, bf16[3072,256]{1,0:T(8,128)(2,1)S(1)} %get-tuple-element.70.rhs_ref, f32[6144,128]{1,0:T(8,128)S(1)} %get-tuple-element.71.picked_ref), custom_call_target="tpu_custom_call" | custom-call | flops 8000000000 | bytes 10000000 | tf_op jit(solution)/shard_map/inner_terms/pallas_call | solution.py:426
  37.7 3.3 %edge_terms.4 = (f32[1024,128]{1,0:T(8,128)S(1)}, f32[3072,128]{1,0:T(8,128)S(1)}, bf16[3072,256]{1,0:T(8,128)(2,1)S(1)}, f32[256,128]{1,0:T(8,128)S(1)}, f32[6144,128]{1,0:T(8,128)S(1)}) custom-call(s32[2048]{0:T(1024)S(1)} %bitcast.20, f32[128,128]{1,0:T(8,128)S(1)} %copy-done.1, f32[6,32,128]{2,1,0:T(8,128)S(1)} %get-tuple-element.61.refs_0_, ...), custom_call_target="tpu_custom_call" | custom-call | tf_op jit(solution)/shard_map/edge_terms/pallas_call | solution.py:436
  40.9 1.5 %collective-permute-start.12 = (f32[256,128]{1,0:T(8,128)S(1)}, f32[256,128]{1,0:T(8,128)S(1)}, u32[]{:S(2)}, u32[]{:S(2)}) collective-permute-start(f32[256,128]{1,0:T(8,128)S(1)} %get-tuple-element.74), channel_id=1, source_target_pairs={{0,24},{8,16},{16,8},{24,0},{1,25},{9,17},{17,9},{25,1},{2,26},{10... | collective-permute-start | bytes 393224 | tf_op jit(solution)/shard_map/sum_over_columns/ppermute | solution.py:455
  42.4 1.9 %edge_terms.5 = (f32[256,128]{1,0:T(8,128)S(1)}, f32[6144,128]{1,0:T(8,128)S(1)}) custom-call(s32[2048]{0:T(1024)S(1)} %bitcast.21, f32[1024,128]{1,0:T(8,128)S(1)} %get-tuple-element.72.carry_ref, f32[3072,128]{1,0:T(8,128)S(1)} %get-tuple-element.73.slope_ref, bf16[3072,256]{1,0:T(8,128)(2,1)S(1)} %get-tuple-element.67.rhs_ref, ...), custom_call_target="tpu_custom_call" | custom-call | flops 100000000 | bytes 100000 | tf_op jit(solution)/shard_map/edge_terms/pallas_call | solution.py:463
  44.3 1.2 %collective-permute-start.13 = (f32[256,128]{1,0:T(8,128)S(1)}, f32[256,128]{1,0:T(8,128)S(1)}, u32[]{:S(2)}, u32[]{:S(2)}) collective-permute-start(f32[256,128]{1,0:T(8,128)S(1)} %get-tuple-element.77), channel_id=1, source_target_pairs={{0,16},{8,24},{16,0},{24,8},{1,17},{9,25},{17,1},{25,9},{2,18},{10... | collective-permute-start | bytes 393224 | tf_op jit(solution)/shard_map/sum_over_columns/ppermute | solution.py:455
  45.5 1.8 %edge_terms.6 = (f32[256,128]{1,0:T(8,128)S(1)}, f32[6144,128]{1,0:T(8,128)S(1)}) custom-call(s32[2048]{0:T(1024)S(1)} %bitcast.22, f32[1024,128]{1,0:T(8,128)S(1)} %get-tuple-element.72.carry_ref, f32[3072,128]{1,0:T(8,128)S(1)} %get-tuple-element.73.slope_ref, bf16[3072,256]{1,0:T(8,128)(2,1)S(1)} %get-tuple-element.67.rhs_ref, ...), custom_call_target="tpu_custom_call" | custom-call | flops 100000000 | bytes 100000 | tf_op jit(solution)/shard_map/edge_terms/pallas_call | solution.py:463
  47.3 1.1 %collective-permute-start.14 = (f32[256,128]{1,0:T(8,128)S(1)}, f32[256,128]{1,0:T(8,128)S(1)}, u32[]{:S(2)}, u32[]{:S(2)}) collective-permute-start(f32[256,128]{1,0:T(8,128)S(1)} %get-tuple-element.80), channel_id=1, source_target_pairs={{0,8},{8,0},{16,24},{24,16},{1,9},{9,1},{17,25},{25,17},{2,10},{10... | collective-permute-start | bytes 393224 | tf_op jit(solution)/shard_map/sum_over_columns/ppermute | solution.py:455
  48.3 2.2 %collective-permute-done.13.refs_1_ = f32[256,128]{1,0:T(8,128)S(1)} collective-permute-done((f32[256,128]{1,0:T(8,128)S(1)}, f32[256,128]{1,0:T(8,128)S(1)}, u32[]{:S(2)}, u32[]{:S(2)}) %collective-permute-start.13) | collective-permute-done | bytes 131104 | tf_op jit(solution)/shard_map/sum_over_columns/ppermute | solution.py:455
  50.6 1.1 %edge_terms.7 = f32[256,128]{1,0:T(8,128)S(1)} custom-call(bf16[3072,256]{1,0:T(8,128)(2,1)S(1)} %get-tuple-element.67.rhs_ref, f32[2,256,128]{2,1,0:T(8,128)S(1)} %inner_terms.3.inner_ref, f32[6144,128]{1,0:T(8,128)S(1)} %get-tuple-element.82.picked_ref, f32[256,128]{1,0:T(8,128)S(1)} %collective-permute-done.12.refs_0_, ...), custom_call_target="tpu_custom_call" | custom-call | flops 100000000 | bytes 100000 | tf_op jit(solution)/shard_map/edge_terms/pallas_call | solution.py:473
  51.7 1.0 %collective-permute-done.14 = f32[256,128]{1,0:T(8,128)S(1)} collective-permute-done((f32[256,128]{1,0:T(8,128)S(1)}, f32[256,128]{1,0:T(8,128)S(1)}, u32[]{:S(2)}, u32[]{:S(2)}) %collective-permute-start.14) | collective-permute-done | bytes 131104 | tf_op jit(solution)/shard_map/sum_over_columns/ppermute | solution.py:455
  52.7 0.4 collective-permute-start.15
  53.1 2.5 %collective-permute-start.17 = (f32[64,128]{1,0:T(8,128)S(1)}, f32[64,128]{1,0:T(8,128)S(1)}, u32[]{:S(2)}, u32[]{:S(2)}) collective-permute-start(f32[64,128]{1,0:T(8,128)S(1)} %get-tuple-element.88), channel_id=1, source_target_pairs={{0,6},{1,7},{2,4},{3,5},{4,2},{5,3},{6,0},{7,1},{8,14},{9,15},{10,... | collective-permute-start | bytes 98312 | tf_op jit(solution)/shard_map/sum_over_chips/ppermute | solution.py:488
  55.6 0.7 %collective-permute-start.16 = (f32[64,128]{1,0:T(8,128)S(1)}, f32[64,128]{1,0:T(8,128)S(1)}, u32[]{:S(2)}, u32[]{:S(2)}) collective-permute-start(f32[64,128]{1,0:T(8,128)S(1)} %get-tuple-element.89), channel_id=1, source_target_pairs={{0,4},{1,5},{2,6},{3,7},{4,0},{5,1},{6,2},{7,3},{8,12},{9,13},{10,... | collective-permute-start | bytes 98312 | tf_op jit(solution)/shard_map/sum_over_chips/ppermute | solution.py:488
  56.3 0.8 %collective-permute-done.15 = f32[64,128]{1,0:T(8,128)S(1)} collective-permute-done((f32[64,128]{1,0:T(8,128)S(1)}, f32[64,128]{1,0:T(8,128)S(1)}, u32[]{:S(2)}, u32[]{:S(2)}) %collective-permute-start.15) | collective-permute-done | bytes 32800 | tf_op jit(solution)/shard_map/sum_over_chips/ppermute | solution.py:488
  57.0 1.9 %collective-permute-done.17 = f32[64,128]{1,0:T(8,128)S(1)} collective-permute-done((f32[64,128]{1,0:T(8,128)S(1)}, f32[64,128]{1,0:T(8,128)S(1)}, u32[]{:S(2)}, u32[]{:S(2)}) %collective-permute-start.17) | collective-permute-done | bytes 32800 | tf_op jit(solution)/shard_map/sum_over_chips/ppermute | solution.py:488
  58.9 1.8 %collective-permute-done.16 = f32[64,128]{1,0:T(8,128)S(1)} collective-permute-done((f32[64,128]{1,0:T(8,128)S(1)}, f32[64,128]{1,0:T(8,128)S(1)}, u32[]{:S(2)}, u32[]{:S(2)}) %collective-permute-start.16) | collective-permute-done | bytes 32800 | tf_op jit(solution)/shard_map/sum_over_chips/ppermute | solution.py:488
  60.8 0.6 %fusion.2 = f32[64,128]{1,0:T(8,128)} fusion(f32[64,128]{1,0:T(8,128)S(1)} %collective-permute-done.17, f32[64,128]{1,0:T(8,128)S(1)} %collective-permute-done.16, f32[64,128]{1,0:T(8,128)S(1)} %collective-permute-done.15, f32[256,128]{1,0:T(8,128)S(1)} %add.19), kind=kLoop, calls=%fused_computation.8 | loop fusion | flops 32768 | bytes 163840 | tf_op jit(solution)/shard_map/sum_over_chips/mul | solution.py:489
  (21 shorter events, 0.3 us)
Async XLA Ops:
  3.1 16.2 %collective-permute-start = (f32[4,6,32,128]{3,2,1,0:T(8,128)S(1)}, f32[4,6,32,128]{3,2,1,0:T(8,128)S(1)}, u32[]{:S(2)}, u32[]{:S(2)}) collective-permute-start(f32[4,6,32,128]{3,2,1,0:T(8,128)S(1)} %get-tuple-element.44), channel_id=1, source_target_pairs={{0,7},{1,2},{2,1},{3,4},{4,3},{5,6},{6,5},{7,0},{8,15},{9,10},{10,... | collective-permute-start | bytes 1179656 | tf_op jit(solution)/shard_map/to_next_plane/ppermute | solution.py:391
  7.7 8.1 %collective-permute-start.1 = (f32[13,32,128]{2,1,0:T(8,128)S(1)}, f32[13,32,128]{2,1,0:T(8,128)S(1)}, u32[]{:S(2)}, u32[]{:S(2)}) collective-permute-start(f32[13,32,128]{2,1,0:T(8,128)S(1)} %get-tuple-element.46), channel_id=1, source_target_pairs={{0,8},{8,0},{16,24},{24,16},{1,9},{9,1},{17,25},{25,17},{2,10},{10... | collective-permute-start | bytes 638984 | tf_op jit(solution)/shard_map/to_columns/ppermute | solution.py:393
  9.2 10.2 %collective-permute-start.2 = (f32[13,32,128]{2,1,0:T(8,128)S(1)}, f32[13,32,128]{2,1,0:T(8,128)S(1)}, u32[]{:S(2)}, u32[]{:S(2)}) collective-permute-start(f32[13,32,128]{2,1,0:T(8,128)S(1)} %get-tuple-element.47), channel_id=1, source_target_pairs={{0,16},{8,24},{16,0},{24,8},{1,17},{9,25},{17,1},{25,9},{2,18},{10... | collective-permute-start | bytes 638984 | tf_op jit(solution)/shard_map/to_columns/ppermute | solution.py:393
  10.7 8.7 %collective-permute-start.3 = (f32[13,32,128]{2,1,0:T(8,128)S(1)}, f32[13,32,128]{2,1,0:T(8,128)S(1)}, u32[]{:S(2)}, u32[]{:S(2)}) collective-permute-start(f32[13,32,128]{2,1,0:T(8,128)S(1)} %get-tuple-element.49), channel_id=1, source_target_pairs={{0,24},{8,16},{16,8},{24,0},{1,25},{9,17},{17,9},{25,1},{2,26},{10... | collective-permute-start | bytes 638984 | tf_op jit(solution)/shard_map/to_columns/ppermute | solution.py:393
  19.4 3.0 %collective-permute-start.10 = (f32[13,32,128]{2,1,0:T(8,128)S(1)}, f32[13,32,128]{2,1,0:T(8,128)S(1)}, u32[]{:S(2)}, u32[]{:S(2)}) collective-permute-start(f32[13,32,128]{2,1,0:T(8,128)S(1)} %collective-permute-done.3.refs_3_), channel_id=1, source_target_pairs={{0,1},{1,0},{2,3},{3,2},{4,5},{5,4},{6,7},{7,6},{8,9},{9,8},{10,11... | collective-permute-start | bytes 638984 | tf_op jit(solution)/shard_map/to_other_core/ppermute | solution.py:400
  19.5 3.9 %collective-permute-start.7 = (f32[13,32,128]{2,1,0:T(8,128)S(1)}, f32[13,32,128]{2,1,0:T(8,128)S(1)}, u32[]{:S(2)}, u32[]{:S(2)}) collective-permute-start(f32[13,32,128]{2,1,0:T(8,128)S(1)} %get-tuple-element.54.refs_0_), channel_id=1, source_target_pairs={{0,1},{1,0},{2,3},{3,2},{4,5},{5,4},{6,7},{7,6},{8,9},{9,8},{10,11... | collective-permute-start | bytes 638984 | tf_op jit(solution)/shard_map/to_other_core/ppermute | solution.py:400
  20.0 4.9 %collective-permute-start.8 = (f32[13,32,128]{2,1,0:T(8,128)S(1)}, f32[13,32,128]{2,1,0:T(8,128)S(1)}, u32[]{:S(2)}, u32[]{:S(2)}) collective-permute-start(f32[13,32,128]{2,1,0:T(8,128)S(1)} %collective-permute-done.1.refs_1_), channel_id=1, source_target_pairs={{0,1},{1,0},{2,3},{3,2},{4,5},{5,4},{6,7},{7,6},{8,9},{9,8},{10,11... | collective-permute-start | bytes 638984 | tf_op jit(solution)/shard_map/to_other_core/ppermute | solution.py:400
  20.0 4.8 %collective-permute-start.9 = (f32[13,32,128]{2,1,0:T(8,128)S(1)}, f32[13,32,128]{2,1,0:T(8,128)S(1)}, u32[]{:S(2)}, u32[]{:S(2)}) collective-permute-start(f32[13,32,128]{2,1,0:T(8,128)S(1)} %collective-permute-done.2.refs_2_), channel_id=1, source_target_pairs={{0,1},{1,0},{2,3},{3,2},{4,5},{5,4},{6,7},{7,6},{8,9},{9,8},{10,11... | collective-permute-start | bytes 638984 | tf_op jit(solution)/shard_map/to_other_core/ppermute | solution.py:400
  21.3 11.9 %collective-permute-start.4 = (f32[6,32,128]{2,1,0:T(8,128)S(1)}, f32[6,32,128]{2,1,0:T(8,128)S(1)}, u32[]{:S(2)}, u32[]{:S(2)}) collective-permute-start(f32[6,32,128]{2,1,0:T(8,128)S(1)} %get-tuple-element.51), channel_id=1, source_target_pairs={{0,8},{8,0},{16,24},{24,16},{1,9},{9,1},{17,25},{25,17},{2,10},{10... | collective-permute-start | bytes 294920 | tf_op jit(solution)/shard_map/next_to_columns/ppermute | solution.py:398
  22.4 10.8 %collective-permute-start.5 = (f32[6,32,128]{2,1,0:T(8,128)S(1)}, f32[6,32,128]{2,1,0:T(8,128)S(1)}, u32[]{:S(2)}, u32[]{:S(2)}) collective-permute-start(f32[6,32,128]{2,1,0:T(8,128)S(1)} %get-tuple-element.52), channel_id=1, source_target_pairs={{0,16},{8,24},{16,0},{24,8},{1,17},{9,25},{17,1},{25,9},{2,18},{10... | collective-permute-start | bytes 294920 | tf_op jit(solution)/shard_map/next_to_columns/ppermute | solution.py:398
  23.3 9.9 %collective-permute-start.6 = (f32[6,32,128]{2,1,0:T(8,128)S(1)}, f32[6,32,128]{2,1,0:T(8,128)S(1)}, u32[]{:S(2)}, u32[]{:S(2)}) collective-permute-start(f32[6,32,128]{2,1,0:T(8,128)S(1)} %get-tuple-element.53), channel_id=1, source_target_pairs={{0,24},{8,16},{16,8},{24,0},{1,25},{9,17},{17,9},{25,1},{2,26},{10... | collective-permute-start | bytes 294920 | tf_op jit(solution)/shard_map/next_to_columns/ppermute | solution.py:398
  24.9 0.8 %copy-start = (f32[128,128]{1,0:T(8,128)S(1)}, f32[128,128]{1,0:T(8,128)}, u32[]{:S(2)}) copy-start(f32[128,128]{1,0:T(8,128)} %coeffs_ref.3) | copy-start | bytes 196612
  33.3 4.4 %collective-permute-start.11 = (f32[4,6,32,128]{3,2,1,0:T(8,128)S(1)}, f32[4,6,32,128]{3,2,1,0:T(8,128)S(1)}, u32[]{:S(2)}, u32[]{:S(2)}) collective-permute-start(f32[4,6,32,128]{3,2,1,0:T(8,128)S(1)} %pad_maximum_fusion), channel_id=1, source_target_pairs={{0,1},{1,0},{2,3},{3,2},{4,5},{5,4},{6,7},{7,6},{8,9},{9,8},{10,11... | collective-permute-start | bytes 1179656 | tf_op jit(solution)/shard_map/next_to_other_core/ppermute | solution.py:424
  33.3 4.3 %copy-start.1 = (f32[128,128]{1,0:T(8,128)S(1)}, f32[128,128]{1,0:T(8,128)}, u32[]{:S(2)}) copy-start(f32[128,128]{1,0:T(8,128)} %coeffs_ref.3) | copy-start | bytes 196612
  40.9 9.7 %collective-permute-start.12 = (f32[256,128]{1,0:T(8,128)S(1)}, f32[256,128]{1,0:T(8,128)S(1)}, u32[]{:S(2)}, u32[]{:S(2)}) collective-permute-start(f32[256,128]{1,0:T(8,128)S(1)} %get-tuple-element.74), channel_id=1, source_target_pairs={{0,24},{8,16},{16,8},{24,0},{1,25},{9,17},{17,9},{25,1},{2,26},{10... | collective-permute-start | bytes 393224 | tf_op jit(solution)/shard_map/sum_over_columns/ppermute | solution.py:455
  44.3 6.2 %collective-permute-start.13 = (f32[256,128]{1,0:T(8,128)S(1)}, f32[256,128]{1,0:T(8,128)S(1)}, u32[]{:S(2)}, u32[]{:S(2)}) collective-permute-start(f32[256,128]{1,0:T(8,128)S(1)} %get-tuple-element.77), channel_id=1, source_target_pairs={{0,16},{8,24},{16,0},{24,8},{1,17},{9,25},{17,1},{25,9},{2,18},{10... | collective-permute-start | bytes 393224 | tf_op jit(solution)/shard_map/sum_over_columns/ppermute | solution.py:455
  47.3 5.4 %collective-permute-start.14 = (f32[256,128]{1,0:T(8,128)S(1)}, f32[256,128]{1,0:T(8,128)S(1)}, u32[]{:S(2)}, u32[]{:S(2)}) collective-permute-start(f32[256,128]{1,0:T(8,128)S(1)} %get-tuple-element.80), channel_id=1, source_target_pairs={{0,8},{8,0},{16,24},{24,16},{1,9},{9,1},{17,25},{25,17},{2,10},{10... | collective-permute-start | bytes 393224 | tf_op jit(solution)/shard_map/sum_over_columns/ppermute | solution.py:455
  52.7 4.3 %collective-permute-start.15 = (f32[64,128]{1,0:T(8,128)S(1)}, f32[64,128]{1,0:T(8,128)S(1)}, u32[]{:S(2)}, u32[]{:S(2)}) collective-permute-start(f32[64,128]{1,0:T(8,128)S(1)} %get-tuple-element.87), channel_id=1, source_target_pairs={{0,2},{1,3},{2,0},{3,1},{4,6},{5,7},{6,4},{7,5},{8,10},{9,11},{10,... | collective-permute-start | bytes 98312 | tf_op jit(solution)/shard_map/sum_over_chips/ppermute | solution.py:488
  53.1 5.8 %collective-permute-start.17 = (f32[64,128]{1,0:T(8,128)S(1)}, f32[64,128]{1,0:T(8,128)S(1)}, u32[]{:S(2)}, u32[]{:S(2)}) collective-permute-start(f32[64,128]{1,0:T(8,128)S(1)} %get-tuple-element.88), channel_id=1, source_target_pairs={{0,6},{1,7},{2,4},{3,5},{4,2},{5,3},{6,0},{7,1},{8,14},{9,15},{10,... | collective-permute-start | bytes 98312 | tf_op jit(solution)/shard_map/sum_over_chips/ppermute | solution.py:488
  55.6 5.2 %collective-permute-start.16 = (f32[64,128]{1,0:T(8,128)S(1)}, f32[64,128]{1,0:T(8,128)S(1)}, u32[]{:S(2)}, u32[]{:S(2)}) collective-permute-start(f32[64,128]{1,0:T(8,128)S(1)} %get-tuple-element.89), channel_id=1, source_target_pairs={{0,4},{1,5},{2,6},{3,7},{4,0},{5,1},{6,2},{7,3},{8,12},{9,13},{10,... | collective-permute-start | bytes 98312 | tf_op jit(solution)/shard_map/sum_over_chips/ppermute | solution.py:488

commit v12 on v11

--- a/solution.py
+++ b/solution.py
@@ -45,11 +45,13 @@
     return rows
 
 
-def pack_kernel(field_ref, *refs, sizes):
-    *out_refs, sorted_ref, held_ref, sems = refs
+def pack_kernel(field_ref, pairs_ref, coeffs_ref, *refs, sizes):
+    *out_refs, codes_ref, held_coeffs_ref, sorted_ref, held_ref, held_pairs_ref, sems = refs
     local_s, rows_y, tm_count = sizes
     lanes = field_ref.shape[3]
     copies = [pltpu.make_async_copy(field_ref.at[:, c], held_ref.at[c], sems.at[c]) for c in range(3)]
+    copies.append(pltpu.make_async_copy(pairs_ref, held_pairs_ref, sems.at[3]))
+    copies.append(pltpu.make_async_copy(coeffs_ref, held_coeffs_ref, sems.at[4]))
     for copy in copies:
         copy.start()
     rows_ref = held_ref.reshape(3 * local_s * rows_y, lanes)
@@ -88,6 +90,12 @@
         block = jnp.bitwise_xor(t, peer)
         out_refs[peer][...] = sorted_ref[block]
         out_refs[tm_count][peer] = sorted_ref[block, pl.ds(core * half, half)]
+    copies[3].wait()
+    copies[4].wait()
+    for row in range(codes_ref.shape[0]):
+        here = pl.ds(row * lanes, lanes)
+        first, second = held_pairs_ref[0:1, here], held_pairs_ref[1:2, here]
+        codes_ref[row : row + 1, :] = first * held_coeffs_ref.shape[1] + second
 
 
 def mode_weights(coeffs_ref, local_s, tm_count):
@@ -132,12 +140,14 @@
     chips, share, bits = sizes
     t, chip, core = place_of_device()
     first_chip = jnp.bitwise_xor(t, peer) * chips
+    assert codes_ref.shape[1] % share == 0
 
     def one_share(ahead, _):
         base = ((first_chip + jnp.bitwise_xor(chip, ahead)) * 2 + core) * share
+        row, first = lax.div(base, codes_ref.shape[1]), lax.rem(base, codes_ref.shape[1])
 
         def one(q, _):
-            code = codes_ref[base + q]
+            code = codes_ref[row, first + q]
             one_pair(ahead * share + q, lax.shift_right_logical(code, bits), jnp.bitwise_and(code, 2**bits - 1))
             return 0
 
@@ -226,13 +236,15 @@
 
     codes.wait()
 
+    pick_inner(held_codes_ref, carry_ref, slope_ref, conv_ref, first_peer, (chips, share, bits))
+
     def one_peer(number, _):
-        pick_inner(held_codes_ref, carry_ref, slope_ref, conv_ref, first_peer + number, (chips, share, bits))
         out_ref[number] = project(conv_ref, rhs_ref, chips * share, 3 * height, lanes)
+        following = lax.rem(first_peer + number + 1, tm_count)
+        pick_inner(held_codes_ref, carry_ref, slope_ref, conv_ref, following, (chips, share, bits))
         return 0
 
     lax.fori_loop(0, out_ref.shape[0], one_peer, 0)
-    pick_inner(held_codes_ref, carry_ref, slope_ref, conv_ref, 0, (chips, share, bits))
 
 
 def pick_inner(codes_ref, carry_ref, slope_ref, conv_ref, peer, sizes):
@@ -257,19 +269,26 @@
 def rest_kernel(
     codes_ref, carry_ref, slope_ref, rhs_ref, picked_ref, out_ref, conv_ref, held_codes_ref, sem, *, sizes
 ):
+    del picked_ref
     chips, share, _ = sizes
     codes = copy_of_codes(codes_ref, held_codes_ref, sem)
     block, lanes = chips * share, conv_ref.shape[1]
     places = conv_ref.shape[0] // block
-    out_ref[0] = project(picked_ref, rhs_ref, block, places, lanes)
-    codes.wait()
 
     def one_peer(peer, _):
-        pick_inner(held_codes_ref, carry_ref, slope_ref, conv_ref, peer, sizes)
         out_ref[peer] = project(conv_ref, rhs_ref, block, places, lanes)
+
+        @pl.when(peer == 0)
+        def _():
+            codes.wait()
+
+        @pl.when(peer + 1 < out_ref.shape[0])
+        def _():
+            pick_inner(held_codes_ref, carry_ref, slope_ref, conv_ref, peer + 1, sizes)
+
         return 0
 
-    lax.fori_loop(1, out_ref.shape[0], one_peer, 0)
+    lax.fori_loop(0, out_ref.shape[0], one_peer, 0)
 
 
 def far_kernel(codes_ref, coeffs_ref, *refs, peer, sizes):
@@ -334,9 +353,15 @@
     pick_edge(held_codes_ref, carry_ref, slope_ref, conv_ref, peer - 1, sizes)
 
 
-def last_edge_kernel(rhs_ref, inner_ref, picked_ref, *refs):
-    *arrived_refs, out_ref = refs
-    total = edge_sum(picked_ref, rhs_ref, inner_ref, 0)
+def picked_edge_kernel(rhs_ref, inner_ref, picked_ref, out_ref, *, peer):
+    out_ref[...] = edge_sum(picked_ref, rhs_ref, inner_ref, peer)
+
+
+def own_edge_kernel(codes_ref, carry_ref, slope_ref, rhs_ref, inner_ref, *refs, sizes):
+    *arrived_refs, out_ref, conv_ref, held_codes_ref, sem = refs
+    copy_of_codes(codes_ref, held_codes_ref, sem).wait()
+    pick_edge(held_codes_ref, carry_ref, slope_ref, conv_ref, 0, sizes)
+    total = edge_sum(conv_ref, rhs_ref, inner_ref, 0)
     for arrived_ref in arrived_refs:
         total = total + arrived_ref[...]
     out_ref[...] = total
@@ -361,7 +386,6 @@
     factor = float(space_count * rows_y * lanes) ** (-0.5)
     bits = modes.bit_length() - 1
     assert modes == 2**bits
-    codes = in_vmem(pair_table[:, 0] * modes + pair_table[:, 1])
     vmem = pl.BlockSpec(memory_space=pltpu.VMEM)
     block = chips * share
     height = 2 * block_rows
@@ -373,19 +397,30 @@
         return [(i, i ^ peer) for i in range(tm_count)]
 
     with jax.named_scope("pack"):
-        packed = pl.pallas_call(
+        *packed, codes, held_coeffs = pl.pallas_call(
             functools.partial(pack_kernel, sizes=(local_s, rows_y, tm_count)),
             out_shape=[pltpu.VMEM((slabs, local_s, lanes), F32)] * tm_count
-            + [pltpu.VMEM((tm_count, block_rows // 2 * 3, local_s, lanes), F32)],
-            in_specs=[pl.BlockSpec(memory_space=pltpu.HBM)],
-            out_specs=[vmem] * (tm_count + 1),
+            + [
+                pltpu.VMEM((tm_count, block_rows // 2 * 3, local_s, lanes), F32),
+                pltpu.VMEM((pair_table.shape[0] // lanes, lanes), jnp.int32),
+                pltpu.VMEM(coeffs.shape, F32),
+            ],
+            in_specs=[pl.BlockSpec(memory_space=pltpu.HBM)] * 3,
+            out_specs=[vmem] * (tm_count + 3),
             scratch_shapes=[
                 pltpu.VMEM((tm_count, slabs, local_s, lanes), F32),
                 pltpu.VMEM((3, local_s, rows_y, lanes), F32),
-                pltpu.SemaphoreType.DMA((3,)),
+                pltpu.VMEM((2, pair_table.shape[0]), jnp.int32),
+                pltpu.SemaphoreType.DMA((5,)),
             ],
             compiler_params=vmem_limit(16),
-        )(pltpu.with_memory_space_constraint(snapshots.reshape(local_s, 3, rows_y, lanes), pltpu.HBM))
+        )(
+            *[
+                pltpu.with_memory_space_constraint(array, pltpu.HBM)
+                for array in (snapshots.reshape(local_s, 3, rows_y, lanes), pair_table.T, coeffs)
+            ]
+        )
+        codes, coeffs = in_vmem(codes), in_vmem(held_coeffs)
     with jax.named_scope("to_next_plane"):
         ring = [(place, (place + (1 if place % 2 else -1)) % space_count) for place in range(space_count)]
         across_edge = lax.ppermute(packed[tm_count], "space", ring)
@@ -423,12 +458,13 @@
         next_own, inner_tables = lax.optimization_barrier((next_own, inner_tables))
         next_other = lax.ppermute(jnp.stack(next_own), "space", swap)
     with jax.named_scope("inner_terms"):
-        late_sums = pl.pallas_call(
+        late_sums, _ = pl.pallas_call(
             functools.partial(rest_kernel, sizes=(chips, share, bits)),
-            out_shape=groups,
+            out_shape=[groups, picked],
             in_specs=[vmem] * 5,
-            out_specs=vmem,
-            scratch_shapes=[picked] + held_codes,
+            out_specs=[vmem] * 2,
+            input_output_aliases={4: 1},
+            scratch_shapes=held_codes,
             compiler_params=vmem_limit(16),
             cost_estimate=pl.CostEstimate(flops=8 * 10**9, bytes_accessed=10**7, transcendentals=0),
         )(codes, *[in_vmem(table) for table in (*inner_tables, first_picked)])
@@ -449,7 +485,7 @@
             scratch_shapes=held_codes,
             compiler_params=vmem_limit(16),
         )(codes, coeffs, *[in_vmem(piece) for piece in (*next_own, next_other, near, early_sums)])
-    arrived = []
+    arrived, taken = [], 2
     for peer in reversed(range(tm_count - 1)):
         with jax.named_scope("sum_over_columns"):
             arrived.append(lax.ppermute(summed, "tm", across(peer + 1)))
@@ -459,7 +495,8 @@
                 late_sums, _ = lax.optimization_barrier((late_sums, summed))
         with jax.named_scope("edge_terms"):
             inner_sums = early_sums if peer >= early else late_sums
-            if peer:
+            edge_cost = pl.CostEstimate(flops=10**8, bytes_accessed=10**5, transcendentals=0)
+            if peer > 1:
                 summed, next_picked = pl.pallas_call(
                     functools.partial(edge_kernel, peer=peer, sizes=(chips, share, bits)),
                     out_shape=[pltpu.VMEM((block, modes), F32), picked],
@@ -467,19 +504,30 @@
                     out_specs=[vmem] * 2,
                     scratch_shapes=held_codes,
                     compiler_params=vmem_limit(16),
-                    cost_estimate=pl.CostEstimate(flops=10**8, bytes_accessed=10**5, transcendentals=0),
+                    cost_estimate=edge_cost,
                 )(codes, *[in_vmem(table) for table in (*tables, inner_sums, next_picked)])
+            elif peer:
+                summed = pl.pallas_call(
+                    functools.partial(picked_edge_kernel, peer=peer),
+                    out_shape=pltpu.VMEM((block, modes), F32),
+                    in_specs=[vmem] * 3,
+                    out_specs=vmem,
+                    compiler_params=vmem_limit(16),
+                    cost_estimate=edge_cost,
+                )(*[in_vmem(table) for table in (tables[2], inner_sums, next_picked)])
             else:
                 summed = pl.pallas_call(
-                    last_edge_kernel,
+                    functools.partial(own_edge_kernel, sizes=(chips, share, bits)),
                     out_shape=pltpu.VMEM((block, modes), F32),
-                    in_specs=[vmem] * (2 + len(arrived)),
+                    in_specs=[vmem] * (5 + taken),
                     out_specs=vmem,
+                    scratch_shapes=[picked] + held_codes,
                     compiler_params=vmem_limit(16),
-                    cost_estimate=pl.CostEstimate(flops=10**8, bytes_accessed=10**5, transcendentals=0),
-                )(*[in_vmem(table) for table in (tables[2], inner_sums, next_picked, *arrived[:-1])])
+                    cost_estimate=edge_cost,
+                )(codes, *[in_vmem(table) for table in (*tables, inner_sums, *arrived[:taken])])
     with jax.named_scope("sum_over_columns"):
-        summed = summed + arrived[-1]
+        for part in arrived[taken:]:
+            summed = summed + part
     with jax.named_scope("sum_over_chips"):
         shares = summed.reshape(chips, share, modes)
         result = shares[0]

time: 61.7 us -> 61.5 us (level)
  Pallas kernels: 22.9 us -> 24.9 us
  local copies, waits for them, and re-layouts: 0.88 us -> 0.04 us
  other arithmetic: 1.48 us -> 0.67 us
    pallas_call x1 -> x2, Pallas kernels: 1.07 us -> 3.86 us  [the longest x1 2.79 us: shards(): pl.pallas_call(functools.partial(own_edge_kernel, sizes=(chips, share, bi...]
    pallas_call x2 -> x1, Pallas kernels: 3.72 us -> 2.13 us  [shards(): pl.pallas_call(functools.partial(edge_kernel, peer=peer, sizes=(chips, sh...]
    pallas_call x1, Pallas kernels: 7.49 us -> 8.58 us  [shards(): pl.pallas_call(functools.partial(inner_kernel, first_peer=early, sizes=(l...]
    pallas_call x1, Pallas kernels: 4.28 us -> 3.26 us  [shards(): pl.pallas_call(functools.partial(rest_kernel, sizes=(chips, share, bits))...]
    unnamed x4 -> x0, local copies, waits for them, and re-layouts: 0.84 us -> none
    add x2 -> x1, other arithmetic: 0.83 us -> 0.02 us  [shards(): summed = summed + part]
    pallas_call x1, Pallas kernels: 3.26 us -> 3.99 us  [shards(): pl.pallas_call(functools.partial(far_kernel, peer=tm_count - 1, sizes=(lo...]
  transfers between devices with their start and end apart: 18 -> 18, of which waited for: 7 -> 6; matrix products, arithmetic and copies ran while one was open for 1% -> 0% of each run, Pallas kernels for 27% -> 29%
where the time goes in v12:
time: 61.5 us; the launch traced here: 61.4 us
  Pallas kernels  24.9 us (40%)
  starting transfers between devices  19.9 us (32%)
  waiting for transfers between devices  15.6 us (25%)
  other arithmetic  0.67 us (1%)
    pallas_call x1, Pallas kernels, shards(): pl.pallas_call(functools.partial(inner_kernel, first_peer=early, sizes=(l...  8.58 us
    ppermute x3, waiting for transfers between devices, shards(): lax.ppermute(packed[peer], 'tm', across(peer))  8.18 us
    ppermute x3, waiting for transfers between devices, shards(): result = result + lax.ppermute(shares[step], 'space', pairing)  4.65 us
    ppermute x1, starting transfers between devices, shards(): across_edge = lax.ppermute(packed[tm_count], 'space', ring)  4.55 us
    pallas_call x1, Pallas kernels, shards(): pl.pallas_call(functools.partial(far_kernel, peer=tm_count - 1, sizes=(lo...  3.99 us
    ppermute x3, starting transfers between devices, shards(): arrived.append(lax.ppermute(summed, 'tm', across(peer + 1)))  3.69 us
    ppermute x3, starting transfers between devices, shards(): result = result + lax.ppermute(shares[step], 'space', pairing)  3.55 us
    ppermute x3, starting transfers between devices, shards(): lax.ppermute(parts[peer], 'tm', across(peer))  3.49 us
  transfers between devices with their start and end apart: 18, of which 6 were waited for; matrix products, arithmetic and copies ran while one was open for 0% of the time, Pallas kernels for 29%

profile of v12, /device:TPU:0, one launch (start us, length us, event | category | flops | bytes accessed | tf_op | source)
XLA Modules:
  0.0 61.4 jit_solution(16867827532788727554)
XLA Ops:
  0.0 3.1 %pack.1 = (f32[13,32,128]{2,1,0:T(8,128)S(1)}, f32[13,32,128]{2,1,0:T(8,128)S(1)}, f32[13,32,128]{2,1,0:T(8,128)S(1)}, f32[13,32,128]{2,1,0:T(8,128)S(1)}, f32[4...) custom-call(f32[32,3,16,128]{3,2,1,0:T(8,128)} %bitcast.18, s32[2,2048]{1,0:T(2,128)} %bitcast.19, ...), custom_call_target="tpu_custom_call" | custom-call | tf_op jit(solution)/shard_map/pack/pallas_call | solution.py:400
  3.1 4.6 %collective-permute-start = (f32[4,6,32,128]{3,2,1,0:T(8,128)S(1)}, f32[4,6,32,128]{3,2,1,0:T(8,128)S(1)}, u32[]{:S(2)}, u32[]{:S(2)}) collective-permute-start(f32[4,6,32,128]{3,2,1,0:T(8,128)S(1)} %get-tuple-element.47), channel_id=1, source_target_pairs={{0,7},{1,2},{2,1},{3,4},{4,3},{5,6},{6,5},{7,0},{8,15},{9,10},{10,... | collective-permute-start | bytes 1179656 | tf_op jit(solution)/shard_map/to_next_plane/ppermute | solution.py:426
  7.7 1.5 %collective-permute-start.1 = (f32[13,32,128]{2,1,0:T(8,128)S(1)}, f32[13,32,128]{2,1,0:T(8,128)S(1)}, u32[]{:S(2)}, u32[]{:S(2)}) collective-permute-start(f32[13,32,128]{2,1,0:T(8,128)S(1)} %get-tuple-element.49), channel_id=1, source_target_pairs={{0,8},{8,0},{16,24},{24,16},{1,9},{9,1},{17,25},{25,17},{2,10},{10... | collective-permute-start | bytes 638984 | tf_op jit(solution)/shard_map/to_columns/ppermute | solution.py:428
  9.2 1.5 %collective-permute-start.2 = (f32[13,32,128]{2,1,0:T(8,128)S(1)}, f32[13,32,128]{2,1,0:T(8,128)S(1)}, u32[]{:S(2)}, u32[]{:S(2)}) collective-permute-start(f32[13,32,128]{2,1,0:T(8,128)S(1)} %get-tuple-element.50), channel_id=1, source_target_pairs={{0,16},{8,24},{16,0},{24,8},{1,17},{9,25},{17,1},{25,9},{2,18},{10... | collective-permute-start | bytes 638984 | tf_op jit(solution)/shard_map/to_columns/ppermute | solution.py:428
  10.7 0.5 collective-permute-start.3
  11.2 4.6 %collective-permute-done.1.refs_1_ = f32[13,32,128]{2,1,0:T(8,128)S(1)} collective-permute-done((f32[13,32,128]{2,1,0:T(8,128)S(1)}, f32[13,32,128]{2,1,0:T(8,128)S(1)}, u32[]{:S(2)}, u32[]{:S(2)}) %collective-permute-start.1) | collective-permute-done | bytes 213024 | tf_op jit(solution)/shard_map/to_columns/ppermute | solution.py:428
  15.8 3.6 %collective-permute-done.2.refs_2_ = f32[13,32,128]{2,1,0:T(8,128)S(1)} collective-permute-done((f32[13,32,128]{2,1,0:T(8,128)S(1)}, f32[13,32,128]{2,1,0:T(8,128)S(1)}, u32[]{:S(2)}, u32[]{:S(2)}) %collective-permute-start.2) | collective-permute-done | bytes 213024 | tf_op jit(solution)/shard_map/to_columns/ppermute | solution.py:428
  19.4 0.1 collective-permute-start.10
  19.5 0.5 collective-permute-start.7
  20.0 0.1 collective-permute-start.8
  20.1 0.4 collective-permute-start.9
  20.5 1.0 %collective-permute-start.4 = (f32[6,32,128]{2,1,0:T(8,128)S(1)}, f32[6,32,128]{2,1,0:T(8,128)S(1)}, u32[]{:S(2)}, u32[]{:S(2)}) collective-permute-start(f32[6,32,128]{2,1,0:T(8,128)S(1)} %get-tuple-element.54), channel_id=1, source_target_pairs={{0,8},{8,0},{16,24},{24,16},{1,9},{9,1},{17,25},{25,17},{2,10},{10... | collective-permute-start | bytes 294920 | tf_op jit(solution)/shard_map/next_to_columns/ppermute | solution.py:433
  21.5 0.9 %collective-permute-start.5 = (f32[6,32,128]{2,1,0:T(8,128)S(1)}, f32[6,32,128]{2,1,0:T(8,128)S(1)}, u32[]{:S(2)}, u32[]{:S(2)}) collective-permute-start(f32[6,32,128]{2,1,0:T(8,128)S(1)} %get-tuple-element.55), channel_id=1, source_target_pairs={{0,16},{8,24},{16,0},{24,8},{1,17},{9,25},{17,1},{25,9},{2,18},{10... | collective-permute-start | bytes 294920 | tf_op jit(solution)/shard_map/next_to_columns/ppermute | solution.py:433
  22.5 1.5 %collective-permute-start.6 = (f32[6,32,128]{2,1,0:T(8,128)S(1)}, f32[6,32,128]{2,1,0:T(8,128)S(1)}, u32[]{:S(2)}, u32[]{:S(2)}) collective-permute-start(f32[6,32,128]{2,1,0:T(8,128)S(1)} %get-tuple-element.56), channel_id=1, source_target_pairs={{0,24},{8,16},{16,8},{24,0},{1,25},{9,17},{17,9},{25,1},{2,26},{10... | collective-permute-start | bytes 294920 | tf_op jit(solution)/shard_map/next_to_columns/ppermute | solution.py:433
  24.0 8.6 %inner_terms.2 = (f32[12,128,128]{2,1,0:T(8,128)S(1)}, f32[3072,128]{1,0:T(8,128)S(1)}, f32[9216,128]{1,0:T(8,128)S(1)}, bf16[3072,256]{1,0:T(8,128)(2,1)S(1)}, ...) custom-call(s32[16,128]{1,0:T(8,128)S(1)} %get-tuple-element.45.codes_ref, ...), custom_call_target="tpu_custom_call" | custom-call | flops 12000000000 | bytes 10000000 | tf_op jit(solution)/shard_map/inner_terms/pallas_call | solution.py:441
  32.7 0.1 collective-permute-start.11
  32.7 3.3 %inner_terms.3 = (f32[2,256,128]{2,1,0:T(8,128)S(1)}, f32[6144,128]{1,0:T(8,128)S(1)}) custom-call(s32[16,128]{1,0:T(8,128)S(1)} %get-tuple-element.45.codes_ref, f32[3072,128]{1,0:T(8,128)S(1)} %get-tuple-element.73.carry_ref, f32[9216,128]{1,0:T(8,128)S(1)} %get-tuple-element.74.slope_ref, ...), custom_call_target="tpu_custom_call", output_to_operand_aliasing={{1}: (4, {})} | custom-call | flops 8000000000 | bytes 10000000 | tf_op jit(solution)/shard_map/inner_terms/pallas_call | solution.py:461
  36.0 4.0 %edge_terms.4 = (f32[1024,128]{1,0:T(8,128)S(1)}, f32[3072,128]{1,0:T(8,128)S(1)}, bf16[3072,256]{1,0:T(8,128)(2,1)S(1)}, f32[256,128]{1,0:T(8,128)S(1)}, f32[6144,128]{1,0:T(8,128)S(1)}) custom-call(s32[16,128]{1,0:T(8,128)S(1)} %get-tuple-element.45.codes_ref, f32[128,128]{1,0:T(8,128)S(1)} %get-tuple-element.46.coeffs_ref, ...), custom_call_target="tpu_custom_call" | custom-call | tf_op jit(solution)/shard_map/edge_terms/pallas_call | solution.py:472
  40.0 1.5 %collective-permute-start.12 = (f32[256,128]{1,0:T(8,128)S(1)}, f32[256,128]{1,0:T(8,128)S(1)}, u32[]{:S(2)}, u32[]{:S(2)}) collective-permute-start(f32[256,128]{1,0:T(8,128)S(1)} %get-tuple-element.78), channel_id=1, source_target_pairs={{0,24},{8,16},{16,8},{24,0},{1,25},{9,17},{17,9},{25,1},{2,26},{10... | collective-permute-start | bytes 393224 | tf_op jit(solution)/shard_map/sum_over_columns/ppermute | solution.py:491
  41.5 2.1 %edge_terms.5 = (f32[256,128]{1,0:T(8,128)S(1)}, f32[6144,128]{1,0:T(8,128)S(1)}) custom-call(s32[16,128]{1,0:T(8,128)S(1)} %get-tuple-element.45.codes_ref, f32[1024,128]{1,0:T(8,128)S(1)} %get-tuple-element.70.carry_ref, f32[3072,128]{1,0:T(8,128)S(1)} %get-tuple-element.71.slope_ref, bf16[3072,256]{1,0:T(8,128)(2,1)S(1)} %get-tuple-element.72.rhs_ref, ...), custom_call_target="tpu_custom_call" | custom-call | flops 100000000 | bytes 100000 | tf_op jit(solution)/shard_map/edge_terms/pallas_call | solution.py:500
  43.6 1.2 %collective-permute-start.13 = (f32[256,128]{1,0:T(8,128)S(1)}, f32[256,128]{1,0:T(8,128)S(1)}, u32[]{:S(2)}, u32[]{:S(2)}) collective-permute-start(f32[256,128]{1,0:T(8,128)S(1)} %get-tuple-element.81), channel_id=1, source_target_pairs={{0,16},{8,24},{16,0},{24,8},{1,17},{9,25},{17,1},{25,9},{2,18},{10... | collective-permute-start | bytes 393224 | tf_op jit(solution)/shard_map/sum_over_columns/ppermute | solution.py:491
  44.8 1.1 %edge_terms.6 = f32[256,128]{1,0:T(8,128)S(1)} custom-call(bf16[3072,256]{1,0:T(8,128)(2,1)S(1)} %get-tuple-element.72.rhs_ref, f32[2,256,128]{2,1,0:T(8,128)S(1)} %get-tuple-element.84.inner_ref, f32[6144,128]{1,0:T(8,128)S(1)} %get-tuple-element.83.picked_ref), custom_call_target="tpu_custom_call" | custom-call | flops 100000000 | bytes 100000 | tf_op jit(solution)/shard_map/edge_terms/pallas_call | solution.py:510
  45.9 1.1 %collective-permute-start.14 = (f32[256,128]{1,0:T(8,128)S(1)}, f32[256,128]{1,0:T(8,128)S(1)}, u32[]{:S(2)}, u32[]{:S(2)}) collective-permute-start(f32[256,128]{1,0:T(8,128)S(1)} %edge_terms.6), channel_id=1, source_target_pairs={{0,8},{8,0},{16,24},{24,16},{1,9},{9,1},{17,25},{25,17},{2,10},{10... | collective-permute-start | bytes 393224 | tf_op jit(solution)/shard_map/sum_over_columns/ppermute | solution.py:491
  46.9 2.8 %collective-permute-done.13.refs_1_ = f32[256,128]{1,0:T(8,128)S(1)} collective-permute-done((f32[256,128]{1,0:T(8,128)S(1)}, f32[256,128]{1,0:T(8,128)S(1)}, u32[]{:S(2)}, u32[]{:S(2)}) %collective-permute-start.13) | collective-permute-done | bytes 131104 | tf_op jit(solution)/shard_map/sum_over_columns/ppermute | solution.py:491
  49.7 2.8 %edge_terms.7 = f32[256,128]{1,0:T(8,128)S(1)} custom-call(s32[16,128]{1,0:T(8,128)S(1)} %get-tuple-element.45.codes_ref, f32[1024,128]{1,0:T(8,128)S(1)} %get-tuple-element.70.carry_ref, f32[3072,128]{1,0:T(8,128)S(1)} %get-tuple-element.71.slope_ref, bf16[3072,256]{1,0:T(8,128)(2,1)S(1)} %get-tuple-element.72.rhs_ref, ...), custom_call_target="tpu_custom_call" | custom-call | flops 100000000 | bytes 100000 | tf_op jit(solution)/shard_map/edge_terms/pallas_call | solution.py:519
  52.5 0.9 %collective-permute-start.15 = (f32[64,128]{1,0:T(8,128)S(1)}, f32[64,128]{1,0:T(8,128)S(1)}, u32[]{:S(2)}, u32[]{:S(2)}) collective-permute-start(f32[64,128]{1,0:T(8,128)S(1)} %get-tuple-element.89), channel_id=1, source_target_pairs={{0,2},{1,3},{2,0},{3,1},{4,6},{5,7},{6,4},{7,5},{8,10},{9,11},{10,... | collective-permute-start | bytes 98312 | tf_op jit(solution)/shard_map/sum_over_chips/ppermute | solution.py:536
  53.5 2.5 %collective-permute-start.17 = (f32[64,128]{1,0:T(8,128)S(1)}, f32[64,128]{1,0:T(8,128)S(1)}, u32[]{:S(2)}, u32[]{:S(2)}) collective-permute-start(f32[64,128]{1,0:T(8,128)S(1)} %get-tuple-element.90), channel_id=1, source_target_pairs={{0,6},{1,7},{2,4},{3,5},{4,2},{5,3},{6,0},{7,1},{8,14},{9,15},{10,... | collective-permute-start | bytes 98312 | tf_op jit(solution)/shard_map/sum_over_chips/ppermute | solution.py:536
  55.9 0.2 collective-permute-start.16
  56.1 0.4 collective-permute-done.15
  56.5 2.7 %collective-permute-done.17 = f32[64,128]{1,0:T(8,128)S(1)} collective-permute-done((f32[64,128]{1,0:T(8,128)S(1)}, f32[64,128]{1,0:T(8,128)S(1)}, u32[]{:S(2)}, u32[]{:S(2)}) %collective-permute-start.17) | collective-permute-done | bytes 32800 | tf_op jit(solution)/shard_map/sum_over_chips/ppermute | solution.py:536
  59.2 1.6 %collective-permute-done.16 = f32[64,128]{1,0:T(8,128)S(1)} collective-permute-done((f32[64,128]{1,0:T(8,128)S(1)}, f32[64,128]{1,0:T(8,128)S(1)}, u32[]{:S(2)}, u32[]{:S(2)}) %collective-permute-start.16) | collective-permute-done | bytes 32800 | tf_op jit(solution)/shard_map/sum_over_chips/ppermute | solution.py:536
  60.7 0.6 %fusion.2 = f32[64,128]{1,0:T(8,128)} fusion(f32[64,128]{1,0:T(8,128)S(1)} %collective-permute-done.17, f32[64,128]{1,0:T(8,128)S(1)} %collective-permute-done.16, f32[64,128]{1,0:T(8,128)S(1)} %collective-permute-done.15, f32[256,128]{1,0:T(8,128)S(1)} %add.12), kind=kLoop, calls=%fused_computation.8 | loop fusion | flops 32768 | bytes 163840 | tf_op jit(solution)/shard_map/sum_over_chips/mul | solution.py:537
  (16 shorter events, 0.1 us)
Async XLA Ops:
  3.1 16.2 %collective-permute-start = (f32[4,6,32,128]{3,2,1,0:T(8,128)S(1)}, f32[4,6,32,128]{3,2,1,0:T(8,128)S(1)}, u32[]{:S(2)}, u32[]{:S(2)}) collective-permute-start(f32[4,6,32,128]{3,2,1,0:T(8,128)S(1)} %get-tuple-element.47), channel_id=1, source_target_pairs={{0,7},{1,2},{2,1},{3,4},{4,3},{5,6},{6,5},{7,0},{8,15},{9,10},{10,... | collective-permute-start | bytes 1179656 | tf_op jit(solution)/shard_map/to_next_plane/ppermute | solution.py:426
  7.7 8.1 %collective-permute-start.1 = (f32[13,32,128]{2,1,0:T(8,128)S(1)}, f32[13,32,128]{2,1,0:T(8,128)S(1)}, u32[]{:S(2)}, u32[]{:S(2)}) collective-permute-start(f32[13,32,128]{2,1,0:T(8,128)S(1)} %get-tuple-element.49), channel_id=1, source_target_pairs={{0,8},{8,0},{16,24},{24,16},{1,9},{9,1},{17,25},{25,17},{2,10},{10... | collective-permute-start | bytes 638984 | tf_op jit(solution)/shard_map/to_columns/ppermute | solution.py:428
  9.2 10.2 %collective-permute-start.2 = (f32[13,32,128]{2,1,0:T(8,128)S(1)}, f32[13,32,128]{2,1,0:T(8,128)S(1)}, u32[]{:S(2)}, u32[]{:S(2)}) collective-permute-start(f32[13,32,128]{2,1,0:T(8,128)S(1)} %get-tuple-element.50), channel_id=1, source_target_pairs={{0,16},{8,24},{16,0},{24,8},{1,17},{9,25},{17,1},{25,9},{2,18},{10... | collective-permute-start | bytes 638984 | tf_op jit(solution)/shard_map/to_columns/ppermute | solution.py:428
  10.7 8.7 %collective-permute-start.3 = (f32[13,32,128]{2,1,0:T(8,128)S(1)}, f32[13,32,128]{2,1,0:T(8,128)S(1)}, u32[]{:S(2)}, u32[]{:S(2)}) collective-permute-start(f32[13,32,128]{2,1,0:T(8,128)S(1)} %get-tuple-element.52), channel_id=1, source_target_pairs={{0,24},{8,16},{16,8},{24,0},{1,25},{9,17},{17,9},{25,1},{2,26},{10... | collective-permute-start | bytes 638984 | tf_op jit(solution)/shard_map/to_columns/ppermute | solution.py:428
  19.4 2.1 %collective-permute-start.10 = (f32[13,32,128]{2,1,0:T(8,128)S(1)}, f32[13,32,128]{2,1,0:T(8,128)S(1)}, u32[]{:S(2)}, u32[]{:S(2)}) collective-permute-start(f32[13,32,128]{2,1,0:T(8,128)S(1)} %collective-permute-done.3.refs_3_), channel_id=1, source_target_pairs={{0,1},{1,0},{2,3},{3,2},{4,5},{5,4},{6,7},{7,6},{8,9},{9,8},{10,11... | collective-permute-start | bytes 638984 | tf_op jit(solution)/shard_map/to_other_core/ppermute | solution.py:435
  19.5 3.0 %collective-permute-start.7 = (f32[13,32,128]{2,1,0:T(8,128)S(1)}, f32[13,32,128]{2,1,0:T(8,128)S(1)}, u32[]{:S(2)}, u32[]{:S(2)}) collective-permute-start(f32[13,32,128]{2,1,0:T(8,128)S(1)} %get-tuple-element.57.refs_0_), channel_id=1, source_target_pairs={{0,1},{1,0},{2,3},{3,2},{4,5},{5,4},{6,7},{7,6},{8,9},{9,8},{10,11... | collective-permute-start | bytes 638984 | tf_op jit(solution)/shard_map/to_other_core/ppermute | solution.py:435
  20.0 4.0 %collective-permute-start.8 = (f32[13,32,128]{2,1,0:T(8,128)S(1)}, f32[13,32,128]{2,1,0:T(8,128)S(1)}, u32[]{:S(2)}, u32[]{:S(2)}) collective-permute-start(f32[13,32,128]{2,1,0:T(8,128)S(1)} %collective-permute-done.1.refs_1_), channel_id=1, source_target_pairs={{0,1},{1,0},{2,3},{3,2},{4,5},{5,4},{6,7},{7,6},{8,9},{9,8},{10,11... | collective-permute-start | bytes 638984 | tf_op jit(solution)/shard_map/to_other_core/ppermute | solution.py:435
  20.1 3.9 %collective-permute-start.9 = (f32[13,32,128]{2,1,0:T(8,128)S(1)}, f32[13,32,128]{2,1,0:T(8,128)S(1)}, u32[]{:S(2)}, u32[]{:S(2)}) collective-permute-start(f32[13,32,128]{2,1,0:T(8,128)S(1)} %collective-permute-done.2.refs_2_), channel_id=1, source_target_pairs={{0,1},{1,0},{2,3},{3,2},{4,5},{5,4},{6,7},{7,6},{8,9},{9,8},{10,11... | collective-permute-start | bytes 638984 | tf_op jit(solution)/shard_map/to_other_core/ppermute | solution.py:435
  20.5 12.1 %collective-permute-start.4 = (f32[6,32,128]{2,1,0:T(8,128)S(1)}, f32[6,32,128]{2,1,0:T(8,128)S(1)}, u32[]{:S(2)}, u32[]{:S(2)}) collective-permute-start(f32[6,32,128]{2,1,0:T(8,128)S(1)} %get-tuple-element.54), channel_id=1, source_target_pairs={{0,8},{8,0},{16,24},{24,16},{1,9},{9,1},{17,25},{25,17},{2,10},{10... | collective-permute-start | bytes 294920 | tf_op jit(solution)/shard_map/next_to_columns/ppermute | solution.py:433
  21.5 11.1 %collective-permute-start.5 = (f32[6,32,128]{2,1,0:T(8,128)S(1)}, f32[6,32,128]{2,1,0:T(8,128)S(1)}, u32[]{:S(2)}, u32[]{:S(2)}) collective-permute-start(f32[6,32,128]{2,1,0:T(8,128)S(1)} %get-tuple-element.55), channel_id=1, source_target_pairs={{0,16},{8,24},{16,0},{24,8},{1,17},{9,25},{17,1},{25,9},{2,18},{10... | collective-permute-start | bytes 294920 | tf_op jit(solution)/shard_map/next_to_columns/ppermute | solution.py:433
  22.5 10.1 %collective-permute-start.6 = (f32[6,32,128]{2,1,0:T(8,128)S(1)}, f32[6,32,128]{2,1,0:T(8,128)S(1)}, u32[]{:S(2)}, u32[]{:S(2)}) collective-permute-start(f32[6,32,128]{2,1,0:T(8,128)S(1)} %get-tuple-element.56), channel_id=1, source_target_pairs={{0,24},{8,16},{16,8},{24,0},{1,25},{9,17},{17,9},{25,1},{2,26},{10... | collective-permute-start | bytes 294920 | tf_op jit(solution)/shard_map/next_to_columns/ppermute | solution.py:433
  32.7 3.3 %collective-permute-start.11 = (f32[4,6,32,128]{3,2,1,0:T(8,128)S(1)}, f32[4,6,32,128]{3,2,1,0:T(8,128)S(1)}, u32[]{:S(2)}, u32[]{:S(2)}) collective-permute-start(f32[4,6,32,128]{3,2,1,0:T(8,128)S(1)} %pad_maximum_fusion), channel_id=1, source_target_pairs={{0,1},{1,0},{2,3},{3,2},{4,5},{5,4},{6,7},{7,6},{8,9},{9,8},{10,11... | collective-permute-start | bytes 1179656 | tf_op jit(solution)/shard_map/next_to_other_core/ppermute | solution.py:459
  40.0 9.7 %collective-permute-start.12 = (f32[256,128]{1,0:T(8,128)S(1)}, f32[256,128]{1,0:T(8,128)S(1)}, u32[]{:S(2)}, u32[]{:S(2)}) collective-permute-start(f32[256,128]{1,0:T(8,128)S(1)} %get-tuple-element.78), channel_id=1, source_target_pairs={{0,24},{8,16},{16,8},{24,0},{1,25},{9,17},{17,9},{25,1},{2,26},{10... | collective-permute-start | bytes 393224 | tf_op jit(solution)/shard_map/sum_over_columns/ppermute | solution.py:491
  43.6 6.1 %collective-permute-start.13 = (f32[256,128]{1,0:T(8,128)S(1)}, f32[256,128]{1,0:T(8,128)S(1)}, u32[]{:S(2)}, u32[]{:S(2)}) collective-permute-start(f32[256,128]{1,0:T(8,128)S(1)} %get-tuple-element.81), channel_id=1, source_target_pairs={{0,16},{8,24},{16,0},{24,8},{1,17},{9,25},{17,1},{25,9},{2,18},{10... | collective-permute-start | bytes 393224 | tf_op jit(solution)/shard_map/sum_over_columns/ppermute | solution.py:491
  45.9 6.6 %collective-permute-start.14 = (f32[256,128]{1,0:T(8,128)S(1)}, f32[256,128]{1,0:T(8,128)S(1)}, u32[]{:S(2)}, u32[]{:S(2)}) collective-permute-start(f32[256,128]{1,0:T(8,128)S(1)} %edge_terms.6), channel_id=1, source_target_pairs={{0,8},{8,0},{16,24},{24,16},{1,9},{9,1},{17,25},{25,17},{2,10},{10... | collective-permute-start | bytes 393224 | tf_op jit(solution)/shard_map/sum_over_columns/ppermute | solution.py:491
  52.5 4.0 %collective-permute-start.15 = (f32[64,128]{1,0:T(8,128)S(1)}, f32[64,128]{1,0:T(8,128)S(1)}, u32[]{:S(2)}, u32[]{:S(2)}) collective-permute-start(f32[64,128]{1,0:T(8,128)S(1)} %get-tuple-element.89), channel_id=1, source_target_pairs={{0,2},{1,3},{2,0},{3,1},{4,6},{5,7},{6,4},{7,5},{8,10},{9,11},{10,... | collective-permute-start | bytes 98312 | tf_op jit(solution)/shard_map/sum_over_chips/ppermute | solution.py:536
  53.5 5.7 %collective-permute-start.17 = (f32[64,128]{1,0:T(8,128)S(1)}, f32[64,128]{1,0:T(8,128)S(1)}, u32[]{:S(2)}, u32[]{:S(2)}) collective-permute-start(f32[64,128]{1,0:T(8,128)S(1)} %get-tuple-element.90), channel_id=1, source_target_pairs={{0,6},{1,7},{2,4},{3,5},{4,2},{5,3},{6,0},{7,1},{8,14},{9,15},{10,... | collective-permute-start | bytes 98312 | tf_op jit(solution)/shard_map/sum_over_chips/ppermute | solution.py:536
  55.9 4.8 %collective-permute-start.16 = (f32[64,128]{1,0:T(8,128)S(1)}, f32[64,128]{1,0:T(8,128)S(1)}, u32[]{:S(2)}, u32[]{:S(2)}) collective-permute-start(f32[64,128]{1,0:T(8,128)S(1)} %get-tuple-element.91), channel_id=1, source_target_pairs={{0,4},{1,5},{2,6},{3,7},{4,0},{5,1},{6,2},{7,3},{8,12},{9,13},{10,... | collective-permute-start | bytes 98312 | tf_op jit(solution)/shard_map/sum_over_chips/ppermute | solution.py:536

commit v13 on v12

--- a/solution.py
+++ b/solution.py
@@ -92,10 +92,9 @@
         out_refs[tm_count][peer] = sorted_ref[block, pl.ds(core * half, half)]
     copies[3].wait()
     copies[4].wait()
-    for row in range(codes_ref.shape[0]):
-        here = pl.ds(row * lanes, lanes)
-        first, second = held_pairs_ref[0:1, here], held_pairs_ref[1:2, here]
-        codes_ref[row : row + 1, :] = first * held_coeffs_ref.shape[1] + second
+    for first in range(0, codes_ref.shape[0], lanes):
+        here = pl.ds(first, lanes)
+        codes_ref[here] = held_pairs_ref[0, here] * held_coeffs_ref.shape[1] + held_pairs_ref[1, here]
 
 
 def mode_weights(coeffs_ref, local_s, tm_count):
@@ -140,14 +139,12 @@
     chips, share, bits = sizes
     t, chip, core = place_of_device()
     first_chip = jnp.bitwise_xor(t, peer) * chips
-    assert codes_ref.shape[1] % share == 0
 
     def one_share(ahead, _):
         base = ((first_chip + jnp.bitwise_xor(chip, ahead)) * 2 + core) * share
-        row, first = lax.div(base, codes_ref.shape[1]), lax.rem(base, codes_ref.shape[1])
 
         def one(q, _):
-            code = codes_ref[row, first + q]
+            code = codes_ref[base + q]
             one_pair(ahead * share + q, lax.shift_right_logical(code, bits), jnp.bitwise_and(code, 2**bits - 1))
             return 0
 
@@ -402,7 +399,7 @@
             out_shape=[pltpu.VMEM((slabs, local_s, lanes), F32)] * tm_count
             + [
                 pltpu.VMEM((tm_count, block_rows // 2 * 3, local_s, lanes), F32),
-                pltpu.VMEM((pair_table.shape[0] // lanes, lanes), jnp.int32),
+                pltpu.VMEM((pair_table.shape[0],), jnp.int32),
                 pltpu.VMEM(coeffs.shape, F32),
             ],
             in_specs=[pl.BlockSpec(memory_space=pltpu.HBM)] * 3,

time: 61.5 us -> 59 us (0.959)
  Pallas kernels: 24.9 us -> 22.1 us
    pallas_call x1, Pallas kernels: 8.58 us -> 7.5 us  [shards(): pl.pallas_call(functools.partial(inner_kernel, first_peer=early, sizes=(l...]
    pallas_call x1, Pallas kernels: 3.99 us -> 3.26 us  [shards(): pl.pallas_call(functools.partial(far_kernel, peer=tm_count - 1, sizes=(lo...]
  transfers between devices with their start and end apart: 18 -> 18, of which waited for: 6 -> 6; matrix products, arithmetic and copies ran while one was open for 0% -> 0% of each run, Pallas kernels for 29% -> 27%
where the time goes in v13:
time: 59 us; the launch traced here: 58.8 us
  Pallas kernels  22.1 us (37%)
  starting transfers between devices  19.9 us (34%)
  waiting for transfers between devices  16 us (27%)
  other arithmetic  0.67 us (1%)
    ppermute x3, waiting for transfers between devices, shards(): lax.ppermute(packed[peer], 'tm', across(peer))  8.18 us
    pallas_call x1, Pallas kernels, shards(): pl.pallas_call(functools.partial(inner_kernel, first_peer=early, sizes=(l...  7.5 us
    ppermute x3, waiting for transfers between devices, shards(): result = result + lax.ppermute(shares[step], 'space', pairing)  4.65 us
    ppermute x1, starting transfers between devices, shards(): across_edge = lax.ppermute(packed[tm_count], 'space', ring)  4.55 us
    ppermute x3, starting transfers between devices, shards(): arrived.append(lax.ppermute(summed, 'tm', across(peer + 1)))  3.68 us
    ppermute x3, starting transfers between devices, shards(): result = result + lax.ppermute(shares[step], 'space', pairing)  3.55 us
    ppermute x3, starting transfers between devices, shards(): lax.ppermute(parts[peer], 'tm', across(peer))  3.49 us
    ppermute x3, starting transfers between devices, shards(): lax.ppermute(packed[peer], 'tm', across(peer))  3.49 us
  transfers between devices with their start and end apart: 18, of which 6 were waited for; matrix products, arithmetic and copies ran while one was open for 0% of the time, Pallas kernels for 27%

profile of v13, /device:TPU:0, one launch (start us, length us, event | category | flops | bytes accessed | tf_op | source)
XLA Modules:
  0.0 58.8 jit_solution(5678807298327310331)
XLA Ops:
  0.0 3.1 %pack.1 = (f32[13,32,128]{2,1,0:T(8,128)S(1)}, f32[13,32,128]{2,1,0:T(8,128)S(1)}, f32[13,32,128]{2,1,0:T(8,128)S(1)}, f32[13,32,128]{2,1,0:T(8,128)S(1)}, f32[4...) custom-call(f32[32,3,16,128]{3,2,1,0:T(8,128)} %bitcast.18, s32[2,2048]{1,0:T(2,128)} %bitcast.19, ...), custom_call_target="tpu_custom_call" | custom-call | tf_op jit(solution)/shard_map/pack/pallas_call | solution.py:397
  3.1 4.6 %collective-permute-start = (f32[4,6,32,128]{3,2,1,0:T(8,128)S(1)}, f32[4,6,32,128]{3,2,1,0:T(8,128)S(1)}, u32[]{:S(2)}, u32[]{:S(2)}) collective-permute-start(f32[4,6,32,128]{3,2,1,0:T(8,128)S(1)} %get-tuple-element.47), channel_id=1, source_target_pairs={{0,7},{1,2},{2,1},{3,4},{4,3},{5,6},{6,5},{7,0},{8,15},{9,10},{10,... | collective-permute-start | bytes 1179656 | tf_op jit(solution)/shard_map/to_next_plane/ppermute | solution.py:423
  7.7 1.5 %collective-permute-start.1 = (f32[13,32,128]{2,1,0:T(8,128)S(1)}, f32[13,32,128]{2,1,0:T(8,128)S(1)}, u32[]{:S(2)}, u32[]{:S(2)}) collective-permute-start(f32[13,32,128]{2,1,0:T(8,128)S(1)} %get-tuple-element.49), channel_id=1, source_target_pairs={{0,8},{8,0},{16,24},{24,16},{1,9},{9,1},{17,25},{25,17},{2,10},{10... | collective-permute-start | bytes 638984 | tf_op jit(solution)/shard_map/to_columns/ppermute | solution.py:425
  9.2 1.5 %collective-permute-start.2 = (f32[13,32,128]{2,1,0:T(8,128)S(1)}, f32[13,32,128]{2,1,0:T(8,128)S(1)}, u32[]{:S(2)}, u32[]{:S(2)}) collective-permute-start(f32[13,32,128]{2,1,0:T(8,128)S(1)} %get-tuple-element.50), channel_id=1, source_target_pairs={{0,16},{8,24},{16,0},{24,8},{1,17},{9,25},{17,1},{25,9},{2,18},{10... | collective-permute-start | bytes 638984 | tf_op jit(solution)/shard_map/to_columns/ppermute | solution.py:425
  10.7 0.5 collective-permute-start.3
  11.2 4.6 %collective-permute-done.1.refs_1_ = f32[13,32,128]{2,1,0:T(8,128)S(1)} collective-permute-done((f32[13,32,128]{2,1,0:T(8,128)S(1)}, f32[13,32,128]{2,1,0:T(8,128)S(1)}, u32[]{:S(2)}, u32[]{:S(2)}) %collective-permute-start.1) | collective-permute-done | bytes 213024 | tf_op jit(solution)/shard_map/to_columns/ppermute | solution.py:425
  15.8 3.6 %collective-permute-done.2.refs_2_ = f32[13,32,128]{2,1,0:T(8,128)S(1)} collective-permute-done((f32[13,32,128]{2,1,0:T(8,128)S(1)}, f32[13,32,128]{2,1,0:T(8,128)S(1)}, u32[]{:S(2)}, u32[]{:S(2)}) %collective-permute-start.2) | collective-permute-done | bytes 213024 | tf_op jit(solution)/shard_map/to_columns/ppermute | solution.py:425
  19.4 0.1 collective-permute-start.10
  19.5 0.5 collective-permute-start.7
  20.0 0.1 collective-permute-start.8
  20.1 0.4 collective-permute-start.9
  20.5 1.0 %collective-permute-start.4 = (f32[6,32,128]{2,1,0:T(8,128)S(1)}, f32[6,32,128]{2,1,0:T(8,128)S(1)}, u32[]{:S(2)}, u32[]{:S(2)}) collective-permute-start(f32[6,32,128]{2,1,0:T(8,128)S(1)} %get-tuple-element.54), channel_id=1, source_target_pairs={{0,8},{8,0},{16,24},{24,16},{1,9},{9,1},{17,25},{25,17},{2,10},{10... | collective-permute-start | bytes 294920 | tf_op jit(solution)/shard_map/next_to_columns/ppermute | solution.py:430
  21.6 0.9 %collective-permute-start.5 = (f32[6,32,128]{2,1,0:T(8,128)S(1)}, f32[6,32,128]{2,1,0:T(8,128)S(1)}, u32[]{:S(2)}, u32[]{:S(2)}) collective-permute-start(f32[6,32,128]{2,1,0:T(8,128)S(1)} %get-tuple-element.55), channel_id=1, source_target_pairs={{0,16},{8,24},{16,0},{24,8},{1,17},{9,25},{17,1},{25,9},{2,18},{10... | collective-permute-start | bytes 294920 | tf_op jit(solution)/shard_map/next_to_columns/ppermute | solution.py:430
  22.5 1.5 %collective-permute-start.6 = (f32[6,32,128]{2,1,0:T(8,128)S(1)}, f32[6,32,128]{2,1,0:T(8,128)S(1)}, u32[]{:S(2)}, u32[]{:S(2)}) collective-permute-start(f32[6,32,128]{2,1,0:T(8,128)S(1)} %get-tuple-element.56), channel_id=1, source_target_pairs={{0,24},{8,16},{16,8},{24,0},{1,25},{9,17},{17,9},{25,1},{2,26},{10... | collective-permute-start | bytes 294920 | tf_op jit(solution)/shard_map/next_to_columns/ppermute | solution.py:430
  24.0 7.5 %inner_terms.2 = (f32[12,128,128]{2,1,0:T(8,128)S(1)}, f32[3072,128]{1,0:T(8,128)S(1)}, f32[9216,128]{1,0:T(8,128)S(1)}, bf16[3072,256]{1,0:T(8,128)(2,1)S(1)}, ...) custom-call(s32[2048]{0:T(1024)S(1)} %get-tuple-element.45.codes_ref, f32[128,128]{1,0:T(8,128)S(1)} %get-tuple-element.46.coeffs_ref, ...), custom_call_target="tpu_custom_call" | custom-call | flops 12000000000 | bytes 10000000 | tf_op jit(solution)/shard_map/inner_terms/pallas_call | solution.py:438
  31.6 0.1 collective-permute-start.11
  31.7 2.9 %inner_terms.3 = (f32[2,256,128]{2,1,0:T(8,128)S(1)}, f32[6144,128]{1,0:T(8,128)S(1)}) custom-call(s32[2048]{0:T(1024)S(1)} %get-tuple-element.45.codes_ref, f32[3072,128]{1,0:T(8,128)S(1)} %get-tuple-element.73.carry_ref, f32[9216,128]{1,0:T(8,128)S(1)} %get-tuple-element.74.slope_ref, ...), custom_call_target="tpu_custom_call", output_to_operand_aliasing={{1}: (4, {})} | custom-call | flops 8000000000 | bytes 10000000 | tf_op jit(solution)/shard_map/inner_terms/pallas_call | solution.py:458
  34.6 3.3 %edge_terms.4 = (f32[1024,128]{1,0:T(8,128)S(1)}, f32[3072,128]{1,0:T(8,128)S(1)}, bf16[3072,256]{1,0:T(8,128)(2,1)S(1)}, f32[256,128]{1,0:T(8,128)S(1)}, f32[6144,128]{1,0:T(8,128)S(1)}) custom-call(s32[2048]{0:T(1024)S(1)} %get-tuple-element.45.codes_ref, f32[128,128]{1,0:T(8,128)S(1)} %get-tuple-element.46.coeffs_ref, ...), custom_call_target="tpu_custom_call" | custom-call | tf_op jit(solution)/shard_map/edge_terms/pallas_call | solution.py:469
  37.8 1.5 %collective-permute-start.12 = (f32[256,128]{1,0:T(8,128)S(1)}, f32[256,128]{1,0:T(8,128)S(1)}, u32[]{:S(2)}, u32[]{:S(2)}) collective-permute-start(f32[256,128]{1,0:T(8,128)S(1)} %get-tuple-element.78), channel_id=1, source_target_pairs={{0,24},{8,16},{16,8},{24,0},{1,25},{9,17},{17,9},{25,1},{2,26},{10... | collective-permute-start | bytes 393224 | tf_op jit(solution)/shard_map/sum_over_columns/ppermute | solution.py:488
  39.3 1.8 %edge_terms.5 = (f32[256,128]{1,0:T(8,128)S(1)}, f32[6144,128]{1,0:T(8,128)S(1)}) custom-call(s32[2048]{0:T(1024)S(1)} %get-tuple-element.45.codes_ref, f32[1024,128]{1,0:T(8,128)S(1)} %get-tuple-element.70.carry_ref, f32[3072,128]{1,0:T(8,128)S(1)} %get-tuple-element.71.slope_ref, bf16[3072,256]{1,0:T(8,128)(2,1)S(1)} %get-tuple-element.72.rhs_ref, ...), custom_call_target="tpu_custom_call" | custom-call | flops 100000000 | bytes 100000 | tf_op jit(solution)/shard_map/edge_terms/pallas_call | solution.py:497
  41.1 1.2 %collective-permute-start.13 = (f32[256,128]{1,0:T(8,128)S(1)}, f32[256,128]{1,0:T(8,128)S(1)}, u32[]{:S(2)}, u32[]{:S(2)}) collective-permute-start(f32[256,128]{1,0:T(8,128)S(1)} %get-tuple-element.81), channel_id=1, source_target_pairs={{0,16},{8,24},{16,0},{24,8},{1,17},{9,25},{17,1},{25,9},{2,18},{10... | collective-permute-start | bytes 393224 | tf_op jit(solution)/shard_map/sum_over_columns/ppermute | solution.py:488
  42.3 1.1 %edge_terms.6 = f32[256,128]{1,0:T(8,128)S(1)} custom-call(bf16[3072,256]{1,0:T(8,128)(2,1)S(1)} %get-tuple-element.72.rhs_ref, f32[2,256,128]{2,1,0:T(8,128)S(1)} %get-tuple-element.84.inner_ref, f32[6144,128]{1,0:T(8,128)S(1)} %get-tuple-element.83.picked_ref), custom_call_target="tpu_custom_call" | custom-call | flops 100000000 | bytes 100000 | tf_op jit(solution)/shard_map/edge_terms/pallas_call | solution.py:507
  43.3 1.0 %collective-permute-start.14 = (f32[256,128]{1,0:T(8,128)S(1)}, f32[256,128]{1,0:T(8,128)S(1)}, u32[]{:S(2)}, u32[]{:S(2)}) collective-permute-start(f32[256,128]{1,0:T(8,128)S(1)} %edge_terms.6), channel_id=1, source_target_pairs={{0,8},{8,0},{16,24},{24,16},{1,9},{9,1},{17,25},{25,17},{2,10},{10... | collective-permute-start | bytes 393224 | tf_op jit(solution)/shard_map/sum_over_columns/ppermute | solution.py:488
  44.4 3.1 %collective-permute-done.13.refs_1_ = f32[256,128]{1,0:T(8,128)S(1)} collective-permute-done((f32[256,128]{1,0:T(8,128)S(1)}, f32[256,128]{1,0:T(8,128)S(1)}, u32[]{:S(2)}, u32[]{:S(2)}) %collective-permute-start.13) | collective-permute-done | bytes 131104 | tf_op jit(solution)/shard_map/sum_over_columns/ppermute | solution.py:488
  47.5 2.4 %edge_terms.7 = f32[256,128]{1,0:T(8,128)S(1)} custom-call(s32[2048]{0:T(1024)S(1)} %get-tuple-element.45.codes_ref, f32[1024,128]{1,0:T(8,128)S(1)} %get-tuple-element.70.carry_ref, f32[3072,128]{1,0:T(8,128)S(1)} %get-tuple-element.71.slope_ref, bf16[3072,256]{1,0:T(8,128)(2,1)S(1)} %get-tuple-element.72.rhs_ref, ...), custom_call_target="tpu_custom_call" | custom-call | flops 100000000 | bytes 100000 | tf_op jit(solution)/shard_map/edge_terms/pallas_call | solution.py:516
  50.0 0.9 %collective-permute-start.15 = (f32[64,128]{1,0:T(8,128)S(1)}, f32[64,128]{1,0:T(8,128)S(1)}, u32[]{:S(2)}, u32[]{:S(2)}) collective-permute-start(f32[64,128]{1,0:T(8,128)S(1)} %get-tuple-element.89), channel_id=1, source_target_pairs={{0,2},{1,3},{2,0},{3,1},{4,6},{5,7},{6,4},{7,5},{8,10},{9,11},{10,... | collective-permute-start | bytes 98312 | tf_op jit(solution)/shard_map/sum_over_chips/ppermute | solution.py:533
  50.9 2.5 %collective-permute-start.17 = (f32[64,128]{1,0:T(8,128)S(1)}, f32[64,128]{1,0:T(8,128)S(1)}, u32[]{:S(2)}, u32[]{:S(2)}) collective-permute-start(f32[64,128]{1,0:T(8,128)S(1)} %get-tuple-element.90), channel_id=1, source_target_pairs={{0,6},{1,7},{2,4},{3,5},{4,2},{5,3},{6,0},{7,1},{8,14},{9,15},{10,... | collective-permute-start | bytes 98312 | tf_op jit(solution)/shard_map/sum_over_chips/ppermute | solution.py:533
  53.4 0.2 collective-permute-start.16
  53.6 0.4 collective-permute-done.15
  54.0 2.7 %collective-permute-done.17 = f32[64,128]{1,0:T(8,128)S(1)} collective-permute-done((f32[64,128]{1,0:T(8,128)S(1)}, f32[64,128]{1,0:T(8,128)S(1)}, u32[]{:S(2)}, u32[]{:S(2)}) %collective-permute-start.17) | collective-permute-done | bytes 32800 | tf_op jit(solution)/shard_map/sum_over_chips/ppermute | solution.py:533
  56.6 1.6 %collective-permute-done.16 = f32[64,128]{1,0:T(8,128)S(1)} collective-permute-done((f32[64,128]{1,0:T(8,128)S(1)}, f32[64,128]{1,0:T(8,128)S(1)}, u32[]{:S(2)}, u32[]{:S(2)}) %collective-permute-start.16) | collective-permute-done | bytes 32800 | tf_op jit(solution)/shard_map/sum_over_chips/ppermute | solution.py:533
  58.2 0.6 %fusion.2 = f32[64,128]{1,0:T(8,128)} fusion(f32[64,128]{1,0:T(8,128)S(1)} %collective-permute-done.17, f32[64,128]{1,0:T(8,128)S(1)} %collective-permute-done.16, f32[64,128]{1,0:T(8,128)S(1)} %collective-permute-done.15, f32[256,128]{1,0:T(8,128)S(1)} %add.12), kind=kLoop, calls=%fused_computation.8 | loop fusion | flops 32768 | bytes 163840 | tf_op jit(solution)/shard_map/sum_over_chips/mul | solution.py:534
  (16 shorter events, 0.1 us)
Async XLA Ops:
  3.1 16.2 %collective-permute-start = (f32[4,6,32,128]{3,2,1,0:T(8,128)S(1)}, f32[4,6,32,128]{3,2,1,0:T(8,128)S(1)}, u32[]{:S(2)}, u32[]{:S(2)}) collective-permute-start(f32[4,6,32,128]{3,2,1,0:T(8,128)S(1)} %get-tuple-element.47), channel_id=1, source_target_pairs={{0,7},{1,2},{2,1},{3,4},{4,3},{5,6},{6,5},{7,0},{8,15},{9,10},{10,... | collective-permute-start | bytes 1179656 | tf_op jit(solution)/shard_map/to_next_plane/ppermute | solution.py:423
  7.7 8.1 %collective-permute-start.1 = (f32[13,32,128]{2,1,0:T(8,128)S(1)}, f32[13,32,128]{2,1,0:T(8,128)S(1)}, u32[]{:S(2)}, u32[]{:S(2)}) collective-permute-start(f32[13,32,128]{2,1,0:T(8,128)S(1)} %get-tuple-element.49), channel_id=1, source_target_pairs={{0,8},{8,0},{16,24},{24,16},{1,9},{9,1},{17,25},{25,17},{2,10},{10... | collective-permute-start | bytes 638984 | tf_op jit(solution)/shard_map/to_columns/ppermute | solution.py:425
  9.2 10.2 %collective-permute-start.2 = (f32[13,32,128]{2,1,0:T(8,128)S(1)}, f32[13,32,128]{2,1,0:T(8,128)S(1)}, u32[]{:S(2)}, u32[]{:S(2)}) collective-permute-start(f32[13,32,128]{2,1,0:T(8,128)S(1)} %get-tuple-element.50), channel_id=1, source_target_pairs={{0,16},{8,24},{16,0},{24,8},{1,17},{9,25},{17,1},{25,9},{2,18},{10... | collective-permute-start | bytes 638984 | tf_op jit(solution)/shard_map/to_columns/ppermute | solution.py:425
  10.7 8.7 %collective-permute-start.3 = (f32[13,32,128]{2,1,0:T(8,128)S(1)}, f32[13,32,128]{2,1,0:T(8,128)S(1)}, u32[]{:S(2)}, u32[]{:S(2)}) collective-permute-start(f32[13,32,128]{2,1,0:T(8,128)S(1)} %get-tuple-element.52), channel_id=1, source_target_pairs={{0,24},{8,16},{16,8},{24,0},{1,25},{9,17},{17,9},{25,1},{2,26},{10... | collective-permute-start | bytes 638984 | tf_op jit(solution)/shard_map/to_columns/ppermute | solution.py:425
  19.4 2.1 %collective-permute-start.10 = (f32[13,32,128]{2,1,0:T(8,128)S(1)}, f32[13,32,128]{2,1,0:T(8,128)S(1)}, u32[]{:S(2)}, u32[]{:S(2)}) collective-permute-start(f32[13,32,128]{2,1,0:T(8,128)S(1)} %collective-permute-done.3.refs_3_), channel_id=1, source_target_pairs={{0,1},{1,0},{2,3},{3,2},{4,5},{5,4},{6,7},{7,6},{8,9},{9,8},{10,11... | collective-permute-start | bytes 638984 | tf_op jit(solution)/shard_map/to_other_core/ppermute | solution.py:432
  19.5 3.0 %collective-permute-start.7 = (f32[13,32,128]{2,1,0:T(8,128)S(1)}, f32[13,32,128]{2,1,0:T(8,128)S(1)}, u32[]{:S(2)}, u32[]{:S(2)}) collective-permute-start(f32[13,32,128]{2,1,0:T(8,128)S(1)} %get-tuple-element.57.refs_0_), channel_id=1, source_target_pairs={{0,1},{1,0},{2,3},{3,2},{4,5},{5,4},{6,7},{7,6},{8,9},{9,8},{10,11... | collective-permute-start | bytes 638984 | tf_op jit(solution)/shard_map/to_other_core/ppermute | solution.py:432
  20.0 4.0 %collective-permute-start.8 = (f32[13,32,128]{2,1,0:T(8,128)S(1)}, f32[13,32,128]{2,1,0:T(8,128)S(1)}, u32[]{:S(2)}, u32[]{:S(2)}) collective-permute-start(f32[13,32,128]{2,1,0:T(8,128)S(1)} %collective-permute-done.1.refs_1_), channel_id=1, source_target_pairs={{0,1},{1,0},{2,3},{3,2},{4,5},{5,4},{6,7},{7,6},{8,9},{9,8},{10,11... | collective-permute-start | bytes 638984 | tf_op jit(solution)/shard_map/to_other_core/ppermute | solution.py:432
  20.1 3.9 %collective-permute-start.9 = (f32[13,32,128]{2,1,0:T(8,128)S(1)}, f32[13,32,128]{2,1,0:T(8,128)S(1)}, u32[]{:S(2)}, u32[]{:S(2)}) collective-permute-start(f32[13,32,128]{2,1,0:T(8,128)S(1)} %collective-permute-done.2.refs_2_), channel_id=1, source_target_pairs={{0,1},{1,0},{2,3},{3,2},{4,5},{5,4},{6,7},{7,6},{8,9},{9,8},{10,11... | collective-permute-start | bytes 638984 | tf_op jit(solution)/shard_map/to_other_core/ppermute | solution.py:432
  20.5 11.0 %collective-permute-start.4 = (f32[6,32,128]{2,1,0:T(8,128)S(1)}, f32[6,32,128]{2,1,0:T(8,128)S(1)}, u32[]{:S(2)}, u32[]{:S(2)}) collective-permute-start(f32[6,32,128]{2,1,0:T(8,128)S(1)} %get-tuple-element.54), channel_id=1, source_target_pairs={{0,8},{8,0},{16,24},{24,16},{1,9},{9,1},{17,25},{25,17},{2,10},{10... | collective-permute-start | bytes 294920 | tf_op jit(solution)/shard_map/next_to_columns/ppermute | solution.py:430
  21.6 10.0 %collective-permute-start.5 = (f32[6,32,128]{2,1,0:T(8,128)S(1)}, f32[6,32,128]{2,1,0:T(8,128)S(1)}, u32[]{:S(2)}, u32[]{:S(2)}) collective-permute-start(f32[6,32,128]{2,1,0:T(8,128)S(1)} %get-tuple-element.55), channel_id=1, source_target_pairs={{0,16},{8,24},{16,0},{24,8},{1,17},{9,25},{17,1},{25,9},{2,18},{10... | collective-permute-start | bytes 294920 | tf_op jit(solution)/shard_map/next_to_columns/ppermute | solution.py:430
  22.5 9.1 %collective-permute-start.6 = (f32[6,32,128]{2,1,0:T(8,128)S(1)}, f32[6,32,128]{2,1,0:T(8,128)S(1)}, u32[]{:S(2)}, u32[]{:S(2)}) collective-permute-start(f32[6,32,128]{2,1,0:T(8,128)S(1)} %get-tuple-element.56), channel_id=1, source_target_pairs={{0,24},{8,16},{16,8},{24,0},{1,25},{9,17},{17,9},{25,1},{2,26},{10... | collective-permute-start | bytes 294920 | tf_op jit(solution)/shard_map/next_to_columns/ppermute | solution.py:430
  31.6 3.0 %collective-permute-start.11 = (f32[4,6,32,128]{3,2,1,0:T(8,128)S(1)}, f32[4,6,32,128]{3,2,1,0:T(8,128)S(1)}, u32[]{:S(2)}, u32[]{:S(2)}) collective-permute-start(f32[4,6,32,128]{3,2,1,0:T(8,128)S(1)} %pad_maximum_fusion), channel_id=1, source_target_pairs={{0,1},{1,0},{2,3},{3,2},{4,5},{5,4},{6,7},{7,6},{8,9},{9,8},{10,11... | collective-permute-start | bytes 1179656 | tf_op jit(solution)/shard_map/next_to_other_core/ppermute | solution.py:456
  37.8 9.7 %collective-permute-start.12 = (f32[256,128]{1,0:T(8,128)S(1)}, f32[256,128]{1,0:T(8,128)S(1)}, u32[]{:S(2)}, u32[]{:S(2)}) collective-permute-start(f32[256,128]{1,0:T(8,128)S(1)} %get-tuple-element.78), channel_id=1, source_target_pairs={{0,24},{8,16},{16,8},{24,0},{1,25},{9,17},{17,9},{25,1},{2,26},{10... | collective-permute-start | bytes 393224 | tf_op jit(solution)/shard_map/sum_over_columns/ppermute | solution.py:488
  41.1 6.4 %collective-permute-start.13 = (f32[256,128]{1,0:T(8,128)S(1)}, f32[256,128]{1,0:T(8,128)S(1)}, u32[]{:S(2)}, u32[]{:S(2)}) collective-permute-start(f32[256,128]{1,0:T(8,128)S(1)} %get-tuple-element.81), channel_id=1, source_target_pairs={{0,16},{8,24},{16,0},{24,8},{1,17},{9,25},{17,1},{25,9},{2,18},{10... | collective-permute-start | bytes 393224 | tf_op jit(solution)/shard_map/sum_over_columns/ppermute | solution.py:488
  43.3 6.6 %collective-permute-start.14 = (f32[256,128]{1,0:T(8,128)S(1)}, f32[256,128]{1,0:T(8,128)S(1)}, u32[]{:S(2)}, u32[]{:S(2)}) collective-permute-start(f32[256,128]{1,0:T(8,128)S(1)} %edge_terms.6), channel_id=1, source_target_pairs={{0,8},{8,0},{16,24},{24,16},{1,9},{9,1},{17,25},{25,17},{2,10},{10... | collective-permute-start | bytes 393224 | tf_op jit(solution)/shard_map/sum_over_columns/ppermute | solution.py:488
  50.0 4.0 %collective-permute-start.15 = (f32[64,128]{1,0:T(8,128)S(1)}, f32[64,128]{1,0:T(8,128)S(1)}, u32[]{:S(2)}, u32[]{:S(2)}) collective-permute-start(f32[64,128]{1,0:T(8,128)S(1)} %get-tuple-element.89), channel_id=1, source_target_pairs={{0,2},{1,3},{2,0},{3,1},{4,6},{5,7},{6,4},{7,5},{8,10},{9,11},{10,... | collective-permute-start | bytes 98312 | tf_op jit(solution)/shard_map/sum_over_chips/ppermute | solution.py:533
  50.9 5.7 %collective-permute-start.17 = (f32[64,128]{1,0:T(8,128)S(1)}, f32[64,128]{1,0:T(8,128)S(1)}, u32[]{:S(2)}, u32[]{:S(2)}) collective-permute-start(f32[64,128]{1,0:T(8,128)S(1)} %get-tuple-element.90), channel_id=1, source_target_pairs={{0,6},{1,7},{2,4},{3,5},{4,2},{5,3},{6,0},{7,1},{8,14},{9,15},{10,... | collective-permute-start | bytes 98312 | tf_op jit(solution)/shard_map/sum_over_chips/ppermute | solution.py:533
  53.4 4.8 %collective-permute-start.16 = (f32[64,128]{1,0:T(8,128)S(1)}, f32[64,128]{1,0:T(8,128)S(1)}, u32[]{:S(2)}, u32[]{:S(2)}) collective-permute-start(f32[64,128]{1,0:T(8,128)S(1)} %get-tuple-element.91), channel_id=1, source_target_pairs={{0,4},{1,5},{2,6},{3,7},{4,0},{5,1},{6,2},{7,3},{8,12},{9,13},{10,... | collective-permute-start | bytes 98312 | tf_op jit(solution)/shard_map/sum_over_chips/ppermute | solution.py:533

commit v14 on v13

--- a/solution.py
+++ b/solution.py
@@ -22,13 +22,16 @@
     return high, low
 
 
-def border_lane(rows_y, lanes, c):
+def border_layout(rows_y, lanes, width):
+    per_run = (width + 1) // rows_y
+    if per_run:
+        run = width + 1 + per_run * rows_y
+        firsts = [c // per_run * run + c % per_run * rows_y for c in range(3)]
+        if firsts[2] + width + 1 + rows_y <= lanes:
+            return [(0, first) for first in firsts], width + 1, 1
     per_slab = lanes // (2 * rows_y)
-    return c // per_slab, c % per_slab * 2 * rows_y
-
-
-def border_slabs(rows_y, lanes):
-    return border_lane(rows_y, lanes, 2)[0] + 1
+    places = [(c // per_slab, c % per_slab * 2 * rows_y) for c in range(3)]
+    return places, rows_y, places[2][0] + 1
 
 
 def exchange_blocks(rows, lane, width, lanes):
@@ -58,9 +61,9 @@
     t, _, core = place_of_device()
     width, groups = lanes // tm_count, rows_y // tm_count
     lane = lax.broadcasted_iota(jnp.int32, (local_s, lanes), 1)
-    borders = [[jnp.zeros((local_s, lanes), F32) for _ in range(tm_count)] for _ in range(border_slabs(rows_y, lanes))]
-    for c in range(3):
-        slab, first_lane = border_lane(rows_y, lanes, c)
+    places, offset, border_slabs = border_layout(rows_y, lanes, width)
+    borders = [[jnp.zeros((local_s, lanes), F32) for _ in range(tm_count)] for _ in range(border_slabs)]
+    for c, (slab, first_lane) in enumerate(places):
         copies[c].wait()
 
         def one_group(g, border, c=c, first_lane=first_lane):
@@ -70,13 +73,17 @@
                 y = q * groups + g
                 row = rows_ref[pl.ds(c * local_s * rows_y + y, local_s, stride=rows_y), :]
                 rows.append(row)
-                for side in range(2):
-                    shift = first_lane + side * (rows_y - width - 1) + y
-                    moved = pltpu.roll(row, jnp.bitwise_and(shift, lanes - 1), 1)
-                    for block in range(tm_count):
-                        column = (block + 1) * width if side else block * width - 1
-                        is_here = lane == jnp.bitwise_and(shift + column, lanes - 1)
-                        border[block] = jnp.where(is_here, moved, border[block])
+                before = first_lane + y
+                after = before + offset - (width + 1)
+                moved = pltpu.roll(row, jnp.bitwise_and(before, lanes - 1), 1)
+                moved_after = moved if offset == width + 1 else pltpu.roll(row, jnp.bitwise_and(after, lanes - 1), 1)
+                for block in range(tm_count):
+                    at_before = lane == jnp.bitwise_and(before + block * width - 1, lanes - 1)
+                    at_after = lane == jnp.bitwise_and(after + (block + 1) * width, lanes - 1)
+                    if moved is moved_after:
+                        border[block] = jnp.where(jnp.logical_or(at_before, at_after), moved, border[block])
+                    else:
+                        border[block] = jnp.where(at_before, moved, jnp.where(at_after, moved_after, border[block]))
             for block, main in enumerate(exchange_blocks(rows, lane, width, lanes)):
                 sorted_ref[block, g * 3 + c] = main
             return tuple(border)
@@ -148,7 +155,7 @@
             one_pair(ahead * share + q, lax.shift_right_logical(code, bits), jnp.bitwise_and(code, 2**bits - 1))
             return 0
 
-        return lax.fori_loop(0, share, one, 0, unroll=32)
+        return lax.fori_loop(0, share, one, 0, unroll=True)
 
     lax.fori_loop(0, chips, one_share, 0)
 
@@ -187,15 +194,15 @@
     lane = lax.broadcasted_iota(jnp.int32, (1, lanes), 1)
     part, column = lax.div(lane, width), lax.rem(lane, width)
     has_border = jnp.where(column == 0, -0.5, jnp.where(column == width - 1, 0.5, 0.0))
-    border_of = jnp.where(column == 0, 0, rows_y) + t * width - 1 + part * block_rows
+    places, offset, _ = border_layout(rows_y, lanes, width)
+    border_of = jnp.where(column == 0, 0, offset) + t * width - 1 + part * block_rows
     border_lanes = lax.broadcasted_iota(jnp.int32, (2 * lanes, lanes), 0)
     border_lanes = jnp.where(border_lanes >= lanes, border_lanes - lanes, border_lanes)
     borders = []
     for slab in range(3 * block_rows, slabs):
         both = jnp.concatenate([slab_ref[0, slab], slab_ref[1, slab]], axis=0)
         borders.append(jnp.concatenate(split_high_low(both), axis=1))
-    for c in range(3):
-        slab, first_lane = border_lane(rows_y, lanes, c)
+    for c, (slab, first_lane) in enumerate(places):
         for row in range(block_rows):
             center = row * 3 + c
             if row % 2 == 0:
@@ -233,15 +240,16 @@
 
     codes.wait()
 
-    pick_inner(held_codes_ref, carry_ref, slope_ref, conv_ref, first_peer, (chips, share, bits))
-
     def one_peer(number, _):
-        out_ref[number] = project(conv_ref, rhs_ref, chips * share, 3 * height, lanes)
-        following = lax.rem(first_peer + number + 1, tm_count)
+        @pl.when(number > 0)
+        def _():
+            out_ref[number - 1] = project(conv_ref, rhs_ref, chips * share, 3 * height, lanes)
+
+        following = lax.rem(first_peer + number, tm_count)
         pick_inner(held_codes_ref, carry_ref, slope_ref, conv_ref, following, (chips, share, bits))
         return 0
 
-    lax.fori_loop(0, out_ref.shape[0], one_peer, 0)
+    lax.fori_loop(0, out_ref.shape[0] + 1, one_peer, 0)
 
 
 def pick_inner(codes_ref, carry_ref, slope_ref, conv_ref, peer, sizes):
@@ -350,15 +358,9 @@
     pick_edge(held_codes_ref, carry_ref, slope_ref, conv_ref, peer - 1, sizes)
 
 
-def picked_edge_kernel(rhs_ref, inner_ref, picked_ref, out_ref, *, peer):
-    out_ref[...] = edge_sum(picked_ref, rhs_ref, inner_ref, peer)
-
-
-def own_edge_kernel(codes_ref, carry_ref, slope_ref, rhs_ref, inner_ref, *refs, sizes):
-    *arrived_refs, out_ref, conv_ref, held_codes_ref, sem = refs
-    copy_of_codes(codes_ref, held_codes_ref, sem).wait()
-    pick_edge(held_codes_ref, carry_ref, slope_ref, conv_ref, 0, sizes)
-    total = edge_sum(conv_ref, rhs_ref, inner_ref, 0)
+def own_edge_kernel(rhs_ref, inner_ref, picked_ref, *refs):
+    *arrived_refs, out_ref = refs
+    total = edge_sum(picked_ref, rhs_ref, inner_ref, 0)
     for arrived_ref in arrived_refs:
         total = total + arrived_ref[...]
     out_ref[...] = total
@@ -378,7 +380,7 @@
     local_s, _, _, rows_y, lanes = snapshots.shape
     modes = coeffs.shape[1]
     block_rows = rows_y // tm_count
-    slabs = 3 * block_rows + border_slabs(rows_y, lanes)
+    slabs = 3 * block_rows + border_layout(rows_y, lanes, lanes // tm_count)[2]
     share = pair_table.shape[0] // (tm_count * space_count)
     factor = float(space_count * rows_y * lanes) ** (-0.5)
     bits = modes.bit_length() - 1
@@ -493,7 +495,7 @@
         with jax.named_scope("edge_terms"):
             inner_sums = early_sums if peer >= early else late_sums
             edge_cost = pl.CostEstimate(flops=10**8, bytes_accessed=10**5, transcendentals=0)
-            if peer > 1:
+            if peer:
                 summed, next_picked = pl.pallas_call(
                     functools.partial(edge_kernel, peer=peer, sizes=(chips, share, bits)),
                     out_shape=[pltpu.VMEM((block, modes), F32), picked],
@@ -503,25 +505,15 @@
                     compiler_params=vmem_limit(16),
                     cost_estimate=edge_cost,
                 )(codes, *[in_vmem(table) for table in (*tables, inner_sums, next_picked)])
-            elif peer:
+            else:
                 summed = pl.pallas_call(
-                    functools.partial(picked_edge_kernel, peer=peer),
+                    own_edge_kernel,
                     out_shape=pltpu.VMEM((block, modes), F32),
-                    in_specs=[vmem] * 3,
+                    in_specs=[vmem] * (3 + taken),
                     out_specs=vmem,
                     compiler_params=vmem_limit(16),
                     cost_estimate=edge_cost,
-                )(*[in_vmem(table) for table in (tables[2], inner_sums, next_picked)])
-            else:
-                summed = pl.pallas_call(
-                    functools.partial(own_edge_kernel, sizes=(chips, share, bits)),
-                    out_shape=pltpu.VMEM((block, modes), F32),
-                    in_specs=[vmem] * (5 + taken),
-                    out_specs=vmem,
-                    scratch_shapes=[picked] + held_codes,
-                    compiler_params=vmem_limit(16),
-                    cost_estimate=edge_cost,
-                )(codes, *[in_vmem(table) for table in (*tables, inner_sums, *arrived[:taken])])
+                )(*[in_vmem(table) for table in (tables[2], inner_sums, next_picked, *arrived[:taken])])
     with jax.named_scope("sum_over_columns"):
         for part in arrived[taken:]:
             summed = summed + part

time: 59 us -> 57.7 us (0.978)
  Pallas kernels: 22.1 us -> 20.8 us
    pallas_call x2 -> x1, Pallas kernels: 3.49 us -> 1.07 us  [shards(): pl.pallas_call(own_edge_kernel, out_shape=pltpu.VMEM((block, modes), F32)...]
    pallas_call x1 -> x2, Pallas kernels: 1.77 us -> 3.33 us  [shards(): pl.pallas_call(functools.partial(edge_kernel, peer=peer, sizes=(chips, sh...]
  transfers between devices with their start and end apart: 18 -> 18, of which waited for: 6 -> 7; matrix products, arithmetic and copies ran while one was open for 0% -> 0% of each run, Pallas kernels for 27% -> 25%
where the time goes in v14:
time: 57.7 us; the launch traced here: 57.6 us
  Pallas kernels  20.8 us (36%)
  starting transfers between devices  19.9 us (34%)
  waiting for transfers between devices  16 us (28%)
  other arithmetic  0.67 us (1%)
    ppermute x3, waiting for transfers between devices, shards(): lax.ppermute(packed[peer], 'tm', across(peer))  8.18 us
    pallas_call x1, Pallas kernels, shards(): pl.pallas_call(functools.partial(inner_kernel, first_peer=early, sizes=(l...  7.46 us
    ppermute x1, starting transfers between devices, shards(): across_edge = lax.ppermute(packed[tm_count], 'space', ring)  4.55 us
    ppermute x3, waiting for transfers between devices, shards(): result = result + lax.ppermute(shares[step], 'space', pairing)  4.49 us
    ppermute x3, starting transfers between devices, shards(): arrived.append(lax.ppermute(summed, 'tm', across(peer + 1)))  3.68 us
    ppermute x3, starting transfers between devices, shards(): result = result + lax.ppermute(shares[step], 'space', pairing)  3.55 us
    ppermute x3, starting transfers between devices, shards(): lax.ppermute(parts[peer], 'tm', across(peer))  3.49 us
    ppermute x3, starting transfers between devices, shards(): lax.ppermute(packed[peer], 'tm', across(peer))  3.49 us
  transfers between devices with their start and end apart: 18, of which 7 were waited for; matrix products, arithmetic and copies ran while one was open for 0% of the time, Pallas kernels for 25%

profile of v14, /device:TPU:0, one launch (start us, length us, event | category | flops | bytes accessed | tf_op | source)
XLA Modules:
  0.0 57.6 jit_solution(9466058903565532101)
XLA Ops:
  0.0 3.1 %pack.1 = (f32[13,32,128]{2,1,0:T(8,128)S(1)}, f32[13,32,128]{2,1,0:T(8,128)S(1)}, f32[13,32,128]{2,1,0:T(8,128)S(1)}, f32[13,32,128]{2,1,0:T(8,128)S(1)}, f32[4...) custom-call(f32[32,3,16,128]{3,2,1,0:T(8,128)} %bitcast.18, s32[2,2048]{1,0:T(2,128)} %bitcast.19, ...), custom_call_target="tpu_custom_call" | custom-call | tf_op jit(solution)/shard_map/pack/pallas_call | solution.py:399
  3.2 4.6 %collective-permute-start = (f32[4,6,32,128]{3,2,1,0:T(8,128)S(1)}, f32[4,6,32,128]{3,2,1,0:T(8,128)S(1)}, u32[]{:S(2)}, u32[]{:S(2)}) collective-permute-start(f32[4,6,32,128]{3,2,1,0:T(8,128)S(1)} %get-tuple-element.49), channel_id=1, source_target_pairs={{0,7},{1,2},{2,1},{3,4},{4,3},{5,6},{6,5},{7,0},{8,15},{9,10},{10,... | collective-permute-start | bytes 1179656 | tf_op jit(solution)/shard_map/to_next_plane/ppermute | solution.py:425
  7.7 1.5 %collective-permute-start.1 = (f32[13,32,128]{2,1,0:T(8,128)S(1)}, f32[13,32,128]{2,1,0:T(8,128)S(1)}, u32[]{:S(2)}, u32[]{:S(2)}) collective-permute-start(f32[13,32,128]{2,1,0:T(8,128)S(1)} %get-tuple-element.51), channel_id=1, source_target_pairs={{0,8},{8,0},{16,24},{24,16},{1,9},{9,1},{17,25},{25,17},{2,10},{10... | collective-permute-start | bytes 638984 | tf_op jit(solution)/shard_map/to_columns/ppermute | solution.py:427
  9.2 1.5 %collective-permute-start.2 = (f32[13,32,128]{2,1,0:T(8,128)S(1)}, f32[13,32,128]{2,1,0:T(8,128)S(1)}, u32[]{:S(2)}, u32[]{:S(2)}) collective-permute-start(f32[13,32,128]{2,1,0:T(8,128)S(1)} %get-tuple-element.52), channel_id=1, source_target_pairs={{0,16},{8,24},{16,0},{24,8},{1,17},{9,25},{17,1},{25,9},{2,18},{10... | collective-permute-start | bytes 638984 | tf_op jit(solution)/shard_map/to_columns/ppermute | solution.py:427
  10.7 0.5 collective-permute-start.3
  11.2 4.6 %collective-permute-done.1.refs_1_ = f32[13,32,128]{2,1,0:T(8,128)S(1)} collective-permute-done((f32[13,32,128]{2,1,0:T(8,128)S(1)}, f32[13,32,128]{2,1,0:T(8,128)S(1)}, u32[]{:S(2)}, u32[]{:S(2)}) %collective-permute-start.1) | collective-permute-done | bytes 213024 | tf_op jit(solution)/shard_map/to_columns/ppermute | solution.py:427
  15.8 3.6 %collective-permute-done.2.refs_2_ = f32[13,32,128]{2,1,0:T(8,128)S(1)} collective-permute-done((f32[13,32,128]{2,1,0:T(8,128)S(1)}, f32[13,32,128]{2,1,0:T(8,128)S(1)}, u32[]{:S(2)}, u32[]{:S(2)}) %collective-permute-start.2) | collective-permute-done | bytes 213024 | tf_op jit(solution)/shard_map/to_columns/ppermute | solution.py:427
  19.5 0.5 collective-permute-start.7
  20.0 0.1 collective-permute-start.8
  20.1 0.4 collective-permute-start.9
  20.5 1.0 %collective-permute-start.4 = (f32[6,32,128]{2,1,0:T(8,128)S(1)}, f32[6,32,128]{2,1,0:T(8,128)S(1)}, u32[]{:S(2)}, u32[]{:S(2)}) collective-permute-start(f32[6,32,128]{2,1,0:T(8,128)S(1)} %get-tuple-element.56), channel_id=1, source_target_pairs={{0,8},{8,0},{16,24},{24,16},{1,9},{9,1},{17,25},{25,17},{2,10},{10... | collective-permute-start | bytes 294920 | tf_op jit(solution)/shard_map/next_to_columns/ppermute | solution.py:432
  21.6 0.9 %collective-permute-start.5 = (f32[6,32,128]{2,1,0:T(8,128)S(1)}, f32[6,32,128]{2,1,0:T(8,128)S(1)}, u32[]{:S(2)}, u32[]{:S(2)}) collective-permute-start(f32[6,32,128]{2,1,0:T(8,128)S(1)} %get-tuple-element.57), channel_id=1, source_target_pairs={{0,16},{8,24},{16,0},{24,8},{1,17},{9,25},{17,1},{25,9},{2,18},{10... | collective-permute-start | bytes 294920 | tf_op jit(solution)/shard_map/next_to_columns/ppermute | solution.py:432
  22.5 1.5 %collective-permute-start.6 = (f32[6,32,128]{2,1,0:T(8,128)S(1)}, f32[6,32,128]{2,1,0:T(8,128)S(1)}, u32[]{:S(2)}, u32[]{:S(2)}) collective-permute-start(f32[6,32,128]{2,1,0:T(8,128)S(1)} %get-tuple-element.58), channel_id=1, source_target_pairs={{0,24},{8,16},{16,8},{24,0},{1,25},{9,17},{17,9},{25,1},{2,26},{10... | collective-permute-start | bytes 294920 | tf_op jit(solution)/shard_map/next_to_columns/ppermute | solution.py:432
  24.0 7.5 %inner_terms.2 = (f32[12,128,128]{2,1,0:T(8,128)S(1)}, f32[3072,128]{1,0:T(8,128)S(1)}, f32[9216,128]{1,0:T(8,128)S(1)}, bf16[3072,256]{1,0:T(8,128)(2,1)S(1)}, ...) custom-call(s32[2048]{0:T(1024)S(1)} %get-tuple-element.47.codes_ref, f32[128,128]{1,0:T(8,128)S(1)} %get-tuple-element.48.coeffs_ref, ...), custom_call_target="tpu_custom_call" | custom-call | flops 12000000000 | bytes 10000000 | tf_op jit(solution)/shard_map/inner_terms/pallas_call | solution.py:440
  31.6 0.1 collective-permute-start.11
  31.6 2.8 %inner_terms.3 = (f32[2,256,128]{2,1,0:T(8,128)S(1)}, f32[6144,128]{1,0:T(8,128)S(1)}) custom-call(s32[2048]{0:T(1024)S(1)} %get-tuple-element.47.codes_ref, f32[3072,128]{1,0:T(8,128)S(1)} %get-tuple-element.73.carry_ref, f32[9216,128]{1,0:T(8,128)S(1)} %get-tuple-element.74.slope_ref, ...), custom_call_target="tpu_custom_call", output_to_operand_aliasing={{1}: (4, {})} | custom-call | flops 8000000000 | bytes 10000000 | tf_op jit(solution)/shard_map/inner_terms/pallas_call | solution.py:460
  34.4 3.0 %edge_terms.4 = (f32[1024,128]{1,0:T(8,128)S(1)}, f32[3072,128]{1,0:T(8,128)S(1)}, bf16[3072,256]{1,0:T(8,128)(2,1)S(1)}, f32[256,128]{1,0:T(8,128)S(1)}, f32[6144,128]{1,0:T(8,128)S(1)}) custom-call(s32[2048]{0:T(1024)S(1)} %get-tuple-element.47.codes_ref, f32[128,128]{1,0:T(8,128)S(1)} %get-tuple-element.48.coeffs_ref, ...), custom_call_target="tpu_custom_call" | custom-call | tf_op jit(solution)/shard_map/edge_terms/pallas_call | solution.py:471
  37.5 1.5 %collective-permute-start.12 = (f32[256,128]{1,0:T(8,128)S(1)}, f32[256,128]{1,0:T(8,128)S(1)}, u32[]{:S(2)}, u32[]{:S(2)}) collective-permute-start(f32[256,128]{1,0:T(8,128)S(1)} %get-tuple-element.80), channel_id=1, source_target_pairs={{0,24},{8,16},{16,8},{24,0},{1,25},{9,17},{17,9},{25,1},{2,26},{10... | collective-permute-start | bytes 393224 | tf_op jit(solution)/shard_map/sum_over_columns/ppermute | solution.py:490
  38.9 1.7 %edge_terms.5 = (f32[256,128]{1,0:T(8,128)S(1)}, f32[6144,128]{1,0:T(8,128)S(1)}) custom-call(s32[2048]{0:T(1024)S(1)} %get-tuple-element.47.codes_ref, f32[1024,128]{1,0:T(8,128)S(1)} %get-tuple-element.78.carry_ref, f32[3072,128]{1,0:T(8,128)S(1)} %get-tuple-element.79.slope_ref, bf16[3072,256]{1,0:T(8,128)(2,1)S(1)} %get-tuple-element.72.rhs_ref, ...), custom_call_target="tpu_custom_call" | custom-call | flops 100000000 | bytes 100000 | tf_op jit(solution)/shard_map/edge_terms/pallas_call | solution.py:499
  40.6 1.2 %collective-permute-start.13 = (f32[256,128]{1,0:T(8,128)S(1)}, f32[256,128]{1,0:T(8,128)S(1)}, u32[]{:S(2)}, u32[]{:S(2)}) collective-permute-start(f32[256,128]{1,0:T(8,128)S(1)} %get-tuple-element.83), channel_id=1, source_target_pairs={{0,16},{8,24},{16,0},{24,8},{1,17},{9,25},{17,1},{25,9},{2,18},{10... | collective-permute-start | bytes 393224 | tf_op jit(solution)/shard_map/sum_over_columns/ppermute | solution.py:490
  41.8 1.7 %edge_terms.6 = (f32[256,128]{1,0:T(8,128)S(1)}, f32[6144,128]{1,0:T(8,128)S(1)}) custom-call(s32[2048]{0:T(1024)S(1)} %get-tuple-element.47.codes_ref, f32[1024,128]{1,0:T(8,128)S(1)} %get-tuple-element.78.carry_ref, f32[3072,128]{1,0:T(8,128)S(1)} %get-tuple-element.79.slope_ref, bf16[3072,256]{1,0:T(8,128)(2,1)S(1)} %get-tuple-element.72.rhs_ref, ...), custom_call_target="tpu_custom_call" | custom-call | flops 100000000 | bytes 100000 | tf_op jit(solution)/shard_map/edge_terms/pallas_call | solution.py:499
  43.5 1.1 %collective-permute-start.14 = (f32[256,128]{1,0:T(8,128)S(1)}, f32[256,128]{1,0:T(8,128)S(1)}, u32[]{:S(2)}, u32[]{:S(2)}) collective-permute-start(f32[256,128]{1,0:T(8,128)S(1)} %get-tuple-element.86), channel_id=1, source_target_pairs={{0,8},{8,0},{16,24},{24,16},{1,9},{9,1},{17,25},{25,17},{2,10},{10... | collective-permute-start | bytes 393224 | tf_op jit(solution)/shard_map/sum_over_columns/ppermute | solution.py:490
  44.5 2.6 %collective-permute-done.13.refs_1_ = f32[256,128]{1,0:T(8,128)S(1)} collective-permute-done((f32[256,128]{1,0:T(8,128)S(1)}, f32[256,128]{1,0:T(8,128)S(1)}, u32[]{:S(2)}, u32[]{:S(2)}) %collective-permute-start.13) | collective-permute-done | bytes 131104 | tf_op jit(solution)/shard_map/sum_over_columns/ppermute | solution.py:490
  47.1 1.1 %edge_terms.7 = f32[256,128]{1,0:T(8,128)S(1)} custom-call(bf16[3072,256]{1,0:T(8,128)(2,1)S(1)} %get-tuple-element.72.rhs_ref, f32[2,256,128]{2,1,0:T(8,128)S(1)} %get-tuple-element.87.inner_ref, f32[6144,128]{1,0:T(8,128)S(1)} %get-tuple-element.88.picked_ref, f32[256,128]{1,0:T(8,128)S(1)} %collective-permute-done.12.refs_0_, ...), custom_call_target="tpu_custom_call" | custom-call | flops 100000000 | bytes 100000 | tf_op jit(solution)/shard_map/edge_terms/pallas_call | solution.py:509
  48.2 0.6 %collective-permute-done.14 = f32[256,128]{1,0:T(8,128)S(1)} collective-permute-done((f32[256,128]{1,0:T(8,128)S(1)}, f32[256,128]{1,0:T(8,128)S(1)}, u32[]{:S(2)}, u32[]{:S(2)}) %collective-permute-start.14) | collective-permute-done | bytes 131104 | tf_op jit(solution)/shard_map/sum_over_columns/ppermute | solution.py:490
  48.9 0.4 collective-permute-start.15
  49.3 2.5 %collective-permute-start.17 = (f32[64,128]{1,0:T(8,128)S(1)}, f32[64,128]{1,0:T(8,128)S(1)}, u32[]{:S(2)}, u32[]{:S(2)}) collective-permute-start(f32[64,128]{1,0:T(8,128)S(1)} %get-tuple-element.94), channel_id=1, source_target_pairs={{0,6},{1,7},{2,4},{3,5},{4,2},{5,3},{6,0},{7,1},{8,14},{9,15},{10,... | collective-permute-start | bytes 98312 | tf_op jit(solution)/shard_map/sum_over_chips/ppermute | solution.py:525
  51.8 0.7 %collective-permute-start.16 = (f32[64,128]{1,0:T(8,128)S(1)}, f32[64,128]{1,0:T(8,128)S(1)}, u32[]{:S(2)}, u32[]{:S(2)}) collective-permute-start(f32[64,128]{1,0:T(8,128)S(1)} %get-tuple-element.95), channel_id=1, source_target_pairs={{0,4},{1,5},{2,6},{3,7},{4,0},{5,1},{6,2},{7,3},{8,12},{9,13},{10,... | collective-permute-start | bytes 98312 | tf_op jit(solution)/shard_map/sum_over_chips/ppermute | solution.py:525
  52.4 0.4 collective-permute-done.15
  52.9 2.1 %collective-permute-done.17 = f32[64,128]{1,0:T(8,128)S(1)} collective-permute-done((f32[64,128]{1,0:T(8,128)S(1)}, f32[64,128]{1,0:T(8,128)S(1)}, u32[]{:S(2)}, u32[]{:S(2)}) %collective-permute-start.17) | collective-permute-done | bytes 32800 | tf_op jit(solution)/shard_map/sum_over_chips/ppermute | solution.py:525
  55.0 1.9 %collective-permute-done.16 = f32[64,128]{1,0:T(8,128)S(1)} collective-permute-done((f32[64,128]{1,0:T(8,128)S(1)}, f32[64,128]{1,0:T(8,128)S(1)}, u32[]{:S(2)}, u32[]{:S(2)}) %collective-permute-start.16) | collective-permute-done | bytes 32800 | tf_op jit(solution)/shard_map/sum_over_chips/ppermute | solution.py:525
  56.9 0.6 %fusion.2 = f32[64,128]{1,0:T(8,128)} fusion(f32[64,128]{1,0:T(8,128)S(1)} %collective-permute-done.17, f32[64,128]{1,0:T(8,128)S(1)} %collective-permute-done.16, f32[64,128]{1,0:T(8,128)S(1)} %collective-permute-done.15, f32[256,128]{1,0:T(8,128)S(1)} %add.12), kind=kLoop, calls=%fused_computation.8 | loop fusion | flops 32768 | bytes 163840 | tf_op jit(solution)/shard_map/sum_over_chips/mul | solution.py:526
  (16 shorter events, 0.2 us)
Async XLA Ops:
  3.2 16.2 %collective-permute-start = (f32[4,6,32,128]{3,2,1,0:T(8,128)S(1)}, f32[4,6,32,128]{3,2,1,0:T(8,128)S(1)}, u32[]{:S(2)}, u32[]{:S(2)}) collective-permute-start(f32[4,6,32,128]{3,2,1,0:T(8,128)S(1)} %get-tuple-element.49), channel_id=1, source_target_pairs={{0,7},{1,2},{2,1},{3,4},{4,3},{5,6},{6,5},{7,0},{8,15},{9,10},{10,... | collective-permute-start | bytes 1179656 | tf_op jit(solution)/shard_map/to_next_plane/ppermute | solution.py:425
  7.7 8.1 %collective-permute-start.1 = (f32[13,32,128]{2,1,0:T(8,128)S(1)}, f32[13,32,128]{2,1,0:T(8,128)S(1)}, u32[]{:S(2)}, u32[]{:S(2)}) collective-permute-start(f32[13,32,128]{2,1,0:T(8,128)S(1)} %get-tuple-element.51), channel_id=1, source_target_pairs={{0,8},{8,0},{16,24},{24,16},{1,9},{9,1},{17,25},{25,17},{2,10},{10... | collective-permute-start | bytes 638984 | tf_op jit(solution)/shard_map/to_columns/ppermute | solution.py:427
  9.2 10.2 %collective-permute-start.2 = (f32[13,32,128]{2,1,0:T(8,128)S(1)}, f32[13,32,128]{2,1,0:T(8,128)S(1)}, u32[]{:S(2)}, u32[]{:S(2)}) collective-permute-start(f32[13,32,128]{2,1,0:T(8,128)S(1)} %get-tuple-element.52), channel_id=1, source_target_pairs={{0,16},{8,24},{16,0},{24,8},{1,17},{9,25},{17,1},{25,9},{2,18},{10... | collective-permute-start | bytes 638984 | tf_op jit(solution)/shard_map/to_columns/ppermute | solution.py:427
  10.7 8.7 %collective-permute-start.3 = (f32[13,32,128]{2,1,0:T(8,128)S(1)}, f32[13,32,128]{2,1,0:T(8,128)S(1)}, u32[]{:S(2)}, u32[]{:S(2)}) collective-permute-start(f32[13,32,128]{2,1,0:T(8,128)S(1)} %get-tuple-element.54), channel_id=1, source_target_pairs={{0,24},{8,16},{16,8},{24,0},{1,25},{9,17},{17,9},{25,1},{2,26},{10... | collective-permute-start | bytes 638984 | tf_op jit(solution)/shard_map/to_columns/ppermute | solution.py:427
  19.4 2.1 %collective-permute-start.10 = (f32[13,32,128]{2,1,0:T(8,128)S(1)}, f32[13,32,128]{2,1,0:T(8,128)S(1)}, u32[]{:S(2)}, u32[]{:S(2)}) collective-permute-start(f32[13,32,128]{2,1,0:T(8,128)S(1)} %collective-permute-done.3.refs_3_), channel_id=1, source_target_pairs={{0,1},{1,0},{2,3},{3,2},{4,5},{5,4},{6,7},{7,6},{8,9},{9,8},{10,11... | collective-permute-start | bytes 638984 | tf_op jit(solution)/shard_map/to_other_core/ppermute | solution.py:434
  19.5 3.0 %collective-permute-start.7 = (f32[13,32,128]{2,1,0:T(8,128)S(1)}, f32[13,32,128]{2,1,0:T(8,128)S(1)}, u32[]{:S(2)}, u32[]{:S(2)}) collective-permute-start(f32[13,32,128]{2,1,0:T(8,128)S(1)} %get-tuple-element.59.refs_0_), channel_id=1, source_target_pairs={{0,1},{1,0},{2,3},{3,2},{4,5},{5,4},{6,7},{7,6},{8,9},{9,8},{10,11... | collective-permute-start | bytes 638984 | tf_op jit(solution)/shard_map/to_other_core/ppermute | solution.py:434
  20.0 4.0 %collective-permute-start.8 = (f32[13,32,128]{2,1,0:T(8,128)S(1)}, f32[13,32,128]{2,1,0:T(8,128)S(1)}, u32[]{:S(2)}, u32[]{:S(2)}) collective-permute-start(f32[13,32,128]{2,1,0:T(8,128)S(1)} %collective-permute-done.1.refs_1_), channel_id=1, source_target_pairs={{0,1},{1,0},{2,3},{3,2},{4,5},{5,4},{6,7},{7,6},{8,9},{9,8},{10,11... | collective-permute-start | bytes 638984 | tf_op jit(solution)/shard_map/to_other_core/ppermute | solution.py:434
  20.1 3.9 %collective-permute-start.9 = (f32[13,32,128]{2,1,0:T(8,128)S(1)}, f32[13,32,128]{2,1,0:T(8,128)S(1)}, u32[]{:S(2)}, u32[]{:S(2)}) collective-permute-start(f32[13,32,128]{2,1,0:T(8,128)S(1)} %collective-permute-done.2.refs_2_), channel_id=1, source_target_pairs={{0,1},{1,0},{2,3},{3,2},{4,5},{5,4},{6,7},{7,6},{8,9},{9,8},{10,11... | collective-permute-start | bytes 638984 | tf_op jit(solution)/shard_map/to_other_core/ppermute | solution.py:434
  20.5 11.0 %collective-permute-start.4 = (f32[6,32,128]{2,1,0:T(8,128)S(1)}, f32[6,32,128]{2,1,0:T(8,128)S(1)}, u32[]{:S(2)}, u32[]{:S(2)}) collective-permute-start(f32[6,32,128]{2,1,0:T(8,128)S(1)} %get-tuple-element.56), channel_id=1, source_target_pairs={{0,8},{8,0},{16,24},{24,16},{1,9},{9,1},{17,25},{25,17},{2,10},{10... | collective-permute-start | bytes 294920 | tf_op jit(solution)/shard_map/next_to_columns/ppermute | solution.py:432
  21.6 9.9 %collective-permute-start.5 = (f32[6,32,128]{2,1,0:T(8,128)S(1)}, f32[6,32,128]{2,1,0:T(8,128)S(1)}, u32[]{:S(2)}, u32[]{:S(2)}) collective-permute-start(f32[6,32,128]{2,1,0:T(8,128)S(1)} %get-tuple-element.57), channel_id=1, source_target_pairs={{0,16},{8,24},{16,0},{24,8},{1,17},{9,25},{17,1},{25,9},{2,18},{10... | collective-permute-start | bytes 294920 | tf_op jit(solution)/shard_map/next_to_columns/ppermute | solution.py:432
  22.5 9.0 %collective-permute-start.6 = (f32[6,32,128]{2,1,0:T(8,128)S(1)}, f32[6,32,128]{2,1,0:T(8,128)S(1)}, u32[]{:S(2)}, u32[]{:S(2)}) collective-permute-start(f32[6,32,128]{2,1,0:T(8,128)S(1)} %get-tuple-element.58), channel_id=1, source_target_pairs={{0,24},{8,16},{16,8},{24,0},{1,25},{9,17},{17,9},{25,1},{2,26},{10... | collective-permute-start | bytes 294920 | tf_op jit(solution)/shard_map/next_to_columns/ppermute | solution.py:432
  31.6 2.9 %collective-permute-start.11 = (f32[4,6,32,128]{3,2,1,0:T(8,128)S(1)}, f32[4,6,32,128]{3,2,1,0:T(8,128)S(1)}, u32[]{:S(2)}, u32[]{:S(2)}) collective-permute-start(f32[4,6,32,128]{3,2,1,0:T(8,128)S(1)} %pad_maximum_fusion), channel_id=1, source_target_pairs={{0,1},{1,0},{2,3},{3,2},{4,5},{5,4},{6,7},{7,6},{8,9},{9,8},{10,11... | collective-permute-start | bytes 1179656 | tf_op jit(solution)/shard_map/next_to_other_core/ppermute | solution.py:458
  37.5 9.7 %collective-permute-start.12 = (f32[256,128]{1,0:T(8,128)S(1)}, f32[256,128]{1,0:T(8,128)S(1)}, u32[]{:S(2)}, u32[]{:S(2)}) collective-permute-start(f32[256,128]{1,0:T(8,128)S(1)} %get-tuple-element.80), channel_id=1, source_target_pairs={{0,24},{8,16},{16,8},{24,0},{1,25},{9,17},{17,9},{25,1},{2,26},{10... | collective-permute-start | bytes 393224 | tf_op jit(solution)/shard_map/sum_over_columns/ppermute | solution.py:490
  40.6 6.5 %collective-permute-start.13 = (f32[256,128]{1,0:T(8,128)S(1)}, f32[256,128]{1,0:T(8,128)S(1)}, u32[]{:S(2)}, u32[]{:S(2)}) collective-permute-start(f32[256,128]{1,0:T(8,128)S(1)} %get-tuple-element.83), channel_id=1, source_target_pairs={{0,16},{8,24},{16,0},{24,8},{1,17},{9,25},{17,1},{25,9},{2,18},{10... | collective-permute-start | bytes 393224 | tf_op jit(solution)/shard_map/sum_over_columns/ppermute | solution.py:490
  43.5 5.4 %collective-permute-start.14 = (f32[256,128]{1,0:T(8,128)S(1)}, f32[256,128]{1,0:T(8,128)S(1)}, u32[]{:S(2)}, u32[]{:S(2)}) collective-permute-start(f32[256,128]{1,0:T(8,128)S(1)} %get-tuple-element.86), channel_id=1, source_target_pairs={{0,8},{8,0},{16,24},{24,16},{1,9},{9,1},{17,25},{25,17},{2,10},{10... | collective-permute-start | bytes 393224 | tf_op jit(solution)/shard_map/sum_over_columns/ppermute | solution.py:490
  48.9 4.0 %collective-permute-start.15 = (f32[64,128]{1,0:T(8,128)S(1)}, f32[64,128]{1,0:T(8,128)S(1)}, u32[]{:S(2)}, u32[]{:S(2)}) collective-permute-start(f32[64,128]{1,0:T(8,128)S(1)} %get-tuple-element.93), channel_id=1, source_target_pairs={{0,2},{1,3},{2,0},{3,1},{4,6},{5,7},{6,4},{7,5},{8,10},{9,11},{10,... | collective-permute-start | bytes 98312 | tf_op jit(solution)/shard_map/sum_over_chips/ppermute | solution.py:525
  49.3 5.7 %collective-permute-start.17 = (f32[64,128]{1,0:T(8,128)S(1)}, f32[64,128]{1,0:T(8,128)S(1)}, u32[]{:S(2)}, u32[]{:S(2)}) collective-permute-start(f32[64,128]{1,0:T(8,128)S(1)} %get-tuple-element.94), channel_id=1, source_target_pairs={{0,6},{1,7},{2,4},{3,5},{4,2},{5,3},{6,0},{7,1},{8,14},{9,15},{10,... | collective-permute-start | bytes 98312 | tf_op jit(solution)/shard_map/sum_over_chips/ppermute | solution.py:525
  51.8 5.2 %collective-permute-start.16 = (f32[64,128]{1,0:T(8,128)S(1)}, f32[64,128]{1,0:T(8,128)S(1)}, u32[]{:S(2)}, u32[]{:S(2)}) collective-permute-start(f32[64,128]{1,0:T(8,128)S(1)} %get-tuple-element.95), channel_id=1, source_target_pairs={{0,4},{1,5},{2,6},{3,7},{4,0},{5,1},{6,2},{7,3},{8,12},{9,13},{10,... | collective-permute-start | bytes 98312 | tf_op jit(solution)/shard_map/sum_over_chips/ppermute | solution.py:525

commit v15 on v14

--- a/solution.py
+++ b/solution.py
@@ -96,7 +96,7 @@
     for peer in range(tm_count):
         block = jnp.bitwise_xor(t, peer)
         out_refs[peer][...] = sorted_ref[block]
-        out_refs[tm_count][peer] = sorted_ref[block, pl.ds(core * half, half)]
+        out_refs[tm_count][peer] = sorted_ref[peer, pl.ds(core * half, half)]
     copies[3].wait()
     copies[4].wait()
     for first in range(0, codes_ref.shape[0], lanes):
@@ -104,16 +104,8 @@
         codes_ref[here] = held_pairs_ref[0, here] * held_coeffs_ref.shape[1] + held_pairs_ref[1, here]
 
 
-def mode_weights(coeffs_ref, local_s, tm_count):
-    t, _, _ = place_of_device()
-    ordered = jnp.concatenate(
-        [
-            coeffs_ref[pl.ds(pl.multiple_of(jnp.bitwise_xor(t, peer) * local_s, 8), local_s), :]
-            for peer in range(tm_count)
-        ],
-        axis=0,
-    )
-    high, low = split_high_low(ordered.T)
+def mode_weights(coeffs):
+    high, low = split_high_low(coeffs.T)
     return jnp.concatenate([high, low, high, low], axis=1)
 
 
@@ -174,7 +166,8 @@
     t, _, core = place_of_device()
     modes, lanes = coeffs_ref.shape[1], own[0].shape[2]
     height = 2 * block_rows
-    weights = mode_weights(coeffs_ref, local_s, tm_count)
+    blocks = [pl.ds(pl.multiple_of(jnp.bitwise_xor(t, peer) * local_s, 8), local_s) for peer in range(tm_count)]
+    weights = mode_weights(jnp.concatenate([coeffs_ref[rows, :] for rows in blocks], axis=0))
 
     def one_slab(index, _):
         own_slab = jnp.concatenate([piece[index] for piece in own], axis=0)
@@ -298,17 +291,17 @@
 
 def far_kernel(codes_ref, coeffs_ref, *refs, peer, sizes):
     local_s, block_rows, tm_count, chips, share, bits = sizes
-    next_own, next_other, near_ref, inner_ref = refs[:tm_count], *refs[tm_count : tm_count + 3]
-    carry_ref, slope_ref, rhs_ref, out_ref, conv_ref, held_codes_ref, sem = refs[tm_count + 3 :]
+    next_own, next_other, near_ref, inner_ref = refs[:4]
+    carry_ref, slope_ref, rhs_ref, out_ref, conv_ref, held_codes_ref, sem = refs[4:]
     codes = copy_of_codes(codes_ref, held_codes_ref, sem)
     _, _, core = place_of_device()
     is_first = core == 0
     modes, lanes = near_ref.shape[1:]
     height = 2 * block_rows
     half = block_rows // 2 * 3
-    weights = mode_weights(coeffs_ref, local_s, tm_count)
+    weights = mode_weights(coeffs_ref[...])
     for slab in range(half):
-        mine = jnp.concatenate([next_own[peer][slab] for peer in range(tm_count)], axis=0)
+        mine = jnp.concatenate([next_own[peer, slab] for peer in range(tm_count)], axis=0)
         theirs = jnp.concatenate([next_other[peer, slab] for peer in range(tm_count)], axis=0)
         after, before = jnp.where(is_first, theirs, mine), jnp.where(is_first, mine, theirs)
         result = modes_of(weights, jnp.concatenate([after, before], axis=1))
@@ -427,9 +420,7 @@
         own = [packed[0]] + [lax.ppermute(packed[peer], "tm", across(peer)) for peer in range(1, tm_count)]
     with jax.named_scope("next_to_columns"):
         across_edge, own[:3] = lax.optimization_barrier((across_edge, own[:3]))
-        parts = [across_edge[peer] for peer in range(tm_count)]
-        parts, own[3:] = lax.optimization_barrier((parts, own[3:]))
-        next_own = [parts[0]] + [lax.ppermute(parts[peer], "tm", across(peer)) for peer in range(1, tm_count)]
+        next_own = lax.all_to_all(across_edge, "tm", 0, 0, tiled=True)
     with jax.named_scope("to_other_core"):
         other = [lax.ppermute(piece, "space", swap) for piece in own]
     early = tm_count // 2
@@ -455,7 +446,7 @@
         )(codes, coeffs, *[in_vmem(piece) for piece in (*own, *other)])
     with jax.named_scope("next_to_other_core"):
         next_own, inner_tables = lax.optimization_barrier((next_own, inner_tables))
-        next_other = lax.ppermute(jnp.stack(next_own), "space", swap)
+        next_other = lax.ppermute(next_own, "space", swap)
     with jax.named_scope("inner_terms"):
         late_sums, _ = pl.pallas_call(
             functools.partial(rest_kernel, sizes=(chips, share, bits)),
@@ -479,11 +470,11 @@
                 pltpu.VMEM((block, modes), F32),
                 picked,
             ],
-            in_specs=[vmem] * (tm_count + 5),
+            in_specs=[vmem] * 6,
             out_specs=[vmem] * 5,
             scratch_shapes=held_codes,
             compiler_params=vmem_limit(16),
-        )(codes, coeffs, *[in_vmem(piece) for piece in (*next_own, next_other, near, early_sums)])
+        )(codes, coeffs, *[in_vmem(piece) for piece in (next_own, next_other, near, early_sums)])
     arrived, taken = [], 2
     for peer in reversed(range(tm_count - 1)):
         with jax.named_scope("sum_over_columns"):

time: 57.7 us -> 71.6 us (1.24)
  local copies, waits for them, and re-layouts: 0.04 us -> 13.2 us
    unnamed x0 -> x16, local copies, waits for them, and re-layouts: none -> 13.2 us
    all_to_all x0 -> x1, starting transfers between devices: none -> 3.55 us  [shards(): next_own = lax.all_to_all(across_edge, 'tm', 0, 0, tiled=True)]
    ppermute x4 -> x1, starting transfers between devices: 3.56 us -> 0.35 us  [shards(): next_other = lax.ppermute(next_own, 'space', swap)]
  transfers between devices with their start and end apart: 18 -> 16, of which waited for: 7 -> 7; matrix products, arithmetic and copies ran while one was open for 0% -> 0% of each run, Pallas kernels for 25% -> 21%
where the time goes in v15:
time: 71.6 us; the launch traced here: 71.3 us
  Pallas kernels  20.9 us (29%)
  starting transfers between devices  19.8 us (28%)
  waiting for transfers between devices  16.6 us (23%)
  local copies, waits for them, and re-layouts  13.2 us (18%)
    unnamed x16, local copies, waits for them, and re-layouts  13.2 us
    ppermute x3, waiting for transfers between devices, shards(): lax.ppermute(packed[peer], 'tm', across(peer))  7.87 us
    pallas_call x1, Pallas kernels, shards(): pl.pallas_call(functools.partial(inner_kernel, first_peer=early, sizes=(l...  7.48 us
    ppermute x3, waiting for transfers between devices, shards(): result = result + lax.ppermute(shares[step], 'space', pairing)  4.81 us
    ppermute x1, starting transfers between devices, shards(): across_edge = lax.ppermute(packed[tm_count], 'space', ring)  4.55 us
    ppermute x3, waiting for transfers between devices, shards(): arrived.append(lax.ppermute(summed, 'tm', across(peer + 1)))  3.92 us
    ppermute x3, starting transfers between devices, shards(): arrived.append(lax.ppermute(summed, 'tm', across(peer + 1)))  3.68 us
    ppermute x3, starting transfers between devices, shards(): result = result + lax.ppermute(shares[step], 'space', pairing)  3.62 us
  transfers between devices with their start and end apart: 16, of which 7 were waited for; matrix products, arithmetic and copies ran while one was open for 0% of the time, Pallas kernels for 21%

profile of v15, /device:TPU:0, one launch (start us, length us, event | category | flops | bytes accessed | tf_op | source)
XLA Modules:
  0.0 71.3 jit_solution(6565643947163327187)
XLA Ops:
  0.0 3.1 %pack.1 = (f32[13,32,128]{2,1,0:T(8,128)S(1)}, f32[13,32,128]{2,1,0:T(8,128)S(1)}, f32[13,32,128]{2,1,0:T(8,128)S(1)}, f32[13,32,128]{2,1,0:T(8,128)S(1)}, f32[4...) custom-call(f32[32,3,16,128]{3,2,1,0:T(8,128)} %bitcast.2, s32[2,2048]{1,0:T(2,128)} %bitcast.3, ...), custom_call_target="tpu_custom_call" | custom-call | tf_op jit(solution)/shard_map/pack/pallas_call | solution.py:392
  3.2 4.6 %collective-permute-start = (f32[4,6,32,128]{3,2,1,0:T(8,128)S(1)}, f32[4,6,32,128]{3,2,1,0:T(8,128)}, u32[]{:S(2)}, u32[]{:S(2)}) collective-permute-start(f32[4,6,32,128]{3,2,1,0:T(8,128)S(1)} %get-tuple-element.41), channel_id=1, source_target_pairs={{0,7},{1,2},{2,1},{3,4},{4,3},{5,6},{6,5},{7,0},{8,15},{9,10},{10,... | collective-permute-start | bytes 1179656 | tf_op jit(solution)/shard_map/to_next_plane/ppermute | solution.py:418
  7.7 2.4 %collective-permute-start.3 = (f32[13,32,128]{2,1,0:T(8,128)S(1)}, f32[13,32,128]{2,1,0:T(8,128)S(1)}, u32[]{:S(2)}, u32[]{:S(2)}) collective-permute-start(f32[13,32,128]{2,1,0:T(8,128)S(1)} %get-tuple-element.49), channel_id=1, source_target_pairs={{0,24},{8,16},{16,8},{24,0},{1,25},{9,17},{17,9},{25,1},{2,26},{10... | collective-permute-start | bytes 638984 | tf_op jit(solution)/shard_map/to_columns/ppermute | solution.py:420
  10.2 0.5 collective-permute-start.1
  10.7 0.5 collective-permute-start.2
  11.2 5.5 %collective-permute-done.3.refs_3_ = f32[13,32,128]{2,1,0:T(8,128)S(1)} collective-permute-done((f32[13,32,128]{2,1,0:T(8,128)S(1)}, f32[13,32,128]{2,1,0:T(8,128)S(1)}, u32[]{:S(2)}, u32[]{:S(2)}) %collective-permute-start.3) | collective-permute-done | bytes 213024 | tf_op jit(solution)/shard_map/to_columns/ppermute | solution.py:420
  16.7 2.4 %collective-permute-done.1.refs_1_ = f32[13,32,128]{2,1,0:T(8,128)S(1)} collective-permute-done((f32[13,32,128]{2,1,0:T(8,128)S(1)}, f32[13,32,128]{2,1,0:T(8,128)S(1)}, u32[]{:S(2)}, u32[]{:S(2)}) %collective-permute-start.1) | collective-permute-done | bytes 213024 | tf_op jit(solution)/shard_map/to_columns/ppermute | solution.py:420
  19.1 0.5 collective-permute-start.5
  19.7 3.6 %all-to-all-start = ((f32[4,6,32,128]{3,2,1,0:T(8,128)}), f32[4,6,32,128]{3,2,1,0:T(8,128)S(1)}, u32[]{:S(2)}, u32[]{:S(2)}) async-start(f32[4,6,32,128]{3,2,1,0:T(8,128)} %collective-permute-done), calls=%async_computation | async-start | bytes 786432 | tf_op jit(solution)/shard_map/next_to_columns/all_to_all | solution.py:423
  23.2 7.5 %inner_terms.2 = (f32[12,128,128]{2,1,0:T(8,128)S(1)}, f32[3072,128]{1,0:T(8,128)S(1)}, f32[9216,128]{1,0:T(8,128)S(1)}, bf16[3072,256]{1,0:T(8,128)(2,1)S(1)}, ...) custom-call(s32[2048]{0:T(1024)S(1)} %get-tuple-element.39.codes_ref, f32[128,128]{1,0:T(8,128)S(1)} %get-tuple-element.40.coeffs_ref, ...), custom_call_target="tpu_custom_call" | custom-call | flops 12000000000 | bytes 10000000 | tf_op jit(solution)/shard_map/inner_terms/pallas_call | solution.py:431
  30.7 2.1 %copy-done = f32[9216,128]{1,0:T(8,128)} copy-done((f32[9216,128]{1,0:T(8,128)}, f32[9216,128]{1,0:T(8,128)S(1)}, u32[]{:S(2)}) %copy-start) | copy-done | bytes 4718616
  32.9 1.7 %copy-done.2 = f32[6144,128]{1,0:T(8,128)} copy-done((f32[6144,128]{1,0:T(8,128)}, f32[6144,128]{1,0:T(8,128)S(1)}, u32[]{:S(2)}) %copy-start.2) | copy-done | bytes 3145752
  34.6 1.2 %copy-done.4 = f32[3072,128]{1,0:T(8,128)} copy-done((f32[3072,128]{1,0:T(8,128)}, f32[3072,128]{1,0:T(8,128)S(1)}, u32[]{:S(2)}) %copy-start.4) | copy-done | bytes 1572888
  35.8 1.1 %copy-done.6 = bf16[3072,256]{1,0:T(8,128)(2,1)} copy-done((bf16[3072,256]{1,0:T(8,128)(2,1)}, bf16[3072,256]{1,0:T(8,128)(2,1)S(1)}, u32[]{:S(2)}) %copy-start.6) | copy-done | bytes 1572888
  37.3 2.3 %copy-done.1 = f32[9216,128]{1,0:T(8,128)S(1)} copy-done((f32[9216,128]{1,0:T(8,128)S(1)}, f32[9216,128]{1,0:T(8,128)}, u32[]{:S(2)}) %copy-start.1) | copy-done | bytes 4718616
  39.6 1.9 %copy-done.3 = f32[6144,128]{1,0:T(8,128)S(1)} copy-done((f32[6144,128]{1,0:T(8,128)S(1)}, f32[6144,128]{1,0:T(8,128)}, u32[]{:S(2)}) %copy-start.3) | copy-done | bytes 3145752
  41.5 1.4 %copy-done.5 = f32[3072,128]{1,0:T(8,128)S(1)} copy-done((f32[3072,128]{1,0:T(8,128)S(1)}, f32[3072,128]{1,0:T(8,128)}, u32[]{:S(2)}) %copy-start.5) | copy-done | bytes 1572888
  42.9 1.4 %copy-done.7 = bf16[3072,256]{1,0:T(8,128)(2,1)S(1)} copy-done((bf16[3072,256]{1,0:T(8,128)(2,1)S(1)}, bf16[3072,256]{1,0:T(8,128)(2,1)}, u32[]{:S(2)}) %copy-start.7) | copy-done | bytes 1572888
  44.3 2.8 %inner_terms.3 = (f32[2,256,128]{2,1,0:T(8,128)S(1)}, f32[6144,128]{1,0:T(8,128)S(1)}) custom-call(s32[2048]{0:T(1024)S(1)} %get-tuple-element.39.codes_ref, f32[3072,128]{1,0:T(8,128)S(1)} %copy-done.5, f32[9216,128]{1,0:T(8,128)S(1)} %copy-done.1, bf16[3072,256]{1,0:T(8,128)(2,1)S(1)} %copy-done.7, ...), custom_call_target="tpu_custom_call", output_to_operand_aliasing={{1}: (4, {})} | custom-call | flops 8000000000 | bytes 10000000 | tf_op jit(solution)/shard_map/inner_terms/pallas_call | solution.py:451
  47.1 3.1 %edge_terms.4 = (f32[1024,128]{1,0:T(8,128)S(1)}, f32[3072,128]{1,0:T(8,128)S(1)}, bf16[3072,256]{1,0:T(8,128)(2,1)S(1)}, f32[256,128]{1,0:T(8,128)S(1)}, f32[6144,128]{1,0:T(8,128)S(1)}) custom-call(s32[2048]{0:T(1024)S(1)} %get-tuple-element.39.codes_ref, f32[128,128]{1,0:T(8,128)S(1)} %get-tuple-element.40.coeffs_ref, ...), custom_call_target="tpu_custom_call" | custom-call | tf_op jit(solution)/shard_map/edge_terms/pallas_call | solution.py:462
  50.2 2.7 %collective-permute-start.9 = (f32[256,128]{1,0:T(8,128)S(1)}, f32[256,128]{1,0:T(8,128)S(1)}, u32[]{:S(2)}, u32[]{:S(2)}) collective-permute-start(f32[256,128]{1,0:T(8,128)S(1)} %get-tuple-element.64), channel_id=1, source_target_pairs={{0,24},{8,16},{16,8},{24,0},{1,25},{9,17},{17,9},{25,1},{2,26},{10... | collective-permute-start | bytes 393224 | tf_op jit(solution)/shard_map/sum_over_columns/ppermute | solution.py:481
  52.9 1.7 %edge_terms.5 = (f32[256,128]{1,0:T(8,128)S(1)}, f32[6144,128]{1,0:T(8,128)S(1)}) custom-call(s32[2048]{0:T(1024)S(1)} %get-tuple-element.39.codes_ref, f32[1024,128]{1,0:T(8,128)S(1)} %get-tuple-element.62.carry_ref, f32[3072,128]{1,0:T(8,128)S(1)} %get-tuple-element.63.slope_ref, bf16[3072,256]{1,0:T(8,128)(2,1)S(1)} %get-tuple-element.56.rhs_ref, ...), custom_call_target="tpu_custom_call" | custom-call | flops 100000000 | bytes 100000 | tf_op jit(solution)/shard_map/edge_terms/pallas_call | solution.py:490
  54.5 0.6 collective-permute-start.10
  55.2 1.7 %edge_terms.6 = (f32[256,128]{1,0:T(8,128)S(1)}, f32[6144,128]{1,0:T(8,128)S(1)}) custom-call(s32[2048]{0:T(1024)S(1)} %get-tuple-element.39.codes_ref, f32[1024,128]{1,0:T(8,128)S(1)} %get-tuple-element.62.carry_ref, f32[3072,128]{1,0:T(8,128)S(1)} %get-tuple-element.63.slope_ref, bf16[3072,256]{1,0:T(8,128)(2,1)S(1)} %get-tuple-element.56.rhs_ref, ...), custom_call_target="tpu_custom_call" | custom-call | flops 100000000 | bytes 100000 | tf_op jit(solution)/shard_map/edge_terms/pallas_call | solution.py:490
  57.2 3.0 %collective-permute-done.10.refs_1_ = f32[256,128]{1,0:T(8,128)S(1)} collective-permute-done((f32[256,128]{1,0:T(8,128)S(1)}, f32[256,128]{1,0:T(8,128)S(1)}, u32[]{:S(2)}, u32[]{:S(2)}) %collective-permute-start.10) | collective-permute-done | bytes 131104 | tf_op jit(solution)/shard_map/sum_over_columns/ppermute | solution.py:481
  60.2 1.1 %edge_terms.7 = f32[256,128]{1,0:T(8,128)S(1)} custom-call(bf16[3072,256]{1,0:T(8,128)(2,1)S(1)} %get-tuple-element.56.rhs_ref, f32[2,256,128]{2,1,0:T(8,128)S(1)} %get-tuple-element.71.inner_ref, f32[6144,128]{1,0:T(8,128)S(1)} %get-tuple-element.72.picked_ref, f32[256,128]{1,0:T(8,128)S(1)} %collective-permute-done.9.refs_0_, ...), custom_call_target="tpu_custom_call" | custom-call | flops 100000000 | bytes 100000 | tf_op jit(solution)/shard_map/edge_terms/pallas_call | solution.py:500
  61.3 0.9 %collective-permute-done.11 = f32[256,128]{1,0:T(8,128)S(1)} collective-permute-done((f32[256,128]{1,0:T(8,128)S(1)}, f32[256,128]{1,0:T(8,128)S(1)}, u32[]{:S(2)}, u32[]{:S(2)}) %collective-permute-start.11) | collective-permute-done | bytes 131104 | tf_op jit(solution)/shard_map/sum_over_columns/ppermute | solution.py:481
  62.3 1.1 %collective-permute-start.12 = (f32[64,128]{1,0:T(8,128)S(1)}, f32[64,128]{1,0:T(8,128)S(1)}, u32[]{:S(2)}, u32[]{:S(2)}) collective-permute-start(f32[64,128]{1,0:T(8,128)S(1)} %get-tuple-element.73), channel_id=1, source_target_pairs={{0,2},{1,3},{2,0},{3,1},{4,6},{5,7},{6,4},{7,5},{8,10},{9,11},{10,... | collective-permute-start | bytes 98312 | tf_op jit(solution)/shard_map/sum_over_chips/ppermute | solution.py:516
  63.4 2.5 %collective-permute-start.14 = (f32[64,128]{1,0:T(8,128)S(1)}, f32[64,128]{1,0:T(8,128)S(1)}, u32[]{:S(2)}, u32[]{:S(2)}) collective-permute-start(f32[64,128]{1,0:T(8,128)S(1)} %get-tuple-element.74), channel_id=1, source_target_pairs={{0,6},{1,7},{2,4},{3,5},{4,2},{5,3},{6,0},{7,1},{8,14},{9,15},{10,... | collective-permute-start | bytes 98312 | tf_op jit(solution)/shard_map/sum_over_chips/ppermute | solution.py:516
  66.2 2.9 %collective-permute-done.14 = f32[64,128]{1,0:T(8,128)S(1)} collective-permute-done((f32[64,128]{1,0:T(8,128)S(1)}, f32[64,128]{1,0:T(8,128)S(1)}, u32[]{:S(2)}, u32[]{:S(2)}) %collective-permute-start.14) | collective-permute-done | bytes 32800 | tf_op jit(solution)/shard_map/sum_over_chips/ppermute | solution.py:516
  69.1 1.6 %collective-permute-done.13 = f32[64,128]{1,0:T(8,128)S(1)} collective-permute-done((f32[64,128]{1,0:T(8,128)S(1)}, f32[64,128]{1,0:T(8,128)S(1)}, u32[]{:S(2)}, u32[]{:S(2)}) %collective-permute-start.13) | collective-permute-done | bytes 32800 | tf_op jit(solution)/shard_map/sum_over_chips/ppermute | solution.py:516
  70.7 0.6 fusion.2
  (26 shorter events, 1.3 us)
Async XLA Ops:
  3.2 15.9 %collective-permute-start = (f32[4,6,32,128]{3,2,1,0:T(8,128)S(1)}, f32[4,6,32,128]{3,2,1,0:T(8,128)}, u32[]{:S(2)}, u32[]{:S(2)}) collective-permute-start(f32[4,6,32,128]{3,2,1,0:T(8,128)S(1)} %get-tuple-element.41), channel_id=1, source_target_pairs={{0,7},{1,2},{2,1},{3,4},{4,3},{5,6},{6,5},{7,0},{8,15},{9,10},{10,... | collective-permute-start | bytes 1179656 | tf_op jit(solution)/shard_map/to_next_plane/ppermute | solution.py:418
  7.7 9.0 %collective-permute-start.3 = (f32[13,32,128]{2,1,0:T(8,128)S(1)}, f32[13,32,128]{2,1,0:T(8,128)S(1)}, u32[]{:S(2)}, u32[]{:S(2)}) collective-permute-start(f32[13,32,128]{2,1,0:T(8,128)S(1)} %get-tuple-element.49), channel_id=1, source_target_pairs={{0,24},{8,16},{16,8},{24,0},{1,25},{9,17},{17,9},{25,1},{2,26},{10... | collective-permute-start | bytes 638984 | tf_op jit(solution)/shard_map/to_columns/ppermute | solution.py:420
  10.2 8.9 %collective-permute-start.1 = (f32[13,32,128]{2,1,0:T(8,128)S(1)}, f32[13,32,128]{2,1,0:T(8,128)S(1)}, u32[]{:S(2)}, u32[]{:S(2)}) collective-permute-start(f32[13,32,128]{2,1,0:T(8,128)S(1)} %get-tuple-element.43), channel_id=1, source_target_pairs={{0,8},{8,0},{16,24},{24,16},{1,9},{9,1},{17,25},{25,17},{2,10},{10... | collective-permute-start | bytes 638984 | tf_op jit(solution)/shard_map/to_columns/ppermute | solution.py:420
  10.7 8.4 %collective-permute-start.2 = (f32[13,32,128]{2,1,0:T(8,128)S(1)}, f32[13,32,128]{2,1,0:T(8,128)S(1)}, u32[]{:S(2)}, u32[]{:S(2)}) collective-permute-start(f32[13,32,128]{2,1,0:T(8,128)S(1)} %get-tuple-element.44), channel_id=1, source_target_pairs={{0,16},{8,24},{16,0},{24,8},{1,17},{9,25},{17,1},{25,9},{2,18},{10... | collective-permute-start | bytes 638984 | tf_op jit(solution)/shard_map/to_columns/ppermute | solution.py:420
  16.7 6.5 %collective-permute-start.7 = (f32[13,32,128]{2,1,0:T(8,128)S(1)}, f32[13,32,128]{2,1,0:T(8,128)S(1)}, u32[]{:S(2)}, u32[]{:S(2)}) collective-permute-start(f32[13,32,128]{2,1,0:T(8,128)S(1)} %collective-permute-done.3.refs_3_), channel_id=1, source_target_pairs={{0,1},{1,0},{2,3},{3,2},{4,5},{5,4},{6,7},{7,6},{8,9},{9,8},{10,11... | collective-permute-start | bytes 638984 | tf_op jit(solution)/shard_map/to_other_core/ppermute | solution.py:425
  19.1 4.1 %collective-permute-start.4 = (f32[13,32,128]{2,1,0:T(8,128)S(1)}, f32[13,32,128]{2,1,0:T(8,128)S(1)}, u32[]{:S(2)}, u32[]{:S(2)}) collective-permute-start(f32[13,32,128]{2,1,0:T(8,128)S(1)} %get-tuple-element.46.refs_0_), channel_id=1, source_target_pairs={{0,1},{1,0},{2,3},{3,2},{4,5},{5,4},{6,7},{7,6},{8,9},{9,8},{10,11... | collective-permute-start | bytes 638984 | tf_op jit(solution)/shard_map/to_other_core/ppermute | solution.py:425
  19.1 4.1 %collective-permute-start.5 = (f32[13,32,128]{2,1,0:T(8,128)S(1)}, f32[13,32,128]{2,1,0:T(8,128)S(1)}, u32[]{:S(2)}, u32[]{:S(2)}) collective-permute-start(f32[13,32,128]{2,1,0:T(8,128)S(1)} %collective-permute-done.1.refs_1_), channel_id=1, source_target_pairs={{0,1},{1,0},{2,3},{3,2},{4,5},{5,4},{6,7},{7,6},{8,9},{9,8},{10,11... | collective-permute-start | bytes 638984 | tf_op jit(solution)/shard_map/to_other_core/ppermute | solution.py:425
  19.6 3.6 %collective-permute-start.6 = (f32[13,32,128]{2,1,0:T(8,128)S(1)}, f32[13,32,128]{2,1,0:T(8,128)S(1)}, u32[]{:S(2)}, u32[]{:S(2)}) collective-permute-start(f32[13,32,128]{2,1,0:T(8,128)S(1)} %collective-permute-done.2.refs_2_), channel_id=1, source_target_pairs={{0,1},{1,0},{2,3},{3,2},{4,5},{5,4},{6,7},{7,6},{8,9},{9,8},{10,11... | collective-permute-start | bytes 638984 | tf_op jit(solution)/shard_map/to_other_core/ppermute | solution.py:425
  19.7 17.3 %all-to-all-start = ((f32[4,6,32,128]{3,2,1,0:T(8,128)}), f32[4,6,32,128]{3,2,1,0:T(8,128)S(1)}, u32[]{:S(2)}, u32[]{:S(2)}) async-start(f32[4,6,32,128]{3,2,1,0:T(8,128)} %collective-permute-done), calls=%async_computation | async-start | bytes 786432 | tf_op jit(solution)/shard_map/next_to_columns/all_to_all | solution.py:423
  30.7 2.2 %copy-start = (f32[9216,128]{1,0:T(8,128)}, f32[9216,128]{1,0:T(8,128)S(1)}, u32[]{:S(2)}) copy-start(f32[9216,128]{1,0:T(8,128)S(1)} %get-tuple-element.58.slope_ref) | copy-start | bytes 14155780
  32.9 1.7 %copy-start.2 = (f32[6144,128]{1,0:T(8,128)}, f32[6144,128]{1,0:T(8,128)S(1)}, u32[]{:S(2)}) copy-start(f32[6144,128]{1,0:T(8,128)S(1)} %get-tuple-element.60.picked_ref) | copy-start | bytes 9437188
  34.6 1.2 %copy-start.4 = (f32[3072,128]{1,0:T(8,128)}, f32[3072,128]{1,0:T(8,128)S(1)}, u32[]{:S(2)}) copy-start(f32[3072,128]{1,0:T(8,128)S(1)} %get-tuple-element.57.carry_ref) | copy-start | bytes 4718596
  35.8 1.1 %copy-start.6 = (bf16[3072,256]{1,0:T(8,128)(2,1)}, bf16[3072,256]{1,0:T(8,128)(2,1)S(1)}, u32[]{:S(2)}) copy-start(bf16[3072,256]{1,0:T(8,128)(2,1)S(1)} %get-tuple-element.59.rhs_ref) | copy-start | bytes 4718596
  36.9 10.2 %collective-permute-start.8 = (f32[4,6,32,128]{3,2,1,0:T(8,128)S(1)}, f32[4,6,32,128]{3,2,1,0:T(8,128)S(1)}, u32[]{:S(2)}, u32[]{:S(2)}) collective-permute-start(f32[4,6,32,128]{3,2,1,0:T(8,128)S(1)} %all-to-all-done.refs_0_), channel_id=1, source_target_pairs={{0,1},{1,0},{2,3},{3,2},{4,5},{5,4},{6,7},{7,6},{8,9},{9,8},{10,11... | collective-permute-start | bytes 1179656 | tf_op jit(solution)/shard_map/next_to_other_core/ppermute | solution.py:449
  37.3 2.3 %copy-start.1 = (f32[9216,128]{1,0:T(8,128)S(1)}, f32[9216,128]{1,0:T(8,128)}, u32[]{:S(2)}) copy-start(f32[9216,128]{1,0:T(8,128)} %copy-done) | copy-start | bytes 14155780
  39.6 1.9 %copy-start.3 = (f32[6144,128]{1,0:T(8,128)S(1)}, f32[6144,128]{1,0:T(8,128)}, u32[]{:S(2)}) copy-start(f32[6144,128]{1,0:T(8,128)} %copy-done.2) | copy-start | bytes 9437188
  41.5 1.4 %copy-start.5 = (f32[3072,128]{1,0:T(8,128)S(1)}, f32[3072,128]{1,0:T(8,128)}, u32[]{:S(2)}) copy-start(f32[3072,128]{1,0:T(8,128)} %copy-done.4) | copy-start | bytes 4718596
  42.9 1.4 %copy-start.7 = (bf16[3072,256]{1,0:T(8,128)(2,1)S(1)}, bf16[3072,256]{1,0:T(8,128)(2,1)}, u32[]{:S(2)}) copy-start(bf16[3072,256]{1,0:T(8,128)(2,1)} %copy-done.6) | copy-start | bytes 4718596
  50.2 10.0 %collective-permute-start.9 = (f32[256,128]{1,0:T(8,128)S(1)}, f32[256,128]{1,0:T(8,128)S(1)}, u32[]{:S(2)}, u32[]{:S(2)}) collective-permute-start(f32[256,128]{1,0:T(8,128)S(1)} %get-tuple-element.64), channel_id=1, source_target_pairs={{0,24},{8,16},{16,8},{24,0},{1,25},{9,17},{17,9},{25,1},{2,26},{10... | collective-permute-start | bytes 393224 | tf_op jit(solution)/shard_map/sum_over_columns/ppermute | solution.py:481
  54.5 5.7 %collective-permute-start.10 = (f32[256,128]{1,0:T(8,128)S(1)}, f32[256,128]{1,0:T(8,128)S(1)}, u32[]{:S(2)}, u32[]{:S(2)}) collective-permute-start(f32[256,128]{1,0:T(8,128)S(1)} %get-tuple-element.67), channel_id=1, source_target_pairs={{0,16},{8,24},{16,0},{24,8},{1,17},{9,25},{17,1},{25,9},{2,18},{10... | collective-permute-start | bytes 393224 | tf_op jit(solution)/shard_map/sum_over_columns/ppermute | solution.py:481
  56.8 5.4 %collective-permute-start.11 = (f32[256,128]{1,0:T(8,128)S(1)}, f32[256,128]{1,0:T(8,128)S(1)}, u32[]{:S(2)}, u32[]{:S(2)}) collective-permute-start(f32[256,128]{1,0:T(8,128)S(1)} %get-tuple-element.70), channel_id=1, source_target_pairs={{0,8},{8,0},{16,24},{24,16},{1,9},{9,1},{17,25},{25,17},{2,10},{10... | collective-permute-start | bytes 393224 | tf_op jit(solution)/shard_map/sum_over_columns/ppermute | solution.py:481
  62.3 4.0 %collective-permute-start.12 = (f32[64,128]{1,0:T(8,128)S(1)}, f32[64,128]{1,0:T(8,128)S(1)}, u32[]{:S(2)}, u32[]{:S(2)}) collective-permute-start(f32[64,128]{1,0:T(8,128)S(1)} %get-tuple-element.73), channel_id=1, source_target_pairs={{0,2},{1,3},{2,0},{3,1},{4,6},{5,7},{6,4},{7,5},{8,10},{9,11},{10,... | collective-permute-start | bytes 98312 | tf_op jit(solution)/shard_map/sum_over_chips/ppermute | solution.py:516
  63.4 5.7 %collective-permute-start.14 = (f32[64,128]{1,0:T(8,128)S(1)}, f32[64,128]{1,0:T(8,128)S(1)}, u32[]{:S(2)}, u32[]{:S(2)}) collective-permute-start(f32[64,128]{1,0:T(8,128)S(1)} %get-tuple-element.74), channel_id=1, source_target_pairs={{0,6},{1,7},{2,4},{3,5},{4,2},{5,3},{6,0},{7,1},{8,14},{9,15},{10,... | collective-permute-start | bytes 98312 | tf_op jit(solution)/shard_map/sum_over_chips/ppermute | solution.py:516
  65.9 4.8 %collective-permute-start.13 = (f32[64,128]{1,0:T(8,128)S(1)}, f32[64,128]{1,0:T(8,128)S(1)}, u32[]{:S(2)}, u32[]{:S(2)}) collective-permute-start(f32[64,128]{1,0:T(8,128)S(1)} %get-tuple-element.75), channel_id=1, source_target_pairs={{0,4},{1,5},{2,6},{3,7},{4,0},{5,1},{6,2},{7,3},{8,12},{9,13},{10,... | collective-permute-start | bytes 98312 | tf_op jit(solution)/shard_map/sum_over_chips/ppermute | solution.py:516

commit v16 on v14

--- a/solution.py
+++ b/solution.py
@@ -88,7 +88,7 @@
                 sorted_ref[block, g * 3 + c] = main
             return tuple(border)
 
-        borders[slab] = lax.fori_loop(0, groups, one_group, tuple(borders[slab]))
+        borders[slab] = lax.fori_loop(0, groups, one_group, tuple(borders[slab]), unroll=True)
     half = groups // 2 * 3
     for slab, border in enumerate(borders):
         for block in range(tm_count):

time: 57.7 us -> 57.1 us (0.990)
  Pallas kernels: 20.8 us -> 20.2 us
    pallas_call x1, Pallas kernels: 3.15 us -> 2.33 us  [shards(): pl.pallas_call(functools.partial(pack_kernel, sizes=(local_s, rows_y, tm_...]
  transfers between devices with their start and end apart: 18 -> 18, of which waited for: 7 -> 7; matrix products, arithmetic and copies ran while one was open for 0% -> 0% of each run, Pallas kernels for 25% -> 26%
where the time goes in v16:
time: 57.1 us; the launch traced here: 56.9 us
  Pallas kernels  20.2 us (35%)
  starting transfers between devices  19.9 us (35%)
  waiting for transfers between devices  16 us (28%)
  other arithmetic  0.67 us (1%)
    ppermute x3, waiting for transfers between devices, shards(): lax.ppermute(packed[peer], 'tm', across(peer))  8.19 us
    pallas_call x1, Pallas kernels, shards(): pl.pallas_call(functools.partial(inner_kernel, first_peer=early, sizes=(l...  7.66 us
    ppermute x1, starting transfers between devices, shards(): across_edge = lax.ppermute(packed[tm_count], 'space', ring)  4.55 us
    ppermute x3, waiting for transfers between devices, shards(): result = result + lax.ppermute(shares[step], 'space', pairing)  4.49 us
    ppermute x3, starting transfers between devices, shards(): arrived.append(lax.ppermute(summed, 'tm', across(peer + 1)))  3.68 us
    ppermute x3, starting transfers between devices, shards(): result = result + lax.ppermute(shares[step], 'space', pairing)  3.55 us
    ppermute x3, starting transfers between devices, shards(): lax.ppermute(parts[peer], 'tm', across(peer))  3.49 us
    ppermute x3, starting transfers between devices, shards(): lax.ppermute(packed[peer], 'tm', across(peer))  3.49 us
  transfers between devices with their start and end apart: 18, of which 7 were waited for; matrix products, arithmetic and copies ran while one was open for 0% of the time, Pallas kernels for 26%

profile of v16, /device:TPU:0, one launch (start us, length us, event | category | flops | bytes accessed | tf_op | source)
XLA Modules:
  0.0 56.9 jit_solution(7789740063880113566)
XLA Ops:
  0.0 2.3 %pack.1 = (f32[13,32,128]{2,1,0:T(8,128)S(1)}, f32[13,32,128]{2,1,0:T(8,128)S(1)}, f32[13,32,128]{2,1,0:T(8,128)S(1)}, f32[13,32,128]{2,1,0:T(8,128)S(1)}, f32[4...) custom-call(f32[32,3,16,128]{3,2,1,0:T(8,128)} %bitcast.18, s32[2,2048]{1,0:T(2,128)} %bitcast.19, ...), custom_call_target="tpu_custom_call" | custom-call | tf_op jit(solution)/shard_map/pack/pallas_call | solution.py:399
  2.3 4.6 %collective-permute-start = (f32[4,6,32,128]{3,2,1,0:T(8,128)S(1)}, f32[4,6,32,128]{3,2,1,0:T(8,128)S(1)}, u32[]{:S(2)}, u32[]{:S(2)}) collective-permute-start(f32[4,6,32,128]{3,2,1,0:T(8,128)S(1)} %get-tuple-element.49), channel_id=1, source_target_pairs={{0,7},{1,2},{2,1},{3,4},{4,3},{5,6},{6,5},{7,0},{8,15},{9,10},{10,... | collective-permute-start | bytes 1179656 | tf_op jit(solution)/shard_map/to_next_plane/ppermute | solution.py:425
  6.9 1.5 %collective-permute-start.1 = (f32[13,32,128]{2,1,0:T(8,128)S(1)}, f32[13,32,128]{2,1,0:T(8,128)S(1)}, u32[]{:S(2)}, u32[]{:S(2)}) collective-permute-start(f32[13,32,128]{2,1,0:T(8,128)S(1)} %get-tuple-element.51), channel_id=1, source_target_pairs={{0,8},{8,0},{16,24},{24,16},{1,9},{9,1},{17,25},{25,17},{2,10},{10... | collective-permute-start | bytes 638984 | tf_op jit(solution)/shard_map/to_columns/ppermute | solution.py:427
  8.4 1.5 %collective-permute-start.2 = (f32[13,32,128]{2,1,0:T(8,128)S(1)}, f32[13,32,128]{2,1,0:T(8,128)S(1)}, u32[]{:S(2)}, u32[]{:S(2)}) collective-permute-start(f32[13,32,128]{2,1,0:T(8,128)S(1)} %get-tuple-element.52), channel_id=1, source_target_pairs={{0,16},{8,24},{16,0},{24,8},{1,17},{9,25},{17,1},{25,9},{2,18},{10... | collective-permute-start | bytes 638984 | tf_op jit(solution)/shard_map/to_columns/ppermute | solution.py:427
  9.9 0.5 collective-permute-start.3
  10.4 4.6 %collective-permute-done.1.refs_1_ = f32[13,32,128]{2,1,0:T(8,128)S(1)} collective-permute-done((f32[13,32,128]{2,1,0:T(8,128)S(1)}, f32[13,32,128]{2,1,0:T(8,128)S(1)}, u32[]{:S(2)}, u32[]{:S(2)}) %collective-permute-start.1) | collective-permute-done | bytes 213024 | tf_op jit(solution)/shard_map/to_columns/ppermute | solution.py:427
  14.9 3.6 %collective-permute-done.2.refs_2_ = f32[13,32,128]{2,1,0:T(8,128)S(1)} collective-permute-done((f32[13,32,128]{2,1,0:T(8,128)S(1)}, f32[13,32,128]{2,1,0:T(8,128)S(1)}, u32[]{:S(2)}, u32[]{:S(2)}) %collective-permute-start.2) | collective-permute-done | bytes 213024 | tf_op jit(solution)/shard_map/to_columns/ppermute | solution.py:427
  18.6 0.1 collective-permute-start.10
  18.7 0.5 collective-permute-start.7
  19.2 0.1 collective-permute-start.8
  19.3 0.4 collective-permute-start.9
  19.7 1.0 %collective-permute-start.4 = (f32[6,32,128]{2,1,0:T(8,128)S(1)}, f32[6,32,128]{2,1,0:T(8,128)S(1)}, u32[]{:S(2)}, u32[]{:S(2)}) collective-permute-start(f32[6,32,128]{2,1,0:T(8,128)S(1)} %get-tuple-element.56), channel_id=1, source_target_pairs={{0,8},{8,0},{16,24},{24,16},{1,9},{9,1},{17,25},{25,17},{2,10},{10... | collective-permute-start | bytes 294920 | tf_op jit(solution)/shard_map/next_to_columns/ppermute | solution.py:432
  20.7 0.9 %collective-permute-start.5 = (f32[6,32,128]{2,1,0:T(8,128)S(1)}, f32[6,32,128]{2,1,0:T(8,128)S(1)}, u32[]{:S(2)}, u32[]{:S(2)}) collective-permute-start(f32[6,32,128]{2,1,0:T(8,128)S(1)} %get-tuple-element.57), channel_id=1, source_target_pairs={{0,16},{8,24},{16,0},{24,8},{1,17},{9,25},{17,1},{25,9},{2,18},{10... | collective-permute-start | bytes 294920 | tf_op jit(solution)/shard_map/next_to_columns/ppermute | solution.py:432
  21.7 1.5 %collective-permute-start.6 = (f32[6,32,128]{2,1,0:T(8,128)S(1)}, f32[6,32,128]{2,1,0:T(8,128)S(1)}, u32[]{:S(2)}, u32[]{:S(2)}) collective-permute-start(f32[6,32,128]{2,1,0:T(8,128)S(1)} %get-tuple-element.58), channel_id=1, source_target_pairs={{0,24},{8,16},{16,8},{24,0},{1,25},{9,17},{17,9},{25,1},{2,26},{10... | collective-permute-start | bytes 294920 | tf_op jit(solution)/shard_map/next_to_columns/ppermute | solution.py:432
  23.2 7.7 %inner_terms.2 = (f32[12,128,128]{2,1,0:T(8,128)S(1)}, f32[3072,128]{1,0:T(8,128)S(1)}, f32[9216,128]{1,0:T(8,128)S(1)}, bf16[3072,256]{1,0:T(8,128)(2,1)S(1)}, ...) custom-call(s32[2048]{0:T(1024)S(1)} %get-tuple-element.47.codes_ref, f32[128,128]{1,0:T(8,128)S(1)} %get-tuple-element.48.coeffs_ref, ...), custom_call_target="tpu_custom_call" | custom-call | flops 12000000000 | bytes 10000000 | tf_op jit(solution)/shard_map/inner_terms/pallas_call | solution.py:440
  31.0 2.8 %inner_terms.3 = (f32[2,256,128]{2,1,0:T(8,128)S(1)}, f32[6144,128]{1,0:T(8,128)S(1)}) custom-call(s32[2048]{0:T(1024)S(1)} %get-tuple-element.47.codes_ref, f32[3072,128]{1,0:T(8,128)S(1)} %get-tuple-element.73.carry_ref, f32[9216,128]{1,0:T(8,128)S(1)} %get-tuple-element.74.slope_ref, ...), custom_call_target="tpu_custom_call", output_to_operand_aliasing={{1}: (4, {})} | custom-call | flops 8000000000 | bytes 10000000 | tf_op jit(solution)/shard_map/inner_terms/pallas_call | solution.py:460
  33.8 3.0 %edge_terms.4 = (f32[1024,128]{1,0:T(8,128)S(1)}, f32[3072,128]{1,0:T(8,128)S(1)}, bf16[3072,256]{1,0:T(8,128)(2,1)S(1)}, f32[256,128]{1,0:T(8,128)S(1)}, f32[6144,128]{1,0:T(8,128)S(1)}) custom-call(s32[2048]{0:T(1024)S(1)} %get-tuple-element.47.codes_ref, f32[128,128]{1,0:T(8,128)S(1)} %get-tuple-element.48.coeffs_ref, ...), custom_call_target="tpu_custom_call" | custom-call | tf_op jit(solution)/shard_map/edge_terms/pallas_call | solution.py:471
  36.9 1.5 %collective-permute-start.12 = (f32[256,128]{1,0:T(8,128)S(1)}, f32[256,128]{1,0:T(8,128)S(1)}, u32[]{:S(2)}, u32[]{:S(2)}) collective-permute-start(f32[256,128]{1,0:T(8,128)S(1)} %get-tuple-element.80), channel_id=1, source_target_pairs={{0,24},{8,16},{16,8},{24,0},{1,25},{9,17},{17,9},{25,1},{2,26},{10... | collective-permute-start | bytes 393224 | tf_op jit(solution)/shard_map/sum_over_columns/ppermute | solution.py:490
  38.3 1.7 %edge_terms.5 = (f32[256,128]{1,0:T(8,128)S(1)}, f32[6144,128]{1,0:T(8,128)S(1)}) custom-call(s32[2048]{0:T(1024)S(1)} %get-tuple-element.47.codes_ref, f32[1024,128]{1,0:T(8,128)S(1)} %get-tuple-element.78.carry_ref, f32[3072,128]{1,0:T(8,128)S(1)} %get-tuple-element.79.slope_ref, bf16[3072,256]{1,0:T(8,128)(2,1)S(1)} %get-tuple-element.72.rhs_ref, ...), custom_call_target="tpu_custom_call" | custom-call | flops 100000000 | bytes 100000 | tf_op jit(solution)/shard_map/edge_terms/pallas_call | solution.py:499
  40.0 1.2 %collective-permute-start.13 = (f32[256,128]{1,0:T(8,128)S(1)}, f32[256,128]{1,0:T(8,128)S(1)}, u32[]{:S(2)}, u32[]{:S(2)}) collective-permute-start(f32[256,128]{1,0:T(8,128)S(1)} %get-tuple-element.83), channel_id=1, source_target_pairs={{0,16},{8,24},{16,0},{24,8},{1,17},{9,25},{17,1},{25,9},{2,18},{10... | collective-permute-start | bytes 393224 | tf_op jit(solution)/shard_map/sum_over_columns/ppermute | solution.py:490
  41.2 1.7 %edge_terms.6 = (f32[256,128]{1,0:T(8,128)S(1)}, f32[6144,128]{1,0:T(8,128)S(1)}) custom-call(s32[2048]{0:T(1024)S(1)} %get-tuple-element.47.codes_ref, f32[1024,128]{1,0:T(8,128)S(1)} %get-tuple-element.78.carry_ref, f32[3072,128]{1,0:T(8,128)S(1)} %get-tuple-element.79.slope_ref, bf16[3072,256]{1,0:T(8,128)(2,1)S(1)} %get-tuple-element.72.rhs_ref, ...), custom_call_target="tpu_custom_call" | custom-call | flops 100000000 | bytes 100000 | tf_op jit(solution)/shard_map/edge_terms/pallas_call | solution.py:499
  42.8 1.1 %collective-permute-start.14 = (f32[256,128]{1,0:T(8,128)S(1)}, f32[256,128]{1,0:T(8,128)S(1)}, u32[]{:S(2)}, u32[]{:S(2)}) collective-permute-start(f32[256,128]{1,0:T(8,128)S(1)} %get-tuple-element.86), channel_id=1, source_target_pairs={{0,8},{8,0},{16,24},{24,16},{1,9},{9,1},{17,25},{25,17},{2,10},{10... | collective-permute-start | bytes 393224 | tf_op jit(solution)/shard_map/sum_over_columns/ppermute | solution.py:490
  43.9 2.6 %collective-permute-done.13.refs_1_ = f32[256,128]{1,0:T(8,128)S(1)} collective-permute-done((f32[256,128]{1,0:T(8,128)S(1)}, f32[256,128]{1,0:T(8,128)S(1)}, u32[]{:S(2)}, u32[]{:S(2)}) %collective-permute-start.13) | collective-permute-done | bytes 131104 | tf_op jit(solution)/shard_map/sum_over_columns/ppermute | solution.py:490
  46.5 1.1 %edge_terms.7 = f32[256,128]{1,0:T(8,128)S(1)} custom-call(bf16[3072,256]{1,0:T(8,128)(2,1)S(1)} %get-tuple-element.72.rhs_ref, f32[2,256,128]{2,1,0:T(8,128)S(1)} %get-tuple-element.87.inner_ref, f32[6144,128]{1,0:T(8,128)S(1)} %get-tuple-element.88.picked_ref, f32[256,128]{1,0:T(8,128)S(1)} %collective-permute-done.12.refs_0_, ...), custom_call_target="tpu_custom_call" | custom-call | flops 100000000 | bytes 100000 | tf_op jit(solution)/shard_map/edge_terms/pallas_call | solution.py:509
  47.6 0.6 %collective-permute-done.14 = f32[256,128]{1,0:T(8,128)S(1)} collective-permute-done((f32[256,128]{1,0:T(8,128)S(1)}, f32[256,128]{1,0:T(8,128)S(1)}, u32[]{:S(2)}, u32[]{:S(2)}) %collective-permute-start.14) | collective-permute-done | bytes 131104 | tf_op jit(solution)/shard_map/sum_over_columns/ppermute | solution.py:490
  48.3 0.4 collective-permute-start.15
  48.7 2.5 %collective-permute-start.17 = (f32[64,128]{1,0:T(8,128)S(1)}, f32[64,128]{1,0:T(8,128)S(1)}, u32[]{:S(2)}, u32[]{:S(2)}) collective-permute-start(f32[64,128]{1,0:T(8,128)S(1)} %get-tuple-element.94), channel_id=1, source_target_pairs={{0,6},{1,7},{2,4},{3,5},{4,2},{5,3},{6,0},{7,1},{8,14},{9,15},{10,... | collective-permute-start | bytes 98312 | tf_op jit(solution)/shard_map/sum_over_chips/ppermute | solution.py:525
  51.1 0.7 %collective-permute-start.16 = (f32[64,128]{1,0:T(8,128)S(1)}, f32[64,128]{1,0:T(8,128)S(1)}, u32[]{:S(2)}, u32[]{:S(2)}) collective-permute-start(f32[64,128]{1,0:T(8,128)S(1)} %get-tuple-element.95), channel_id=1, source_target_pairs={{0,4},{1,5},{2,6},{3,7},{4,0},{5,1},{6,2},{7,3},{8,12},{9,13},{10,... | collective-permute-start | bytes 98312 | tf_op jit(solution)/shard_map/sum_over_chips/ppermute | solution.py:525
  51.8 0.4 collective-permute-done.15
  52.2 2.1 %collective-permute-done.17 = f32[64,128]{1,0:T(8,128)S(1)} collective-permute-done((f32[64,128]{1,0:T(8,128)S(1)}, f32[64,128]{1,0:T(8,128)S(1)}, u32[]{:S(2)}, u32[]{:S(2)}) %collective-permute-start.17) | collective-permute-done | bytes 32800 | tf_op jit(solution)/shard_map/sum_over_chips/ppermute | solution.py:525
  54.4 1.9 %collective-permute-done.16 = f32[64,128]{1,0:T(8,128)S(1)} collective-permute-done((f32[64,128]{1,0:T(8,128)S(1)}, f32[64,128]{1,0:T(8,128)S(1)}, u32[]{:S(2)}, u32[]{:S(2)}) %collective-permute-start.16) | collective-permute-done | bytes 32800 | tf_op jit(solution)/shard_map/sum_over_chips/ppermute | solution.py:525
  56.3 0.6 %fusion.2 = f32[64,128]{1,0:T(8,128)} fusion(f32[64,128]{1,0:T(8,128)S(1)} %collective-permute-done.17, f32[64,128]{1,0:T(8,128)S(1)} %collective-permute-done.16, f32[64,128]{1,0:T(8,128)S(1)} %collective-permute-done.15, f32[256,128]{1,0:T(8,128)S(1)} %add.12), kind=kLoop, calls=%fused_computation.8 | loop fusion | flops 32768 | bytes 163840 | tf_op jit(solution)/shard_map/sum_over_chips/mul | solution.py:526
  (16 shorter events, 0.2 us)
Async XLA Ops:
  2.3 16.2 %collective-permute-start = (f32[4,6,32,128]{3,2,1,0:T(8,128)S(1)}, f32[4,6,32,128]{3,2,1,0:T(8,128)S(1)}, u32[]{:S(2)}, u32[]{:S(2)}) collective-permute-start(f32[4,6,32,128]{3,2,1,0:T(8,128)S(1)} %get-tuple-element.49), channel_id=1, source_target_pairs={{0,7},{1,2},{2,1},{3,4},{4,3},{5,6},{6,5},{7,0},{8,15},{9,10},{10,... | collective-permute-start | bytes 1179656 | tf_op jit(solution)/shard_map/to_next_plane/ppermute | solution.py:425
  6.9 8.0 %collective-permute-start.1 = (f32[13,32,128]{2,1,0:T(8,128)S(1)}, f32[13,32,128]{2,1,0:T(8,128)S(1)}, u32[]{:S(2)}, u32[]{:S(2)}) collective-permute-start(f32[13,32,128]{2,1,0:T(8,128)S(1)} %get-tuple-element.51), channel_id=1, source_target_pairs={{0,8},{8,0},{16,24},{24,16},{1,9},{9,1},{17,25},{25,17},{2,10},{10... | collective-permute-start | bytes 638984 | tf_op jit(solution)/shard_map/to_columns/ppermute | solution.py:427
  8.4 10.2 %collective-permute-start.2 = (f32[13,32,128]{2,1,0:T(8,128)S(1)}, f32[13,32,128]{2,1,0:T(8,128)S(1)}, u32[]{:S(2)}, u32[]{:S(2)}) collective-permute-start(f32[13,32,128]{2,1,0:T(8,128)S(1)} %get-tuple-element.52), channel_id=1, source_target_pairs={{0,16},{8,24},{16,0},{24,8},{1,17},{9,25},{17,1},{25,9},{2,18},{10... | collective-permute-start | bytes 638984 | tf_op jit(solution)/shard_map/to_columns/ppermute | solution.py:427
  9.9 8.7 %collective-permute-start.3 = (f32[13,32,128]{2,1,0:T(8,128)S(1)}, f32[13,32,128]{2,1,0:T(8,128)S(1)}, u32[]{:S(2)}, u32[]{:S(2)}) collective-permute-start(f32[13,32,128]{2,1,0:T(8,128)S(1)} %get-tuple-element.54), channel_id=1, source_target_pairs={{0,24},{8,16},{16,8},{24,0},{1,25},{9,17},{17,9},{25,1},{2,26},{10... | collective-permute-start | bytes 638984 | tf_op jit(solution)/shard_map/to_columns/ppermute | solution.py:427
  18.6 2.1 %collective-permute-start.10 = (f32[13,32,128]{2,1,0:T(8,128)S(1)}, f32[13,32,128]{2,1,0:T(8,128)S(1)}, u32[]{:S(2)}, u32[]{:S(2)}) collective-permute-start(f32[13,32,128]{2,1,0:T(8,128)S(1)} %collective-permute-done.3.refs_3_), channel_id=1, source_target_pairs={{0,1},{1,0},{2,3},{3,2},{4,5},{5,4},{6,7},{7,6},{8,9},{9,8},{10,11... | collective-permute-start | bytes 638984 | tf_op jit(solution)/shard_map/to_other_core/ppermute | solution.py:434
  18.7 3.0 %collective-permute-start.7 = (f32[13,32,128]{2,1,0:T(8,128)S(1)}, f32[13,32,128]{2,1,0:T(8,128)S(1)}, u32[]{:S(2)}, u32[]{:S(2)}) collective-permute-start(f32[13,32,128]{2,1,0:T(8,128)S(1)} %get-tuple-element.59.refs_0_), channel_id=1, source_target_pairs={{0,1},{1,0},{2,3},{3,2},{4,5},{5,4},{6,7},{7,6},{8,9},{9,8},{10,11... | collective-permute-start | bytes 638984 | tf_op jit(solution)/shard_map/to_other_core/ppermute | solution.py:434
  19.2 4.0 %collective-permute-start.8 = (f32[13,32,128]{2,1,0:T(8,128)S(1)}, f32[13,32,128]{2,1,0:T(8,128)S(1)}, u32[]{:S(2)}, u32[]{:S(2)}) collective-permute-start(f32[13,32,128]{2,1,0:T(8,128)S(1)} %collective-permute-done.1.refs_1_), channel_id=1, source_target_pairs={{0,1},{1,0},{2,3},{3,2},{4,5},{5,4},{6,7},{7,6},{8,9},{9,8},{10,11... | collective-permute-start | bytes 638984 | tf_op jit(solution)/shard_map/to_other_core/ppermute | solution.py:434
  19.3 3.9 %collective-permute-start.9 = (f32[13,32,128]{2,1,0:T(8,128)S(1)}, f32[13,32,128]{2,1,0:T(8,128)S(1)}, u32[]{:S(2)}, u32[]{:S(2)}) collective-permute-start(f32[13,32,128]{2,1,0:T(8,128)S(1)} %collective-permute-done.2.refs_2_), channel_id=1, source_target_pairs={{0,1},{1,0},{2,3},{3,2},{4,5},{5,4},{6,7},{7,6},{8,9},{9,8},{10,11... | collective-permute-start | bytes 638984 | tf_op jit(solution)/shard_map/to_other_core/ppermute | solution.py:434
  19.7 11.2 %collective-permute-start.4 = (f32[6,32,128]{2,1,0:T(8,128)S(1)}, f32[6,32,128]{2,1,0:T(8,128)S(1)}, u32[]{:S(2)}, u32[]{:S(2)}) collective-permute-start(f32[6,32,128]{2,1,0:T(8,128)S(1)} %get-tuple-element.56), channel_id=1, source_target_pairs={{0,8},{8,0},{16,24},{24,16},{1,9},{9,1},{17,25},{25,17},{2,10},{10... | collective-permute-start | bytes 294920 | tf_op jit(solution)/shard_map/next_to_columns/ppermute | solution.py:432
  20.7 10.1 %collective-permute-start.5 = (f32[6,32,128]{2,1,0:T(8,128)S(1)}, f32[6,32,128]{2,1,0:T(8,128)S(1)}, u32[]{:S(2)}, u32[]{:S(2)}) collective-permute-start(f32[6,32,128]{2,1,0:T(8,128)S(1)} %get-tuple-element.57), channel_id=1, source_target_pairs={{0,16},{8,24},{16,0},{24,8},{1,17},{9,25},{17,1},{25,9},{2,18},{10... | collective-permute-start | bytes 294920 | tf_op jit(solution)/shard_map/next_to_columns/ppermute | solution.py:432
  21.7 9.2 %collective-permute-start.6 = (f32[6,32,128]{2,1,0:T(8,128)S(1)}, f32[6,32,128]{2,1,0:T(8,128)S(1)}, u32[]{:S(2)}, u32[]{:S(2)}) collective-permute-start(f32[6,32,128]{2,1,0:T(8,128)S(1)} %get-tuple-element.58), channel_id=1, source_target_pairs={{0,24},{8,16},{16,8},{24,0},{1,25},{9,17},{17,9},{25,1},{2,26},{10... | collective-permute-start | bytes 294920 | tf_op jit(solution)/shard_map/next_to_columns/ppermute | solution.py:432
  30.9 2.9 %collective-permute-start.11 = (f32[4,6,32,128]{3,2,1,0:T(8,128)S(1)}, f32[4,6,32,128]{3,2,1,0:T(8,128)S(1)}, u32[]{:S(2)}, u32[]{:S(2)}) collective-permute-start(f32[4,6,32,128]{3,2,1,0:T(8,128)S(1)} %pad_maximum_fusion), channel_id=1, source_target_pairs={{0,1},{1,0},{2,3},{3,2},{4,5},{5,4},{6,7},{7,6},{8,9},{9,8},{10,11... | collective-permute-start | bytes 1179656 | tf_op jit(solution)/shard_map/next_to_other_core/ppermute | solution.py:458
  36.9 9.7 %collective-permute-start.12 = (f32[256,128]{1,0:T(8,128)S(1)}, f32[256,128]{1,0:T(8,128)S(1)}, u32[]{:S(2)}, u32[]{:S(2)}) collective-permute-start(f32[256,128]{1,0:T(8,128)S(1)} %get-tuple-element.80), channel_id=1, source_target_pairs={{0,24},{8,16},{16,8},{24,0},{1,25},{9,17},{17,9},{25,1},{2,26},{10... | collective-permute-start | bytes 393224 | tf_op jit(solution)/shard_map/sum_over_columns/ppermute | solution.py:490
  40.0 6.5 %collective-permute-start.13 = (f32[256,128]{1,0:T(8,128)S(1)}, f32[256,128]{1,0:T(8,128)S(1)}, u32[]{:S(2)}, u32[]{:S(2)}) collective-permute-start(f32[256,128]{1,0:T(8,128)S(1)} %get-tuple-element.83), channel_id=1, source_target_pairs={{0,16},{8,24},{16,0},{24,8},{1,17},{9,25},{17,1},{25,9},{2,18},{10... | collective-permute-start | bytes 393224 | tf_op jit(solution)/shard_map/sum_over_columns/ppermute | solution.py:490
  42.8 5.4 %collective-permute-start.14 = (f32[256,128]{1,0:T(8,128)S(1)}, f32[256,128]{1,0:T(8,128)S(1)}, u32[]{:S(2)}, u32[]{:S(2)}) collective-permute-start(f32[256,128]{1,0:T(8,128)S(1)} %get-tuple-element.86), channel_id=1, source_target_pairs={{0,8},{8,0},{16,24},{24,16},{1,9},{9,1},{17,25},{25,17},{2,10},{10... | collective-permute-start | bytes 393224 | tf_op jit(solution)/shard_map/sum_over_columns/ppermute | solution.py:490
  48.3 4.0 %collective-permute-start.15 = (f32[64,128]{1,0:T(8,128)S(1)}, f32[64,128]{1,0:T(8,128)S(1)}, u32[]{:S(2)}, u32[]{:S(2)}) collective-permute-start(f32[64,128]{1,0:T(8,128)S(1)} %get-tuple-element.93), channel_id=1, source_target_pairs={{0,2},{1,3},{2,0},{3,1},{4,6},{5,7},{6,4},{7,5},{8,10},{9,11},{10,... | collective-permute-start | bytes 98312 | tf_op jit(solution)/shard_map/sum_over_chips/ppermute | solution.py:525
  48.7 5.7 %collective-permute-start.17 = (f32[64,128]{1,0:T(8,128)S(1)}, f32[64,128]{1,0:T(8,128)S(1)}, u32[]{:S(2)}, u32[]{:S(2)}) collective-permute-start(f32[64,128]{1,0:T(8,128)S(1)} %get-tuple-element.94), channel_id=1, source_target_pairs={{0,6},{1,7},{2,4},{3,5},{4,2},{5,3},{6,0},{7,1},{8,14},{9,15},{10,... | collective-permute-start | bytes 98312 | tf_op jit(solution)/shard_map/sum_over_chips/ppermute | solution.py:525
  51.1 5.2 %collective-permute-start.16 = (f32[64,128]{1,0:T(8,128)S(1)}, f32[64,128]{1,0:T(8,128)S(1)}, u32[]{:S(2)}, u32[]{:S(2)}) collective-permute-start(f32[64,128]{1,0:T(8,128)S(1)} %get-tuple-element.95), channel_id=1, source_target_pairs={{0,4},{1,5},{2,6},{3,7},{4,0},{5,1},{6,2},{7,3},{8,12},{9,13},{10,... | collective-permute-start | bytes 98312 | tf_op jit(solution)/shard_map/sum_over_chips/ppermute | solution.py:525

commit v17 on v16

--- a/solution.py
+++ b/solution.py
@@ -1,4 +1,6 @@
 import functools
+import itertools
+import math
 
 import jax
 import jax.numpy as jnp
@@ -202,6 +204,7 @@
     for slab in range(3 * block_rows, slabs):
         both = jnp.concatenate([slab_ref[0, slab], slab_ref[1, slab]], axis=0)
         borders.append(jnp.concatenate(split_high_low(both), axis=1))
+    some = math.gcd(modes, 32)
     for c, (slab, first_lane) in enumerate(places):
         for row in range(block_rows):
             center = row * 3 + c
@@ -213,31 +216,34 @@
                     for k in range(2)
                 ]
                 border = jnp.dot(borders[slab], jnp.concatenate(picks, axis=1), preferred_element_type=F32)
-            for plane in range(2):
+            for plane, first in itertools.product(range(2), range(0, modes, some)):
                 place = plane * block_rows + row
-                value = slab_ref[plane, center]
-                stream = slab_ref[1 - plane, center] * (0.5 if plane == 0 else -0.5)
+                here = pl.ds(first, some)
+                value = slab_ref[plane, center, here, :]
+                stream = slab_ref[1 - plane, center, here, :] * (0.5 if plane == 0 else -0.5)
                 if row + 1 < block_rows:
-                    above = slab_ref[plane, center + 3]
+                    above = slab_ref[plane, center + 3, here, :]
                 else:
-                    above = pltpu.roll(slab_ref[plane, c], lanes - width, 1)
+                    above = pltpu.roll(slab_ref[plane, c, here, :], lanes - width, 1)
                     above = jnp.where(lane < lanes - width, above, 0.0)
                 if row > 0:
-                    below = slab_ref[plane, center - 3]
+                    below = slab_ref[plane, center - 3, here, :]
                 else:
-                    below = pltpu.roll(slab_ref[plane, 3 * (block_rows - 1) + c], width, 1)
+                    below = pltpu.roll(slab_ref[plane, 3 * (block_rows - 1) + c, here, :], width, 1)
                     below = jnp.where(lane >= width, below, 0.0)
                 normal = (above - below) * 0.5
                 after = jnp.where(column < width - 1, pltpu.roll(value, lanes - 1, 1), 0.0)
                 before = jnp.where(column > 0, pltpu.roll(value, 1, 1), 0.0)
-                span = (after - before) * 0.5 + border[plane * modes : (plane + 1) * modes, row % 2 * lanes : (row % 2 + 1) * lanes]
-                carry_ref[pl.ds(c * height + place, modes, stride=3 * height), :] = value
+                beside = border[plane * modes + first :, row % 2 * lanes :][:some, :lanes]
+                span = (after - before) * 0.5 + beside
+                carry_ref[pl.ds(first * (3 * height) + c * height + place, some, stride=3 * height), :] = value
                 for d, slope in enumerate((stream, normal, span)):
-                    slope_ref[pl.ds((d * 3 + c) * height + place, modes, stride=9 * height), :] = slope
-                store_projection(rhs_ref, c * height + place, value)
+                    start = first * (9 * height) + (d * 3 + c) * height + place
+                    slope_ref[pl.ds(start, some, stride=9 * height), :] = slope
                 if (plane == 1) == (row < block_rows // 2):
-                    near_ref[center] = value
-
+                    near_ref[center, here, :] = value
+            for plane in range(2):
+                store_projection(rhs_ref, c * height + plane * block_rows + row, slab_ref[plane, center])
     codes.wait()
 
     def one_peer(number, _):
@@ -519,10 +525,12 @@
             summed = summed + part
     with jax.named_scope("sum_over_chips"):
         shares = summed.reshape(chips, share, modes)
-        result = shares[0]
-        for step in range(1, chips):
+        parts = None
+        for step in reversed(range(1, chips)):
             pairing = [(2 * chip + c, 2 * (chip ^ step) + c) for chip in range(chips) for c in range(2)]
-            result = result + lax.ppermute(shares[step], "space", pairing)
+            part = lax.ppermute(shares[step], "space", pairing)
+            parts = part if parts is None else part + parts
+        result = shares[0] + parts
         return result * factor
 
 

time: 57.1 us -> 55.4 us (0.970)
  waiting for transfers between devices: 16 us -> 14.2 us
  starting transfers between devices: 19.9 us -> 20.8 us
  Pallas kernels: 20.2 us -> 19.4 us
    ppermute x3, waiting for transfers between devices: 4.49 us -> 2.68 us  [shards(): part = lax.ppermute(shares[step], 'space', pairing)]
    ppermute x3, starting transfers between devices: 3.55 us -> 4.45 us  [shards(): part = lax.ppermute(shares[step], 'space', pairing)]
    pallas_call x1, Pallas kernels: 7.66 us -> 6.89 us  [shards(): pl.pallas_call(functools.partial(inner_kernel, first_peer=early, sizes=(l...]
  transfers between devices with their start and end apart: 18 -> 18, of which waited for: 7 -> 6; matrix products, arithmetic and copies ran while one was open for 0% -> 0% of each run, Pallas kernels for 26% -> 25%
where the time goes in v17:
time: 55.4 us; the launch traced here: 55.3 us
  starting transfers between devices  20.8 us (38%)
  Pallas kernels  19.4 us (35%)
  waiting for transfers between devices  14.2 us (26%)
  other arithmetic  0.67 us (1%)
    ppermute x3, waiting for transfers between devices, shards(): lax.ppermute(packed[peer], 'tm', across(peer))  8.19 us
    pallas_call x1, Pallas kernels, shards(): pl.pallas_call(functools.partial(inner_kernel, first_peer=early, sizes=(l...  6.89 us
    ppermute x1, starting transfers between devices, shards(): across_edge = lax.ppermute(packed[tm_count], 'space', ring)  4.55 us
    ppermute x3, starting transfers between devices, shards(): part = lax.ppermute(shares[step], 'space', pairing)  4.45 us
    ppermute x3, starting transfers between devices, shards(): arrived.append(lax.ppermute(summed, 'tm', across(peer + 1)))  3.68 us
    ppermute x3, starting transfers between devices, shards(): lax.ppermute(parts[peer], 'tm', across(peer))  3.49 us
    ppermute x3, starting transfers between devices, shards(): lax.ppermute(packed[peer], 'tm', across(peer))  3.49 us
    pallas_call x2, Pallas kernels, shards(): pl.pallas_call(functools.partial(edge_kernel, peer=peer, sizes=(chips, sh...  3.33 us
  transfers between devices with their start and end apart: 18, of which 6 were waited for; matrix products, arithmetic and copies ran while one was open for 0% of the time, Pallas kernels for 25%

profile of v17, /device:TPU:0, one launch (start us, length us, event | category | flops | bytes accessed | tf_op | source)
XLA Modules:
  0.0 55.3 jit_solution(16672863694693777109)
XLA Ops:
  0.0 2.3 %pack.1 = (f32[13,32,128]{2,1,0:T(8,128)S(1)}, f32[13,32,128]{2,1,0:T(8,128)S(1)}, f32[13,32,128]{2,1,0:T(8,128)S(1)}, f32[13,32,128]{2,1,0:T(8,128)S(1)}, f32[4...) custom-call(f32[32,3,16,128]{3,2,1,0:T(8,128)} %bitcast.18, s32[2,2048]{1,0:T(2,128)} %bitcast.19, ...), custom_call_target="tpu_custom_call" | custom-call | tf_op jit(solution)/shard_map/pack/pallas_call | solution.py:405
  2.3 4.6 %collective-permute-start = (f32[4,6,32,128]{3,2,1,0:T(8,128)S(1)}, f32[4,6,32,128]{3,2,1,0:T(8,128)S(1)}, u32[]{:S(2)}, u32[]{:S(2)}) collective-permute-start(f32[4,6,32,128]{3,2,1,0:T(8,128)S(1)} %get-tuple-element.49), channel_id=1, source_target_pairs={{0,7},{1,2},{2,1},{3,4},{4,3},{5,6},{6,5},{7,0},{8,15},{9,10},{10,... | collective-permute-start | bytes 1179656 | tf_op jit(solution)/shard_map/to_next_plane/ppermute | solution.py:431
  6.9 1.5 %collective-permute-start.1 = (f32[13,32,128]{2,1,0:T(8,128)S(1)}, f32[13,32,128]{2,1,0:T(8,128)S(1)}, u32[]{:S(2)}, u32[]{:S(2)}) collective-permute-start(f32[13,32,128]{2,1,0:T(8,128)S(1)} %get-tuple-element.51), channel_id=1, source_target_pairs={{0,8},{8,0},{16,24},{24,16},{1,9},{9,1},{17,25},{25,17},{2,10},{10... | collective-permute-start | bytes 638984 | tf_op jit(solution)/shard_map/to_columns/ppermute | solution.py:433
  8.4 1.5 %collective-permute-start.2 = (f32[13,32,128]{2,1,0:T(8,128)S(1)}, f32[13,32,128]{2,1,0:T(8,128)S(1)}, u32[]{:S(2)}, u32[]{:S(2)}) collective-permute-start(f32[13,32,128]{2,1,0:T(8,128)S(1)} %get-tuple-element.52), channel_id=1, source_target_pairs={{0,16},{8,24},{16,0},{24,8},{1,17},{9,25},{17,1},{25,9},{2,18},{10... | collective-permute-start | bytes 638984 | tf_op jit(solution)/shard_map/to_columns/ppermute | solution.py:433
  9.9 0.5 collective-permute-start.3
  10.4 4.6 %collective-permute-done.1.refs_1_ = f32[13,32,128]{2,1,0:T(8,128)S(1)} collective-permute-done((f32[13,32,128]{2,1,0:T(8,128)S(1)}, f32[13,32,128]{2,1,0:T(8,128)S(1)}, u32[]{:S(2)}, u32[]{:S(2)}) %collective-permute-start.1) | collective-permute-done | bytes 213024 | tf_op jit(solution)/shard_map/to_columns/ppermute | solution.py:433
  14.9 3.6 %collective-permute-done.2.refs_2_ = f32[13,32,128]{2,1,0:T(8,128)S(1)} collective-permute-done((f32[13,32,128]{2,1,0:T(8,128)S(1)}, f32[13,32,128]{2,1,0:T(8,128)S(1)}, u32[]{:S(2)}, u32[]{:S(2)}) %collective-permute-start.2) | collective-permute-done | bytes 213024 | tf_op jit(solution)/shard_map/to_columns/ppermute | solution.py:433
  18.6 0.0 collective-permute-done.3.refs_3_
  18.6 0.1 collective-permute-start.10
  18.7 0.5 collective-permute-start.7
  19.2 0.1 collective-permute-start.8
  19.3 0.4 collective-permute-start.9
  19.7 1.0 %collective-permute-start.4 = (f32[6,32,128]{2,1,0:T(8,128)S(1)}, f32[6,32,128]{2,1,0:T(8,128)S(1)}, u32[]{:S(2)}, u32[]{:S(2)}) collective-permute-start(f32[6,32,128]{2,1,0:T(8,128)S(1)} %get-tuple-element.56), channel_id=1, source_target_pairs={{0,8},{8,0},{16,24},{24,16},{1,9},{9,1},{17,25},{25,17},{2,10},{10... | collective-permute-start | bytes 294920 | tf_op jit(solution)/shard_map/next_to_columns/ppermute | solution.py:438
  20.7 0.9 %collective-permute-start.5 = (f32[6,32,128]{2,1,0:T(8,128)S(1)}, f32[6,32,128]{2,1,0:T(8,128)S(1)}, u32[]{:S(2)}, u32[]{:S(2)}) collective-permute-start(f32[6,32,128]{2,1,0:T(8,128)S(1)} %get-tuple-element.57), channel_id=1, source_target_pairs={{0,16},{8,24},{16,0},{24,8},{1,17},{9,25},{17,1},{25,9},{2,18},{10... | collective-permute-start | bytes 294920 | tf_op jit(solution)/shard_map/next_to_columns/ppermute | solution.py:438
  21.7 1.5 %collective-permute-start.6 = (f32[6,32,128]{2,1,0:T(8,128)S(1)}, f32[6,32,128]{2,1,0:T(8,128)S(1)}, u32[]{:S(2)}, u32[]{:S(2)}) collective-permute-start(f32[6,32,128]{2,1,0:T(8,128)S(1)} %get-tuple-element.58), channel_id=1, source_target_pairs={{0,24},{8,16},{16,8},{24,0},{1,25},{9,17},{17,9},{25,1},{2,26},{10... | collective-permute-start | bytes 294920 | tf_op jit(solution)/shard_map/next_to_columns/ppermute | solution.py:438
  23.2 6.9 %inner_terms.2 = (f32[12,128,128]{2,1,0:T(8,128)S(1)}, f32[3072,128]{1,0:T(8,128)S(1)}, f32[9216,128]{1,0:T(8,128)S(1)}, bf16[3072,256]{1,0:T(8,128)(2,1)S(1)}, ...) custom-call(s32[2048]{0:T(1024)S(1)} %get-tuple-element.47.codes_ref, f32[128,128]{1,0:T(8,128)S(1)} %get-tuple-element.48.coeffs_ref, ...), custom_call_target="tpu_custom_call" | custom-call | flops 12000000000 | bytes 10000000 | tf_op jit(solution)/shard_map/inner_terms/pallas_call | solution.py:446
  30.2 0.1 collective-permute-start.11
  30.2 2.8 %inner_terms.3 = (f32[2,256,128]{2,1,0:T(8,128)S(1)}, f32[6144,128]{1,0:T(8,128)S(1)}) custom-call(s32[2048]{0:T(1024)S(1)} %get-tuple-element.47.codes_ref, f32[3072,128]{1,0:T(8,128)S(1)} %get-tuple-element.73.carry_ref, f32[9216,128]{1,0:T(8,128)S(1)} %get-tuple-element.74.slope_ref, ...), custom_call_target="tpu_custom_call", output_to_operand_aliasing={{1}: (4, {})} | custom-call | flops 8000000000 | bytes 10000000 | tf_op jit(solution)/shard_map/inner_terms/pallas_call | solution.py:466
  33.0 3.0 %edge_terms.4 = (f32[1024,128]{1,0:T(8,128)S(1)}, f32[3072,128]{1,0:T(8,128)S(1)}, bf16[3072,256]{1,0:T(8,128)(2,1)S(1)}, f32[256,128]{1,0:T(8,128)S(1)}, f32[6144,128]{1,0:T(8,128)S(1)}) custom-call(s32[2048]{0:T(1024)S(1)} %get-tuple-element.47.codes_ref, f32[128,128]{1,0:T(8,128)S(1)} %get-tuple-element.48.coeffs_ref, ...), custom_call_target="tpu_custom_call" | custom-call | tf_op jit(solution)/shard_map/edge_terms/pallas_call | solution.py:477
  36.1 1.5 %collective-permute-start.12 = (f32[256,128]{1,0:T(8,128)S(1)}, f32[256,128]{1,0:T(8,128)S(1)}, u32[]{:S(2)}, u32[]{:S(2)}) collective-permute-start(f32[256,128]{1,0:T(8,128)S(1)} %get-tuple-element.80), channel_id=1, source_target_pairs={{0,24},{8,16},{16,8},{24,0},{1,25},{9,17},{17,9},{25,1},{2,26},{10... | collective-permute-start | bytes 393224 | tf_op jit(solution)/shard_map/sum_over_columns/ppermute | solution.py:496
  37.6 1.7 %edge_terms.5 = (f32[256,128]{1,0:T(8,128)S(1)}, f32[6144,128]{1,0:T(8,128)S(1)}) custom-call(s32[2048]{0:T(1024)S(1)} %get-tuple-element.47.codes_ref, f32[1024,128]{1,0:T(8,128)S(1)} %get-tuple-element.78.carry_ref, f32[3072,128]{1,0:T(8,128)S(1)} %get-tuple-element.79.slope_ref, bf16[3072,256]{1,0:T(8,128)(2,1)S(1)} %get-tuple-element.72.rhs_ref, ...), custom_call_target="tpu_custom_call" | custom-call | flops 100000000 | bytes 100000 | tf_op jit(solution)/shard_map/edge_terms/pallas_call | solution.py:505
  39.2 1.2 %collective-permute-start.13 = (f32[256,128]{1,0:T(8,128)S(1)}, f32[256,128]{1,0:T(8,128)S(1)}, u32[]{:S(2)}, u32[]{:S(2)}) collective-permute-start(f32[256,128]{1,0:T(8,128)S(1)} %get-tuple-element.83), channel_id=1, source_target_pairs={{0,16},{8,24},{16,0},{24,8},{1,17},{9,25},{17,1},{25,9},{2,18},{10... | collective-permute-start | bytes 393224 | tf_op jit(solution)/shard_map/sum_over_columns/ppermute | solution.py:496
  40.4 1.7 %edge_terms.6 = (f32[256,128]{1,0:T(8,128)S(1)}, f32[6144,128]{1,0:T(8,128)S(1)}) custom-call(s32[2048]{0:T(1024)S(1)} %get-tuple-element.47.codes_ref, f32[1024,128]{1,0:T(8,128)S(1)} %get-tuple-element.78.carry_ref, f32[3072,128]{1,0:T(8,128)S(1)} %get-tuple-element.79.slope_ref, bf16[3072,256]{1,0:T(8,128)(2,1)S(1)} %get-tuple-element.72.rhs_ref, ...), custom_call_target="tpu_custom_call" | custom-call | flops 100000000 | bytes 100000 | tf_op jit(solution)/shard_map/edge_terms/pallas_call | solution.py:505
  42.1 1.0 %collective-permute-start.14 = (f32[256,128]{1,0:T(8,128)S(1)}, f32[256,128]{1,0:T(8,128)S(1)}, u32[]{:S(2)}, u32[]{:S(2)}) collective-permute-start(f32[256,128]{1,0:T(8,128)S(1)} %get-tuple-element.86), channel_id=1, source_target_pairs={{0,8},{8,0},{16,24},{24,16},{1,9},{9,1},{17,25},{25,17},{2,10},{10... | collective-permute-start | bytes 393224 | tf_op jit(solution)/shard_map/sum_over_columns/ppermute | solution.py:496
  43.1 2.6 %collective-permute-done.13.refs_1_ = f32[256,128]{1,0:T(8,128)S(1)} collective-permute-done((f32[256,128]{1,0:T(8,128)S(1)}, f32[256,128]{1,0:T(8,128)S(1)}, u32[]{:S(2)}, u32[]{:S(2)}) %collective-permute-start.13) | collective-permute-done | bytes 131104 | tf_op jit(solution)/shard_map/sum_over_columns/ppermute | solution.py:496
  45.8 1.1 %edge_terms.7 = f32[256,128]{1,0:T(8,128)S(1)} custom-call(bf16[3072,256]{1,0:T(8,128)(2,1)S(1)} %get-tuple-element.72.rhs_ref, f32[2,256,128]{2,1,0:T(8,128)S(1)} %get-tuple-element.87.inner_ref, f32[6144,128]{1,0:T(8,128)S(1)} %get-tuple-element.88.picked_ref, f32[256,128]{1,0:T(8,128)S(1)} %collective-permute-done.12.refs_0_, ...), custom_call_target="tpu_custom_call" | custom-call | flops 100000000 | bytes 100000 | tf_op jit(solution)/shard_map/edge_terms/pallas_call | solution.py:515
  46.8 0.6 %collective-permute-done.14 = f32[256,128]{1,0:T(8,128)S(1)} collective-permute-done((f32[256,128]{1,0:T(8,128)S(1)}, f32[256,128]{1,0:T(8,128)S(1)}, u32[]{:S(2)}, u32[]{:S(2)}) %collective-permute-start.14) | collective-permute-done | bytes 131104 | tf_op jit(solution)/shard_map/sum_over_columns/ppermute | solution.py:496
  47.5 2.3 %collective-permute-start.17 = (f32[64,128]{1,0:T(8,128)S(1)}, f32[64,128]{1,0:T(8,128)S(1)}, u32[]{:S(2)}, u32[]{:S(2)}) collective-permute-start(f32[64,128]{1,0:T(8,128)S(1)} %get-tuple-element.93), channel_id=1, source_target_pairs={{0,6},{1,7},{2,4},{3,5},{4,2},{5,3},{6,0},{7,1},{8,14},{9,15},{10,... | collective-permute-start | bytes 98312 | tf_op jit(solution)/shard_map/sum_over_chips/ppermute | solution.py:531
  49.8 2.1 %collective-permute-start.15 = (f32[64,128]{1,0:T(8,128)S(1)}, f32[64,128]{1,0:T(8,128)S(1)}, u32[]{:S(2)}, u32[]{:S(2)}) collective-permute-start(f32[64,128]{1,0:T(8,128)S(1)} %get-tuple-element.95), channel_id=1, source_target_pairs={{0,2},{1,3},{2,0},{3,1},{4,6},{5,7},{6,4},{7,5},{8,10},{9,11},{10,... | collective-permute-start | bytes 98312 | tf_op jit(solution)/shard_map/sum_over_chips/ppermute | solution.py:531
  52.0 1.3 %collective-permute-done.17 = f32[64,128]{1,0:T(8,128)S(1)} collective-permute-done((f32[64,128]{1,0:T(8,128)S(1)}, f32[64,128]{1,0:T(8,128)S(1)}, u32[]{:S(2)}, u32[]{:S(2)}) %collective-permute-start.17) | collective-permute-done | bytes 32800 | tf_op jit(solution)/shard_map/sum_over_chips/ppermute | solution.py:531
  53.3 1.4 %collective-permute-done.16 = f32[64,128]{1,0:T(8,128)S(1)} collective-permute-done((f32[64,128]{1,0:T(8,128)S(1)}, f32[64,128]{1,0:T(8,128)S(1)}, u32[]{:S(2)}, u32[]{:S(2)}) %collective-permute-start.16) | collective-permute-done | bytes 32800 | tf_op jit(solution)/shard_map/sum_over_chips/ppermute | solution.py:531
  54.6 0.6 %fusion = f32[64,128]{1,0:T(8,128)} fusion(f32[256,128]{1,0:T(8,128)S(1)} %add.12, f32[64,128]{1,0:T(8,128)S(1)} %collective-permute-done.15, f32[64,128]{1,0:T(8,128)S(1)} %collective-permute-done.16, f32[64,128]{1,0:T(8,128)S(1)} %collective-permute-done.17), kind=kLoop, calls=%fused_computation.6 | loop fusion | flops 32768 | bytes 163840 | tf_op jit(solution)/shard_map/sum_over_chips/mul | solution.py:534
  (16 shorter events, 0.1 us)
Async XLA Ops:
  2.3 16.2 %collective-permute-start = (f32[4,6,32,128]{3,2,1,0:T(8,128)S(1)}, f32[4,6,32,128]{3,2,1,0:T(8,128)S(1)}, u32[]{:S(2)}, u32[]{:S(2)}) collective-permute-start(f32[4,6,32,128]{3,2,1,0:T(8,128)S(1)} %get-tuple-element.49), channel_id=1, source_target_pairs={{0,7},{1,2},{2,1},{3,4},{4,3},{5,6},{6,5},{7,0},{8,15},{9,10},{10,... | collective-permute-start | bytes 1179656 | tf_op jit(solution)/shard_map/to_next_plane/ppermute | solution.py:431
  6.9 8.0 %collective-permute-start.1 = (f32[13,32,128]{2,1,0:T(8,128)S(1)}, f32[13,32,128]{2,1,0:T(8,128)S(1)}, u32[]{:S(2)}, u32[]{:S(2)}) collective-permute-start(f32[13,32,128]{2,1,0:T(8,128)S(1)} %get-tuple-element.51), channel_id=1, source_target_pairs={{0,8},{8,0},{16,24},{24,16},{1,9},{9,1},{17,25},{25,17},{2,10},{10... | collective-permute-start | bytes 638984 | tf_op jit(solution)/shard_map/to_columns/ppermute | solution.py:433
  8.4 10.2 %collective-permute-start.2 = (f32[13,32,128]{2,1,0:T(8,128)S(1)}, f32[13,32,128]{2,1,0:T(8,128)S(1)}, u32[]{:S(2)}, u32[]{:S(2)}) collective-permute-start(f32[13,32,128]{2,1,0:T(8,128)S(1)} %get-tuple-element.52), channel_id=1, source_target_pairs={{0,16},{8,24},{16,0},{24,8},{1,17},{9,25},{17,1},{25,9},{2,18},{10... | collective-permute-start | bytes 638984 | tf_op jit(solution)/shard_map/to_columns/ppermute | solution.py:433
  9.9 8.7 %collective-permute-start.3 = (f32[13,32,128]{2,1,0:T(8,128)S(1)}, f32[13,32,128]{2,1,0:T(8,128)S(1)}, u32[]{:S(2)}, u32[]{:S(2)}) collective-permute-start(f32[13,32,128]{2,1,0:T(8,128)S(1)} %get-tuple-element.54), channel_id=1, source_target_pairs={{0,24},{8,16},{16,8},{24,0},{1,25},{9,17},{17,9},{25,1},{2,26},{10... | collective-permute-start | bytes 638984 | tf_op jit(solution)/shard_map/to_columns/ppermute | solution.py:433
  18.6 2.1 %collective-permute-start.10 = (f32[13,32,128]{2,1,0:T(8,128)S(1)}, f32[13,32,128]{2,1,0:T(8,128)S(1)}, u32[]{:S(2)}, u32[]{:S(2)}) collective-permute-start(f32[13,32,128]{2,1,0:T(8,128)S(1)} %collective-permute-done.3.refs_3_), channel_id=1, source_target_pairs={{0,1},{1,0},{2,3},{3,2},{4,5},{5,4},{6,7},{7,6},{8,9},{9,8},{10,11... | collective-permute-start | bytes 638984 | tf_op jit(solution)/shard_map/to_other_core/ppermute | solution.py:440
  18.7 3.0 %collective-permute-start.7 = (f32[13,32,128]{2,1,0:T(8,128)S(1)}, f32[13,32,128]{2,1,0:T(8,128)S(1)}, u32[]{:S(2)}, u32[]{:S(2)}) collective-permute-start(f32[13,32,128]{2,1,0:T(8,128)S(1)} %get-tuple-element.59.refs_0_), channel_id=1, source_target_pairs={{0,1},{1,0},{2,3},{3,2},{4,5},{5,4},{6,7},{7,6},{8,9},{9,8},{10,11... | collective-permute-start | bytes 638984 | tf_op jit(solution)/shard_map/to_other_core/ppermute | solution.py:440
  19.2 4.0 %collective-permute-start.8 = (f32[13,32,128]{2,1,0:T(8,128)S(1)}, f32[13,32,128]{2,1,0:T(8,128)S(1)}, u32[]{:S(2)}, u32[]{:S(2)}) collective-permute-start(f32[13,32,128]{2,1,0:T(8,128)S(1)} %collective-permute-done.1.refs_1_), channel_id=1, source_target_pairs={{0,1},{1,0},{2,3},{3,2},{4,5},{5,4},{6,7},{7,6},{8,9},{9,8},{10,11... | collective-permute-start | bytes 638984 | tf_op jit(solution)/shard_map/to_other_core/ppermute | solution.py:440
  19.3 3.9 %collective-permute-start.9 = (f32[13,32,128]{2,1,0:T(8,128)S(1)}, f32[13,32,128]{2,1,0:T(8,128)S(1)}, u32[]{:S(2)}, u32[]{:S(2)}) collective-permute-start(f32[13,32,128]{2,1,0:T(8,128)S(1)} %collective-permute-done.2.refs_2_), channel_id=1, source_target_pairs={{0,1},{1,0},{2,3},{3,2},{4,5},{5,4},{6,7},{7,6},{8,9},{9,8},{10,11... | collective-permute-start | bytes 638984 | tf_op jit(solution)/shard_map/to_other_core/ppermute | solution.py:440
  19.7 10.4 %collective-permute-start.4 = (f32[6,32,128]{2,1,0:T(8,128)S(1)}, f32[6,32,128]{2,1,0:T(8,128)S(1)}, u32[]{:S(2)}, u32[]{:S(2)}) collective-permute-start(f32[6,32,128]{2,1,0:T(8,128)S(1)} %get-tuple-element.56), channel_id=1, source_target_pairs={{0,8},{8,0},{16,24},{24,16},{1,9},{9,1},{17,25},{25,17},{2,10},{10... | collective-permute-start | bytes 294920 | tf_op jit(solution)/shard_map/next_to_columns/ppermute | solution.py:438
  20.7 9.4 %collective-permute-start.5 = (f32[6,32,128]{2,1,0:T(8,128)S(1)}, f32[6,32,128]{2,1,0:T(8,128)S(1)}, u32[]{:S(2)}, u32[]{:S(2)}) collective-permute-start(f32[6,32,128]{2,1,0:T(8,128)S(1)} %get-tuple-element.57), channel_id=1, source_target_pairs={{0,16},{8,24},{16,0},{24,8},{1,17},{9,25},{17,1},{25,9},{2,18},{10... | collective-permute-start | bytes 294920 | tf_op jit(solution)/shard_map/next_to_columns/ppermute | solution.py:438
  21.7 8.5 %collective-permute-start.6 = (f32[6,32,128]{2,1,0:T(8,128)S(1)}, f32[6,32,128]{2,1,0:T(8,128)S(1)}, u32[]{:S(2)}, u32[]{:S(2)}) collective-permute-start(f32[6,32,128]{2,1,0:T(8,128)S(1)} %get-tuple-element.58), channel_id=1, source_target_pairs={{0,24},{8,16},{16,8},{24,0},{1,25},{9,17},{17,9},{25,1},{2,26},{10... | collective-permute-start | bytes 294920 | tf_op jit(solution)/shard_map/next_to_columns/ppermute | solution.py:438
  30.2 2.9 %collective-permute-start.11 = (f32[4,6,32,128]{3,2,1,0:T(8,128)S(1)}, f32[4,6,32,128]{3,2,1,0:T(8,128)S(1)}, u32[]{:S(2)}, u32[]{:S(2)}) collective-permute-start(f32[4,6,32,128]{3,2,1,0:T(8,128)S(1)} %pad_maximum_fusion), channel_id=1, source_target_pairs={{0,1},{1,0},{2,3},{3,2},{4,5},{5,4},{6,7},{7,6},{8,9},{9,8},{10,11... | collective-permute-start | bytes 1179656 | tf_op jit(solution)/shard_map/next_to_other_core/ppermute | solution.py:464
  36.1 9.7 %collective-permute-start.12 = (f32[256,128]{1,0:T(8,128)S(1)}, f32[256,128]{1,0:T(8,128)S(1)}, u32[]{:S(2)}, u32[]{:S(2)}) collective-permute-start(f32[256,128]{1,0:T(8,128)S(1)} %get-tuple-element.80), channel_id=1, source_target_pairs={{0,24},{8,16},{16,8},{24,0},{1,25},{9,17},{17,9},{25,1},{2,26},{10... | collective-permute-start | bytes 393224 | tf_op jit(solution)/shard_map/sum_over_columns/ppermute | solution.py:496
  39.2 6.5 %collective-permute-start.13 = (f32[256,128]{1,0:T(8,128)S(1)}, f32[256,128]{1,0:T(8,128)S(1)}, u32[]{:S(2)}, u32[]{:S(2)}) collective-permute-start(f32[256,128]{1,0:T(8,128)S(1)} %get-tuple-element.83), channel_id=1, source_target_pairs={{0,16},{8,24},{16,0},{24,8},{1,17},{9,25},{17,1},{25,9},{2,18},{10... | collective-permute-start | bytes 393224 | tf_op jit(solution)/shard_map/sum_over_columns/ppermute | solution.py:496
  42.1 5.4 %collective-permute-start.14 = (f32[256,128]{1,0:T(8,128)S(1)}, f32[256,128]{1,0:T(8,128)S(1)}, u32[]{:S(2)}, u32[]{:S(2)}) collective-permute-start(f32[256,128]{1,0:T(8,128)S(1)} %get-tuple-element.86), channel_id=1, source_target_pairs={{0,8},{8,0},{16,24},{24,16},{1,9},{9,1},{17,25},{25,17},{2,10},{10... | collective-permute-start | bytes 393224 | tf_op jit(solution)/shard_map/sum_over_columns/ppermute | solution.py:496
  47.5 5.8 %collective-permute-start.17 = (f32[64,128]{1,0:T(8,128)S(1)}, f32[64,128]{1,0:T(8,128)S(1)}, u32[]{:S(2)}, u32[]{:S(2)}) collective-permute-start(f32[64,128]{1,0:T(8,128)S(1)} %get-tuple-element.93), channel_id=1, source_target_pairs={{0,6},{1,7},{2,4},{3,5},{4,2},{5,3},{6,0},{7,1},{8,14},{9,15},{10,... | collective-permute-start | bytes 98312 | tf_op jit(solution)/shard_map/sum_over_chips/ppermute | solution.py:531
  49.8 4.8 %collective-permute-start.16 = (f32[64,128]{1,0:T(8,128)S(1)}, f32[64,128]{1,0:T(8,128)S(1)}, u32[]{:S(2)}, u32[]{:S(2)}) collective-permute-start(f32[64,128]{1,0:T(8,128)S(1)} %get-tuple-element.94), channel_id=1, source_target_pairs={{0,4},{1,5},{2,6},{3,7},{4,0},{5,1},{6,2},{7,3},{8,12},{9,13},{10,... | collective-permute-start | bytes 98312 | tf_op jit(solution)/shard_map/sum_over_chips/ppermute | solution.py:531
  49.8 4.8 %collective-permute-start.15 = (f32[64,128]{1,0:T(8,128)S(1)}, f32[64,128]{1,0:T(8,128)S(1)}, u32[]{:S(2)}, u32[]{:S(2)}) collective-permute-start(f32[64,128]{1,0:T(8,128)S(1)} %get-tuple-element.95), channel_id=1, source_target_pairs={{0,2},{1,3},{2,0},{3,1},{4,6},{5,7},{6,4},{7,5},{8,10},{9,11},{10,... | collective-permute-start | bytes 98312 | tf_op jit(solution)/shard_map/sum_over_chips/ppermute | solution.py:531

commit v18 on v17

--- a/solution.py
+++ b/solution.py
@@ -312,6 +312,7 @@
     modes, lanes = near_ref.shape[1:]
     height = 2 * block_rows
     half = block_rows // 2 * 3
+    some = math.gcd(modes, 32)
     weights = mode_weights(coeffs_ref, local_s, tm_count)
     for slab in range(half):
         mine = jnp.concatenate([next_own[peer][slab] for peer in range(tm_count)], axis=0)
@@ -322,13 +323,15 @@
         edges = ((near_ref[slab], result[:, :lanes]), (result[:, lanes:], near_ref[half + slab]))
         for number, (low, high) in enumerate(edges):
             place = number * block_rows + 2 * row
-            for at, value, across in ((place, low, high * 0.5), (place + 1, high, low * -0.5)):
-                if c == 0:
-                    carry_ref[pl.ds(at, modes, stride=height), :] = value
-                slope_ref[pl.ds(c * height + at, modes, stride=3 * height), :] = across
-                store_projection(rhs_ref, c * height + at, value)
-
-
+            for first in range(0, modes, some):
+                one, two = low[first : first + some], high[first : first + some]
+                for at, value, across in ((place, one, two * 0.5), (place + 1, two, one * -0.5)):
+                    if c == 0:
+                        carry_ref[pl.ds(first * height + at, some, stride=height), :] = value
+                    start = first * (3 * height) + c * height + at
+                    slope_ref[pl.ds(start, some, stride=3 * height), :] = across
+            store_projection(rhs_ref, c * height + place, low)
+            store_projection(rhs_ref, c * height + place + 1, high)
     codes.wait()
     pick_edge(held_codes_ref, carry_ref, slope_ref, conv_ref, peer, (chips, share, bits))
     out_ref[...] = edge_sum(conv_ref, rhs_ref, inner_ref, peer)
@@ -364,9 +367,22 @@
     pick_edge(held_codes_ref, carry_ref, slope_ref, conv_ref, peer - 1, sizes)
 
 
-def own_edge_kernel(rhs_ref, inner_ref, picked_ref, *refs):
+def picked_edge_kernel(rhs_ref, inner_ref, picked_ref, out_ref, *, peer):
+    out_ref[...] = edge_sum(picked_ref, rhs_ref, inner_ref, peer)
+
+
+def own_edge_kernel(
+    codes_ref, carry_ref, slope_ref, rhs_ref, inner_ref, after_ref, out_ref, conv_ref, held_codes_ref, sem, *, sizes
+):
+    del after_ref
+    copy_of_codes(codes_ref, held_codes_ref, sem).wait()
+    pick_edge(held_codes_ref, carry_ref, slope_ref, conv_ref, 0, sizes)
+    out_ref[...] = edge_sum(conv_ref, rhs_ref, inner_ref, 0)
+
+
+def add_kernel(own_ref, *refs):
     *arrived_refs, out_ref = refs
-    total = edge_sum(picked_ref, rhs_ref, inner_ref, 0)
+    total = own_ref[...]
     for arrived_ref in arrived_refs:
         total = total + arrived_ref[...]
     out_ref[...] = total
@@ -501,7 +517,7 @@
         with jax.named_scope("edge_terms"):
             inner_sums = early_sums if peer >= early else late_sums
             edge_cost = pl.CostEstimate(flops=10**8, bytes_accessed=10**5, transcendentals=0)
-            if peer:
+            if peer > 1:
                 summed, next_picked = pl.pallas_call(
                     functools.partial(edge_kernel, peer=peer, sizes=(chips, share, bits)),
                     out_shape=[pltpu.VMEM((block, modes), F32), picked],
@@ -511,15 +527,31 @@
                     compiler_params=vmem_limit(16),
                     cost_estimate=edge_cost,
                 )(codes, *[in_vmem(table) for table in (*tables, inner_sums, next_picked)])
-            else:
+            elif peer:
                 summed = pl.pallas_call(
-                    own_edge_kernel,
+                    functools.partial(picked_edge_kernel, peer=peer),
                     out_shape=pltpu.VMEM((block, modes), F32),
-                    in_specs=[vmem] * (3 + taken),
+                    in_specs=[vmem] * 3,
                     out_specs=vmem,
                     compiler_params=vmem_limit(16),
                     cost_estimate=edge_cost,
-                )(*[in_vmem(table) for table in (tables[2], inner_sums, next_picked, *arrived[:taken])])
+                )(*[in_vmem(table) for table in (tables[2], inner_sums, next_picked)])
+            else:
+                summed = pl.pallas_call(
+                    functools.partial(own_edge_kernel, sizes=(chips, share, bits)),
+                    out_shape=pltpu.VMEM((block, modes), F32),
+                    in_specs=[vmem] * 6,
+                    out_specs=vmem,
+                    scratch_shapes=[picked] + held_codes,
+                    compiler_params=vmem_limit(16),
+                    cost_estimate=edge_cost,
+                )(codes, *[in_vmem(table) for table in (*tables, inner_sums, summed)])
+                summed = pl.pallas_call(
+                    add_kernel,
+                    out_shape=pltpu.VMEM((block, modes), F32),
+                    in_specs=[vmem] * (1 + taken),
+                    out_specs=vmem,
+                )(*[in_vmem(table) for table in (summed, *arrived[:taken])])
     with jax.named_scope("sum_over_columns"):
         for part in arrived[taken:]:
             summed = summed + part

time: 55.4 us -> 54.8 us (0.989)
  waiting for transfers between devices: 14.2 us -> 12.9 us
  Pallas kernels: 19.4 us -> 20.1 us
    pallas_call x1 -> x3, Pallas kernels: 1.07 us -> 3.39 us  [the longest x1 2.3 us: shards(): pl.pallas_call(functools.partial(own_edge_kernel, sizes=(chips, share, bi...]
    pallas_call x2 -> x1, Pallas kernels: 3.33 us -> 1.67 us  [shards(): pl.pallas_call(functools.partial(edge_kernel, peer=peer, sizes=(chips, sh...]
    ppermute x3, waiting for transfers between devices: 3.28 us -> 2.02 us  [shards(): arrived.append(lax.ppermute(summed, 'tm', across(peer + 1)))]
  transfers between devices with their start and end apart: 18 -> 18, of which waited for: 6 -> 6; matrix products, arithmetic and copies ran while one was open for 0% -> 0% of each run, Pallas kernels for 25% -> 27%
where the time goes in v18:
time: 54.8 us; the launch traced here: 54.7 us
  starting transfers between devices  20.8 us (38%)
  Pallas kernels  20.1 us (37%)
  waiting for transfers between devices  12.9 us (24%)
  other arithmetic  0.67 us (1%)
    ppermute x3, waiting for transfers between devices, shards(): lax.ppermute(packed[peer], 'tm', across(peer))  8.19 us
    pallas_call x1, Pallas kernels, shards(): pl.pallas_call(functools.partial(inner_kernel, first_peer=early, sizes=(l...  6.89 us
    ppermute x1, starting transfers between devices, shards(): across_edge = lax.ppermute(packed[tm_count], 'space', ring)  4.55 us
    ppermute x3, starting transfers between devices, shards(): part = lax.ppermute(shares[step], 'space', pairing)  4.45 us
    ppermute x3, starting transfers between devices, shards(): arrived.append(lax.ppermute(summed, 'tm', across(peer + 1)))  3.68 us
    ppermute x3, starting transfers between devices, shards(): lax.ppermute(parts[peer], 'tm', across(peer))  3.49 us
    ppermute x3, starting transfers between devices, shards(): lax.ppermute(packed[peer], 'tm', across(peer))  3.49 us
    pallas_call x1, Pallas kernels, shards(): pl.pallas_call(functools.partial(far_kernel, peer=tm_count - 1, sizes=(lo...  3.04 us
  transfers between devices with their start and end apart: 18, of which 6 were waited for; matrix products, arithmetic and copies ran while one was open for 0% of the time, Pallas kernels for 27%

profile of v18, /device:TPU:0, one launch (start us, length us, event | category | flops | bytes accessed | tf_op | source)
XLA Modules:
  0.0 54.7 jit_solution(12686605209478099333)
XLA Ops:
  0.0 2.3 %pack.1 = (f32[13,32,128]{2,1,0:T(8,128)S(1)}, f32[13,32,128]{2,1,0:T(8,128)S(1)}, f32[13,32,128]{2,1,0:T(8,128)S(1)}, f32[13,32,128]{2,1,0:T(8,128)S(1)}, f32[4...) custom-call(f32[32,3,16,128]{3,2,1,0:T(8,128)} %bitcast.18, s32[2,2048]{1,0:T(2,128)} %bitcast.19, ...), custom_call_target="tpu_custom_call" | custom-call | tf_op jit(solution)/shard_map/pack/pallas_call | solution.py:421
  2.3 4.6 %collective-permute-start = (f32[4,6,32,128]{3,2,1,0:T(8,128)S(1)}, f32[4,6,32,128]{3,2,1,0:T(8,128)S(1)}, u32[]{:S(2)}, u32[]{:S(2)}) collective-permute-start(f32[4,6,32,128]{3,2,1,0:T(8,128)S(1)} %get-tuple-element.47), channel_id=1, source_target_pairs={{0,7},{1,2},{2,1},{3,4},{4,3},{5,6},{6,5},{7,0},{8,15},{9,10},{10,... | collective-permute-start | bytes 1179656 | tf_op jit(solution)/shard_map/to_next_plane/ppermute | solution.py:447
  6.9 1.5 %collective-permute-start.1 = (f32[13,32,128]{2,1,0:T(8,128)S(1)}, f32[13,32,128]{2,1,0:T(8,128)S(1)}, u32[]{:S(2)}, u32[]{:S(2)}) collective-permute-start(f32[13,32,128]{2,1,0:T(8,128)S(1)} %get-tuple-element.49), channel_id=1, source_target_pairs={{0,8},{8,0},{16,24},{24,16},{1,9},{9,1},{17,25},{25,17},{2,10},{10... | collective-permute-start | bytes 638984 | tf_op jit(solution)/shard_map/to_columns/ppermute | solution.py:449
  8.4 1.5 %collective-permute-start.2 = (f32[13,32,128]{2,1,0:T(8,128)S(1)}, f32[13,32,128]{2,1,0:T(8,128)S(1)}, u32[]{:S(2)}, u32[]{:S(2)}) collective-permute-start(f32[13,32,128]{2,1,0:T(8,128)S(1)} %get-tuple-element.50), channel_id=1, source_target_pairs={{0,16},{8,24},{16,0},{24,8},{1,17},{9,25},{17,1},{25,9},{2,18},{10... | collective-permute-start | bytes 638984 | tf_op jit(solution)/shard_map/to_columns/ppermute | solution.py:449
  9.9 0.5 collective-permute-start.3
  10.4 4.6 %collective-permute-done.1.refs_1_ = f32[13,32,128]{2,1,0:T(8,128)S(1)} collective-permute-done((f32[13,32,128]{2,1,0:T(8,128)S(1)}, f32[13,32,128]{2,1,0:T(8,128)S(1)}, u32[]{:S(2)}, u32[]{:S(2)}) %collective-permute-start.1) | collective-permute-done | bytes 213024 | tf_op jit(solution)/shard_map/to_columns/ppermute | solution.py:449
  14.9 3.6 %collective-permute-done.2.refs_2_ = f32[13,32,128]{2,1,0:T(8,128)S(1)} collective-permute-done((f32[13,32,128]{2,1,0:T(8,128)S(1)}, f32[13,32,128]{2,1,0:T(8,128)S(1)}, u32[]{:S(2)}, u32[]{:S(2)}) %collective-permute-start.2) | collective-permute-done | bytes 213024 | tf_op jit(solution)/shard_map/to_columns/ppermute | solution.py:449
  18.6 0.0 collective-permute-done.3.refs_3_
  18.6 0.1 collective-permute-start.10
  18.7 0.5 collective-permute-start.7
  19.2 0.1 collective-permute-start.8
  19.3 0.4 collective-permute-start.9
  19.7 1.0 %collective-permute-start.4 = (f32[6,32,128]{2,1,0:T(8,128)S(1)}, f32[6,32,128]{2,1,0:T(8,128)S(1)}, u32[]{:S(2)}, u32[]{:S(2)}) collective-permute-start(f32[6,32,128]{2,1,0:T(8,128)S(1)} %get-tuple-element.54), channel_id=1, source_target_pairs={{0,8},{8,0},{16,24},{24,16},{1,9},{9,1},{17,25},{25,17},{2,10},{10... | collective-permute-start | bytes 294920 | tf_op jit(solution)/shard_map/next_to_columns/ppermute | solution.py:454
  20.7 0.9 %collective-permute-start.5 = (f32[6,32,128]{2,1,0:T(8,128)S(1)}, f32[6,32,128]{2,1,0:T(8,128)S(1)}, u32[]{:S(2)}, u32[]{:S(2)}) collective-permute-start(f32[6,32,128]{2,1,0:T(8,128)S(1)} %get-tuple-element.55), channel_id=1, source_target_pairs={{0,16},{8,24},{16,0},{24,8},{1,17},{9,25},{17,1},{25,9},{2,18},{10... | collective-permute-start | bytes 294920 | tf_op jit(solution)/shard_map/next_to_columns/ppermute | solution.py:454
  21.7 1.5 %collective-permute-start.6 = (f32[6,32,128]{2,1,0:T(8,128)S(1)}, f32[6,32,128]{2,1,0:T(8,128)S(1)}, u32[]{:S(2)}, u32[]{:S(2)}) collective-permute-start(f32[6,32,128]{2,1,0:T(8,128)S(1)} %get-tuple-element.56), channel_id=1, source_target_pairs={{0,24},{8,16},{16,8},{24,0},{1,25},{9,17},{17,9},{25,1},{2,26},{10... | collective-permute-start | bytes 294920 | tf_op jit(solution)/shard_map/next_to_columns/ppermute | solution.py:454
  23.2 6.9 %inner_terms.2 = (f32[12,128,128]{2,1,0:T(8,128)S(1)}, f32[3072,128]{1,0:T(8,128)S(1)}, f32[9216,128]{1,0:T(8,128)S(1)}, bf16[3072,256]{1,0:T(8,128)(2,1)S(1)}, ...) custom-call(s32[2048]{0:T(1024)S(1)} %get-tuple-element.45.codes_ref, f32[128,128]{1,0:T(8,128)S(1)} %get-tuple-element.46.coeffs_ref, ...), custom_call_target="tpu_custom_call" | custom-call | flops 12000000000 | bytes 10000000 | tf_op jit(solution)/shard_map/inner_terms/pallas_call | solution.py:462
  30.2 0.1 collective-permute-start.11
  30.2 2.8 %inner_terms.3 = (f32[2,256,128]{2,1,0:T(8,128)S(1)}, f32[6144,128]{1,0:T(8,128)S(1)}) custom-call(s32[2048]{0:T(1024)S(1)} %get-tuple-element.45.codes_ref, f32[3072,128]{1,0:T(8,128)S(1)} %get-tuple-element.73.carry_ref, f32[9216,128]{1,0:T(8,128)S(1)} %get-tuple-element.74.slope_ref, ...), custom_call_target="tpu_custom_call", output_to_operand_aliasing={{1}: (4, {})} | custom-call | flops 8000000000 | bytes 10000000 | tf_op jit(solution)/shard_map/inner_terms/pallas_call | solution.py:482
  33.0 3.0 %edge_terms.5 = (f32[1024,128]{1,0:T(8,128)S(1)}, f32[3072,128]{1,0:T(8,128)S(1)}, bf16[3072,256]{1,0:T(8,128)(2,1)S(1)}, f32[256,128]{1,0:T(8,128)S(1)}, f32[6144,128]{1,0:T(8,128)S(1)}) custom-call(s32[2048]{0:T(1024)S(1)} %get-tuple-element.45.codes_ref, f32[128,128]{1,0:T(8,128)S(1)} %get-tuple-element.46.coeffs_ref, ...), custom_call_target="tpu_custom_call" | custom-call | tf_op jit(solution)/shard_map/edge_terms/pallas_call | solution.py:493
  36.1 1.5 %collective-permute-start.12 = (f32[256,128]{1,0:T(8,128)S(1)}, f32[256,128]{1,0:T(8,128)S(1)}, u32[]{:S(2)}, u32[]{:S(2)}) collective-permute-start(f32[256,128]{1,0:T(8,128)S(1)} %get-tuple-element.78), channel_id=1, source_target_pairs={{0,24},{8,16},{16,8},{24,0},{1,25},{9,17},{17,9},{25,1},{2,26},{10... | collective-permute-start | bytes 393224 | tf_op jit(solution)/shard_map/sum_over_columns/ppermute | solution.py:512
  37.5 1.7 %edge_terms.6 = (f32[256,128]{1,0:T(8,128)S(1)}, f32[6144,128]{1,0:T(8,128)S(1)}) custom-call(s32[2048]{0:T(1024)S(1)} %get-tuple-element.45.codes_ref, f32[1024,128]{1,0:T(8,128)S(1)} %get-tuple-element.70.carry_ref, f32[3072,128]{1,0:T(8,128)S(1)} %get-tuple-element.71.slope_ref, bf16[3072,256]{1,0:T(8,128)(2,1)S(1)} %get-tuple-element.72.rhs_ref, ...), custom_call_target="tpu_custom_call" | custom-call | flops 100000000 | bytes 100000 | tf_op jit(solution)/shard_map/edge_terms/pallas_call | solution.py:521
  39.2 1.2 %collective-permute-start.13 = (f32[256,128]{1,0:T(8,128)S(1)}, f32[256,128]{1,0:T(8,128)S(1)}, u32[]{:S(2)}, u32[]{:S(2)}) collective-permute-start(f32[256,128]{1,0:T(8,128)S(1)} %get-tuple-element.81), channel_id=1, source_target_pairs={{0,16},{8,24},{16,0},{24,8},{1,17},{9,25},{17,1},{25,9},{2,18},{10... | collective-permute-start | bytes 393224 | tf_op jit(solution)/shard_map/sum_over_columns/ppermute | solution.py:512
  40.4 1.1 %edge_terms.7.after_ref = f32[256,128]{1,0:T(8,128)S(1)} custom-call(bf16[3072,256]{1,0:T(8,128)(2,1)S(1)} %get-tuple-element.72.rhs_ref, f32[2,256,128]{2,1,0:T(8,128)S(1)} %get-tuple-element.84.inner_ref, f32[6144,128]{1,0:T(8,128)S(1)} %get-tuple-element.83.picked_ref), custom_call_target="tpu_custom_call" | custom-call | flops 100000000 | bytes 100000 | tf_op jit(solution)/shard_map/edge_terms/pallas_call | solution.py:531
  41.5 1.0 %collective-permute-start.14 = (f32[256,128]{1,0:T(8,128)S(1)}, f32[256,128]{1,0:T(8,128)S(1)}, u32[]{:S(2)}, u32[]{:S(2)}) collective-permute-start(f32[256,128]{1,0:T(8,128)S(1)} %edge_terms.7.after_ref), channel_id=1, source_target_pairs={{0,8},{8,0},{16,24},{24,16},{1,9},{9,1},{17,25},{25,17},{2,10},{10... | collective-permute-start | bytes 393224 | tf_op jit(solution)/shard_map/sum_over_columns/ppermute | solution.py:512
  42.5 2.3 %edge_terms.8.own_ref = f32[256,128]{1,0:T(8,128)S(1)} custom-call(s32[2048]{0:T(1024)S(1)} %get-tuple-element.45.codes_ref, f32[1024,128]{1,0:T(8,128)S(1)} %get-tuple-element.70.carry_ref, f32[3072,128]{1,0:T(8,128)S(1)} %get-tuple-element.71.slope_ref, bf16[3072,256]{1,0:T(8,128)(2,1)S(1)} %get-tuple-element.72.rhs_ref, ...), custom_call_target="tpu_custom_call" | custom-call | flops 100000000 | bytes 100000 | tf_op jit(solution)/shard_map/edge_terms/pallas_call | solution.py:540
  44.8 0.9 %collective-permute-done.13.refs_1_ = f32[256,128]{1,0:T(8,128)S(1)} collective-permute-done((f32[256,128]{1,0:T(8,128)S(1)}, f32[256,128]{1,0:T(8,128)S(1)}, u32[]{:S(2)}, u32[]{:S(2)}) %collective-permute-start.13) | collective-permute-done | bytes 131104 | tf_op jit(solution)/shard_map/sum_over_columns/ppermute | solution.py:512
  45.8 1.1 %collective-permute-done.14 = f32[256,128]{1,0:T(8,128)S(1)} collective-permute-done((f32[256,128]{1,0:T(8,128)S(1)}, f32[256,128]{1,0:T(8,128)S(1)}, u32[]{:S(2)}, u32[]{:S(2)}) %collective-permute-start.14) | collective-permute-done | bytes 131104 | tf_op jit(solution)/shard_map/sum_over_columns/ppermute | solution.py:512
  46.9 2.3 %collective-permute-start.17 = (f32[64,128]{1,0:T(8,128)S(1)}, f32[64,128]{1,0:T(8,128)S(1)}, u32[]{:S(2)}, u32[]{:S(2)}) collective-permute-start(f32[64,128]{1,0:T(8,128)S(1)} %get-tuple-element.89), channel_id=1, source_target_pairs={{0,6},{1,7},{2,4},{3,5},{4,2},{5,3},{6,0},{7,1},{8,14},{9,15},{10,... | collective-permute-start | bytes 98312 | tf_op jit(solution)/shard_map/sum_over_chips/ppermute | solution.py:563
  49.2 2.1 %collective-permute-start.15 = (f32[64,128]{1,0:T(8,128)S(1)}, f32[64,128]{1,0:T(8,128)S(1)}, u32[]{:S(2)}, u32[]{:S(2)}) collective-permute-start(f32[64,128]{1,0:T(8,128)S(1)} %get-tuple-element.91), channel_id=1, source_target_pairs={{0,2},{1,3},{2,0},{3,1},{4,6},{5,7},{6,4},{7,5},{8,10},{9,11},{10,... | collective-permute-start | bytes 98312 | tf_op jit(solution)/shard_map/sum_over_chips/ppermute | solution.py:563
  51.4 1.3 %collective-permute-done.17 = f32[64,128]{1,0:T(8,128)S(1)} collective-permute-done((f32[64,128]{1,0:T(8,128)S(1)}, f32[64,128]{1,0:T(8,128)S(1)}, u32[]{:S(2)}, u32[]{:S(2)}) %collective-permute-start.17) | collective-permute-done | bytes 32800 | tf_op jit(solution)/shard_map/sum_over_chips/ppermute | solution.py:563
  52.7 1.4 %collective-permute-done.16 = f32[64,128]{1,0:T(8,128)S(1)} collective-permute-done((f32[64,128]{1,0:T(8,128)S(1)}, f32[64,128]{1,0:T(8,128)S(1)}, u32[]{:S(2)}, u32[]{:S(2)}) %collective-permute-start.16) | collective-permute-done | bytes 32800 | tf_op jit(solution)/shard_map/sum_over_chips/ppermute | solution.py:563
  54.0 0.6 %fusion = f32[64,128]{1,0:T(8,128)} fusion(f32[256,128]{1,0:T(8,128)S(1)} %add.12, f32[64,128]{1,0:T(8,128)S(1)} %collective-permute-done.15, f32[64,128]{1,0:T(8,128)S(1)} %collective-permute-done.16, f32[64,128]{1,0:T(8,128)S(1)} %collective-permute-done.17), kind=kLoop, calls=%fused_computation.6 | loop fusion | flops 32768 | bytes 163840 | tf_op jit(solution)/shard_map/sum_over_chips/mul | solution.py:566
  (17 shorter events, 0.1 us)
Async XLA Ops:
  2.3 16.2 %collective-permute-start = (f32[4,6,32,128]{3,2,1,0:T(8,128)S(1)}, f32[4,6,32,128]{3,2,1,0:T(8,128)S(1)}, u32[]{:S(2)}, u32[]{:S(2)}) collective-permute-start(f32[4,6,32,128]{3,2,1,0:T(8,128)S(1)} %get-tuple-element.47), channel_id=1, source_target_pairs={{0,7},{1,2},{2,1},{3,4},{4,3},{5,6},{6,5},{7,0},{8,15},{9,10},{10,... | collective-permute-start | bytes 1179656 | tf_op jit(solution)/shard_map/to_next_plane/ppermute | solution.py:447
  6.9 8.0 %collective-permute-start.1 = (f32[13,32,128]{2,1,0:T(8,128)S(1)}, f32[13,32,128]{2,1,0:T(8,128)S(1)}, u32[]{:S(2)}, u32[]{:S(2)}) collective-permute-start(f32[13,32,128]{2,1,0:T(8,128)S(1)} %get-tuple-element.49), channel_id=1, source_target_pairs={{0,8},{8,0},{16,24},{24,16},{1,9},{9,1},{17,25},{25,17},{2,10},{10... | collective-permute-start | bytes 638984 | tf_op jit(solution)/shard_map/to_columns/ppermute | solution.py:449
  8.4 10.2 %collective-permute-start.2 = (f32[13,32,128]{2,1,0:T(8,128)S(1)}, f32[13,32,128]{2,1,0:T(8,128)S(1)}, u32[]{:S(2)}, u32[]{:S(2)}) collective-permute-start(f32[13,32,128]{2,1,0:T(8,128)S(1)} %get-tuple-element.50), channel_id=1, source_target_pairs={{0,16},{8,24},{16,0},{24,8},{1,17},{9,25},{17,1},{25,9},{2,18},{10... | collective-permute-start | bytes 638984 | tf_op jit(solution)/shard_map/to_columns/ppermute | solution.py:449
  9.9 8.7 %collective-permute-start.3 = (f32[13,32,128]{2,1,0:T(8,128)S(1)}, f32[13,32,128]{2,1,0:T(8,128)S(1)}, u32[]{:S(2)}, u32[]{:S(2)}) collective-permute-start(f32[13,32,128]{2,1,0:T(8,128)S(1)} %get-tuple-element.52), channel_id=1, source_target_pairs={{0,24},{8,16},{16,8},{24,0},{1,25},{9,17},{17,9},{25,1},{2,26},{10... | collective-permute-start | bytes 638984 | tf_op jit(solution)/shard_map/to_columns/ppermute | solution.py:449
  18.6 2.1 %collective-permute-start.10 = (f32[13,32,128]{2,1,0:T(8,128)S(1)}, f32[13,32,128]{2,1,0:T(8,128)S(1)}, u32[]{:S(2)}, u32[]{:S(2)}) collective-permute-start(f32[13,32,128]{2,1,0:T(8,128)S(1)} %collective-permute-done.3.refs_3_), channel_id=1, source_target_pairs={{0,1},{1,0},{2,3},{3,2},{4,5},{5,4},{6,7},{7,6},{8,9},{9,8},{10,11... | collective-permute-start | bytes 638984 | tf_op jit(solution)/shard_map/to_other_core/ppermute | solution.py:456
  18.7 3.0 %collective-permute-start.7 = (f32[13,32,128]{2,1,0:T(8,128)S(1)}, f32[13,32,128]{2,1,0:T(8,128)S(1)}, u32[]{:S(2)}, u32[]{:S(2)}) collective-permute-start(f32[13,32,128]{2,1,0:T(8,128)S(1)} %get-tuple-element.57.refs_0_), channel_id=1, source_target_pairs={{0,1},{1,0},{2,3},{3,2},{4,5},{5,4},{6,7},{7,6},{8,9},{9,8},{10,11... | collective-permute-start | bytes 638984 | tf_op jit(solution)/shard_map/to_other_core/ppermute | solution.py:456
  19.2 4.0 %collective-permute-start.8 = (f32[13,32,128]{2,1,0:T(8,128)S(1)}, f32[13,32,128]{2,1,0:T(8,128)S(1)}, u32[]{:S(2)}, u32[]{:S(2)}) collective-permute-start(f32[13,32,128]{2,1,0:T(8,128)S(1)} %collective-permute-done.1.refs_1_), channel_id=1, source_target_pairs={{0,1},{1,0},{2,3},{3,2},{4,5},{5,4},{6,7},{7,6},{8,9},{9,8},{10,11... | collective-permute-start | bytes 638984 | tf_op jit(solution)/shard_map/to_other_core/ppermute | solution.py:456
  19.3 3.9 %collective-permute-start.9 = (f32[13,32,128]{2,1,0:T(8,128)S(1)}, f32[13,32,128]{2,1,0:T(8,128)S(1)}, u32[]{:S(2)}, u32[]{:S(2)}) collective-permute-start(f32[13,32,128]{2,1,0:T(8,128)S(1)} %collective-permute-done.2.refs_2_), channel_id=1, source_target_pairs={{0,1},{1,0},{2,3},{3,2},{4,5},{5,4},{6,7},{7,6},{8,9},{9,8},{10,11... | collective-permute-start | bytes 638984 | tf_op jit(solution)/shard_map/to_other_core/ppermute | solution.py:456
  19.7 10.4 %collective-permute-start.4 = (f32[6,32,128]{2,1,0:T(8,128)S(1)}, f32[6,32,128]{2,1,0:T(8,128)S(1)}, u32[]{:S(2)}, u32[]{:S(2)}) collective-permute-start(f32[6,32,128]{2,1,0:T(8,128)S(1)} %get-tuple-element.54), channel_id=1, source_target_pairs={{0,8},{8,0},{16,24},{24,16},{1,9},{9,1},{17,25},{25,17},{2,10},{10... | collective-permute-start | bytes 294920 | tf_op jit(solution)/shard_map/next_to_columns/ppermute | solution.py:454
  20.7 9.4 %collective-permute-start.5 = (f32[6,32,128]{2,1,0:T(8,128)S(1)}, f32[6,32,128]{2,1,0:T(8,128)S(1)}, u32[]{:S(2)}, u32[]{:S(2)}) collective-permute-start(f32[6,32,128]{2,1,0:T(8,128)S(1)} %get-tuple-element.55), channel_id=1, source_target_pairs={{0,16},{8,24},{16,0},{24,8},{1,17},{9,25},{17,1},{25,9},{2,18},{10... | collective-permute-start | bytes 294920 | tf_op jit(solution)/shard_map/next_to_columns/ppermute | solution.py:454
  21.7 8.4 %collective-permute-start.6 = (f32[6,32,128]{2,1,0:T(8,128)S(1)}, f32[6,32,128]{2,1,0:T(8,128)S(1)}, u32[]{:S(2)}, u32[]{:S(2)}) collective-permute-start(f32[6,32,128]{2,1,0:T(8,128)S(1)} %get-tuple-element.56), channel_id=1, source_target_pairs={{0,24},{8,16},{16,8},{24,0},{1,25},{9,17},{17,9},{25,1},{2,26},{10... | collective-permute-start | bytes 294920 | tf_op jit(solution)/shard_map/next_to_columns/ppermute | solution.py:454
  30.2 2.9 %collective-permute-start.11 = (f32[4,6,32,128]{3,2,1,0:T(8,128)S(1)}, f32[4,6,32,128]{3,2,1,0:T(8,128)S(1)}, u32[]{:S(2)}, u32[]{:S(2)}) collective-permute-start(f32[4,6,32,128]{3,2,1,0:T(8,128)S(1)} %pad_maximum_fusion), channel_id=1, source_target_pairs={{0,1},{1,0},{2,3},{3,2},{4,5},{5,4},{6,7},{7,6},{8,9},{9,8},{10,11... | collective-permute-start | bytes 1179656 | tf_op jit(solution)/shard_map/next_to_other_core/ppermute | solution.py:480
  36.1 9.7 %collective-permute-start.12 = (f32[256,128]{1,0:T(8,128)S(1)}, f32[256,128]{1,0:T(8,128)S(1)}, u32[]{:S(2)}, u32[]{:S(2)}) collective-permute-start(f32[256,128]{1,0:T(8,128)S(1)} %get-tuple-element.78), channel_id=1, source_target_pairs={{0,24},{8,16},{16,8},{24,0},{1,25},{9,17},{17,9},{25,1},{2,26},{10... | collective-permute-start | bytes 393224 | tf_op jit(solution)/shard_map/sum_over_columns/ppermute | solution.py:512
  39.2 6.5 %collective-permute-start.13 = (f32[256,128]{1,0:T(8,128)S(1)}, f32[256,128]{1,0:T(8,128)S(1)}, u32[]{:S(2)}, u32[]{:S(2)}) collective-permute-start(f32[256,128]{1,0:T(8,128)S(1)} %get-tuple-element.81), channel_id=1, source_target_pairs={{0,16},{8,24},{16,0},{24,8},{1,17},{9,25},{17,1},{25,9},{2,18},{10... | collective-permute-start | bytes 393224 | tf_op jit(solution)/shard_map/sum_over_columns/ppermute | solution.py:512
  41.5 5.4 %collective-permute-start.14 = (f32[256,128]{1,0:T(8,128)S(1)}, f32[256,128]{1,0:T(8,128)S(1)}, u32[]{:S(2)}, u32[]{:S(2)}) collective-permute-start(f32[256,128]{1,0:T(8,128)S(1)} %edge_terms.7.after_ref), channel_id=1, source_target_pairs={{0,8},{8,0},{16,24},{24,16},{1,9},{9,1},{17,25},{25,17},{2,10},{10... | collective-permute-start | bytes 393224 | tf_op jit(solution)/shard_map/sum_over_columns/ppermute | solution.py:512
  46.9 5.8 %collective-permute-start.17 = (f32[64,128]{1,0:T(8,128)S(1)}, f32[64,128]{1,0:T(8,128)S(1)}, u32[]{:S(2)}, u32[]{:S(2)}) collective-permute-start(f32[64,128]{1,0:T(8,128)S(1)} %get-tuple-element.89), channel_id=1, source_target_pairs={{0,6},{1,7},{2,4},{3,5},{4,2},{5,3},{6,0},{7,1},{8,14},{9,15},{10,... | collective-permute-start | bytes 98312 | tf_op jit(solution)/shard_map/sum_over_chips/ppermute | solution.py:563
  49.2 4.8 %collective-permute-start.16 = (f32[64,128]{1,0:T(8,128)S(1)}, f32[64,128]{1,0:T(8,128)S(1)}, u32[]{:S(2)}, u32[]{:S(2)}) collective-permute-start(f32[64,128]{1,0:T(8,128)S(1)} %get-tuple-element.90), channel_id=1, source_target_pairs={{0,4},{1,5},{2,6},{3,7},{4,0},{5,1},{6,2},{7,3},{8,12},{9,13},{10,... | collective-permute-start | bytes 98312 | tf_op jit(solution)/shard_map/sum_over_chips/ppermute | solution.py:563
  49.2 4.8 %collective-permute-start.15 = (f32[64,128]{1,0:T(8,128)S(1)}, f32[64,128]{1,0:T(8,128)S(1)}, u32[]{:S(2)}, u32[]{:S(2)}) collective-permute-start(f32[64,128]{1,0:T(8,128)S(1)} %get-tuple-element.91), channel_id=1, source_target_pairs={{0,2},{1,3},{2,0},{3,1},{4,6},{5,7},{6,4},{7,5},{8,10},{9,11},{10,... | collective-permute-start | bytes 98312 | tf_op jit(solution)/shard_map/sum_over_chips/ppermute | solution.py:563

commit v19 on v18

--- a/solution.py
+++ b/solution.py
@@ -448,12 +448,13 @@
     with jax.named_scope("to_columns"):
         own = [packed[0]] + [lax.ppermute(packed[peer], "tm", across(peer)) for peer in range(1, tm_count)]
     with jax.named_scope("next_to_columns"):
+        early_other = [lax.ppermute(piece, "space", swap) for piece in own[:3]]
         across_edge, own[:3] = lax.optimization_barrier((across_edge, own[:3]))
         parts = [across_edge[peer] for peer in range(tm_count)]
         parts, own[3:] = lax.optimization_barrier((parts, own[3:]))
         next_own = [parts[0]] + [lax.ppermute(parts[peer], "tm", across(peer)) for peer in range(1, tm_count)]
     with jax.named_scope("to_other_core"):
-        other = [lax.ppermute(piece, "space", swap) for piece in own]
+        other = early_other + [lax.ppermute(piece, "space", swap) for piece in own[3:]]
     early = tm_count // 2
     picked = pltpu.VMEM((block * 3 * height, lanes), F32)
     held_codes = [pltpu.SMEM(codes.shape, jnp.int32), pltpu.SemaphoreType.DMA]

time: 54.8 us -> 53.8 us (0.982)
  no operation moved by 1% of the time
where the time goes in v19:
time: 53.8 us; the launch traced here: 53.6 us
  starting transfers between devices  20.3 us (38%)
  Pallas kernels  20.1 us (37%)
  waiting for transfers between devices  12.4 us (23%)
  other arithmetic  0.67 us (1%)
    ppermute x3, waiting for transfers between devices, shards(): lax.ppermute(packed[peer], 'tm', across(peer))  8.18 us
    pallas_call x1, Pallas kernels, shards(): pl.pallas_call(functools.partial(inner_kernel, first_peer=early, sizes=(l...  6.87 us
    ppermute x1, starting transfers between devices, shards(): across_edge = lax.ppermute(packed[tm_count], 'space', ring)  4.55 us
    ppermute x3, starting transfers between devices, shards(): part = lax.ppermute(shares[step], 'space', pairing)  4.45 us
    ppermute x3, starting transfers between devices, shards(): arrived.append(lax.ppermute(summed, 'tm', across(peer + 1)))  3.68 us
    ppermute x3, starting transfers between devices, shards(): lax.ppermute(parts[peer], 'tm', across(peer))  3.49 us
    ppermute x3, starting transfers between devices, shards(): lax.ppermute(packed[peer], 'tm', across(peer))  3.49 us
    pallas_call x1, Pallas kernels, shards(): pl.pallas_call(functools.partial(far_kernel, peer=tm_count - 1, sizes=(lo...  3.03 us
  transfers between devices with their start and end apart: 18, of which 6 were waited for; matrix products, arithmetic and copies ran while one was open for 0% of the time, Pallas kernels for 27%

profile of v19, /device:TPU:0, one launch (start us, length us, event | category | flops | bytes accessed | tf_op | source)
XLA Modules:
  0.0 53.6 jit_solution(13944556658583615827)
XLA Ops:
  0.0 2.3 %pack.1 = (f32[13,32,128]{2,1,0:T(8,128)S(1)}, f32[13,32,128]{2,1,0:T(8,128)S(1)}, f32[13,32,128]{2,1,0:T(8,128)S(1)}, f32[13,32,128]{2,1,0:T(8,128)S(1)}, f32[4...) custom-call(f32[32,3,16,128]{3,2,1,0:T(8,128)} %bitcast.18, s32[2,2048]{1,0:T(2,128)} %bitcast.19, ...), custom_call_target="tpu_custom_call" | custom-call | tf_op jit(solution)/shard_map/pack/pallas_call | solution.py:421
  2.3 4.6 %collective-permute-start = (f32[4,6,32,128]{3,2,1,0:T(8,128)S(1)}, f32[4,6,32,128]{3,2,1,0:T(8,128)S(1)}, u32[]{:S(2)}, u32[]{:S(2)}) collective-permute-start(f32[4,6,32,128]{3,2,1,0:T(8,128)S(1)} %get-tuple-element.47), channel_id=1, source_target_pairs={{0,7},{1,2},{2,1},{3,4},{4,3},{5,6},{6,5},{7,0},{8,15},{9,10},{10,... | collective-permute-start | bytes 1179656 | tf_op jit(solution)/shard_map/to_next_plane/ppermute | solution.py:447
  6.9 1.5 %collective-permute-start.1 = (f32[13,32,128]{2,1,0:T(8,128)S(1)}, f32[13,32,128]{2,1,0:T(8,128)S(1)}, u32[]{:S(2)}, u32[]{:S(2)}) collective-permute-start(f32[13,32,128]{2,1,0:T(8,128)S(1)} %get-tuple-element.49), channel_id=1, source_target_pairs={{0,8},{8,0},{16,24},{24,16},{1,9},{9,1},{17,25},{25,17},{2,10},{10... | collective-permute-start | bytes 638984 | tf_op jit(solution)/shard_map/to_columns/ppermute | solution.py:449
  8.4 1.5 %collective-permute-start.2 = (f32[13,32,128]{2,1,0:T(8,128)S(1)}, f32[13,32,128]{2,1,0:T(8,128)S(1)}, u32[]{:S(2)}, u32[]{:S(2)}) collective-permute-start(f32[13,32,128]{2,1,0:T(8,128)S(1)} %get-tuple-element.50), channel_id=1, source_target_pairs={{0,16},{8,24},{16,0},{24,8},{1,17},{9,25},{17,1},{25,9},{2,18},{10... | collective-permute-start | bytes 638984 | tf_op jit(solution)/shard_map/to_columns/ppermute | solution.py:449
  9.9 0.5 collective-permute-start.3
  10.4 4.6 %collective-permute-done.1.refs_1_ = f32[13,32,128]{2,1,0:T(8,128)S(1)} collective-permute-done((f32[13,32,128]{2,1,0:T(8,128)S(1)}, f32[13,32,128]{2,1,0:T(8,128)S(1)}, u32[]{:S(2)}, u32[]{:S(2)}) %collective-permute-start.1) | collective-permute-done | bytes 213024 | tf_op jit(solution)/shard_map/to_columns/ppermute | solution.py:449
  14.9 0.0 collective-permute-start.8
  14.9 3.6 %collective-permute-done.2.refs_2_ = f32[13,32,128]{2,1,0:T(8,128)S(1)} collective-permute-done((f32[13,32,128]{2,1,0:T(8,128)S(1)}, f32[13,32,128]{2,1,0:T(8,128)S(1)}, u32[]{:S(2)}, u32[]{:S(2)}) %collective-permute-start.2) | collective-permute-done | bytes 213024 | tf_op jit(solution)/shard_map/to_columns/ppermute | solution.py:449
  18.6 0.0 collective-permute-start.9
  18.6 0.0 collective-permute-done
  18.6 0.0 collective-permute-done.3.refs_3_
  18.6 0.6 %collective-permute-start.10 = (f32[13,32,128]{2,1,0:T(8,128)S(1)}, f32[13,32,128]{2,1,0:T(8,128)S(1)}, u32[]{:S(2)}, u32[]{:S(2)}) collective-permute-start(f32[13,32,128]{2,1,0:T(8,128)S(1)} %collective-permute-done.3.refs_3_), channel_id=1, source_target_pairs={{0,1},{1,0},{2,3},{3,2},{4,5},{5,4},{6,7},{7,6},{8,9},{9,8},{10,11... | collective-permute-start | bytes 638984 | tf_op jit(solution)/shard_map/to_other_core/ppermute | solution.py:457
  19.2 0.5 collective-permute-start.4
  19.7 1.4 %collective-permute-start.5 = (f32[6,32,128]{2,1,0:T(8,128)S(1)}, f32[6,32,128]{2,1,0:T(8,128)S(1)}, u32[]{:S(2)}, u32[]{:S(2)}) collective-permute-start(f32[6,32,128]{2,1,0:T(8,128)S(1)} %get-tuple-element.55), channel_id=1, source_target_pairs={{0,16},{8,24},{16,0},{24,8},{1,17},{9,25},{17,1},{25,9},{2,18},{10... | collective-permute-start | bytes 294920 | tf_op jit(solution)/shard_map/next_to_columns/ppermute | solution.py:455
  21.2 1.5 %collective-permute-start.6 = (f32[6,32,128]{2,1,0:T(8,128)S(1)}, f32[6,32,128]{2,1,0:T(8,128)S(1)}, u32[]{:S(2)}, u32[]{:S(2)}) collective-permute-start(f32[6,32,128]{2,1,0:T(8,128)S(1)} %get-tuple-element.56), channel_id=1, source_target_pairs={{0,24},{8,16},{16,8},{24,0},{1,25},{9,17},{17,9},{25,1},{2,26},{10... | collective-permute-start | bytes 294920 | tf_op jit(solution)/shard_map/next_to_columns/ppermute | solution.py:455
  22.7 6.9 %inner_terms.2 = (f32[12,128,128]{2,1,0:T(8,128)S(1)}, f32[3072,128]{1,0:T(8,128)S(1)}, f32[9216,128]{1,0:T(8,128)S(1)}, bf16[3072,256]{1,0:T(8,128)(2,1)S(1)}, ...) custom-call(s32[2048]{0:T(1024)S(1)} %get-tuple-element.45.codes_ref, f32[128,128]{1,0:T(8,128)S(1)} %get-tuple-element.46.coeffs_ref, ...), custom_call_target="tpu_custom_call" | custom-call | flops 12000000000 | bytes 10000000 | tf_op jit(solution)/shard_map/inner_terms/pallas_call | solution.py:463
  29.6 0.1 collective-permute-start.11
  29.7 2.8 %inner_terms.3 = (f32[2,256,128]{2,1,0:T(8,128)S(1)}, f32[6144,128]{1,0:T(8,128)S(1)}) custom-call(s32[2048]{0:T(1024)S(1)} %get-tuple-element.45.codes_ref, f32[3072,128]{1,0:T(8,128)S(1)} %get-tuple-element.73.carry_ref, f32[9216,128]{1,0:T(8,128)S(1)} %get-tuple-element.74.slope_ref, ...), custom_call_target="tpu_custom_call", output_to_operand_aliasing={{1}: (4, {})} | custom-call | flops 8000000000 | bytes 10000000 | tf_op jit(solution)/shard_map/inner_terms/pallas_call | solution.py:483
  32.5 3.0 %edge_terms.5 = (f32[1024,128]{1,0:T(8,128)S(1)}, f32[3072,128]{1,0:T(8,128)S(1)}, bf16[3072,256]{1,0:T(8,128)(2,1)S(1)}, f32[256,128]{1,0:T(8,128)S(1)}, f32[6144,128]{1,0:T(8,128)S(1)}) custom-call(s32[2048]{0:T(1024)S(1)} %get-tuple-element.45.codes_ref, f32[128,128]{1,0:T(8,128)S(1)} %get-tuple-element.46.coeffs_ref, ...), custom_call_target="tpu_custom_call" | custom-call | tf_op jit(solution)/shard_map/edge_terms/pallas_call | solution.py:494
  35.5 1.5 %collective-permute-start.12 = (f32[256,128]{1,0:T(8,128)S(1)}, f32[256,128]{1,0:T(8,128)S(1)}, u32[]{:S(2)}, u32[]{:S(2)}) collective-permute-start(f32[256,128]{1,0:T(8,128)S(1)} %get-tuple-element.78), channel_id=1, source_target_pairs={{0,24},{8,16},{16,8},{24,0},{1,25},{9,17},{17,9},{25,1},{2,26},{10... | collective-permute-start | bytes 393224 | tf_op jit(solution)/shard_map/sum_over_columns/ppermute | solution.py:513
  37.0 1.7 %edge_terms.6 = (f32[256,128]{1,0:T(8,128)S(1)}, f32[6144,128]{1,0:T(8,128)S(1)}) custom-call(s32[2048]{0:T(1024)S(1)} %get-tuple-element.45.codes_ref, f32[1024,128]{1,0:T(8,128)S(1)} %get-tuple-element.70.carry_ref, f32[3072,128]{1,0:T(8,128)S(1)} %get-tuple-element.71.slope_ref, bf16[3072,256]{1,0:T(8,128)(2,1)S(1)} %get-tuple-element.72.rhs_ref, ...), custom_call_target="tpu_custom_call" | custom-call | flops 100000000 | bytes 100000 | tf_op jit(solution)/shard_map/edge_terms/pallas_call | solution.py:522
  38.7 0.7 %collective-permute-start.13 = (f32[256,128]{1,0:T(8,128)S(1)}, f32[256,128]{1,0:T(8,128)S(1)}, u32[]{:S(2)}, u32[]{:S(2)}) collective-permute-start(f32[256,128]{1,0:T(8,128)S(1)} %get-tuple-element.81), channel_id=1, source_target_pairs={{0,16},{8,24},{16,0},{24,8},{1,17},{9,25},{17,1},{25,9},{2,18},{10... | collective-permute-start | bytes 393224 | tf_op jit(solution)/shard_map/sum_over_columns/ppermute | solution.py:513
  39.4 1.1 %edge_terms.7.after_ref = f32[256,128]{1,0:T(8,128)S(1)} custom-call(bf16[3072,256]{1,0:T(8,128)(2,1)S(1)} %get-tuple-element.72.rhs_ref, f32[2,256,128]{2,1,0:T(8,128)S(1)} %get-tuple-element.84.inner_ref, f32[6144,128]{1,0:T(8,128)S(1)} %get-tuple-element.83.picked_ref), custom_call_target="tpu_custom_call" | custom-call | flops 100000000 | bytes 100000 | tf_op jit(solution)/shard_map/edge_terms/pallas_call | solution.py:532
  40.4 1.5 %collective-permute-start.14 = (f32[256,128]{1,0:T(8,128)S(1)}, f32[256,128]{1,0:T(8,128)S(1)}, u32[]{:S(2)}, u32[]{:S(2)}) collective-permute-start(f32[256,128]{1,0:T(8,128)S(1)} %edge_terms.7.after_ref), channel_id=1, source_target_pairs={{0,8},{8,0},{16,24},{24,16},{1,9},{9,1},{17,25},{25,17},{2,10},{10... | collective-permute-start | bytes 393224 | tf_op jit(solution)/shard_map/sum_over_columns/ppermute | solution.py:513
  42.0 2.3 %edge_terms.8.own_ref = f32[256,128]{1,0:T(8,128)S(1)} custom-call(s32[2048]{0:T(1024)S(1)} %get-tuple-element.45.codes_ref, f32[1024,128]{1,0:T(8,128)S(1)} %get-tuple-element.70.carry_ref, f32[3072,128]{1,0:T(8,128)S(1)} %get-tuple-element.71.slope_ref, bf16[3072,256]{1,0:T(8,128)(2,1)S(1)} %get-tuple-element.72.rhs_ref, ...), custom_call_target="tpu_custom_call" | custom-call | flops 100000000 | bytes 100000 | tf_op jit(solution)/shard_map/edge_terms/pallas_call | solution.py:541
  44.3 0.9 %collective-permute-done.13.refs_1_ = f32[256,128]{1,0:T(8,128)S(1)} collective-permute-done((f32[256,128]{1,0:T(8,128)S(1)}, f32[256,128]{1,0:T(8,128)S(1)}, u32[]{:S(2)}, u32[]{:S(2)}) %collective-permute-start.13) | collective-permute-done | bytes 131104 | tf_op jit(solution)/shard_map/sum_over_columns/ppermute | solution.py:513
  45.2 0.6 %collective-permute-done.14 = f32[256,128]{1,0:T(8,128)S(1)} collective-permute-done((f32[256,128]{1,0:T(8,128)S(1)}, f32[256,128]{1,0:T(8,128)S(1)}, u32[]{:S(2)}, u32[]{:S(2)}) %collective-permute-start.14) | collective-permute-done | bytes 131104 | tf_op jit(solution)/shard_map/sum_over_columns/ppermute | solution.py:513
  45.9 2.3 %collective-permute-start.17 = (f32[64,128]{1,0:T(8,128)S(1)}, f32[64,128]{1,0:T(8,128)S(1)}, u32[]{:S(2)}, u32[]{:S(2)}) collective-permute-start(f32[64,128]{1,0:T(8,128)S(1)} %get-tuple-element.89), channel_id=1, source_target_pairs={{0,6},{1,7},{2,4},{3,5},{4,2},{5,3},{6,0},{7,1},{8,14},{9,15},{10,... | collective-permute-start | bytes 98312 | tf_op jit(solution)/shard_map/sum_over_chips/ppermute | solution.py:564
  48.2 2.1 %collective-permute-start.15 = (f32[64,128]{1,0:T(8,128)S(1)}, f32[64,128]{1,0:T(8,128)S(1)}, u32[]{:S(2)}, u32[]{:S(2)}) collective-permute-start(f32[64,128]{1,0:T(8,128)S(1)} %get-tuple-element.91), channel_id=1, source_target_pairs={{0,2},{1,3},{2,0},{3,1},{4,6},{5,7},{6,4},{7,5},{8,10},{9,11},{10,... | collective-permute-start | bytes 98312 | tf_op jit(solution)/shard_map/sum_over_chips/ppermute | solution.py:564
  50.3 1.3 %collective-permute-done.17 = f32[64,128]{1,0:T(8,128)S(1)} collective-permute-done((f32[64,128]{1,0:T(8,128)S(1)}, f32[64,128]{1,0:T(8,128)S(1)}, u32[]{:S(2)}, u32[]{:S(2)}) %collective-permute-start.17) | collective-permute-done | bytes 32800 | tf_op jit(solution)/shard_map/sum_over_chips/ppermute | solution.py:564
  51.7 1.4 %collective-permute-done.16 = f32[64,128]{1,0:T(8,128)S(1)} collective-permute-done((f32[64,128]{1,0:T(8,128)S(1)}, f32[64,128]{1,0:T(8,128)S(1)}, u32[]{:S(2)}, u32[]{:S(2)}) %collective-permute-start.16) | collective-permute-done | bytes 32800 | tf_op jit(solution)/shard_map/sum_over_chips/ppermute | solution.py:564
  53.0 0.6 %fusion = f32[64,128]{1,0:T(8,128)} fusion(f32[256,128]{1,0:T(8,128)S(1)} %add.12, f32[64,128]{1,0:T(8,128)S(1)} %collective-permute-done.15, f32[64,128]{1,0:T(8,128)S(1)} %collective-permute-done.16, f32[64,128]{1,0:T(8,128)S(1)} %collective-permute-done.17), kind=kLoop, calls=%fused_computation.6 | loop fusion | flops 32768 | bytes 163840 | tf_op jit(solution)/shard_map/sum_over_chips/mul | solution.py:567
  (17 shorter events, 0.1 us)
Async XLA Ops:
  2.3 16.2 %collective-permute-start = (f32[4,6,32,128]{3,2,1,0:T(8,128)S(1)}, f32[4,6,32,128]{3,2,1,0:T(8,128)S(1)}, u32[]{:S(2)}, u32[]{:S(2)}) collective-permute-start(f32[4,6,32,128]{3,2,1,0:T(8,128)S(1)} %get-tuple-element.47), channel_id=1, source_target_pairs={{0,7},{1,2},{2,1},{3,4},{4,3},{5,6},{6,5},{7,0},{8,15},{9,10},{10,... | collective-permute-start | bytes 1179656 | tf_op jit(solution)/shard_map/to_next_plane/ppermute | solution.py:447
  6.9 8.0 %collective-permute-start.1 = (f32[13,32,128]{2,1,0:T(8,128)S(1)}, f32[13,32,128]{2,1,0:T(8,128)S(1)}, u32[]{:S(2)}, u32[]{:S(2)}) collective-permute-start(f32[13,32,128]{2,1,0:T(8,128)S(1)} %get-tuple-element.49), channel_id=1, source_target_pairs={{0,8},{8,0},{16,24},{24,16},{1,9},{9,1},{17,25},{25,17},{2,10},{10... | collective-permute-start | bytes 638984 | tf_op jit(solution)/shard_map/to_columns/ppermute | solution.py:449
  8.4 10.2 %collective-permute-start.2 = (f32[13,32,128]{2,1,0:T(8,128)S(1)}, f32[13,32,128]{2,1,0:T(8,128)S(1)}, u32[]{:S(2)}, u32[]{:S(2)}) collective-permute-start(f32[13,32,128]{2,1,0:T(8,128)S(1)} %get-tuple-element.50), channel_id=1, source_target_pairs={{0,16},{8,24},{16,0},{24,8},{1,17},{9,25},{17,1},{25,9},{2,18},{10... | collective-permute-start | bytes 638984 | tf_op jit(solution)/shard_map/to_columns/ppermute | solution.py:449
  9.9 8.7 %collective-permute-start.3 = (f32[13,32,128]{2,1,0:T(8,128)S(1)}, f32[13,32,128]{2,1,0:T(8,128)S(1)}, u32[]{:S(2)}, u32[]{:S(2)}) collective-permute-start(f32[13,32,128]{2,1,0:T(8,128)S(1)} %get-tuple-element.52), channel_id=1, source_target_pairs={{0,24},{8,16},{16,8},{24,0},{1,25},{9,17},{17,9},{25,1},{2,26},{10... | collective-permute-start | bytes 638984 | tf_op jit(solution)/shard_map/to_columns/ppermute | solution.py:449
  10.4 9.3 %collective-permute-start.7 = (f32[13,32,128]{2,1,0:T(8,128)S(1)}, f32[13,32,128]{2,1,0:T(8,128)S(1)}, u32[]{:S(2)}, u32[]{:S(2)}) collective-permute-start(f32[13,32,128]{2,1,0:T(8,128)S(1)} %get-tuple-element.57.refs_0_), channel_id=1, source_target_pairs={{0,1},{1,0},{2,3},{3,2},{4,5},{5,4},{6,7},{7,6},{8,9},{9,8},{10,11... | collective-permute-start | bytes 638984 | tf_op jit(solution)/shard_map/next_to_columns/ppermute | solution.py:451
  14.9 6.2 %collective-permute-start.8 = (f32[13,32,128]{2,1,0:T(8,128)S(1)}, f32[13,32,128]{2,1,0:T(8,128)S(1)}, u32[]{:S(2)}, u32[]{:S(2)}) collective-permute-start(f32[13,32,128]{2,1,0:T(8,128)S(1)} %collective-permute-done.1.refs_1_), channel_id=1, source_target_pairs={{0,1},{1,0},{2,3},{3,2},{4,5},{5,4},{6,7},{7,6},{8,9},{9,8},{10,11... | collective-permute-start | bytes 638984 | tf_op jit(solution)/shard_map/next_to_columns/ppermute | solution.py:451
  18.6 4.1 %collective-permute-start.9 = (f32[13,32,128]{2,1,0:T(8,128)S(1)}, f32[13,32,128]{2,1,0:T(8,128)S(1)}, u32[]{:S(2)}, u32[]{:S(2)}) collective-permute-start(f32[13,32,128]{2,1,0:T(8,128)S(1)} %collective-permute-done.2.refs_2_), channel_id=1, source_target_pairs={{0,1},{1,0},{2,3},{3,2},{4,5},{5,4},{6,7},{7,6},{8,9},{9,8},{10,11... | collective-permute-start | bytes 638984 | tf_op jit(solution)/shard_map/next_to_columns/ppermute | solution.py:451
  18.6 4.1 %collective-permute-start.10 = (f32[13,32,128]{2,1,0:T(8,128)S(1)}, f32[13,32,128]{2,1,0:T(8,128)S(1)}, u32[]{:S(2)}, u32[]{:S(2)}) collective-permute-start(f32[13,32,128]{2,1,0:T(8,128)S(1)} %collective-permute-done.3.refs_3_), channel_id=1, source_target_pairs={{0,1},{1,0},{2,3},{3,2},{4,5},{5,4},{6,7},{7,6},{8,9},{9,8},{10,11... | collective-permute-start | bytes 638984 | tf_op jit(solution)/shard_map/to_other_core/ppermute | solution.py:457
  19.2 10.4 %collective-permute-start.4 = (f32[6,32,128]{2,1,0:T(8,128)S(1)}, f32[6,32,128]{2,1,0:T(8,128)S(1)}, u32[]{:S(2)}, u32[]{:S(2)}) collective-permute-start(f32[6,32,128]{2,1,0:T(8,128)S(1)} %get-tuple-element.54), channel_id=1, source_target_pairs={{0,8},{8,0},{16,24},{24,16},{1,9},{9,1},{17,25},{25,17},{2,10},{10... | collective-permute-start | bytes 294920 | tf_op jit(solution)/shard_map/next_to_columns/ppermute | solution.py:455
  19.7 9.9 %collective-permute-start.5 = (f32[6,32,128]{2,1,0:T(8,128)S(1)}, f32[6,32,128]{2,1,0:T(8,128)S(1)}, u32[]{:S(2)}, u32[]{:S(2)}) collective-permute-start(f32[6,32,128]{2,1,0:T(8,128)S(1)} %get-tuple-element.55), channel_id=1, source_target_pairs={{0,16},{8,24},{16,0},{24,8},{1,17},{9,25},{17,1},{25,9},{2,18},{10... | collective-permute-start | bytes 294920 | tf_op jit(solution)/shard_map/next_to_columns/ppermute | solution.py:455
  21.2 8.4 %collective-permute-start.6 = (f32[6,32,128]{2,1,0:T(8,128)S(1)}, f32[6,32,128]{2,1,0:T(8,128)S(1)}, u32[]{:S(2)}, u32[]{:S(2)}) collective-permute-start(f32[6,32,128]{2,1,0:T(8,128)S(1)} %get-tuple-element.56), channel_id=1, source_target_pairs={{0,24},{8,16},{16,8},{24,0},{1,25},{9,17},{17,9},{25,1},{2,26},{10... | collective-permute-start | bytes 294920 | tf_op jit(solution)/shard_map/next_to_columns/ppermute | solution.py:455
  29.6 2.9 %collective-permute-start.11 = (f32[4,6,32,128]{3,2,1,0:T(8,128)S(1)}, f32[4,6,32,128]{3,2,1,0:T(8,128)S(1)}, u32[]{:S(2)}, u32[]{:S(2)}) collective-permute-start(f32[4,6,32,128]{3,2,1,0:T(8,128)S(1)} %pad_maximum_fusion), channel_id=1, source_target_pairs={{0,1},{1,0},{2,3},{3,2},{4,5},{5,4},{6,7},{7,6},{8,9},{9,8},{10,11... | collective-permute-start | bytes 1179656 | tf_op jit(solution)/shard_map/next_to_other_core/ppermute | solution.py:481
  35.5 9.7 %collective-permute-start.12 = (f32[256,128]{1,0:T(8,128)S(1)}, f32[256,128]{1,0:T(8,128)S(1)}, u32[]{:S(2)}, u32[]{:S(2)}) collective-permute-start(f32[256,128]{1,0:T(8,128)S(1)} %get-tuple-element.78), channel_id=1, source_target_pairs={{0,24},{8,16},{16,8},{24,0},{1,25},{9,17},{17,9},{25,1},{2,26},{10... | collective-permute-start | bytes 393224 | tf_op jit(solution)/shard_map/sum_over_columns/ppermute | solution.py:513
  38.7 6.5 %collective-permute-start.13 = (f32[256,128]{1,0:T(8,128)S(1)}, f32[256,128]{1,0:T(8,128)S(1)}, u32[]{:S(2)}, u32[]{:S(2)}) collective-permute-start(f32[256,128]{1,0:T(8,128)S(1)} %get-tuple-element.81), channel_id=1, source_target_pairs={{0,16},{8,24},{16,0},{24,8},{1,17},{9,25},{17,1},{25,9},{2,18},{10... | collective-permute-start | bytes 393224 | tf_op jit(solution)/shard_map/sum_over_columns/ppermute | solution.py:513
  40.4 5.4 %collective-permute-start.14 = (f32[256,128]{1,0:T(8,128)S(1)}, f32[256,128]{1,0:T(8,128)S(1)}, u32[]{:S(2)}, u32[]{:S(2)}) collective-permute-start(f32[256,128]{1,0:T(8,128)S(1)} %edge_terms.7.after_ref), channel_id=1, source_target_pairs={{0,8},{8,0},{16,24},{24,16},{1,9},{9,1},{17,25},{25,17},{2,10},{10... | collective-permute-start | bytes 393224 | tf_op jit(solution)/shard_map/sum_over_columns/ppermute | solution.py:513
  45.9 5.8 %collective-permute-start.17 = (f32[64,128]{1,0:T(8,128)S(1)}, f32[64,128]{1,0:T(8,128)S(1)}, u32[]{:S(2)}, u32[]{:S(2)}) collective-permute-start(f32[64,128]{1,0:T(8,128)S(1)} %get-tuple-element.89), channel_id=1, source_target_pairs={{0,6},{1,7},{2,4},{3,5},{4,2},{5,3},{6,0},{7,1},{8,14},{9,15},{10,... | collective-permute-start | bytes 98312 | tf_op jit(solution)/shard_map/sum_over_chips/ppermute | solution.py:564
  48.2 4.8 %collective-permute-start.16 = (f32[64,128]{1,0:T(8,128)S(1)}, f32[64,128]{1,0:T(8,128)S(1)}, u32[]{:S(2)}, u32[]{:S(2)}) collective-permute-start(f32[64,128]{1,0:T(8,128)S(1)} %get-tuple-element.90), channel_id=1, source_target_pairs={{0,4},{1,5},{2,6},{3,7},{4,0},{5,1},{6,2},{7,3},{8,12},{9,13},{10,... | collective-permute-start | bytes 98312 | tf_op jit(solution)/shard_map/sum_over_chips/ppermute | solution.py:564
  48.2 4.8 %collective-permute-start.15 = (f32[64,128]{1,0:T(8,128)S(1)}, f32[64,128]{1,0:T(8,128)S(1)}, u32[]{:S(2)}, u32[]{:S(2)}) collective-permute-start(f32[64,128]{1,0:T(8,128)S(1)} %get-tuple-element.91), channel_id=1, source_target_pairs={{0,2},{1,3},{2,0},{3,1},{4,6},{5,7},{6,4},{7,5},{8,10},{9,11},{10,... | collective-permute-start | bytes 98312 | tf_op jit(solution)/shard_map/sum_over_chips/ppermute | solution.py:564

commit v20 on v18

--- a/solution.py
+++ b/solution.py
@@ -445,15 +445,19 @@
     with jax.named_scope("to_next_plane"):
         ring = [(place, (place + (1 if place % 2 else -1)) % space_count) for place in range(space_count)]
         across_edge = lax.ppermute(packed[tm_count], "space", ring)
+    order = [0, tm_count - 1, *range(1, tm_count - 1)]
     with jax.named_scope("to_columns"):
-        own = [packed[0]] + [lax.ppermute(packed[peer], "tm", across(peer)) for peer in range(1, tm_count)]
+        sent = [packed[peer] if peer == 0 else lax.ppermute(packed[peer], "tm", across(peer)) for peer in order]
+    with jax.named_scope("to_other_core"):
+        swapped = [lax.ppermute(piece, "space", swap) for piece in sent[:3]]
     with jax.named_scope("next_to_columns"):
-        across_edge, own[:3] = lax.optimization_barrier((across_edge, own[:3]))
+        across_edge, sent[:3] = lax.optimization_barrier((across_edge, sent[:3]))
         parts = [across_edge[peer] for peer in range(tm_count)]
-        parts, own[3:] = lax.optimization_barrier((parts, own[3:]))
+        parts, sent[3:] = lax.optimization_barrier((parts, sent[3:]))
         next_own = [parts[0]] + [lax.ppermute(parts[peer], "tm", across(peer)) for peer in range(1, tm_count)]
     with jax.named_scope("to_other_core"):
-        other = [lax.ppermute(piece, "space", swap) for piece in own]
+        swapped = swapped + [lax.ppermute(piece, "space", swap) for piece in sent[3:]]
+    own, other = ([pieces[order.index(peer)] for peer in range(tm_count)] for pieces in (sent, swapped))
     early = tm_count // 2
     picked = pltpu.VMEM((block * 3 * height, lanes), F32)
     held_codes = [pltpu.SMEM(codes.shape, jnp.int32), pltpu.SemaphoreType.DMA]

time: 54.8 us -> 54.4 us (level)
  no operation moved by 1% of the time
where the time goes in v20:
time: 54.4 us; the launch traced here: 54.3 us
  starting transfers between devices  20.3 us (37%)
  Pallas kernels  20.1 us (37%)
  waiting for transfers between devices  13 us (24%)
  other arithmetic  0.67 us (1%)
    ppermute x3, waiting for transfers between devices, shards(): lax.ppermute(packed[peer], 'tm', across(peer))  7.87 us
    pallas_call x1, Pallas kernels, shards(): pl.pallas_call(functools.partial(inner_kernel, first_peer=early, sizes=(l...  6.87 us
    ppermute x1, starting transfers between devices, shards(): across_edge = lax.ppermute(packed[tm_count], 'space', ring)  4.55 us
    ppermute x3, starting transfers between devices, shards(): part = lax.ppermute(shares[step], 'space', pairing)  4.45 us
    ppermute x3, starting transfers between devices, shards(): arrived.append(lax.ppermute(summed, 'tm', across(peer + 1)))  3.69 us
    ppermute x3, starting transfers between devices, shards(): lax.ppermute(parts[peer], 'tm', across(peer))  3.49 us
    ppermute x3, starting transfers between devices, shards(): lax.ppermute(packed[peer], 'tm', across(peer))  3.49 us
    pallas_call x1, Pallas kernels, shards(): pl.pallas_call(functools.partial(far_kernel, peer=tm_count - 1, sizes=(lo...  3.04 us
  transfers between devices with their start and end apart: 18, of which 6 were waited for; matrix products, arithmetic and copies ran while one was open for 0% of the time, Pallas kernels for 27%

profile of v20, /device:TPU:0, one launch (start us, length us, event | category | flops | bytes accessed | tf_op | source)
XLA Modules:
  0.0 54.3 jit_solution(4588241083670441802)
XLA Ops:
  0.0 2.3 %pack.1 = (f32[13,32,128]{2,1,0:T(8,128)S(1)}, f32[13,32,128]{2,1,0:T(8,128)S(1)}, f32[13,32,128]{2,1,0:T(8,128)S(1)}, f32[13,32,128]{2,1,0:T(8,128)S(1)}, f32[4...) custom-call(f32[32,3,16,128]{3,2,1,0:T(8,128)} %bitcast.18, s32[2,2048]{1,0:T(2,128)} %bitcast.19, ...), custom_call_target="tpu_custom_call" | custom-call | tf_op jit(solution)/shard_map/pack/pallas_call | solution.py:421
  2.3 4.6 %collective-permute-start = (f32[4,6,32,128]{3,2,1,0:T(8,128)S(1)}, f32[4,6,32,128]{3,2,1,0:T(8,128)S(1)}, u32[]{:S(2)}, u32[]{:S(2)}) collective-permute-start(f32[4,6,32,128]{3,2,1,0:T(8,128)S(1)} %get-tuple-element.47), channel_id=1, source_target_pairs={{0,7},{1,2},{2,1},{3,4},{4,3},{5,6},{6,5},{7,0},{8,15},{9,10},{10,... | collective-permute-start | bytes 1179656 | tf_op jit(solution)/shard_map/to_next_plane/ppermute | solution.py:447
  6.9 2.5 %collective-permute-start.1 = (f32[13,32,128]{2,1,0:T(8,128)S(1)}, f32[13,32,128]{2,1,0:T(8,128)S(1)}, u32[]{:S(2)}, u32[]{:S(2)}) collective-permute-start(f32[13,32,128]{2,1,0:T(8,128)S(1)} %get-tuple-element.49), channel_id=1, source_target_pairs={{0,24},{8,16},{16,8},{24,0},{1,25},{9,17},{17,9},{25,1},{2,26},{10... | collective-permute-start | bytes 638984 | tf_op jit(solution)/shard_map/to_columns/ppermute | solution.py:450
  9.3 0.5 collective-permute-start.2
  9.9 0.5 collective-permute-start.3
  10.4 0.0 collective-permute-start.7
  10.4 5.5 %collective-permute-done.1.refs_3_ = f32[13,32,128]{2,1,0:T(8,128)S(1)} collective-permute-done((f32[13,32,128]{2,1,0:T(8,128)S(1)}, f32[13,32,128]{2,1,0:T(8,128)S(1)}, u32[]{:S(2)}, u32[]{:S(2)}) %collective-permute-start.1) | collective-permute-done | bytes 213024 | tf_op jit(solution)/shard_map/to_columns/ppermute | solution.py:450
  15.9 0.0 collective-permute-start.10
  15.9 2.4 %collective-permute-done.2.refs_1_ = f32[13,32,128]{2,1,0:T(8,128)S(1)} collective-permute-done((f32[13,32,128]{2,1,0:T(8,128)S(1)}, f32[13,32,128]{2,1,0:T(8,128)S(1)}, u32[]{:S(2)}, u32[]{:S(2)}) %collective-permute-start.2) | collective-permute-done | bytes 213024 | tf_op jit(solution)/shard_map/to_columns/ppermute | solution.py:450
  18.3 0.0 collective-permute-done.3.refs_2_
  18.3 0.6 %collective-permute-start.9 = (f32[13,32,128]{2,1,0:T(8,128)S(1)}, f32[13,32,128]{2,1,0:T(8,128)S(1)}, u32[]{:S(2)}, u32[]{:S(2)}) collective-permute-start(f32[13,32,128]{2,1,0:T(8,128)S(1)} %collective-permute-done.3.refs_2_), channel_id=1, source_target_pairs={{0,1},{1,0},{2,3},{3,2},{4,5},{5,4},{6,7},{7,6},{8,9},{9,8},{10,11... | collective-permute-start | bytes 638984 | tf_op jit(solution)/shard_map/to_other_core/ppermute | solution.py:459
  18.9 1.5 %collective-permute-start.4 = (f32[6,32,128]{2,1,0:T(8,128)S(1)}, f32[6,32,128]{2,1,0:T(8,128)S(1)}, u32[]{:S(2)}, u32[]{:S(2)}) collective-permute-start(f32[6,32,128]{2,1,0:T(8,128)S(1)} %get-tuple-element.54), channel_id=1, source_target_pairs={{0,8},{8,0},{16,24},{24,16},{1,9},{9,1},{17,25},{25,17},{2,10},{10... | collective-permute-start | bytes 294920 | tf_op jit(solution)/shard_map/next_to_columns/ppermute | solution.py:457
  20.4 0.8 %collective-permute-start.5 = (f32[6,32,128]{2,1,0:T(8,128)S(1)}, f32[6,32,128]{2,1,0:T(8,128)S(1)}, u32[]{:S(2)}, u32[]{:S(2)}) collective-permute-start(f32[6,32,128]{2,1,0:T(8,128)S(1)} %get-tuple-element.55), channel_id=1, source_target_pairs={{0,16},{8,24},{16,0},{24,8},{1,17},{9,25},{17,1},{25,9},{2,18},{10... | collective-permute-start | bytes 294920 | tf_op jit(solution)/shard_map/next_to_columns/ppermute | solution.py:457
  21.2 1.2 %collective-permute-start.6 = (f32[6,32,128]{2,1,0:T(8,128)S(1)}, f32[6,32,128]{2,1,0:T(8,128)S(1)}, u32[]{:S(2)}, u32[]{:S(2)}) collective-permute-start(f32[6,32,128]{2,1,0:T(8,128)S(1)} %get-tuple-element.56), channel_id=1, source_target_pairs={{0,24},{8,16},{16,8},{24,0},{1,25},{9,17},{17,9},{25,1},{2,26},{10... | collective-permute-start | bytes 294920 | tf_op jit(solution)/shard_map/next_to_columns/ppermute | solution.py:457
  22.4 0.0 collective-permute-done.8.refs_5_
  22.4 6.9 %inner_terms.2 = (f32[12,128,128]{2,1,0:T(8,128)S(1)}, f32[3072,128]{1,0:T(8,128)S(1)}, f32[9216,128]{1,0:T(8,128)S(1)}, bf16[3072,256]{1,0:T(8,128)(2,1)S(1)}, ...) custom-call(s32[2048]{0:T(1024)S(1)} %get-tuple-element.45.codes_ref, f32[128,128]{1,0:T(8,128)S(1)} %get-tuple-element.46.coeffs_ref, ...), custom_call_target="tpu_custom_call" | custom-call | flops 12000000000 | bytes 10000000 | tf_op jit(solution)/shard_map/inner_terms/pallas_call | solution.py:466
  29.3 0.1 collective-permute-start.11
  29.4 2.8 %inner_terms.3 = (f32[2,256,128]{2,1,0:T(8,128)S(1)}, f32[6144,128]{1,0:T(8,128)S(1)}) custom-call(s32[2048]{0:T(1024)S(1)} %get-tuple-element.45.codes_ref, f32[3072,128]{1,0:T(8,128)S(1)} %get-tuple-element.73.carry_ref, f32[9216,128]{1,0:T(8,128)S(1)} %get-tuple-element.74.slope_ref, ...), custom_call_target="tpu_custom_call", output_to_operand_aliasing={{1}: (4, {})} | custom-call | flops 8000000000 | bytes 10000000 | tf_op jit(solution)/shard_map/inner_terms/pallas_call | solution.py:486
  32.2 3.0 %edge_terms.5 = (f32[1024,128]{1,0:T(8,128)S(1)}, f32[3072,128]{1,0:T(8,128)S(1)}, bf16[3072,256]{1,0:T(8,128)(2,1)S(1)}, f32[256,128]{1,0:T(8,128)S(1)}, f32[6144,128]{1,0:T(8,128)S(1)}) custom-call(s32[2048]{0:T(1024)S(1)} %get-tuple-element.45.codes_ref, f32[128,128]{1,0:T(8,128)S(1)} %get-tuple-element.46.coeffs_ref, ...), custom_call_target="tpu_custom_call" | custom-call | tf_op jit(solution)/shard_map/edge_terms/pallas_call | solution.py:497
  35.2 1.8 %collective-permute-start.12 = (f32[256,128]{1,0:T(8,128)S(1)}, f32[256,128]{1,0:T(8,128)S(1)}, u32[]{:S(2)}, u32[]{:S(2)}) collective-permute-start(f32[256,128]{1,0:T(8,128)S(1)} %get-tuple-element.78), channel_id=1, source_target_pairs={{0,24},{8,16},{16,8},{24,0},{1,25},{9,17},{17,9},{25,1},{2,26},{10... | collective-permute-start | bytes 393224 | tf_op jit(solution)/shard_map/sum_over_columns/ppermute | solution.py:516
  37.0 1.7 %edge_terms.6 = (f32[256,128]{1,0:T(8,128)S(1)}, f32[6144,128]{1,0:T(8,128)S(1)}) custom-call(s32[2048]{0:T(1024)S(1)} %get-tuple-element.45.codes_ref, f32[1024,128]{1,0:T(8,128)S(1)} %get-tuple-element.70.carry_ref, f32[3072,128]{1,0:T(8,128)S(1)} %get-tuple-element.71.slope_ref, bf16[3072,256]{1,0:T(8,128)(2,1)S(1)} %get-tuple-element.72.rhs_ref, ...), custom_call_target="tpu_custom_call" | custom-call | flops 100000000 | bytes 100000 | tf_op jit(solution)/shard_map/edge_terms/pallas_call | solution.py:525
  38.7 1.3 %collective-permute-start.13 = (f32[256,128]{1,0:T(8,128)S(1)}, f32[256,128]{1,0:T(8,128)S(1)}, u32[]{:S(2)}, u32[]{:S(2)}) collective-permute-start(f32[256,128]{1,0:T(8,128)S(1)} %get-tuple-element.81), channel_id=1, source_target_pairs={{0,16},{8,24},{16,0},{24,8},{1,17},{9,25},{17,1},{25,9},{2,18},{10... | collective-permute-start | bytes 393224 | tf_op jit(solution)/shard_map/sum_over_columns/ppermute | solution.py:516
  40.0 1.1 %edge_terms.7.after_ref = f32[256,128]{1,0:T(8,128)S(1)} custom-call(bf16[3072,256]{1,0:T(8,128)(2,1)S(1)} %get-tuple-element.72.rhs_ref, f32[2,256,128]{2,1,0:T(8,128)S(1)} %get-tuple-element.84.inner_ref, f32[6144,128]{1,0:T(8,128)S(1)} %get-tuple-element.83.picked_ref), custom_call_target="tpu_custom_call" | custom-call | flops 100000000 | bytes 100000 | tf_op jit(solution)/shard_map/edge_terms/pallas_call | solution.py:535
  41.1 0.6 %collective-permute-start.14 = (f32[256,128]{1,0:T(8,128)S(1)}, f32[256,128]{1,0:T(8,128)S(1)}, u32[]{:S(2)}, u32[]{:S(2)}) collective-permute-start(f32[256,128]{1,0:T(8,128)S(1)} %edge_terms.7.after_ref), channel_id=1, source_target_pairs={{0,8},{8,0},{16,24},{24,16},{1,9},{9,1},{17,25},{25,17},{2,10},{10... | collective-permute-start | bytes 393224 | tf_op jit(solution)/shard_map/sum_over_columns/ppermute | solution.py:516
  41.7 2.3 %edge_terms.8.own_ref = f32[256,128]{1,0:T(8,128)S(1)} custom-call(s32[2048]{0:T(1024)S(1)} %get-tuple-element.45.codes_ref, f32[1024,128]{1,0:T(8,128)S(1)} %get-tuple-element.70.carry_ref, f32[3072,128]{1,0:T(8,128)S(1)} %get-tuple-element.71.slope_ref, bf16[3072,256]{1,0:T(8,128)(2,1)S(1)} %get-tuple-element.72.rhs_ref, ...), custom_call_target="tpu_custom_call" | custom-call | flops 100000000 | bytes 100000 | tf_op jit(solution)/shard_map/edge_terms/pallas_call | solution.py:544
  44.0 0.9 %collective-permute-done.13.refs_1_ = f32[256,128]{1,0:T(8,128)S(1)} collective-permute-done((f32[256,128]{1,0:T(8,128)S(1)}, f32[256,128]{1,0:T(8,128)S(1)}, u32[]{:S(2)}, u32[]{:S(2)}) %collective-permute-start.13) | collective-permute-done | bytes 131104 | tf_op jit(solution)/shard_map/sum_over_columns/ppermute | solution.py:516
  44.9 1.5 %collective-permute-done.14 = f32[256,128]{1,0:T(8,128)S(1)} collective-permute-done((f32[256,128]{1,0:T(8,128)S(1)}, f32[256,128]{1,0:T(8,128)S(1)}, u32[]{:S(2)}, u32[]{:S(2)}) %collective-permute-start.14) | collective-permute-done | bytes 131104 | tf_op jit(solution)/shard_map/sum_over_columns/ppermute | solution.py:516
  46.5 2.3 %collective-permute-start.17 = (f32[64,128]{1,0:T(8,128)S(1)}, f32[64,128]{1,0:T(8,128)S(1)}, u32[]{:S(2)}, u32[]{:S(2)}) collective-permute-start(f32[64,128]{1,0:T(8,128)S(1)} %get-tuple-element.89), channel_id=1, source_target_pairs={{0,6},{1,7},{2,4},{3,5},{4,2},{5,3},{6,0},{7,1},{8,14},{9,15},{10,... | collective-permute-start | bytes 98312 | tf_op jit(solution)/shard_map/sum_over_chips/ppermute | solution.py:567
  48.8 2.1 %collective-permute-start.15 = (f32[64,128]{1,0:T(8,128)S(1)}, f32[64,128]{1,0:T(8,128)S(1)}, u32[]{:S(2)}, u32[]{:S(2)}) collective-permute-start(f32[64,128]{1,0:T(8,128)S(1)} %get-tuple-element.91), channel_id=1, source_target_pairs={{0,2},{1,3},{2,0},{3,1},{4,6},{5,7},{6,4},{7,5},{8,10},{9,11},{10,... | collective-permute-start | bytes 98312 | tf_op jit(solution)/shard_map/sum_over_chips/ppermute | solution.py:567
  51.0 1.3 %collective-permute-done.17 = f32[64,128]{1,0:T(8,128)S(1)} collective-permute-done((f32[64,128]{1,0:T(8,128)S(1)}, f32[64,128]{1,0:T(8,128)S(1)}, u32[]{:S(2)}, u32[]{:S(2)}) %collective-permute-start.17) | collective-permute-done | bytes 32800 | tf_op jit(solution)/shard_map/sum_over_chips/ppermute | solution.py:567
  52.3 1.4 %collective-permute-done.16 = f32[64,128]{1,0:T(8,128)S(1)} collective-permute-done((f32[64,128]{1,0:T(8,128)S(1)}, f32[64,128]{1,0:T(8,128)S(1)}, u32[]{:S(2)}, u32[]{:S(2)}) %collective-permute-start.16) | collective-permute-done | bytes 32800 | tf_op jit(solution)/shard_map/sum_over_chips/ppermute | solution.py:567
  53.7 0.6 %fusion = f32[64,128]{1,0:T(8,128)} fusion(f32[256,128]{1,0:T(8,128)S(1)} %add.12, f32[64,128]{1,0:T(8,128)S(1)} %collective-permute-done.15, f32[64,128]{1,0:T(8,128)S(1)} %collective-permute-done.16, f32[64,128]{1,0:T(8,128)S(1)} %collective-permute-done.17), kind=kLoop, calls=%fused_computation.6 | loop fusion | flops 32768 | bytes 163840 | tf_op jit(solution)/shard_map/sum_over_chips/mul | solution.py:570
  (17 shorter events, 0.1 us)
Async XLA Ops:
  2.3 15.9 %collective-permute-start = (f32[4,6,32,128]{3,2,1,0:T(8,128)S(1)}, f32[4,6,32,128]{3,2,1,0:T(8,128)S(1)}, u32[]{:S(2)}, u32[]{:S(2)}) collective-permute-start(f32[4,6,32,128]{3,2,1,0:T(8,128)S(1)} %get-tuple-element.47), channel_id=1, source_target_pairs={{0,7},{1,2},{2,1},{3,4},{4,3},{5,6},{6,5},{7,0},{8,15},{9,10},{10,... | collective-permute-start | bytes 1179656 | tf_op jit(solution)/shard_map/to_next_plane/ppermute | solution.py:447
  6.9 9.0 %collective-permute-start.1 = (f32[13,32,128]{2,1,0:T(8,128)S(1)}, f32[13,32,128]{2,1,0:T(8,128)S(1)}, u32[]{:S(2)}, u32[]{:S(2)}) collective-permute-start(f32[13,32,128]{2,1,0:T(8,128)S(1)} %get-tuple-element.49), channel_id=1, source_target_pairs={{0,24},{8,16},{16,8},{24,0},{1,25},{9,17},{17,9},{25,1},{2,26},{10... | collective-permute-start | bytes 638984 | tf_op jit(solution)/shard_map/to_columns/ppermute | solution.py:450
  9.3 8.9 %collective-permute-start.2 = (f32[13,32,128]{2,1,0:T(8,128)S(1)}, f32[13,32,128]{2,1,0:T(8,128)S(1)}, u32[]{:S(2)}, u32[]{:S(2)}) collective-permute-start(f32[13,32,128]{2,1,0:T(8,128)S(1)} %get-tuple-element.50), channel_id=1, source_target_pairs={{0,8},{8,0},{16,24},{24,16},{1,9},{9,1},{17,25},{25,17},{2,10},{10... | collective-permute-start | bytes 638984 | tf_op jit(solution)/shard_map/to_columns/ppermute | solution.py:450
  9.9 8.4 %collective-permute-start.3 = (f32[13,32,128]{2,1,0:T(8,128)S(1)}, f32[13,32,128]{2,1,0:T(8,128)S(1)}, u32[]{:S(2)}, u32[]{:S(2)}) collective-permute-start(f32[13,32,128]{2,1,0:T(8,128)S(1)} %get-tuple-element.52), channel_id=1, source_target_pairs={{0,16},{8,24},{16,0},{24,8},{1,17},{9,25},{17,1},{25,9},{2,18},{10... | collective-permute-start | bytes 638984 | tf_op jit(solution)/shard_map/to_columns/ppermute | solution.py:450
  10.4 10.0 %collective-permute-start.7 = (f32[13,32,128]{2,1,0:T(8,128)S(1)}, f32[13,32,128]{2,1,0:T(8,128)S(1)}, u32[]{:S(2)}, u32[]{:S(2)}) collective-permute-start(f32[13,32,128]{2,1,0:T(8,128)S(1)} %get-tuple-element.57.refs_0_), channel_id=1, source_target_pairs={{0,1},{1,0},{2,3},{3,2},{4,5},{5,4},{6,7},{7,6},{8,9},{9,8},{10,11... | collective-permute-start | bytes 638984 | tf_op jit(solution)/shard_map/to_other_core/ppermute | solution.py:452
  15.9 5.3 %collective-permute-start.10 = (f32[13,32,128]{2,1,0:T(8,128)S(1)}, f32[13,32,128]{2,1,0:T(8,128)S(1)}, u32[]{:S(2)}, u32[]{:S(2)}) collective-permute-start(f32[13,32,128]{2,1,0:T(8,128)S(1)} %collective-permute-done.1.refs_3_), channel_id=1, source_target_pairs={{0,1},{1,0},{2,3},{3,2},{4,5},{5,4},{6,7},{7,6},{8,9},{9,8},{10,11... | collective-permute-start | bytes 638984 | tf_op jit(solution)/shard_map/to_other_core/ppermute | solution.py:452
  18.3 4.1 %collective-permute-start.8 = (f32[13,32,128]{2,1,0:T(8,128)S(1)}, f32[13,32,128]{2,1,0:T(8,128)S(1)}, u32[]{:S(2)}, u32[]{:S(2)}) collective-permute-start(f32[13,32,128]{2,1,0:T(8,128)S(1)} %collective-permute-done.2.refs_1_), channel_id=1, source_target_pairs={{0,1},{1,0},{2,3},{3,2},{4,5},{5,4},{6,7},{7,6},{8,9},{9,8},{10,11... | collective-permute-start | bytes 638984 | tf_op jit(solution)/shard_map/to_other_core/ppermute | solution.py:452
  18.3 4.1 %collective-permute-start.9 = (f32[13,32,128]{2,1,0:T(8,128)S(1)}, f32[13,32,128]{2,1,0:T(8,128)S(1)}, u32[]{:S(2)}, u32[]{:S(2)}) collective-permute-start(f32[13,32,128]{2,1,0:T(8,128)S(1)} %collective-permute-done.3.refs_2_), channel_id=1, source_target_pairs={{0,1},{1,0},{2,3},{3,2},{4,5},{5,4},{6,7},{7,6},{8,9},{9,8},{10,11... | collective-permute-start | bytes 638984 | tf_op jit(solution)/shard_map/to_other_core/ppermute | solution.py:459
  18.9 10.4 %collective-permute-start.4 = (f32[6,32,128]{2,1,0:T(8,128)S(1)}, f32[6,32,128]{2,1,0:T(8,128)S(1)}, u32[]{:S(2)}, u32[]{:S(2)}) collective-permute-start(f32[6,32,128]{2,1,0:T(8,128)S(1)} %get-tuple-element.54), channel_id=1, source_target_pairs={{0,8},{8,0},{16,24},{24,16},{1,9},{9,1},{17,25},{25,17},{2,10},{10... | collective-permute-start | bytes 294920 | tf_op jit(solution)/shard_map/next_to_columns/ppermute | solution.py:457
  20.4 8.9 %collective-permute-start.5 = (f32[6,32,128]{2,1,0:T(8,128)S(1)}, f32[6,32,128]{2,1,0:T(8,128)S(1)}, u32[]{:S(2)}, u32[]{:S(2)}) collective-permute-start(f32[6,32,128]{2,1,0:T(8,128)S(1)} %get-tuple-element.55), channel_id=1, source_target_pairs={{0,16},{8,24},{16,0},{24,8},{1,17},{9,25},{17,1},{25,9},{2,18},{10... | collective-permute-start | bytes 294920 | tf_op jit(solution)/shard_map/next_to_columns/ppermute | solution.py:457
  21.2 8.1 %collective-permute-start.6 = (f32[6,32,128]{2,1,0:T(8,128)S(1)}, f32[6,32,128]{2,1,0:T(8,128)S(1)}, u32[]{:S(2)}, u32[]{:S(2)}) collective-permute-start(f32[6,32,128]{2,1,0:T(8,128)S(1)} %get-tuple-element.56), channel_id=1, source_target_pairs={{0,24},{8,16},{16,8},{24,0},{1,25},{9,17},{17,9},{25,1},{2,26},{10... | collective-permute-start | bytes 294920 | tf_op jit(solution)/shard_map/next_to_columns/ppermute | solution.py:457
  29.3 2.9 %collective-permute-start.11 = (f32[4,6,32,128]{3,2,1,0:T(8,128)S(1)}, f32[4,6,32,128]{3,2,1,0:T(8,128)S(1)}, u32[]{:S(2)}, u32[]{:S(2)}) collective-permute-start(f32[4,6,32,128]{3,2,1,0:T(8,128)S(1)} %pad_maximum_fusion), channel_id=1, source_target_pairs={{0,1},{1,0},{2,3},{3,2},{4,5},{5,4},{6,7},{7,6},{8,9},{9,8},{10,11... | collective-permute-start | bytes 1179656 | tf_op jit(solution)/shard_map/next_to_other_core/ppermute | solution.py:484
  35.2 9.7 %collective-permute-start.12 = (f32[256,128]{1,0:T(8,128)S(1)}, f32[256,128]{1,0:T(8,128)S(1)}, u32[]{:S(2)}, u32[]{:S(2)}) collective-permute-start(f32[256,128]{1,0:T(8,128)S(1)} %get-tuple-element.78), channel_id=1, source_target_pairs={{0,24},{8,16},{16,8},{24,0},{1,25},{9,17},{17,9},{25,1},{2,26},{10... | collective-permute-start | bytes 393224 | tf_op jit(solution)/shard_map/sum_over_columns/ppermute | solution.py:516
  38.7 6.2 %collective-permute-start.13 = (f32[256,128]{1,0:T(8,128)S(1)}, f32[256,128]{1,0:T(8,128)S(1)}, u32[]{:S(2)}, u32[]{:S(2)}) collective-permute-start(f32[256,128]{1,0:T(8,128)S(1)} %get-tuple-element.81), channel_id=1, source_target_pairs={{0,16},{8,24},{16,0},{24,8},{1,17},{9,25},{17,1},{25,9},{2,18},{10... | collective-permute-start | bytes 393224 | tf_op jit(solution)/shard_map/sum_over_columns/ppermute | solution.py:516
  41.1 5.4 %collective-permute-start.14 = (f32[256,128]{1,0:T(8,128)S(1)}, f32[256,128]{1,0:T(8,128)S(1)}, u32[]{:S(2)}, u32[]{:S(2)}) collective-permute-start(f32[256,128]{1,0:T(8,128)S(1)} %edge_terms.7.after_ref), channel_id=1, source_target_pairs={{0,8},{8,0},{16,24},{24,16},{1,9},{9,1},{17,25},{25,17},{2,10},{10... | collective-permute-start | bytes 393224 | tf_op jit(solution)/shard_map/sum_over_columns/ppermute | solution.py:516
  46.5 5.8 %collective-permute-start.17 = (f32[64,128]{1,0:T(8,128)S(1)}, f32[64,128]{1,0:T(8,128)S(1)}, u32[]{:S(2)}, u32[]{:S(2)}) collective-permute-start(f32[64,128]{1,0:T(8,128)S(1)} %get-tuple-element.89), channel_id=1, source_target_pairs={{0,6},{1,7},{2,4},{3,5},{4,2},{5,3},{6,0},{7,1},{8,14},{9,15},{10,... | collective-permute-start | bytes 98312 | tf_op jit(solution)/shard_map/sum_over_chips/ppermute | solution.py:567
  48.8 4.8 %collective-permute-start.16 = (f32[64,128]{1,0:T(8,128)S(1)}, f32[64,128]{1,0:T(8,128)S(1)}, u32[]{:S(2)}, u32[]{:S(2)}) collective-permute-start(f32[64,128]{1,0:T(8,128)S(1)} %get-tuple-element.90), channel_id=1, source_target_pairs={{0,4},{1,5},{2,6},{3,7},{4,0},{5,1},{6,2},{7,3},{8,12},{9,13},{10,... | collective-permute-start | bytes 98312 | tf_op jit(solution)/shard_map/sum_over_chips/ppermute | solution.py:567
  48.8 4.8 %collective-permute-start.15 = (f32[64,128]{1,0:T(8,128)S(1)}, f32[64,128]{1,0:T(8,128)S(1)}, u32[]{:S(2)}, u32[]{:S(2)}) collective-permute-start(f32[64,128]{1,0:T(8,128)S(1)} %get-tuple-element.91), channel_id=1, source_target_pairs={{0,2},{1,3},{2,0},{3,1},{4,6},{5,7},{6,4},{7,5},{8,10},{9,11},{10,... | collective-permute-start | bytes 98312 | tf_op jit(solution)/shard_map/sum_over_chips/ppermute | solution.py:567

commit v21 on v19

--- a/solution.py
+++ b/solution.py
@@ -159,7 +159,7 @@
 
         return lax.fori_loop(0, share, one, 0, unroll=True)
 
-    lax.fori_loop(0, chips, one_share, 0)
+    lax.fori_loop(0, chips, one_share, 0, unroll=2)
 
 
 def copy_of_codes(codes_ref, held_codes_ref, sem):

time: 53.8 us -> 53.8 us (level)
  no operation moved by 1% of the time
where the time goes in v21:
time: 53.8 us; the launch traced here: 53.7 us
  starting transfers between devices  20.3 us (38%)
  Pallas kernels  20.1 us (37%)
  waiting for transfers between devices  12.4 us (23%)
  other arithmetic  0.67 us (1%)
    ppermute x3, waiting for transfers between devices, shards(): lax.ppermute(packed[peer], 'tm', across(peer))  8.18 us
    pallas_call x1, Pallas kernels, shards(): pl.pallas_call(functools.partial(inner_kernel, first_peer=early, sizes=(l...  6.94 us
    ppermute x1, starting transfers between devices, shards(): across_edge = lax.ppermute(packed[tm_count], 'space', ring)  4.55 us
    ppermute x3, starting transfers between devices, shards(): part = lax.ppermute(shares[step], 'space', pairing)  4.45 us
    ppermute x3, starting transfers between devices, shards(): arrived.append(lax.ppermute(summed, 'tm', across(peer + 1)))  3.68 us
    ppermute x3, starting transfers between devices, shards(): lax.ppermute(parts[peer], 'tm', across(peer))  3.49 us
    ppermute x3, starting transfers between devices, shards(): lax.ppermute(packed[peer], 'tm', across(peer))  3.49 us
    pallas_call x1, Pallas kernels, shards(): pl.pallas_call(functools.partial(far_kernel, peer=tm_count - 1, sizes=(lo...  3.01 us
  transfers between devices with their start and end apart: 18, of which 6 were waited for; matrix products, arithmetic and copies ran while one was open for 0% of the time, Pallas kernels for 27%

profile of v21, /device:TPU:0, one launch (start us, length us, event | category | flops | bytes accessed | tf_op | source)
XLA Modules:
  0.0 53.7 jit_solution(13239657386107641923)
XLA Ops:
  0.0 2.3 %pack.1 = (f32[13,32,128]{2,1,0:T(8,128)S(1)}, f32[13,32,128]{2,1,0:T(8,128)S(1)}, f32[13,32,128]{2,1,0:T(8,128)S(1)}, f32[13,32,128]{2,1,0:T(8,128)S(1)}, f32[4...) custom-call(f32[32,3,16,128]{3,2,1,0:T(8,128)} %bitcast.18, s32[2,2048]{1,0:T(2,128)} %bitcast.19, ...), custom_call_target="tpu_custom_call" | custom-call | tf_op jit(solution)/shard_map/pack/pallas_call | solution.py:421
  2.3 4.6 %collective-permute-start = (f32[4,6,32,128]{3,2,1,0:T(8,128)S(1)}, f32[4,6,32,128]{3,2,1,0:T(8,128)S(1)}, u32[]{:S(2)}, u32[]{:S(2)}) collective-permute-start(f32[4,6,32,128]{3,2,1,0:T(8,128)S(1)} %get-tuple-element.47), channel_id=1, source_target_pairs={{0,7},{1,2},{2,1},{3,4},{4,3},{5,6},{6,5},{7,0},{8,15},{9,10},{10,... | collective-permute-start | bytes 1179656 | tf_op jit(solution)/shard_map/to_next_plane/ppermute | solution.py:447
  6.9 1.5 %collective-permute-start.1 = (f32[13,32,128]{2,1,0:T(8,128)S(1)}, f32[13,32,128]{2,1,0:T(8,128)S(1)}, u32[]{:S(2)}, u32[]{:S(2)}) collective-permute-start(f32[13,32,128]{2,1,0:T(8,128)S(1)} %get-tuple-element.49), channel_id=1, source_target_pairs={{0,8},{8,0},{16,24},{24,16},{1,9},{9,1},{17,25},{25,17},{2,10},{10... | collective-permute-start | bytes 638984 | tf_op jit(solution)/shard_map/to_columns/ppermute | solution.py:449
  8.4 1.5 %collective-permute-start.2 = (f32[13,32,128]{2,1,0:T(8,128)S(1)}, f32[13,32,128]{2,1,0:T(8,128)S(1)}, u32[]{:S(2)}, u32[]{:S(2)}) collective-permute-start(f32[13,32,128]{2,1,0:T(8,128)S(1)} %get-tuple-element.50), channel_id=1, source_target_pairs={{0,16},{8,24},{16,0},{24,8},{1,17},{9,25},{17,1},{25,9},{2,18},{10... | collective-permute-start | bytes 638984 | tf_op jit(solution)/shard_map/to_columns/ppermute | solution.py:449
  9.9 0.5 collective-permute-start.3
  10.4 0.0 collective-permute-start.7
  10.4 4.6 %collective-permute-done.1.refs_1_ = f32[13,32,128]{2,1,0:T(8,128)S(1)} collective-permute-done((f32[13,32,128]{2,1,0:T(8,128)S(1)}, f32[13,32,128]{2,1,0:T(8,128)S(1)}, u32[]{:S(2)}, u32[]{:S(2)}) %collective-permute-start.1) | collective-permute-done | bytes 213024 | tf_op jit(solution)/shard_map/to_columns/ppermute | solution.py:449
  14.9 3.6 %collective-permute-done.2.refs_2_ = f32[13,32,128]{2,1,0:T(8,128)S(1)} collective-permute-done((f32[13,32,128]{2,1,0:T(8,128)S(1)}, f32[13,32,128]{2,1,0:T(8,128)S(1)}, u32[]{:S(2)}, u32[]{:S(2)}) %collective-permute-start.2) | collective-permute-done | bytes 213024 | tf_op jit(solution)/shard_map/to_columns/ppermute | solution.py:449
  18.6 0.0 collective-permute-done.3.refs_3_
  18.6 0.6 %collective-permute-start.10 = (f32[13,32,128]{2,1,0:T(8,128)S(1)}, f32[13,32,128]{2,1,0:T(8,128)S(1)}, u32[]{:S(2)}, u32[]{:S(2)}) collective-permute-start(f32[13,32,128]{2,1,0:T(8,128)S(1)} %collective-permute-done.3.refs_3_), channel_id=1, source_target_pairs={{0,1},{1,0},{2,3},{3,2},{4,5},{5,4},{6,7},{7,6},{8,9},{9,8},{10,11... | collective-permute-start | bytes 638984 | tf_op jit(solution)/shard_map/to_other_core/ppermute | solution.py:457
  19.2 0.5 collective-permute-start.4
  19.7 1.4 %collective-permute-start.5 = (f32[6,32,128]{2,1,0:T(8,128)S(1)}, f32[6,32,128]{2,1,0:T(8,128)S(1)}, u32[]{:S(2)}, u32[]{:S(2)}) collective-permute-start(f32[6,32,128]{2,1,0:T(8,128)S(1)} %get-tuple-element.55), channel_id=1, source_target_pairs={{0,16},{8,24},{16,0},{24,8},{1,17},{9,25},{17,1},{25,9},{2,18},{10... | collective-permute-start | bytes 294920 | tf_op jit(solution)/shard_map/next_to_columns/ppermute | solution.py:455
  21.2 0.0 collective-permute-done.8.refs_5_
  21.2 1.5 %collective-permute-start.6 = (f32[6,32,128]{2,1,0:T(8,128)S(1)}, f32[6,32,128]{2,1,0:T(8,128)S(1)}, u32[]{:S(2)}, u32[]{:S(2)}) collective-permute-start(f32[6,32,128]{2,1,0:T(8,128)S(1)} %get-tuple-element.56), channel_id=1, source_target_pairs={{0,24},{8,16},{16,8},{24,0},{1,25},{9,17},{17,9},{25,1},{2,26},{10... | collective-permute-start | bytes 294920 | tf_op jit(solution)/shard_map/next_to_columns/ppermute | solution.py:455
  22.7 0.0 collective-permute-done.9.refs_6_
  22.7 6.9 %inner_terms.2 = (f32[12,128,128]{2,1,0:T(8,128)S(1)}, f32[3072,128]{1,0:T(8,128)S(1)}, f32[9216,128]{1,0:T(8,128)S(1)}, bf16[3072,256]{1,0:T(8,128)(2,1)S(1)}, ...) custom-call(s32[2048]{0:T(1024)S(1)} %get-tuple-element.45.codes_ref, f32[128,128]{1,0:T(8,128)S(1)} %get-tuple-element.46.coeffs_ref, ...), custom_call_target="tpu_custom_call" | custom-call | flops 12000000000 | bytes 10000000 | tf_op jit(solution)/shard_map/inner_terms/pallas_call | solution.py:463
  29.7 0.1 collective-permute-start.11
  29.8 2.8 %inner_terms.3 = (f32[2,256,128]{2,1,0:T(8,128)S(1)}, f32[6144,128]{1,0:T(8,128)S(1)}) custom-call(s32[2048]{0:T(1024)S(1)} %get-tuple-element.45.codes_ref, f32[3072,128]{1,0:T(8,128)S(1)} %get-tuple-element.73.carry_ref, f32[9216,128]{1,0:T(8,128)S(1)} %get-tuple-element.74.slope_ref, ...), custom_call_target="tpu_custom_call", output_to_operand_aliasing={{1}: (4, {})} | custom-call | flops 8000000000 | bytes 10000000 | tf_op jit(solution)/shard_map/inner_terms/pallas_call | solution.py:483
  32.5 3.0 %edge_terms.5 = (f32[1024,128]{1,0:T(8,128)S(1)}, f32[3072,128]{1,0:T(8,128)S(1)}, bf16[3072,256]{1,0:T(8,128)(2,1)S(1)}, f32[256,128]{1,0:T(8,128)S(1)}, f32[6144,128]{1,0:T(8,128)S(1)}) custom-call(s32[2048]{0:T(1024)S(1)} %get-tuple-element.45.codes_ref, f32[128,128]{1,0:T(8,128)S(1)} %get-tuple-element.46.coeffs_ref, ...), custom_call_target="tpu_custom_call" | custom-call | tf_op jit(solution)/shard_map/edge_terms/pallas_call | solution.py:494
  35.6 1.5 %collective-permute-start.12 = (f32[256,128]{1,0:T(8,128)S(1)}, f32[256,128]{1,0:T(8,128)S(1)}, u32[]{:S(2)}, u32[]{:S(2)}) collective-permute-start(f32[256,128]{1,0:T(8,128)S(1)} %get-tuple-element.78), channel_id=1, source_target_pairs={{0,24},{8,16},{16,8},{24,0},{1,25},{9,17},{17,9},{25,1},{2,26},{10... | collective-permute-start | bytes 393224 | tf_op jit(solution)/shard_map/sum_over_columns/ppermute | solution.py:513
  37.1 1.7 %edge_terms.6 = (f32[256,128]{1,0:T(8,128)S(1)}, f32[6144,128]{1,0:T(8,128)S(1)}) custom-call(s32[2048]{0:T(1024)S(1)} %get-tuple-element.45.codes_ref, f32[1024,128]{1,0:T(8,128)S(1)} %get-tuple-element.70.carry_ref, f32[3072,128]{1,0:T(8,128)S(1)} %get-tuple-element.71.slope_ref, bf16[3072,256]{1,0:T(8,128)(2,1)S(1)} %get-tuple-element.72.rhs_ref, ...), custom_call_target="tpu_custom_call" | custom-call | flops 100000000 | bytes 100000 | tf_op jit(solution)/shard_map/edge_terms/pallas_call | solution.py:522
  38.7 0.7 %collective-permute-start.13 = (f32[256,128]{1,0:T(8,128)S(1)}, f32[256,128]{1,0:T(8,128)S(1)}, u32[]{:S(2)}, u32[]{:S(2)}) collective-permute-start(f32[256,128]{1,0:T(8,128)S(1)} %get-tuple-element.81), channel_id=1, source_target_pairs={{0,16},{8,24},{16,0},{24,8},{1,17},{9,25},{17,1},{25,9},{2,18},{10... | collective-permute-start | bytes 393224 | tf_op jit(solution)/shard_map/sum_over_columns/ppermute | solution.py:513
  39.4 1.1 %edge_terms.7.after_ref = f32[256,128]{1,0:T(8,128)S(1)} custom-call(bf16[3072,256]{1,0:T(8,128)(2,1)S(1)} %get-tuple-element.72.rhs_ref, f32[2,256,128]{2,1,0:T(8,128)S(1)} %get-tuple-element.84.inner_ref, f32[6144,128]{1,0:T(8,128)S(1)} %get-tuple-element.83.picked_ref), custom_call_target="tpu_custom_call" | custom-call | flops 100000000 | bytes 100000 | tf_op jit(solution)/shard_map/edge_terms/pallas_call | solution.py:532
  40.4 1.5 %collective-permute-start.14 = (f32[256,128]{1,0:T(8,128)S(1)}, f32[256,128]{1,0:T(8,128)S(1)}, u32[]{:S(2)}, u32[]{:S(2)}) collective-permute-start(f32[256,128]{1,0:T(8,128)S(1)} %edge_terms.7.after_ref), channel_id=1, source_target_pairs={{0,8},{8,0},{16,24},{24,16},{1,9},{9,1},{17,25},{25,17},{2,10},{10... | collective-permute-start | bytes 393224 | tf_op jit(solution)/shard_map/sum_over_columns/ppermute | solution.py:513
  42.0 2.3 %edge_terms.8.own_ref = f32[256,128]{1,0:T(8,128)S(1)} custom-call(s32[2048]{0:T(1024)S(1)} %get-tuple-element.45.codes_ref, f32[1024,128]{1,0:T(8,128)S(1)} %get-tuple-element.70.carry_ref, f32[3072,128]{1,0:T(8,128)S(1)} %get-tuple-element.71.slope_ref, bf16[3072,256]{1,0:T(8,128)(2,1)S(1)} %get-tuple-element.72.rhs_ref, ...), custom_call_target="tpu_custom_call" | custom-call | flops 100000000 | bytes 100000 | tf_op jit(solution)/shard_map/edge_terms/pallas_call | solution.py:541
  44.3 0.9 %collective-permute-done.13.refs_1_ = f32[256,128]{1,0:T(8,128)S(1)} collective-permute-done((f32[256,128]{1,0:T(8,128)S(1)}, f32[256,128]{1,0:T(8,128)S(1)}, u32[]{:S(2)}, u32[]{:S(2)}) %collective-permute-start.13) | collective-permute-done | bytes 131104 | tf_op jit(solution)/shard_map/sum_over_columns/ppermute | solution.py:513
  45.3 0.6 %collective-permute-done.14 = f32[256,128]{1,0:T(8,128)S(1)} collective-permute-done((f32[256,128]{1,0:T(8,128)S(1)}, f32[256,128]{1,0:T(8,128)S(1)}, u32[]{:S(2)}, u32[]{:S(2)}) %collective-permute-start.14) | collective-permute-done | bytes 131104 | tf_op jit(solution)/shard_map/sum_over_columns/ppermute | solution.py:513
  45.9 2.3 %collective-permute-start.17 = (f32[64,128]{1,0:T(8,128)S(1)}, f32[64,128]{1,0:T(8,128)S(1)}, u32[]{:S(2)}, u32[]{:S(2)}) collective-permute-start(f32[64,128]{1,0:T(8,128)S(1)} %get-tuple-element.89), channel_id=1, source_target_pairs={{0,6},{1,7},{2,4},{3,5},{4,2},{5,3},{6,0},{7,1},{8,14},{9,15},{10,... | collective-permute-start | bytes 98312 | tf_op jit(solution)/shard_map/sum_over_chips/ppermute | solution.py:564
  48.2 2.1 %collective-permute-start.15 = (f32[64,128]{1,0:T(8,128)S(1)}, f32[64,128]{1,0:T(8,128)S(1)}, u32[]{:S(2)}, u32[]{:S(2)}) collective-permute-start(f32[64,128]{1,0:T(8,128)S(1)} %get-tuple-element.91), channel_id=1, source_target_pairs={{0,2},{1,3},{2,0},{3,1},{4,6},{5,7},{6,4},{7,5},{8,10},{9,11},{10,... | collective-permute-start | bytes 98312 | tf_op jit(solution)/shard_map/sum_over_chips/ppermute | solution.py:564
  50.3 1.3 %collective-permute-done.17 = f32[64,128]{1,0:T(8,128)S(1)} collective-permute-done((f32[64,128]{1,0:T(8,128)S(1)}, f32[64,128]{1,0:T(8,128)S(1)}, u32[]{:S(2)}, u32[]{:S(2)}) %collective-permute-start.17) | collective-permute-done | bytes 32800 | tf_op jit(solution)/shard_map/sum_over_chips/ppermute | solution.py:564
  51.7 1.4 %collective-permute-done.16 = f32[64,128]{1,0:T(8,128)S(1)} collective-permute-done((f32[64,128]{1,0:T(8,128)S(1)}, f32[64,128]{1,0:T(8,128)S(1)}, u32[]{:S(2)}, u32[]{:S(2)}) %collective-permute-start.16) | collective-permute-done | bytes 32800 | tf_op jit(solution)/shard_map/sum_over_chips/ppermute | solution.py:564
  53.0 0.6 %fusion = f32[64,128]{1,0:T(8,128)} fusion(f32[256,128]{1,0:T(8,128)S(1)} %add.12, f32[64,128]{1,0:T(8,128)S(1)} %collective-permute-done.15, f32[64,128]{1,0:T(8,128)S(1)} %collective-permute-done.16, f32[64,128]{1,0:T(8,128)S(1)} %collective-permute-done.17), kind=kLoop, calls=%fused_computation.6 | loop fusion | flops 32768 | bytes 163840 | tf_op jit(solution)/shard_map/sum_over_chips/mul | solution.py:567
  (17 shorter events, 0.1 us)
Async XLA Ops:
  2.3 16.2 %collective-permute-start = (f32[4,6,32,128]{3,2,1,0:T(8,128)S(1)}, f32[4,6,32,128]{3,2,1,0:T(8,128)S(1)}, u32[]{:S(2)}, u32[]{:S(2)}) collective-permute-start(f32[4,6,32,128]{3,2,1,0:T(8,128)S(1)} %get-tuple-element.47), channel_id=1, source_target_pairs={{0,7},{1,2},{2,1},{3,4},{4,3},{5,6},{6,5},{7,0},{8,15},{9,10},{10,... | collective-permute-start | bytes 1179656 | tf_op jit(solution)/shard_map/to_next_plane/ppermute | solution.py:447
  6.9 8.0 %collective-permute-start.1 = (f32[13,32,128]{2,1,0:T(8,128)S(1)}, f32[13,32,128]{2,1,0:T(8,128)S(1)}, u32[]{:S(2)}, u32[]{:S(2)}) collective-permute-start(f32[13,32,128]{2,1,0:T(8,128)S(1)} %get-tuple-element.49), channel_id=1, source_target_pairs={{0,8},{8,0},{16,24},{24,16},{1,9},{9,1},{17,25},{25,17},{2,10},{10... | collective-permute-start | bytes 638984 | tf_op jit(solution)/shard_map/to_columns/ppermute | solution.py:449
  8.4 10.2 %collective-permute-start.2 = (f32[13,32,128]{2,1,0:T(8,128)S(1)}, f32[13,32,128]{2,1,0:T(8,128)S(1)}, u32[]{:S(2)}, u32[]{:S(2)}) collective-permute-start(f32[13,32,128]{2,1,0:T(8,128)S(1)} %get-tuple-element.50), channel_id=1, source_target_pairs={{0,16},{8,24},{16,0},{24,8},{1,17},{9,25},{17,1},{25,9},{2,18},{10... | collective-permute-start | bytes 638984 | tf_op jit(solution)/shard_map/to_columns/ppermute | solution.py:449
  9.9 8.7 %collective-permute-start.3 = (f32[13,32,128]{2,1,0:T(8,128)S(1)}, f32[13,32,128]{2,1,0:T(8,128)S(1)}, u32[]{:S(2)}, u32[]{:S(2)}) collective-permute-start(f32[13,32,128]{2,1,0:T(8,128)S(1)} %get-tuple-element.52), channel_id=1, source_target_pairs={{0,24},{8,16},{16,8},{24,0},{1,25},{9,17},{17,9},{25,1},{2,26},{10... | collective-permute-start | bytes 638984 | tf_op jit(solution)/shard_map/to_columns/ppermute | solution.py:449
  10.4 9.3 %collective-permute-start.7 = (f32[13,32,128]{2,1,0:T(8,128)S(1)}, f32[13,32,128]{2,1,0:T(8,128)S(1)}, u32[]{:S(2)}, u32[]{:S(2)}) collective-permute-start(f32[13,32,128]{2,1,0:T(8,128)S(1)} %get-tuple-element.57.refs_0_), channel_id=1, source_target_pairs={{0,1},{1,0},{2,3},{3,2},{4,5},{5,4},{6,7},{7,6},{8,9},{9,8},{10,11... | collective-permute-start | bytes 638984 | tf_op jit(solution)/shard_map/next_to_columns/ppermute | solution.py:451
  14.9 6.2 %collective-permute-start.8 = (f32[13,32,128]{2,1,0:T(8,128)S(1)}, f32[13,32,128]{2,1,0:T(8,128)S(1)}, u32[]{:S(2)}, u32[]{:S(2)}) collective-permute-start(f32[13,32,128]{2,1,0:T(8,128)S(1)} %collective-permute-done.1.refs_1_), channel_id=1, source_target_pairs={{0,1},{1,0},{2,3},{3,2},{4,5},{5,4},{6,7},{7,6},{8,9},{9,8},{10,11... | collective-permute-start | bytes 638984 | tf_op jit(solution)/shard_map/next_to_columns/ppermute | solution.py:451
  18.6 4.1 %collective-permute-start.9 = (f32[13,32,128]{2,1,0:T(8,128)S(1)}, f32[13,32,128]{2,1,0:T(8,128)S(1)}, u32[]{:S(2)}, u32[]{:S(2)}) collective-permute-start(f32[13,32,128]{2,1,0:T(8,128)S(1)} %collective-permute-done.2.refs_2_), channel_id=1, source_target_pairs={{0,1},{1,0},{2,3},{3,2},{4,5},{5,4},{6,7},{7,6},{8,9},{9,8},{10,11... | collective-permute-start | bytes 638984 | tf_op jit(solution)/shard_map/next_to_columns/ppermute | solution.py:451
  18.6 4.1 %collective-permute-start.10 = (f32[13,32,128]{2,1,0:T(8,128)S(1)}, f32[13,32,128]{2,1,0:T(8,128)S(1)}, u32[]{:S(2)}, u32[]{:S(2)}) collective-permute-start(f32[13,32,128]{2,1,0:T(8,128)S(1)} %collective-permute-done.3.refs_3_), channel_id=1, source_target_pairs={{0,1},{1,0},{2,3},{3,2},{4,5},{5,4},{6,7},{7,6},{8,9},{9,8},{10,11... | collective-permute-start | bytes 638984 | tf_op jit(solution)/shard_map/to_other_core/ppermute | solution.py:457
  19.2 10.4 %collective-permute-start.4 = (f32[6,32,128]{2,1,0:T(8,128)S(1)}, f32[6,32,128]{2,1,0:T(8,128)S(1)}, u32[]{:S(2)}, u32[]{:S(2)}) collective-permute-start(f32[6,32,128]{2,1,0:T(8,128)S(1)} %get-tuple-element.54), channel_id=1, source_target_pairs={{0,8},{8,0},{16,24},{24,16},{1,9},{9,1},{17,25},{25,17},{2,10},{10... | collective-permute-start | bytes 294920 | tf_op jit(solution)/shard_map/next_to_columns/ppermute | solution.py:455
  19.7 9.9 %collective-permute-start.5 = (f32[6,32,128]{2,1,0:T(8,128)S(1)}, f32[6,32,128]{2,1,0:T(8,128)S(1)}, u32[]{:S(2)}, u32[]{:S(2)}) collective-permute-start(f32[6,32,128]{2,1,0:T(8,128)S(1)} %get-tuple-element.55), channel_id=1, source_target_pairs={{0,16},{8,24},{16,0},{24,8},{1,17},{9,25},{17,1},{25,9},{2,18},{10... | collective-permute-start | bytes 294920 | tf_op jit(solution)/shard_map/next_to_columns/ppermute | solution.py:455
  21.2 8.5 %collective-permute-start.6 = (f32[6,32,128]{2,1,0:T(8,128)S(1)}, f32[6,32,128]{2,1,0:T(8,128)S(1)}, u32[]{:S(2)}, u32[]{:S(2)}) collective-permute-start(f32[6,32,128]{2,1,0:T(8,128)S(1)} %get-tuple-element.56), channel_id=1, source_target_pairs={{0,24},{8,16},{16,8},{24,0},{1,25},{9,17},{17,9},{25,1},{2,26},{10... | collective-permute-start | bytes 294920 | tf_op jit(solution)/shard_map/next_to_columns/ppermute | solution.py:455
  29.7 2.8 %collective-permute-start.11 = (f32[4,6,32,128]{3,2,1,0:T(8,128)S(1)}, f32[4,6,32,128]{3,2,1,0:T(8,128)S(1)}, u32[]{:S(2)}, u32[]{:S(2)}) collective-permute-start(f32[4,6,32,128]{3,2,1,0:T(8,128)S(1)} %pad_maximum_fusion), channel_id=1, source_target_pairs={{0,1},{1,0},{2,3},{3,2},{4,5},{5,4},{6,7},{7,6},{8,9},{9,8},{10,11... | collective-permute-start | bytes 1179656 | tf_op jit(solution)/shard_map/next_to_other_core/ppermute | solution.py:481
  35.6 9.7 %collective-permute-start.12 = (f32[256,128]{1,0:T(8,128)S(1)}, f32[256,128]{1,0:T(8,128)S(1)}, u32[]{:S(2)}, u32[]{:S(2)}) collective-permute-start(f32[256,128]{1,0:T(8,128)S(1)} %get-tuple-element.78), channel_id=1, source_target_pairs={{0,24},{8,16},{16,8},{24,0},{1,25},{9,17},{17,9},{25,1},{2,26},{10... | collective-permute-start | bytes 393224 | tf_op jit(solution)/shard_map/sum_over_columns/ppermute | solution.py:513
  38.7 6.5 %collective-permute-start.13 = (f32[256,128]{1,0:T(8,128)S(1)}, f32[256,128]{1,0:T(8,128)S(1)}, u32[]{:S(2)}, u32[]{:S(2)}) collective-permute-start(f32[256,128]{1,0:T(8,128)S(1)} %get-tuple-element.81), channel_id=1, source_target_pairs={{0,16},{8,24},{16,0},{24,8},{1,17},{9,25},{17,1},{25,9},{2,18},{10... | collective-permute-start | bytes 393224 | tf_op jit(solution)/shard_map/sum_over_columns/ppermute | solution.py:513
  40.4 5.4 %collective-permute-start.14 = (f32[256,128]{1,0:T(8,128)S(1)}, f32[256,128]{1,0:T(8,128)S(1)}, u32[]{:S(2)}, u32[]{:S(2)}) collective-permute-start(f32[256,128]{1,0:T(8,128)S(1)} %edge_terms.7.after_ref), channel_id=1, source_target_pairs={{0,8},{8,0},{16,24},{24,16},{1,9},{9,1},{17,25},{25,17},{2,10},{10... | collective-permute-start | bytes 393224 | tf_op jit(solution)/shard_map/sum_over_columns/ppermute | solution.py:513
  45.9 5.8 %collective-permute-start.17 = (f32[64,128]{1,0:T(8,128)S(1)}, f32[64,128]{1,0:T(8,128)S(1)}, u32[]{:S(2)}, u32[]{:S(2)}) collective-permute-start(f32[64,128]{1,0:T(8,128)S(1)} %get-tuple-element.89), channel_id=1, source_target_pairs={{0,6},{1,7},{2,4},{3,5},{4,2},{5,3},{6,0},{7,1},{8,14},{9,15},{10,... | collective-permute-start | bytes 98312 | tf_op jit(solution)/shard_map/sum_over_chips/ppermute | solution.py:564
  48.2 4.9 %collective-permute-start.16 = (f32[64,128]{1,0:T(8,128)S(1)}, f32[64,128]{1,0:T(8,128)S(1)}, u32[]{:S(2)}, u32[]{:S(2)}) collective-permute-start(f32[64,128]{1,0:T(8,128)S(1)} %get-tuple-element.90), channel_id=1, source_target_pairs={{0,4},{1,5},{2,6},{3,7},{4,0},{5,1},{6,2},{7,3},{8,12},{9,13},{10,... | collective-permute-start | bytes 98312 | tf_op jit(solution)/shard_map/sum_over_chips/ppermute | solution.py:564
  48.2 4.9 %collective-permute-start.15 = (f32[64,128]{1,0:T(8,128)S(1)}, f32[64,128]{1,0:T(8,128)S(1)}, u32[]{:S(2)}, u32[]{:S(2)}) collective-permute-start(f32[64,128]{1,0:T(8,128)S(1)} %get-tuple-element.91), channel_id=1, source_target_pairs={{0,2},{1,3},{2,0},{3,1},{4,6},{5,7},{6,4},{7,5},{8,10},{9,11},{10,... | collective-permute-start | bytes 98312 | tf_op jit(solution)/shard_map/sum_over_chips/ppermute | solution.py:564
